TPU v7x, 32 devices: a whole 2x2x4 slice. The times are simulated.
32 devices in a mesh: groups: 2 (over y), row: 8 (over z, x), col: 2 (over core).
Axes of the slice: x: 2, y: 2, z: 4, core: 2. Of those that a mesh axis runs over, the one named last changes fastest.
Arguments:
- cross_spectra: bfloat16 [4, 2, 8192, 8192], P('groups', None, 'row', 'col'), parts along dimension 0
- replicas: bfloat16 [4, 2, 2, 4096, 512], P('groups', None, 'col', 'row'), parts along dimension 0
- tile_order: int32 [32], P('groups'), parts along dimension 0, may hold values from 0 to 15, each once
Outputs:
- beam: float32 [4, 512], P('groups', 'col'), parts along dimension 0
- refined: float32 [4, 16, 32], P('groups'), parts along dimension 0
There are 2 independent parts, one for each index of `groups`. A program takes and returns all parts, laid end to end along the dimension named above; each array names one. Nothing has to cross between parts.
Inputs may be any that keep to these rules, and one draw needn't show every extreme that they name: `tile_order`: each tile number appears once.
All inputs are finite; a program needn't handle non-finite values. Where the computation divides by a largest or mean magnitude, that divisor is 1e-20 or more.
Results may differ from a plain program's by a relative error of at most 0.0003.
Values may be sent and summed in bfloat16 or wider, within the bound.
No kernel may reach another device: no remote copies, remote signals or barrier semaphores. Data moves between devices by JAX's collectives and lax.ppermute only.
A program may use at most 192 MiB of HBM per device.

v0:
```python
import jax
import jax.numpy as jnp
from jax import lax
from jax.sharding import PartitionSpec as P


def from_partner(value, axis, bit):
    mask = 2**bit
    pairs = [(source, source ^ mask) for source in range(lax.axis_size(axis))]
    return lax.ppermute(value, axis, pairs)


def combine_parts(parts):
    return jnp.stack([parts[:, 0, 0] - parts[:, 1, 1], parts[:, 0, 1] + parts[:, 1, 0]], axis=1)


def body(cross_spectra, replicas, tile_order):
    fnum = cross_spectra.shape[0]
    rows = cross_spectra.shape[2]
    half = cross_spectra.shape[3]
    sources = replicas.shape[4]
    row_index = lax.axis_index("row")
    col_index = lax.axis_index("col")
    first_row = row_index * rows
    holder = first_row // half
    offset = first_row - holder * half
    own_shard = replicas[:, :, 0].astype(jnp.float32)
    norm_terms = jnp.sum(own_shard * own_shard, axis=(1, 2))
    whole = lax.all_gather(replicas, "row", axis=3, tiled=True)[:, :, 0]
    parts = jnp.einsum("fark,fbks->fabrs", cross_spectra, whole, preferred_element_type=jnp.float32)
    field = combine_parts(parts)
    own_rows = lax.dynamic_slice_in_dim(whole, offset, rows, 2)
    partner_rows = from_partner(own_rows, "col", 0)
    block_rows = jnp.where(holder == col_index, own_rows, partner_rows).astype(jnp.float32)
    width = sources // 2
    field_part, norm_part = (
        lax.psum_scatter(field, "col", scatter_dimension=3, tiled=True),
        lax.psum_scatter(norm_terms, "col", scatter_dimension=1, tiled=True),
    )
    rows_half = lax.dynamic_slice_in_dim(block_rows, col_index * width, width, 3)
    numer = jnp.sum(rows_half * field_part, axis=(1, 2))
    numer, norms = lax.psum((numer, norm_part), "row")
    beam_half = numer / (norms + 1e-06)
    beam_full = lax.all_gather(beam_half, "col", axis=1, tiled=True)
    peak = jnp.max(jnp.abs(beam_full), axis=1) + 1e-06
    count = tile_order.shape[0]
    tile = sources // count
    picker = (tile_order[:, None] == jnp.arange(count, dtype=jnp.int32)[None, :]).astype(
        jnp.float32
    )
    tiles = beam_full.reshape(fnum, count, tile)
    refined = (
        jnp.einsum("tu,fup->ftp", picker, tiles, precision=lax.Precision.HIGHEST)
        / peak[:, None, None]
    )
    return (beam_half, refined)


def solution(mesh):
    in_specs = (P("groups", None, "row", "col"), P("groups", None, "col", "row", None), P("groups"))
    out_specs = (P("groups", "col"), P("groups", None, None))
    return jax.shard_map(body, mesh=mesh, in_specs=in_specs, out_specs=out_specs, check_vma=False)
```

profile of v0, /device:TPU:0, one launch (start us, length us, event | category | flops | bytes accessed | tf_op | source)
XLA Modules:
  0.0 355.0 jit_solution(14133889159474872928)
XLA Ops:
  8.0 0.0 copy-start
  8.0 0.0 all-gather.2.cloned.1.call-start
  8.1 4.3 %copy.14 = bf16[2,2,1,512,512]{3,4,1,0,2:T(8,128)(2,1)} copy(bf16[2,2,1,512,512]{4,3,2,1,0:T(8,128)(2,1)} %param.4) | data formatting | bytes 4194304 | tf_op args[1]
  12.4 0.0 all-gather.2.cloned.1.call-update
  12.4 0.0 reduce-scatter.7.cloned.1.call-start
  12.4 0.0 copy-done
  12.4 0.4 multiply_reduce_fusion
  12.9 0.9 copy.24
  13.8 0.0 reduce-scatter.7.cloned.1.call-update
  13.8 0.0 reduce-scatter.5.cloned.1.call-start
  13.8 229.2 %all-gather.2.cloned.1.call-done = bf16[2,2,1,4096,512]{3,4,1,0,2:T(8,128)(2,1)} async-done(((bf16[2,2,1,512,512]{3,4,1,0,2:T(8,128)(2,1)}), bf16[2,2,1,4096,512]{3,4,1,0,2:T(8,128)(2,1)}) %all-gather.2.cloned.1.call-update) | async-done | bytes 16777232 | tf_op jit(solution)/shard_map/all_gather | solution.py:29
  243.0 43.2 %fusion.3 = f32[2,2,2,1024,512]{3,4,1,2,0:T(8,128)} fusion(bf16[2,2,1024,4096]{3,2,1,0:T(8,128)(2,1)} %param.3, bf16[2,2,1,4096,512]{3,4,1,0,2:T(8,128)(2,1)} %all-gather.2.cloned.1.call-done), kind=kOutput, calls=%fused_computation.4 | convolution fusion | flops 34359738368 | bytes 67108864 | tf_op jit(solution)/shard_map/fark,fbks->fabrs/dot_general | solution.py:30
  286.2 4.4 %fusion.8 = f32[2,1,1024,512]{2,3,0,1:T(8,128)S(1)} fusion(f32[2,2,2,1024,512]{3,4,1,2,0:T(8,128)} %fusion.3), kind=kLoop, calls=%fused_computation.6 | loop fusion | flops 1048576 | bytes 12582912 | tf_op jit(solution)/shard_map/add | solution.py:14
  290.6 4.4 %fusion.10 = f32[2,1,1024,512]{2,3,0,1:T(8,128)S(1)} fusion(f32[2,2,2,1024,512]{3,4,1,2,0:T(8,128)} %fusion.3), kind=kLoop, calls=%fused_computation.9 | loop fusion | flops 1048576 | bytes 12582912 | tf_op jit(solution)/shard_map/sub | solution.py:14
  295.0 4.1 %pad_maximum_fusion = f32[2,2,1024,512]{2,3,0,1:T(8,128)} fusion(f32[2,1,1024,512]{2,3,0,1:T(8,128)S(1)} %fusion.8, f32[2,1,1024,512]{2,3,0,1:T(8,128)S(1)} %fusion.10), kind=kLoop, calls=%fused_computation.3 | loop fusion | flops 2097152 | bytes 16777216 | tf_op jit(solution)/shard_map/stack | solution.py:14
  299.1 0.0 reduce-scatter.5.cloned.1.call-update
  299.1 2.6 dynamic-slice_bitcast_fusion
  301.8 2.5 copy.17
  304.3 0.0 collective-permute-start
  304.3 0.0 reduce-scatter.7.cloned.1.call-done
  304.3 1.0 copy.25
  305.3 0.0 copy-start.2
  305.3 7.9 %collective-permute-done = bf16[2,2,1024,512]{2,3,0,1:T(8,128)(2,1)} collective-permute-done((bf16[2,2,1024,512]{2,3,0,1:T(8,128)(2,1)}, bf16[2,2,1024,512]{2,3,0,1:T(8,128)(2,1)}, u32[]{:S(2)}, u32[]{:S(2)}) %collective-permute-start) | collective-permute-done | bytes 4194336 | tf_op jit(solution)/shard_map/ppermute | solution.py:10
  313.2 6.3 %reduce-scatter.5.cloned.1.call-done = f32[2,2,1024,256]{2,3,0,1:T(8,128)} async-done(((f32[2,2,1024,512]{2,3,0,1:T(8,128)}), f32[2,2,1024,256]{2,3,0,1:T(8,128)}) %reduce-scatter.5.cloned.1.call-update) | async-done | bytes 4194320 | tf_op jit(solution)/shard_map/reduce_scatter | solution.py:37
  319.4 4.2 %multiply_reduce_fusion.1 = f32[2,256]{1,0:T(2,128)S(1)} fusion(f32[2,2,1024,256]{2,3,0,1:T(8,128)} %reduce-scatter.5.cloned.1.call-done, bf16[2,2,1024,512]{2,3,0,1:T(8,128)(2,1)} %collective-permute-done, s32[]{:T(128)S(6)} %select_n.23, pred[]{:T(512)S(6)} %eq.16, bf16[2,2,1,4096,512]{3,4,1,0,2:T(8,128)(2,1)} %all-gather.2.cloned.1.call-done, s32[]{:T(128)S(6)} %select_n.21), kind=kLoop, calls=%fused_computation.12 | loop fusion | flops 4193792 | bytes 10487817 | tf_op jit(solution)/shard_map/reduce_sum | solution.py:41
  323.7 21.0 %all-reduce = (f32[2,256]{1,0:T(2,128)S(1)}, f32[2,256]{1,0:T(2,128)S(1)}) all-reduce(f32[2,256]{1,0:T(2,128)S(1)} %multiply_reduce_fusion.1, f32[2,256]{1,0:T(2,128)S(1)} %copy.25), channel_id=1, replica_groups=mesh['groups'=2,'row'=8,'col'=2] {'row'}, use_global_device_ids=true, to_apply=%region_2.3 | all-reduce | flops 1024 | bytes 8192 | tf_op jit(solution)/shard_map/psum | solution.py:42
  344.7 0.0 copy-start.1
  344.7 1.8 all_gather.7
  346.5 0.1 reshape.50
  346.6 0.1 abs_reduce_fusion
  346.7 0.0 copy-done.2
  346.7 0.8 fusion.11
  347.5 0.0 copy-done.1
  (2 shorter events, 0.0 us)
Async XLA Ops:
  8.0 4.4 %copy-start = (bf16[2,2,1,512,512]{4,3,2,1,0:T(8,128)(2,1)S(1)}, bf16[2,2,1,512,512]{4,3,2,1,0:T(8,128)(2,1)}, u32[]{:S(2)}) copy-start(bf16[2,2,1,512,512]{4,3,2,1,0:T(8,128)(2,1)} %param.4) | copy-start | bytes 6291460
  8.0 235.0 %all-gather.2.cloned.1.call-start = ((), (), s32[]{:S(2)}) async-start(), calls=%async_computation.2 | async-start | bytes 18874368 | tf_op jit(solution)/shard_map/all_gather | solution.py:29
  12.4 291.9 %reduce-scatter.7.cloned.1.call-start = ((), (), s32[]{:S(2)}) async-start(), calls=%async_computation.4 | async-start | bytes 393216
  13.8 305.7 %reduce-scatter.5.cloned.1.call-start = ((), (), s32[]{:S(2)}) async-start(), calls=%async_computation.3 | async-start | bytes 12582912 | tf_op jit(solution)/shard_map/reduce_scatter | solution.py:37
  304.3 8.9 %collective-permute-start = (bf16[2,2,1024,512]{2,3,0,1:T(8,128)(2,1)}, bf16[2,2,1024,512]{2,3,0,1:T(8,128)(2,1)}, u32[]{:S(2)}, u32[]{:S(2)}) collective-permute-start(bf16[2,2,1024,512]{2,3,0,1:T(8,128)(2,1)} %copy.17), channel_id=1, source_target_pairs={{0,1},{1,0},{2,3},{3,2},{4,5},{5,4},{6,7},{7,6},{8,9},{9,8},{10,11... | collective-permute-start | bytes 12582920 | tf_op jit(solution)/shard_map/ppermute | solution.py:10
  305.3 41.4 %copy-start.2 = (s32[16]{0:T(128)S(1)}, s32[16]{0:T(128)}, u32[]{:S(2)}) copy-start(s32[16]{0:T(128)} %param.5) | copy-start | bytes 196
  344.7 2.8 copy-start.1
Sparse Core Ops, SparseCore 0:
  12.5 230.4 all-gather.1
Sparse Core Ops, SparseCore 1:
  15.1 10.3 reduce-scatter.6
  299.2 20.2 reduce-scatter.4
where the time goes:
time: 355 us
  waiting for transfers between devices  243 us (68%)
  matrix products  44 us (12%)
  blocking collectives  22.8 us (6%)
  other arithmetic  17.7 us (5%)
  between operations  15.5 us (4%)
  local copies, waits for them, and re-layouts  11.4 us (3%)
    all_gather x1, waiting for transfers between devices, body(): whole = lax.all_gather(replicas, 'row', axis=3, tiled=True)[:, :, 0]  229 us
    dot_general x1, matrix products, body(): jnp.einsum('fark,fbks->fabrs', cross_spectra, whole, preferred_element_ty...  43.2 us
    psum x1, blocking collectives, body(): numer, norms = lax.psum((numer, norm_part), 'row')  21 us
    ppermute x1, waiting for transfers between devices, from_partner(): return lax.ppermute(value, axis, pairs)  7.87 us
  transfers between devices with their start and end apart: 4, of which 3 were waited for; matrix products, arithmetic and copies ran while one was open for 18% of the time, Pallas kernels for 0%

commit v1 on v0

v1 whole, which is shorter than its diff:
```python
import functools

import jax
import jax.numpy as jnp
from jax import lax
from jax.experimental import pallas as pl
from jax.experimental.pallas import tpu as pltpu
from jax.sharding import PartitionSpec as P

ROW_TILE = 256
VMEM_LIMIT = 48 * 1024 * 1024


def swap(value, axis, mask):
    pairs = [(source, source ^ mask) for source in range(lax.axis_size(axis))]
    return lax.ppermute(value, axis, pairs)


def field_tile(r_refs, w_refs):
    re, im = None, None
    for r_ref, w_ref in zip(r_refs, w_refs):
        rows_re, rows_im = r_ref[0, 0], r_ref[0, 1]
        w_re, w_im = w_ref[0], w_ref[1]
        dot = functools.partial(jnp.dot, preferred_element_type=jnp.float32)
        step_re = dot(rows_re, w_re) - dot(rows_im, w_im)
        step_im = dot(rows_re, w_im) + dot(rows_im, w_re)
        re = step_re if re is None else re + step_re
        im = step_im if im is None else im + step_im
    return re, im


def field_kernel(count, has_total, ids, *refs):
    r_refs, w_refs = refs[:count], refs[count : 2 * count]
    out = refs[-1]
    re, im = field_tile(r_refs, w_refs)
    if has_total:
        total = refs[2 * count]
        re, im = re + total[0], im + total[1]
    out[0] = re
    out[1] = im


def numer_kernel(count, half, ids, *refs):
    r_refs, w_refs = refs[:count], refs[count : 2 * count]
    total, rows, out = refs[2 * count], refs[2 * count + 1], refs[-1]
    re, im = field_tile(r_refs, w_refs)
    re, im = re + total[0], im + total[1]
    product = rows[0].astype(jnp.float32) * re + rows[1].astype(jnp.float32) * im
    part = jnp.sum(product.reshape(-1, 8, product.shape[-1]), axis=0)

    @pl.when(pl.program_id(0) == 0)
    def _():
        out[...] = jnp.zeros_like(out)

    out[...] += part


def spectra_spec(freq, tile, width, which):
    return pl.BlockSpec((1, 2, tile, width), lambda i, ids: (freq, 0, i, ids[which]))


def operand_specs(freq, tile, pieces):
    width, sources = pieces[0].shape[1:]
    specs = [spectra_spec(freq, tile, width, k) for k in range(len(pieces))]
    return specs + [pl.BlockSpec((2, width, sources), lambda i, ids: (0, 0, 0))] * len(pieces)


def cost(rows, pieces, extra):
    width, sources = pieces[0].shape[1:]
    count = len(pieces)
    return pl.CostEstimate(
        flops=8 * count * rows * width * sources,
        bytes_accessed=count * (4 * rows * width + 4 * width * sources) + extra,
        transcendentals=0,
    )


def add_field(cross, freq, ids, pieces, total):
    rows, sources = cross.shape[2], pieces[0].shape[2]
    tile = min(ROW_TILE, rows)
    block = pl.BlockSpec((2, tile, sources), lambda i, ids: (0, i, 0))
    specs = operand_specs(freq, tile, pieces)
    args = [cross] * len(pieces) + list(pieces)
    if total is not None:
        specs, args = specs + [block], args + [total]
    return pl.pallas_call(
        functools.partial(field_kernel, len(pieces), total is not None),
        out_shape=jax.ShapeDtypeStruct((2, rows, sources), jnp.float32),
        grid_spec=pltpu.PrefetchScalarGridSpec(
            num_scalar_prefetch=1, grid=(rows // tile,), in_specs=specs, out_specs=block
        ),
        compiler_params=pltpu.CompilerParams(vmem_limit_bytes=VMEM_LIMIT),
        cost_estimate=cost(rows, pieces, 8 * rows * sources),
    )(ids, *args)


def finish(cross, freq, ids, pieces, total, local_rows):
    rows, sources = cross.shape[2], pieces[0].shape[2]
    tile = min(ROW_TILE, rows)
    block = pl.BlockSpec((2, tile, sources), lambda i, ids: (0, i, 0))
    specs = operand_specs(freq, tile, pieces) + [block, block]
    args = [cross] * len(pieces) + list(pieces) + [total, local_rows]
    out = pl.pallas_call(
        functools.partial(numer_kernel, len(pieces), None),
        out_shape=jax.ShapeDtypeStruct((8, sources), jnp.float32),
        grid_spec=pltpu.PrefetchScalarGridSpec(
            num_scalar_prefetch=1,
            grid=(rows // tile,),
            in_specs=specs,
            out_specs=pl.BlockSpec((8, sources), lambda i, ids: (0, 0)),
        ),
        compiler_params=pltpu.CompilerParams(vmem_limit_bytes=VMEM_LIMIT),
        cost_estimate=cost(rows, pieces, 12 * rows * sources),
    )(ids, *args)
    return jnp.sum(out, axis=0)


def pick_kernel(ids, *refs):
    pieces, out, sem = refs[:-2], refs[-2], refs[-1]
    width = pieces[0].shape[1]
    for slot in range(2):
        for k, piece in enumerate(pieces):

            @pl.when(ids[slot] == k)
            def _():
                pltpu.make_async_copy(
                    piece, out.at[:, pl.ds(slot * width, width)], sem.at[slot]
                ).start()

    for slot in range(2):
        pltpu.make_async_copy(
            pieces[0], out.at[:, pl.ds(slot * width, width)], sem.at[slot]
        ).wait()


def pick_rows(ids, pieces):
    _, width, sources = pieces[0].shape
    return pl.pallas_call(
        pick_kernel,
        out_shape=jax.ShapeDtypeStruct((2, 2 * width, sources), pieces[0].dtype),
        grid_spec=pltpu.PrefetchScalarGridSpec(
            num_scalar_prefetch=1,
            grid=(1,),
            in_specs=[pl.BlockSpec(memory_space=pl.ANY)] * len(pieces),
            out_specs=pl.BlockSpec(memory_space=pl.ANY),
            scratch_shapes=[pltpu.SemaphoreType.DMA((2,))],
        ),
    )(ids, *pieces)


def numer_by_swaps(cross, replicas):
    freqs, rows = cross.shape[0], cross.shape[2]
    me = lax.axis_index("row").astype(jnp.int32)
    col = lax.axis_index("col").astype(jnp.int32)
    width = replicas.shape[3]
    half = cross.shape[3]
    holder = me * rows // half
    first = (me * rows - holder * half) // width
    row_ids = jnp.stack([first ^ me, (first + 1) ^ me])

    pieces = [[None] * 8 for _ in range(freqs)]
    for f in range(freqs):
        pieces[f][0] = replicas[f, :, 0]
    for f in range(freqs):
        pieces[f][1] = swap(pieces[f][0], "row", 1)
        pieces[f][4] = swap(pieces[f][0], "row", 4)
        pieces[f][2] = swap(pieces[f][0], "row", 2)
    for f in range(freqs):
        pieces[f][5] = swap(pieces[f][4], "row", 1)
        pieces[f][6] = swap(pieces[f][4], "row", 2)
        pieces[f][3] = swap(pieces[f][1], "row", 2) if f % 2 == 0 else swap(pieces[f][2], "row", 1)
    for f in range(freqs):
        pieces[f][7] = swap(pieces[f][6], "row", 1)

    numer = []
    for f in range(freqs):
        part = pieces[f]
        mine = pick_rows(row_ids, part)
        other = swap(mine, "col", 1)
        local_rows = jnp.where(holder == col, mine, other)
        total = add_field(cross, f, me ^ jnp.array([0, 1, 2], jnp.int32), part[:3], None)
        total = add_field(cross, f, me ^ jnp.array([4, 5, 3], jnp.int32), [part[4], part[5], part[3]], total)
        numer.append(finish(cross, f, me ^ jnp.array([6, 7], jnp.int32), part[6:], total, local_rows))
    return jnp.stack(numer)


def numer_by_gather(cross, replicas):
    rows, half = cross.shape[2], cross.shape[3]
    row_index, col_index = lax.axis_index("row"), lax.axis_index("col")
    first_row = row_index * rows
    holder = first_row // half
    whole = lax.all_gather(replicas, "row", axis=3, tiled=True)[:, :, 0]
    parts = jnp.einsum("fark,fbks->fabrs", cross, whole, preferred_element_type=jnp.float32)
    field = jnp.stack([parts[:, 0, 0] - parts[:, 1, 1], parts[:, 0, 1] + parts[:, 1, 0]], axis=1)
    own_rows = lax.dynamic_slice_in_dim(whole, first_row - holder * half, rows, 2)
    block_rows = jnp.where(holder == col_index, own_rows, swap(own_rows, "col", 1))
    return jnp.sum(block_rows.astype(jnp.float32) * field, axis=(1, 2))


def body(cross_spectra, replicas, tile_order):
    fnum = cross_spectra.shape[0]
    sources = replicas.shape[4]
    own = replicas[:, :, 0].astype(jnp.float32)
    norm_part = jnp.sum(own * own, axis=(1, 2))
    doubling = (
        lax.axis_size("row") == 8
        and replicas.shape[3] % 128 == 0
        and cross_spectra.shape[2] == 2 * replicas.shape[3]
    )
    numer_part = (numer_by_swaps if doubling else numer_by_gather)(cross_spectra, replicas)
    sums = lax.psum(jnp.stack([numer_part, norm_part]), ("row", "col"))
    beam = sums[0] / (sums[1] + 1e-06)
    width = sources // lax.axis_size("col")
    beam_half = lax.dynamic_slice_in_dim(beam, lax.axis_index("col") * width, width, 1)
    peak = jnp.max(jnp.abs(beam), axis=1) + 1e-06
    count = tile_order.shape[0]
    picker = (tile_order[:, None] == jnp.arange(count, dtype=jnp.int32)[None, :]).astype(jnp.float32)
    tiles = beam.reshape(fnum, count, sources // count)
    refined = (
        jnp.einsum("tu,fup->ftp", picker, tiles, precision=lax.Precision.HIGHEST)
        / peak[:, None, None]
    )
    return (beam_half, refined)


def solution(mesh):
    in_specs = (P("groups", None, "row", "col"), P("groups", None, "col", "row", None), P("groups"))
    out_specs = (P("groups", "col"), P("groups", None, None))
    return jax.shard_map(body, mesh=mesh, in_specs=in_specs, out_specs=out_specs, check_vma=False)
```

time: 355 us -> 408 us (1.15)
  Pallas kernels: 0 us -> 193 us
  waiting for transfers between devices: 243 us -> 80.7 us
  starting transfers between devices: 0.13 us -> 84.1 us
  matrix products: 44 us -> 0.8 us
  between operations: 15.5 us -> 0.83 us
  blocking collectives: 22.8 us -> 35.6 us
  other arithmetic: 17.7 us -> 5.42 us
  local copies, waits for them, and re-layouts: 11.4 us -> 6.87 us
    all_gather x1 -> x0, waiting for transfers between devices: 229 us -> none  [body(): whole = lax.all_gather(replicas, 'row', axis=3, tiled=True)[:, :, 0]]
    pallas_call x0 -> x8, Pallas kernels: none -> 193 us  [the longest x2 131 us: pick_rows(): pl.pallas_call(pick_kernel, out_shape=jax.ShapeDtypeStruct((2, 2 * width,...]
    ppermute x1 -> x16, starting transfers between devices: 0.01 us -> 84.1 us  [swap(): return lax.ppermute(value, axis, pairs)]
    ppermute x1 -> x16, waiting for transfers between devices: 7.87 us -> 80.7 us  [swap(): return lax.ppermute(value, axis, pairs)]
    dot_general x1 -> x0, matrix products: 43.2 us -> none  [body(): jnp.einsum('fark,fbks->fabrs', cross_spectra, whole, preferred_element_ty...]
    psum x1, blocking collectives: 21 us -> 35.6 us  [body(): sums = lax.psum(jnp.stack([numer_part, norm_part]), ('row', 'col'))]
    reduce_scatter x1 -> x0, waiting for transfers between devices: 6.28 us -> none  [body(): lax.psum_scatter(field, 'col', scatter_dimension=3, tiled=True)]
    dynamic_slice x2 -> x1, local copies, waits for them, and re-layouts: 5.17 us -> 0.59 us  [body(): lax.dynamic_slice_in_dim(beam, lax.axis_index('col') * width, width, 1)]
  transfers between devices with their start and end apart: 4 -> 16, of which waited for: 3 -> 6; matrix products, arithmetic and copies ran while one was open for 18% -> 1% of each run, Pallas kernels for 0% -> 45%
where the time goes in v1:
time: 408 us
  Pallas kernels  193 us (47%)
  starting transfers between devices  84.1 us (21%)
  waiting for transfers between devices  80.7 us (20%)
  blocking collectives  35.6 us (9%)
  local copies, waits for them, and re-layouts  6.87 us (2%)
  other arithmetic  5.42 us (1%)
    pallas_call x2, Pallas kernels, pick_rows(): pl.pallas_call(pick_kernel, out_shape=jax.ShapeDtypeStruct((2, 2 * width,...  131 us
    ppermute x16, starting transfers between devices, swap(): return lax.ppermute(value, axis, pairs)  84.1 us
    ppermute x16, waiting for transfers between devices, swap(): return lax.ppermute(value, axis, pairs)  80.7 us
    pallas_call x4, Pallas kernels, add_field(): pl.pallas_call(functools.partial(field_kernel, len(pieces), total is not...  45.9 us
    psum x1, blocking collectives, body(): sums = lax.psum(jnp.stack([numer_part, norm_part]), ('row', 'col'))  35.6 us
    pallas_call x2, Pallas kernels, finish(): pl.pallas_call(functools.partial(numer_kernel, len(pieces), None), out_sh...  16.6 us
  transfers between devices with their start and end apart: 16, of which 6 were waited for; matrix products, arithmetic and copies ran while one was open for 1% of the time, Pallas kernels for 45%

profile of v1, /device:TPU:0, one launch (start us, length us, event | category | flops | bytes accessed | tf_op | source)
XLA Modules:
  0.0 407.5 jit_solution(2385452975663880097)
XLA Ops:
  0.6 0.0 copy-start.12
  0.6 0.0 copy-start.11
  0.7 2.7 slice_bitcast_fusion.1
  3.4 4.0 collective-permute-start
  7.4 1.5 collective-permute-start.4
  8.9 1.6 collective-permute-start.6
  10.5 0.3 collective-permute-start.8
  10.8 44.0 %collective-permute-done.refs_3_.refs_4_ = bf16[2,512,512]{2,1,0:T(8,128)(2,1)S(1)} collective-permute-done((bf16[2,512,512]{2,1,0:T(8,128)(2,1)S(1)}, bf16[2,512,512]{2,1,0:T(8,128)(2,1)S(1)}, u32[]{:S(2)}, u32[]{:S(2)}) %collective-permute-start) | collective-permute-done | bytes 1048608 | tf_op jit(solution)/shard_map/ppermute | solution.py:16
  54.8 0.0 collective-permute-start.1
  54.8 2.0 collective-permute-start.12
  56.8 0.0 collective-permute-done.4.refs_4_.refs_1_
  56.8 22.4 %collective-permute-start.3 = (bf16[2,512,512]{2,1,0:T(8,128)(2,1)S(1)}, bf16[2,512,512]{2,1,0:T(8,128)(2,1)}, u32[]{:S(2)}, u32[]{:S(2)}) collective-permute-start(bf16[2,512,512]{2,1,0:T(8,128)(2,1)S(1)} %collective-permute-done.refs_3_.refs_4_), channel_id=1, source_target_pairs={{0,2},{2,0},{4,6},{6,4},{8,10},{10,8},{12,14},{14,12},{1,3},{3,1},... | collective-permute-start | bytes 3145736 | tf_op jit(solution)/shard_map/ppermute | solution.py:16
  79.2 0.0 collective-permute-start.5
  79.3 19.0 %collective-permute-done.8.refs_3_.refs_4_ = bf16[2,512,512]{2,1,0:T(8,128)(2,1)} collective-permute-done((bf16[2,512,512]{2,1,0:T(8,128)(2,1)}, bf16[2,512,512]{2,1,0:T(8,128)(2,1)}, u32[]{:S(2)}, u32[]{:S(2)}) %collective-permute-start.8) | collective-permute-done | bytes 1048608 | tf_op jit(solution)/shard_map/ppermute | solution.py:16
  98.3 0.7 collective-permute-start.9
  98.9 3.3 collective-permute-done.1.refs_6_.refs_2_
  102.2 20.0 %collective-permute-start.2 = (bf16[2,512,512]{2,1,0:T(8,128)(2,1)S(1)}, bf16[2,512,512]{2,1,0:T(8,128)(2,1)}, u32[]{:S(2)}, u32[]{:S(2)}) collective-permute-start(bf16[2,512,512]{2,1,0:T(8,128)(2,1)S(1)} %collective-permute-done.1.refs_6_.refs_2_), channel_id=1, source_target_pairs={{0,2},{2,0},{4,6},{6,4},{8,10},{10,8},{12,14},{14,12},{1,3},{3,1},... | collective-permute-start | bytes 3145736 | tf_op jit(solution)/shard_map/ppermute | solution.py:16
  122.2 0.6 pad_add_fusion.ids
  122.8 2.0 collective-permute-done.12.refs_5_.refs_2_
  124.8 20.0 %collective-permute-start.14 = (bf16[2,512,512]{2,1,0:T(8,128)(2,1)}, bf16[2,512,512]{2,1,0:T(8,128)(2,1)}, u32[]{:S(2)}, u32[]{:S(2)}) collective-permute-start(bf16[2,512,512]{2,1,0:T(8,128)(2,1)} %get-tuple-element.5.refs_3_.refs_0_), channel_id=1, source_target_pairs={{0,2},{2,0},{4,6},{6,4},{8,10},{10,8},{12,14},{14,12},{1,3},{3,1},... | collective-permute-start | bytes 3145736 | tf_op jit(solution)/shard_map/ppermute | solution.py:16
  144.8 0.0 collective-permute-start.11
  144.8 2.4 collective-permute-done.5.refs_5_.refs_3_
  147.3 9.7 %collective-permute-start.13 = (bf16[2,512,512]{2,1,0:T(8,128)(2,1)}, bf16[2,512,512]{2,1,0:T(8,128)(2,1)}, u32[]{:S(2)}, u32[]{:S(2)}) collective-permute-start(bf16[2,512,512]{2,1,0:T(8,128)(2,1)} %collective-permute-done.12.refs_5_.refs_2_), channel_id=1, source_target_pairs={{0,2},{2,0},{4,6},{6,4},{8,10},{10,8},{12,14},{14,12},{1,3},{3,1},... | collective-permute-start | bytes 3145736 | tf_op jit(solution)/shard_map/ppermute | solution.py:16
  156.9 10.1 %collective-permute-done.9.refs_6_.refs_2_ = bf16[2,512,512]{2,1,0:T(8,128)(2,1)} collective-permute-done((bf16[2,512,512]{2,1,0:T(8,128)(2,1)}, bf16[2,512,512]{2,1,0:T(8,128)(2,1)}, u32[]{:S(2)}, u32[]{:S(2)}) %collective-permute-start.9) | collective-permute-done | bytes 1048608 | tf_op jit(solution)/shard_map/ppermute | solution.py:16
  167.0 1.1 collective-permute-start.10
  168.2 2.6 multiply_reduce_fusion
  170.8 65.3 %shard_map.106 = bf16[2,1024,512]{2,1,0:T(8,128)(2,1)} custom-call(s32[2]{0:T(128)} %pad_add_fusion.ids, bf16[2,512,512]{2,1,0:T(8,128)(2,1)} %copy-done, bf16[2,512,512]{2,1,0:T(8,128)(2,1)} %collective-permute-done.4.refs_4_.refs_1_, bf16[2,512,512]{2,1,0:T(8,128)(2,1)} %copy-done.6, bf16[2,512,512]{2,1,0:T(8,128)(2,1)} %collective-permute-done.5.refs_5_.refs_3_, ...), custom_call_target="tpu_custom_call" | custom-call | tf_op jit(solution)/shard_map/pallas_call | solution.py:138
  236.1 0.1 collective-permute-start.7
  236.2 1.2 copy-done.1
  237.4 1.2 copy-done.7
  238.7 10.8 %shard_map.104.refs_6_ = f32[2,1024,512]{2,1,0:T(8,128)} custom-call(s32[3]{0:T(128)S(1)} %iota_xor_fusion.ids, bf16[2,2,1024,4096]{3,2,1,0:T(8,128)(2,1)} %refs_1_.11, bf16[2,2,1024,4096]{3,2,1,0:T(8,128)(2,1)} %refs_1_.11, bf16[2,2,1024,4096]{3,2,1,0:T(8,128)(2,1)} %refs_1_.11, bf16[2,512,512]{2,1,0:T(8,128)(2,1)S(1)} %copy-done.1, ...), custom_call_target="tpu_custom_call" | custom-call | flops 6442450944 | bytes 13631488 | tf_op jit(solution)/shard_map/pallas_call | solution.py:86
  249.5 65.3 %shard_map.110 = bf16[2,1024,512]{2,1,0:T(8,128)(2,1)} custom-call(s32[2]{0:T(128)} %pad_add_fusion.ids, bf16[2,512,512]{2,1,0:T(8,128)(2,1)} %get-tuple-element.5.refs_3_.refs_0_, bf16[2,512,512]{2,1,0:T(8,128)(2,1)} %collective-permute-done.14.refs_4_.refs_1_, bf16[2,512,512]{2,1,0:T(8,128)(2,1)} %collective-permute-done.12.refs_5_.refs_2_, ...), custom_call_target="tpu_custom_call" | custom-call | tf_op jit(solution)/shard_map/pallas_call | solution.py:138
  314.8 0.6 collective-permute-start.15
  315.4 11.5 %shard_map.108.refs_6_ = f32[2,1024,512]{2,1,0:T(8,128)} custom-call(s32[3]{0:T(128)S(1)} %iota_xor_fusion.ids, bf16[2,2,1024,4096]{3,2,1,0:T(8,128)(2,1)} %refs_1_.11, bf16[2,2,1024,4096]{3,2,1,0:T(8,128)(2,1)} %refs_1_.11, bf16[2,2,1024,4096]{3,2,1,0:T(8,128)(2,1)} %refs_1_.11, bf16[2,512,512]{2,1,0:T(8,128)(2,1)} %get-tuple-element.5.refs_3_.refs_0_, ...), custom_call_target="tpu_custom_call" | custom-call | flops 6442450944 | bytes 13631488 | tf_op jit(solution)/shard_map/pallas_call | solution.py:86
  326.8 11.7 %shard_map.105.refs_4_ = f32[2,1024,512]{2,1,0:T(8,128)} custom-call(s32[3]{0:T(128)S(1)} %broadcast_xor_fusion.ids, bf16[2,2,1024,4096]{3,2,1,0:T(8,128)(2,1)} %refs_1_.11, bf16[2,2,1024,4096]{3,2,1,0:T(8,128)(2,1)} %refs_1_.11, bf16[2,2,1024,4096]{3,2,1,0:T(8,128)(2,1)} %refs_1_.11, bf16[2,512,512]{2,1,0:T(8,128)(2,1)S(1)} %copy-done.3, ...), custom_call_target="tpu_custom_call" | custom-call | flops 6442450944 | bytes 13631488 | tf_op jit(solution)/shard_map/pallas_call | solution.py:86
  338.5 12.0 %shard_map.109.refs_4_ = f32[2,1024,512]{2,1,0:T(8,128)} custom-call(s32[3]{0:T(128)S(1)} %broadcast_xor_fusion.ids, bf16[2,2,1024,4096]{3,2,1,0:T(8,128)(2,1)} %refs_1_.11, bf16[2,2,1024,4096]{3,2,1,0:T(8,128)(2,1)} %refs_1_.11, bf16[2,2,1024,4096]{3,2,1,0:T(8,128)(2,1)} %refs_1_.11, bf16[2,512,512]{2,1,0:T(8,128)(2,1)} %collective-permute-done.8.refs_3_.refs_4_, ...), custom_call_target="tpu_custom_call" | custom-call | flops 6442450944 | bytes 13631488 | tf_op jit(solution)/shard_map/pallas_call | solution.py:86
  350.5 0.2 broadcast_select_fusion.1.refs_5_
  350.8 1.0 copy-done.5
  351.7 8.1 %shard_map.107 = f32[8,512]{1,0:T(8,128)S(1)} custom-call(s32[2]{0:T(128)S(1)} %broadcast_xor_fusion.1.ids, bf16[2,2,1024,4096]{3,2,1,0:T(8,128)(2,1)} %refs_1_.11, bf16[2,2,1024,4096]{3,2,1,0:T(8,128)(2,1)} %refs_1_.11, bf16[2,512,512]{2,1,0:T(8,128)(2,1)S(1)} %copy-done.5, bf16[2,512,512]{2,1,0:T(8,128)(2,1)} %collective-permute-done.2.refs_7_.refs_3_, ...), custom_call_target="tpu_custom_call" | custom-call | flops 4294967296 | bytes 12582912 | tf_op jit(solution)/shard_map/pallas_call | solution.py:103
  359.9 1.8 broadcast_select_fusion.refs_5_
  361.7 0.0 copy-start.9
  361.8 0.0 copy-start.10
  361.8 8.5 %shard_map.111 = f32[8,512]{1,0:T(8,128)S(1)} custom-call(s32[2]{0:T(128)S(1)} %broadcast_xor_fusion.1.ids, bf16[2,2,1024,4096]{3,2,1,0:T(8,128)(2,1)} %refs_1_.11, bf16[2,2,1024,4096]{3,2,1,0:T(8,128)(2,1)} %refs_1_.11, bf16[2,512,512]{2,1,0:T(8,128)(2,1)} %collective-permute-done.9.refs_6_.refs_2_, ...), custom_call_target="tpu_custom_call" | custom-call | flops 4294967296 | bytes 12582912 | tf_op jit(solution)/shard_map/pallas_call | solution.py:103
  370.3 35.6 %psum.7 = f32[2,2,512]{2,1,0:T(2,128)S(1)} all-reduce(f32[2,2,512]{2,1,0:T(2,128)S(1)} %pad_maximum_fusion), channel_id=1, replica_groups=mesh['groups'=2,'row'=8,'col'=2] {'row','col'}, use_global_device_ids=true, to_apply=%region_3.4 | all-reduce | flops 2048 | bytes 16384 | tf_op jit(solution)/shard_map/psum | solution.py:211
  405.9 0.1 abs_reduce_fusion
  406.0 0.1 div.41
  406.1 0.6 dynamic-slice_bitcast_fusion
  406.7 0.8 fusion
  (36 shorter events, 0.1 us)
Async XLA Ops:
  0.6 122.2 %copy-start.12 = (s32[3]{0:T(128)S(1)}, s32[3]{0:T(128)}, u32[]{:S(2)}) copy-start(s32[3]{0:T(128)} %constant.57.clone) | copy-start | bytes 40
  0.6 167.5 %copy-start.11 = (s32[2]{0:T(128)S(1)}, s32[2]{0:T(128)}, u32[]{:S(2)}) copy-start(s32[2]{0:T(128)} %constant.58.clone) | copy-start | bytes 28
  3.4 167.4 %copy-start = (bf16[2,512,512]{2,1,0:T(8,128)(2,1)}, bf16[2,512,512]{2,1,0:T(8,128)(2,1)S(1)}, u32[]{:S(2)}) copy-start(bf16[2,512,512]{2,1,0:T(8,128)(2,1)S(1)} %get-tuple-element.4.refs_3_.refs_0_) | copy-start | bytes 3145732
  3.4 51.4 %collective-permute-start = (bf16[2,512,512]{2,1,0:T(8,128)(2,1)S(1)}, bf16[2,512,512]{2,1,0:T(8,128)(2,1)S(1)}, u32[]{:S(2)}, u32[]{:S(2)}) collective-permute-start(bf16[2,512,512]{2,1,0:T(8,128)(2,1)S(1)} %get-tuple-element.4.refs_3_.refs_0_), channel_id=1, source_target_pairs={{0,8},{2,10},{4,12},{6,14},{8,0},{10,2},{12,4},{14,6},{1,9},{3,11}... | collective-permute-start | bytes 3145736 | tf_op jit(solution)/shard_map/ppermute | solution.py:16
  7.4 49.4 %collective-permute-start.4 = (bf16[2,512,512]{2,1,0:T(8,128)(2,1)S(1)}, bf16[2,512,512]{2,1,0:T(8,128)(2,1)}, u32[]{:S(2)}, u32[]{:S(2)}) collective-permute-start(bf16[2,512,512]{2,1,0:T(8,128)(2,1)S(1)} %get-tuple-element.4.refs_3_.refs_0_), channel_id=1, source_target_pairs={{0,2},{2,0},{4,6},{6,4},{8,10},{10,8},{12,14},{14,12},{1,3},{3,1},... | collective-permute-start | bytes 3145736 | tf_op jit(solution)/shard_map/ppermute | solution.py:16
  8.9 70.3 %collective-permute-start.6 = (bf16[2,512,512]{2,1,0:T(8,128)(2,1)S(1)}, bf16[2,512,512]{2,1,0:T(8,128)(2,1)S(1)}, u32[]{:S(2)}, u32[]{:S(2)}) collective-permute-start(bf16[2,512,512]{2,1,0:T(8,128)(2,1)S(1)} %get-tuple-element.4.refs_3_.refs_0_), channel_id=1, source_target_pairs={{0,4},{2,6},{4,0},{6,2},{8,12},{10,14},{12,8},{14,10},{1,5},{3,7},... | collective-permute-start | bytes 3145736 | tf_op jit(solution)/shard_map/ppermute | solution.py:16
  10.5 87.8 %collective-permute-start.8 = (bf16[2,512,512]{2,1,0:T(8,128)(2,1)}, bf16[2,512,512]{2,1,0:T(8,128)(2,1)}, u32[]{:S(2)}, u32[]{:S(2)}) collective-permute-start(bf16[2,512,512]{2,1,0:T(8,128)(2,1)} %get-tuple-element.5.refs_3_.refs_0_), channel_id=1, source_target_pairs={{0,8},{2,10},{4,12},{6,14},{8,0},{10,2},{12,4},{14,6},{1,9},{3,11}... | collective-permute-start | bytes 3145736 | tf_op jit(solution)/shard_map/ppermute | solution.py:16
  54.8 116.0 %copy-start.2 = (bf16[2,512,512]{2,1,0:T(8,128)(2,1)}, bf16[2,512,512]{2,1,0:T(8,128)(2,1)S(1)}, u32[]{:S(2)}) copy-start(bf16[2,512,512]{2,1,0:T(8,128)(2,1)S(1)} %collective-permute-done.refs_3_.refs_4_) | copy-start | bytes 3145732
  54.8 47.4 %collective-permute-start.1 = (bf16[2,512,512]{2,1,0:T(8,128)(2,1)S(1)}, bf16[2,512,512]{2,1,0:T(8,128)(2,1)S(1)}, u32[]{:S(2)}, u32[]{:S(2)}) collective-permute-start(bf16[2,512,512]{2,1,0:T(8,128)(2,1)S(1)} %collective-permute-done.refs_3_.refs_4_), channel_id=1, source_target_pairs={{0,4},{2,6},{4,0},{6,2},{8,12},{10,14},{12,8},{14,10},{1,5},{3,7},... | collective-permute-start | bytes 3145736 | tf_op jit(solution)/shard_map/ppermute | solution.py:16
  54.8 69.9 %collective-permute-start.12 = (bf16[2,512,512]{2,1,0:T(8,128)(2,1)}, bf16[2,512,512]{2,1,0:T(8,128)(2,1)}, u32[]{:S(2)}, u32[]{:S(2)}) collective-permute-start(bf16[2,512,512]{2,1,0:T(8,128)(2,1)} %get-tuple-element.5.refs_3_.refs_0_), channel_id=1, source_target_pairs={{0,4},{2,6},{4,0},{6,2},{8,12},{10,14},{12,8},{14,10},{1,5},{3,7},... | collective-permute-start | bytes 3145736 | tf_op jit(solution)/shard_map/ppermute | solution.py:16
  56.8 88.0 %collective-permute-start.3 = (bf16[2,512,512]{2,1,0:T(8,128)(2,1)S(1)}, bf16[2,512,512]{2,1,0:T(8,128)(2,1)}, u32[]{:S(2)}, u32[]{:S(2)}) collective-permute-start(bf16[2,512,512]{2,1,0:T(8,128)(2,1)S(1)} %collective-permute-done.refs_3_.refs_4_), channel_id=1, source_target_pairs={{0,2},{2,0},{4,6},{6,4},{8,10},{10,8},{12,14},{14,12},{1,3},{3,1},... | collective-permute-start | bytes 3145736 | tf_op jit(solution)/shard_map/ppermute | solution.py:16
  79.2 23.0 %copy-start.6 = (bf16[2,512,512]{2,1,0:T(8,128)(2,1)}, bf16[2,512,512]{2,1,0:T(8,128)(2,1)S(1)}, u32[]{:S(2)}) copy-start(bf16[2,512,512]{2,1,0:T(8,128)(2,1)S(1)} %collective-permute-done.6.refs_5_.refs_2_) | copy-start | bytes 3145732
  79.2 68.0 %collective-permute-start.5 = (bf16[2,512,512]{2,1,0:T(8,128)(2,1)}, bf16[2,512,512]{2,1,0:T(8,128)(2,1)}, u32[]{:S(2)}, u32[]{:S(2)}) collective-permute-start(bf16[2,512,512]{2,1,0:T(8,128)(2,1)} %collective-permute-done.4.refs_4_.refs_1_), channel_id=1, source_target_pairs={{0,4},{2,6},{4,0},{6,2},{8,12},{10,14},{12,8},{14,10},{1,5},{3,7},... | collective-permute-start | bytes 3145736 | tf_op jit(solution)/shard_map/ppermute | solution.py:16
  98.3 68.8 %collective-permute-start.9 = (bf16[2,512,512]{2,1,0:T(8,128)(2,1)}, bf16[2,512,512]{2,1,0:T(8,128)(2,1)}, u32[]{:S(2)}, u32[]{:S(2)}) collective-permute-start(bf16[2,512,512]{2,1,0:T(8,128)(2,1)} %collective-permute-done.8.refs_3_.refs_4_), channel_id=1, source_target_pairs={{0,4},{2,6},{4,0},{6,2},{8,12},{10,14},{12,8},{14,10},{1,5},{3,7},... | collective-permute-start | bytes 3145736 | tf_op jit(solution)/shard_map/ppermute | solution.py:16
  102.2 68.6 %copy-start.4 = (bf16[2,512,512]{2,1,0:T(8,128)(2,1)}, bf16[2,512,512]{2,1,0:T(8,128)(2,1)S(1)}, u32[]{:S(2)}) copy-start(bf16[2,512,512]{2,1,0:T(8,128)(2,1)S(1)} %collective-permute-done.1.refs_6_.refs_2_) | copy-start | bytes 3145732
  102.2 68.6 %collective-permute-start.2 = (bf16[2,512,512]{2,1,0:T(8,128)(2,1)S(1)}, bf16[2,512,512]{2,1,0:T(8,128)(2,1)}, u32[]{:S(2)}, u32[]{:S(2)}) collective-permute-start(bf16[2,512,512]{2,1,0:T(8,128)(2,1)S(1)} %collective-permute-done.1.refs_6_.refs_2_), channel_id=1, source_target_pairs={{0,2},{2,0},{4,6},{6,4},{8,10},{10,8},{12,14},{14,12},{1,3},{3,1},... | collective-permute-start | bytes 3145736 | tf_op jit(solution)/shard_map/ppermute | solution.py:16
  124.8 124.7 %collective-permute-start.14 = (bf16[2,512,512]{2,1,0:T(8,128)(2,1)}, bf16[2,512,512]{2,1,0:T(8,128)(2,1)}, u32[]{:S(2)}, u32[]{:S(2)}) collective-permute-start(bf16[2,512,512]{2,1,0:T(8,128)(2,1)} %get-tuple-element.5.refs_3_.refs_0_), channel_id=1, source_target_pairs={{0,2},{2,0},{4,6},{6,4},{8,10},{10,8},{12,14},{14,12},{1,3},{3,1},... | collective-permute-start | bytes 3145736 | tf_op jit(solution)/shard_map/ppermute | solution.py:16
  144.8 104.6 %collective-permute-start.11 = (bf16[2,512,512]{2,1,0:T(8,128)(2,1)}, bf16[2,512,512]{2,1,0:T(8,128)(2,1)}, u32[]{:S(2)}, u32[]{:S(2)}) collective-permute-start(bf16[2,512,512]{2,1,0:T(8,128)(2,1)} %collective-permute-done.8.refs_3_.refs_4_), channel_id=1, source_target_pairs={{0,2},{2,0},{4,6},{6,4},{8,10},{10,8},{12,14},{14,12},{1,3},{3,1},... | collective-permute-start | bytes 3145736 | tf_op jit(solution)/shard_map/ppermute | solution.py:16
  147.3 102.2 %collective-permute-start.13 = (bf16[2,512,512]{2,1,0:T(8,128)(2,1)}, bf16[2,512,512]{2,1,0:T(8,128)(2,1)}, u32[]{:S(2)}, u32[]{:S(2)}) collective-permute-start(bf16[2,512,512]{2,1,0:T(8,128)(2,1)} %collective-permute-done.12.refs_5_.refs_2_), channel_id=1, source_target_pairs={{0,2},{2,0},{4,6},{6,4},{8,10},{10,8},{12,14},{14,12},{1,3},{3,1},... | collective-permute-start | bytes 3145736 | tf_op jit(solution)/shard_map/ppermute | solution.py:16
  167.0 82.4 %collective-permute-start.10 = (bf16[2,512,512]{2,1,0:T(8,128)(2,1)}, bf16[2,512,512]{2,1,0:T(8,128)(2,1)}, u32[]{:S(2)}, u32[]{:S(2)}) collective-permute-start(bf16[2,512,512]{2,1,0:T(8,128)(2,1)} %collective-permute-done.9.refs_6_.refs_2_), channel_id=1, source_target_pairs={{0,2},{2,0},{4,6},{6,4},{8,10},{10,8},{12,14},{14,12},{1,3},{3,1},... | collective-permute-start | bytes 3145736 | tf_op jit(solution)/shard_map/ppermute | solution.py:16
  236.1 114.4 %collective-permute-start.7 = (bf16[2,1024,512]{2,1,0:T(8,128)(2,1)}, bf16[2,1024,512]{2,1,0:T(8,128)(2,1)}, u32[]{:S(2)}, u32[]{:S(2)}) collective-permute-start(bf16[2,1024,512]{2,1,0:T(8,128)(2,1)} %shard_map.106), channel_id=1, source_target_pairs={{0,1},{1,0},{2,3},{3,2},{4,5},{5,4},{6,7},{7,6},{8,9},{9,8},{10,11... | collective-permute-start | bytes 6291464 | tf_op jit(solution)/shard_map/ppermute | solution.py:16
  236.2 1.2 copy-start.1
  237.4 1.2 copy-start.7
  314.8 12.0 %copy-start.3 = (bf16[2,512,512]{2,1,0:T(8,128)(2,1)S(1)}, bf16[2,512,512]{2,1,0:T(8,128)(2,1)}, u32[]{:S(2)}) copy-start(bf16[2,512,512]{2,1,0:T(8,128)(2,1)} %copy-done.2) | copy-start | bytes 3145732
  314.8 45.1 %collective-permute-start.15 = (bf16[2,1024,512]{2,1,0:T(8,128)(2,1)}, bf16[2,1024,512]{2,1,0:T(8,128)(2,1)}, u32[]{:S(2)}, u32[]{:S(2)}) collective-permute-start(bf16[2,1024,512]{2,1,0:T(8,128)(2,1)} %shard_map.110), channel_id=1, source_target_pairs={{0,1},{1,0},{2,3},{3,2},{4,5},{5,4},{6,7},{7,6},{8,9},{9,8},{10,11... | collective-permute-start | bytes 6291464 | tf_op jit(solution)/shard_map/ppermute | solution.py:16
  338.5 12.0 %copy-start.8 = (bf16[2,1024,512]{2,1,0:T(8,128)(2,1)S(1)}, bf16[2,1024,512]{2,1,0:T(8,128)(2,1)}, u32[]{:S(2)}) copy-start(bf16[2,1024,512]{2,1,0:T(8,128)(2,1)} %shard_map.106) | copy-start | bytes 6291460
  350.5 1.2 copy-start.5
  361.7 8.5 %copy-start.9 = (f32[2,512]{1,0:T(2,128)S(1)}, f32[2,512]{1,0:T(2,128)}, u32[]{:S(2)}) copy-start(f32[2,512]{1,0:T(2,128)} %multiply_reduce_fusion) | copy-start | bytes 12292
  361.8 45.0 %copy-start.10 = (s32[16]{0:T(128)S(1)}, s32[16]{0:T(128)}, u32[]{:S(2)}) copy-start(s32[16]{0:T(128)} %param.11) | copy-start | bytes 196

commit v2 on v1

v2 whole, which is shorter than its diff:
```python
import functools
import math

import jax
import jax.numpy as jnp
from jax import lax
from jax.experimental import pallas as pl
from jax.experimental.pallas import tpu as pltpu
from jax.sharding import PartitionSpec as P

VMEM_LIMIT = 48 * 1024 * 1024


def swap(value, axis, mask):
    size = math.prod(lax.axis_size(name) for name in (axis if isinstance(axis, tuple) else (axis,)))
    return lax.ppermute(value, axis, [(source, source ^ mask) for source in range(size)])


def after(value, *others):
    return lax.optimization_barrier((value, *others))[0]


def sum_all(value):
    axes = ("row", "col")
    size = lax.axis_size("row") * lax.axis_size("col")
    if size > 16 or size & (size - 1):
        return lax.psum(value, axes)
    mask = 1
    while mask < size:
        near = value + swap(value, axes, mask)
        if 2 * mask < size:
            near = near + (swap(value, axes, 2 * mask) + swap(value, axes, 3 * mask))
        value, mask = near, 4 * mask
    return value


def field_tile(r_refs, w_refs, re, im):
    for r_ref, w_ref in zip(r_refs, w_refs):
        rows_re, rows_im = r_ref[0, 0], r_ref[0, 1]
        w_re, w_im = w_ref[0, 0], w_ref[0, 1]
        dot = functools.partial(jnp.dot, preferred_element_type=jnp.float32)
        re = dot(rows_re, w_re) if re is None else re + dot(rows_re, w_re)
        re = re + dot(rows_im, -w_im)
        im = dot(rows_re, w_im) if im is None else im + dot(rows_re, w_im)
        im = im + dot(rows_im, w_re)
    return re, im


def field_kernel(count, has_total, ids, *refs):
    r_refs, w_refs = refs[:count], refs[count : 2 * count]
    out = refs[-1]
    re, im = (refs[2 * count][0], refs[2 * count][1]) if has_total else (None, None)
    re, im = field_tile(r_refs, w_refs, re, im)
    out[0] = re
    out[1] = im


def numer_kernel(count, late, ids, *refs):
    r_refs, w_refs = refs[:count], refs[count : 2 * count]
    total, mine, other = refs[2 * count : 2 * count + 3]
    late_refs = refs[2 * count + 3 : 2 * count + 3 + late]
    out, rows, sem = refs[-3:]
    step = pl.program_id(0)
    tile = rows.shape[2]
    slots = rows.shape[0]

    @pl.when(step == 0)
    def _():
        out[...] = jnp.zeros_like(out)
        for slot in range(slots):
            view = [ref.at[0, :, pl.ds(slot * tile, tile)] for ref in (mine, other)]
            view += [ref.at[0] for ref in late_refs]
            for k, source in enumerate(view):

                @pl.when(ids[count + slot] == k)
                def _(source=source, slot=slot):
                    pltpu.make_async_copy(source, rows.at[slot], sem.at[slot]).start()

    re, im = field_tile(r_refs, w_refs, total[0], total[1])
    for slot in range(slots):

        @pl.when(step == slot)
        def _(slot=slot):
            source = mine.at[0, :, pl.ds(slot * tile, tile)]
            pltpu.make_async_copy(source, rows.at[slot], sem.at[slot]).wait()

    product = rows[step, 0].astype(jnp.float32) * re + rows[step, 1].astype(jnp.float32) * im
    out[...] += jnp.sum(product.reshape(-1, 8, product.shape[-1]), axis=0)


def operand_specs(freq, tile, pieces):
    width, sources = pieces[0].shape[2:]
    specs = [
        pl.BlockSpec((1, 2, tile, width), lambda i, ids, k=k: (freq, 0, i, ids[k]))
        for k in range(len(pieces))
    ]
    for piece in pieces:
        which = freq if piece.shape[0] > 1 else 0
        specs.append(
            pl.BlockSpec((1, 2, width, sources), lambda i, ids, which=which: (which, 0, 0, 0))
        )
    return specs


def cost(rows, pieces, extra):
    width, sources = pieces[0].shape[2:]
    count = len(pieces)
    return pl.CostEstimate(
        flops=8 * count * rows * width * sources,
        bytes_accessed=count * (4 * rows * width + 4 * width * sources) + extra,
        transcendentals=0,
    )


def add_field(cross, freq, ids, pieces, total=None):
    rows, (tile, sources) = cross.shape[2], pieces[0].shape[2:]
    block = pl.BlockSpec((2, tile, sources), lambda i, ids: (0, i, 0))
    specs = operand_specs(freq, tile, pieces)
    args = [cross] * len(pieces) + list(pieces)
    if total is not None:
        specs, args = specs + [block], args + [total]
    return pl.pallas_call(
        functools.partial(field_kernel, len(pieces), total is not None),
        out_shape=jax.ShapeDtypeStruct((2, rows, sources), jnp.float32),
        grid_spec=pltpu.PrefetchScalarGridSpec(
            num_scalar_prefetch=1, grid=(rows // tile,), in_specs=specs, out_specs=block
        ),
        compiler_params=pltpu.CompilerParams(vmem_limit_bytes=VMEM_LIMIT),
        cost_estimate=cost(rows, pieces, 8 * rows * sources),
    )(ids, *args)


def finish(cross, freq, ids, pieces, total, mine, other, late):
    rows, (tile, sources) = cross.shape[2], pieces[0].shape[2:]
    block = pl.BlockSpec((2, tile, sources), lambda i, ids: (0, i, 0))
    anywhere = pl.BlockSpec(memory_space=pl.ANY)
    specs = operand_specs(freq, tile, pieces) + [block] + [anywhere] * (2 + len(late))
    args = [cross] * len(pieces) + list(pieces) + [total, mine, other, *late]
    out = pl.pallas_call(
        functools.partial(numer_kernel, len(pieces), len(late)),
        out_shape=jax.ShapeDtypeStruct((8, sources), jnp.float32),
        grid_spec=pltpu.PrefetchScalarGridSpec(
            num_scalar_prefetch=1,
            grid=(rows // tile,),
            in_specs=specs,
            out_specs=pl.BlockSpec((8, sources), lambda i, ids: (0, 0)),
            scratch_shapes=[
                pltpu.VMEM((rows // tile, 2, tile, sources), mine.dtype),
                pltpu.SemaphoreType.DMA((rows // tile,)),
            ],
        ),
        compiler_params=pltpu.CompilerParams(vmem_limit_bytes=VMEM_LIMIT),
        cost_estimate=cost(rows, pieces, 12 * rows * sources),
    )(ids, *args)
    return jnp.sum(out, axis=0)


def pick_kernel(freq, ids, *refs):
    pieces, out, sem = refs[:-2], refs[-2], refs[-1]
    width = pieces[0].shape[2]
    for slot in range(2):
        for k, piece in enumerate(pieces):

            @pl.when(ids[slot] == k)
            def _(slot=slot, piece=piece):
                source = piece.at[freq if piece.shape[0] > 1 else 0]
                pltpu.make_async_copy(
                    source, out.at[0, :, pl.ds(slot * width, width)], sem.at[slot]
                ).start()

    for slot in range(2):

        @pl.when(ids[slot] < len(pieces))
        def _(slot=slot):
            pltpu.make_async_copy(
                pieces[0].at[0], out.at[0, :, pl.ds(slot * width, width)], sem.at[slot]
            ).wait()


def pick_rows(freq, ids, pieces):
    _, _, width, sources = pieces[0].shape
    return pl.pallas_call(
        functools.partial(pick_kernel, freq),
        out_shape=jax.ShapeDtypeStruct((1, 2, 2 * width, sources), pieces[0].dtype),
        grid_spec=pltpu.PrefetchScalarGridSpec(
            num_scalar_prefetch=1,
            grid=(1,),
            in_specs=[pl.BlockSpec(memory_space=pl.ANY)] * len(pieces),
            out_specs=pl.BlockSpec((1, 2, 2 * width, sources), lambda i, ids: (0, 0, 0, 0)),
            scratch_shapes=[pltpu.SemaphoreType.DMA((2,))],
        ),
        cost_estimate=pl.CostEstimate(
            flops=0, bytes_accessed=16 * width * sources, transcendentals=0
        ),
    )(ids, *pieces)


def numer_by_swaps(cross, replicas, norms):
    rows, half = cross.shape[2], cross.shape[3]
    width = replicas.shape[3]
    me = lax.axis_index("row").astype(jnp.int32)
    col = lax.axis_index("col").astype(jnp.int32)
    holder = me * rows // half
    first = (me * rows - holder * half) // width
    masks = jnp.stack([first ^ me, (first + 1) ^ me])
    ids = lambda *wanted: me ^ jnp.array(wanted, jnp.int32)

    own = replicas[:, :, 0]
    own_a, own_b = own[0:1], own[1:2]
    x = swap(own, "row", 1)
    pa = swap(own_a, "row", 4)
    na = swap(own_a, "row", 2)
    pb = swap(after(own_b, pa), "row", 4)
    ga = swap(pa, "row", 2)
    xpa = swap(pa, "row", 1)
    xna = swap(na, "row", 1)
    a0 = add_field(cross, 0, ids(0, 1, 2, 4), [own, x, na, pa])
    a1 = add_field(cross, 1, ids(0, 1), [own, x])
    gb = swap(pb, "row", 2)
    xga = swap(after(ga, a0, norms), "row", 1)
    xpb = swap(after(pb, a1), "row", 1)
    nb = swap(after(own_b, ga), "row", 2)
    b0 = add_field(cross, 0, ids(3, 5, 6), [xna, xpa, ga], a0)
    d = swap(after(x[1:2], gb), "row", 2)
    xgb = swap(after(gb, b0), "row", 1)
    b1 = add_field(cross, 1, ids(4, 6, 5, 2), [pb, gb, xpb, nb], a1)

    holds = holder == col
    mine_a = pick_rows(0, masks, [own, x, na, xna, pa, xpa, ga, xga])
    other_a = swap(mine_a, "col", 1)
    where_a = jnp.where(holds, 0, 1) * jnp.ones_like(masks)
    c0 = finish(cross, 0, jnp.concatenate([ids(7), where_a]), [xga], b0, mine_a, other_a, [])

    order = jnp.where(masks == 3, 7, masks - (masks > 3))
    mine_b = pick_rows(1, order, [own, x, nb, pb, xpb, gb])
    other_b = swap(mine_b, "col", 1)
    late = [xgb, d]
    late = late + [swap(after(piece, b1, c0), "col", 1) for piece in late]
    where_b = jnp.where(masks == 7, jnp.where(holds, 2, 4), where_a)
    where_b = jnp.where(masks == 3, jnp.where(holds, 3, 5), where_b)
    c1 = finish(
        cross, 1, jnp.concatenate([ids(3, 7), where_b]), [d, xgb], b1, mine_b, other_b, late
    )
    return jnp.stack([c0, c1])


def numer_by_gather(cross, replicas, norms):
    rows, half = cross.shape[2], cross.shape[3]
    row_index, col_index = lax.axis_index("row"), lax.axis_index("col")
    first_row = row_index * rows
    holder = first_row // half
    whole = lax.all_gather(replicas, "row", axis=3, tiled=True)[:, :, 0]
    parts = jnp.einsum("fark,fbks->fabrs", cross, whole, preferred_element_type=jnp.float32)
    field = jnp.stack([parts[:, 0, 0] - parts[:, 1, 1], parts[:, 0, 1] + parts[:, 1, 0]], axis=1)
    own_rows = lax.dynamic_slice_in_dim(whole, first_row - holder * half, rows, 2)
    block_rows = jnp.where(holder == col_index, own_rows, swap(own_rows, "col", 1))
    return jnp.sum(block_rows.astype(jnp.float32) * field, axis=(1, 2))


def body(cross_spectra, replicas, tile_order):
    fnum = cross_spectra.shape[0]
    sources = replicas.shape[4]
    own = replicas[:, :, 0].astype(jnp.float32)
    norms = sum_all(jnp.sum(own * own, axis=(1, 2)))
    doubling = (
        lax.axis_size("row") == 8
        and replicas.shape[3] % 128 == 0
        and cross_spectra.shape[2] == 2 * replicas.shape[3]
    )
    numer = (numer_by_swaps if doubling else numer_by_gather)(cross_spectra, replicas, norms)
    beam = sum_all(numer) / (norms + 1e-06)
    width = sources // lax.axis_size("col")
    beam_half = lax.dynamic_slice_in_dim(beam, lax.axis_index("col") * width, width, 1)
    peak = jnp.max(jnp.abs(beam), axis=1) + 1e-06
    count = tile_order.shape[0]
    picker = (tile_order[:, None] == jnp.arange(count, dtype=jnp.int32)[None, :]).astype(jnp.float32)
    tiles = beam.reshape(fnum, count, sources // count)
    refined = (
        jnp.einsum("tu,fup->ftp", picker, tiles, precision=lax.Precision.HIGHEST)
        / peak[:, None, None]
    )
    return (beam_half, refined)


def solution(mesh):
    in_specs = (P("groups", None, "row", "col"), P("groups", None, "col", "row", None), P("groups"))
    out_specs = (P("groups", "col"), P("groups", None, None))
    return jax.shard_map(body, mesh=mesh, in_specs=in_specs, out_specs=out_specs, check_vma=False)
```

time: 408 us -> 224 us (0.55)
  Pallas kernels: 193 us -> 70.9 us
  starting transfers between devices: 84.1 us -> 30.3 us
  blocking collectives: 35.6 us -> 0 us
  waiting for transfers between devices: 80.7 us -> 110 us
    pallas_call x4, Pallas kernels: 147 us -> 21.3 us  [the longest x2 13.9 us: finish(): pl.pallas_call(functools.partial(numer_kernel, len(pieces), len(late)), o...]
    ppermute x16 -> x29, starting transfers between devices: 84.1 us -> 30.3 us  [swap(): lax.ppermute(value, axis, [(source, source ^ mask) for source in range(si...]
    psum x1 -> x0, blocking collectives: 35.6 us -> none  [body(): sums = lax.psum(jnp.stack([numer_part, norm_part]), ('row', 'col'))]
    ppermute x16 -> x29, waiting for transfers between devices: 80.7 us -> 110 us  [swap(): lax.ppermute(value, axis, [(source, source ^ mask) for source in range(si...]
    slice x0 -> x2, local copies, waits for them, and re-layouts: none -> 5.44 us  [the longest x1 3.17 us: numer_by_swaps(): own_a, own_b = (own[0:1], own[1:2])]
  transfers between devices with their start and end apart: 16 -> 29, of which waited for: 6 -> 16; matrix products, arithmetic and copies ran while one was open for 1% -> 3% of each run, Pallas kernels for 45% -> 28%
where the time goes in v2:
time: 224 us
  waiting for transfers between devices  110 us (49%)
  Pallas kernels  70.9 us (32%)
  starting transfers between devices  30.3 us (14%)
  local copies, waits for them, and re-layouts  8.41 us (4%)
    ppermute x29, waiting for transfers between devices, swap(): lax.ppermute(value, axis, [(source, source ^ mask) for source in range(si...  110 us
    pallas_call x4, Pallas kernels, add_field(): pl.pallas_call(functools.partial(field_kernel, len(pieces), total is not...  49.6 us
    ppermute x29, starting transfers between devices, swap(): lax.ppermute(value, axis, [(source, source ^ mask) for source in range(si...  30.3 us
    pallas_call x2, Pallas kernels, finish(): pl.pallas_call(functools.partial(numer_kernel, len(pieces), len(late)), o...  13.9 us
    pallas_call x2, Pallas kernels, pick_rows(): pl.pallas_call(functools.partial(pick_kernel, freq), out_shape=jax.ShapeD...  7.41 us
  transfers between devices with their start and end apart: 29, of which 16 were waited for; matrix products, arithmetic and copies ran while one was open for 3% of the time, Pallas kernels for 28%

profile of v2, /device:TPU:0, one launch (start us, length us, event | category | flops | bytes accessed | tf_op | source)
XLA Modules:
  0.0 223.8 jit_solution(17689077087602437136)
XLA Ops:
  0.6 3.0 %collective-permute-start.2 = (bf16[2,2,512,512]{3,2,1,0:T(8,128)(2,1)}, bf16[2,2,512,512]{3,2,1,0:T(8,128)(2,1)}, u32[]{:S(2)}, u32[]{:S(2)}) collective-permute-start(bf16[2,2,512,512]{3,2,1,0:T(8,128)(2,1)} %bitcast.19), channel_id=1, source_target_pairs={{0,2},{2,0},{4,6},{6,4},{8,10},{10,8},{12,14},{14,12},{1,3},{3,1},... | collective-permute-start | bytes 6291464 | tf_op jit(solution)/shard_map/ppermute | solution.py:16
  3.6 3.2 %slice_bitcast_fusion.1 = (bf16[1,2,512,512]{3,2,1,0:T(8,128)(2,1)}, bf16[1,2,512,512]{3,2,1,0:T(8,128)(2,1)}) fusion(bf16[2,2,1,512,512]{4,3,1,2,0:T(8,128)(2,1)} %bitcast.20), kind=kLoop, calls=%fused_computation.4 | loop fusion | bytes 4194304 | tf_op jit(solution)/shard_map/slice | solution.py:209
  6.8 2.6 %collective-permute-start = (bf16[1,2,512,512]{3,2,1,0:T(8,128)(2,1)}, bf16[1,2,512,512]{3,2,1,0:T(8,128)(2,1)S(1)}, u32[]{:S(2)}, u32[]{:S(2)}) collective-permute-start(bf16[1,2,512,512]{3,2,1,0:T(8,128)(2,1)} %get-tuple-element.22), channel_id=1, source_target_pairs={{0,8},{2,10},{4,12},{6,14},{8,0},{10,2},{12,4},{14,6},{1,9},{3,11}... | collective-permute-start | bytes 3145736 | tf_op jit(solution)/shard_map/ppermute | solution.py:16
  9.4 1.6 collective-permute-start.3
  11.5 0.6 collective-permute-start.5
  12.1 0.6 collective-permute-done.4
  12.7 0.7 collective-permute-start.6
  13.4 36.3 %collective-permute-done.5 = f32[2,512]{1,0:T(2,128)S(1)} collective-permute-done((f32[2,512]{1,0:T(2,128)S(1)}, f32[2,512]{1,0:T(2,128)S(1)}, u32[]{:S(2)}, u32[]{:S(2)}) %collective-permute-start.5) | collective-permute-done | bytes 4128 | tf_op jit(solution)/shard_map/ppermute | solution.py:16
  49.7 1.9 collective-permute-start.7
  51.6 2.6 %collective-permute-start.8 = (f32[2,512]{1,0:T(2,128)S(1)}, f32[2,512]{1,0:T(2,128)S(1)}, u32[]{:S(2)}, u32[]{:S(2)}) collective-permute-start(f32[2,512]{1,0:T(2,128)S(1)} %add_add_fusion.2), channel_id=1, source_target_pairs={{0,8},{1,9},{2,10},{3,11},{4,12},{5,13},{6,14},{7,15},{8,0},{9,1},... | collective-permute-start | bytes 12296 | tf_op jit(solution)/shard_map/ppermute | solution.py:16
  54.2 1.3 collective-permute-done.7
  55.5 2.0 collective-permute-start.9
  57.6 3.4 %collective-permute-done.9 = f32[2,512]{1,0:T(2,128)S(1)} collective-permute-done((f32[2,512]{1,0:T(2,128)S(1)}, f32[2,512]{1,0:T(2,128)S(1)}, u32[]{:S(2)}, u32[]{:S(2)}) %collective-permute-start.9) | collective-permute-done | bytes 4128 | tf_op jit(solution)/shard_map/ppermute | solution.py:16
  61.0 0.6 add_add_fusion.1
  62.1 1.6 collective-permute-start.11
  63.6 13.8 %shard_map.104.refs_6_ = f32[2,1024,512]{2,1,0:T(8,128)} custom-call(s32[4]{0:T(128)S(1)} %broadcast_xor_fusion.3.ids, bf16[2,2,1024,4096]{3,2,1,0:T(8,128)(2,1)} %refs_1_.9, bf16[2,2,1024,4096]{3,2,1,0:T(8,128)(2,1)} %refs_1_.9, bf16[2,2,1024,4096]{3,2,1,0:T(8,128)(2,1)} %refs_1_.9, bf16[2,2,1024,4096]{3,2,1,0:T(8,128)(2,1)} %refs_1_.9, ...), custom_call_target="tpu_custom_call" | custom-call | flops 8589934592 | bytes 16777216 | tf_op jit(solution)/shard_map/pallas_call | solution.py:122
  77.5 22.7 %collective-permute-done.1.refs_5_.refs_6_ = bf16[1,2,512,512]{3,2,1,0:T(8,128)(2,1)} collective-permute-done((bf16[1,2,512,512]{3,2,1,0:T(8,128)(2,1)S(1)}, bf16[1,2,512,512]{3,2,1,0:T(8,128)(2,1)}, u32[]{:S(2)}, u32[]{:S(2)}) %collective-permute-start.1) | collective-permute-done | bytes 1048608 | tf_op jit(solution)/shard_map/ppermute | solution.py:16
  100.2 1.6 collective-permute-start.10
  101.7 0.7 compare_select_fusion.1
  102.4 6.9 %collective-permute-done.14.refs_4_.refs_3_ = bf16[1,2,512,512]{3,2,1,0:T(8,128)(2,1)} collective-permute-done((bf16[1,2,512,512]{3,2,1,0:T(8,128)(2,1)}, bf16[1,2,512,512]{3,2,1,0:T(8,128)(2,1)}, u32[]{:S(2)}, u32[]{:S(2)}) %collective-permute-start.14) | collective-permute-done | bytes 1048608 | tf_op jit(solution)/shard_map/ppermute | solution.py:16
  109.3 1.0 collective-permute-done.11.refs_3_
  110.3 20.2 %collective-permute-done.10.refs_7_.refs_1_ = bf16[1,2,512,512]{3,2,1,0:T(8,128)(2,1)S(1)} collective-permute-done((bf16[1,2,512,512]{3,2,1,0:T(8,128)(2,1)}, bf16[1,2,512,512]{3,2,1,0:T(8,128)(2,1)S(1)}, u32[]{:S(2)}, u32[]{:S(2)}) %collective-permute-start.10) | collective-permute-done | bytes 1048608 | tf_op jit(solution)/shard_map/ppermute | solution.py:16
  130.5 1.0 copy-done.6
  131.5 3.7 %shard_map.106.refs_3_ = bf16[1,2,1024,512]{3,2,1,0:T(8,128)(2,1)} custom-call(s32[2]{0:T(128)} %get-tuple-element.21.ids, bf16[2,2,512,512]{3,2,1,0:T(8,128)(2,1)} %bitcast.21, bf16[2,2,512,512]{3,2,1,0:T(8,128)(2,1)} %collective-permute-done.2.refs_5_.refs_1_.refs_3_, bf16[1,2,512,512]{3,2,1,0:T(8,128)(2,1)} %collective-permute-done.3.refs_6_.refs_2_, ...), custom_call_target="tpu_custom_call" | custom-call | bytes 4194304 | tf_op jit(solution)/shard_map/pallas_call | solution.py:182
  135.3 8.5 %shard_map.108.refs_8_ = f32[2,1024,512]{2,1,0:T(8,128)} custom-call(s32[2]{0:T(128)S(1)} %iota_xor_fusion.ids, bf16[2,2,1024,4096]{3,2,1,0:T(8,128)(2,1)} %refs_1_.9, bf16[2,2,1024,4096]{3,2,1,0:T(8,128)(2,1)} %refs_1_.9, bf16[2,2,512,512]{3,2,1,0:T(8,128)(2,1)S(1)} %bitcast.24, bf16[2,2,512,512]{3,2,1,0:T(8,128)(2,1)} %collective-permute-done.2.refs_5_.refs_1_.refs_3_), custom_call_target="tpu_custom_call" | custom-call | flops 4294967296 | bytes 10485760 | tf_op jit(solution)/shard_map/pallas_call | solution.py:122
  144.1 2.8 %collective-permute-start.19 = (bf16[1,2,512,512]{3,2,1,0:T(8,128)(2,1)S(1)}, bf16[1,2,512,512]{3,2,1,0:T(8,128)(2,1)}, u32[]{:S(2)}, u32[]{:S(2)}) collective-permute-start(bf16[1,2,512,512]{3,2,1,0:T(8,128)(2,1)S(1)} %copy-done.8), channel_id=1, source_target_pairs={{0,4},{2,6},{4,0},{6,2},{8,12},{10,14},{12,8},{14,10},{1,5},{3,7},... | collective-permute-start | bytes 3145736 | tf_op jit(solution)/shard_map/ppermute | solution.py:16
  146.9 2.3 %slice.21 = bf16[1,2,512,512]{3,2,1,0:T(8,128)(2,1)} slice(bf16[2,2,512,512]{3,2,1,0:T(8,128)(2,1)} %collective-permute-done.2.refs_5_.refs_1_.refs_3_), slice={[1:2], [0:2], [0:512], [0:512]} | slice | bytes 2097152 | tf_op jit(solution)/shard_map/slice | solution.py:224
  149.2 12.3 %shard_map.105.refs_2_ = f32[2,1024,512]{2,1,0:T(8,128)} custom-call(s32[3]{0:T(128)S(1)} %broadcast_xor_fusion.1.ids, bf16[2,2,1024,4096]{3,2,1,0:T(8,128)(2,1)} %refs_1_.9, bf16[2,2,1024,4096]{3,2,1,0:T(8,128)(2,1)} %refs_1_.9, bf16[2,2,1024,4096]{3,2,1,0:T(8,128)(2,1)} %refs_1_.9, bf16[1,2,512,512]{3,2,1,0:T(8,128)(2,1)} %collective-permute-done.11.refs_3_, ...), custom_call_target="tpu_custom_call" | custom-call | flops 6442450944 | bytes 13631488 | tf_op jit(solution)/shard_map/pallas_call | solution.py:122
  161.5 0.9 collective-permute-start.17
  162.4 7.5 %collective-permute-done.18.refs_6_.refs_4_ = bf16[1,2,512,512]{3,2,1,0:T(8,128)(2,1)S(1)} collective-permute-done((bf16[1,2,512,512]{3,2,1,0:T(8,128)(2,1)}, bf16[1,2,512,512]{3,2,1,0:T(8,128)(2,1)S(1)}, u32[]{:S(2)}, u32[]{:S(2)}) %collective-permute-start.18) | collective-permute-done | bytes 1048608 | tf_op jit(solution)/shard_map/ppermute | solution.py:16
  169.9 1.0 collective-permute-done.19.refs_7_.refs_2_
  170.9 3.7 %shard_map.110.refs_5_ = bf16[1,2,1024,512]{3,2,1,0:T(8,128)(2,1)} custom-call(s32[2]{0:T(128)} %get-tuple-element.20.ids, bf16[2,2,512,512]{3,2,1,0:T(8,128)(2,1)} %bitcast.22, bf16[2,2,512,512]{3,2,1,0:T(8,128)(2,1)} %collective-permute-done.2.refs_5_.refs_1_.refs_3_, bf16[1,2,512,512]{3,2,1,0:T(8,128)(2,1)} %collective-permute-done.19.refs_7_.refs_2_, ...), custom_call_target="tpu_custom_call" | custom-call | bytes 4194304 | tf_op jit(solution)/shard_map/pallas_call | solution.py:182
  174.8 1.2 copy-done.5
  176.0 15.1 %shard_map.109.refs_4_ = f32[2,1024,512]{2,1,0:T(8,128)} custom-call(s32[4]{0:T(128)S(1)} %broadcast_xor_fusion.2.ids, bf16[2,2,1024,4096]{3,2,1,0:T(8,128)(2,1)} %refs_1_.9, bf16[2,2,1024,4096]{3,2,1,0:T(8,128)(2,1)} %refs_1_.9, bf16[2,2,1024,4096]{3,2,1,0:T(8,128)(2,1)} %refs_1_.9, bf16[2,2,1024,4096]{3,2,1,0:T(8,128)(2,1)} %refs_1_.9, ...), custom_call_target="tpu_custom_call" | custom-call | flops 8589934592 | bytes 16777216 | tf_op jit(solution)/shard_map/pallas_call | solution.py:122
  191.1 5.8 %shard_map.107 = f32[8,512]{1,0:T(8,128)S(1)} custom-call(s32[3]{0:T(128)S(1)} %concatenate.6.ids, bf16[2,2,1024,4096]{3,2,1,0:T(8,128)(2,1)} %refs_1_.9, bf16[1,2,512,512]{3,2,1,0:T(8,128)(2,1)S(1)} %copy-done.7, f32[2,1024,512]{2,1,0:T(8,128)} %shard_map.105.refs_2_, bf16[1,2,1024,512]{3,2,1,0:T(8,128)(2,1)S(1)} %copy-done.2, ...), custom_call_target="tpu_custom_call" | custom-call | flops 2147483648 | bytes 9437184 | tf_op jit(solution)/shard_map/pallas_call | solution.py:139
  197.7 2.7 %collective-permute-done.22.refs_10_ = bf16[1,2,512,512]{3,2,1,0:T(8,128)(2,1)S(1)} collective-permute-done((bf16[1,2,512,512]{3,2,1,0:T(8,128)(2,1)S(1)}, bf16[1,2,512,512]{3,2,1,0:T(8,128)(2,1)S(1)}, u32[]{:S(2)}, u32[]{:S(2)}) %collective-permute-start.22) | collective-permute-done | bytes 1048608 | tf_op jit(solution)/shard_map/ppermute | solution.py:16
  200.4 1.0 collective-permute-done.21.refs_9_
  201.4 8.1 %shard_map.111 = f32[8,512]{1,0:T(8,128)S(1)} custom-call(s32[4]{0:T(128)S(1)} %pad_add_fusion.1.ids, bf16[2,2,1024,4096]{3,2,1,0:T(8,128)(2,1)} %refs_1_.9, bf16[2,2,1024,4096]{3,2,1,0:T(8,128)(2,1)} %refs_1_.9, bf16[1,2,512,512]{3,2,1,0:T(8,128)(2,1)S(1)} %collective-permute-done.16.refs_2_.refs_8_, ...), custom_call_target="tpu_custom_call" | custom-call | flops 4294967296 | bytes 12582912 | tf_op jit(solution)/shard_map/pallas_call | solution.py:139
  210.0 0.8 collective-permute-start.24
  210.7 0.7 collective-permute-start.25
  211.5 2.1 collective-permute-done.24
  213.8 2.4 %collective-permute-start.26 = (f32[2,512]{1,0:T(2,128)S(1)}, f32[2,512]{1,0:T(2,128)S(1)}, u32[]{:S(2)}, u32[]{:S(2)}) collective-permute-start(f32[2,512]{1,0:T(2,128)S(1)} %add_add_fusion), channel_id=1, source_target_pairs={{0,4},{1,5},{2,6},{3,7},{4,0},{5,1},{6,2},{7,3},{8,12},{9,13},{10,... | collective-permute-start | bytes 12296 | tf_op jit(solution)/shard_map/ppermute | solution.py:16
  216.2 0.5 collective-permute-start.27
  216.7 1.9 collective-permute-start.28
  218.6 2.1 collective-permute-done.27
  220.7 1.4 collective-permute-done.28
  222.4 0.6 constant_dynamic-slice_fusion
  222.9 0.8 fusion
  (73 shorter events, 3.2 us)
Async XLA Ops:
  0.6 63.0 %collective-permute-start.2 = (bf16[2,2,512,512]{3,2,1,0:T(8,128)(2,1)}, bf16[2,2,512,512]{3,2,1,0:T(8,128)(2,1)}, u32[]{:S(2)}, u32[]{:S(2)}) collective-permute-start(bf16[2,2,512,512]{3,2,1,0:T(8,128)(2,1)} %bitcast.19), channel_id=1, source_target_pairs={{0,2},{2,0},{4,6},{6,4},{8,10},{10,8},{12,14},{14,12},{1,3},{3,1},... | collective-permute-start | bytes 6291464 | tf_op jit(solution)/shard_map/ppermute | solution.py:16
  3.6 7.3 %copy-start = (bf16[2,2,1,512,512]{4,3,2,1,0:T(8,128)(2,1)S(1)}, bf16[2,2,1,512,512]{4,3,2,1,0:T(8,128)(2,1)}, u32[]{:S(2)}) copy-start(bf16[2,2,1,512,512]{4,3,2,1,0:T(8,128)(2,1)} %param.10) | copy-start | bytes 6291460
  6.8 50.7 %copy-start.15 = (s32[4]{0:T(128)S(1)}, s32[4]{0:T(128)}, u32[]{:S(2)}) copy-start(s32[4]{0:T(128)} %constant.74.clone) | copy-start | bytes 52
  6.8 50.7 %collective-permute-start = (bf16[1,2,512,512]{3,2,1,0:T(8,128)(2,1)}, bf16[1,2,512,512]{3,2,1,0:T(8,128)(2,1)S(1)}, u32[]{:S(2)}, u32[]{:S(2)}) collective-permute-start(bf16[1,2,512,512]{3,2,1,0:T(8,128)(2,1)} %get-tuple-element.22), channel_id=1, source_target_pairs={{0,8},{2,10},{4,12},{6,14},{8,0},{10,2},{12,4},{14,6},{1,9},{3,11}... | collective-permute-start | bytes 3145736 | tf_op jit(solution)/shard_map/ppermute | solution.py:16
  9.4 52.7 %collective-permute-start.3 = (bf16[1,2,512,512]{3,2,1,0:T(8,128)(2,1)}, bf16[1,2,512,512]{3,2,1,0:T(8,128)(2,1)}, u32[]{:S(2)}, u32[]{:S(2)}) collective-permute-start(bf16[1,2,512,512]{3,2,1,0:T(8,128)(2,1)} %get-tuple-element.22), channel_id=1, source_target_pairs={{0,4},{2,6},{4,0},{6,2},{8,12},{10,14},{12,8},{14,10},{1,5},{3,7},... | collective-permute-start | bytes 3145736 | tf_op jit(solution)/shard_map/ppermute | solution.py:16
  11.4 1.2 collective-permute-start.4
  11.5 38.2 %collective-permute-start.5 = (f32[2,512]{1,0:T(2,128)S(1)}, f32[2,512]{1,0:T(2,128)S(1)}, u32[]{:S(2)}, u32[]{:S(2)}) collective-permute-start(f32[2,512]{1,0:T(2,128)S(1)} %multiply_reduce_fusion), channel_id=1, source_target_pairs={{0,2},{1,3},{2,0},{3,1},{4,6},{5,7},{6,4},{7,5},{8,10},{9,11},{10,... | collective-permute-start | bytes 12296 | tf_op jit(solution)/shard_map/ppermute | solution.py:16
  12.7 37.0 %collective-permute-start.6 = (f32[2,512]{1,0:T(2,128)S(1)}, f32[2,512]{1,0:T(2,128)S(1)}, u32[]{:S(2)}, u32[]{:S(2)}) collective-permute-start(f32[2,512]{1,0:T(2,128)S(1)} %multiply_reduce_fusion), channel_id=1, source_target_pairs={{0,3},{1,2},{2,1},{3,0},{4,7},{5,6},{6,5},{7,4},{8,11},{9,10},{10,... | collective-permute-start | bytes 12296 | tf_op jit(solution)/shard_map/ppermute | solution.py:16
  49.7 5.8 %collective-permute-start.7 = (f32[2,512]{1,0:T(2,128)S(1)}, f32[2,512]{1,0:T(2,128)S(1)}, u32[]{:S(2)}, u32[]{:S(2)}) collective-permute-start(f32[2,512]{1,0:T(2,128)S(1)} %add_add_fusion.2), channel_id=1, source_target_pairs={{0,4},{1,5},{2,6},{3,7},{4,0},{5,1},{6,2},{7,3},{8,12},{9,13},{10,... | collective-permute-start | bytes 12296 | tf_op jit(solution)/shard_map/ppermute | solution.py:16
  51.6 6.0 %collective-permute-start.8 = (f32[2,512]{1,0:T(2,128)S(1)}, f32[2,512]{1,0:T(2,128)S(1)}, u32[]{:S(2)}, u32[]{:S(2)}) collective-permute-start(f32[2,512]{1,0:T(2,128)S(1)} %add_add_fusion.2), channel_id=1, source_target_pairs={{0,8},{1,9},{2,10},{3,11},{4,12},{5,13},{6,14},{7,15},{8,0},{9,1},... | collective-permute-start | bytes 12296 | tf_op jit(solution)/shard_map/ppermute | solution.py:16
  55.5 5.5 %collective-permute-start.9 = (f32[2,512]{1,0:T(2,128)S(1)}, f32[2,512]{1,0:T(2,128)S(1)}, u32[]{:S(2)}, u32[]{:S(2)}) collective-permute-start(f32[2,512]{1,0:T(2,128)S(1)} %add_add_fusion.2), channel_id=1, source_target_pairs={{0,12},{1,13},{2,14},{3,15},{4,8},{5,9},{6,10},{7,11},{8,4},{9,5},... | collective-permute-start | bytes 12296 | tf_op jit(solution)/shard_map/ppermute | solution.py:16
  57.5 19.9 %copy-start.3 = (bf16[1,2,512,512]{3,2,1,0:T(8,128)(2,1)}, bf16[1,2,512,512]{3,2,1,0:T(8,128)(2,1)S(1)}, u32[]{:S(2)}) copy-start(bf16[1,2,512,512]{3,2,1,0:T(8,128)(2,1)S(1)} %collective-permute-done.refs_7_.refs_4_) | copy-start | bytes 3145732
  57.6 42.6 %collective-permute-start.1 = (bf16[1,2,512,512]{3,2,1,0:T(8,128)(2,1)S(1)}, bf16[1,2,512,512]{3,2,1,0:T(8,128)(2,1)}, u32[]{:S(2)}, u32[]{:S(2)}) collective-permute-start(bf16[1,2,512,512]{3,2,1,0:T(8,128)(2,1)S(1)} %collective-permute-done.refs_7_.refs_4_), channel_id=1, source_target_pairs={{0,4},{2,6},{4,0},{6,2},{8,12},{10,14},{12,8},{14,10},{1,5},{3,7},... | collective-permute-start | bytes 3145736 | tf_op jit(solution)/shard_map/ppermute | solution.py:16
  61.6 47.7 %collective-permute-start.14 = (bf16[1,2,512,512]{3,2,1,0:T(8,128)(2,1)}, bf16[1,2,512,512]{3,2,1,0:T(8,128)(2,1)}, u32[]{:S(2)}, u32[]{:S(2)}) collective-permute-start(bf16[1,2,512,512]{3,2,1,0:T(8,128)(2,1)} %get-tuple-element.15), channel_id=1, source_target_pairs={{0,8},{2,10},{4,12},{6,14},{8,0},{10,2},{12,4},{14,6},{1,9},{3,11}... | collective-permute-start | bytes 3145736 | tf_op jit(solution)/shard_map/ppermute | solution.py:16
  61.6 47.7 %collective-permute-start.12 = (bf16[1,2,512,512]{3,2,1,0:T(8,128)(2,1)S(1)}, bf16[1,2,512,512]{3,2,1,0:T(8,128)(2,1)}, u32[]{:S(2)}, u32[]{:S(2)}) collective-permute-start(bf16[1,2,512,512]{3,2,1,0:T(8,128)(2,1)S(1)} %collective-permute-done.refs_7_.refs_4_), channel_id=1, source_target_pairs={{0,2},{2,0},{4,6},{6,4},{8,10},{10,8},{12,14},{14,12},{1,3},{3,1},... | collective-permute-start | bytes 3145736 | tf_op jit(solution)/shard_map/ppermute | solution.py:16
  62.1 48.2 %collective-permute-start.11 = (bf16[1,2,512,512]{3,2,1,0:T(8,128)(2,1)}, bf16[1,2,512,512]{3,2,1,0:T(8,128)(2,1)}, u32[]{:S(2)}, u32[]{:S(2)}) collective-permute-start(bf16[1,2,512,512]{3,2,1,0:T(8,128)(2,1)} %collective-permute-done.3.refs_6_.refs_2_), channel_id=1, source_target_pairs={{0,2},{2,0},{4,6},{6,4},{8,10},{10,8},{12,14},{14,12},{1,3},{3,1},... | collective-permute-start | bytes 3145736 | tf_op jit(solution)/shard_map/ppermute | solution.py:16
  100.2 30.3 %collective-permute-start.10 = (bf16[1,2,512,512]{3,2,1,0:T(8,128)(2,1)}, bf16[1,2,512,512]{3,2,1,0:T(8,128)(2,1)S(1)}, u32[]{:S(2)}, u32[]{:S(2)}) collective-permute-start(bf16[1,2,512,512]{3,2,1,0:T(8,128)(2,1)} %collective-permute-done.1.refs_5_.refs_6_), channel_id=1, source_target_pairs={{0,2},{2,0},{4,6},{6,4},{8,10},{10,8},{12,14},{14,12},{1,3},{3,1},... | collective-permute-start | bytes 3145736 | tf_op jit(solution)/shard_map/ppermute | solution.py:16
  109.3 52.1 %collective-permute-start.15 = (bf16[1,2,512,512]{3,2,1,0:T(8,128)(2,1)}, bf16[1,2,512,512]{3,2,1,0:T(8,128)(2,1)}, u32[]{:S(2)}, u32[]{:S(2)}) collective-permute-start(bf16[1,2,512,512]{3,2,1,0:T(8,128)(2,1)} %collective-permute-done.14.refs_4_.refs_3_), channel_id=1, source_target_pairs={{0,4},{2,6},{4,0},{6,2},{8,12},{10,14},{12,8},{14,10},{1,5},{3,7},... | collective-permute-start | bytes 3145736 | tf_op jit(solution)/shard_map/ppermute | solution.py:16
  130.5 1.0 copy-start.6
  131.5 3.8 %copy-start.1 = (bf16[2,2,1,512,512]{4,3,2,1,0:T(8,128)(2,1)S(1)}, bf16[2,2,1,512,512]{4,3,2,1,0:T(8,128)(2,1)}, u32[]{:S(2)}) copy-start(bf16[2,2,1,512,512]{4,3,2,1,0:T(8,128)(2,1)} %param.10) | copy-start | bytes 6291460
  135.2 8.9 %copy-start.8 = (bf16[1,2,512,512]{3,2,1,0:T(8,128)(2,1)S(1)}, bf16[1,2,512,512]{3,2,1,0:T(8,128)(2,1)}, u32[]{:S(2)}) copy-start(bf16[1,2,512,512]{3,2,1,0:T(8,128)(2,1)} %get-tuple-element.15) | copy-start | bytes 3145732
  135.2 11.7 %copy-start.14 = (s32[3]{0:T(128)S(1)}, s32[3]{0:T(128)}, u32[]{:S(2)}) copy-start(s32[3]{0:T(128)} %constant.75.clone) | copy-start | bytes 40
  135.2 55.9 %collective-permute-start.13 = (bf16[1,2,1024,512]{3,2,1,0:T(8,128)(2,1)}, bf16[1,2,1024,512]{3,2,1,0:T(8,128)(2,1)}, u32[]{:S(2)}, u32[]{:S(2)}) collective-permute-start(bf16[1,2,1024,512]{3,2,1,0:T(8,128)(2,1)} %shard_map.106.refs_3_), channel_id=1, source_target_pairs={{0,1},{1,0},{2,3},{3,2},{4,5},{5,4},{6,7},{7,6},{8,9},{9,8},{10,11... | collective-permute-start | bytes 6291464 | tf_op jit(solution)/shard_map/ppermute | solution.py:16
  143.8 26.2 %collective-permute-start.18 = (bf16[1,2,512,512]{3,2,1,0:T(8,128)(2,1)}, bf16[1,2,512,512]{3,2,1,0:T(8,128)(2,1)S(1)}, u32[]{:S(2)}, u32[]{:S(2)}) collective-permute-start(bf16[1,2,512,512]{3,2,1,0:T(8,128)(2,1)} %collective-permute-done.14.refs_4_.refs_3_), channel_id=1, source_target_pairs={{0,2},{2,0},{4,6},{6,4},{8,10},{10,8},{12,14},{14,12},{1,3},{3,1},... | collective-permute-start | bytes 3145736 | tf_op jit(solution)/shard_map/ppermute | solution.py:16
  144.1 26.8 %collective-permute-start.19 = (bf16[1,2,512,512]{3,2,1,0:T(8,128)(2,1)S(1)}, bf16[1,2,512,512]{3,2,1,0:T(8,128)(2,1)}, u32[]{:S(2)}, u32[]{:S(2)}) collective-permute-start(bf16[1,2,512,512]{3,2,1,0:T(8,128)(2,1)S(1)} %copy-done.8), channel_id=1, source_target_pairs={{0,4},{2,6},{4,0},{6,2},{8,12},{10,14},{12,8},{14,10},{1,5},{3,7},... | collective-permute-start | bytes 3145736 | tf_op jit(solution)/shard_map/ppermute | solution.py:16
  161.4 35.5 %collective-permute-start.16 = (bf16[1,2,512,512]{3,2,1,0:T(8,128)(2,1)}, bf16[1,2,512,512]{3,2,1,0:T(8,128)(2,1)S(1)}, u32[]{:S(2)}, u32[]{:S(2)}) collective-permute-start(bf16[1,2,512,512]{3,2,1,0:T(8,128)(2,1)} %slice.21), channel_id=1, source_target_pairs={{0,4},{2,6},{4,0},{6,2},{8,12},{10,14},{12,8},{14,10},{1,5},{3,7},... | collective-permute-start | bytes 3145736 | tf_op jit(solution)/shard_map/ppermute | solution.py:16
  161.5 36.0 %collective-permute-start.17 = (bf16[1,2,512,512]{3,2,1,0:T(8,128)(2,1)}, bf16[1,2,512,512]{3,2,1,0:T(8,128)(2,1)S(1)}, u32[]{:S(2)}, u32[]{:S(2)}) collective-permute-start(bf16[1,2,512,512]{3,2,1,0:T(8,128)(2,1)} %collective-permute-done.15.refs_5_), channel_id=1, source_target_pairs={{0,2},{2,0},{4,6},{6,4},{8,10},{10,8},{12,14},{14,12},{1,3},{3,1},... | collective-permute-start | bytes 3145736 | tf_op jit(solution)/shard_map/ppermute | solution.py:16
  169.9 1.0 copy-start.4
  170.9 3.8 %copy-start.13 = (s32[4]{0:T(128)S(1)}, s32[4]{0:T(128)}, u32[]{:S(2)}) copy-start(s32[4]{0:T(128)} %constant.76.clone) | copy-start | bytes 52
  174.7 23.0 %collective-permute-start.20 = (bf16[1,2,1024,512]{3,2,1,0:T(8,128)(2,1)}, bf16[1,2,1024,512]{3,2,1,0:T(8,128)(2,1)}, u32[]{:S(2)}, u32[]{:S(2)}) collective-permute-start(bf16[1,2,1024,512]{3,2,1,0:T(8,128)(2,1)} %shard_map.110.refs_5_), channel_id=1, source_target_pairs={{0,1},{1,0},{2,3},{3,2},{4,5},{5,4},{6,7},{7,6},{8,9},{9,8},{10,11... | collective-permute-start | bytes 6291464 | tf_op jit(solution)/shard_map/ppermute | solution.py:16
  174.8 1.2 copy-start.5
  176.0 15.1 %copy-start.2 = (bf16[1,2,1024,512]{3,2,1,0:T(8,128)(2,1)S(1)}, bf16[1,2,1024,512]{3,2,1,0:T(8,128)(2,1)}, u32[]{:S(2)}) copy-start(bf16[1,2,1024,512]{3,2,1,0:T(8,128)(2,1)} %shard_map.106.refs_3_) | copy-start | bytes 6291460
  176.0 15.1 %copy-start.7 = (bf16[1,2,512,512]{3,2,1,0:T(8,128)(2,1)S(1)}, bf16[1,2,512,512]{3,2,1,0:T(8,128)(2,1)}, u32[]{:S(2)}) copy-start(bf16[1,2,512,512]{3,2,1,0:T(8,128)(2,1)} %copy-done.6) | copy-start | bytes 3145732
  191.1 6.5 %copy-start.12 = (s32[2]{0:T(128)S(1)}, s32[2]{0:T(128)}, u32[]{:S(2)}) copy-start(s32[2]{0:T(128)} %constant.78.clone) | copy-start | bytes 28
  191.1 6.5 %copy-start.10 = (s32[2]{0:T(128)S(1)}, s32[2]{0:T(128)}, u32[]{:S(2)}) copy-start(s32[2]{0:T(128)} %get-tuple-element.21.ids) | copy-start | bytes 28
  197.0 3.4 %collective-permute-start.22 = (bf16[1,2,512,512]{3,2,1,0:T(8,128)(2,1)S(1)}, bf16[1,2,512,512]{3,2,1,0:T(8,128)(2,1)S(1)}, u32[]{:S(2)}, u32[]{:S(2)}) collective-permute-start(bf16[1,2,512,512]{3,2,1,0:T(8,128)(2,1)S(1)} %collective-permute-done.16.refs_2_.refs_8_), channel_id=1, source_target_pairs={{0,1},{1,0},{2,3},{3,2},{4,5},{5,4},{6,7},{7,6},{8,9},{9,8},{10,11... | collective-permute-start | bytes 3145736 | tf_op jit(solution)/shard_map/ppermute | solution.py:16
  197.5 3.9 %collective-permute-start.21 = (bf16[1,2,512,512]{3,2,1,0:T(8,128)(2,1)S(1)}, bf16[1,2,512,512]{3,2,1,0:T(8,128)(2,1)}, u32[]{:S(2)}, u32[]{:S(2)}) collective-permute-start(bf16[1,2,512,512]{3,2,1,0:T(8,128)(2,1)S(1)} %collective-permute-done.17.refs_3_.refs_7_), channel_id=1, source_target_pairs={{0,1},{1,0},{2,3},{3,2},{4,5},{5,4},{6,7},{7,6},{8,9},{9,8},{10,11... | collective-permute-start | bytes 3145736 | tf_op jit(solution)/shard_map/ppermute | solution.py:16
  197.7 24.5 %copy-start.9 = (f32[2,512]{1,0:T(2,128)S(1)}, f32[2,512]{1,0:T(2,128)}, u32[]{:S(2)}) copy-start(f32[2,512]{1,0:T(2,128)} %add_add_fusion.1) | copy-start | bytes 12292
  197.7 25.3 %copy-start.11 = (s32[16]{0:T(128)S(1)}, s32[16]{0:T(128)}, u32[]{:S(2)}) copy-start(s32[16]{0:T(128)} %param.11) | copy-start | bytes 196
  209.5 1.9 collective-permute-start.23
  210.0 3.6 %collective-permute-start.24 = (f32[2,512]{1,0:T(2,128)S(1)}, f32[2,512]{1,0:T(2,128)S(1)}, u32[]{:S(2)}, u32[]{:S(2)}) collective-permute-start(f32[2,512]{1,0:T(2,128)S(1)} %pad_maximum_fusion), channel_id=1, source_target_pairs={{0,2},{1,3},{2,0},{3,1},{4,6},{5,7},{6,4},{7,5},{8,10},{9,11},{10,... | collective-permute-start | bytes 12296 | tf_op jit(solution)/shard_map/ppermute | solution.py:16
  210.7 3.0 %collective-permute-start.25 = (f32[2,512]{1,0:T(2,128)S(1)}, f32[2,512]{1,0:T(2,128)S(1)}, u32[]{:S(2)}, u32[]{:S(2)}) collective-permute-start(f32[2,512]{1,0:T(2,128)S(1)} %pad_maximum_fusion), channel_id=1, source_target_pairs={{0,3},{1,2},{2,1},{3,0},{4,7},{5,6},{6,5},{7,4},{8,11},{9,10},{10,... | collective-permute-start | bytes 12296 | tf_op jit(solution)/shard_map/ppermute | solution.py:16
  213.8 4.9 %collective-permute-start.26 = (f32[2,512]{1,0:T(2,128)S(1)}, f32[2,512]{1,0:T(2,128)S(1)}, u32[]{:S(2)}, u32[]{:S(2)}) collective-permute-start(f32[2,512]{1,0:T(2,128)S(1)} %add_add_fusion), channel_id=1, source_target_pairs={{0,4},{1,5},{2,6},{3,7},{4,0},{5,1},{6,2},{7,3},{8,12},{9,13},{10,... | collective-permute-start | bytes 12296 | tf_op jit(solution)/shard_map/ppermute | solution.py:16
  216.2 4.5 %collective-permute-start.27 = (f32[2,512]{1,0:T(2,128)S(1)}, f32[2,512]{1,0:T(2,128)S(1)}, u32[]{:S(2)}, u32[]{:S(2)}) collective-permute-start(f32[2,512]{1,0:T(2,128)S(1)} %add_add_fusion), channel_id=1, source_target_pairs={{0,8},{1,9},{2,10},{3,11},{4,12},{5,13},{6,14},{7,15},{8,0},{9,1},... | collective-permute-start | bytes 12296 | tf_op jit(solution)/shard_map/ppermute | solution.py:16
  216.7 5.4 %collective-permute-start.28 = (f32[2,512]{1,0:T(2,128)S(1)}, f32[2,512]{1,0:T(2,128)S(1)}, u32[]{:S(2)}, u32[]{:S(2)}) collective-permute-start(f32[2,512]{1,0:T(2,128)S(1)} %add_add_fusion), channel_id=1, source_target_pairs={{0,12},{1,13},{2,14},{3,15},{4,8},{5,9},{6,10},{7,11},{8,4},{9,5},... | collective-permute-start | bytes 12296 | tf_op jit(solution)/shard_map/ppermute | solution.py:16

commit v3 on v2

v3 whole, which is shorter than its diff:
```python
import functools
import math

import jax
import jax.numpy as jnp
from jax import lax
from jax.experimental import pallas as pl
from jax.experimental.pallas import tpu as pltpu
from jax.sharding import PartitionSpec as P

VMEM_LIMIT = 28 * 1024 * 1024
HINT = pl.CostEstimate(flops=1, bytes_accessed=1, transcendentals=0)


def swap(value, axis, mask):
    size = math.prod(lax.axis_size(name) for name in (axis if isinstance(axis, tuple) else (axis,)))
    return lax.ppermute(value, axis, [(source, source ^ mask) for source in range(size)])


def after(value, *others):
    return lax.optimization_barrier((value, *others))[0]


def sum_all(value):
    axes = ("row", "col")
    size = lax.axis_size("row") * lax.axis_size("col")
    if size > 16 or size & (size - 1):
        return lax.psum(value, axes)
    mask = 1
    while mask < size:
        near = value + swap(value, axes, mask)
        if 2 * mask < size:
            near = near + (swap(value, axes, 2 * mask) + swap(value, axes, 3 * mask))
        value, mask = near, 4 * mask
    return value


def add_piece(r_ref, w, re_ref, im_ref):
    rows_re, rows_im = r_ref[0, 0], r_ref[0, 1]
    w_re, w_im = w[0], w[1]
    dot = functools.partial(jnp.dot, preferred_element_type=jnp.float32)
    re_ref[...] = re_ref[...] + dot(rows_re, w_re) + dot(rows_im, -w_im)
    im_ref[...] = im_ref[...] + dot(rows_re, w_im) + dot(rows_im, w_re)


def start_pieces(freq, w_refs, held, sem):
    for k, ref in enumerate(w_refs):
        source = ref.at[freq if ref.shape[0] > 1 else 0]
        pltpu.make_async_copy(source, held.at[k], sem.at[k]).start()


def accumulate(freq, has_total, r_ref, w_refs, total, held, sem, field):
    piece, step = pl.program_id(0), pl.program_id(1)

    @pl.when((piece == 0) & (step == 0))
    def _():
        start_pieces(freq, w_refs, held, sem)

    @pl.when(step == 0)
    def _():
        source = w_refs[0].at[0]
        pltpu.make_async_copy(source, held.at[piece], sem.at[piece]).wait()

    @pl.when(piece == 0)
    def _():
        field[step] = total[...] if has_total else jnp.zeros_like(field[step])

    add_piece(r_ref, held.at[piece], field.at[step, 0], field.at[step, 1])


def field_kernel(freq, count, has_total, ids, r_ref, *refs):
    w_refs, total = refs[:count], refs[count]
    out, held, sem, field = refs[-4:]
    accumulate(freq, has_total, r_ref, w_refs, total, held, sem, field)

    @pl.when(pl.program_id(0) == count - 1)
    def _():
        out[...] = field[pl.program_id(1)]


def numer_kernel(freq, count, late, ids, r_ref, *refs):
    w_refs = refs[:count]
    total, mine, other = refs[count : count + 3]
    late_refs = refs[count + 3 : count + 3 + late]
    out, held, sem, field, rows, row_sem = refs[-6:]
    tile = rows.shape[2]
    slots = rows.shape[0]
    last = pl.program_id(0) == count - 1
    step = pl.program_id(1)
    accumulate(freq, True, r_ref, w_refs, total, held, sem, field)

    @pl.when((pl.program_id(0) == 0) & (step == 0))
    def _():
        out[...] = jnp.zeros_like(out)
        for slot in range(slots):
            view = [ref.at[0, :, pl.ds(slot * tile, tile)] for ref in (mine, other)]
            view += [ref.at[0] for ref in late_refs]
            for k, source in enumerate(view):

                @pl.when(ids[count + slot] == k)
                def _(source=source, slot=slot):
                    pltpu.make_async_copy(source, rows.at[slot], row_sem.at[slot]).start()

    @pl.when(last)
    def _():
        source = mine.at[0, :, pl.ds(0, tile)]
        pltpu.make_async_copy(source, rows.at[step], row_sem.at[step]).wait()
        product = rows[step, 0].astype(jnp.float32) * field[step, 0]
        product += rows[step, 1].astype(jnp.float32) * field[step, 1]
        out[...] += jnp.sum(product.reshape(-1, 8, product.shape[-1]), axis=0)


def call(kernel, cross, freq, ids, pieces, total, rest, out_shape, out_spec, scratch):
    rows, (tile, sources) = cross.shape[2], pieces[0].shape[2:]
    count, steps = len(pieces), cross.shape[2] // tile
    anywhere = pl.BlockSpec(memory_space=pl.ANY)
    specs = [pl.BlockSpec((1, 2, tile, tile), lambda p, i, ids: (freq, 0, i, ids[p]))]
    specs += [anywhere] * count
    args = [cross, *pieces]
    if total is not None:
        held_at = lambda p, i, ids: (0, jnp.where(p == 0, i, steps - 1), 0)
        specs, args = specs + [pl.BlockSpec((2, tile, sources), held_at)], args + [total]
    specs, args = specs + [anywhere] * len(rest), args + list(rest)
    return pl.pallas_call(
        kernel,
        out_shape=out_shape,
        grid_spec=pltpu.PrefetchScalarGridSpec(
            num_scalar_prefetch=1,
            grid=(count, steps),
            in_specs=specs,
            out_specs=out_spec,
            scratch_shapes=[
                pltpu.VMEM((count, 2, tile, sources), pieces[0].dtype),
                pltpu.SemaphoreType.DMA((count,)),
                pltpu.VMEM((steps, 2, tile, sources), jnp.float32),
                *scratch,
            ],
        ),
        compiler_params=pltpu.CompilerParams(vmem_limit_bytes=VMEM_LIMIT),
        cost_estimate=HINT,
    )(ids, *args)


def add_field(cross, freq, ids, pieces, total=None):
    rows, (tile, sources) = cross.shape[2], pieces[0].shape[2:]
    count = len(pieces)
    return call(
        functools.partial(field_kernel, freq, count, total is not None),
        cross,
        freq,
        ids,
        pieces,
        total,
        [],
        jax.ShapeDtypeStruct((2, rows, sources), jnp.float32),
        pl.BlockSpec(
            (2, tile, sources), lambda p, i, ids: (0, jnp.where(p == count - 1, i, 0), 0)
        ),
        [],
    )


def finish(cross, freq, ids, pieces, total, mine, other, late):
    steps, (tile, sources) = cross.shape[2] // pieces[0].shape[2], pieces[0].shape[2:]
    out = call(
        functools.partial(numer_kernel, freq, len(pieces), len(late)),
        cross,
        freq,
        ids,
        pieces,
        total,
        [mine, other, *late],
        jax.ShapeDtypeStruct((8, sources), jnp.float32),
        pl.BlockSpec((8, sources), lambda p, i, ids: (0, 0)),
        [pltpu.VMEM((steps, 2, tile, sources), mine.dtype), pltpu.SemaphoreType.DMA((steps,))],
    )
    return jnp.sum(out, axis=0)


def pick_kernel(freq, ids, *refs):
    pieces, out, sem = refs[:-2], refs[-2], refs[-1]
    width = pieces[0].shape[2]
    for slot in range(2):
        for k, piece in enumerate(pieces):

            @pl.when(ids[slot] == k)
            def _(slot=slot, piece=piece):
                source = piece.at[freq if piece.shape[0] > 1 else 0]
                pltpu.make_async_copy(
                    source, out.at[0, :, pl.ds(slot * width, width)], sem.at[slot]
                ).start()

    for slot in range(2):

        @pl.when(ids[slot] < len(pieces))
        def _(slot=slot):
            pltpu.make_async_copy(
                pieces[0].at[0], out.at[0, :, pl.ds(slot * width, width)], sem.at[slot]
            ).wait()


def pick_rows(freq, ids, pieces):
    _, _, width, sources = pieces[0].shape
    return pl.pallas_call(
        functools.partial(pick_kernel, freq),
        out_shape=jax.ShapeDtypeStruct((1, 2, 2 * width, sources), pieces[0].dtype),
        grid_spec=pltpu.PrefetchScalarGridSpec(
            num_scalar_prefetch=1,
            grid=(1,),
            in_specs=[pl.BlockSpec(memory_space=pl.ANY)] * len(pieces),
            out_specs=pl.BlockSpec((1, 2, 2 * width, sources), lambda i, ids: (0, 0, 0, 0)),
            scratch_shapes=[pltpu.SemaphoreType.DMA((2,))],
        ),
        cost_estimate=HINT,
    )(ids, *pieces)


def numer_by_swaps(cross, replicas):
    rows, half = cross.shape[2], cross.shape[3]
    width = replicas.shape[3]
    me = lax.axis_index("row").astype(jnp.int32)
    col = lax.axis_index("col").astype(jnp.int32)
    holder = me * rows // half
    first = (me * rows - holder * half) // width
    masks = jnp.stack([first ^ me, (first + 1) ^ me])
    ids = lambda *wanted: me ^ jnp.array(wanted, jnp.int32)

    own = replicas[:, :, 0]
    x = swap(own, "row", 1)
    own_a = own[0:1]
    pa = swap(own_a, "row", 4)
    na = swap(own_a, "row", 2)
    own_b = own[1:2]
    x, pa, na, own_b = lax.optimization_barrier((x, pa, na, own_b))

    pb = swap(own_b, "row", 4)
    ga = swap(pa, "row", 2)
    xpa = swap(pa, "row", 1)
    xna = swap(na, "row", 1)
    a0 = add_field(cross, 0, ids(0, 1, 2, 4), [own, x, na, pa])
    a1 = add_field(cross, 1, ids(0, 1), [own, x])
    x_b = x[1:2]
    pb, ga, xpa, xna, a0, a1, x_b, own_b = lax.optimization_barrier(
        (pb, ga, xpa, xna, a0, a1, x_b, own_b)
    )

    gb = swap(pb, "row", 2)
    xga = swap(ga, "row", 1)
    nb = swap(own_b, "row", 2)
    b0 = add_field(cross, 0, ids(3, 5, 6), [xna, xpa, ga], a0)
    xpb = swap(pb, "row", 1)
    a1 = add_field(cross, 1, ids(4), [pb], a1)
    gb, xga, nb, xpb, a1, b0 = lax.optimization_barrier((gb, xga, nb, xpb, a1, b0))

    d = swap(x_b, "row", 2)
    xgb = swap(gb, "row", 1)
    b1 = add_field(cross, 1, ids(6, 5, 2), [gb, xpb, nb], a1)

    holds = holder == col
    mine_a = pick_rows(0, masks, [own, x, na, xna, pa, xpa, ga, xga])
    other_a = swap(mine_a, "col", 1)
    where_a = jnp.where(holds, 0, 1) * jnp.ones_like(masks)
    c0 = finish(cross, 0, jnp.concatenate([ids(7), where_a]), [xga], b0, mine_a, other_a, [])

    order = jnp.where(masks == 3, 7, masks - (masks > 3))
    mine_b = pick_rows(1, order, [own, x, nb, pb, xpb, gb])
    other_b = swap(mine_b, "col", 1)
    late = [xgb, d]
    late = late + [swap(after(piece, b1, c0), "col", 1) for piece in late]
    where_b = jnp.where(masks == 7, jnp.where(holds, 2, 4), where_a)
    where_b = jnp.where(masks == 3, jnp.where(holds, 3, 5), where_b)
    c1 = finish(
        cross, 1, jnp.concatenate([ids(3, 7), where_b]), [d, xgb], b1, mine_b, other_b, late
    )
    return jnp.stack([c0, c1])


def numer_by_gather(cross, replicas):
    rows, half = cross.shape[2], cross.shape[3]
    row_index, col_index = lax.axis_index("row"), lax.axis_index("col")
    first_row = row_index * rows
    holder = first_row // half
    whole = lax.all_gather(replicas, "row", axis=3, tiled=True)[:, :, 0]
    parts = jnp.einsum("fark,fbks->fabrs", cross, whole, preferred_element_type=jnp.float32)
    field = jnp.stack([parts[:, 0, 0] - parts[:, 1, 1], parts[:, 0, 1] + parts[:, 1, 0]], axis=1)
    own_rows = lax.dynamic_slice_in_dim(whole, first_row - holder * half, rows, 2)
    block_rows = jnp.where(holder == col_index, own_rows, swap(own_rows, "col", 1))
    return jnp.sum(block_rows.astype(jnp.float32) * field, axis=(1, 2))


def body(cross_spectra, replicas, tile_order):
    fnum = cross_spectra.shape[0]
    sources = replicas.shape[4]
    own = replicas[:, :, 0].astype(jnp.float32)
    norms = jnp.sum(own * own, axis=(1, 2))
    doubling = (
        lax.axis_size("row") == 8
        and replicas.shape[3] % 128 == 0
        and cross_spectra.shape[2] == 2 * replicas.shape[3]
    )
    numer = (numer_by_swaps if doubling else numer_by_gather)(cross_spectra, replicas)
    numer, norms = sum_all(jnp.stack([numer, norms]))
    beam = numer / (norms + 1e-06)
    width = sources // lax.axis_size("col")
    beam_half = lax.dynamic_slice_in_dim(beam, lax.axis_index("col") * width, width, 1)
    peak = jnp.max(jnp.abs(beam), axis=1) + 1e-06
    count = tile_order.shape[0]
    picker = (tile_order[:, None] == jnp.arange(count, dtype=jnp.int32)[None, :]).astype(jnp.float32)
    tiles = beam.reshape(fnum, count, sources // count)
    refined = (
        jnp.einsum("tu,fup->ftp", picker, tiles, precision=lax.Precision.HIGHEST)
        / peak[:, None, None]
    )
    return (beam_half, refined)


def solution(mesh):
    in_specs = (P("groups", None, "row", "col"), P("groups", None, "col", "row", None), P("groups"))
    out_specs = (P("groups", "col"), P("groups", None, None))
    return jax.shard_map(body, mesh=mesh, in_specs=in_specs, out_specs=out_specs, check_vma=False)
```

time: 224 us -> 218 us (0.973)
  waiting for transfers between devices: 110 us -> 87.7 us
  local copies, waits for them, and re-layouts: 8.41 us -> 26.5 us
    ppermute x29 -> x23, waiting for transfers between devices: 110 us -> 87.7 us  [swap(): lax.ppermute(value, axis, [(source, source ^ mask) for source in range(si...]
    unnamed x32 -> x60, local copies, waits for them, and re-layouts: 2.3 us -> 22.1 us
    ppermute x29 -> x23, starting transfers between devices: 30.3 us -> 28.1 us  [swap(): lax.ppermute(value, axis, [(source, source ^ mask) for source in range(si...]
    pallas_call x6 -> x7, Pallas kernels: 63.5 us -> 64.9 us  [call(): pl.pallas_call(kernel, out_shape=out_shape, grid_spec=pltpu.PrefetchScala...]
  transfers between devices with their start and end apart: 29 -> 23, of which waited for: 16 -> 13; matrix products, arithmetic and copies ran while one was open for 3% -> 2% of each run, Pallas kernels for 28% -> 28%
where the time goes in v3:
time: 218 us
  waiting for transfers between devices  87.7 us (40%)
  Pallas kernels  72.2 us (33%)
  starting transfers between devices  28.1 us (13%)
  local copies, waits for them, and re-layouts  26.5 us (12%)
    ppermute x23, waiting for transfers between devices, swap(): lax.ppermute(value, axis, [(source, source ^ mask) for source in range(si...  87.7 us
    pallas_call x7, Pallas kernels, call(): pl.pallas_call(kernel, out_shape=out_shape, grid_spec=pltpu.PrefetchScala...  64.9 us
    ppermute x23, starting transfers between devices, swap(): lax.ppermute(value, axis, [(source, source ^ mask) for source in range(si...  28.1 us
    unnamed x60, local copies, waits for them, and re-layouts  22.1 us
    pallas_call x2, Pallas kernels, pick_rows(): pl.pallas_call(functools.partial(pick_kernel, freq), out_shape=jax.ShapeD...  7.25 us
  transfers between devices with their start and end apart: 23, of which 13 were waited for; matrix products, arithmetic and copies ran while one was open for 2% of the time, Pallas kernels for 28%

profile of v3, /device:TPU:0, one launch (start us, length us, event | category | flops | bytes accessed | tf_op | source)
XLA Modules:
  0.0 217.7 jit_solution(4122210201866501663)
XLA Ops:
  0.7 3.0 %collective-permute-start = (bf16[2,2,512,512]{3,2,1,0:T(8,128)(2,1)}, bf16[2,2,512,512]{3,2,1,0:T(8,128)(2,1)S(1)}, u32[]{:S(2)}, u32[]{:S(2)}) collective-permute-start(bf16[2,2,512,512]{3,2,1,0:T(8,128)(2,1)} %bitcast.25), channel_id=1, source_target_pairs={{0,2},{2,0},{4,6},{6,4},{8,10},{10,8},{12,14},{14,12},{1,3},{3,1},... | collective-permute-start | bytes 6291464 | tf_op jit(solution)/shard_map/ppermute | solution.py:17
  3.7 2.7 %slice_bitcast_fusion = (bf16[1,2,512,512]{3,2,1,0:T(8,128)(2,1)}, bf16[1,2,512,512]{3,2,1,0:T(8,128)(2,1)S(1)}) fusion(bf16[2,2,1,512,512]{4,3,1,2,0:T(8,128)(2,1)} %bitcast.26), kind=kLoop, calls=%fused_computation.3 | loop fusion | bytes 4194304 | tf_op jit(solution)/shard_map/slice | solution.py:233
  6.4 2.6 %collective-permute-start.1 = (bf16[1,2,512,512]{3,2,1,0:T(8,128)(2,1)S(1)}, bf16[1,2,512,512]{3,2,1,0:T(8,128)(2,1)S(1)}, u32[]{:S(2)}, u32[]{:S(2)}) collective-permute-start(bf16[1,2,512,512]{3,2,1,0:T(8,128)(2,1)S(1)} %get-tuple-element.47), channel_id=1, source_target_pairs={{0,8},{2,10},{4,12},{6,14},{8,0},{10,2},{12,4},{14,6},{1,9},{3,11}... | collective-permute-start | bytes 3145736 | tf_op jit(solution)/shard_map/ppermute | solution.py:17
  9.0 1.6 collective-permute-start.2
  10.5 43.9 %collective-permute-done.1.refs_3_.refs_4_ = bf16[1,2,512,512]{3,2,1,0:T(8,128)(2,1)S(1)} collective-permute-done((bf16[1,2,512,512]{3,2,1,0:T(8,128)(2,1)S(1)}, bf16[1,2,512,512]{3,2,1,0:T(8,128)(2,1)S(1)}, u32[]{:S(2)}, u32[]{:S(2)}) %collective-permute-start.1) | collective-permute-done | bytes 1048608 | tf_op jit(solution)/shard_map/ppermute | solution.py:17
  54.8 1.3 copy-done.2
  56.1 1.4 collective-permute-start.4
  58.2 1.3 collective-permute-start.6
  59.6 2.2 %collective-permute-start.3 = (bf16[1,2,512,512]{3,2,1,0:T(8,128)(2,1)}, bf16[1,2,512,512]{3,2,1,0:T(8,128)(2,1)}, u32[]{:S(2)}, u32[]{:S(2)}) collective-permute-start(bf16[1,2,512,512]{3,2,1,0:T(8,128)(2,1)} %get-tuple-element.28), channel_id=1, source_target_pairs={{0,8},{2,10},{4,12},{6,14},{8,0},{10,2},{12,4},{14,6},{1,9},{3,11}... | collective-permute-start | bytes 3145736 | tf_op jit(solution)/shard_map/ppermute | solution.py:17
  61.8 1.6 copy-done.3
  63.4 13.3 %shard_map.113.refs_3_ = f32[2,1024,512]{2,1,0:T(8,128)S(1)} custom-call(s32[4]{0:T(128)S(1)} %broadcast_xor_fusion.3.ids, bf16[2,2,1024,4096]{3,2,1,0:T(8,128)(2,1)} %r_ref.13, bf16[2,2,512,512]{3,2,1,0:T(8,128)(2,1)S(1)} %bitcast.29, bf16[2,2,512,512]{3,2,1,0:T(8,128)(2,1)S(1)} %copy-done.3, bf16[1,2,512,512]{3,2,1,0:T(8,128)(2,1)} %collective-permute-done.2.refs_2_, ...), custom_call_target="tpu_custom_call" | custom-call | flops 1 | bytes 1 | tf_op jit(solution)/shard_map/pallas_call | solution.py:124
  76.7 2.0 copy-done.5
  78.7 1.0 copy-done.17
  79.7 7.9 %shard_map.114.refs_1_ = f32[2,1024,512]{2,1,0:T(8,128)S(1)} custom-call(s32[2]{0:T(128)S(1)} %iota_xor_fusion.ids, bf16[2,2,1024,4096]{3,2,1,0:T(8,128)(2,1)} %r_ref.13, bf16[2,2,512,512]{3,2,1,0:T(8,128)(2,1)S(1)} %bitcast.30, bf16[2,2,512,512]{3,2,1,0:T(8,128)(2,1)S(1)} %copy-done.4), custom_call_target="tpu_custom_call" | custom-call | flops 1 | bytes 1 | tf_op jit(solution)/shard_map/pallas_call | solution.py:124
  87.7 2.0 copy-done.13
  89.6 1.1 slice.19
  90.7 9.7 %collective-permute-done.4.refs_2_.refs_6_ = bf16[1,2,512,512]{3,2,1,0:T(8,128)(2,1)} collective-permute-done((bf16[1,2,512,512]{3,2,1,0:T(8,128)(2,1)S(1)}, bf16[1,2,512,512]{3,2,1,0:T(8,128)(2,1)}, u32[]{:S(2)}, u32[]{:S(2)}) %collective-permute-start.4) | collective-permute-done | bytes 1048608 | tf_op jit(solution)/shard_map/ppermute | solution.py:17
  100.4 3.3 %collective-permute-done.6.refs_0_.refs_3_ = bf16[1,2,512,512]{3,2,1,0:T(8,128)(2,1)} collective-permute-done((bf16[1,2,512,512]{3,2,1,0:T(8,128)(2,1)}, bf16[1,2,512,512]{3,2,1,0:T(8,128)(2,1)}, u32[]{:S(2)}, u32[]{:S(2)}) %collective-permute-start.6) | collective-permute-done | bytes 1048608 | tf_op jit(solution)/shard_map/ppermute | solution.py:17
  103.7 3.4 %collective-permute-done.3.refs_0_.refs_3_ = bf16[1,2,512,512]{3,2,1,0:T(8,128)(2,1)} collective-permute-done((bf16[1,2,512,512]{3,2,1,0:T(8,128)(2,1)}, bf16[1,2,512,512]{3,2,1,0:T(8,128)(2,1)}, u32[]{:S(2)}, u32[]{:S(2)}) %collective-permute-start.3) | collective-permute-done | bytes 1048608 | tf_op jit(solution)/shard_map/ppermute | solution.py:17
  107.8 1.3 collective-permute-start.8
  109.2 2.0 collective-permute-start.9
  111.8 2.2 %copy-done.14 = f32[2,1024,512]{2,1,0:T(8,128)S(1)} copy-done((f32[2,1024,512]{2,1,0:T(8,128)S(1)}, f32[2,1024,512]{2,1,0:T(8,128)}, u32[]{:S(2)}) %copy-start.14) | copy-done | bytes 4194328
  114.0 5.7 %shard_map.115.refs_3_ = f32[2,1024,512]{2,1,0:T(8,128)S(1)} custom-call(s32[1]{0:T(128)} %bitcast.6.ids, bf16[2,2,1024,4096]{3,2,1,0:T(8,128)(2,1)} %r_ref.13, bf16[1,2,512,512]{3,2,1,0:T(8,128)(2,1)} %collective-permute-done.3.refs_0_.refs_3_, f32[2,1024,512]{2,1,0:T(8,128)S(1)} %copy-done.14), custom_call_target="tpu_custom_call" | custom-call | flops 1 | bytes 1 | tf_op jit(solution)/shard_map/pallas_call | solution.py:124
  119.7 2.0 copy-done.11
  121.7 11.8 %shard_map.116.refs_1_ = f32[2,1024,512]{2,1,0:T(8,128)S(1)} custom-call(s32[3]{0:T(128)S(1)} %broadcast_xor_fusion.1.ids, bf16[2,2,1024,4096]{3,2,1,0:T(8,128)(2,1)} %r_ref.13, bf16[1,2,512,512]{3,2,1,0:T(8,128)(2,1)} %collective-permute-done.6.refs_0_.refs_3_, bf16[1,2,512,512]{3,2,1,0:T(8,128)(2,1)} %collective-permute-done.5.refs_1_.refs_5_, ...), custom_call_target="tpu_custom_call" | custom-call | flops 1 | bytes 1 | tf_op jit(solution)/shard_map/pallas_call | solution.py:124
  133.4 2.0 copy-done.9
  135.5 13.7 %collective-permute-done.8.refs_7_.refs_0_ = bf16[1,2,512,512]{3,2,1,0:T(8,128)(2,1)S(1)} collective-permute-done((bf16[1,2,512,512]{3,2,1,0:T(8,128)(2,1)}, bf16[1,2,512,512]{3,2,1,0:T(8,128)(2,1)S(1)}, u32[]{:S(2)}, u32[]{:S(2)}) %collective-permute-start.8) | collective-permute-done | bytes 1048608 | tf_op jit(solution)/shard_map/ppermute | solution.py:17
  149.2 2.8 %collective-permute-done.9.refs_2_ = bf16[1,2,512,512]{3,2,1,0:T(8,128)(2,1)S(1)} collective-permute-done((bf16[1,2,512,512]{3,2,1,0:T(8,128)(2,1)}, bf16[1,2,512,512]{3,2,1,0:T(8,128)(2,1)S(1)}, u32[]{:S(2)}, u32[]{:S(2)}) %collective-permute-start.9) | collective-permute-done | bytes 1048608 | tf_op jit(solution)/shard_map/ppermute | solution.py:17
  151.9 3.5 %shard_map.117.refs_2_ = bf16[1,2,1024,512]{3,2,1,0:T(8,128)(2,1)} custom-call(s32[2]{0:T(128)} %get-tuple-element.45.ids, bf16[2,2,512,512]{3,2,1,0:T(8,128)(2,1)} %bitcast.27, bf16[2,2,512,512]{3,2,1,0:T(8,128)(2,1)} %copy-done.2, bf16[1,2,512,512]{3,2,1,0:T(8,128)(2,1)} %collective-permute-done.2.refs_2_, ...), custom_call_target="tpu_custom_call" | custom-call | flops 1 | bytes 1 | tf_op jit(solution)/shard_map/pallas_call | solution.py:204
  155.6 2.1 collective-permute-start.12
  157.7 0.8 collective-permute-start.13
  158.4 3.7 %shard_map.120.refs_3_ = bf16[1,2,1024,512]{3,2,1,0:T(8,128)(2,1)} custom-call(s32[2]{0:T(128)} %get-tuple-element.44.ids, bf16[2,2,512,512]{3,2,1,0:T(8,128)(2,1)} %bitcast.28, bf16[2,2,512,512]{3,2,1,0:T(8,128)(2,1)} %copy-done.2, bf16[1,2,512,512]{3,2,1,0:T(8,128)(2,1)} %copy-done.20, bf16[1,2,512,512]{3,2,1,0:T(8,128)(2,1)} %collective-permute-done.3.refs_0_.refs_3_, ...), custom_call_target="tpu_custom_call" | custom-call | flops 1 | bytes 1 | tf_op jit(solution)/shard_map/pallas_call | solution.py:204
  162.3 2.2 %copy-done.12 = f32[2,1024,512]{2,1,0:T(8,128)S(1)} copy-done((f32[2,1024,512]{2,1,0:T(8,128)S(1)}, f32[2,1024,512]{2,1,0:T(8,128)}, u32[]{:S(2)}) %copy-start.12) | copy-done | bytes 4194328
  164.5 12.8 %shard_map.119.refs_2_ = f32[2,1024,512]{2,1,0:T(8,128)S(1)} custom-call(s32[3]{0:T(128)S(1)} %broadcast_xor_fusion.ids, bf16[2,2,1024,4096]{3,2,1,0:T(8,128)(2,1)} %r_ref.13, bf16[1,2,512,512]{3,2,1,0:T(8,128)(2,1)} %collective-permute-done.7.refs_0_.refs_5_, bf16[1,2,512,512]{3,2,1,0:T(8,128)(2,1)S(1)} %copy-done.19, ...), custom_call_target="tpu_custom_call" | custom-call | flops 1 | bytes 1 | tf_op jit(solution)/shard_map/pallas_call | solution.py:124
  177.3 2.0 copy-done.7
  179.3 5.3 %shard_map.118 = f32[8,512]{1,0:T(8,128)S(1)} custom-call(s32[3]{0:T(128)S(1)} %concatenate.6.ids, bf16[2,2,1024,4096]{3,2,1,0:T(8,128)(2,1)} %r_ref.13, bf16[1,2,512,512]{3,2,1,0:T(8,128)(2,1)S(1)} %copy-done.23, f32[2,1024,512]{2,1,0:T(8,128)S(1)} %copy-done.10, bf16[1,2,1024,512]{3,2,1,0:T(8,128)(2,1)S(1)} %copy-done.16, ...), custom_call_target="tpu_custom_call" | custom-call | flops 1 | bytes 1 | tf_op jit(solution)/shard_map/pallas_call | solution.py:124
  184.7 1.6 collective-permute-start.16
  186.9 2.4 %collective-permute-done.16.refs_8_ = bf16[1,2,512,512]{3,2,1,0:T(8,128)(2,1)} collective-permute-done((bf16[1,2,512,512]{3,2,1,0:T(8,128)(2,1)S(1)}, bf16[1,2,512,512]{3,2,1,0:T(8,128)(2,1)}, u32[]{:S(2)}, u32[]{:S(2)}) %collective-permute-start.16) | collective-permute-done | bytes 1048608 | tf_op jit(solution)/shard_map/ppermute | solution.py:17
  189.3 1.1 collective-permute-done.15.refs_7_
  190.4 2.2 %copy-done.8 = f32[2,1024,512]{2,1,0:T(8,128)S(1)} copy-done((f32[2,1024,512]{2,1,0:T(8,128)S(1)}, f32[2,1024,512]{2,1,0:T(8,128)}, u32[]{:S(2)}) %copy-start.8) | copy-done | bytes 4194328
  192.6 1.6 copy-done.15
  194.2 8.2 %shard_map.121 = f32[8,512]{1,0:T(8,128)S(1)} custom-call(s32[4]{0:T(128)S(1)} %pad_add_fusion.1.ids, bf16[2,2,1024,4096]{3,2,1,0:T(8,128)(2,1)} %r_ref.13, bf16[1,2,512,512]{3,2,1,0:T(8,128)(2,1)S(1)} %collective-permute-done.12.refs_0_.refs_6_, bf16[1,2,512,512]{3,2,1,0:T(8,128)(2,1)} %collective-permute-done.13.refs_1_.refs_5_, ...), custom_call_target="tpu_custom_call" | custom-call | flops 1 | bytes 1 | tf_op jit(solution)/shard_map/pallas_call | solution.py:124
  203.1 1.0 collective-permute-start.18
  204.5 2.2 %collective-permute-done.18 = f32[2,2,512]{2,1,0:T(2,128)S(1)} collective-permute-done((f32[2,2,512]{2,1,0:T(2,128)S(1)}, f32[2,2,512]{2,1,0:T(2,128)S(1)}, u32[]{:S(2)}, u32[]{:S(2)}) %collective-permute-start.18) | collective-permute-done | bytes 8224 | tf_op jit(solution)/shard_map/ppermute | solution.py:17
  207.7 2.9 %collective-permute-start.21 = (f32[2,2,512]{2,1,0:T(2,128)S(1)}, f32[2,2,512]{2,1,0:T(2,128)S(1)}, u32[]{:S(2)}, u32[]{:S(2)}) collective-permute-start(f32[2,2,512]{2,1,0:T(2,128)S(1)} %add_add_fusion.1), channel_id=1, source_target_pairs={{0,8},{1,9},{2,10},{3,11},{4,12},{5,13},{6,14},{7,15},{8,0},{9,1},... | collective-permute-start | bytes 24584 | tf_op jit(solution)/shard_map/ppermute | solution.py:17
  210.6 1.1 collective-permute-start.22
  212.3 3.8 %collective-permute-done.22 = f32[2,2,512]{2,1,0:T(2,128)S(1)} collective-permute-done((f32[2,2,512]{2,1,0:T(2,128)S(1)}, f32[2,2,512]{2,1,0:T(2,128)S(1)}, u32[]{:S(2)}, u32[]{:S(2)}) %collective-permute-start.22) | collective-permute-done | bytes 8224 | tf_op jit(solution)/shard_map/ppermute | solution.py:17
  216.9 0.8 fusion
  (90 shorter events, 6.7 us)
Async XLA Ops:
  0.6 61.2 %copy-start.29 = (s32[4]{0:T(128)S(1)}, s32[4]{0:T(128)}, u32[]{:S(2)}) copy-start(s32[4]{0:T(128)} %constant.77.clone) | copy-start | bytes 52
  0.6 61.1 %copy-start = (bf16[2,2,1,512,512]{4,3,2,1,0:T(8,128)(2,1)S(1)}, bf16[2,2,1,512,512]{4,3,2,1,0:T(8,128)(2,1)}, u32[]{:S(2)}) copy-start(bf16[2,2,1,512,512]{4,3,2,1,0:T(8,128)(2,1)} %param.11) | copy-start | bytes 6291460
  0.7 54.1 %collective-permute-start = (bf16[2,2,512,512]{3,2,1,0:T(8,128)(2,1)}, bf16[2,2,512,512]{3,2,1,0:T(8,128)(2,1)S(1)}, u32[]{:S(2)}, u32[]{:S(2)}) collective-permute-start(bf16[2,2,512,512]{3,2,1,0:T(8,128)(2,1)} %bitcast.25), channel_id=1, source_target_pairs={{0,2},{2,0},{4,6},{6,4},{8,10},{10,8},{12,14},{14,12},{1,3},{3,1},... | collective-permute-start | bytes 6291464 | tf_op jit(solution)/shard_map/ppermute | solution.py:17
  6.4 48.1 %collective-permute-start.1 = (bf16[1,2,512,512]{3,2,1,0:T(8,128)(2,1)S(1)}, bf16[1,2,512,512]{3,2,1,0:T(8,128)(2,1)S(1)}, u32[]{:S(2)}, u32[]{:S(2)}) collective-permute-start(bf16[1,2,512,512]{3,2,1,0:T(8,128)(2,1)S(1)} %get-tuple-element.47), channel_id=1, source_target_pairs={{0,8},{2,10},{4,12},{6,14},{8,0},{10,2},{12,4},{14,6},{1,9},{3,11}... | collective-permute-start | bytes 3145736 | tf_op jit(solution)/shard_map/ppermute | solution.py:17
  9.0 45.8 %collective-permute-start.2 = (bf16[1,2,512,512]{3,2,1,0:T(8,128)(2,1)S(1)}, bf16[1,2,512,512]{3,2,1,0:T(8,128)(2,1)}, u32[]{:S(2)}, u32[]{:S(2)}) collective-permute-start(bf16[1,2,512,512]{3,2,1,0:T(8,128)(2,1)S(1)} %get-tuple-element.47), channel_id=1, source_target_pairs={{0,4},{2,6},{4,0},{6,2},{8,12},{10,14},{12,8},{14,10},{1,5},{3,7},... | collective-permute-start | bytes 3145736 | tf_op jit(solution)/shard_map/ppermute | solution.py:17
  56.1 44.3 %collective-permute-start.4 = (bf16[1,2,512,512]{3,2,1,0:T(8,128)(2,1)S(1)}, bf16[1,2,512,512]{3,2,1,0:T(8,128)(2,1)}, u32[]{:S(2)}, u32[]{:S(2)}) collective-permute-start(bf16[1,2,512,512]{3,2,1,0:T(8,128)(2,1)S(1)} %collective-permute-done.1.refs_3_.refs_4_), channel_id=1, source_target_pairs={{0,4},{2,6},{4,0},{6,2},{8,12},{10,14},{12,8},{14,10},{1,5},{3,7},... | collective-permute-start | bytes 3145736 | tf_op jit(solution)/shard_map/ppermute | solution.py:17
  57.5 42.9 %collective-permute-start.5 = (bf16[1,2,512,512]{3,2,1,0:T(8,128)(2,1)S(1)}, bf16[1,2,512,512]{3,2,1,0:T(8,128)(2,1)}, u32[]{:S(2)}, u32[]{:S(2)}) collective-permute-start(bf16[1,2,512,512]{3,2,1,0:T(8,128)(2,1)S(1)} %collective-permute-done.1.refs_3_.refs_4_), channel_id=1, source_target_pairs={{0,2},{2,0},{4,6},{6,4},{8,10},{10,8},{12,14},{14,12},{1,3},{3,1},... | collective-permute-start | bytes 3145736 | tf_op jit(solution)/shard_map/ppermute | solution.py:17
  58.2 45.5 %collective-permute-start.6 = (bf16[1,2,512,512]{3,2,1,0:T(8,128)(2,1)}, bf16[1,2,512,512]{3,2,1,0:T(8,128)(2,1)}, u32[]{:S(2)}, u32[]{:S(2)}) collective-permute-start(bf16[1,2,512,512]{3,2,1,0:T(8,128)(2,1)} %collective-permute-done.2.refs_2_), channel_id=1, source_target_pairs={{0,2},{2,0},{4,6},{6,4},{8,10},{10,8},{12,14},{14,12},{1,3},{3,1},... | collective-permute-start | bytes 3145736 | tf_op jit(solution)/shard_map/ppermute | solution.py:17
  59.6 47.6 %collective-permute-start.3 = (bf16[1,2,512,512]{3,2,1,0:T(8,128)(2,1)}, bf16[1,2,512,512]{3,2,1,0:T(8,128)(2,1)}, u32[]{:S(2)}, u32[]{:S(2)}) collective-permute-start(bf16[1,2,512,512]{3,2,1,0:T(8,128)(2,1)} %get-tuple-element.28), channel_id=1, source_target_pairs={{0,8},{2,10},{4,12},{6,14},{8,0},{10,2},{12,4},{14,6},{1,9},{3,11}... | collective-permute-start | bytes 3145736 | tf_op jit(solution)/shard_map/ppermute | solution.py:17
  63.4 16.3 %copy-start.4 = (bf16[2,2,512,512]{3,2,1,0:T(8,128)(2,1)S(1)}, bf16[2,2,512,512]{3,2,1,0:T(8,128)(2,1)}, u32[]{:S(2)}) copy-start(bf16[2,2,512,512]{3,2,1,0:T(8,128)(2,1)} %copy-done.2) | copy-start | bytes 6291460
  76.7 2.0 copy-start.5
  79.7 32.1 %copy-start.28 = (s32[3]{0:T(128)S(1)}, s32[3]{0:T(128)}, u32[]{:S(2)}) copy-start(s32[3]{0:T(128)} %constant.78.clone) | copy-start | bytes 40
  87.7 2.0 copy-start.13
  107.1 28.3 %collective-permute-start.10 = (bf16[1,2,512,512]{3,2,1,0:T(8,128)(2,1)}, bf16[1,2,512,512]{3,2,1,0:T(8,128)(2,1)S(1)}, u32[]{:S(2)}, u32[]{:S(2)}) collective-permute-start(bf16[1,2,512,512]{3,2,1,0:T(8,128)(2,1)} %collective-permute-done.3.refs_0_.refs_3_), channel_id=1, source_target_pairs={{0,2},{2,0},{4,6},{6,4},{8,10},{10,8},{12,14},{14,12},{1,3},{3,1},... | collective-permute-start | bytes 3145736 | tf_op jit(solution)/shard_map/ppermute | solution.py:17
  107.8 27.7 %collective-permute-start.7 = (bf16[1,2,512,512]{3,2,1,0:T(8,128)(2,1)}, bf16[1,2,512,512]{3,2,1,0:T(8,128)(2,1)}, u32[]{:S(2)}, u32[]{:S(2)}) collective-permute-start(bf16[1,2,512,512]{3,2,1,0:T(8,128)(2,1)} %collective-permute-done.3.refs_0_.refs_3_), channel_id=1, source_target_pairs={{0,4},{2,6},{4,0},{6,2},{8,12},{10,14},{12,8},{14,10},{1,5},{3,7},... | collective-permute-start | bytes 3145736 | tf_op jit(solution)/shard_map/ppermute | solution.py:17
  107.8 41.3 %collective-permute-start.8 = (bf16[1,2,512,512]{3,2,1,0:T(8,128)(2,1)}, bf16[1,2,512,512]{3,2,1,0:T(8,128)(2,1)S(1)}, u32[]{:S(2)}, u32[]{:S(2)}) collective-permute-start(bf16[1,2,512,512]{3,2,1,0:T(8,128)(2,1)} %collective-permute-done.4.refs_2_.refs_6_), channel_id=1, source_target_pairs={{0,2},{2,0},{4,6},{6,4},{8,10},{10,8},{12,14},{14,12},{1,3},{3,1},... | collective-permute-start | bytes 3145736 | tf_op jit(solution)/shard_map/ppermute | solution.py:17
  109.2 42.8 %collective-permute-start.9 = (bf16[1,2,512,512]{3,2,1,0:T(8,128)(2,1)}, bf16[1,2,512,512]{3,2,1,0:T(8,128)(2,1)S(1)}, u32[]{:S(2)}, u32[]{:S(2)}) collective-permute-start(bf16[1,2,512,512]{3,2,1,0:T(8,128)(2,1)} %get-tuple-element.28), channel_id=1, source_target_pairs={{0,4},{2,6},{4,0},{6,2},{8,12},{10,14},{12,8},{14,10},{1,5},{3,7},... | collective-permute-start | bytes 3145736 | tf_op jit(solution)/shard_map/ppermute | solution.py:17
  111.8 2.2 %copy-start.14 = (f32[2,1024,512]{2,1,0:T(8,128)S(1)}, f32[2,1024,512]{2,1,0:T(8,128)}, u32[]{:S(2)}) copy-start(f32[2,1024,512]{2,1,0:T(8,128)} %copy-done.13) | copy-start | bytes 12582916
  114.0 7.6 %copy-start.6 = (f32[2,1024,512]{2,1,0:T(8,128)S(1)}, f32[2,1024,512]{2,1,0:T(8,128)}, u32[]{:S(2)}) copy-start(f32[2,1024,512]{2,1,0:T(8,128)} %copy-done.5) | copy-start | bytes 12582916
  119.7 2.0 copy-start.11
  133.4 2.0 copy-start.9
  135.5 20.0 %copy-start.18 = (bf16[1,2,512,512]{3,2,1,0:T(8,128)(2,1)}, bf16[1,2,512,512]{3,2,1,0:T(8,128)(2,1)S(1)}, u32[]{:S(2)}) copy-start(bf16[1,2,512,512]{3,2,1,0:T(8,128)(2,1)S(1)} %collective-permute-done.10.refs_1_.refs_4_) | copy-start | bytes 3145732
  149.1 2.8 %copy-start.22 = (bf16[1,2,512,512]{3,2,1,0:T(8,128)(2,1)}, bf16[1,2,512,512]{3,2,1,0:T(8,128)(2,1)S(1)}, u32[]{:S(2)}) copy-start(bf16[1,2,512,512]{3,2,1,0:T(8,128)(2,1)S(1)} %collective-permute-done.8.refs_7_.refs_0_) | copy-start | bytes 3145732
  151.9 3.5 %copy-start.20 = (bf16[1,2,512,512]{3,2,1,0:T(8,128)(2,1)}, bf16[1,2,512,512]{3,2,1,0:T(8,128)(2,1)S(1)}, u32[]{:S(2)}) copy-start(bf16[1,2,512,512]{3,2,1,0:T(8,128)(2,1)S(1)} %collective-permute-done.9.refs_2_) | copy-start | bytes 3145732
  155.5 23.8 %collective-permute-start.11 = (bf16[1,2,1024,512]{3,2,1,0:T(8,128)(2,1)}, bf16[1,2,1024,512]{3,2,1,0:T(8,128)(2,1)}, u32[]{:S(2)}, u32[]{:S(2)}) collective-permute-start(bf16[1,2,1024,512]{3,2,1,0:T(8,128)(2,1)} %shard_map.117.refs_2_), channel_id=1, source_target_pairs={{0,1},{1,0},{2,3},{3,2},{4,5},{5,4},{6,7},{7,6},{8,9},{9,8},{10,11... | collective-permute-start | bytes 6291464 | tf_op jit(solution)/shard_map/ppermute | solution.py:17
  155.6 29.1 %collective-permute-start.12 = (bf16[1,2,512,512]{3,2,1,0:T(8,128)(2,1)}, bf16[1,2,512,512]{3,2,1,0:T(8,128)(2,1)S(1)}, u32[]{:S(2)}, u32[]{:S(2)}) collective-permute-start(bf16[1,2,512,512]{3,2,1,0:T(8,128)(2,1)} %slice.19), channel_id=1, source_target_pairs={{0,4},{2,6},{4,0},{6,2},{8,12},{10,14},{12,8},{14,10},{1,5},{3,7},... | collective-permute-start | bytes 3145736 | tf_op jit(solution)/shard_map/ppermute | solution.py:17
  157.7 28.6 %collective-permute-start.13 = (bf16[1,2,512,512]{3,2,1,0:T(8,128)(2,1)}, bf16[1,2,512,512]{3,2,1,0:T(8,128)(2,1)}, u32[]{:S(2)}, u32[]{:S(2)}) collective-permute-start(bf16[1,2,512,512]{3,2,1,0:T(8,128)(2,1)} %collective-permute-done.7.refs_0_.refs_5_), channel_id=1, source_target_pairs={{0,2},{2,0},{4,6},{6,4},{8,10},{10,8},{12,14},{14,12},{1,3},{3,1},... | collective-permute-start | bytes 3145736 | tf_op jit(solution)/shard_map/ppermute | solution.py:17
  158.4 3.9 %copy-start.27 = (s32[3]{0:T(128)S(1)}, s32[3]{0:T(128)}, u32[]{:S(2)}) copy-start(s32[3]{0:T(128)} %constant.80.clone) | copy-start | bytes 40
  158.4 3.9 %copy-start.19 = (bf16[1,2,512,512]{3,2,1,0:T(8,128)(2,1)S(1)}, bf16[1,2,512,512]{3,2,1,0:T(8,128)(2,1)}, u32[]{:S(2)}) copy-start(bf16[1,2,512,512]{3,2,1,0:T(8,128)(2,1)} %copy-done.18) | copy-start | bytes 3145732
  158.4 3.9 %copy-start.21 = (bf16[1,2,512,512]{3,2,1,0:T(8,128)(2,1)S(1)}, bf16[1,2,512,512]{3,2,1,0:T(8,128)(2,1)}, u32[]{:S(2)}) copy-start(bf16[1,2,512,512]{3,2,1,0:T(8,128)(2,1)} %copy-done.20) | copy-start | bytes 3145732
  162.2 24.7 %collective-permute-start.14 = (bf16[1,2,1024,512]{3,2,1,0:T(8,128)(2,1)}, bf16[1,2,1024,512]{3,2,1,0:T(8,128)(2,1)}, u32[]{:S(2)}, u32[]{:S(2)}) collective-permute-start(bf16[1,2,1024,512]{3,2,1,0:T(8,128)(2,1)} %shard_map.120.refs_3_), channel_id=1, source_target_pairs={{0,1},{1,0},{2,3},{3,2},{4,5},{5,4},{6,7},{7,6},{8,9},{9,8},{10,11... | collective-permute-start | bytes 6291464 | tf_op jit(solution)/shard_map/ppermute | solution.py:17
  162.3 2.2 %copy-start.12 = (f32[2,1024,512]{2,1,0:T(8,128)S(1)}, f32[2,1024,512]{2,1,0:T(8,128)}, u32[]{:S(2)}) copy-start(f32[2,1024,512]{2,1,0:T(8,128)} %copy-done.11) | copy-start | bytes 12582916
  164.5 14.8 %copy-start.10 = (f32[2,1024,512]{2,1,0:T(8,128)S(1)}, f32[2,1024,512]{2,1,0:T(8,128)}, u32[]{:S(2)}) copy-start(f32[2,1024,512]{2,1,0:T(8,128)} %copy-done.9) | copy-start | bytes 12582916
  164.5 14.8 %copy-start.16 = (bf16[1,2,1024,512]{3,2,1,0:T(8,128)(2,1)S(1)}, bf16[1,2,1024,512]{3,2,1,0:T(8,128)(2,1)}, u32[]{:S(2)}) copy-start(bf16[1,2,1024,512]{3,2,1,0:T(8,128)(2,1)} %shard_map.117.refs_2_) | copy-start | bytes 6291460
  164.5 14.8 %copy-start.23 = (bf16[1,2,512,512]{3,2,1,0:T(8,128)(2,1)S(1)}, bf16[1,2,512,512]{3,2,1,0:T(8,128)(2,1)}, u32[]{:S(2)}) copy-start(bf16[1,2,512,512]{3,2,1,0:T(8,128)(2,1)} %copy-done.22) | copy-start | bytes 3145732
  179.3 7.1 %copy-start.26 = (s32[2]{0:T(128)S(1)}, s32[2]{0:T(128)}, u32[]{:S(2)}) copy-start(s32[2]{0:T(128)} %constant.82.clone) | copy-start | bytes 28
  179.3 7.1 %copy-start.24 = (s32[2]{0:T(128)S(1)}, s32[2]{0:T(128)}, u32[]{:S(2)}) copy-start(s32[2]{0:T(128)} %get-tuple-element.45.ids) | copy-start | bytes 28
  179.3 7.2 %copy-start.1 = (bf16[2,2,1,512,512]{4,3,2,1,0:T(8,128)(2,1)S(1)}, bf16[2,2,1,512,512]{4,3,2,1,0:T(8,128)(2,1)}, u32[]{:S(2)}) copy-start(bf16[2,2,1,512,512]{4,3,2,1,0:T(8,128)(2,1)} %param.11) | copy-start | bytes 6291460
  184.7 4.6 %collective-permute-start.16 = (bf16[1,2,512,512]{3,2,1,0:T(8,128)(2,1)S(1)}, bf16[1,2,512,512]{3,2,1,0:T(8,128)(2,1)}, u32[]{:S(2)}, u32[]{:S(2)}) collective-permute-start(bf16[1,2,512,512]{3,2,1,0:T(8,128)(2,1)S(1)} %collective-permute-done.12.refs_0_.refs_6_), channel_id=1, source_target_pairs={{0,1},{1,0},{2,3},{3,2},{4,5},{5,4},{6,7},{7,6},{8,9},{9,8},{10,11... | collective-permute-start | bytes 3145736 | tf_op jit(solution)/shard_map/ppermute | solution.py:17
  186.3 4.1 %collective-permute-start.15 = (bf16[1,2,512,512]{3,2,1,0:T(8,128)(2,1)}, bf16[1,2,512,512]{3,2,1,0:T(8,128)(2,1)}, u32[]{:S(2)}, u32[]{:S(2)}) collective-permute-start(bf16[1,2,512,512]{3,2,1,0:T(8,128)(2,1)} %collective-permute-done.13.refs_1_.refs_5_), channel_id=1, source_target_pairs={{0,1},{1,0},{2,3},{3,2},{4,5},{5,4},{6,7},{7,6},{8,9},{9,8},{10,11... | collective-permute-start | bytes 3145736 | tf_op jit(solution)/shard_map/ppermute | solution.py:17
  186.5 30.4 %copy-start.25 = (s32[16]{0:T(128)S(1)}, s32[16]{0:T(128)}, u32[]{:S(2)}) copy-start(s32[16]{0:T(128)} %param.12) | copy-start | bytes 196
  190.4 2.2 %copy-start.8 = (f32[2,1024,512]{2,1,0:T(8,128)S(1)}, f32[2,1024,512]{2,1,0:T(8,128)}, u32[]{:S(2)}) copy-start(f32[2,1024,512]{2,1,0:T(8,128)} %copy-done.7) | copy-start | bytes 12582916
  202.4 2.1 collective-permute-start.17
  203.1 3.7 %collective-permute-start.18 = (f32[2,2,512]{2,1,0:T(2,128)S(1)}, f32[2,2,512]{2,1,0:T(2,128)S(1)}, u32[]{:S(2)}, u32[]{:S(2)}) collective-permute-start(f32[2,2,512]{2,1,0:T(2,128)S(1)} %pad_maximum_fusion), channel_id=1, source_target_pairs={{0,2},{1,3},{2,0},{3,1},{4,6},{5,7},{6,4},{7,5},{8,10},{9,11},{10,... | collective-permute-start | bytes 24584 | tf_op jit(solution)/shard_map/ppermute | solution.py:17
  204.1 3.1 %collective-permute-start.19 = (f32[2,2,512]{2,1,0:T(2,128)S(1)}, f32[2,2,512]{2,1,0:T(2,128)S(1)}, u32[]{:S(2)}, u32[]{:S(2)}) collective-permute-start(f32[2,2,512]{2,1,0:T(2,128)S(1)} %pad_maximum_fusion), channel_id=1, source_target_pairs={{0,3},{1,2},{2,1},{3,0},{4,7},{5,6},{6,5},{7,4},{8,11},{9,10},{10,... | collective-permute-start | bytes 24584 | tf_op jit(solution)/shard_map/ppermute | solution.py:17
  207.2 4.5 %collective-permute-start.20 = (f32[2,2,512]{2,1,0:T(2,128)S(1)}, f32[2,2,512]{2,1,0:T(2,128)S(1)}, u32[]{:S(2)}, u32[]{:S(2)}) collective-permute-start(f32[2,2,512]{2,1,0:T(2,128)S(1)} %add_add_fusion.1), channel_id=1, source_target_pairs={{0,4},{1,5},{2,6},{3,7},{4,0},{5,1},{6,2},{7,3},{8,12},{9,13},{10,... | collective-permute-start | bytes 24584 | tf_op jit(solution)/shard_map/ppermute | solution.py:17
  207.7 4.6 %collective-permute-start.21 = (f32[2,2,512]{2,1,0:T(2,128)S(1)}, f32[2,2,512]{2,1,0:T(2,128)S(1)}, u32[]{:S(2)}, u32[]{:S(2)}) collective-permute-start(f32[2,2,512]{2,1,0:T(2,128)S(1)} %add_add_fusion.1), channel_id=1, source_target_pairs={{0,8},{1,9},{2,10},{3,11},{4,12},{5,13},{6,14},{7,15},{8,0},{9,1},... | collective-permute-start | bytes 24584 | tf_op jit(solution)/shard_map/ppermute | solution.py:17
  210.6 5.4 %collective-permute-start.22 = (f32[2,2,512]{2,1,0:T(2,128)S(1)}, f32[2,2,512]{2,1,0:T(2,128)S(1)}, u32[]{:S(2)}, u32[]{:S(2)}) collective-permute-start(f32[2,2,512]{2,1,0:T(2,128)S(1)} %add_add_fusion.1), channel_id=1, source_target_pairs={{0,12},{1,13},{2,14},{3,15},{4,8},{5,9},{6,10},{7,11},{8,4},{9,5},... | collective-permute-start | bytes 24584 | tf_op jit(solution)/shard_map/ppermute | solution.py:17
  (5 other events, 7.5 us)

commit v4 on v3

--- a/solution.py
+++ b/solution.py
@@ -8,7 +8,7 @@
 from jax.experimental.pallas import tpu as pltpu
 from jax.sharding import PartitionSpec as P
 
-VMEM_LIMIT = 28 * 1024 * 1024
+VMEM_LIMIT = 60 * 1024 * 1024
 HINT = pl.CostEstimate(flops=1, bytes_accessed=1, transcendentals=0)
 
 
@@ -226,19 +226,24 @@
     ids = lambda *wanted: me ^ jnp.array(wanted, jnp.int32)
 
     own = replicas[:, :, 0]
-    x = swap(own, "row", 1)
+    holds = holder == col
+    where_a = jnp.where(holds, 0, 1) * jnp.ones_like(masks)
+
     own_a = own[0:1]
+    x = swap(after(own, own_a), "row", 1)
     pa = swap(own_a, "row", 4)
     na = swap(own_a, "row", 2)
-    own_b = own[1:2]
-    x, pa, na, own_b = lax.optimization_barrier((x, pa, na, own_b))
+    a0 = add_field(cross, 0, ids(0), [own])
+    a1 = add_field(cross, 1, ids(0), [own])
+    own_b = after(own, a0)[1:2]
+    x, pa, na, own_b, a0, a1 = lax.optimization_barrier((x, pa, na, own_b, a0, a1))
 
     pb = swap(own_b, "row", 4)
     ga = swap(pa, "row", 2)
     xpa = swap(pa, "row", 1)
     xna = swap(na, "row", 1)
-    a0 = add_field(cross, 0, ids(0, 1, 2, 4), [own, x, na, pa])
-    a1 = add_field(cross, 1, ids(0, 1), [own, x])
+    a0 = add_field(cross, 0, ids(1, 2, 4), [x, na, pa], a0)
+    a1 = add_field(cross, 1, ids(1), [x], a1)
     x_b = x[1:2]
     pb, ga, xpa, xna, a0, a1, x_b, own_b = lax.optimization_barrier(
         (pb, ga, xpa, xna, a0, a1, x_b, own_b)
@@ -246,27 +251,24 @@
 
     gb = swap(pb, "row", 2)
     xga = swap(ga, "row", 1)
-    nb = swap(own_b, "row", 2)
     b0 = add_field(cross, 0, ids(3, 5, 6), [xna, xpa, ga], a0)
     xpb = swap(pb, "row", 1)
+    nb = swap(own_b, "row", 2)
     a1 = add_field(cross, 1, ids(4), [pb], a1)
-    gb, xga, nb, xpb, a1, b0 = lax.optimization_barrier((gb, xga, nb, xpb, a1, b0))
-
-    d = swap(x_b, "row", 2)
+    d = swap(after(x_b, gb), "row", 2)
     xgb = swap(gb, "row", 1)
+    gb, nb, xga, xpb, b0, a1 = lax.optimization_barrier((gb, nb, xga, xpb, b0, a1))
+
     b1 = add_field(cross, 1, ids(6, 5, 2), [gb, xpb, nb], a1)
-
-    holds = holder == col
-    mine_a = pick_rows(0, masks, [own, x, na, xna, pa, xpa, ga, xga])
+    mine_a = pick_rows(0, after(masks, b1), [own, x, na, xna, pa, xpa, ga, xga])
     other_a = swap(mine_a, "col", 1)
-    where_a = jnp.where(holds, 0, 1) * jnp.ones_like(masks)
     c0 = finish(cross, 0, jnp.concatenate([ids(7), where_a]), [xga], b0, mine_a, other_a, [])
 
     order = jnp.where(masks == 3, 7, masks - (masks > 3))
     mine_b = pick_rows(1, order, [own, x, nb, pb, xpb, gb])
     other_b = swap(mine_b, "col", 1)
     late = [xgb, d]
-    late = late + [swap(after(piece, b1, c0), "col", 1) for piece in late]
+    late = late + [swap(after(piece, b1, mine_b), "col", 1) for piece in late]
     where_b = jnp.where(masks == 7, jnp.where(holds, 2, 4), where_a)
     where_b = jnp.where(masks == 3, jnp.where(holds, 3, 5), where_b)
     c1 = finish(
@@ -299,7 +301,8 @@
         and cross_spectra.shape[2] == 2 * replicas.shape[3]
     )
     numer = (numer_by_swaps if doubling else numer_by_gather)(cross_spectra, replicas)
-    numer, norms = sum_all(jnp.stack([numer, norms]))
+    sums = sum_all(jnp.concatenate([numer, norms]))
+    numer, norms = sums[:fnum], sums[fnum:]
     beam = numer / (norms + 1e-06)
     width = sources // lax.axis_size("col")
     beam_half = lax.dynamic_slice_in_dim(beam, lax.axis_index("col") * width, width, 1)

time: 218 us -> 236 us (1.083)
  Pallas kernels: 72.2 us -> 96.6 us
  local copies, waits for them, and re-layouts: 26.5 us -> 7.9 us
  waiting for transfers between devices: 87.7 us -> 97.6 us
  other arithmetic: 1.39 us -> 4.9 us
    pallas_call x7 -> x9, Pallas kernels: 64.9 us -> 89.3 us  [call(): pl.pallas_call(kernel, out_shape=out_shape, grid_spec=pltpu.PrefetchScala...]
    unnamed x60 -> x26, local copies, waits for them, and re-layouts: 22.1 us -> 1.02 us
    ppermute x23, waiting for transfers between devices: 87.7 us -> 97.6 us  [swap(): lax.ppermute(value, axis, [(source, source ^ mask) for source in range(si...]
  transfers between devices with their start and end apart: 23 -> 23, of which waited for: 13 -> 13; matrix products, arithmetic and copies ran while one was open for 2% -> 3% of each run, Pallas kernels for 28% -> 30%
where the time goes in v4:
time: 236 us
  waiting for transfers between devices  97.6 us (41%)
  Pallas kernels  96.6 us (41%)
  starting transfers between devices  27.2 us (12%)
  local copies, waits for them, and re-layouts  7.9 us (3%)
  other arithmetic  4.9 us (2%)
    ppermute x23, waiting for transfers between devices, swap(): lax.ppermute(value, axis, [(source, source ^ mask) for source in range(si...  97.6 us
    pallas_call x9, Pallas kernels, call(): pl.pallas_call(kernel, out_shape=out_shape, grid_spec=pltpu.PrefetchScala...  89.3 us
    ppermute x23, starting transfers between devices, swap(): lax.ppermute(value, axis, [(source, source ^ mask) for source in range(si...  27.2 us
    pallas_call x2, Pallas kernels, pick_rows(): pl.pallas_call(functools.partial(pick_kernel, freq), out_shape=jax.ShapeD...  7.3 us
  transfers between devices with their start and end apart: 23, of which 13 were waited for; matrix products, arithmetic and copies ran while one was open for 3% of the time, Pallas kernels for 30%

profile of v4, /device:TPU:0, one launch (start us, length us, event | category | flops | bytes accessed | tf_op | source)
XLA Modules:
  0.0 235.8 jit_solution(9707051563250436536)
XLA Ops:
  0.6 2.3 slice_bitcast_fusion
  2.9 2.9 %collective-permute-start = (bf16[2,2,512,512]{3,2,1,0:T(8,128)(2,1)}, bf16[2,2,512,512]{3,2,1,0:T(8,128)(2,1)}, u32[]{:S(2)}, u32[]{:S(2)}) collective-permute-start(bf16[2,2,512,512]{3,2,1,0:T(8,128)(2,1)} %bitcast.17), channel_id=1, source_target_pairs={{0,2},{2,0},{4,6},{6,4},{8,10},{10,8},{12,14},{14,12},{1,3},{3,1},... | collective-permute-start | bytes 6291464 | tf_op jit(solution)/shard_map/ppermute | solution.py:17
  5.9 2.6 %collective-permute-start.1 = (bf16[1,2,512,512]{3,2,1,0:T(8,128)(2,1)}, bf16[1,2,512,512]{3,2,1,0:T(8,128)(2,1)S(1)}, u32[]{:S(2)}, u32[]{:S(2)}) collective-permute-start(bf16[1,2,512,512]{3,2,1,0:T(8,128)(2,1)} %slice_bitcast_fusion), channel_id=1, source_target_pairs={{0,8},{2,10},{4,12},{6,14},{8,0},{10,2},{12,4},{14,6},{1,9},{3,11}... | collective-permute-start | bytes 3145736 | tf_op jit(solution)/shard_map/ppermute | solution.py:17
  8.5 1.6 collective-permute-start.2
  10.0 6.4 %shard_map.131.refs_3_ = f32[2,1024,512]{2,1,0:T(8,128)} custom-call(s32[1]{0:T(128)} %bitcast.ids, bf16[2,2,1024,4096]{3,2,1,0:T(8,128)(2,1)} %r_ref.17, bf16[2,2,512,512]{3,2,1,0:T(8,128)(2,1)} %bitcast.18), custom_call_target="tpu_custom_call" | custom-call | flops 1 | bytes 1 | tf_op jit(solution)/shard_map/pallas_call | solution.py:124
  16.4 6.6 %shard_map.132.refs_1_ = f32[2,1024,512]{2,1,0:T(8,128)} custom-call(s32[1]{0:T(128)} %bitcast.ids, bf16[2,2,1024,4096]{3,2,1,0:T(8,128)(2,1)} %r_ref.17, bf16[2,2,512,512]{3,2,1,0:T(8,128)(2,1)} %bitcast.19), custom_call_target="tpu_custom_call" | custom-call | flops 1 | bytes 1 | tf_op jit(solution)/shard_map/pallas_call | solution.py:124
  23.0 1.0 slice.20
  24.1 30.1 %collective-permute-done.1.refs_2_.refs_4_ = bf16[1,2,512,512]{3,2,1,0:T(8,128)(2,1)S(1)} collective-permute-done((bf16[1,2,512,512]{3,2,1,0:T(8,128)(2,1)}, bf16[1,2,512,512]{3,2,1,0:T(8,128)(2,1)S(1)}, u32[]{:S(2)}, u32[]{:S(2)}) %collective-permute-start.1) | collective-permute-done | bytes 1048608 | tf_op jit(solution)/shard_map/ppermute | solution.py:17
  54.5 1.4 collective-permute-start.4
  55.9 0.5 collective-permute-start.5
  56.4 1.5 collective-permute-start.6
  57.9 2.3 collective-permute-start.3
  60.7 13.9 %shard_map.133.refs_3_ = f32[2,1024,512]{2,1,0:T(8,128)} custom-call(s32[3]{0:T(128)} %broadcast_xor_fusion.3.ids, bf16[2,2,1024,4096]{3,2,1,0:T(8,128)(2,1)} %r_ref.17, bf16[2,2,512,512]{3,2,1,0:T(8,128)(2,1)} %collective-permute-done.refs_0_.refs_1_, bf16[1,2,512,512]{3,2,1,0:T(8,128)(2,1)} %collective-permute-done.2.refs_1_.refs_2_, ...), custom_call_target="tpu_custom_call" | custom-call | flops 1 | bytes 1 | tf_op jit(solution)/shard_map/pallas_call | solution.py:124
  74.7 7.2 %shard_map.134.refs_1_ = f32[2,1024,512]{2,1,0:T(8,128)} custom-call(s32[1]{0:T(128)S(6)} %xor.54.ids, bf16[2,2,1024,4096]{3,2,1,0:T(8,128)(2,1)} %r_ref.17, bf16[2,2,512,512]{3,2,1,0:T(8,128)(2,1)} %collective-permute-done.refs_0_.refs_1_, f32[2,1024,512]{2,1,0:T(8,128)} %shard_map.132.refs_1_), custom_call_target="tpu_custom_call" | custom-call | flops 1 | bytes 1 | tf_op jit(solution)/shard_map/pallas_call | solution.py:124
  81.9 2.3 slice.21
  84.2 14.6 %collective-permute-done.4.refs_2_.refs_6_ = bf16[1,2,512,512]{3,2,1,0:T(8,128)(2,1)S(1)} collective-permute-done((bf16[1,2,512,512]{3,2,1,0:T(8,128)(2,1)S(1)}, bf16[1,2,512,512]{3,2,1,0:T(8,128)(2,1)S(1)}, u32[]{:S(2)}, u32[]{:S(2)}) %collective-permute-start.4) | collective-permute-done | bytes 1048608 | tf_op jit(solution)/shard_map/ppermute | solution.py:17
  98.8 3.5 %collective-permute-done.6.refs_0_.refs_3_ = bf16[1,2,512,512]{3,2,1,0:T(8,128)(2,1)} collective-permute-done((bf16[1,2,512,512]{3,2,1,0:T(8,128)(2,1)}, bf16[1,2,512,512]{3,2,1,0:T(8,128)(2,1)}, u32[]{:S(2)}, u32[]{:S(2)}) %collective-permute-start.6) | collective-permute-done | bytes 1048608 | tf_op jit(solution)/shard_map/ppermute | solution.py:17
  102.3 3.3 %collective-permute-done.3.refs_0_.refs_3_ = bf16[1,2,512,512]{3,2,1,0:T(8,128)(2,1)} collective-permute-done((bf16[1,2,512,512]{3,2,1,0:T(8,128)(2,1)}, bf16[1,2,512,512]{3,2,1,0:T(8,128)(2,1)}, u32[]{:S(2)}, u32[]{:S(2)}) %collective-permute-start.3) | collective-permute-done | bytes 1048608 | tf_op jit(solution)/shard_map/ppermute | solution.py:17
  106.1 2.0 collective-permute-start.8
  108.1 1.5 collective-permute-start.9
  109.6 0.7 compare_select_fusion.1
  110.3 0.5 broadcast_xor_fusion.2.ids
  111.4 7.2 %shard_map.136.refs_3_ = f32[2,1024,512]{2,1,0:T(8,128)} custom-call(s32[1]{0:T(128)S(6)} %xor.56.ids, bf16[2,2,1024,4096]{3,2,1,0:T(8,128)(2,1)} %r_ref.17, bf16[1,2,512,512]{3,2,1,0:T(8,128)(2,1)} %collective-permute-done.3.refs_0_.refs_3_, f32[2,1024,512]{2,1,0:T(8,128)} %shard_map.134.refs_1_), custom_call_target="tpu_custom_call" | custom-call | flops 1 | bytes 1 | tf_op jit(solution)/shard_map/pallas_call | solution.py:124
  118.6 13.8 %shard_map.135.refs_1_ = f32[2,1024,512]{2,1,0:T(8,128)} custom-call(s32[3]{0:T(128)} %broadcast_xor_fusion.2.ids, bf16[2,2,1024,4096]{3,2,1,0:T(8,128)(2,1)} %r_ref.17, bf16[1,2,512,512]{3,2,1,0:T(8,128)(2,1)} %collective-permute-done.6.refs_0_.refs_3_, bf16[1,2,512,512]{3,2,1,0:T(8,128)(2,1)} %collective-permute-done.5.refs_1_.refs_5_, ...), custom_call_target="tpu_custom_call" | custom-call | flops 1 | bytes 1 | tf_op jit(solution)/shard_map/pallas_call | solution.py:124
  132.5 17.9 %collective-permute-done.8.refs_2_ = bf16[1,2,512,512]{3,2,1,0:T(8,128)(2,1)S(1)} collective-permute-done((bf16[1,2,512,512]{3,2,1,0:T(8,128)(2,1)}, bf16[1,2,512,512]{3,2,1,0:T(8,128)(2,1)S(1)}, u32[]{:S(2)}, u32[]{:S(2)}) %collective-permute-start.8) | collective-permute-done | bytes 1048608 | tf_op jit(solution)/shard_map/ppermute | solution.py:17
  150.4 1.0 copy-done.6
  151.4 13.9 %shard_map.137.refs_2_ = f32[2,1024,512]{2,1,0:T(8,128)} custom-call(s32[3]{0:T(128)} %broadcast_xor_fusion.1.ids, bf16[2,2,1024,4096]{3,2,1,0:T(8,128)(2,1)} %r_ref.17, bf16[1,2,512,512]{3,2,1,0:T(8,128)(2,1)} %collective-permute-done.7.refs_0_.refs_5_, bf16[1,2,512,512]{3,2,1,0:T(8,128)(2,1)} %copy-done.5, bf16[1,2,512,512]{3,2,1,0:T(8,128)(2,1)} %copy-done.6, ...), custom_call_target="tpu_custom_call" | custom-call | flops 1 | bytes 1 | tf_op jit(solution)/shard_map/pallas_call | solution.py:124
  165.3 1.4 collective-permute-start.12
  166.7 3.6 %shard_map.138.refs_2_ = bf16[1,2,1024,512]{3,2,1,0:T(8,128)(2,1)} custom-call(s32[2]{0:T(128)} %get-tuple-element.49.ids, bf16[2,2,512,512]{3,2,1,0:T(8,128)(2,1)} %bitcast.20, bf16[2,2,512,512]{3,2,1,0:T(8,128)(2,1)} %collective-permute-done.refs_0_.refs_1_, bf16[1,2,512,512]{3,2,1,0:T(8,128)(2,1)} %collective-permute-done.2.refs_1_.refs_2_, ...), custom_call_target="tpu_custom_call" | custom-call | flops 1 | bytes 1 | tf_op jit(solution)/shard_map/pallas_call | solution.py:204
  170.4 1.6 collective-permute-start.13
  172.0 3.7 %shard_map.140.refs_3_ = bf16[1,2,1024,512]{3,2,1,0:T(8,128)(2,1)} custom-call(s32[2]{0:T(128)} %get-tuple-element.56.ids, bf16[2,2,512,512]{3,2,1,0:T(8,128)(2,1)} %bitcast.21, bf16[2,2,512,512]{3,2,1,0:T(8,128)(2,1)} %collective-permute-done.refs_0_.refs_1_, bf16[1,2,512,512]{3,2,1,0:T(8,128)(2,1)} %copy-done.6, ...), custom_call_target="tpu_custom_call" | custom-call | flops 1 | bytes 1 | tf_op jit(solution)/shard_map/pallas_call | solution.py:204
  175.9 11.4 %collective-permute-done.12.refs_0_.refs_6_ = bf16[1,2,512,512]{3,2,1,0:T(8,128)(2,1)S(1)} collective-permute-done((bf16[1,2,512,512]{3,2,1,0:T(8,128)(2,1)}, bf16[1,2,512,512]{3,2,1,0:T(8,128)(2,1)S(1)}, u32[]{:S(2)}, u32[]{:S(2)}) %collective-permute-start.12) | collective-permute-done | bytes 1048608 | tf_op jit(solution)/shard_map/ppermute | solution.py:17
  187.3 9.0 %collective-permute-done.13.refs_1_.refs_5_ = bf16[1,2,512,512]{3,2,1,0:T(8,128)(2,1)} collective-permute-done((bf16[1,2,512,512]{3,2,1,0:T(8,128)(2,1)}, bf16[1,2,512,512]{3,2,1,0:T(8,128)(2,1)}, u32[]{:S(2)}, u32[]{:S(2)}) %collective-permute-start.13) | collective-permute-done | bytes 1048608 | tf_op jit(solution)/shard_map/ppermute | solution.py:17
  196.3 0.6 concatenate.9.ids
  196.9 0.6 pad_add_fusion.1.ids
  197.9 9.1 %shard_map.139 = f32[8,512]{1,0:T(8,128)} custom-call(s32[3]{0:T(128)} %concatenate.9.ids, bf16[2,2,1024,4096]{3,2,1,0:T(8,128)(2,1)} %r_ref.17, bf16[1,2,512,512]{3,2,1,0:T(8,128)(2,1)} %collective-permute-done.9.refs_7_.refs_0_, f32[2,1024,512]{2,1,0:T(8,128)} %shard_map.135.refs_1_, bf16[1,2,1024,512]{3,2,1,0:T(8,128)(2,1)} %shard_map.138.refs_2_, ...), custom_call_target="tpu_custom_call" | custom-call | flops 1 | bytes 1 | tf_op jit(solution)/shard_map/pallas_call | solution.py:124
  207.0 0.7 reduce_sum.27
  207.8 11.2 %shard_map.141 = f32[8,512]{1,0:T(8,128)} custom-call(s32[4]{0:T(128)} %pad_add_fusion.1.ids, bf16[2,2,1024,4096]{3,2,1,0:T(8,128)(2,1)} %r_ref.17, bf16[1,2,512,512]{3,2,1,0:T(8,128)(2,1)} %copy-done.4, bf16[1,2,512,512]{3,2,1,0:T(8,128)(2,1)} %collective-permute-done.13.refs_1_.refs_5_, f32[2,1024,512]{2,1,0:T(8,128)} %shard_map.137.refs_2_, ...), custom_call_target="tpu_custom_call" | custom-call | flops 1 | bytes 1 | tf_op jit(solution)/shard_map/pallas_call | solution.py:124
  219.0 0.7 reduce_sum.28
  219.8 0.6 collective-permute-start.17
  220.3 1.5 collective-permute-start.18
  221.8 2.2 collective-permute-done.18
  224.0 1.0 collective-permute-done.19
  225.4 3.4 %collective-permute-start.21 = (f32[4,512]{1,0:T(4,128)S(1)}, f32[4,512]{1,0:T(4,128)S(1)}, u32[]{:S(2)}, u32[]{:S(2)}) collective-permute-start(f32[4,512]{1,0:T(4,128)S(1)} %add_add_fusion.1), channel_id=1, source_target_pairs={{0,8},{1,9},{2,10},{3,11},{4,12},{5,13},{6,14},{7,15},{8,0},{9,1},... | collective-permute-start | bytes 24584 | tf_op jit(solution)/shard_map/ppermute | solution.py:17
  228.8 1.2 collective-permute-start.22
  230.4 3.8 %collective-permute-done.22 = f32[4,512]{1,0:T(4,128)S(1)} collective-permute-done((f32[4,512]{1,0:T(4,128)S(1)}, f32[4,512]{1,0:T(4,128)S(1)}, u32[]{:S(2)}, u32[]{:S(2)}) %collective-permute-start.22) | collective-permute-done | bytes 8224 | tf_op jit(solution)/shard_map/ppermute | solution.py:17
  234.4 0.6 constant_dynamic-slice_fusion
  235.0 0.8 fusion
  (56 shorter events, 3.8 us)
Async XLA Ops:
  2.9 51.5 %collective-permute-start = (bf16[2,2,512,512]{3,2,1,0:T(8,128)(2,1)}, bf16[2,2,512,512]{3,2,1,0:T(8,128)(2,1)}, u32[]{:S(2)}, u32[]{:S(2)}) collective-permute-start(bf16[2,2,512,512]{3,2,1,0:T(8,128)(2,1)} %bitcast.17), channel_id=1, source_target_pairs={{0,2},{2,0},{4,6},{6,4},{8,10},{10,8},{12,14},{14,12},{1,3},{3,1},... | collective-permute-start | bytes 6291464 | tf_op jit(solution)/shard_map/ppermute | solution.py:17
  5.9 48.3 %collective-permute-start.1 = (bf16[1,2,512,512]{3,2,1,0:T(8,128)(2,1)}, bf16[1,2,512,512]{3,2,1,0:T(8,128)(2,1)S(1)}, u32[]{:S(2)}, u32[]{:S(2)}) collective-permute-start(bf16[1,2,512,512]{3,2,1,0:T(8,128)(2,1)} %slice_bitcast_fusion), channel_id=1, source_target_pairs={{0,8},{2,10},{4,12},{6,14},{8,0},{10,2},{12,4},{14,6},{1,9},{3,11}... | collective-permute-start | bytes 3145736 | tf_op jit(solution)/shard_map/ppermute | solution.py:17
  8.5 46.0 %collective-permute-start.2 = (bf16[1,2,512,512]{3,2,1,0:T(8,128)(2,1)}, bf16[1,2,512,512]{3,2,1,0:T(8,128)(2,1)}, u32[]{:S(2)}, u32[]{:S(2)}) collective-permute-start(bf16[1,2,512,512]{3,2,1,0:T(8,128)(2,1)} %slice_bitcast_fusion), channel_id=1, source_target_pairs={{0,4},{2,6},{4,0},{6,2},{8,12},{10,14},{12,8},{14,10},{1,5},{3,7},... | collective-permute-start | bytes 3145736 | tf_op jit(solution)/shard_map/ppermute | solution.py:17
  16.4 6.6 %copy-start = (bf16[2,2,1,512,512]{4,3,2,1,0:T(8,128)(2,1)S(1)}, bf16[2,2,1,512,512]{4,3,2,1,0:T(8,128)(2,1)}, u32[]{:S(2)}) copy-start(bf16[2,2,1,512,512]{4,3,2,1,0:T(8,128)(2,1)} %param.13) | copy-start | bytes 6291460
  16.4 43.8 %copy-start.12 = (s32[3]{0:T(128)S(1)}, s32[3]{0:T(128)}, u32[]{:S(2)}) copy-start(s32[3]{0:T(128)} %constant.79.clone) | copy-start | bytes 40
  54.2 6.6 %copy-start.2 = (bf16[1,2,512,512]{3,2,1,0:T(8,128)(2,1)}, bf16[1,2,512,512]{3,2,1,0:T(8,128)(2,1)S(1)}, u32[]{:S(2)}) copy-start(bf16[1,2,512,512]{3,2,1,0:T(8,128)(2,1)S(1)} %collective-permute-done.1.refs_2_.refs_4_) | copy-start | bytes 3145732
  54.5 44.3 %collective-permute-start.4 = (bf16[1,2,512,512]{3,2,1,0:T(8,128)(2,1)S(1)}, bf16[1,2,512,512]{3,2,1,0:T(8,128)(2,1)S(1)}, u32[]{:S(2)}, u32[]{:S(2)}) collective-permute-start(bf16[1,2,512,512]{3,2,1,0:T(8,128)(2,1)S(1)} %collective-permute-done.1.refs_2_.refs_4_), channel_id=1, source_target_pairs={{0,4},{2,6},{4,0},{6,2},{8,12},{10,14},{12,8},{14,10},{1,5},{3,7},... | collective-permute-start | bytes 3145736 | tf_op jit(solution)/shard_map/ppermute | solution.py:17
  55.9 42.9 %collective-permute-start.5 = (bf16[1,2,512,512]{3,2,1,0:T(8,128)(2,1)S(1)}, bf16[1,2,512,512]{3,2,1,0:T(8,128)(2,1)}, u32[]{:S(2)}, u32[]{:S(2)}) collective-permute-start(bf16[1,2,512,512]{3,2,1,0:T(8,128)(2,1)S(1)} %collective-permute-done.1.refs_2_.refs_4_), channel_id=1, source_target_pairs={{0,2},{2,0},{4,6},{6,4},{8,10},{10,8},{12,14},{14,12},{1,3},{3,1},... | collective-permute-start | bytes 3145736 | tf_op jit(solution)/shard_map/ppermute | solution.py:17
  56.4 45.8 %collective-permute-start.6 = (bf16[1,2,512,512]{3,2,1,0:T(8,128)(2,1)}, bf16[1,2,512,512]{3,2,1,0:T(8,128)(2,1)}, u32[]{:S(2)}, u32[]{:S(2)}) collective-permute-start(bf16[1,2,512,512]{3,2,1,0:T(8,128)(2,1)} %collective-permute-done.2.refs_1_.refs_2_), channel_id=1, source_target_pairs={{0,2},{2,0},{4,6},{6,4},{8,10},{10,8},{12,14},{14,12},{1,3},{3,1},... | collective-permute-start | bytes 3145736 | tf_op jit(solution)/shard_map/ppermute | solution.py:17
  57.9 47.6 %collective-permute-start.3 = (bf16[1,2,512,512]{3,2,1,0:T(8,128)(2,1)}, bf16[1,2,512,512]{3,2,1,0:T(8,128)(2,1)}, u32[]{:S(2)}, u32[]{:S(2)}) collective-permute-start(bf16[1,2,512,512]{3,2,1,0:T(8,128)(2,1)} %slice.20), channel_id=1, source_target_pairs={{0,8},{2,10},{4,12},{6,14},{8,0},{10,2},{12,4},{14,6},{1,9},{3,11}... | collective-permute-start | bytes 3145736 | tf_op jit(solution)/shard_map/ppermute | solution.py:17
  74.6 35.7 %copy-start.11 = (s32[3]{0:T(128)S(1)}, s32[3]{0:T(128)}, u32[]{:S(2)}) copy-start(s32[3]{0:T(128)} %constant.81.clone) | copy-start | bytes 40
  74.6 36.2 %copy-start.10 = (s32[3]{0:T(128)S(1)}, s32[3]{0:T(128)}, u32[]{:S(2)}) copy-start(s32[3]{0:T(128)} %constant.83.clone) | copy-start | bytes 40
  98.8 19.8 %copy-start.3 = (bf16[1,2,512,512]{3,2,1,0:T(8,128)(2,1)}, bf16[1,2,512,512]{3,2,1,0:T(8,128)(2,1)S(1)}, u32[]{:S(2)}) copy-start(bf16[1,2,512,512]{3,2,1,0:T(8,128)(2,1)S(1)} %collective-permute-done.4.refs_2_.refs_6_) | copy-start | bytes 3145732
  105.6 26.8 %collective-permute-start.10 = (bf16[1,2,512,512]{3,2,1,0:T(8,128)(2,1)}, bf16[1,2,512,512]{3,2,1,0:T(8,128)(2,1)S(1)}, u32[]{:S(2)}, u32[]{:S(2)}) collective-permute-start(bf16[1,2,512,512]{3,2,1,0:T(8,128)(2,1)} %collective-permute-done.3.refs_0_.refs_3_), channel_id=1, source_target_pairs={{0,2},{2,0},{4,6},{6,4},{8,10},{10,8},{12,14},{14,12},{1,3},{3,1},... | collective-permute-start | bytes 3145736 | tf_op jit(solution)/shard_map/ppermute | solution.py:17
  106.1 26.4 %collective-permute-start.7 = (bf16[1,2,512,512]{3,2,1,0:T(8,128)(2,1)}, bf16[1,2,512,512]{3,2,1,0:T(8,128)(2,1)}, u32[]{:S(2)}, u32[]{:S(2)}) collective-permute-start(bf16[1,2,512,512]{3,2,1,0:T(8,128)(2,1)} %collective-permute-done.3.refs_0_.refs_3_), channel_id=1, source_target_pairs={{0,4},{2,6},{4,0},{6,2},{8,12},{10,14},{12,8},{14,10},{1,5},{3,7},... | collective-permute-start | bytes 3145736 | tf_op jit(solution)/shard_map/ppermute | solution.py:17
  106.1 44.3 %collective-permute-start.8 = (bf16[1,2,512,512]{3,2,1,0:T(8,128)(2,1)}, bf16[1,2,512,512]{3,2,1,0:T(8,128)(2,1)S(1)}, u32[]{:S(2)}, u32[]{:S(2)}) collective-permute-start(bf16[1,2,512,512]{3,2,1,0:T(8,128)(2,1)} %slice.20), channel_id=1, source_target_pairs={{0,4},{2,6},{4,0},{6,2},{8,12},{10,14},{12,8},{14,10},{1,5},{3,7},... | collective-permute-start | bytes 3145736 | tf_op jit(solution)/shard_map/ppermute | solution.py:17
  108.1 42.3 %collective-permute-start.9 = (bf16[1,2,512,512]{3,2,1,0:T(8,128)(2,1)S(1)}, bf16[1,2,512,512]{3,2,1,0:T(8,128)(2,1)}, u32[]{:S(2)}, u32[]{:S(2)}) collective-permute-start(bf16[1,2,512,512]{3,2,1,0:T(8,128)(2,1)S(1)} %collective-permute-done.4.refs_2_.refs_6_), channel_id=1, source_target_pairs={{0,2},{2,0},{4,6},{6,4},{8,10},{10,8},{12,14},{14,12},{1,3},{3,1},... | collective-permute-start | bytes 3145736 | tf_op jit(solution)/shard_map/ppermute | solution.py:17
  132.4 18.0 %copy-start.5 = (bf16[1,2,512,512]{3,2,1,0:T(8,128)(2,1)}, bf16[1,2,512,512]{3,2,1,0:T(8,128)(2,1)S(1)}, u32[]{:S(2)}) copy-start(bf16[1,2,512,512]{3,2,1,0:T(8,128)(2,1)S(1)} %collective-permute-done.10.refs_1_.refs_4_) | copy-start | bytes 3145732
  150.4 1.0 copy-start.6
  165.3 22.0 %collective-permute-start.12 = (bf16[1,2,512,512]{3,2,1,0:T(8,128)(2,1)}, bf16[1,2,512,512]{3,2,1,0:T(8,128)(2,1)S(1)}, u32[]{:S(2)}, u32[]{:S(2)}) collective-permute-start(bf16[1,2,512,512]{3,2,1,0:T(8,128)(2,1)} %slice.21), channel_id=1, source_target_pairs={{0,4},{2,6},{4,0},{6,2},{8,12},{10,14},{12,8},{14,10},{1,5},{3,7},... | collective-permute-start | bytes 3145736 | tf_op jit(solution)/shard_map/ppermute | solution.py:17
  170.3 27.6 %collective-permute-start.11 = (bf16[1,2,1024,512]{3,2,1,0:T(8,128)(2,1)}, bf16[1,2,1024,512]{3,2,1,0:T(8,128)(2,1)}, u32[]{:S(2)}, u32[]{:S(2)}) collective-permute-start(bf16[1,2,1024,512]{3,2,1,0:T(8,128)(2,1)} %shard_map.138.refs_2_), channel_id=1, source_target_pairs={{0,1},{1,0},{2,3},{3,2},{4,5},{5,4},{6,7},{7,6},{8,9},{9,8},{10,11... | collective-permute-start | bytes 6291464 | tf_op jit(solution)/shard_map/ppermute | solution.py:17
  170.4 25.9 %collective-permute-start.13 = (bf16[1,2,512,512]{3,2,1,0:T(8,128)(2,1)}, bf16[1,2,512,512]{3,2,1,0:T(8,128)(2,1)}, u32[]{:S(2)}, u32[]{:S(2)}) collective-permute-start(bf16[1,2,512,512]{3,2,1,0:T(8,128)(2,1)} %collective-permute-done.7.refs_0_.refs_5_), channel_id=1, source_target_pairs={{0,2},{2,0},{4,6},{6,4},{8,10},{10,8},{12,14},{14,12},{1,3},{3,1},... | collective-permute-start | bytes 3145736 | tf_op jit(solution)/shard_map/ppermute | solution.py:17
  172.0 24.9 %copy-start.7 = (s32[2]{0:T(128)S(1)}, s32[2]{0:T(128)}, u32[]{:S(2)}) copy-start(s32[2]{0:T(128)} %get-tuple-element.49.ids) | copy-start | bytes 28
  172.0 24.9 %copy-start.8 = (s32[2]{0:T(128)S(1)}, s32[2]{0:T(128)}, u32[]{:S(2)}) copy-start(s32[2]{0:T(128)} %constant.85.clone) | copy-start | bytes 28
  172.0 25.5 %copy-start.1 = (bf16[2,2,1,512,512]{4,3,2,1,0:T(8,128)(2,1)S(1)}, bf16[2,2,1,512,512]{4,3,2,1,0:T(8,128)(2,1)}, u32[]{:S(2)}) copy-start(bf16[2,2,1,512,512]{4,3,2,1,0:T(8,128)(2,1)} %param.13) | copy-start | bytes 6291460
  175.7 32.1 %collective-permute-start.14 = (bf16[1,2,1024,512]{3,2,1,0:T(8,128)(2,1)}, bf16[1,2,1024,512]{3,2,1,0:T(8,128)(2,1)}, u32[]{:S(2)}, u32[]{:S(2)}) collective-permute-start(bf16[1,2,1024,512]{3,2,1,0:T(8,128)(2,1)} %shard_map.140.refs_3_), channel_id=1, source_target_pairs={{0,1},{1,0},{2,3},{3,2},{4,5},{5,4},{6,7},{7,6},{8,9},{9,8},{10,11... | collective-permute-start | bytes 6291464 | tf_op jit(solution)/shard_map/ppermute | solution.py:17
  187.3 19.7 %copy-start.4 = (bf16[1,2,512,512]{3,2,1,0:T(8,128)(2,1)}, bf16[1,2,512,512]{3,2,1,0:T(8,128)(2,1)S(1)}, u32[]{:S(2)}) copy-start(bf16[1,2,512,512]{3,2,1,0:T(8,128)(2,1)S(1)} %collective-permute-done.12.refs_0_.refs_6_) | copy-start | bytes 3145732
  187.3 20.5 %collective-permute-start.16 = (bf16[1,2,512,512]{3,2,1,0:T(8,128)(2,1)S(1)}, bf16[1,2,512,512]{3,2,1,0:T(8,128)(2,1)}, u32[]{:S(2)}, u32[]{:S(2)}) collective-permute-start(bf16[1,2,512,512]{3,2,1,0:T(8,128)(2,1)S(1)} %collective-permute-done.12.refs_0_.refs_6_), channel_id=1, source_target_pairs={{0,1},{1,0},{2,3},{3,2},{4,5},{5,4},{6,7},{7,6},{8,9},{9,8},{10,11... | collective-permute-start | bytes 3145736 | tf_op jit(solution)/shard_map/ppermute | solution.py:17
  196.3 11.5 %collective-permute-start.15 = (bf16[1,2,512,512]{3,2,1,0:T(8,128)(2,1)}, bf16[1,2,512,512]{3,2,1,0:T(8,128)(2,1)}, u32[]{:S(2)}, u32[]{:S(2)}) collective-permute-start(bf16[1,2,512,512]{3,2,1,0:T(8,128)(2,1)} %collective-permute-done.13.refs_1_.refs_5_), channel_id=1, source_target_pairs={{0,1},{1,0},{2,3},{3,2},{4,5},{5,4},{6,7},{7,6},{8,9},{9,8},{10,11... | collective-permute-start | bytes 3145736 | tf_op jit(solution)/shard_map/ppermute | solution.py:17
  207.8 27.2 %copy-start.9 = (s32[16]{0:T(128)S(1)}, s32[16]{0:T(128)}, u32[]{:S(2)}) copy-start(s32[16]{0:T(128)} %param.14) | copy-start | bytes 196
  219.8 2.1 collective-permute-start.17
  220.3 3.7 %collective-permute-start.18 = (f32[4,512]{1,0:T(4,128)S(1)}, f32[4,512]{1,0:T(4,128)S(1)}, u32[]{:S(2)}, u32[]{:S(2)}) collective-permute-start(f32[4,512]{1,0:T(4,128)S(1)} %pad_maximum_fusion), channel_id=1, source_target_pairs={{0,2},{1,3},{2,0},{3,1},{4,6},{5,7},{6,4},{7,5},{8,10},{9,11},{10,... | collective-permute-start | bytes 24584 | tf_op jit(solution)/shard_map/ppermute | solution.py:17
  221.8 3.1 %collective-permute-start.19 = (f32[4,512]{1,0:T(4,128)S(1)}, f32[4,512]{1,0:T(4,128)S(1)}, u32[]{:S(2)}, u32[]{:S(2)}) collective-permute-start(f32[4,512]{1,0:T(4,128)S(1)} %pad_maximum_fusion), channel_id=1, source_target_pairs={{0,3},{1,2},{2,1},{3,0},{4,7},{5,6},{6,5},{7,4},{8,11},{9,10},{10,... | collective-permute-start | bytes 24584 | tf_op jit(solution)/shard_map/ppermute | solution.py:17
  225.0 4.9 %collective-permute-start.20 = (f32[4,512]{1,0:T(4,128)S(1)}, f32[4,512]{1,0:T(4,128)S(1)}, u32[]{:S(2)}, u32[]{:S(2)}) collective-permute-start(f32[4,512]{1,0:T(4,128)S(1)} %add_add_fusion.1), channel_id=1, source_target_pairs={{0,4},{1,5},{2,6},{3,7},{4,0},{5,1},{6,2},{7,3},{8,12},{9,13},{10,... | collective-permute-start | bytes 24584 | tf_op jit(solution)/shard_map/ppermute | solution.py:17
  225.4 5.0 %collective-permute-start.21 = (f32[4,512]{1,0:T(4,128)S(1)}, f32[4,512]{1,0:T(4,128)S(1)}, u32[]{:S(2)}, u32[]{:S(2)}) collective-permute-start(f32[4,512]{1,0:T(4,128)S(1)} %add_add_fusion.1), channel_id=1, source_target_pairs={{0,8},{1,9},{2,10},{3,11},{4,12},{5,13},{6,14},{7,15},{8,0},{9,1},... | collective-permute-start | bytes 24584 | tf_op jit(solution)/shard_map/ppermute | solution.py:17
  228.8 5.4 %collective-permute-start.22 = (f32[4,512]{1,0:T(4,128)S(1)}, f32[4,512]{1,0:T(4,128)S(1)}, u32[]{:S(2)}, u32[]{:S(2)}) collective-permute-start(f32[4,512]{1,0:T(4,128)S(1)} %add_add_fusion.1), channel_id=1, source_target_pairs={{0,12},{1,13},{2,14},{3,15},{4,8},{5,9},{6,10},{7,11},{8,4},{9,5},... | collective-permute-start | bytes 24584 | tf_op jit(solution)/shard_map/ppermute | solution.py:17

commit v5 on v4

v5 whole, which is shorter than its diff:
```python
import functools
import math

import jax
import jax.numpy as jnp
from jax import lax
from jax.experimental import pallas as pl
from jax.experimental.pallas import tpu as pltpu
from jax.sharding import PartitionSpec as P

LANES = 256
VMEM_LIMIT = 60 * 1024 * 1024
HINT = pl.CostEstimate(flops=1, bytes_accessed=1, transcendentals=0)


def swap(value, axis, mask):
    size = math.prod(lax.axis_size(name) for name in (axis if isinstance(axis, tuple) else (axis,)))
    return lax.ppermute(value, axis, [(source, source ^ mask) for source in range(size)])


def after(value, *others):
    return lax.optimization_barrier((value, *others))[0]


def sum_all(value):
    axes = ("row", "col")
    size = lax.axis_size("row") * lax.axis_size("col")
    if size > 16 or size & (size - 1):
        return lax.psum(value, axes)
    mask = 1
    while mask < size:
        near = value + swap(value, axes, mask)
        if 2 * mask < size:
            near = near + (swap(value, axes, 2 * mask) + swap(value, axes, 3 * mask))
        value, mask = near, 4 * mask
    return value


def accumulate(freq, first, r_ref, w_refs, total, held, sem, field, tot, tot_sem):
    piece, step = pl.program_id(0), pl.program_id(1)
    lanes = field.shape[3]

    @pl.when((piece == 0) & (step == 0))
    def _():
        for k, ref in enumerate(w_refs):
            source = ref.at[freq if ref.shape[0] > 1 else 0]
            pltpu.make_async_copy(source, held.at[k], sem.at[k]).start()
        if total is not None:
            pltpu.make_async_copy(total, tot, tot_sem.at[0]).start()
        first()

    @pl.when(step == 0)
    def _():
        pltpu.make_async_copy(w_refs[0].at[0], held.at[piece], sem.at[piece]).wait()

    here = pl.ds(pl.multiple_of(step * lanes, lanes), lanes)
    rows_re, rows_im = r_ref[0, 0], r_ref[0, 1]
    w_re, w_im = held[piece, 0, :, here], held[piece, 1, :, here]
    dot = functools.partial(jnp.dot, preferred_element_type=jnp.float32)

    @pl.when(piece == 0)
    def _():
        field[step, 0] = dot(rows_re, w_re) + dot(rows_im, -w_im)
        field[step, 1] = dot(rows_re, w_im) + dot(rows_im, w_re)

    @pl.when(piece > 0)
    def _():
        field[step, 0] += dot(rows_re, w_re) + dot(rows_im, -w_im)
        field[step, 1] += dot(rows_re, w_im) + dot(rows_im, w_re)

    if total is not None:

        @pl.when((piece == len(w_refs) - 1) & (step == 0))
        def _():
            pltpu.make_async_copy(total, tot, tot_sem.at[0]).wait()


def field_kernel(freq, count, ids, r_ref, *refs):
    w_refs, (total, out, held, sem, field, tot, tot_sem) = refs[:count], refs[count:]
    accumulate(freq, lambda: None, r_ref, w_refs, total, held, sem, field, tot, tot_sem)
    step = pl.program_id(1)

    @pl.when(pl.program_id(0) == count - 1)
    def _():
        out[0] = field[step] + tot[step]


def first_kernel(freq, count, ids, r_ref, *refs):
    w_refs, (out, held, sem, field) = refs[:count], refs[count:]
    accumulate(freq, lambda: None, r_ref, w_refs, None, held, sem, field, None, None)

    @pl.when(pl.program_id(0) == count - 1)
    def _():
        out[0] = field[pl.program_id(1)]


def start_rows(freq, ids, base, whole, singles, rows, sem):
    width = rows.shape[1] // 2
    for slot in range(2):
        here = pl.ds(slot * width, width)
        views = [ref.at[freq, :, here] for ref in whole] + [ref.at[0] for ref in singles]
        for k, source in enumerate(views):

            @pl.when(ids[base + slot] == k)
            def _(source=source, slot=slot, here=here):
                pltpu.make_async_copy(source, rows.at[:, here], sem.at[slot]).start()


def wait_rows(slot, singles, rows, sem):
    width = rows.shape[1] // 2
    here = pl.ds(slot * width, width)
    pltpu.make_async_copy(singles[0].at[0], rows.at[:, here], sem.at[slot]).wait()


def fold(rows_re, rows_im, re, im):
    product = rows_re.astype(jnp.float32) * re + rows_im.astype(jnp.float32) * im
    return jnp.sum(product.reshape(-1, 8, product.shape[-1]), axis=0)


def numer_kernel(freq, count, ids, r_ref, *refs):
    w_refs, total, whole = refs[:count], refs[count], refs[count + 1 : count + 3]
    singles = refs[count + 3 : -8]
    out, held, sem, field, tot, tot_sem, rows, row_sem = refs[-8:]
    begin = lambda: start_rows(freq, ids, count, whole, singles, rows, row_sem)
    accumulate(freq, begin, r_ref, w_refs, total, held, sem, field, tot, tot_sem)
    step = pl.program_id(1)
    lanes = field.shape[3]
    last = pl.program_id(0) == count - 1

    @pl.when(last & (step == 0))
    def _():
        for slot in range(2):
            wait_rows(slot, singles, rows, row_sem)

    @pl.when(last)
    def _():
        here = pl.ds(pl.multiple_of(step * lanes, lanes), lanes)
        re, im = field[step, 0] + tot[step, 0], field[step, 1] + tot[step, 1]
        out[...] = fold(rows[0, :, here], rows[1, :, here], re, im)


def dot_kernel(freq, ids, field, *refs):
    whole, singles, (out, rows, sem) = refs[:2], refs[2:-3], refs[-3:]
    step = pl.program_id(0)
    lanes = field.shape[3]

    @pl.when(step == 0)
    def _():
        start_rows(freq, ids, 0, whole, singles, rows, sem)
        for slot in range(2):
            wait_rows(slot, singles, rows, sem)

    here = pl.ds(pl.multiple_of(step * lanes, lanes), lanes)
    out[...] = fold(rows[0, :, here], rows[1, :, here], field[0, 0], field[0, 1])


ANYWHERE = pl.BlockSpec(memory_space=pl.ANY)


def call(kernel, cross, freq, ids, pieces, rest, out_shape, out_spec, has_total, scratch):
    rows, (width, sources) = cross.shape[2], pieces[0].shape[2:]
    count, steps = len(pieces), sources // LANES
    total = [pltpu.VMEM((steps, 2, rows, LANES), jnp.float32), pltpu.SemaphoreType.DMA((1,))]
    return pl.pallas_call(
        functools.partial(kernel, freq, count),
        out_shape=out_shape,
        grid_spec=pltpu.PrefetchScalarGridSpec(
            num_scalar_prefetch=1,
            grid=(count, steps),
            in_specs=[pl.BlockSpec((1, 2, rows, width), lambda p, n, ids: (freq, 0, 0, ids[p]))]
            + [ANYWHERE] * (count + len(rest)),
            out_specs=out_spec,
            scratch_shapes=[
                pltpu.VMEM((count, 2, width, sources), pieces[0].dtype),
                pltpu.SemaphoreType.DMA((count,)),
                pltpu.VMEM((steps, 2, rows, LANES), jnp.float32),
                *(total if has_total else []),
                *scratch,
            ],
        ),
        compiler_params=pltpu.CompilerParams(vmem_limit_bytes=VMEM_LIMIT),
        cost_estimate=HINT,
    )(ids, cross, *pieces, *rest)


def add_field(cross, freq, ids, pieces, total=None):
    rows, sources = cross.shape[2], pieces[0].shape[3]
    count = len(pieces)
    return call(
        first_kernel if total is None else field_kernel,
        cross,
        freq,
        ids,
        pieces,
        [] if total is None else [total],
        jax.ShapeDtypeStruct((sources // LANES, 2, rows, LANES), jnp.float32),
        pl.BlockSpec(
            (1, 2, rows, LANES), lambda p, n, ids: (jnp.where(p == count - 1, n, 0), 0, 0, 0)
        ),
        total is not None,
        [],
    )


def row_scratch(rows, sources, dtype):
    return [pltpu.VMEM((2, rows, sources), dtype), pltpu.SemaphoreType.DMA((2,))]


def finish(cross, freq, ids, pieces, total, whole, singles):
    rows, sources = cross.shape[2], pieces[0].shape[3]
    count = len(pieces)
    out = call(
        numer_kernel,
        cross,
        freq,
        ids,
        pieces,
        [total, *whole, *singles],
        jax.ShapeDtypeStruct((8, sources), jnp.float32),
        pl.BlockSpec((8, LANES), lambda p, n, ids: (0, jnp.where(p == count - 1, n, 0))),
        True,
        row_scratch(rows, sources, pieces[0].dtype),
    )
    return jnp.sum(out, axis=0)


def dot_rows(freq, ids, field, whole, singles):
    steps, _, rows, lanes = field.shape
    sources = steps * lanes
    out = pl.pallas_call(
        functools.partial(dot_kernel, freq),
        out_shape=jax.ShapeDtypeStruct((8, sources), jnp.float32),
        grid_spec=pltpu.PrefetchScalarGridSpec(
            num_scalar_prefetch=1,
            grid=(steps,),
            in_specs=[pl.BlockSpec((1, 2, rows, lanes), lambda n, ids: (n, 0, 0, 0))]
            + [ANYWHERE] * (2 + len(singles)),
            out_specs=pl.BlockSpec((8, lanes), lambda n, ids: (0, n)),
            scratch_shapes=row_scratch(rows, sources, whole[0].dtype),
        ),
        compiler_params=pltpu.CompilerParams(vmem_limit_bytes=VMEM_LIMIT),
        cost_estimate=HINT,
    )(ids, field, *whole, *singles)
    return jnp.sum(out, axis=0)


def pick_kernel(plan, ids, *refs):
    pieces, out, sem = refs[:-2], refs[-2], refs[-1]
    width = pieces[0].shape[2]
    for wait in (False, True):
        for place, (freq, slots, choices) in enumerate(plan):
            for slot in range(2):
                for mask, k in choices:

                    @pl.when(ids[slot] == mask)
                    def _(place=place, freq=freq, slots=slots, slot=slot, k=k):
                        piece = pieces[k]
                        source = piece.at[freq if piece.shape[0] > 1 else 0]
                        start = slot * width if slots == 2 else 0
                        copy = pltpu.make_async_copy(
                            source, out.at[place, :, pl.ds(start, width)], sem.at[place, slot]
                        )
                        copy.wait() if wait else copy.start()


def pick_rows(ids, plan, pieces):
    _, _, width, sources = pieces[0].shape
    shape = (len(plan), 2, plan[0][1] * width, sources)
    return pl.pallas_call(
        functools.partial(pick_kernel, plan),
        out_shape=jax.ShapeDtypeStruct(shape, pieces[0].dtype),
        grid_spec=pltpu.PrefetchScalarGridSpec(
            num_scalar_prefetch=1,
            grid=(1,),
            in_specs=[ANYWHERE] * len(pieces),
            out_specs=pl.BlockSpec(shape, lambda i, ids: (0, 0, 0, 0)),
            scratch_shapes=[pltpu.SemaphoreType.DMA((len(plan), 2))],
        ),
        compiler_params=pltpu.CompilerParams(vmem_limit_bytes=VMEM_LIMIT),
        cost_estimate=HINT,
    )(ids, *pieces)


def numer_by_swaps(cross, replicas):
    rows, half = cross.shape[2], cross.shape[3]
    width = replicas.shape[3]
    me = lax.axis_index("row").astype(jnp.int32)
    col = lax.axis_index("col").astype(jnp.int32)
    holder = me * rows // half
    first = (me * rows - holder * half) // width
    masks = jnp.stack([first ^ me, (first + 1) ^ me])
    holds = holder == col
    ids = lambda *wanted: me ^ jnp.array(wanted, jnp.int32)
    barrier = lambda *values: lax.optimization_barrier(values)
    own = replicas[:, :, 0]

    own_a = own[0:1]
    x = swap(after(own, own_a), "row", 1)
    pa = swap(own_a, "row", 4)
    na = swap(own_a, "row", 2)
    a0 = add_field(cross, 0, ids(0), [own])
    a1 = add_field(cross, 1, ids(0), [own])
    own_b = after(own, a0)[1:2]
    x, pa, na, own_b, a0, a1 = barrier(x, pa, na, own_b, a0, a1)

    pb = swap(own_b, "row", 4)
    ga = swap(pa, "row", 2)
    xpa = swap(pa, "row", 1)
    xna = swap(na, "row", 1)
    a0 = add_field(cross, 0, ids(1, 2, 4), [x, na, pa], a0)
    a1 = add_field(cross, 1, ids(1), [x], a1)
    x_b = x[1:2]
    pb, ga, xpa, xna, a0, a1, x_b, own_b = barrier(pb, ga, xpa, xna, a0, a1, x_b, own_b)

    gb = swap(pb, "row", 2)
    xga = swap(ga, "row", 1)
    xpb = swap(pb, "row", 1)
    nb = swap(own_b, "row", 2)
    b0 = add_field(cross, 0, ids(3, 5, 6), [xna, xpa, ga], a0)
    a1 = add_field(cross, 1, ids(4), [pb], a1)
    plan = [
        (0, 2, [(0, 0), (1, 1), (2, 2), (3, 3), (4, 4), (5, 5), (6, 6)]),
        (1, 2, [(0, 0), (1, 1), (4, 7)]),
    ]
    mine = pick_rows(after(masks, b0), plan, [own, x, na, xna, pa, xpa, ga, pb])
    gb, nb, xga, xpb, b0, a1, x_b, mine = barrier(gb, nb, xga, xpb, b0, a1, x_b, mine)

    other = swap(mine, "col", 1)
    other_xga = swap(xga, "col", 1)
    d = swap(x_b, "row", 2)
    xgb = swap(gb, "row", 1)
    b1 = add_field(cross, 1, ids(6, 5, 2), [gb, xpb, nb], a1)
    plan = [(0, 1, [(6, 0), (5, 1), (2, 2)])]
    mine_b = pick_rows(after(masks, b1), plan, [gb, xpb, nb])
    whole = jnp.where(holds, 0, 1)
    where = jnp.where(masks == 7, jnp.where(holds, 2, 3), whole)
    c0 = finish(
        cross, 0, jnp.concatenate([ids(7), where]), [xga], b0, [mine, other], [xga, other_xga]
    )
    d, xgb, b1, mine_b, c0 = barrier(d, xgb, b1, mine_b, c0)

    other_b, other_d, other_xgb = (swap(piece, "col", 1) for piece in (mine_b, d, xgb))
    field = add_field(cross, 1, ids(3, 7), [d, xgb], b1)
    where = jnp.full_like(masks, whole)
    for k, mask in enumerate((6, 5, 2)):
        where = jnp.where(masks == mask, jnp.where(holds, 2 + k, 5), where)
    where = jnp.where(masks == 3, jnp.where(holds, 6, 7), where)
    where = jnp.where(masks == 7, jnp.where(holds, 8, 9), where)
    singles = [gb, xpb, nb, other_b, d, other_d, xgb, other_xgb]
    c1 = dot_rows(1, where, field, [mine, other], singles)
    return jnp.stack([c0, c1])


def numer_by_gather(cross, replicas):
    rows, half = cross.shape[2], cross.shape[3]
    row_index, col_index = lax.axis_index("row"), lax.axis_index("col")
    first_row = row_index * rows
    holder = first_row // half
    whole = lax.all_gather(replicas, "row", axis=3, tiled=True)[:, :, 0]
    parts = jnp.einsum("fark,fbks->fabrs", cross, whole, preferred_element_type=jnp.float32)
    field = jnp.stack([parts[:, 0, 0] - parts[:, 1, 1], parts[:, 0, 1] + parts[:, 1, 0]], axis=1)
    own_rows = lax.dynamic_slice_in_dim(whole, first_row - holder * half, rows, 2)
    block_rows = jnp.where(holder == col_index, own_rows, swap(own_rows, "col", 1))
    return jnp.sum(block_rows.astype(jnp.float32) * field, axis=(1, 2))


def body(cross_spectra, replicas, tile_order):
    fnum = cross_spectra.shape[0]
    sources = replicas.shape[4]
    own = replicas[:, :, 0].astype(jnp.float32)
    norms = jnp.sum(own * own, axis=(1, 2))
    doubling = (
        lax.axis_size("row") == 8
        and replicas.shape[3] % 128 == 0
        and cross_spectra.shape[2] == 2 * replicas.shape[3]
    )
    numer = (numer_by_swaps if doubling else numer_by_gather)(cross_spectra, replicas)
    sums = sum_all(jnp.concatenate([numer, norms]))
    numer, norms = sums[:fnum], sums[fnum:]
    beam = numer / (norms + 1e-06)
    width = sources // lax.axis_size("col")
    beam_half = lax.dynamic_slice_in_dim(beam, lax.axis_index("col") * width, width, 1)
    peak = jnp.max(jnp.abs(beam), axis=1) + 1e-06
    count = tile_order.shape[0]
    picker = (tile_order[:, None] == jnp.arange(count, dtype=jnp.int32)[None, :]).astype(jnp.float32)
    tiles = beam.reshape(fnum, count, sources // count)
    refined = (
        jnp.einsum("tu,fup->ftp", picker, tiles, precision=lax.Precision.HIGHEST)
        / peak[:, None, None]
    )
    return (beam_half, refined)


def solution(mesh):
    in_specs = (P("groups", None, "row", "col"), P("groups", None, "col", "row", None), P("groups"))
    out_specs = (P("groups", "col"), P("groups", None, None))
    return jax.shard_map(body, mesh=mesh, in_specs=in_specs, out_specs=out_specs, check_vma=False)
```

time: 236 us -> 217 us (0.919)
  waiting for transfers between devices: 97.6 us -> 71.2 us
  Pallas kernels: 96.6 us -> 103 us
    ppermute x23 -> x24, waiting for transfers between devices: 97.6 us -> 71.2 us  [swap(): lax.ppermute(value, axis, [(source, source ^ mask) for source in range(si...]
    pallas_call x11 -> x12, Pallas kernels: 96.6 us -> 103 us  [the longest x9 90.9 us: call(): pl.pallas_call(functools.partial(kernel, freq, count), out_shape=out_shap...]
    ppermute x23 -> x24, starting transfers between devices: 27.2 us -> 28.1 us  [swap(): lax.ppermute(value, axis, [(source, source ^ mask) for source in range(si...]
  transfers between devices with their start and end apart: 23 -> 24, of which waited for: 13 -> 10; matrix products, arithmetic and copies ran while one was open for 3% -> 4% of each run, Pallas kernels for 30% -> 45%
where the time goes in v5:
time: 217 us; the launch traced here: 216 us
  Pallas kernels  103 us (47%)
  waiting for transfers between devices  71.2 us (33%)
  starting transfers between devices  28.1 us (13%)
  local copies, waits for them, and re-layouts  6.37 us (3%)
  other arithmetic  5.87 us (3%)
    pallas_call x9, Pallas kernels, call(): pl.pallas_call(functools.partial(kernel, freq, count), out_shape=out_shap...  90.9 us
    ppermute x24, waiting for transfers between devices, swap(): lax.ppermute(value, axis, [(source, source ^ mask) for source in range(si...  71.2 us
    ppermute x24, starting transfers between devices, swap(): lax.ppermute(value, axis, [(source, source ^ mask) for source in range(si...  28.1 us
    pallas_call x2, Pallas kernels, pick_rows(): pl.pallas_call(functools.partial(pick_kernel, plan), out_shape=jax.ShapeD...  6.53 us
    pallas_call x1, Pallas kernels, dot_rows(): pl.pallas_call(functools.partial(dot_kernel, freq), out_shape=jax.ShapeDt...  5.25 us
  transfers between devices with their start and end apart: 24, of which 10 were waited for; matrix products, arithmetic and copies ran while one was open for 4% of the time, Pallas kernels for 45%

profile of v5, /device:TPU:0, one launch (start us, length us, event | category | flops | bytes accessed | tf_op | source)
XLA Modules:
  0.0 216.0 jit_solution(14487349478246500692)
XLA Ops:
  0.6 2.3 %slice_bitcast_fusion = bf16[1,2,512,512]{3,2,1,0:T(8,128)(2,1)} fusion(bf16[2,2,1,512,512]{4,3,1,2,0:T(8,128)(2,1)} %bitcast.16), kind=kLoop, calls=%fused_computation.3 | loop fusion | bytes 2097152 | tf_op jit(solution)/shard_map/slice | solution.py:297
  2.9 2.9 %collective-permute-start = (bf16[2,2,512,512]{3,2,1,0:T(8,128)(2,1)}, bf16[2,2,512,512]{3,2,1,0:T(8,128)(2,1)}, u32[]{:S(2)}, u32[]{:S(2)}) collective-permute-start(bf16[2,2,512,512]{3,2,1,0:T(8,128)(2,1)} %bitcast.17), channel_id=1, source_target_pairs={{0,2},{2,0},{4,6},{6,4},{8,10},{10,8},{12,14},{14,12},{1,3},{3,1},... | collective-permute-start | bytes 6291464 | tf_op jit(solution)/shard_map/ppermute | solution.py:18
  5.9 2.6 %collective-permute-start.1 = (bf16[1,2,512,512]{3,2,1,0:T(8,128)(2,1)}, bf16[1,2,512,512]{3,2,1,0:T(8,128)(2,1)S(1)}, u32[]{:S(2)}, u32[]{:S(2)}) collective-permute-start(bf16[1,2,512,512]{3,2,1,0:T(8,128)(2,1)} %slice_bitcast_fusion), channel_id=1, source_target_pairs={{0,8},{2,10},{4,12},{6,14},{8,0},{10,2},{12,4},{14,6},{1,9},{3,11}... | collective-permute-start | bytes 3145736 | tf_op jit(solution)/shard_map/ppermute | solution.py:18
  8.4 1.6 collective-permute-start.2
  10.0 6.7 %shard_map.131.refs_3_ = f32[2,2,1024,256]{3,2,1,0:T(8,128)} custom-call(s32[1]{0:T(128)} %bitcast.3.ids, bf16[2,2,1024,4096]{3,2,1,0:T(8,128)(2,1)} %r_ref.17, bf16[2,2,512,512]{3,2,1,0:T(8,128)(2,1)} %bitcast.18), custom_call_target="tpu_custom_call" | custom-call | flops 1 | bytes 1 | tf_op jit(solution)/shard_map/pallas_call | solution.py:164
  16.8 6.9 %shard_map.132.refs_1_ = f32[2,2,1024,256]{3,2,1,0:T(8,128)} custom-call(s32[1]{0:T(128)} %bitcast.3.ids, bf16[2,2,1024,4096]{3,2,1,0:T(8,128)(2,1)} %r_ref.17, bf16[2,2,512,512]{3,2,1,0:T(8,128)(2,1)} %bitcast.19), custom_call_target="tpu_custom_call" | custom-call | flops 1 | bytes 1 | tf_op jit(solution)/shard_map/pallas_call | solution.py:164
  23.7 1.1 slice.20
  24.8 29.4 %collective-permute-done.1.refs_2_.refs_4_ = bf16[1,2,512,512]{3,2,1,0:T(8,128)(2,1)S(1)} collective-permute-done((bf16[1,2,512,512]{3,2,1,0:T(8,128)(2,1)}, bf16[1,2,512,512]{3,2,1,0:T(8,128)(2,1)S(1)}, u32[]{:S(2)}, u32[]{:S(2)}) %collective-permute-start.1) | collective-permute-done | bytes 1048608 | tf_op jit(solution)/shard_map/ppermute | solution.py:18
  54.5 1.4 collective-permute-start.4
  55.9 0.5 collective-permute-start.5
  56.4 1.5 collective-permute-start.6
  57.9 2.3 %collective-permute-start.3 = (bf16[1,2,512,512]{3,2,1,0:T(8,128)(2,1)}, bf16[1,2,512,512]{3,2,1,0:T(8,128)(2,1)}, u32[]{:S(2)}, u32[]{:S(2)}) collective-permute-start(bf16[1,2,512,512]{3,2,1,0:T(8,128)(2,1)} %slice.20), channel_id=1, source_target_pairs={{0,8},{2,10},{4,12},{6,14},{8,0},{10,2},{12,4},{14,6},{1,9},{3,11}... | collective-permute-start | bytes 3145736 | tf_op jit(solution)/shard_map/ppermute | solution.py:18
  60.2 0.5 broadcast_xor_fusion.3.ids
  60.7 14.4 %shard_map.133.refs_3_ = f32[2,2,1024,256]{3,2,1,0:T(8,128)} custom-call(s32[3]{0:T(128)} %broadcast_xor_fusion.3.ids, bf16[2,2,1024,4096]{3,2,1,0:T(8,128)(2,1)} %r_ref.17, bf16[2,2,512,512]{3,2,1,0:T(8,128)(2,1)} %collective-permute-done.refs_0_.refs_1_, bf16[1,2,512,512]{3,2,1,0:T(8,128)(2,1)} %collective-permute-done.2.refs_1_.refs_2_, ...), custom_call_target="tpu_custom_call" | custom-call | flops 1 | bytes 1 | tf_op jit(solution)/shard_map/pallas_call | solution.py:164
  75.1 7.3 %shard_map.134.refs_1_ = f32[2,2,1024,256]{3,2,1,0:T(8,128)} custom-call(s32[1]{0:T(128)S(6)} %xor.53.ids, bf16[2,2,1024,4096]{3,2,1,0:T(8,128)(2,1)} %r_ref.17, bf16[2,2,512,512]{3,2,1,0:T(8,128)(2,1)} %collective-permute-done.refs_0_.refs_1_, f32[2,2,1024,256]{3,2,1,0:T(8,128)} %shard_map.132.refs_1_), custom_call_target="tpu_custom_call" | custom-call | flops 1 | bytes 1 | tf_op jit(solution)/shard_map/pallas_call | solution.py:164
  82.4 2.3 %slice.21 = bf16[1,2,512,512]{3,2,1,0:T(8,128)(2,1)} slice(bf16[2,2,512,512]{3,2,1,0:T(8,128)(2,1)} %collective-permute-done.refs_0_.refs_1_), slice={[1:2], [0:2], [0:512], [0:512]} | slice | bytes 2097152 | tf_op jit(solution)/shard_map/slice | solution.py:312
  84.6 14.2 %collective-permute-done.4.refs_2_.refs_6_ = bf16[1,2,512,512]{3,2,1,0:T(8,128)(2,1)S(1)} collective-permute-done((bf16[1,2,512,512]{3,2,1,0:T(8,128)(2,1)S(1)}, bf16[1,2,512,512]{3,2,1,0:T(8,128)(2,1)S(1)}, u32[]{:S(2)}, u32[]{:S(2)}) %collective-permute-start.4) | collective-permute-done | bytes 1048608 | tf_op jit(solution)/shard_map/ppermute | solution.py:18
  98.8 3.5 %collective-permute-done.6.refs_0_.refs_3_ = bf16[1,2,512,512]{3,2,1,0:T(8,128)(2,1)} collective-permute-done((bf16[1,2,512,512]{3,2,1,0:T(8,128)(2,1)}, bf16[1,2,512,512]{3,2,1,0:T(8,128)(2,1)}, u32[]{:S(2)}, u32[]{:S(2)}) %collective-permute-start.6) | collective-permute-done | bytes 1048608 | tf_op jit(solution)/shard_map/ppermute | solution.py:18
  102.3 3.3 %collective-permute-done.3.refs_0_.refs_7_ = bf16[1,2,512,512]{3,2,1,0:T(8,128)(2,1)} collective-permute-done((bf16[1,2,512,512]{3,2,1,0:T(8,128)(2,1)}, bf16[1,2,512,512]{3,2,1,0:T(8,128)(2,1)}, u32[]{:S(2)}, u32[]{:S(2)}) %collective-permute-start.3) | collective-permute-done | bytes 1048608 | tf_op jit(solution)/shard_map/ppermute | solution.py:18
  106.1 2.0 collective-permute-start.8
  108.1 1.5 collective-permute-start.9
  109.6 0.6 compare_select_fusion.5
  110.7 14.4 %shard_map.135.refs_1_ = f32[2,2,1024,256]{3,2,1,0:T(8,128)} custom-call(s32[3]{0:T(128)} %broadcast_xor_fusion.2.ids, bf16[2,2,1024,4096]{3,2,1,0:T(8,128)(2,1)} %r_ref.17, bf16[1,2,512,512]{3,2,1,0:T(8,128)(2,1)} %collective-permute-done.6.refs_0_.refs_3_, bf16[1,2,512,512]{3,2,1,0:T(8,128)(2,1)} %copy-done.6, bf16[1,2,512,512]{3,2,1,0:T(8,128)(2,1)} %copy-done.5, ...), custom_call_target="tpu_custom_call" | custom-call | flops 1 | bytes 1 | tf_op jit(solution)/shard_map/pallas_call | solution.py:164
  125.1 4.8 %shard_map.137.refs_2_.refs_0_ = bf16[2,2,1024,512]{3,2,1,0:T(8,128)(2,1)} custom-call(s32[2]{0:T(128)} %get-tuple-element.55.ids, bf16[2,2,512,512]{3,2,1,0:T(8,128)(2,1)} %bitcast.20, bf16[2,2,512,512]{3,2,1,0:T(8,128)(2,1)} %collective-permute-done.refs_0_.refs_1_, bf16[1,2,512,512]{3,2,1,0:T(8,128)(2,1)} %collective-permute-done.2.refs_1_.refs_2_, ...), custom_call_target="tpu_custom_call" | custom-call | flops 1 | bytes 1 | tf_op jit(solution)/shard_map/pallas_call | solution.py:269
  130.0 7.2 %shard_map.136.refs_3_ = f32[2,2,1024,256]{3,2,1,0:T(8,128)} custom-call(s32[1]{0:T(128)S(6)} %xor.55.ids, bf16[2,2,1024,4096]{3,2,1,0:T(8,128)(2,1)} %r_ref.17, bf16[1,2,512,512]{3,2,1,0:T(8,128)(2,1)} %collective-permute-done.3.refs_0_.refs_7_, f32[2,2,1024,256]{3,2,1,0:T(8,128)} %shard_map.134.refs_1_), custom_call_target="tpu_custom_call" | custom-call | flops 1 | bytes 1 | tf_op jit(solution)/shard_map/pallas_call | solution.py:164
  137.2 13.2 %collective-permute-done.8.refs_2_.refs_4_ = bf16[1,2,512,512]{3,2,1,0:T(8,128)(2,1)S(1)} collective-permute-done((bf16[1,2,512,512]{3,2,1,0:T(8,128)(2,1)}, bf16[1,2,512,512]{3,2,1,0:T(8,128)(2,1)S(1)}, u32[]{:S(2)}, u32[]{:S(2)}) %collective-permute-start.8) | collective-permute-done | bytes 1048608 | tf_op jit(solution)/shard_map/ppermute | solution.py:18
  150.9 1.4 collective-permute-start.11
  152.3 1.5 collective-permute-start.12
  153.8 0.6 pad_add_fusion.1.ids
  154.4 0.5 broadcast_xor_fusion.1.ids
  154.9 14.5 %shard_map.138.refs_2_ = f32[2,2,1024,256]{3,2,1,0:T(8,128)} custom-call(s32[3]{0:T(128)} %broadcast_xor_fusion.1.ids, bf16[2,2,1024,4096]{3,2,1,0:T(8,128)(2,1)} %r_ref.17, bf16[1,2,512,512]{3,2,1,0:T(8,128)(2,1)} %collective-permute-done.7.refs_0_.refs_2_, bf16[1,2,512,512]{3,2,1,0:T(8,128)(2,1)} %copy-done.2, bf16[1,2,512,512]{3,2,1,0:T(8,128)(2,1)} %copy-done.3, ...), custom_call_target="tpu_custom_call" | custom-call | flops 1 | bytes 1 | tf_op jit(solution)/shard_map/pallas_call | solution.py:164
  169.5 1.7 shard_map.139
  171.3 8.3 %shard_map.140 = f32[8,512]{1,0:T(8,128)} custom-call(s32[3]{0:T(128)} %pad_add_fusion.1.ids, bf16[2,2,1024,4096]{3,2,1,0:T(8,128)(2,1)} %r_ref.17, bf16[1,2,512,512]{3,2,1,0:T(8,128)(2,1)} %collective-permute-done.9.refs_0_.refs_4_, f32[2,2,1024,256]{3,2,1,0:T(8,128)} %shard_map.135.refs_1_, bf16[2,2,1024,512]{3,2,1,0:T(8,128)(2,1)} %shard_map.137.refs_2_.refs_0_, ...), custom_call_target="tpu_custom_call" | custom-call | flops 1 | bytes 1 | tf_op jit(solution)/shard_map/pallas_call | solution.py:164
  179.6 0.7 reduce_sum.27
  181.5 0.5 compare_select_fusion.4.ids
  182.5 11.3 %shard_map.141.field = f32[2,2,1024,256]{3,2,1,0:T(8,128)} custom-call(s32[2]{0:T(128)} %broadcast_xor_fusion.ids, bf16[2,2,1024,4096]{3,2,1,0:T(8,128)(2,1)} %r_ref.17, bf16[1,2,512,512]{3,2,1,0:T(8,128)(2,1)} %copy-done.7, bf16[1,2,512,512]{3,2,1,0:T(8,128)(2,1)} %collective-permute-done.12.refs_1_.refs_8_, f32[2,2,1024,256]{3,2,1,0:T(8,128)} %shard_map.138.refs_2_), custom_call_target="tpu_custom_call" | custom-call | flops 1 | bytes 1 | tf_op jit(solution)/shard_map/pallas_call | solution.py:164
  193.8 5.2 %shard_map.142 = f32[8,512]{1,0:T(8,128)} custom-call(s32[2]{0:T(128)} %compare_select_fusion.4.ids, f32[2,2,1024,256]{3,2,1,0:T(8,128)} %shard_map.141.field, bf16[2,2,1024,512]{3,2,1,0:T(8,128)(2,1)} %shard_map.137.refs_2_.refs_0_, bf16[2,2,1024,512]{3,2,1,0:T(8,128)(2,1)} %collective-permute-done.13.refs_3_.refs_1_, ...), custom_call_target="tpu_custom_call" | custom-call | flops 1 | bytes 1 | tf_op jit(solution)/shard_map/pallas_call | solution.py:230
  199.1 0.7 reduce_sum.28
  200.3 1.7 collective-permute-start.19
  202.1 1.9 collective-permute-done.19
  204.0 1.2 collective-permute-done.20
  205.2 1.4 collective-permute-start.21
  206.6 2.3 %collective-permute-start.22 = (f32[4,512]{1,0:T(4,128)S(1)}, f32[4,512]{1,0:T(4,128)S(1)}, u32[]{:S(2)}, u32[]{:S(2)}) collective-permute-start(f32[4,512]{1,0:T(4,128)S(1)} %add_add_fusion.1), channel_id=1, source_target_pairs={{0,8},{1,9},{2,10},{3,11},{4,12},{5,13},{6,14},{7,15},{8,0},{9,1},... | collective-permute-start | bytes 24584 | tf_op jit(solution)/shard_map/ppermute | solution.py:18
  208.9 1.2 collective-permute-start.23
  210.1 1.0 collective-permute-done.22
  211.2 3.2 %collective-permute-done.23 = f32[4,512]{1,0:T(4,128)S(1)} collective-permute-done((f32[4,512]{1,0:T(4,128)S(1)}, f32[4,512]{1,0:T(4,128)S(1)}, u32[]{:S(2)}, u32[]{:S(2)}) %collective-permute-start.23) | collective-permute-done | bytes 8224 | tf_op jit(solution)/shard_map/ppermute | solution.py:18
  214.6 0.6 constant_dynamic-slice_fusion
  215.2 0.8 fusion
  (61 shorter events, 4.3 us)
Async XLA Ops:
  2.9 51.5 %collective-permute-start = (bf16[2,2,512,512]{3,2,1,0:T(8,128)(2,1)}, bf16[2,2,512,512]{3,2,1,0:T(8,128)(2,1)}, u32[]{:S(2)}, u32[]{:S(2)}) collective-permute-start(bf16[2,2,512,512]{3,2,1,0:T(8,128)(2,1)} %bitcast.17), channel_id=1, source_target_pairs={{0,2},{2,0},{4,6},{6,4},{8,10},{10,8},{12,14},{14,12},{1,3},{3,1},... | collective-permute-start | bytes 6291464 | tf_op jit(solution)/shard_map/ppermute | solution.py:18
  5.9 48.3 %collective-permute-start.1 = (bf16[1,2,512,512]{3,2,1,0:T(8,128)(2,1)}, bf16[1,2,512,512]{3,2,1,0:T(8,128)(2,1)S(1)}, u32[]{:S(2)}, u32[]{:S(2)}) collective-permute-start(bf16[1,2,512,512]{3,2,1,0:T(8,128)(2,1)} %slice_bitcast_fusion), channel_id=1, source_target_pairs={{0,8},{2,10},{4,12},{6,14},{8,0},{10,2},{12,4},{14,6},{1,9},{3,11}... | collective-permute-start | bytes 3145736 | tf_op jit(solution)/shard_map/ppermute | solution.py:18
  8.4 46.0 %collective-permute-start.2 = (bf16[1,2,512,512]{3,2,1,0:T(8,128)(2,1)}, bf16[1,2,512,512]{3,2,1,0:T(8,128)(2,1)}, u32[]{:S(2)}, u32[]{:S(2)}) collective-permute-start(bf16[1,2,512,512]{3,2,1,0:T(8,128)(2,1)} %slice_bitcast_fusion), channel_id=1, source_target_pairs={{0,4},{2,6},{4,0},{6,2},{8,12},{10,14},{12,8},{14,10},{1,5},{3,7},... | collective-permute-start | bytes 3145736 | tf_op jit(solution)/shard_map/ppermute | solution.py:18
  16.8 6.9 %copy-start = (bf16[2,2,1,512,512]{4,3,2,1,0:T(8,128)(2,1)S(1)}, bf16[2,2,1,512,512]{4,3,2,1,0:T(8,128)(2,1)}, u32[]{:S(2)}) copy-start(bf16[2,2,1,512,512]{4,3,2,1,0:T(8,128)(2,1)} %param.13) | copy-start | bytes 6291460
  16.8 43.4 %copy-start.13 = (s32[3]{0:T(128)S(1)}, s32[3]{0:T(128)}, u32[]{:S(2)}) copy-start(s32[3]{0:T(128)} %constant.87.clone) | copy-start | bytes 40
  54.2 6.6 %copy-start.4 = (bf16[1,2,512,512]{3,2,1,0:T(8,128)(2,1)}, bf16[1,2,512,512]{3,2,1,0:T(8,128)(2,1)S(1)}, u32[]{:S(2)}) copy-start(bf16[1,2,512,512]{3,2,1,0:T(8,128)(2,1)S(1)} %collective-permute-done.1.refs_2_.refs_4_) | copy-start | bytes 3145732
  54.5 44.3 %collective-permute-start.4 = (bf16[1,2,512,512]{3,2,1,0:T(8,128)(2,1)S(1)}, bf16[1,2,512,512]{3,2,1,0:T(8,128)(2,1)S(1)}, u32[]{:S(2)}, u32[]{:S(2)}) collective-permute-start(bf16[1,2,512,512]{3,2,1,0:T(8,128)(2,1)S(1)} %collective-permute-done.1.refs_2_.refs_4_), channel_id=1, source_target_pairs={{0,4},{2,6},{4,0},{6,2},{8,12},{10,14},{12,8},{14,10},{1,5},{3,7},... | collective-permute-start | bytes 3145736 | tf_op jit(solution)/shard_map/ppermute | solution.py:18
  55.9 42.9 %collective-permute-start.5 = (bf16[1,2,512,512]{3,2,1,0:T(8,128)(2,1)S(1)}, bf16[1,2,512,512]{3,2,1,0:T(8,128)(2,1)S(1)}, u32[]{:S(2)}, u32[]{:S(2)}) collective-permute-start(bf16[1,2,512,512]{3,2,1,0:T(8,128)(2,1)S(1)} %collective-permute-done.1.refs_2_.refs_4_), channel_id=1, source_target_pairs={{0,2},{2,0},{4,6},{6,4},{8,10},{10,8},{12,14},{14,12},{1,3},{3,1},... | collective-permute-start | bytes 3145736 | tf_op jit(solution)/shard_map/ppermute | solution.py:18
  56.4 45.8 %collective-permute-start.6 = (bf16[1,2,512,512]{3,2,1,0:T(8,128)(2,1)}, bf16[1,2,512,512]{3,2,1,0:T(8,128)(2,1)}, u32[]{:S(2)}, u32[]{:S(2)}) collective-permute-start(bf16[1,2,512,512]{3,2,1,0:T(8,128)(2,1)} %collective-permute-done.2.refs_1_.refs_2_), channel_id=1, source_target_pairs={{0,2},{2,0},{4,6},{6,4},{8,10},{10,8},{12,14},{14,12},{1,3},{3,1},... | collective-permute-start | bytes 3145736 | tf_op jit(solution)/shard_map/ppermute | solution.py:18
  57.9 47.6 %collective-permute-start.3 = (bf16[1,2,512,512]{3,2,1,0:T(8,128)(2,1)}, bf16[1,2,512,512]{3,2,1,0:T(8,128)(2,1)}, u32[]{:S(2)}, u32[]{:S(2)}) collective-permute-start(bf16[1,2,512,512]{3,2,1,0:T(8,128)(2,1)} %slice.20), channel_id=1, source_target_pairs={{0,8},{2,10},{4,12},{6,14},{8,0},{10,2},{12,4},{14,6},{1,9},{3,11}... | collective-permute-start | bytes 3145736 | tf_op jit(solution)/shard_map/ppermute | solution.py:18
  75.1 35.1 %copy-start.12 = (s32[3]{0:T(128)S(1)}, s32[3]{0:T(128)}, u32[]{:S(2)}) copy-start(s32[3]{0:T(128)} %constant.89.clone) | copy-start | bytes 40
  98.8 11.9 %copy-start.5 = (bf16[1,2,512,512]{3,2,1,0:T(8,128)(2,1)}, bf16[1,2,512,512]{3,2,1,0:T(8,128)(2,1)S(1)}, u32[]{:S(2)}) copy-start(bf16[1,2,512,512]{3,2,1,0:T(8,128)(2,1)S(1)} %collective-permute-done.4.refs_2_.refs_6_) | copy-start | bytes 3145732
  98.8 7.3 %copy-start.6 = (bf16[1,2,512,512]{3,2,1,0:T(8,128)(2,1)}, bf16[1,2,512,512]{3,2,1,0:T(8,128)(2,1)S(1)}, u32[]{:S(2)}) copy-start(bf16[1,2,512,512]{3,2,1,0:T(8,128)(2,1)S(1)} %collective-permute-done.5.refs_1_.refs_5_) | copy-start | bytes 3145732
  105.6 31.6 %collective-permute-start.10 = (bf16[1,2,512,512]{3,2,1,0:T(8,128)(2,1)}, bf16[1,2,512,512]{3,2,1,0:T(8,128)(2,1)S(1)}, u32[]{:S(2)}, u32[]{:S(2)}) collective-permute-start(bf16[1,2,512,512]{3,2,1,0:T(8,128)(2,1)} %collective-permute-done.3.refs_0_.refs_7_), channel_id=1, source_target_pairs={{0,2},{2,0},{4,6},{6,4},{8,10},{10,8},{12,14},{14,12},{1,3},{3,1},... | collective-permute-start | bytes 3145736 | tf_op jit(solution)/shard_map/ppermute | solution.py:18
  106.1 31.1 %collective-permute-start.7 = (bf16[1,2,512,512]{3,2,1,0:T(8,128)(2,1)}, bf16[1,2,512,512]{3,2,1,0:T(8,128)(2,1)}, u32[]{:S(2)}, u32[]{:S(2)}) collective-permute-start(bf16[1,2,512,512]{3,2,1,0:T(8,128)(2,1)} %collective-permute-done.3.refs_0_.refs_7_), channel_id=1, source_target_pairs={{0,4},{2,6},{4,0},{6,2},{8,12},{10,14},{12,8},{14,10},{1,5},{3,7},... | collective-permute-start | bytes 3145736 | tf_op jit(solution)/shard_map/ppermute | solution.py:18
  106.1 44.3 %collective-permute-start.8 = (bf16[1,2,512,512]{3,2,1,0:T(8,128)(2,1)}, bf16[1,2,512,512]{3,2,1,0:T(8,128)(2,1)S(1)}, u32[]{:S(2)}, u32[]{:S(2)}) collective-permute-start(bf16[1,2,512,512]{3,2,1,0:T(8,128)(2,1)} %slice.20), channel_id=1, source_target_pairs={{0,4},{2,6},{4,0},{6,2},{8,12},{10,14},{12,8},{14,10},{1,5},{3,7},... | collective-permute-start | bytes 3145736 | tf_op jit(solution)/shard_map/ppermute | solution.py:18
  108.1 42.3 %collective-permute-start.9 = (bf16[1,2,512,512]{3,2,1,0:T(8,128)(2,1)S(1)}, bf16[1,2,512,512]{3,2,1,0:T(8,128)(2,1)}, u32[]{:S(2)}, u32[]{:S(2)}) collective-permute-start(bf16[1,2,512,512]{3,2,1,0:T(8,128)(2,1)S(1)} %collective-permute-done.4.refs_2_.refs_6_), channel_id=1, source_target_pairs={{0,2},{2,0},{4,6},{6,4},{8,10},{10,8},{12,14},{14,12},{1,3},{3,1},... | collective-permute-start | bytes 3145736 | tf_op jit(solution)/shard_map/ppermute | solution.py:18
  129.9 24.5 %copy-start.11 = (s32[3]{0:T(128)S(1)}, s32[3]{0:T(128)}, u32[]{:S(2)}) copy-start(s32[3]{0:T(128)} %constant.91.clone) | copy-start | bytes 40
  137.1 17.8 %copy-start.2 = (bf16[1,2,512,512]{3,2,1,0:T(8,128)(2,1)}, bf16[1,2,512,512]{3,2,1,0:T(8,128)(2,1)S(1)}, u32[]{:S(2)}) copy-start(bf16[1,2,512,512]{3,2,1,0:T(8,128)(2,1)S(1)} %collective-permute-done.10.refs_1_.refs_3_) | copy-start | bytes 3145732
  150.4 4.6 %copy-start.3 = (bf16[1,2,512,512]{3,2,1,0:T(8,128)(2,1)}, bf16[1,2,512,512]{3,2,1,0:T(8,128)(2,1)S(1)}, u32[]{:S(2)}) copy-start(bf16[1,2,512,512]{3,2,1,0:T(8,128)(2,1)S(1)} %collective-permute-done.8.refs_2_.refs_4_) | copy-start | bytes 3145732
  150.4 20.9 %collective-permute-start.13 = (bf16[2,2,1024,512]{3,2,1,0:T(8,128)(2,1)}, bf16[2,2,1024,512]{3,2,1,0:T(8,128)(2,1)}, u32[]{:S(2)}, u32[]{:S(2)}) collective-permute-start(bf16[2,2,1024,512]{3,2,1,0:T(8,128)(2,1)} %shard_map.137.refs_2_.refs_0_), channel_id=1, source_target_pairs={{0,1},{1,0},{2,3},{3,2},{4,5},{5,4},{6,7},{7,6},{8,9},{9,8},{10,11... | collective-permute-start | bytes 12582920 | tf_op jit(solution)/shard_map/ppermute | solution.py:18
  150.4 20.8 %collective-permute-start.14 = (bf16[1,2,512,512]{3,2,1,0:T(8,128)(2,1)}, bf16[1,2,512,512]{3,2,1,0:T(8,128)(2,1)}, u32[]{:S(2)}, u32[]{:S(2)}) collective-permute-start(bf16[1,2,512,512]{3,2,1,0:T(8,128)(2,1)} %collective-permute-done.9.refs_0_.refs_4_), channel_id=1, source_target_pairs={{0,1},{1,0},{2,3},{3,2},{4,5},{5,4},{6,7},{7,6},{8,9},{9,8},{10,11... | collective-permute-start | bytes 3145736 | tf_op jit(solution)/shard_map/ppermute | solution.py:18
  150.9 29.4 %collective-permute-start.11 = (bf16[1,2,512,512]{3,2,1,0:T(8,128)(2,1)}, bf16[1,2,512,512]{3,2,1,0:T(8,128)(2,1)S(1)}, u32[]{:S(2)}, u32[]{:S(2)}) collective-permute-start(bf16[1,2,512,512]{3,2,1,0:T(8,128)(2,1)} %slice.21), channel_id=1, source_target_pairs={{0,4},{2,6},{4,0},{6,2},{8,12},{10,14},{12,8},{14,10},{1,5},{3,7},... | collective-permute-start | bytes 3145736 | tf_op jit(solution)/shard_map/ppermute | solution.py:18
  152.3 28.1 %collective-permute-start.12 = (bf16[1,2,512,512]{3,2,1,0:T(8,128)(2,1)}, bf16[1,2,512,512]{3,2,1,0:T(8,128)(2,1)}, u32[]{:S(2)}, u32[]{:S(2)}) collective-permute-start(bf16[1,2,512,512]{3,2,1,0:T(8,128)(2,1)} %collective-permute-done.7.refs_0_.refs_2_), channel_id=1, source_target_pairs={{0,2},{2,0},{4,6},{6,4},{8,10},{10,8},{12,14},{14,12},{1,3},{3,1},... | collective-permute-start | bytes 3145736 | tf_op jit(solution)/shard_map/ppermute | solution.py:18
  171.2 9.8 %copy-start.10 = (s32[2]{0:T(128)S(1)}, s32[2]{0:T(128)}, u32[]{:S(2)}) copy-start(s32[2]{0:T(128)} %constant.93.clone) | copy-start | bytes 28
  171.2 10.3 %copy-start.8 = (s32[2]{0:T(128)S(1)}, s32[2]{0:T(128)}, u32[]{:S(2)}) copy-start(s32[2]{0:T(128)} %get-tuple-element.55.ids) | copy-start | bytes 28
  171.2 10.8 %copy-start.1 = (bf16[2,2,1,512,512]{4,3,2,1,0:T(8,128)(2,1)S(1)}, bf16[2,2,1,512,512]{4,3,2,1,0:T(8,128)(2,1)}, u32[]{:S(2)}) copy-start(bf16[2,2,1,512,512]{4,3,2,1,0:T(8,128)(2,1)} %param.13) | copy-start | bytes 6291460
  180.3 2.2 %copy-start.7 = (bf16[1,2,512,512]{3,2,1,0:T(8,128)(2,1)}, bf16[1,2,512,512]{3,2,1,0:T(8,128)(2,1)S(1)}, u32[]{:S(2)}) copy-start(bf16[1,2,512,512]{3,2,1,0:T(8,128)(2,1)S(1)} %collective-permute-done.11.refs_0_.refs_6_) | copy-start | bytes 3145732
  180.3 13.4 %collective-permute-start.15 = (bf16[1,2,512,512]{3,2,1,0:T(8,128)(2,1)}, bf16[1,2,512,512]{3,2,1,0:T(8,128)(2,1)}, u32[]{:S(2)}, u32[]{:S(2)}) collective-permute-start(bf16[1,2,512,512]{3,2,1,0:T(8,128)(2,1)} %shard_map.139), channel_id=1, source_target_pairs={{0,1},{1,0},{2,3},{3,2},{4,5},{5,4},{6,7},{7,6},{8,9},{9,8},{10,11... | collective-permute-start | bytes 3145736 | tf_op jit(solution)/shard_map/ppermute | solution.py:18
  180.4 13.4 %collective-permute-start.16 = (bf16[1,2,512,512]{3,2,1,0:T(8,128)(2,1)S(1)}, bf16[1,2,512,512]{3,2,1,0:T(8,128)(2,1)}, u32[]{:S(2)}, u32[]{:S(2)}) collective-permute-start(bf16[1,2,512,512]{3,2,1,0:T(8,128)(2,1)S(1)} %collective-permute-done.11.refs_0_.refs_6_), channel_id=1, source_target_pairs={{0,1},{1,0},{2,3},{3,2},{4,5},{5,4},{6,7},{7,6},{8,9},{9,8},{10,11... | collective-permute-start | bytes 3145736 | tf_op jit(solution)/shard_map/ppermute | solution.py:18
  180.9 12.9 %collective-permute-start.17 = (bf16[1,2,512,512]{3,2,1,0:T(8,128)(2,1)}, bf16[1,2,512,512]{3,2,1,0:T(8,128)(2,1)}, u32[]{:S(2)}, u32[]{:S(2)}) collective-permute-start(bf16[1,2,512,512]{3,2,1,0:T(8,128)(2,1)} %collective-permute-done.12.refs_1_.refs_8_), channel_id=1, source_target_pairs={{0,1},{1,0},{2,3},{3,2},{4,5},{5,4},{6,7},{7,6},{8,9},{9,8},{10,11... | collective-permute-start | bytes 3145736 | tf_op jit(solution)/shard_map/ppermute | solution.py:18
  193.8 21.4 %copy-start.9 = (s32[16]{0:T(128)S(1)}, s32[16]{0:T(128)}, u32[]{:S(2)}) copy-start(s32[16]{0:T(128)} %param.14) | copy-start | bytes 196
  199.8 2.2 %collective-permute-start.18 = (f32[4,512]{1,0:T(4,128)S(1)}, f32[4,512]{1,0:T(4,128)S(1)}, u32[]{:S(2)}, u32[]{:S(2)}) collective-permute-start(f32[4,512]{1,0:T(4,128)S(1)} %pad_maximum_fusion), channel_id=1, source_target_pairs={{0,1},{1,0},{2,3},{3,2},{4,5},{5,4},{6,7},{7,6},{8,9},{9,8},{10,11... | collective-permute-start | bytes 24584 | tf_op jit(solution)/shard_map/ppermute | solution.py:18
  200.3 3.7 %collective-permute-start.19 = (f32[4,512]{1,0:T(4,128)S(1)}, f32[4,512]{1,0:T(4,128)S(1)}, u32[]{:S(2)}, u32[]{:S(2)}) collective-permute-start(f32[4,512]{1,0:T(4,128)S(1)} %pad_maximum_fusion), channel_id=1, source_target_pairs={{0,2},{1,3},{2,0},{3,1},{4,6},{5,7},{6,4},{7,5},{8,10},{9,11},{10,... | collective-permute-start | bytes 24584 | tf_op jit(solution)/shard_map/ppermute | solution.py:18
  202.1 3.1 %collective-permute-start.20 = (f32[4,512]{1,0:T(4,128)S(1)}, f32[4,512]{1,0:T(4,128)S(1)}, u32[]{:S(2)}, u32[]{:S(2)}) collective-permute-start(f32[4,512]{1,0:T(4,128)S(1)} %pad_maximum_fusion), channel_id=1, source_target_pairs={{0,3},{1,2},{2,1},{3,0},{4,7},{5,6},{6,5},{7,4},{8,11},{9,10},{10,... | collective-permute-start | bytes 24584 | tf_op jit(solution)/shard_map/ppermute | solution.py:18
  205.2 4.9 %collective-permute-start.21 = (f32[4,512]{1,0:T(4,128)S(1)}, f32[4,512]{1,0:T(4,128)S(1)}, u32[]{:S(2)}, u32[]{:S(2)}) collective-permute-start(f32[4,512]{1,0:T(4,128)S(1)} %add_add_fusion.1), channel_id=1, source_target_pairs={{0,4},{1,5},{2,6},{3,7},{4,0},{5,1},{6,2},{7,3},{8,12},{9,13},{10,... | collective-permute-start | bytes 24584 | tf_op jit(solution)/shard_map/ppermute | solution.py:18
  206.6 4.5 %collective-permute-start.22 = (f32[4,512]{1,0:T(4,128)S(1)}, f32[4,512]{1,0:T(4,128)S(1)}, u32[]{:S(2)}, u32[]{:S(2)}) collective-permute-start(f32[4,512]{1,0:T(4,128)S(1)} %add_add_fusion.1), channel_id=1, source_target_pairs={{0,8},{1,9},{2,10},{3,11},{4,12},{5,13},{6,14},{7,15},{8,0},{9,1},... | collective-permute-start | bytes 24584 | tf_op jit(solution)/shard_map/ppermute | solution.py:18
  208.9 5.4 %collective-permute-start.23 = (f32[4,512]{1,0:T(4,128)S(1)}, f32[4,512]{1,0:T(4,128)S(1)}, u32[]{:S(2)}, u32[]{:S(2)}) collective-permute-start(f32[4,512]{1,0:T(4,128)S(1)} %add_add_fusion.1), channel_id=1, source_target_pairs={{0,12},{1,13},{2,14},{3,15},{4,8},{5,9},{6,10},{7,11},{8,4},{9,5},... | collective-permute-start | bytes 24584 | tf_op jit(solution)/shard_map/ppermute | solution.py:18

commit v6 on v5

--- a/solution.py
+++ b/solution.py
@@ -8,7 +8,6 @@
 from jax.experimental.pallas import tpu as pltpu
 from jax.sharding import PartitionSpec as P
 
-LANES = 256
 VMEM_LIMIT = 60 * 1024 * 1024
 HINT = pl.CostEstimate(flops=1, bytes_accessed=1, transcendentals=0)
 
@@ -36,58 +35,76 @@
     return value
 
 
-def accumulate(freq, first, r_ref, w_refs, total, held, sem, field, tot, tot_sem):
-    piece, step = pl.program_id(0), pl.program_id(1)
-    lanes = field.shape[3]
-
-    @pl.when((piece == 0) & (step == 0))
-    def _():
-        for k, ref in enumerate(w_refs):
-            source = ref.at[freq if ref.shape[0] > 1 else 0]
-            pltpu.make_async_copy(source, held.at[k], sem.at[k]).start()
+def piece_copies(freq, ids, cross, ref, k, left, right, sem):
+    width = ref.shape[2]
+    columns = pl.ds(pl.multiple_of(ids[k] * width, width), width)
+    which = freq if ref.shape[0] > 1 else 0
+    low, high = pl.ds(0, width), pl.ds(width, width)
+    return [
+        pltpu.make_async_copy(ref.at[which, 0], right.at[k, 0, low], sem.at[k, 0]),
+        pltpu.make_async_copy(ref.at[which, 1], right.at[k, 1, low], sem.at[k, 1]),
+        pltpu.make_async_copy(ref.at[which, 0], right.at[k, 1, high], sem.at[k, 2]),
+        pltpu.make_async_copy(cross.at[freq, 0, :, columns], left.at[k, :, low], sem.at[k, 3]),
+        pltpu.make_async_copy(cross.at[freq, 1, :, columns], left.at[k, :, high], sem.at[k, 4]),
+    ]
+
+
+def accumulate(freq, ids, first, cross, w_refs, total, left, right, sem, field, tot, tot_sem):
+    piece, part = pl.program_id(0), pl.program_id(1)
+    copies = [
+        piece_copies(freq, ids, cross, ref, k, left, right, sem) for k, ref in enumerate(w_refs)
+    ]
+
+    @pl.when((piece == 0) & (part == 0))
+    def _():
+        for group in copies:
+            for copy in group:
+                copy.start()
         if total is not None:
             pltpu.make_async_copy(total, tot, tot_sem.at[0]).start()
         first()
 
-    @pl.when(step == 0)
-    def _():
-        pltpu.make_async_copy(w_refs[0].at[0], held.at[piece], sem.at[piece]).wait()
-
-    here = pl.ds(pl.multiple_of(step * lanes, lanes), lanes)
-    rows_re, rows_im = r_ref[0, 0], r_ref[0, 1]
-    w_re, w_im = held[piece, 0, :, here], held[piece, 1, :, here]
+    for k, group in enumerate(copies):
+
+        @pl.when((piece == k) & (part == 0))
+        def _(k=k, group=group):
+            for copy in group:
+                copy.wait()
+            width = right.shape[2] // 2
+            right[k, 0, width:] = -right[k, 1, :width]
+
     dot = functools.partial(jnp.dot, preferred_element_type=jnp.float32)
 
     @pl.when(piece == 0)
     def _():
-        field[step, 0] = dot(rows_re, w_re) + dot(rows_im, -w_im)
-        field[step, 1] = dot(rows_re, w_im) + dot(rows_im, w_re)
+        field[part] = dot(left[piece], right[piece, part])
 
     @pl.when(piece > 0)
     def _():
-        field[step, 0] += dot(rows_re, w_re) + dot(rows_im, -w_im)
-        field[step, 1] += dot(rows_re, w_im) + dot(rows_im, w_re)
+        field[part] += dot(left[piece], right[piece, part])
 
     if total is not None:
 
-        @pl.when((piece == len(w_refs) - 1) & (step == 0))
+        @pl.when((piece == len(w_refs) - 1) & (part == 0))
         def _():
             pltpu.make_async_copy(total, tot, tot_sem.at[0]).wait()
 
 
-def field_kernel(freq, count, ids, r_ref, *refs):
-    w_refs, (total, out, held, sem, field, tot, tot_sem) = refs[:count], refs[count:]
-    accumulate(freq, lambda: None, r_ref, w_refs, total, held, sem, field, tot, tot_sem)
-    step = pl.program_id(1)
+def field_kernel(freq, count, ids, cross, *refs):
+    w_refs, (total, out, left, right, sem, field, tot, tot_sem) = refs[:count], refs[count:]
+    accumulate(
+        freq, ids, lambda: None, cross, w_refs, total, left, right, sem, field, tot, tot_sem
+    )
+    part = pl.program_id(1)
 
     @pl.when(pl.program_id(0) == count - 1)
     def _():
-        out[0] = field[step] + tot[step]
-
-
-def first_kernel(freq, count, ids, r_ref, *refs):
-    w_refs, (out, held, sem, field) = refs[:count], refs[count:]
-    accumulate(freq, lambda: None, r_ref, w_refs, None, held, sem, field, None, None)
+        out[0] = field[part] + tot[part]
+
+
+def first_kernel(freq, count, ids, cross, *refs):
+    w_refs, (out, left, right, sem, field) = refs[:count], refs[count:]
+    accumulate(freq, ids, lambda: None, cross, w_refs, None, left, right, sem, field, None, None)
 
     @pl.when(pl.program_id(0) == count - 1)
     def _():
@@ -112,46 +129,49 @@
     pltpu.make_async_copy(singles[0].at[0], rows.at[:, here], sem.at[slot]).wait()
 
 
-def fold(rows_re, rows_im, re, im):
-    product = rows_re.astype(jnp.float32) * re + rows_im.astype(jnp.float32) * im
+def fold(rows, field):
+    product = rows.astype(jnp.float32) * field
     return jnp.sum(product.reshape(-1, 8, product.shape[-1]), axis=0)
 
 
-def numer_kernel(freq, count, ids, r_ref, *refs):
+def numer_kernel(freq, count, ids, cross, *refs):
     w_refs, total, whole = refs[:count], refs[count], refs[count + 1 : count + 3]
-    singles = refs[count + 3 : -8]
-    out, held, sem, field, tot, tot_sem, rows, row_sem = refs[-8:]
+    singles = refs[count + 3 : -9]
+    out, left, right, sem, field, tot, tot_sem, rows, row_sem = refs[-9:]
     begin = lambda: start_rows(freq, ids, count, whole, singles, rows, row_sem)
-    accumulate(freq, begin, r_ref, w_refs, total, held, sem, field, tot, tot_sem)
-    step = pl.program_id(1)
-    lanes = field.shape[3]
+    accumulate(freq, ids, begin, cross, w_refs, total, left, right, sem, field, tot, tot_sem)
+    part = pl.program_id(1)
     last = pl.program_id(0) == count - 1
 
-    @pl.when(last & (step == 0))
-    def _():
+    @pl.when(last & (part == 0))
+    def _():
+        out[...] = jnp.zeros_like(out)
         for slot in range(2):
             wait_rows(slot, singles, rows, row_sem)
 
     @pl.when(last)
     def _():
-        here = pl.ds(pl.multiple_of(step * lanes, lanes), lanes)
-        re, im = field[step, 0] + tot[step, 0], field[step, 1] + tot[step, 1]
-        out[...] = fold(rows[0, :, here], rows[1, :, here], re, im)
+        out[...] += fold(rows[part], field[part] + tot[part])
 
 
 def dot_kernel(freq, ids, field, *refs):
     whole, singles, (out, rows, sem) = refs[:2], refs[2:-3], refs[-3:]
-    step = pl.program_id(0)
-    lanes = field.shape[3]
-
-    @pl.when(step == 0)
-    def _():
+    slot, part = pl.program_id(0), pl.program_id(1)
+    width = field.shape[1]
+
+    @pl.when((slot == 0) & (part == 0))
+    def _():
+        out[...] = jnp.zeros_like(out)
         start_rows(freq, ids, 0, whole, singles, rows, sem)
-        for slot in range(2):
-            wait_rows(slot, singles, rows, sem)
-
-    here = pl.ds(pl.multiple_of(step * lanes, lanes), lanes)
-    out[...] = fold(rows[0, :, here], rows[1, :, here], field[0, 0], field[0, 1])
+
+    for k in range(2):
+
+        @pl.when((slot == k) & (part == 0))
+        def _(k=k):
+            wait_rows(k, singles, rows, sem)
+
+    here = pl.ds(pl.multiple_of(slot * width, width), width)
+    out[...] += fold(rows[part, here], field[0])
 
 
 ANYWHERE = pl.BlockSpec(memory_space=pl.ANY)
@@ -159,21 +179,21 @@
 
 def call(kernel, cross, freq, ids, pieces, rest, out_shape, out_spec, has_total, scratch):
     rows, (width, sources) = cross.shape[2], pieces[0].shape[2:]
-    count, steps = len(pieces), sources // LANES
-    total = [pltpu.VMEM((steps, 2, rows, LANES), jnp.float32), pltpu.SemaphoreType.DMA((1,))]
+    count, dtype = len(pieces), pieces[0].dtype
+    total = [pltpu.VMEM((2, rows, sources), jnp.float32), pltpu.SemaphoreType.DMA((1,))]
     return pl.pallas_call(
         functools.partial(kernel, freq, count),
         out_shape=out_shape,
         grid_spec=pltpu.PrefetchScalarGridSpec(
             num_scalar_prefetch=1,
-            grid=(count, steps),
-            in_specs=[pl.BlockSpec((1, 2, rows, width), lambda p, n, ids: (freq, 0, 0, ids[p]))]
-            + [ANYWHERE] * (count + len(rest)),
+            grid=(count, 2),
+            in_specs=[ANYWHERE] * (1 + count + len(rest)),
             out_specs=out_spec,
             scratch_shapes=[
-                pltpu.VMEM((count, 2, width, sources), pieces[0].dtype),
-                pltpu.SemaphoreType.DMA((count,)),
-                pltpu.VMEM((steps, 2, rows, LANES), jnp.float32),
+                pltpu.VMEM((count, rows, 2 * width), dtype),
+                pltpu.VMEM((count, 2, 2 * width, sources), dtype),
+                pltpu.SemaphoreType.DMA((count, 5)),
+                pltpu.VMEM((2, rows, sources), jnp.float32),
                 *(total if has_total else []),
                 *scratch,
             ],
@@ -193,9 +213,9 @@
         ids,
         pieces,
         [] if total is None else [total],
-        jax.ShapeDtypeStruct((sources // LANES, 2, rows, LANES), jnp.float32),
+        jax.ShapeDtypeStruct((2, rows, sources), jnp.float32),
         pl.BlockSpec(
-            (1, 2, rows, LANES), lambda p, n, ids: (jnp.where(p == count - 1, n, 0), 0, 0, 0)
+            (1, rows, sources), lambda p, part, ids: (jnp.where(p == count - 1, part, 0), 0, 0)
         ),
         total is not None,
         [],
@@ -208,7 +228,6 @@
 
 def finish(cross, freq, ids, pieces, total, whole, singles):
     rows, sources = cross.shape[2], pieces[0].shape[3]
-    count = len(pieces)
     out = call(
         numer_kernel,
         cross,
@@ -217,7 +236,7 @@
         pieces,
         [total, *whole, *singles],
         jax.ShapeDtypeStruct((8, sources), jnp.float32),
-        pl.BlockSpec((8, LANES), lambda p, n, ids: (0, jnp.where(p == count - 1, n, 0))),
+        pl.BlockSpec((8, sources), lambda p, part, ids: (0, 0)),
         True,
         row_scratch(rows, sources, pieces[0].dtype),
     )
@@ -225,17 +244,18 @@
 
 
 def dot_rows(freq, ids, field, whole, singles):
-    steps, _, rows, lanes = field.shape
-    sources = steps * lanes
+    _, rows, sources = field.shape
     out = pl.pallas_call(
         functools.partial(dot_kernel, freq),
         out_shape=jax.ShapeDtypeStruct((8, sources), jnp.float32),
         grid_spec=pltpu.PrefetchScalarGridSpec(
             num_scalar_prefetch=1,
-            grid=(steps,),
-            in_specs=[pl.BlockSpec((1, 2, rows, lanes), lambda n, ids: (n, 0, 0, 0))]
+            grid=(2, 2),
+            in_specs=[
+                pl.BlockSpec((1, rows // 2, sources), lambda slot, part, ids: (part, slot, 0))
+            ]
             + [ANYWHERE] * (2 + len(singles)),
-            out_specs=pl.BlockSpec((8, lanes), lambda n, ids: (0, n)),
+            out_specs=pl.BlockSpec((8, sources), lambda slot, part, ids: (0, 0)),
             scratch_shapes=row_scratch(rows, sources, whole[0].dtype),
         ),
         compiler_params=pltpu.CompilerParams(vmem_limit_bytes=VMEM_LIMIT),

time: 217 us -> 213 us (0.982)
  Pallas kernels: 103 us -> 92.2 us
  waiting for transfers between devices: 71.2 us -> 78.1 us
    pallas_call x9, Pallas kernels: 90.9 us -> 79.9 us  [call(): pl.pallas_call(functools.partial(kernel, freq, count), out_shape=out_shap...]
    ppermute x24, waiting for transfers between devices: 71.2 us -> 78.1 us  [swap(): lax.ppermute(value, axis, [(source, source ^ mask) for source in range(si...]
  transfers between devices with their start and end apart: 24 -> 24, of which waited for: 10 -> 10; matrix products, arithmetic and copies ran while one was open for 4% -> 4% of each run, Pallas kernels for 45% -> 41%
where the time goes in v6:
time: 213 us; the launch traced here: 212 us
  Pallas kernels  92.2 us (43%)
  waiting for transfers between devices  78.1 us (37%)
  starting transfers between devices  28.1 us (13%)
  local copies, waits for them, and re-layouts  6.37 us (3%)
  other arithmetic  5.87 us (3%)
    pallas_call x9, Pallas kernels, call(): pl.pallas_call(functools.partial(kernel, freq, count), out_shape=out_shap...  79.9 us
    ppermute x24, waiting for transfers between devices, swap(): lax.ppermute(value, axis, [(source, source ^ mask) for source in range(si...  78.1 us
    ppermute x24, starting transfers between devices, swap(): lax.ppermute(value, axis, [(source, source ^ mask) for source in range(si...  28.1 us
    pallas_call x2, Pallas kernels, pick_rows(): pl.pallas_call(functools.partial(pick_kernel, plan), out_shape=jax.ShapeD...  6.53 us
    pallas_call x1, Pallas kernels, dot_rows(): pl.pallas_call(functools.partial(dot_kernel, freq), out_shape=jax.ShapeDt...  5.7 us
  transfers between devices with their start and end apart: 24, of which 10 were waited for; matrix products, arithmetic and copies ran while one was open for 4% of the time, Pallas kernels for 41%

profile of v6, /device:TPU:0, one launch (start us, length us, event | category | flops | bytes accessed | tf_op | source)
XLA Modules:
  0.0 212.4 jit_solution(6172644639328740242)
XLA Ops:
  0.6 2.3 %slice_bitcast_fusion = bf16[1,2,512,512]{3,2,1,0:T(8,128)(2,1)} fusion(bf16[2,2,1,512,512]{4,3,1,2,0:T(8,128)(2,1)} %bitcast.16), kind=kLoop, calls=%fused_computation.3 | loop fusion | bytes 2097152 | tf_op jit(solution)/shard_map/slice | solution.py:317
  2.9 2.9 %collective-permute-start = (bf16[2,2,512,512]{3,2,1,0:T(8,128)(2,1)}, bf16[2,2,512,512]{3,2,1,0:T(8,128)(2,1)}, u32[]{:S(2)}, u32[]{:S(2)}) collective-permute-start(bf16[2,2,512,512]{3,2,1,0:T(8,128)(2,1)} %bitcast.17), channel_id=1, source_target_pairs={{0,2},{2,0},{4,6},{6,4},{8,10},{10,8},{12,14},{14,12},{1,3},{3,1},... | collective-permute-start | bytes 6291464 | tf_op jit(solution)/shard_map/ppermute | solution.py:17
  5.9 2.6 %collective-permute-start.1 = (bf16[1,2,512,512]{3,2,1,0:T(8,128)(2,1)}, bf16[1,2,512,512]{3,2,1,0:T(8,128)(2,1)S(1)}, u32[]{:S(2)}, u32[]{:S(2)}) collective-permute-start(bf16[1,2,512,512]{3,2,1,0:T(8,128)(2,1)} %slice_bitcast_fusion), channel_id=1, source_target_pairs={{0,8},{2,10},{4,12},{6,14},{8,0},{10,2},{12,4},{14,6},{1,9},{3,11}... | collective-permute-start | bytes 3145736 | tf_op jit(solution)/shard_map/ppermute | solution.py:17
  8.4 1.6 collective-permute-start.2
  10.0 6.0 %shard_map.131.refs_3_ = f32[2,1024,512]{2,1,0:T(8,128)} custom-call(s32[1]{0:T(128)} %bitcast.3.ids, bf16[2,2,1024,4096]{3,2,1,0:T(8,128)(2,1)} %cross.17, bf16[2,2,512,512]{3,2,1,0:T(8,128)(2,1)} %bitcast.18), custom_call_target="tpu_custom_call" | custom-call | flops 1 | bytes 1 | tf_op jit(solution)/shard_map/pallas_call | solution.py:184
  16.1 6.1 %shard_map.132.refs_1_ = f32[2,1024,512]{2,1,0:T(8,128)} custom-call(s32[1]{0:T(128)} %bitcast.3.ids, bf16[2,2,1024,4096]{3,2,1,0:T(8,128)(2,1)} %cross.17, bf16[2,2,512,512]{3,2,1,0:T(8,128)(2,1)} %bitcast.19), custom_call_target="tpu_custom_call" | custom-call | flops 1 | bytes 1 | tf_op jit(solution)/shard_map/pallas_call | solution.py:184
  22.2 1.1 slice.20
  23.3 30.9 %collective-permute-done.1.refs_2_.refs_4_ = bf16[1,2,512,512]{3,2,1,0:T(8,128)(2,1)S(1)} collective-permute-done((bf16[1,2,512,512]{3,2,1,0:T(8,128)(2,1)}, bf16[1,2,512,512]{3,2,1,0:T(8,128)(2,1)S(1)}, u32[]{:S(2)}, u32[]{:S(2)}) %collective-permute-start.1) | collective-permute-done | bytes 1048608 | tf_op jit(solution)/shard_map/ppermute | solution.py:17
  54.5 1.4 collective-permute-start.4
  55.9 0.5 collective-permute-start.5
  56.4 1.5 collective-permute-start.6
  57.9 2.3 %collective-permute-start.3 = (bf16[1,2,512,512]{3,2,1,0:T(8,128)(2,1)}, bf16[1,2,512,512]{3,2,1,0:T(8,128)(2,1)}, u32[]{:S(2)}, u32[]{:S(2)}) collective-permute-start(bf16[1,2,512,512]{3,2,1,0:T(8,128)(2,1)} %slice.20), channel_id=1, source_target_pairs={{0,8},{2,10},{4,12},{6,14},{8,0},{10,2},{12,4},{14,6},{1,9},{3,11}... | collective-permute-start | bytes 3145736 | tf_op jit(solution)/shard_map/ppermute | solution.py:17
  60.2 0.5 broadcast_xor_fusion.3.ids
  60.7 12.4 %shard_map.133.refs_3_ = f32[2,1024,512]{2,1,0:T(8,128)} custom-call(s32[3]{0:T(128)} %broadcast_xor_fusion.3.ids, bf16[2,2,1024,4096]{3,2,1,0:T(8,128)(2,1)} %cross.17, bf16[2,2,512,512]{3,2,1,0:T(8,128)(2,1)} %collective-permute-done.refs_0_.refs_1_, bf16[1,2,512,512]{3,2,1,0:T(8,128)(2,1)} %collective-permute-done.2.refs_1_.refs_2_, ...), custom_call_target="tpu_custom_call" | custom-call | flops 1 | bytes 1 | tf_op jit(solution)/shard_map/pallas_call | solution.py:184
  73.2 6.5 %shard_map.134.refs_1_ = f32[2,1024,512]{2,1,0:T(8,128)} custom-call(s32[1]{0:T(128)S(6)} %xor.53.ids, bf16[2,2,1024,4096]{3,2,1,0:T(8,128)(2,1)} %cross.17, bf16[2,2,512,512]{3,2,1,0:T(8,128)(2,1)} %collective-permute-done.refs_0_.refs_1_, f32[2,1024,512]{2,1,0:T(8,128)} %shard_map.132.refs_1_), custom_call_target="tpu_custom_call" | custom-call | flops 1 | bytes 1 | tf_op jit(solution)/shard_map/pallas_call | solution.py:184
  79.7 2.3 %slice.21 = bf16[1,2,512,512]{3,2,1,0:T(8,128)(2,1)} slice(bf16[2,2,512,512]{3,2,1,0:T(8,128)(2,1)} %collective-permute-done.refs_0_.refs_1_), slice={[1:2], [0:2], [0:512], [0:512]} | slice | bytes 2097152 | tf_op jit(solution)/shard_map/slice | solution.py:332
  82.0 16.8 %collective-permute-done.4.refs_2_.refs_6_ = bf16[1,2,512,512]{3,2,1,0:T(8,128)(2,1)S(1)} collective-permute-done((bf16[1,2,512,512]{3,2,1,0:T(8,128)(2,1)S(1)}, bf16[1,2,512,512]{3,2,1,0:T(8,128)(2,1)S(1)}, u32[]{:S(2)}, u32[]{:S(2)}) %collective-permute-start.4) | collective-permute-done | bytes 1048608 | tf_op jit(solution)/shard_map/ppermute | solution.py:17
  98.8 3.5 %collective-permute-done.6.refs_0_.refs_3_ = bf16[1,2,512,512]{3,2,1,0:T(8,128)(2,1)} collective-permute-done((bf16[1,2,512,512]{3,2,1,0:T(8,128)(2,1)}, bf16[1,2,512,512]{3,2,1,0:T(8,128)(2,1)}, u32[]{:S(2)}, u32[]{:S(2)}) %collective-permute-start.6) | collective-permute-done | bytes 1048608 | tf_op jit(solution)/shard_map/ppermute | solution.py:17
  102.3 3.3 %collective-permute-done.3.refs_0_.refs_7_ = bf16[1,2,512,512]{3,2,1,0:T(8,128)(2,1)} collective-permute-done((bf16[1,2,512,512]{3,2,1,0:T(8,128)(2,1)}, bf16[1,2,512,512]{3,2,1,0:T(8,128)(2,1)}, u32[]{:S(2)}, u32[]{:S(2)}) %collective-permute-start.3) | collective-permute-done | bytes 1048608 | tf_op jit(solution)/shard_map/ppermute | solution.py:17
  106.1 2.0 collective-permute-start.8
  108.1 1.5 collective-permute-start.9
  109.6 0.6 compare_select_fusion.5
  110.2 0.5 broadcast_xor_fusion.2.ids
  110.7 12.5 %shard_map.135.refs_1_ = f32[2,1024,512]{2,1,0:T(8,128)} custom-call(s32[3]{0:T(128)} %broadcast_xor_fusion.2.ids, bf16[2,2,1024,4096]{3,2,1,0:T(8,128)(2,1)} %cross.17, bf16[1,2,512,512]{3,2,1,0:T(8,128)(2,1)} %collective-permute-done.6.refs_0_.refs_3_, bf16[1,2,512,512]{3,2,1,0:T(8,128)(2,1)} %copy-done.6, bf16[1,2,512,512]{3,2,1,0:T(8,128)(2,1)} %copy-done.5, ...), custom_call_target="tpu_custom_call" | custom-call | flops 1 | bytes 1 | tf_op jit(solution)/shard_map/pallas_call | solution.py:184
  123.2 4.8 %shard_map.137.refs_2_.refs_0_ = bf16[2,2,1024,512]{3,2,1,0:T(8,128)(2,1)} custom-call(s32[2]{0:T(128)} %get-tuple-element.55.ids, bf16[2,2,512,512]{3,2,1,0:T(8,128)(2,1)} %bitcast.20, bf16[2,2,512,512]{3,2,1,0:T(8,128)(2,1)} %collective-permute-done.refs_0_.refs_1_, bf16[1,2,512,512]{3,2,1,0:T(8,128)(2,1)} %collective-permute-done.2.refs_1_.refs_2_, ...), custom_call_target="tpu_custom_call" | custom-call | flops 1 | bytes 1 | tf_op jit(solution)/shard_map/pallas_call | solution.py:289
  128.1 6.4 %shard_map.136.refs_3_ = f32[2,1024,512]{2,1,0:T(8,128)} custom-call(s32[1]{0:T(128)S(6)} %xor.55.ids, bf16[2,2,1024,4096]{3,2,1,0:T(8,128)(2,1)} %cross.17, bf16[1,2,512,512]{3,2,1,0:T(8,128)(2,1)} %collective-permute-done.3.refs_0_.refs_7_, f32[2,1024,512]{2,1,0:T(8,128)} %shard_map.134.refs_1_), custom_call_target="tpu_custom_call" | custom-call | flops 1 | bytes 1 | tf_op jit(solution)/shard_map/pallas_call | solution.py:184
  134.5 15.9 %collective-permute-done.8.refs_2_.refs_4_ = bf16[1,2,512,512]{3,2,1,0:T(8,128)(2,1)S(1)} collective-permute-done((bf16[1,2,512,512]{3,2,1,0:T(8,128)(2,1)}, bf16[1,2,512,512]{3,2,1,0:T(8,128)(2,1)S(1)}, u32[]{:S(2)}, u32[]{:S(2)}) %collective-permute-start.8) | collective-permute-done | bytes 1048608 | tf_op jit(solution)/shard_map/ppermute | solution.py:17
  150.9 1.4 collective-permute-start.11
  152.3 1.5 collective-permute-start.12
  153.8 0.6 pad_add_fusion.1.ids
  154.4 0.5 broadcast_xor_fusion.1.ids
  154.9 12.4 %shard_map.138.refs_2_ = f32[2,1024,512]{2,1,0:T(8,128)} custom-call(s32[3]{0:T(128)} %broadcast_xor_fusion.1.ids, bf16[2,2,1024,4096]{3,2,1,0:T(8,128)(2,1)} %cross.17, bf16[1,2,512,512]{3,2,1,0:T(8,128)(2,1)} %collective-permute-done.7.refs_0_.refs_2_, bf16[1,2,512,512]{3,2,1,0:T(8,128)(2,1)} %copy-done.2, bf16[1,2,512,512]{3,2,1,0:T(8,128)(2,1)} %copy-done.3, ...), custom_call_target="tpu_custom_call" | custom-call | flops 1 | bytes 1 | tf_op jit(solution)/shard_map/pallas_call | solution.py:184
  167.4 1.7 shard_map.139
  169.2 7.8 %shard_map.140 = f32[8,512]{1,0:T(8,128)} custom-call(s32[3]{0:T(128)} %pad_add_fusion.1.ids, bf16[2,2,1024,4096]{3,2,1,0:T(8,128)(2,1)} %cross.17, bf16[1,2,512,512]{3,2,1,0:T(8,128)(2,1)} %collective-permute-done.9.refs_0_.refs_4_, f32[2,1024,512]{2,1,0:T(8,128)} %shard_map.135.refs_1_, bf16[2,2,1024,512]{3,2,1,0:T(8,128)(2,1)} %shard_map.137.refs_2_.refs_0_, ...), custom_call_target="tpu_custom_call" | custom-call | flops 1 | bytes 1 | tf_op jit(solution)/shard_map/pallas_call | solution.py:184
  176.9 0.7 reduce_sum.27
  178.9 0.5 compare_select_fusion.4.ids
  179.8 9.8 %shard_map.141.field = f32[2,1024,512]{2,1,0:T(8,128)} custom-call(s32[2]{0:T(128)} %broadcast_xor_fusion.ids, bf16[2,2,1024,4096]{3,2,1,0:T(8,128)(2,1)} %cross.17, bf16[1,2,512,512]{3,2,1,0:T(8,128)(2,1)} %copy-done.7, bf16[1,2,512,512]{3,2,1,0:T(8,128)(2,1)} %collective-permute-done.12.refs_1_.refs_8_, f32[2,1024,512]{2,1,0:T(8,128)} %shard_map.138.refs_2_), custom_call_target="tpu_custom_call" | custom-call | flops 1 | bytes 1 | tf_op jit(solution)/shard_map/pallas_call | solution.py:184
  189.7 5.7 %shard_map.142 = f32[8,512]{1,0:T(8,128)} custom-call(s32[2]{0:T(128)} %compare_select_fusion.4.ids, f32[2,1024,512]{2,1,0:T(8,128)} %shard_map.141.field, bf16[2,2,1024,512]{3,2,1,0:T(8,128)(2,1)} %shard_map.137.refs_2_.refs_0_, bf16[2,2,1024,512]{3,2,1,0:T(8,128)(2,1)} %collective-permute-done.13.refs_3_.refs_1_, ...), custom_call_target="tpu_custom_call" | custom-call | flops 1 | bytes 1 | tf_op jit(solution)/shard_map/pallas_call | solution.py:248
  195.4 0.7 reduce_sum.28
  196.6 1.8 collective-permute-start.19
  198.4 1.9 collective-permute-done.19
  200.3 1.2 collective-permute-done.20
  201.5 0.7 collective-permute-start.21
  202.3 3.0 %collective-permute-start.22 = (f32[4,512]{1,0:T(4,128)S(1)}, f32[4,512]{1,0:T(4,128)S(1)}, u32[]{:S(2)}, u32[]{:S(2)}) collective-permute-start(f32[4,512]{1,0:T(4,128)S(1)} %add_add_fusion.1), channel_id=1, source_target_pairs={{0,8},{1,9},{2,10},{3,11},{4,12},{5,13},{6,14},{7,15},{8,0},{9,1},... | collective-permute-start | bytes 24584 | tf_op jit(solution)/shard_map/ppermute | solution.py:17
  205.3 1.2 collective-permute-start.23
  206.9 3.8 %collective-permute-done.23 = f32[4,512]{1,0:T(4,128)S(1)} collective-permute-done((f32[4,512]{1,0:T(4,128)S(1)}, f32[4,512]{1,0:T(4,128)S(1)}, u32[]{:S(2)}, u32[]{:S(2)}) %collective-permute-start.23) | collective-permute-done | bytes 8224 | tf_op jit(solution)/shard_map/ppermute | solution.py:17
  211.0 0.6 constant_dynamic-slice_fusion
  211.6 0.8 fusion
  (61 shorter events, 4.2 us)
Async XLA Ops:
  2.9 51.5 %collective-permute-start = (bf16[2,2,512,512]{3,2,1,0:T(8,128)(2,1)}, bf16[2,2,512,512]{3,2,1,0:T(8,128)(2,1)}, u32[]{:S(2)}, u32[]{:S(2)}) collective-permute-start(bf16[2,2,512,512]{3,2,1,0:T(8,128)(2,1)} %bitcast.17), channel_id=1, source_target_pairs={{0,2},{2,0},{4,6},{6,4},{8,10},{10,8},{12,14},{14,12},{1,3},{3,1},... | collective-permute-start | bytes 6291464 | tf_op jit(solution)/shard_map/ppermute | solution.py:17
  5.9 48.3 %collective-permute-start.1 = (bf16[1,2,512,512]{3,2,1,0:T(8,128)(2,1)}, bf16[1,2,512,512]{3,2,1,0:T(8,128)(2,1)S(1)}, u32[]{:S(2)}, u32[]{:S(2)}) collective-permute-start(bf16[1,2,512,512]{3,2,1,0:T(8,128)(2,1)} %slice_bitcast_fusion), channel_id=1, source_target_pairs={{0,8},{2,10},{4,12},{6,14},{8,0},{10,2},{12,4},{14,6},{1,9},{3,11}... | collective-permute-start | bytes 3145736 | tf_op jit(solution)/shard_map/ppermute | solution.py:17
  8.4 46.0 %collective-permute-start.2 = (bf16[1,2,512,512]{3,2,1,0:T(8,128)(2,1)}, bf16[1,2,512,512]{3,2,1,0:T(8,128)(2,1)}, u32[]{:S(2)}, u32[]{:S(2)}) collective-permute-start(bf16[1,2,512,512]{3,2,1,0:T(8,128)(2,1)} %slice_bitcast_fusion), channel_id=1, source_target_pairs={{0,4},{2,6},{4,0},{6,2},{8,12},{10,14},{12,8},{14,10},{1,5},{3,7},... | collective-permute-start | bytes 3145736 | tf_op jit(solution)/shard_map/ppermute | solution.py:17
  16.0 6.1 %copy-start = (bf16[2,2,1,512,512]{4,3,2,1,0:T(8,128)(2,1)S(1)}, bf16[2,2,1,512,512]{4,3,2,1,0:T(8,128)(2,1)}, u32[]{:S(2)}) copy-start(bf16[2,2,1,512,512]{4,3,2,1,0:T(8,128)(2,1)} %param.13) | copy-start | bytes 6291460
  16.1 44.2 %copy-start.13 = (s32[3]{0:T(128)S(1)}, s32[3]{0:T(128)}, u32[]{:S(2)}) copy-start(s32[3]{0:T(128)} %constant.87.clone) | copy-start | bytes 40
  54.2 6.6 %copy-start.4 = (bf16[1,2,512,512]{3,2,1,0:T(8,128)(2,1)}, bf16[1,2,512,512]{3,2,1,0:T(8,128)(2,1)S(1)}, u32[]{:S(2)}) copy-start(bf16[1,2,512,512]{3,2,1,0:T(8,128)(2,1)S(1)} %collective-permute-done.1.refs_2_.refs_4_) | copy-start | bytes 3145732
  54.5 44.3 %collective-permute-start.4 = (bf16[1,2,512,512]{3,2,1,0:T(8,128)(2,1)S(1)}, bf16[1,2,512,512]{3,2,1,0:T(8,128)(2,1)S(1)}, u32[]{:S(2)}, u32[]{:S(2)}) collective-permute-start(bf16[1,2,512,512]{3,2,1,0:T(8,128)(2,1)S(1)} %collective-permute-done.1.refs_2_.refs_4_), channel_id=1, source_target_pairs={{0,4},{2,6},{4,0},{6,2},{8,12},{10,14},{12,8},{14,10},{1,5},{3,7},... | collective-permute-start | bytes 3145736 | tf_op jit(solution)/shard_map/ppermute | solution.py:17
  55.9 42.9 %collective-permute-start.5 = (bf16[1,2,512,512]{3,2,1,0:T(8,128)(2,1)S(1)}, bf16[1,2,512,512]{3,2,1,0:T(8,128)(2,1)S(1)}, u32[]{:S(2)}, u32[]{:S(2)}) collective-permute-start(bf16[1,2,512,512]{3,2,1,0:T(8,128)(2,1)S(1)} %collective-permute-done.1.refs_2_.refs_4_), channel_id=1, source_target_pairs={{0,2},{2,0},{4,6},{6,4},{8,10},{10,8},{12,14},{14,12},{1,3},{3,1},... | collective-permute-start | bytes 3145736 | tf_op jit(solution)/shard_map/ppermute | solution.py:17
  56.4 45.8 %collective-permute-start.6 = (bf16[1,2,512,512]{3,2,1,0:T(8,128)(2,1)}, bf16[1,2,512,512]{3,2,1,0:T(8,128)(2,1)}, u32[]{:S(2)}, u32[]{:S(2)}) collective-permute-start(bf16[1,2,512,512]{3,2,1,0:T(8,128)(2,1)} %collective-permute-done.2.refs_1_.refs_2_), channel_id=1, source_target_pairs={{0,2},{2,0},{4,6},{6,4},{8,10},{10,8},{12,14},{14,12},{1,3},{3,1},... | collective-permute-start | bytes 3145736 | tf_op jit(solution)/shard_map/ppermute | solution.py:17
  57.9 47.6 %collective-permute-start.3 = (bf16[1,2,512,512]{3,2,1,0:T(8,128)(2,1)}, bf16[1,2,512,512]{3,2,1,0:T(8,128)(2,1)}, u32[]{:S(2)}, u32[]{:S(2)}) collective-permute-start(bf16[1,2,512,512]{3,2,1,0:T(8,128)(2,1)} %slice.20), channel_id=1, source_target_pairs={{0,8},{2,10},{4,12},{6,14},{8,0},{10,2},{12,4},{14,6},{1,9},{3,11}... | collective-permute-start | bytes 3145736 | tf_op jit(solution)/shard_map/ppermute | solution.py:17
  73.2 37.0 %copy-start.12 = (s32[3]{0:T(128)S(1)}, s32[3]{0:T(128)}, u32[]{:S(2)}) copy-start(s32[3]{0:T(128)} %constant.89.clone) | copy-start | bytes 40
  98.8 11.9 %copy-start.5 = (bf16[1,2,512,512]{3,2,1,0:T(8,128)(2,1)}, bf16[1,2,512,512]{3,2,1,0:T(8,128)(2,1)S(1)}, u32[]{:S(2)}) copy-start(bf16[1,2,512,512]{3,2,1,0:T(8,128)(2,1)S(1)} %collective-permute-done.4.refs_2_.refs_6_) | copy-start | bytes 3145732
  98.8 7.3 %copy-start.6 = (bf16[1,2,512,512]{3,2,1,0:T(8,128)(2,1)}, bf16[1,2,512,512]{3,2,1,0:T(8,128)(2,1)S(1)}, u32[]{:S(2)}) copy-start(bf16[1,2,512,512]{3,2,1,0:T(8,128)(2,1)S(1)} %collective-permute-done.5.refs_1_.refs_5_) | copy-start | bytes 3145732
  105.6 28.9 %collective-permute-start.10 = (bf16[1,2,512,512]{3,2,1,0:T(8,128)(2,1)}, bf16[1,2,512,512]{3,2,1,0:T(8,128)(2,1)S(1)}, u32[]{:S(2)}, u32[]{:S(2)}) collective-permute-start(bf16[1,2,512,512]{3,2,1,0:T(8,128)(2,1)} %collective-permute-done.3.refs_0_.refs_7_), channel_id=1, source_target_pairs={{0,2},{2,0},{4,6},{6,4},{8,10},{10,8},{12,14},{14,12},{1,3},{3,1},... | collective-permute-start | bytes 3145736 | tf_op jit(solution)/shard_map/ppermute | solution.py:17
  106.1 28.4 %collective-permute-start.7 = (bf16[1,2,512,512]{3,2,1,0:T(8,128)(2,1)}, bf16[1,2,512,512]{3,2,1,0:T(8,128)(2,1)}, u32[]{:S(2)}, u32[]{:S(2)}) collective-permute-start(bf16[1,2,512,512]{3,2,1,0:T(8,128)(2,1)} %collective-permute-done.3.refs_0_.refs_7_), channel_id=1, source_target_pairs={{0,4},{2,6},{4,0},{6,2},{8,12},{10,14},{12,8},{14,10},{1,5},{3,7},... | collective-permute-start | bytes 3145736 | tf_op jit(solution)/shard_map/ppermute | solution.py:17
  106.1 44.3 %collective-permute-start.8 = (bf16[1,2,512,512]{3,2,1,0:T(8,128)(2,1)}, bf16[1,2,512,512]{3,2,1,0:T(8,128)(2,1)S(1)}, u32[]{:S(2)}, u32[]{:S(2)}) collective-permute-start(bf16[1,2,512,512]{3,2,1,0:T(8,128)(2,1)} %slice.20), channel_id=1, source_target_pairs={{0,4},{2,6},{4,0},{6,2},{8,12},{10,14},{12,8},{14,10},{1,5},{3,7},... | collective-permute-start | bytes 3145736 | tf_op jit(solution)/shard_map/ppermute | solution.py:17
  108.1 42.3 %collective-permute-start.9 = (bf16[1,2,512,512]{3,2,1,0:T(8,128)(2,1)S(1)}, bf16[1,2,512,512]{3,2,1,0:T(8,128)(2,1)}, u32[]{:S(2)}, u32[]{:S(2)}) collective-permute-start(bf16[1,2,512,512]{3,2,1,0:T(8,128)(2,1)S(1)} %collective-permute-done.4.refs_2_.refs_6_), channel_id=1, source_target_pairs={{0,2},{2,0},{4,6},{6,4},{8,10},{10,8},{12,14},{14,12},{1,3},{3,1},... | collective-permute-start | bytes 3145736 | tf_op jit(solution)/shard_map/ppermute | solution.py:17
  128.0 26.4 %copy-start.11 = (s32[3]{0:T(128)S(1)}, s32[3]{0:T(128)}, u32[]{:S(2)}) copy-start(s32[3]{0:T(128)} %constant.91.clone) | copy-start | bytes 40
  134.5 20.4 %copy-start.2 = (bf16[1,2,512,512]{3,2,1,0:T(8,128)(2,1)}, bf16[1,2,512,512]{3,2,1,0:T(8,128)(2,1)S(1)}, u32[]{:S(2)}) copy-start(bf16[1,2,512,512]{3,2,1,0:T(8,128)(2,1)S(1)} %collective-permute-done.10.refs_1_.refs_3_) | copy-start | bytes 3145732
  150.4 4.6 %copy-start.3 = (bf16[1,2,512,512]{3,2,1,0:T(8,128)(2,1)}, bf16[1,2,512,512]{3,2,1,0:T(8,128)(2,1)S(1)}, u32[]{:S(2)}) copy-start(bf16[1,2,512,512]{3,2,1,0:T(8,128)(2,1)S(1)} %collective-permute-done.8.refs_2_.refs_4_) | copy-start | bytes 3145732
  150.4 18.8 %collective-permute-start.13 = (bf16[2,2,1024,512]{3,2,1,0:T(8,128)(2,1)}, bf16[2,2,1024,512]{3,2,1,0:T(8,128)(2,1)}, u32[]{:S(2)}, u32[]{:S(2)}) collective-permute-start(bf16[2,2,1024,512]{3,2,1,0:T(8,128)(2,1)} %shard_map.137.refs_2_.refs_0_), channel_id=1, source_target_pairs={{0,1},{1,0},{2,3},{3,2},{4,5},{5,4},{6,7},{7,6},{8,9},{9,8},{10,11... | collective-permute-start | bytes 12582920 | tf_op jit(solution)/shard_map/ppermute | solution.py:17
  150.4 18.8 %collective-permute-start.14 = (bf16[1,2,512,512]{3,2,1,0:T(8,128)(2,1)}, bf16[1,2,512,512]{3,2,1,0:T(8,128)(2,1)}, u32[]{:S(2)}, u32[]{:S(2)}) collective-permute-start(bf16[1,2,512,512]{3,2,1,0:T(8,128)(2,1)} %collective-permute-done.9.refs_0_.refs_4_), channel_id=1, source_target_pairs={{0,1},{1,0},{2,3},{3,2},{4,5},{5,4},{6,7},{7,6},{8,9},{9,8},{10,11... | collective-permute-start | bytes 3145736 | tf_op jit(solution)/shard_map/ppermute | solution.py:17
  150.9 26.8 %collective-permute-start.11 = (bf16[1,2,512,512]{3,2,1,0:T(8,128)(2,1)}, bf16[1,2,512,512]{3,2,1,0:T(8,128)(2,1)S(1)}, u32[]{:S(2)}, u32[]{:S(2)}) collective-permute-start(bf16[1,2,512,512]{3,2,1,0:T(8,128)(2,1)} %slice.21), channel_id=1, source_target_pairs={{0,4},{2,6},{4,0},{6,2},{8,12},{10,14},{12,8},{14,10},{1,5},{3,7},... | collective-permute-start | bytes 3145736 | tf_op jit(solution)/shard_map/ppermute | solution.py:17
  152.3 25.4 %collective-permute-start.12 = (bf16[1,2,512,512]{3,2,1,0:T(8,128)(2,1)}, bf16[1,2,512,512]{3,2,1,0:T(8,128)(2,1)}, u32[]{:S(2)}, u32[]{:S(2)}) collective-permute-start(bf16[1,2,512,512]{3,2,1,0:T(8,128)(2,1)} %collective-permute-done.7.refs_0_.refs_2_), channel_id=1, source_target_pairs={{0,2},{2,0},{4,6},{6,4},{8,10},{10,8},{12,14},{14,12},{1,3},{3,1},... | collective-permute-start | bytes 3145736 | tf_op jit(solution)/shard_map/ppermute | solution.py:17
  169.1 9.2 %copy-start.10 = (s32[2]{0:T(128)S(1)}, s32[2]{0:T(128)}, u32[]{:S(2)}) copy-start(s32[2]{0:T(128)} %constant.93.clone) | copy-start | bytes 28
  169.1 9.7 %copy-start.8 = (s32[2]{0:T(128)S(1)}, s32[2]{0:T(128)}, u32[]{:S(2)}) copy-start(s32[2]{0:T(128)} %get-tuple-element.55.ids) | copy-start | bytes 28
  169.1 10.3 %copy-start.1 = (bf16[2,2,1,512,512]{4,3,2,1,0:T(8,128)(2,1)S(1)}, bf16[2,2,1,512,512]{4,3,2,1,0:T(8,128)(2,1)}, u32[]{:S(2)}) copy-start(bf16[2,2,1,512,512]{4,3,2,1,0:T(8,128)(2,1)} %param.13) | copy-start | bytes 6291460
  177.7 2.2 %copy-start.7 = (bf16[1,2,512,512]{3,2,1,0:T(8,128)(2,1)}, bf16[1,2,512,512]{3,2,1,0:T(8,128)(2,1)S(1)}, u32[]{:S(2)}) copy-start(bf16[1,2,512,512]{3,2,1,0:T(8,128)(2,1)S(1)} %collective-permute-done.11.refs_0_.refs_6_) | copy-start | bytes 3145732
  177.7 12.0 %collective-permute-start.15 = (bf16[1,2,512,512]{3,2,1,0:T(8,128)(2,1)}, bf16[1,2,512,512]{3,2,1,0:T(8,128)(2,1)}, u32[]{:S(2)}, u32[]{:S(2)}) collective-permute-start(bf16[1,2,512,512]{3,2,1,0:T(8,128)(2,1)} %shard_map.139), channel_id=1, source_target_pairs={{0,1},{1,0},{2,3},{3,2},{4,5},{5,4},{6,7},{7,6},{8,9},{9,8},{10,11... | collective-permute-start | bytes 3145736 | tf_op jit(solution)/shard_map/ppermute | solution.py:17
  177.8 11.9 %collective-permute-start.16 = (bf16[1,2,512,512]{3,2,1,0:T(8,128)(2,1)S(1)}, bf16[1,2,512,512]{3,2,1,0:T(8,128)(2,1)}, u32[]{:S(2)}, u32[]{:S(2)}) collective-permute-start(bf16[1,2,512,512]{3,2,1,0:T(8,128)(2,1)S(1)} %collective-permute-done.11.refs_0_.refs_6_), channel_id=1, source_target_pairs={{0,1},{1,0},{2,3},{3,2},{4,5},{5,4},{6,7},{7,6},{8,9},{9,8},{10,11... | collective-permute-start | bytes 3145736 | tf_op jit(solution)/shard_map/ppermute | solution.py:17
  178.3 11.4 %collective-permute-start.17 = (bf16[1,2,512,512]{3,2,1,0:T(8,128)(2,1)}, bf16[1,2,512,512]{3,2,1,0:T(8,128)(2,1)}, u32[]{:S(2)}, u32[]{:S(2)}) collective-permute-start(bf16[1,2,512,512]{3,2,1,0:T(8,128)(2,1)} %collective-permute-done.12.refs_1_.refs_8_), channel_id=1, source_target_pairs={{0,1},{1,0},{2,3},{3,2},{4,5},{5,4},{6,7},{7,6},{8,9},{9,8},{10,11... | collective-permute-start | bytes 3145736 | tf_op jit(solution)/shard_map/ppermute | solution.py:17
  189.6 21.9 %copy-start.9 = (s32[16]{0:T(128)S(1)}, s32[16]{0:T(128)}, u32[]{:S(2)}) copy-start(s32[16]{0:T(128)} %param.14) | copy-start | bytes 196
  196.1 2.2 %collective-permute-start.18 = (f32[4,512]{1,0:T(4,128)S(1)}, f32[4,512]{1,0:T(4,128)S(1)}, u32[]{:S(2)}, u32[]{:S(2)}) collective-permute-start(f32[4,512]{1,0:T(4,128)S(1)} %pad_maximum_fusion), channel_id=1, source_target_pairs={{0,1},{1,0},{2,3},{3,2},{4,5},{5,4},{6,7},{7,6},{8,9},{9,8},{10,11... | collective-permute-start | bytes 24584 | tf_op jit(solution)/shard_map/ppermute | solution.py:17
  196.6 3.7 %collective-permute-start.19 = (f32[4,512]{1,0:T(4,128)S(1)}, f32[4,512]{1,0:T(4,128)S(1)}, u32[]{:S(2)}, u32[]{:S(2)}) collective-permute-start(f32[4,512]{1,0:T(4,128)S(1)} %pad_maximum_fusion), channel_id=1, source_target_pairs={{0,2},{1,3},{2,0},{3,1},{4,6},{5,7},{6,4},{7,5},{8,10},{9,11},{10,... | collective-permute-start | bytes 24584 | tf_op jit(solution)/shard_map/ppermute | solution.py:17
  198.4 3.1 %collective-permute-start.20 = (f32[4,512]{1,0:T(4,128)S(1)}, f32[4,512]{1,0:T(4,128)S(1)}, u32[]{:S(2)}, u32[]{:S(2)}) collective-permute-start(f32[4,512]{1,0:T(4,128)S(1)} %pad_maximum_fusion), channel_id=1, source_target_pairs={{0,3},{1,2},{2,1},{3,0},{4,7},{5,6},{6,5},{7,4},{8,11},{9,10},{10,... | collective-permute-start | bytes 24584 | tf_op jit(solution)/shard_map/ppermute | solution.py:17
  201.5 4.9 %collective-permute-start.21 = (f32[4,512]{1,0:T(4,128)S(1)}, f32[4,512]{1,0:T(4,128)S(1)}, u32[]{:S(2)}, u32[]{:S(2)}) collective-permute-start(f32[4,512]{1,0:T(4,128)S(1)} %add_add_fusion.1), channel_id=1, source_target_pairs={{0,4},{1,5},{2,6},{3,7},{4,0},{5,1},{6,2},{7,3},{8,12},{9,13},{10,... | collective-permute-start | bytes 24584 | tf_op jit(solution)/shard_map/ppermute | solution.py:17
  202.3 4.7 %collective-permute-start.22 = (f32[4,512]{1,0:T(4,128)S(1)}, f32[4,512]{1,0:T(4,128)S(1)}, u32[]{:S(2)}, u32[]{:S(2)}) collective-permute-start(f32[4,512]{1,0:T(4,128)S(1)} %add_add_fusion.1), channel_id=1, source_target_pairs={{0,8},{1,9},{2,10},{3,11},{4,12},{5,13},{6,14},{7,15},{8,0},{9,1},... | collective-permute-start | bytes 24584 | tf_op jit(solution)/shard_map/ppermute | solution.py:17
  205.3 5.4 %collective-permute-start.23 = (f32[4,512]{1,0:T(4,128)S(1)}, f32[4,512]{1,0:T(4,128)S(1)}, u32[]{:S(2)}, u32[]{:S(2)}) collective-permute-start(f32[4,512]{1,0:T(4,128)S(1)} %add_add_fusion.1), channel_id=1, source_target_pairs={{0,12},{1,13},{2,14},{3,15},{4,8},{5,9},{6,10},{7,11},{8,4},{9,5},... | collective-permute-start | bytes 24584 | tf_op jit(solution)/shard_map/ppermute | solution.py:17

commit v7 on v6

--- a/solution.py
+++ b/solution.py
@@ -8,7 +8,7 @@
 from jax.experimental.pallas import tpu as pltpu
 from jax.sharding import PartitionSpec as P
 
-VMEM_LIMIT = 60 * 1024 * 1024
+VMEM_LIMIT = 63 * 1024 * 1024
 HINT = pl.CostEstimate(flops=1, bytes_accessed=1, transcendentals=0)
 
 
@@ -43,9 +43,8 @@
     return [
         pltpu.make_async_copy(ref.at[which, 0], right.at[k, 0, low], sem.at[k, 0]),
         pltpu.make_async_copy(ref.at[which, 1], right.at[k, 1, low], sem.at[k, 1]),
-        pltpu.make_async_copy(ref.at[which, 0], right.at[k, 1, high], sem.at[k, 2]),
-        pltpu.make_async_copy(cross.at[freq, 0, :, columns], left.at[k, :, low], sem.at[k, 3]),
-        pltpu.make_async_copy(cross.at[freq, 1, :, columns], left.at[k, :, high], sem.at[k, 4]),
+        pltpu.make_async_copy(cross.at[freq, 0, :, columns], left.at[k, :, low], sem.at[k, 2]),
+        pltpu.make_async_copy(cross.at[freq, 1, :, columns], left.at[k, :, high], sem.at[k, 3]),
     ]
 
 
@@ -55,23 +54,25 @@
         piece_copies(freq, ids, cross, ref, k, left, right, sem) for k, ref in enumerate(w_refs)
     ]
 
-    @pl.when((piece == 0) & (part == 0))
-    def _():
-        for group in copies:
-            for copy in group:
-                copy.start()
-        if total is not None:
-            pltpu.make_async_copy(total, tot, tot_sem.at[0]).start()
-        first()
-
     for k, group in enumerate(copies):
 
         @pl.when((piece == k) & (part == 0))
         def _(k=k, group=group):
+            if k == 0:
+                for copy in group:
+                    copy.start()
             for copy in group:
                 copy.wait()
+            if k + 1 < len(copies):
+                for copy in copies[k + 1]:
+                    copy.start()
+            if k == 0:
+                if total is not None:
+                    pltpu.make_async_copy(total, tot, tot_sem.at[0]).start()
+                first()
             width = right.shape[2] // 2
             right[k, 0, width:] = -right[k, 1, :width]
+            right[k, 1, width:] = right[k, 0, :width]
 
     dot = functools.partial(jnp.dot, preferred_element_type=jnp.float32)
 
@@ -154,14 +155,14 @@
         out[...] += fold(rows[part], field[part] + tot[part])
 
 
-def dot_kernel(freq, ids, field, *refs):
-    whole, singles, (out, rows, sem) = refs[:2], refs[2:-3], refs[-3:]
+def dot_kernel(freq, ids, field, before, norms, *refs):
+    whole, singles, (out, rows, sem, sums) = refs[:2], refs[2:-4], refs[-4:]
     slot, part = pl.program_id(0), pl.program_id(1)
     width = field.shape[1]
 
     @pl.when((slot == 0) & (part == 0))
     def _():
-        out[...] = jnp.zeros_like(out)
+        sums[...] = jnp.zeros_like(sums)
         start_rows(freq, ids, 0, whole, singles, rows, sem)
 
     for k in range(2):
@@ -171,7 +172,13 @@
             wait_rows(k, singles, rows, sem)
 
     here = pl.ds(pl.multiple_of(slot * width, width), width)
-    out[...] += fold(rows[part, here], field[0])
+    sums[...] += fold(rows[part, here], field[0])
+
+    @pl.when((slot == 1) & (part == 1))
+    def _():
+        out[0:1] = jnp.sum(before[...], axis=0, keepdims=True)
+        out[1:2] = jnp.sum(sums[...], axis=0, keepdims=True)
+        out[2:4] = norms[...]
 
 
 ANYWHERE = pl.BlockSpec(memory_space=pl.ANY)
@@ -192,7 +199,7 @@
             scratch_shapes=[
                 pltpu.VMEM((count, rows, 2 * width), dtype),
                 pltpu.VMEM((count, 2, 2 * width, sources), dtype),
-                pltpu.SemaphoreType.DMA((count, 5)),
+                pltpu.SemaphoreType.DMA((count, 4)),
                 pltpu.VMEM((2, rows, sources), jnp.float32),
                 *(total if has_total else []),
                 *scratch,
@@ -228,7 +235,7 @@
 
 def finish(cross, freq, ids, pieces, total, whole, singles):
     rows, sources = cross.shape[2], pieces[0].shape[3]
-    out = call(
+    return call(
         numer_kernel,
         cross,
         freq,
@@ -240,28 +247,31 @@
         True,
         row_scratch(rows, sources, pieces[0].dtype),
     )
-    return jnp.sum(out, axis=0)
-
-
-def dot_rows(freq, ids, field, whole, singles):
+
+
+def dot_rows(freq, ids, field, before, norms, whole, singles):
     _, rows, sources = field.shape
-    out = pl.pallas_call(
+    return pl.pallas_call(
         functools.partial(dot_kernel, freq),
-        out_shape=jax.ShapeDtypeStruct((8, sources), jnp.float32),
+        out_shape=jax.ShapeDtypeStruct((4, sources), jnp.float32),
         grid_spec=pltpu.PrefetchScalarGridSpec(
             num_scalar_prefetch=1,
             grid=(2, 2),
             in_specs=[
-                pl.BlockSpec((1, rows // 2, sources), lambda slot, part, ids: (part, slot, 0))
+                pl.BlockSpec((1, rows // 2, sources), lambda slot, part, ids: (part, slot, 0)),
+                pl.BlockSpec((8, sources), lambda slot, part, ids: (0, 0)),
+                pl.BlockSpec((2, sources), lambda slot, part, ids: (0, 0)),
             ]
             + [ANYWHERE] * (2 + len(singles)),
-            out_specs=pl.BlockSpec((8, sources), lambda slot, part, ids: (0, 0)),
-            scratch_shapes=row_scratch(rows, sources, whole[0].dtype),
+            out_specs=pl.BlockSpec((4, sources), lambda slot, part, ids: (0, 0)),
+            scratch_shapes=[
+                *row_scratch(rows, sources, whole[0].dtype),
+                pltpu.VMEM((8, sources), jnp.float32),
+            ],
         ),
         compiler_params=pltpu.CompilerParams(vmem_limit_bytes=VMEM_LIMIT),
         cost_estimate=HINT,
-    )(ids, field, *whole, *singles)
-    return jnp.sum(out, axis=0)
+    )(ids, field, before, norms, *whole, *singles)
 
 
 def pick_kernel(plan, ids, *refs):
@@ -301,7 +311,7 @@
     )(ids, *pieces)
 
 
-def numer_by_swaps(cross, replicas):
+def sums_by_swaps(cross, replicas, norms):
     rows, half = cross.shape[2], cross.shape[3]
     width = replicas.shape[3]
     me = lax.axis_index("row").astype(jnp.int32)
@@ -313,22 +323,35 @@
     ids = lambda *wanted: me ^ jnp.array(wanted, jnp.int32)
     barrier = lambda *values: lax.optimization_barrier(values)
     own = replicas[:, :, 0]
+    numbers = [ids(0), ids(1, 2, 4), ids(1), ids(3, 5, 6), ids(4), ids(6, 5, 2), ids(3, 7)]
+
+    whole = jnp.where(holds, 0, 1)
+    where_a = jnp.where(masks == 7, jnp.where(holds, 2, 3), whole)
+    where_b = jnp.full_like(masks, whole)
+    for k, mask in enumerate((6, 5, 2)):
+        where_b = jnp.where(masks == mask, jnp.where(holds, 2 + k, 5), where_b)
+    where_b = jnp.where(masks == 3, jnp.where(holds, 6, 7), where_b)
+    where_b = jnp.where(masks == 7, jnp.where(holds, 8, 9), where_b)
+    numbers += [jnp.concatenate([ids(7), where_a]), where_b, masks]
 
     own_a = own[0:1]
     x = swap(after(own, own_a), "row", 1)
     pa = swap(own_a, "row", 4)
     na = swap(own_a, "row", 2)
-    a0 = add_field(cross, 0, ids(0), [own])
-    a1 = add_field(cross, 1, ids(0), [own])
+    a0 = add_field(cross, 0, numbers[0], [own])
+    a1 = add_field(cross, 1, numbers[0], [own])
     own_b = after(own, a0)[1:2]
-    x, pa, na, own_b, a0, a1 = barrier(x, pa, na, own_b, a0, a1)
-
-    pb = swap(own_b, "row", 4)
+    pb = swap(after(own_b, pa), "row", 4)
+    x, pa, na, own_b, a0, a1, norms, *numbers = barrier(
+        x, pa, na, own_b, a0, a1, norms, *numbers
+    )
+    _, ids_a0, ids_a1, ids_b0, ids_b1, ids_c1, ids_d1, ids_c0, where_b, masks = numbers
+
     ga = swap(pa, "row", 2)
     xpa = swap(pa, "row", 1)
     xna = swap(na, "row", 1)
-    a0 = add_field(cross, 0, ids(1, 2, 4), [x, na, pa], a0)
-    a1 = add_field(cross, 1, ids(1), [x], a1)
+    a0 = add_field(cross, 0, ids_a0, [x, na, pa], a0)
+    a1 = add_field(cross, 1, ids_a1, [x], a1)
     x_b = x[1:2]
     pb, ga, xpa, xna, a0, a1, x_b, own_b = barrier(pb, ga, xpa, xna, a0, a1, x_b, own_b)
 
@@ -336,8 +359,8 @@
     xga = swap(ga, "row", 1)
     xpb = swap(pb, "row", 1)
     nb = swap(own_b, "row", 2)
-    b0 = add_field(cross, 0, ids(3, 5, 6), [xna, xpa, ga], a0)
-    a1 = add_field(cross, 1, ids(4), [pb], a1)
+    b0 = add_field(cross, 0, ids_b0, [xna, xpa, ga], a0)
+    a1 = add_field(cross, 1, ids_b1, [pb], a1)
     plan = [
         (0, 2, [(0, 0), (1, 1), (2, 2), (3, 3), (4, 4), (5, 5), (6, 6)]),
         (1, 2, [(0, 0), (1, 1), (4, 7)]),
@@ -349,29 +372,19 @@
     other_xga = swap(xga, "col", 1)
     d = swap(x_b, "row", 2)
     xgb = swap(gb, "row", 1)
-    b1 = add_field(cross, 1, ids(6, 5, 2), [gb, xpb, nb], a1)
+    b1 = add_field(cross, 1, ids_c1, [gb, xpb, nb], a1)
     plan = [(0, 1, [(6, 0), (5, 1), (2, 2)])]
     mine_b = pick_rows(after(masks, b1), plan, [gb, xpb, nb])
-    whole = jnp.where(holds, 0, 1)
-    where = jnp.where(masks == 7, jnp.where(holds, 2, 3), whole)
-    c0 = finish(
-        cross, 0, jnp.concatenate([ids(7), where]), [xga], b0, [mine, other], [xga, other_xga]
-    )
+    c0 = finish(cross, 0, ids_c0, [xga], b0, [mine, other], [xga, other_xga])
     d, xgb, b1, mine_b, c0 = barrier(d, xgb, b1, mine_b, c0)
 
     other_b, other_d, other_xgb = (swap(piece, "col", 1) for piece in (mine_b, d, xgb))
-    field = add_field(cross, 1, ids(3, 7), [d, xgb], b1)
-    where = jnp.full_like(masks, whole)
-    for k, mask in enumerate((6, 5, 2)):
-        where = jnp.where(masks == mask, jnp.where(holds, 2 + k, 5), where)
-    where = jnp.where(masks == 3, jnp.where(holds, 6, 7), where)
-    where = jnp.where(masks == 7, jnp.where(holds, 8, 9), where)
+    field = add_field(cross, 1, ids_d1, [d, xgb], b1)
     singles = [gb, xpb, nb, other_b, d, other_d, xgb, other_xgb]
-    c1 = dot_rows(1, where, field, [mine, other], singles)
-    return jnp.stack([c0, c1])
-
-
-def numer_by_gather(cross, replicas):
+    return dot_rows(1, where_b, field, c0, norms, [mine, other], singles)
+
+
+def sums_by_gather(cross, replicas, norms):
     rows, half = cross.shape[2], cross.shape[3]
     row_index, col_index = lax.axis_index("row"), lax.axis_index("col")
     first_row = row_index * rows
@@ -381,7 +394,8 @@
     field = jnp.stack([parts[:, 0, 0] - parts[:, 1, 1], parts[:, 0, 1] + parts[:, 1, 0]], axis=1)
     own_rows = lax.dynamic_slice_in_dim(whole, first_row - holder * half, rows, 2)
     block_rows = jnp.where(holder == col_index, own_rows, swap(own_rows, "col", 1))
-    return jnp.sum(block_rows.astype(jnp.float32) * field, axis=(1, 2))
+    numer = jnp.sum(block_rows.astype(jnp.float32) * field, axis=(1, 2))
+    return jnp.concatenate([numer, norms])
 
 
 def body(cross_spectra, replicas, tile_order):
@@ -391,11 +405,12 @@
     norms = jnp.sum(own * own, axis=(1, 2))
     doubling = (
         lax.axis_size("row") == 8
+        and fnum == 2
         and replicas.shape[3] % 128 == 0
         and cross_spectra.shape[2] == 2 * replicas.shape[3]
     )
-    numer = (numer_by_swaps if doubling else numer_by_gather)(cross_spectra, replicas)
-    sums = sum_all(jnp.concatenate([numer, norms]))
+    sums = (sums_by_swaps if doubling else sums_by_gather)(cross_spectra, replicas, norms)
+    sums = sum_all(sums)
     numer, norms = sums[:fnum], sums[fnum:]
     beam = numer / (norms + 1e-06)
     width = sources // lax.axis_size("col")

time: 213 us -> 210 us (0.986)
  waiting for transfers between devices: 78.1 us -> 73.9 us
    ppermute x24, waiting for transfers between devices: 78.1 us -> 73.9 us  [swap(): lax.ppermute(value, axis, [(source, source ^ mask) for source in range(si...]
    reduce_sum x1, other arithmetic: 0.44 us -> 2.62 us  [body(): norms = jnp.sum(own * own, axis=(1, 2))]
  transfers between devices with their start and end apart: 24 -> 24, of which waited for: 10 -> 12; matrix products, arithmetic and copies ran while one was open for 4% -> 5% of each run, Pallas kernels for 41% -> 42%
where the time goes in v7:
time: 210 us
  Pallas kernels  93.4 us (44%)
  waiting for transfers between devices  73.9 us (35%)
  starting transfers between devices  26.6 us (13%)
  local copies, waits for them, and re-layouts  7.56 us (4%)
  other arithmetic  6.49 us (3%)
    pallas_call x9, Pallas kernels, call(): pl.pallas_call(functools.partial(kernel, freq, count), out_shape=out_shap...  81.1 us
    ppermute x24, waiting for transfers between devices, swap(): lax.ppermute(value, axis, [(source, source ^ mask) for source in range(si...  73.9 us
    ppermute x24, starting transfers between devices, swap(): lax.ppermute(value, axis, [(source, source ^ mask) for source in range(si...  26.6 us
    pallas_call x2, Pallas kernels, pick_rows(): pl.pallas_call(functools.partial(pick_kernel, plan), out_shape=jax.ShapeD...  6.59 us
    pallas_call x1, Pallas kernels, dot_rows(): pl.pallas_call(functools.partial(dot_kernel, freq), out_shape=jax.ShapeDt...  5.73 us
  transfers between devices with their start and end apart: 24, of which 12 were waited for; matrix products, arithmetic and copies ran while one was open for 5% of the time, Pallas kernels for 42%

profile of v7, /device:TPU:0, one launch (start us, length us, event | category | flops | bytes accessed | tf_op | source)
XLA Modules:
  0.0 209.6 jit_solution(16874294354744204641)
XLA Ops:
  0.6 2.3 %slice_bitcast_fusion = bf16[1,2,512,512]{3,2,1,0:T(8,128)(2,1)} fusion(bf16[2,2,1,512,512]{4,3,1,2,0:T(8,128)(2,1)} %bitcast.14), kind=kLoop, calls=%fused_computation.3 | loop fusion | bytes 2097152 | tf_op jit(solution)/shard_map/slice | solution.py:337
  2.9 2.9 %collective-permute-start = (bf16[2,2,512,512]{3,2,1,0:T(8,128)(2,1)}, bf16[2,2,512,512]{3,2,1,0:T(8,128)(2,1)}, u32[]{:S(2)}, u32[]{:S(2)}) collective-permute-start(bf16[2,2,512,512]{3,2,1,0:T(8,128)(2,1)} %bitcast.15), channel_id=1, source_target_pairs={{0,2},{2,0},{4,6},{6,4},{8,10},{10,8},{12,14},{14,12},{1,3},{3,1},... | collective-permute-start | bytes 6291464 | tf_op jit(solution)/shard_map/ppermute | solution.py:17
  5.9 2.6 %collective-permute-start.1 = (bf16[1,2,512,512]{3,2,1,0:T(8,128)(2,1)}, bf16[1,2,512,512]{3,2,1,0:T(8,128)(2,1)}, u32[]{:S(2)}, u32[]{:S(2)}) collective-permute-start(bf16[1,2,512,512]{3,2,1,0:T(8,128)(2,1)} %slice_bitcast_fusion), channel_id=1, source_target_pairs={{0,8},{2,10},{4,12},{6,14},{8,0},{10,2},{12,4},{14,6},{1,9},{3,11}... | collective-permute-start | bytes 3145736 | tf_op jit(solution)/shard_map/ppermute | solution.py:17
  8.4 1.6 collective-permute-start.2
  10.0 1.2 compare_select_fusion.4
  11.3 5.8 %shard_map.122.refs_3_ = f32[2,1024,512]{2,1,0:T(8,128)} custom-call(s32[1]{0:T(128)} %bitcast.3.ids, bf16[2,2,1024,4096]{3,2,1,0:T(8,128)(2,1)} %cross.17, bf16[2,2,512,512]{3,2,1,0:T(8,128)(2,1)} %bitcast.16), custom_call_target="tpu_custom_call" | custom-call | flops 1 | bytes 1 | tf_op jit(solution)/shard_map/pallas_call | solution.py:191
  17.1 5.8 %shard_map.123.refs_1_ = f32[2,1024,512]{2,1,0:T(8,128)} custom-call(s32[1]{0:T(128)} %bitcast.3.ids, bf16[2,2,1024,4096]{3,2,1,0:T(8,128)(2,1)} %cross.17, bf16[2,2,512,512]{3,2,1,0:T(8,128)(2,1)} %bitcast.17), custom_call_target="tpu_custom_call" | custom-call | flops 1 | bytes 1 | tf_op jit(solution)/shard_map/pallas_call | solution.py:191
  22.9 2.3 %slice.20 = bf16[1,2,512,512]{3,2,1,0:T(8,128)(2,1)} slice(bf16[2,2,512,512]{3,2,1,0:T(8,128)(2,1)} %bitcast.18), slice={[1:2], [0:2], [0:512], [0:512]} | slice | bytes 2097152 | tf_op jit(solution)/shard_map/slice | solution.py:343
  25.2 0.7 pad_add_fusion.1.ids
  25.9 0.6 broadcast_xor_fusion.3.ids
  26.5 0.5 broadcast_xor_fusion.1
  27.0 2.6 %multiply_reduce_fusion.norms = f32[2,512]{1,0:T(2,128)} fusion(bf16[2,2,1,512,512]{4,3,2,1,0:T(8,128)(2,1)} %param.12), kind=kLoop, calls=%fused_computation | loop fusion | flops 3144704 | bytes 2101248 | tf_op jit(solution)/shard_map/reduce_sum | solution.py:405
  29.6 24.6 %collective-permute-done.1.refs_2_.refs_4_ = bf16[1,2,512,512]{3,2,1,0:T(8,128)(2,1)} collective-permute-done((bf16[1,2,512,512]{3,2,1,0:T(8,128)(2,1)}, bf16[1,2,512,512]{3,2,1,0:T(8,128)(2,1)}, u32[]{:S(2)}, u32[]{:S(2)}) %collective-permute-start.1) | collective-permute-done | bytes 1048608 | tf_op jit(solution)/shard_map/ppermute | solution.py:17
  54.5 3.8 %collective-permute-start.4 = (bf16[1,2,512,512]{3,2,1,0:T(8,128)(2,1)}, bf16[1,2,512,512]{3,2,1,0:T(8,128)(2,1)}, u32[]{:S(2)}, u32[]{:S(2)}) collective-permute-start(bf16[1,2,512,512]{3,2,1,0:T(8,128)(2,1)} %collective-permute-done.1.refs_2_.refs_4_), channel_id=1, source_target_pairs={{0,4},{2,6},{4,0},{6,2},{8,12},{10,14},{12,8},{14,10},{1,5},{3,7},... | collective-permute-start | bytes 3145736 | tf_op jit(solution)/shard_map/ppermute | solution.py:17
  58.2 0.5 collective-permute-start.5
  58.8 1.5 collective-permute-start.6
  60.2 7.2 %shard_map.125.refs_1_ = f32[2,1024,512]{2,1,0:T(8,128)} custom-call(s32[1]{0:T(128)S(6)} %xor.48.ids, bf16[2,2,1024,4096]{3,2,1,0:T(8,128)(2,1)} %cross.17, bf16[2,2,512,512]{3,2,1,0:T(8,128)(2,1)} %collective-permute-done.refs_0_.refs_1_, f32[2,1024,512]{2,1,0:T(8,128)} %shard_map.123.refs_1_), custom_call_target="tpu_custom_call" | custom-call | flops 1 | bytes 1 | tf_op jit(solution)/shard_map/pallas_call | solution.py:191
  67.4 12.4 %shard_map.124.refs_3_ = f32[2,1024,512]{2,1,0:T(8,128)} custom-call(s32[3]{0:T(128)} %broadcast_xor_fusion.3.ids, bf16[2,2,1024,4096]{3,2,1,0:T(8,128)(2,1)} %cross.17, bf16[2,2,512,512]{3,2,1,0:T(8,128)(2,1)} %collective-permute-done.refs_0_.refs_1_, bf16[1,2,512,512]{3,2,1,0:T(8,128)(2,1)} %collective-permute-done.2.refs_1_.refs_2_, ...), custom_call_target="tpu_custom_call" | custom-call | flops 1 | bytes 1 | tf_op jit(solution)/shard_map/pallas_call | solution.py:191
  79.8 2.3 %slice.21 = bf16[1,2,512,512]{3,2,1,0:T(8,128)(2,1)} slice(bf16[2,2,512,512]{3,2,1,0:T(8,128)(2,1)} %collective-permute-done.refs_0_.refs_1_), slice={[1:2], [0:2], [0:512], [0:512]} | slice | bytes 2097152 | tf_op jit(solution)/shard_map/slice | solution.py:355
  82.1 19.9 %collective-permute-done.3.refs_0_.refs_7_ = bf16[1,2,512,512]{3,2,1,0:T(8,128)(2,1)} collective-permute-done((bf16[1,2,512,512]{3,2,1,0:T(8,128)(2,1)}, bf16[1,2,512,512]{3,2,1,0:T(8,128)(2,1)}, u32[]{:S(2)}, u32[]{:S(2)}) %collective-permute-start.3) | collective-permute-done | bytes 1048608 | tf_op jit(solution)/shard_map/ppermute | solution.py:17
  102.1 3.4 %collective-permute-done.6.refs_0_.refs_3_ = bf16[1,2,512,512]{3,2,1,0:T(8,128)(2,1)} collective-permute-done((bf16[1,2,512,512]{3,2,1,0:T(8,128)(2,1)}, bf16[1,2,512,512]{3,2,1,0:T(8,128)(2,1)}, u32[]{:S(2)}, u32[]{:S(2)}) %collective-permute-start.6) | collective-permute-done | bytes 1048608 | tf_op jit(solution)/shard_map/ppermute | solution.py:17
  105.5 0.5 collective-permute-start.10
  106.4 1.7 collective-permute-start.8
  108.1 1.5 collective-permute-start.9
  109.6 12.4 %shard_map.126.refs_1_ = f32[2,1024,512]{2,1,0:T(8,128)} custom-call(s32[3]{0:T(128)} %get-tuple-element.60.ids, bf16[2,2,1024,4096]{3,2,1,0:T(8,128)(2,1)} %cross.17, bf16[1,2,512,512]{3,2,1,0:T(8,128)(2,1)} %collective-permute-done.6.refs_0_.refs_3_, bf16[1,2,512,512]{3,2,1,0:T(8,128)(2,1)} %collective-permute-done.5.refs_1_.refs_5_, ...), custom_call_target="tpu_custom_call" | custom-call | flops 1 | bytes 1 | tf_op jit(solution)/shard_map/pallas_call | solution.py:191
  122.0 4.9 %shard_map.128.refs_2_.refs_0_ = bf16[2,2,1024,512]{3,2,1,0:T(8,128)(2,1)} custom-call(s32[2]{0:T(128)} %copy-done, bf16[2,2,512,512]{3,2,1,0:T(8,128)(2,1)} %bitcast.19, bf16[2,2,512,512]{3,2,1,0:T(8,128)(2,1)} %collective-permute-done.refs_0_.refs_1_, bf16[1,2,512,512]{3,2,1,0:T(8,128)(2,1)} %collective-permute-done.2.refs_1_.refs_2_, ...), custom_call_target="tpu_custom_call" | custom-call | flops 1 | bytes 1 | tf_op jit(solution)/shard_map/pallas_call | solution.py:299
  126.8 7.2 %shard_map.127.refs_3_ = f32[2,1024,512]{2,1,0:T(8,128)} custom-call(s32[1]{0:T(128)S(6)} %xor.50.ids, bf16[2,2,1024,4096]{3,2,1,0:T(8,128)(2,1)} %cross.17, bf16[1,2,512,512]{3,2,1,0:T(8,128)(2,1)} %collective-permute-done.3.refs_0_.refs_7_, f32[2,1024,512]{2,1,0:T(8,128)} %shard_map.125.refs_1_), custom_call_target="tpu_custom_call" | custom-call | flops 1 | bytes 1 | tf_op jit(solution)/shard_map/pallas_call | solution.py:191
  134.0 18.2 %collective-permute-done.8.refs_2_.refs_4_ = bf16[1,2,512,512]{3,2,1,0:T(8,128)(2,1)} collective-permute-done((bf16[1,2,512,512]{3,2,1,0:T(8,128)(2,1)}, bf16[1,2,512,512]{3,2,1,0:T(8,128)(2,1)}, u32[]{:S(2)}, u32[]{:S(2)}) %collective-permute-start.8) | collective-permute-done | bytes 1048608 | tf_op jit(solution)/shard_map/ppermute | solution.py:17
  152.7 0.7 collective-permute-start.11
  153.4 1.5 collective-permute-start.12
  154.8 12.4 %shard_map.129.refs_2_ = f32[2,1024,512]{2,1,0:T(8,128)} custom-call(s32[3]{0:T(128)} %get-tuple-element.71.ids, bf16[2,2,1024,4096]{3,2,1,0:T(8,128)(2,1)} %cross.17, bf16[1,2,512,512]{3,2,1,0:T(8,128)(2,1)} %collective-permute-done.7.refs_0_.refs_2_, bf16[1,2,512,512]{3,2,1,0:T(8,128)(2,1)} %collective-permute-done.10.refs_1_.refs_3_, ...), custom_call_target="tpu_custom_call" | custom-call | flops 1 | bytes 1 | tf_op jit(solution)/shard_map/pallas_call | solution.py:191
  167.3 1.7 shard_map.130
  169.1 8.4 %shard_map.131.before = f32[8,512]{1,0:T(8,128)} custom-call(s32[3]{0:T(128)} %pad_add_fusion.1.ids, bf16[2,2,1024,4096]{3,2,1,0:T(8,128)(2,1)} %cross.17, bf16[1,2,512,512]{3,2,1,0:T(8,128)(2,1)} %collective-permute-done.9.refs_0_.refs_4_, f32[2,1024,512]{2,1,0:T(8,128)} %shard_map.126.refs_1_, bf16[2,2,1024,512]{3,2,1,0:T(8,128)(2,1)} %shard_map.128.refs_2_.refs_0_, ...), custom_call_target="tpu_custom_call" | custom-call | flops 1 | bytes 1 | tf_op jit(solution)/shard_map/pallas_call | solution.py:191
  177.4 0.6 collective-permute-done.11.refs_0_.refs_6_
  179.0 9.7 %shard_map.132.field = f32[2,1024,512]{2,1,0:T(8,128)} custom-call(s32[2]{0:T(128)} %get-tuple-element.47.ids, bf16[2,2,1024,4096]{3,2,1,0:T(8,128)(2,1)} %cross.17, bf16[1,2,512,512]{3,2,1,0:T(8,128)(2,1)} %collective-permute-done.11.refs_0_.refs_6_, bf16[1,2,512,512]{3,2,1,0:T(8,128)(2,1)} %collective-permute-done.12.refs_1_.refs_8_, ...), custom_call_target="tpu_custom_call" | custom-call | flops 1 | bytes 1 | tf_op jit(solution)/shard_map/pallas_call | solution.py:191
  188.7 5.7 %shard_map.133 = f32[4,512]{1,0:T(4,128)} custom-call(s32[2]{0:T(128)} %get-tuple-element.46.ids, f32[2,1024,512]{2,1,0:T(8,128)} %shard_map.132.field, f32[8,512]{1,0:T(8,128)} %shard_map.131.before, f32[2,512]{1,0:T(2,128)} %multiply_reduce_fusion.norms, bf16[2,2,1024,512]{3,2,1,0:T(8,128)(2,1)} %shard_map.128.refs_2_.refs_0_, ...), custom_call_target="tpu_custom_call" | custom-call | flops 1 | bytes 1 | tf_op jit(solution)/shard_map/pallas_call | solution.py:254
  194.4 0.6 collective-permute-start.18
  195.0 1.5 collective-permute-start.19
  196.5 2.4 %collective-permute-done.19 = f32[4,512]{1,0:T(4,128)S(1)} collective-permute-done((f32[4,512]{1,0:T(4,128)}, f32[4,512]{1,0:T(4,128)S(1)}, u32[]{:S(2)}, u32[]{:S(2)}) %collective-permute-start.19) | collective-permute-done | bytes 8224 | tf_op jit(solution)/shard_map/ppermute | solution.py:17
  198.9 1.0 collective-permute-done.20
  199.8 0.7 add_add_fusion.1
  200.5 1.4 collective-permute-start.21
  201.9 0.7 collective-permute-start.22
  202.6 2.4 %collective-permute-start.23 = (f32[4,512]{1,0:T(4,128)S(1)}, f32[4,512]{1,0:T(4,128)S(1)}, u32[]{:S(2)}, u32[]{:S(2)}) collective-permute-start(f32[4,512]{1,0:T(4,128)S(1)} %add_add_fusion.1), channel_id=1, source_target_pairs={{0,12},{1,13},{2,14},{3,15},{4,8},{5,9},{6,10},{7,11},{8,4},{9,5},... | collective-permute-start | bytes 24584 | tf_op jit(solution)/shard_map/ppermute | solution.py:17
  204.9 1.5 collective-permute-done.22
  206.5 1.6 collective-permute-done.23
  208.2 0.6 constant_dynamic-slice_fusion
  208.8 0.8 fusion
  (38 shorter events, 2.3 us)
Async XLA Ops:
  2.9 51.5 %collective-permute-start = (bf16[2,2,512,512]{3,2,1,0:T(8,128)(2,1)}, bf16[2,2,512,512]{3,2,1,0:T(8,128)(2,1)}, u32[]{:S(2)}, u32[]{:S(2)}) collective-permute-start(bf16[2,2,512,512]{3,2,1,0:T(8,128)(2,1)} %bitcast.15), channel_id=1, source_target_pairs={{0,2},{2,0},{4,6},{6,4},{8,10},{10,8},{12,14},{14,12},{1,3},{3,1},... | collective-permute-start | bytes 6291464 | tf_op jit(solution)/shard_map/ppermute | solution.py:17
  5.9 48.4 %collective-permute-start.1 = (bf16[1,2,512,512]{3,2,1,0:T(8,128)(2,1)}, bf16[1,2,512,512]{3,2,1,0:T(8,128)(2,1)}, u32[]{:S(2)}, u32[]{:S(2)}) collective-permute-start(bf16[1,2,512,512]{3,2,1,0:T(8,128)(2,1)} %slice_bitcast_fusion), channel_id=1, source_target_pairs={{0,8},{2,10},{4,12},{6,14},{8,0},{10,2},{12,4},{14,6},{1,9},{3,11}... | collective-permute-start | bytes 3145736 | tf_op jit(solution)/shard_map/ppermute | solution.py:17
  8.4 46.0 %collective-permute-start.2 = (bf16[1,2,512,512]{3,2,1,0:T(8,128)(2,1)}, bf16[1,2,512,512]{3,2,1,0:T(8,128)(2,1)}, u32[]{:S(2)}, u32[]{:S(2)}) collective-permute-start(bf16[1,2,512,512]{3,2,1,0:T(8,128)(2,1)} %slice_bitcast_fusion), channel_id=1, source_target_pairs={{0,4},{2,6},{4,0},{6,2},{8,12},{10,14},{12,8},{14,10},{1,5},{3,7},... | collective-permute-start | bytes 3145736 | tf_op jit(solution)/shard_map/ppermute | solution.py:17
  11.3 13.9 %copy-start = (s32[2]{0:T(128)}, s32[2]{0:T(128)S(1)}, u32[]{:S(2)}) copy-start(s32[2]{0:T(128)S(1)} %get-tuple-element.75.ids) | copy-start | bytes 28
  17.1 8.8 %copy-start.4 = (s32[3]{0:T(128)S(1)}, s32[3]{0:T(128)}, u32[]{:S(2)}) copy-start(s32[3]{0:T(128)} %constant.87.clone) | copy-start | bytes 40
  17.1 9.4 %copy-start.1 = (s32[3]{0:T(128)S(1)}, s32[3]{0:T(128)}, u32[]{:S(2)}) copy-start(s32[3]{0:T(128)} %constant.89.clone) | copy-start | bytes 40
  17.1 9.4 %copy-start.2 = (s32[3]{0:T(128)S(1)}, s32[3]{0:T(128)}, u32[]{:S(2)}) copy-start(s32[3]{0:T(128)} %constant.91.clone) | copy-start | bytes 40
  54.3 47.7 %collective-permute-start.3 = (bf16[1,2,512,512]{3,2,1,0:T(8,128)(2,1)}, bf16[1,2,512,512]{3,2,1,0:T(8,128)(2,1)}, u32[]{:S(2)}, u32[]{:S(2)}) collective-permute-start(bf16[1,2,512,512]{3,2,1,0:T(8,128)(2,1)} %slice.20), channel_id=1, source_target_pairs={{0,8},{2,10},{4,12},{6,14},{8,0},{10,2},{12,4},{14,6},{1,9},{3,11}... | collective-permute-start | bytes 3145736 | tf_op jit(solution)/shard_map/ppermute | solution.py:17
  54.5 47.6 %collective-permute-start.4 = (bf16[1,2,512,512]{3,2,1,0:T(8,128)(2,1)}, bf16[1,2,512,512]{3,2,1,0:T(8,128)(2,1)}, u32[]{:S(2)}, u32[]{:S(2)}) collective-permute-start(bf16[1,2,512,512]{3,2,1,0:T(8,128)(2,1)} %collective-permute-done.1.refs_2_.refs_4_), channel_id=1, source_target_pairs={{0,4},{2,6},{4,0},{6,2},{8,12},{10,14},{12,8},{14,10},{1,5},{3,7},... | collective-permute-start | bytes 3145736 | tf_op jit(solution)/shard_map/ppermute | solution.py:17
  58.2 43.9 %collective-permute-start.5 = (bf16[1,2,512,512]{3,2,1,0:T(8,128)(2,1)}, bf16[1,2,512,512]{3,2,1,0:T(8,128)(2,1)}, u32[]{:S(2)}, u32[]{:S(2)}) collective-permute-start(bf16[1,2,512,512]{3,2,1,0:T(8,128)(2,1)} %collective-permute-done.1.refs_2_.refs_4_), channel_id=1, source_target_pairs={{0,2},{2,0},{4,6},{6,4},{8,10},{10,8},{12,14},{14,12},{1,3},{3,1},... | collective-permute-start | bytes 3145736 | tf_op jit(solution)/shard_map/ppermute | solution.py:17
  58.8 46.8 %collective-permute-start.6 = (bf16[1,2,512,512]{3,2,1,0:T(8,128)(2,1)}, bf16[1,2,512,512]{3,2,1,0:T(8,128)(2,1)}, u32[]{:S(2)}, u32[]{:S(2)}) collective-permute-start(bf16[1,2,512,512]{3,2,1,0:T(8,128)(2,1)} %collective-permute-done.2.refs_1_.refs_2_), channel_id=1, source_target_pairs={{0,2},{2,0},{4,6},{6,4},{8,10},{10,8},{12,14},{14,12},{1,3},{3,1},... | collective-permute-start | bytes 3145736 | tf_op jit(solution)/shard_map/ppermute | solution.py:17
  105.5 28.5 %collective-permute-start.10 = (bf16[1,2,512,512]{3,2,1,0:T(8,128)(2,1)}, bf16[1,2,512,512]{3,2,1,0:T(8,128)(2,1)}, u32[]{:S(2)}, u32[]{:S(2)}) collective-permute-start(bf16[1,2,512,512]{3,2,1,0:T(8,128)(2,1)} %collective-permute-done.3.refs_0_.refs_7_), channel_id=1, source_target_pairs={{0,2},{2,0},{4,6},{6,4},{8,10},{10,8},{12,14},{14,12},{1,3},{3,1},... | collective-permute-start | bytes 3145736 | tf_op jit(solution)/shard_map/ppermute | solution.py:17
  106.1 27.9 %collective-permute-start.7 = (bf16[1,2,512,512]{3,2,1,0:T(8,128)(2,1)}, bf16[1,2,512,512]{3,2,1,0:T(8,128)(2,1)}, u32[]{:S(2)}, u32[]{:S(2)}) collective-permute-start(bf16[1,2,512,512]{3,2,1,0:T(8,128)(2,1)} %collective-permute-done.3.refs_0_.refs_7_), channel_id=1, source_target_pairs={{0,4},{2,6},{4,0},{6,2},{8,12},{10,14},{12,8},{14,10},{1,5},{3,7},... | collective-permute-start | bytes 3145736 | tf_op jit(solution)/shard_map/ppermute | solution.py:17
  106.4 45.8 %collective-permute-start.8 = (bf16[1,2,512,512]{3,2,1,0:T(8,128)(2,1)}, bf16[1,2,512,512]{3,2,1,0:T(8,128)(2,1)}, u32[]{:S(2)}, u32[]{:S(2)}) collective-permute-start(bf16[1,2,512,512]{3,2,1,0:T(8,128)(2,1)} %slice.20), channel_id=1, source_target_pairs={{0,4},{2,6},{4,0},{6,2},{8,12},{10,14},{12,8},{14,10},{1,5},{3,7},... | collective-permute-start | bytes 3145736 | tf_op jit(solution)/shard_map/ppermute | solution.py:17
  108.1 44.1 %collective-permute-start.9 = (bf16[1,2,512,512]{3,2,1,0:T(8,128)(2,1)}, bf16[1,2,512,512]{3,2,1,0:T(8,128)(2,1)}, u32[]{:S(2)}, u32[]{:S(2)}) collective-permute-start(bf16[1,2,512,512]{3,2,1,0:T(8,128)(2,1)} %collective-permute-done.4.refs_2_.refs_6_), channel_id=1, source_target_pairs={{0,2},{2,0},{4,6},{6,4},{8,10},{10,8},{12,14},{14,12},{1,3},{3,1},... | collective-permute-start | bytes 3145736 | tf_op jit(solution)/shard_map/ppermute | solution.py:17
  152.2 16.9 %collective-permute-start.13 = (bf16[2,2,1024,512]{3,2,1,0:T(8,128)(2,1)}, bf16[2,2,1024,512]{3,2,1,0:T(8,128)(2,1)}, u32[]{:S(2)}, u32[]{:S(2)}) collective-permute-start(bf16[2,2,1024,512]{3,2,1,0:T(8,128)(2,1)} %shard_map.128.refs_2_.refs_0_), channel_id=1, source_target_pairs={{0,1},{1,0},{2,3},{3,2},{4,5},{5,4},{6,7},{7,6},{8,9},{9,8},{10,11... | collective-permute-start | bytes 12582920 | tf_op jit(solution)/shard_map/ppermute | solution.py:17
  152.2 16.9 %collective-permute-start.14 = (bf16[1,2,512,512]{3,2,1,0:T(8,128)(2,1)}, bf16[1,2,512,512]{3,2,1,0:T(8,128)(2,1)}, u32[]{:S(2)}, u32[]{:S(2)}) collective-permute-start(bf16[1,2,512,512]{3,2,1,0:T(8,128)(2,1)} %collective-permute-done.9.refs_0_.refs_4_), channel_id=1, source_target_pairs={{0,1},{1,0},{2,3},{3,2},{4,5},{5,4},{6,7},{7,6},{8,9},{9,8},{10,11... | collective-permute-start | bytes 3145736 | tf_op jit(solution)/shard_map/ppermute | solution.py:17
  152.7 25.4 %collective-permute-start.11 = (bf16[1,2,512,512]{3,2,1,0:T(8,128)(2,1)}, bf16[1,2,512,512]{3,2,1,0:T(8,128)(2,1)}, u32[]{:S(2)}, u32[]{:S(2)}) collective-permute-start(bf16[1,2,512,512]{3,2,1,0:T(8,128)(2,1)} %slice.21), channel_id=1, source_target_pairs={{0,4},{2,6},{4,0},{6,2},{8,12},{10,14},{12,8},{14,10},{1,5},{3,7},... | collective-permute-start | bytes 3145736 | tf_op jit(solution)/shard_map/ppermute | solution.py:17
  153.4 25.1 %collective-permute-start.12 = (bf16[1,2,512,512]{3,2,1,0:T(8,128)(2,1)}, bf16[1,2,512,512]{3,2,1,0:T(8,128)(2,1)}, u32[]{:S(2)}, u32[]{:S(2)}) collective-permute-start(bf16[1,2,512,512]{3,2,1,0:T(8,128)(2,1)} %collective-permute-done.7.refs_0_.refs_2_), channel_id=1, source_target_pairs={{0,2},{2,0},{4,6},{6,4},{8,10},{10,8},{12,14},{14,12},{1,3},{3,1},... | collective-permute-start | bytes 3145736 | tf_op jit(solution)/shard_map/ppermute | solution.py:17
  178.5 10.2 %collective-permute-start.15 = (bf16[1,2,512,512]{3,2,1,0:T(8,128)(2,1)}, bf16[1,2,512,512]{3,2,1,0:T(8,128)(2,1)}, u32[]{:S(2)}, u32[]{:S(2)}) collective-permute-start(bf16[1,2,512,512]{3,2,1,0:T(8,128)(2,1)} %shard_map.130), channel_id=1, source_target_pairs={{0,1},{1,0},{2,3},{3,2},{4,5},{5,4},{6,7},{7,6},{8,9},{9,8},{10,11... | collective-permute-start | bytes 3145736 | tf_op jit(solution)/shard_map/ppermute | solution.py:17
  178.5 10.2 %collective-permute-start.16 = (bf16[1,2,512,512]{3,2,1,0:T(8,128)(2,1)}, bf16[1,2,512,512]{3,2,1,0:T(8,128)(2,1)}, u32[]{:S(2)}, u32[]{:S(2)}) collective-permute-start(bf16[1,2,512,512]{3,2,1,0:T(8,128)(2,1)} %collective-permute-done.11.refs_0_.refs_6_), channel_id=1, source_target_pairs={{0,1},{1,0},{2,3},{3,2},{4,5},{5,4},{6,7},{7,6},{8,9},{9,8},{10,11... | collective-permute-start | bytes 3145736 | tf_op jit(solution)/shard_map/ppermute | solution.py:17
  179.0 9.7 %collective-permute-start.17 = (bf16[1,2,512,512]{3,2,1,0:T(8,128)(2,1)}, bf16[1,2,512,512]{3,2,1,0:T(8,128)(2,1)}, u32[]{:S(2)}, u32[]{:S(2)}) collective-permute-start(bf16[1,2,512,512]{3,2,1,0:T(8,128)(2,1)} %collective-permute-done.12.refs_1_.refs_8_), channel_id=1, source_target_pairs={{0,1},{1,0},{2,3},{3,2},{4,5},{5,4},{6,7},{7,6},{8,9},{9,8},{10,11... | collective-permute-start | bytes 3145736 | tf_op jit(solution)/shard_map/ppermute | solution.py:17
  188.6 20.2 %copy-start.3 = (s32[16]{0:T(128)S(1)}, s32[16]{0:T(128)}, u32[]{:S(2)}) copy-start(s32[16]{0:T(128)} %param.13) | copy-start | bytes 196
  194.4 2.1 collective-permute-start.18
  195.0 3.9 %collective-permute-start.19 = (f32[4,512]{1,0:T(4,128)}, f32[4,512]{1,0:T(4,128)S(1)}, u32[]{:S(2)}, u32[]{:S(2)}) collective-permute-start(f32[4,512]{1,0:T(4,128)} %shard_map.133), channel_id=1, source_target_pairs={{0,2},{1,3},{2,0},{3,1},{4,6},{5,7},{6,4},{7,5},{8,10},{9,11},{10,... | collective-permute-start | bytes 24584 | tf_op jit(solution)/shard_map/ppermute | solution.py:17
  196.5 3.4 %collective-permute-start.20 = (f32[4,512]{1,0:T(4,128)}, f32[4,512]{1,0:T(4,128)S(1)}, u32[]{:S(2)}, u32[]{:S(2)}) collective-permute-start(f32[4,512]{1,0:T(4,128)} %shard_map.133), channel_id=1, source_target_pairs={{0,3},{1,2},{2,1},{3,0},{4,7},{5,6},{6,5},{7,4},{8,11},{9,10},{10,... | collective-permute-start | bytes 24584 | tf_op jit(solution)/shard_map/ppermute | solution.py:17
  200.5 4.4 %collective-permute-start.21 = (f32[4,512]{1,0:T(4,128)S(1)}, f32[4,512]{1,0:T(4,128)S(1)}, u32[]{:S(2)}, u32[]{:S(2)}) collective-permute-start(f32[4,512]{1,0:T(4,128)S(1)} %add_add_fusion.1), channel_id=1, source_target_pairs={{0,4},{1,5},{2,6},{3,7},{4,0},{5,1},{6,2},{7,3},{8,12},{9,13},{10,... | collective-permute-start | bytes 24584 | tf_op jit(solution)/shard_map/ppermute | solution.py:17
  201.9 4.5 %collective-permute-start.22 = (f32[4,512]{1,0:T(4,128)S(1)}, f32[4,512]{1,0:T(4,128)S(1)}, u32[]{:S(2)}, u32[]{:S(2)}) collective-permute-start(f32[4,512]{1,0:T(4,128)S(1)} %add_add_fusion.1), channel_id=1, source_target_pairs={{0,8},{1,9},{2,10},{3,11},{4,12},{5,13},{6,14},{7,15},{8,0},{9,1},... | collective-permute-start | bytes 24584 | tf_op jit(solution)/shard_map/ppermute | solution.py:17
  202.6 5.4 %collective-permute-start.23 = (f32[4,512]{1,0:T(4,128)S(1)}, f32[4,512]{1,0:T(4,128)S(1)}, u32[]{:S(2)}, u32[]{:S(2)}) collective-permute-start(f32[4,512]{1,0:T(4,128)S(1)} %add_add_fusion.1), channel_id=1, source_target_pairs={{0,12},{1,13},{2,14},{3,15},{4,8},{5,9},{6,10},{7,11},{8,4},{9,5},... | collective-permute-start | bytes 24584 | tf_op jit(solution)/shard_map/ppermute | solution.py:17

commit v8 on v0

v8 whole, which is shorter than its diff:
```python
import functools
import math

import jax
import jax.numpy as jnp
from jax import lax
from jax.experimental import pallas as pl
from jax.experimental.pallas import tpu as pltpu
from jax.sharding import PartitionSpec as P

VMEM_LIMIT = 63 * 1024 * 1024
HINT = pl.CostEstimate(flops=1, bytes_accessed=1, transcendentals=0)
ANYWHERE = pl.BlockSpec(memory_space=pl.ANY)


def swap(value, axis, mask):
    size = math.prod(lax.axis_size(name) for name in (axis if isinstance(axis, tuple) else (axis,)))
    return lax.ppermute(value, axis, [(source, source ^ mask) for source in range(size)])


def swap_some(value, mask, wanted):
    size = lax.axis_size("row")
    return lax.ppermute(value, "row", [(k, k ^ mask) for k in range(size) if wanted(k)])


def middle(index):
    return (index // 2) % 4 in (1, 2)


def end(index):
    return not middle(index)


def after(value, *others):
    return lax.optimization_barrier((value, *others))[0]


def sum_all(value):
    axes = ("row", "col")
    size = lax.axis_size("row") * lax.axis_size("col")
    if size > 16 or size & (size - 1):
        return lax.psum(value, axes)
    mask = 1
    while mask < size:
        near = value + swap(value, axes, mask)
        if 2 * mask < size:
            near = near + (swap(value, axes, 2 * mask) + swap(value, axes, 3 * mask))
        value, mask = near, 4 * mask
    return value


def dot(a, b):
    return jnp.dot(a, b, preferred_element_type=jnp.float32)


def at_freq(ref, freq):
    return ref.at[freq if ref.shape[0] > 1 else 0]


def weight_copies(freq, ref, right, sem):
    low = pl.ds(0, ref.shape[2])
    source = at_freq(ref, freq)
    return [
        pltpu.make_async_copy(source.at[0], right.at[0, low], sem.at[0]),
        pltpu.make_async_copy(source.at[1], right.at[1, low], sem.at[1]),
    ]


def spread(right):
    width = right.shape[1] // 2
    right[0, width:] = -right[1, :width]
    right[1, width:] = right[0, :width]


def spectra_copies(freq, column, cross, left, sem):
    width = left.shape[1] // 2
    columns = pl.ds(pl.multiple_of(column * width, width), width)
    return [
        pltpu.make_async_copy(
            cross.at[freq, part, :, columns], left.at[:, pl.ds(part * width, width)], sem.at[part]
        )
        for part in range(2)
    ]


def field_kernel(freq, count, has_total, ids, cross, *refs):
    w_refs, refs = refs[:count], refs[count:]
    total, refs = (refs[0], refs[1:]) if has_total else (None, refs)
    out, left, right, l_sem, w_sem, field, tot, tot_sem = refs
    piece, part = pl.program_id(0), pl.program_id(1)
    copies = [
        weight_copies(freq, ref, right.at[k], w_sem.at[k])
        + spectra_copies(freq, ids[k], cross, left.at[k], l_sem.at[k])
        for k, ref in enumerate(w_refs)
    ]
    for k, group in enumerate(copies):

        @pl.when((piece == k) & (part == 0))
        def _(k=k, group=group):
            if k == 0:
                for copy in group:
                    copy.start()
            for copy in group:
                copy.wait()
            if k + 1 < count:
                for copy in copies[k + 1]:
                    copy.start()
            if k == 0 and has_total:
                pltpu.make_async_copy(total, tot, tot_sem.at[0]).start()
            spread(right.at[k])

    last = piece == count - 1
    if count > 1:

        @pl.when(piece == 0)
        def _():
            field[part] = dot(left[piece], right[piece, part])

        @pl.when((piece > 0) & (piece < count - 1))
        def _():
            field[part] += dot(left[piece], right[piece, part])

    @pl.when(last)
    def _():
        value = dot(left[piece], right[piece, part])
        if count > 1:
            value += field[part]
        if has_total:

            @pl.when(part == 0)
            def _():
                pltpu.make_async_copy(total, tot, tot_sem.at[0]).wait()

            value += tot[part]
        out[0] = value


def add_field(cross, freq, ids, pieces, total=None):
    rows, (width, sources) = cross.shape[2], pieces[0].shape[2:]
    count, dtype = len(pieces), pieces[0].dtype
    has_total = total is not None
    return pl.pallas_call(
        functools.partial(field_kernel, freq, count, has_total),
        out_shape=jax.ShapeDtypeStruct((2, rows, sources), jnp.float32),
        grid_spec=pltpu.PrefetchScalarGridSpec(
            num_scalar_prefetch=1,
            grid=(count, 2),
            in_specs=[ANYWHERE] * (1 + count + has_total),
            out_specs=pl.BlockSpec(
                (1, rows, sources), lambda p, part, ids: (jnp.where(p == count - 1, part, 0), 0, 0)
            ),
            scratch_shapes=[
                pltpu.VMEM((count, rows, 2 * width), dtype),
                pltpu.VMEM((count, 2, 2 * width, sources), dtype),
                pltpu.SemaphoreType.DMA((count, 2)),
                pltpu.SemaphoreType.DMA((count, 2)),
                pltpu.VMEM((2, rows, sources), jnp.float32),
                pltpu.VMEM((2, rows, sources), jnp.float32),
                pltpu.SemaphoreType.DMA((1,)),
            ],
        ),
        compiler_params=pltpu.CompilerParams(vmem_limit_bytes=VMEM_LIMIT),
        cost_estimate=HINT,
    )(ids, cross, *pieces, *([total] if has_total else []))


def start_rows(freq, ids, base, refs, rows, sem):
    width = rows.shape[1] // 2
    views = []
    for picked, *pieces in (refs[:4], refs[4:]):
        views += [picked.at[freq, :, pl.ds(slot * width, width)] for slot in range(2)]
        views += [at_freq(ref, freq) for ref in pieces]
    for slot in range(2):
        here = pl.ds(slot * width, width)
        for k, source in enumerate(views):

            @pl.when(ids[base + slot] == k)
            def _(source=source, slot=slot, here=here):
                pltpu.make_async_copy(source, rows.at[:, here], sem.at[slot]).start()


def wait_rows(freq, slot, refs, rows, sem):
    width = rows.shape[1] // 2
    source = refs[0].at[freq, :, pl.ds(0, width)]
    here = rows.at[:, pl.ds(slot * width, width)]
    pltpu.make_async_copy(source, here, sem.at[slot]).wait()


def fold(rows, field):
    product = rows.astype(jnp.float32) * field
    return jnp.sum(product.reshape(-1, 8, product.shape[-1]), axis=0)


def late_kernel(freq, ids, cross, w5, w6, w7, block_re, block_im, total, *refs):
    row_refs, refs = refs[:8], refs[8:]
    sums, field_out, left, right, l_sem, w_sem, field, tot, sem, rows, row_sem = refs
    step, part = pl.program_id(0), pl.program_id(1)
    width = w5.shape[2]
    first = weight_copies(freq, w5, right.at[0], w_sem.at[0]) + spectra_copies(
        freq, ids[0], cross, left.at[0], l_sem.at[0]
    )
    six = weight_copies(freq, w6, right.at[1], w_sem.at[1])
    seven = weight_copies(freq, w7, right.at[1], w_sem.at[1])
    second = spectra_copies(freq, ids[1], cross, left.at[1], l_sem.at[1])
    third = [
        pltpu.make_async_copy(
            ref.at[0, min(k, ref.shape[1] - 1)],
            left.at[2, :, pl.ds(k * width, width)],
            l_sem.at[2, k],
        )
        for k, ref in enumerate((block_re, block_im))
    ]
    total_copy = pltpu.make_async_copy(total, tot, sem.at[0])
    out_copies = [
        pltpu.make_async_copy(field.at[k], field_out.at[k], sem.at[1 + k]) for k in range(2)
    ]

    @pl.when((step == 0) & (part == 0))
    def _():
        sums[...] = jnp.zeros_like(sums)
        for copy in first:
            copy.start()
        for copy in first:
            copy.wait()
        for copy in second:
            copy.start()

        @pl.when(ids[2] == 1)
        def _():
            for copy in seven:
                copy.start()

        @pl.when(ids[2] == 0)
        def _():
            for copy in six:
                copy.start()

        total_copy.start()
        spread(right.at[0])

    @pl.when((step == 1) & (part == 0))
    def _():
        for copy in second + six:
            copy.wait()
        for copy in third:
            copy.start()
        start_rows(freq, ids, 5, row_refs, rows, row_sem)
        total_copy.wait()
        spread(right.at[1])

    @pl.when((step == 2) & (part == 0))
    def _():
        for copy in third:
            copy.wait()
        for slot in range(2):
            wait_rows(freq, slot, row_refs, rows, row_sem)

    @pl.when(step == 0)
    def _():
        field[part] = dot(left[0], right[0, part])

    for k in range(2):

        @pl.when((step == 1) & (part == k))
        def _(k=k):
            field[k] = field[k] + tot[k] + dot(left[1], right[1, k])
            out_copies[k].start()

    @pl.when(step == 2)
    def _():
        sums[...] += fold(rows[part], dot(left[2], right[0, part]))

    @pl.when((step == 2) & (part == 1))
    def _():
        for copy in out_copies:
            copy.wait()


def add_late(cross, freq, ids, pieces, blocks, total, row_refs):
    rows, (width, sources) = cross.shape[2], pieces[0].shape[2:]
    dtype = pieces[0].dtype
    return pl.pallas_call(
        functools.partial(late_kernel, freq),
        out_shape=(
            jax.ShapeDtypeStruct((8, sources), jnp.float32),
            jax.ShapeDtypeStruct(total.shape, total.dtype),
        ),
        grid_spec=pltpu.PrefetchScalarGridSpec(
            num_scalar_prefetch=1,
            grid=(3, 2),
            in_specs=[ANYWHERE] * (7 + len(row_refs)),
            out_specs=(pl.BlockSpec((8, sources), lambda step, part, ids: (0, 0)), ANYWHERE),
            scratch_shapes=[
                pltpu.VMEM((3, rows, 2 * width), dtype),
                pltpu.VMEM((2, 2, 2 * width, sources), dtype),
                pltpu.SemaphoreType.DMA((3, 2)),
                pltpu.SemaphoreType.DMA((2, 2)),
                pltpu.VMEM((2, rows, sources), jnp.float32),
                pltpu.VMEM((2, rows, sources), jnp.float32),
                pltpu.SemaphoreType.DMA((3,)),
                pltpu.VMEM((2, rows, sources), dtype),
                pltpu.SemaphoreType.DMA((2,)),
            ],
        ),
        compiler_params=pltpu.CompilerParams(vmem_limit_bytes=VMEM_LIMIT),
        cost_estimate=HINT,
    )(ids, cross, *pieces, *blocks, total, *row_refs)


def dot_kernel(ids, norms, *refs):
    groups, (out, rows, row_sem, field, sem) = (refs[:10], refs[10:20]), refs[20:]
    width = rows.shape[2] // 2
    pairs = [(slot, part) for slot in range(2) for part in range(2)]
    copies = {}
    for freq, (field_ref, _, *row_refs) in enumerate(groups):
        start_rows(freq, ids, 3, row_refs, rows.at[freq], row_sem.at[freq])
        for slot, part in pairs:
            here = pl.ds(slot * width, width)
            copies[freq, slot, part] = pltpu.make_async_copy(
                field_ref.at[part, here], field.at[freq, part, here], sem.at[freq, 2 * slot + part]
            )
            copies[freq, slot, part].start()
    for freq, (_, sums_ref, *row_refs) in enumerate(groups):
        sums = sums_ref[...]
        for slot, part in pairs:
            if part == 0:
                wait_rows(freq, slot, row_refs, rows.at[freq], row_sem.at[freq])
            copies[freq, slot, part].wait()
            here = slice(slot * width, (slot + 1) * width)
            sums += fold(rows[freq, part, here], field[freq, part, here])
        out[freq : freq + 1] = jnp.sum(sums, axis=0, keepdims=True)
    out[2:4] = norms[...]


def dot_rows(ids, norms, groups):
    _, rows, sources = groups[0][0].shape
    whole = lambda shape: pl.BlockSpec(shape, lambda i, ids: (0, 0))
    return pl.pallas_call(
        dot_kernel,
        out_shape=jax.ShapeDtypeStruct((4, sources), jnp.float32),
        grid_spec=pltpu.PrefetchScalarGridSpec(
            num_scalar_prefetch=1,
            grid=(1,),
            in_specs=[whole((2, sources))] + [ANYWHERE, whole((8, sources)), *[ANYWHERE] * 8] * 2,
            out_specs=whole((4, sources)),
            scratch_shapes=[
                pltpu.VMEM((2, 2, rows, sources), groups[0][2].dtype),
                pltpu.SemaphoreType.DMA((2, 2)),
                pltpu.VMEM((2, 2, rows, sources), jnp.float32),
                pltpu.SemaphoreType.DMA((2, 4)),
            ],
        ),
        compiler_params=pltpu.CompilerParams(vmem_limit_bytes=VMEM_LIMIT),
        cost_estimate=HINT,
    )(ids, norms, *groups[0], *groups[1])


def copy_call(kernel, ids, shape, dtype, args, copies):
    return pl.pallas_call(
        kernel,
        out_shape=jax.ShapeDtypeStruct(shape, dtype),
        grid_spec=pltpu.PrefetchScalarGridSpec(
            num_scalar_prefetch=1,
            grid=(1,),
            in_specs=[ANYWHERE] * len(args),
            out_specs=pl.BlockSpec(shape, lambda i, ids: (0,) * len(shape)),
            scratch_shapes=[pltpu.SemaphoreType.DMA((copies,))],
        ),
        compiler_params=pltpu.CompilerParams(vmem_limit_bytes=VMEM_LIMIT),
        cost_estimate=HINT,
    )(ids, *args)


def block_kernel(freq, first, ids, cross, out, sem):
    width = out.shape[3]
    columns = pl.ds(pl.multiple_of(ids[0] * width, width), width)
    copies = [
        pltpu.make_async_copy(cross.at[freq, first + k, :, columns], out.at[0, k], sem.at[k])
        for k in range(out.shape[1])
    ]
    for copy in copies:
        copy.start()
    for copy in copies:
        copy.wait()


def take_block(cross, freq, parts, ids, width):
    shape = (1, len(parts), cross.shape[2], width)
    kernel = functools.partial(block_kernel, freq, parts[0])
    return copy_call(kernel, ids, shape, cross.dtype, [cross], len(parts))


def pair_kernel(ids, own, x, n, m, out, sem):
    width = own.shape[2]
    for pair in (0, 1):
        copies = [
            pltpu.make_async_copy(
                ref.at[freq], out.at[freq, :, pl.ds(slot * width, width)], sem.at[2 * freq + slot]
            )
            for freq in range(out.shape[0])
            for slot, ref in enumerate(((own, x), (n, m))[pair])
        ]

        @pl.when(ids[0] == pair)
        def _(copies=copies):
            for copy in copies:
                copy.start()
            for copy in copies:
                copy.wait()


def take_pair(ids, own, x, n, m):
    freqs, _, width, sources = own.shape
    shape = (freqs, 2, 2 * width, sources)
    return copy_call(pair_kernel, ids, shape, own.dtype, [own, x, n, m], 2 * freqs)


def either_kernel(freqs, ids, first, second, out, sem):
    for k, ref in enumerate((first, second)):

        @pl.when(ids[0] == k)
        def _(ref=ref):
            copies = [
                pltpu.make_async_copy(at_freq(ref, freq), out.at[slot], sem.at[slot])
                for slot, freq in enumerate(freqs)
            ]
            for copy in copies:
                copy.start()
            for copy in copies:
                copy.wait()


def take_either(freqs, ids, first, second):
    shape = (len(freqs), *first.shape[1:])
    kernel = functools.partial(either_kernel, freqs)
    return copy_call(kernel, ids, shape, first.dtype, [first, second], len(freqs))


def sums_by_swaps(cross, replicas, norms):
    rows, half = cross.shape[2], cross.shape[3]
    width = replicas.shape[3]
    me = lax.axis_index("row").astype(jnp.int32)
    col = lax.axis_index("col").astype(jnp.int32)
    holds = me * rows // half == col
    mid = ((me // 2) % 4 == 1) | ((me // 2) % 4 == 2)
    flag = lambda value: jnp.where(value, 1, 0).astype(jnp.int32).reshape(1)
    ids = lambda *wanted: me ^ jnp.array(wanted, jnp.int32)
    barrier = lambda *values: lax.optimization_barrier(values)

    slots = jnp.arange(2, dtype=jnp.int32)
    per_half = half // width
    own_masks = (2 * me % per_half + slots) ^ me
    next_masks = ((2 * (me ^ 2) % per_half + slots) ^ me) & 3
    table = lambda masks: sum(
        jnp.where(masks == mask, place, 0)
        for mask, place in enumerate((0, 1, 0, 2, 2, 4, 1, 3))
    ) + jnp.where(holds, 0, 5)
    late_ids = jnp.concatenate(
        [
            ids(5),
            jnp.where(mid, ids(7), ids(6)),
            flag(mid),
            table(own_masks),
            table(next_masks),
        ]
    ).astype(jnp.int32)
    pair = flag(((me >> 1) ^ me) & 1 != 0)
    numbers = [ids(1, 2, 6), ids(3, 4), ids(7), late_ids, pair, flag(mid)]

    own = replicas[:, :, 0]
    x = swap(own, "row", 1)
    n = swap(own, "row", 2)
    m = swap_some(own, 6, middle)
    a0 = add_field(cross, 0, ids(0), [own])
    a1 = add_field(cross, 1, ids(0), [own])
    block_a = take_block(cross, 0, (0, 1), ids(7), width)
    x, n, m, a0, a1, block_a, norms, *numbers = barrier(x, n, m, a0, a1, block_a, norms, *numbers)
    ids_a, ids_b, ids_7, late_ids, pair, is_mid = numbers

    g = swap_some(m, 2, middle)
    m2 = swap_some(n, 6, middle)
    xn = swap(n, "row", 1)
    block_a = swap_some(block_a, 2, end)
    a0 = add_field(cross, 0, ids_a, [x, n, m], a0)
    a1 = add_field(cross, 1, ids_a, [x, n, m], a1)
    block_re = take_block(cross, 1, (0,), ids_7, width)
    block_im = take_block(cross, 1, (1,), ids_7, width)
    mine = take_pair(pair, own, x, n, m)
    x_a, x_b = x[0:1], x[1:2]
    g, m2, xn, block_a, a0, a1, block_re, block_im, mine, x_a, x_b = barrier(
        g, m2, xn, block_a, a0, a1, block_re, block_im, mine, x_a, x_b
    )

    w4_a = take_either((0,), is_mid, g, m2)
    x5_a = swap(w4_a, "row", 1)
    w6_a = swap_some(w4_a, 2, middle)
    w7_a = swap_some(x_a, 6, middle)
    block_re = swap_some(block_re, 2, end)
    other = swap(mine, "col", 1)
    b0 = add_field(cross, 0, ids_b, [xn, w4_a], a0)
    w4_b = take_either((1,), after(is_mid, b0), g, m2)
    later = take_either((0, 1), after(pair, b0), m2, xn)
    b1 = add_field(cross, 1, ids_b, [xn, w4_b], a1)
    x5_a, w6_a, w7_a, block_re, other, b0, w4_b, later, x_b, block_im = barrier(
        x5_a, w6_a, w7_a, block_re, other, b0, w4_b, later, x_b, block_im
    )

    x5_b = swap(w4_b, "row", 1)
    w6_b = swap_some(w4_b, 2, middle)
    w7_b = swap_some(x_b, 6, middle)
    block_im = swap_some(block_im, 2, end)
    other_later = swap(later, "col", 1)
    early = [mine, later, later, later, other, other_later, other_later, other_later]
    sums_a, field_a = add_late(
        cross, 0, late_ids, [x5_a, w6_a, w7_a], [block_a, block_a], b0, early
    )
    late_a = take_either((0,), pair, x5_a, w7_a)
    x5_b, w6_b, w7_b, block_im, sums_a, field_a, b1, late_a, other_later = barrier(
        x5_b, w6_b, w7_b, block_im, sums_a, field_a, b1, late_a, other_later
    )

    other_late_a = swap(late_a, "col", 1)
    other_w7_b = swap(w7_b, "col", 1)
    other_x5_b = swap(x5_b, "col", 1)
    early[5:] = [other_later] * 3
    sums_b, field_b = add_late(
        cross, 1, late_ids, [x5_b, w6_b, w7_b], [block_re, block_im], b1, early
    )
    rows_a = [mine, later, late_a, late_a, other, other_later, other_late_a, other_late_a]
    rows_b = [mine, later, w7_b, x5_b, other, other_later, other_w7_b, other_x5_b]
    groups = [(field_a, sums_a, *rows_a), (field_b, sums_b, *rows_b)]
    return dot_rows(late_ids, norms, groups)


def sums_by_gather(cross, replicas, norms):
    rows, half = cross.shape[2], cross.shape[3]
    row_index, col_index = lax.axis_index("row"), lax.axis_index("col")
    first_row = row_index * rows
    holder = first_row // half
    whole = lax.all_gather(replicas, "row", axis=3, tiled=True)[:, :, 0]
    parts = jnp.einsum("fark,fbks->fabrs", cross, whole, preferred_element_type=jnp.float32)
    field = jnp.stack([parts[:, 0, 0] - parts[:, 1, 1], parts[:, 0, 1] + parts[:, 1, 0]], axis=1)
    own_rows = lax.dynamic_slice_in_dim(whole, first_row - holder * half, rows, 2)
    block_rows = jnp.where(holder == col_index, own_rows, swap(own_rows, "col", 1))
    numer = jnp.sum(block_rows.astype(jnp.float32) * field, axis=(1, 2))
    return jnp.concatenate([numer, norms])


def body(cross_spectra, replicas, tile_order):
    fnum = cross_spectra.shape[0]
    sources = replicas.shape[4]
    own = replicas[:, :, 0].astype(jnp.float32)
    norms = jnp.sum(own * own, axis=(1, 2))
    doubling = (
        lax.axis_size("row") == 8
        and fnum == 2
        and replicas.shape[3] % 128 == 0
        and cross_spectra.shape[2] == 2 * replicas.shape[3]
    )
    sums = (sums_by_swaps if doubling else sums_by_gather)(cross_spectra, replicas, norms)
    sums = sum_all(sums)
    numer, norms = sums[:fnum], sums[fnum:]
    beam = numer / (norms + 1e-06)
    width = sources // lax.axis_size("col")
    beam_half = lax.dynamic_slice_in_dim(beam, lax.axis_index("col") * width, width, 1)
    peak = jnp.max(jnp.abs(beam), axis=1) + 1e-06
    count = tile_order.shape[0]
    picker = (tile_order[:, None] == jnp.arange(count, dtype=jnp.int32)[None, :]).astype(jnp.float32)
    tiles = beam.reshape(fnum, count, sources // count)
    refined = (
        jnp.einsum("tu,fup->ftp", picker, tiles, precision=lax.Precision.HIGHEST)
        / peak[:, None, None]
    )
    return (beam_half, refined)


def solution(mesh):
    in_specs = (P("groups", None, "row", "col"), P("groups", None, "col", "row", None), P("groups"))
    out_specs = (P("groups", "col"), P("groups", None, None))
    return jax.shard_map(body, mesh=mesh, in_specs=in_specs, out_specs=out_specs, check_vma=False)
```

time: 355 us -> 213 us (0.60)
  waiting for transfers between devices: 243 us -> 42.9 us
  Pallas kernels: 0 us -> 107 us
  starting transfers between devices: 0.13 us -> 51.3 us
  matrix products: 44 us -> 0.8 us
  blocking collectives: 22.8 us -> 0 us
  between operations: 15.5 us -> 1.01 us
  other arithmetic: 17.7 us -> 4.53 us
  local copies, waits for them, and re-layouts: 11.4 us -> 4.47 us
    all_gather x1 -> x0, waiting for transfers between devices: 229 us -> none  [body(): whole = lax.all_gather(replicas, 'row', axis=3, tiled=True)[:, :, 0]]
    pallas_call x0 -> x17, Pallas kernels: none -> 107 us  [the longest x6 55.6 us: add_field(): pl.pallas_call(functools.partial(field_kernel, freq, count, has_total), o...]
    ppermute x1 -> x26, starting transfers between devices: 0.01 us -> 51.3 us  [the longest x10 37.1 us: swap_some(): lax.ppermute(value, 'row', [(k, k ^ mask) for k in range(size) if wanted(...]
    dot_general x1 -> x0, matrix products: 43.2 us -> none  [body(): jnp.einsum('fark,fbks->fabrs', cross_spectra, whole, preferred_element_ty...]
    ppermute x1 -> x26, waiting for transfers between devices: 7.87 us -> 42.9 us  [the longest x16 32.2 us: swap(): lax.ppermute(value, axis, [(source, source ^ mask) for source in range(si...]
    psum x1 -> x0, blocking collectives: 21 us -> none  [body(): numer, norms = lax.psum((numer, norm_part), 'row')]
    reduce_scatter x1 -> x0, waiting for transfers between devices: 6.28 us -> none  [body(): lax.psum_scatter(field, 'col', scatter_dimension=3, tiled=True)]
    unnamed x9 -> x6, local copies, waits for them, and re-layouts: 6.16 us -> 0.02 us
  transfers between devices with their start and end apart: 4 -> 26, of which waited for: 3 -> 10; matrix products, arithmetic and copies ran while one was open for 18% -> 4% of each run, Pallas kernels for 0% -> 47%
where the time goes in v8:
time: 213 us; the launch traced here: 212 us
  Pallas kernels  107 us (50%)
  starting transfers between devices  51.3 us (24%)
  waiting for transfers between devices  42.9 us (20%)
  other arithmetic  4.53 us (2%)
  local copies, waits for them, and re-layouts  4.47 us (2%)
    pallas_call x6, Pallas kernels, add_field(): pl.pallas_call(functools.partial(field_kernel, freq, count, has_total), o...  55.6 us
    ppermute x10, starting transfers between devices, swap_some(): lax.ppermute(value, 'row', [(k, k ^ mask) for k in range(size) if wanted(...  37.1 us
    ppermute x16, waiting for transfers between devices, swap(): lax.ppermute(value, axis, [(source, source ^ mask) for source in range(si...  32.2 us
    pallas_call x2, Pallas kernels, add_late(): pl.pallas_call(functools.partial(late_kernel, freq), out_shape=(jax.Shape...  23.4 us
    pallas_call x8, Pallas kernels, copy_call(): pl.pallas_call(kernel, out_shape=jax.ShapeDtypeStruct(shape, dtype), grid...  21.3 us
    ppermute x16, starting transfers between devices, swap(): lax.ppermute(value, axis, [(source, source ^ mask) for source in range(si...  14.2 us
    ppermute x10, waiting for transfers between devices, swap_some(): lax.ppermute(value, 'row', [(k, k ^ mask) for k in range(size) if wanted(...  10.7 us
    pallas_call x1, Pallas kernels, dot_rows(): pl.pallas_call(dot_kernel, out_shape=jax.ShapeDtypeStruct((4, sources), j...  6.87 us
  transfers between devices with their start and end apart: 26, of which 10 were waited for; matrix products, arithmetic and copies ran while one was open for 4% of the time, Pallas kernels for 47%

profile of v8, /device:TPU:0, one launch (start us, length us, event | category | flops | bytes accessed | tf_op | source)
XLA Modules:
  0.0 212.1 jit_solution(3905125697467841791)
XLA Ops:
  0.6 3.0 %collective-permute-start = (bf16[2,2,512,512]{3,2,1,0:T(8,128)(2,1)}, bf16[2,2,512,512]{3,2,1,0:T(8,128)(2,1)}, u32[]{:S(2)}, u32[]{:S(2)}) collective-permute-start(bf16[2,2,512,512]{3,2,1,0:T(8,128)(2,1)} %bitcast.12), channel_id=1, source_target_pairs={{0,2},{2,0},{4,6},{6,4},{8,10},{10,8},{12,14},{14,12},{1,3},{3,1},... | collective-permute-start | bytes 6291464 | tf_op jit(solution)/shard_map/ppermute | solution.py:18
  3.6 1.6 collective-permute-start.1
  5.2 1.9 collective-permute-start.2
  7.2 5.9 %shard_map.131.refs_3_ = f32[2,1024,512]{2,1,0:T(8,128)} custom-call(s32[1]{0:T(128)} %bitcast.1.ids, bf16[2,2,1024,4096]{3,2,1,0:T(8,128)(2,1)} %cross.21, bf16[2,2,512,512]{3,2,1,0:T(8,128)(2,1)} %bitcast.15), custom_call_target="tpu_custom_call" | custom-call | flops 1 | bytes 1 | tf_op jit(solution)/shard_map/pallas_call | solution.py:142
  13.1 5.8 %shard_map.132.refs_3_ = f32[2,1024,512]{2,1,0:T(8,128)} custom-call(s32[1]{0:T(128)} %bitcast.1.ids, bf16[2,2,1024,4096]{3,2,1,0:T(8,128)(2,1)} %cross.21, bf16[2,2,512,512]{3,2,1,0:T(8,128)(2,1)} %bitcast.16), custom_call_target="tpu_custom_call" | custom-call | flops 1 | bytes 1 | tf_op jit(solution)/shard_map/pallas_call | solution.py:142
  18.9 2.9 %shard_map.133 = bf16[1,2,1024,512]{3,2,1,0:T(8,128)(2,1)} custom-call(s32[1]{0:T(128)S(6)} %xor.59.ids, bf16[2,2,1024,4096]{3,2,1,0:T(8,128)(2,1)} %cross.21), custom_call_target="tpu_custom_call" | custom-call | flops 1 | bytes 1 | tf_op jit(solution)/shard_map/pallas_call | solution.py:359
  22.0 0.7 concatenate.3.ids
  23.7 2.6 %multiply_reduce_fusion.norms = f32[2,512]{1,0:T(2,128)} fusion(bf16[2,2,1,512,512]{4,3,2,1,0:T(8,128)(2,1)} %param.13), kind=kLoop, calls=%fused_computation | loop fusion | flops 3144704 | bytes 2101248 | tf_op jit(solution)/shard_map/reduce_sum | solution.py:553
  26.3 23.3 %collective-permute-done.refs_0_.x = bf16[2,2,512,512]{3,2,1,0:T(8,128)(2,1)} collective-permute-done((bf16[2,2,512,512]{3,2,1,0:T(8,128)(2,1)}, bf16[2,2,512,512]{3,2,1,0:T(8,128)(2,1)}, u32[]{:S(2)}, u32[]{:S(2)}) %collective-permute-start) | collective-permute-done | bytes 2097184 | tf_op jit(solution)/shard_map/ppermute | solution.py:18
  49.6 1.5 collective-permute-done.1.refs_1_.n
  51.0 1.3 collective-permute-start.3
  52.3 2.0 collective-permute-start.4
  54.7 11.1 %collective-permute-start.6 = (bf16[1,2,1024,512]{3,2,1,0:T(8,128)(2,1)}, bf16[1,2,1024,512]{3,2,1,0:T(8,128)(2,1)}, u32[]{:S(2)}, u32[]{:S(2)}) collective-permute-start(bf16[1,2,1024,512]{3,2,1,0:T(8,128)(2,1)} %shard_map.133), channel_id=1, source_target_pairs={{0,4},{2,6},{12,8},{14,10},{1,5},{3,7},{13,9},{15,11},{16,20},{18,... | collective-permute-start | bytes 6291464 | tf_op jit(solution)/shard_map/ppermute | solution.py:23
  65.8 2.2 %shard_map.136 = bf16[1,1,1024,512]{3,2,1,0:T(8,128)(2,1)} custom-call(s32[1]{0:T(128)S(6)} %xor.59.ids, bf16[2,2,1024,4096]{3,2,1,0:T(8,128)(2,1)} %cross.21), custom_call_target="tpu_custom_call" | custom-call | flops 1 | bytes 1 | tf_op jit(solution)/shard_map/pallas_call | solution.py:359
  68.0 2.2 %shard_map.137 = bf16[1,1,1024,512]{3,2,1,0:T(8,128)(2,1)} custom-call(s32[1]{0:T(128)S(6)} %xor.59.ids, bf16[2,2,1024,4096]{3,2,1,0:T(8,128)(2,1)} %cross.21), custom_call_target="tpu_custom_call" | custom-call | flops 1 | bytes 1 | tf_op jit(solution)/shard_map/pallas_call | solution.py:359
  70.2 4.2 %shard_map.138.refs_0_.refs_2_.refs_12_ = bf16[2,2,1024,512]{3,2,1,0:T(8,128)(2,1)} custom-call(s32[1]{0:T(128)} %bitcast.4.ids, bf16[2,2,512,512]{3,2,1,0:T(8,128)(2,1)} %bitcast.17, bf16[2,2,512,512]{3,2,1,0:T(8,128)(2,1)} %collective-permute-done.refs_0_.x, bf16[2,2,512,512]{3,2,1,0:T(8,128)(2,1)} %collective-permute-done.1.refs_1_.n, ...), custom_call_target="tpu_custom_call" | custom-call | flops 1 | bytes 1 | tf_op jit(solution)/shard_map/pallas_call | solution.py:359
  74.4 12.4 %shard_map.135.refs_2_ = f32[2,1024,512]{2,1,0:T(8,128)} custom-call(s32[3]{0:T(128)} %broadcast_xor_fusion.1.ids, bf16[2,2,1024,4096]{3,2,1,0:T(8,128)(2,1)} %cross.21, bf16[2,2,512,512]{3,2,1,0:T(8,128)(2,1)} %collective-permute-done.refs_0_.x, bf16[2,2,512,512]{3,2,1,0:T(8,128)(2,1)} %collective-permute-done.1.refs_1_.n, ...), custom_call_target="tpu_custom_call" | custom-call | flops 1 | bytes 1 | tf_op jit(solution)/shard_map/pallas_call | solution.py:142
  86.8 12.3 %shard_map.134.refs_2_ = f32[2,1024,512]{2,1,0:T(8,128)} custom-call(s32[3]{0:T(128)} %broadcast_xor_fusion.1.ids, bf16[2,2,1024,4096]{3,2,1,0:T(8,128)(2,1)} %cross.21, bf16[2,2,512,512]{3,2,1,0:T(8,128)(2,1)} %collective-permute-done.refs_0_.x, bf16[2,2,512,512]{3,2,1,0:T(8,128)(2,1)} %collective-permute-done.1.refs_1_.n, ...), custom_call_target="tpu_custom_call" | custom-call | flops 1 | bytes 1 | tf_op jit(solution)/shard_map/pallas_call | solution.py:142
  99.1 3.1 %fusion.18 = (bf16[1,2,512,512]{3,2,1,0:T(8,128)(2,1)}, bf16[1,2,512,512]{3,2,1,0:T(8,128)(2,1)}) fusion(bf16[2,2,512,512]{3,2,1,0:T(8,128)(2,1)} %collective-permute-done.refs_0_.x), kind=kLoop, calls=%fused_computation.39 | loop fusion | bytes 4194304 | tf_op jit(solution)/shard_map/slice | solution.py:489
  102.2 5.3 %collective-permute-done.6.block_re.block_im = bf16[1,2,1024,512]{3,2,1,0:T(8,128)(2,1)} collective-permute-done((bf16[1,2,1024,512]{3,2,1,0:T(8,128)(2,1)}, bf16[1,2,1024,512]{3,2,1,0:T(8,128)(2,1)}, u32[]{:S(2)}, u32[]{:S(2)}) %collective-permute-start.6) | collective-permute-done | bytes 2097184 | tf_op jit(solution)/shard_map/ppermute | solution.py:23
  107.6 2.2 %shard_map.139.refs_1_ = bf16[1,2,512,512]{3,2,1,0:T(8,128)(2,1)} custom-call(s32[1]{0:T(128)} %bitcast.3.ids, bf16[2,2,512,512]{3,2,1,0:T(8,128)(2,1)} %collective-permute-done.3.first, bf16[2,2,512,512]{3,2,1,0:T(8,128)(2,1)} %collective-permute-done.4.second.first), custom_call_target="tpu_custom_call" | custom-call | flops 1 | bytes 1 | tf_op jit(solution)/shard_map/pallas_call | solution.py:359
  109.8 1.6 collective-permute-start.7
  111.4 1.3 collective-permute-start.8
  112.7 6.5 %collective-permute-start.10 = (bf16[1,1,1024,512]{3,2,1,0:T(8,128)(2,1)}, bf16[1,1,1024,512]{3,2,1,0:T(8,128)(2,1)}, u32[]{:S(2)}, u32[]{:S(2)}) collective-permute-start(bf16[1,1,1024,512]{3,2,1,0:T(8,128)(2,1)} %shard_map.136), channel_id=1, source_target_pairs={{0,4},{2,6},{12,8},{14,10},{1,5},{3,7},{13,9},{15,11},{16,20},{18,... | collective-permute-start | bytes 3145736 | tf_op jit(solution)/shard_map/ppermute | solution.py:23
  119.2 1.6 collective-permute-start.9
  120.8 9.6 %shard_map.140.total = f32[2,1024,512]{2,1,0:T(8,128)} custom-call(s32[2]{0:T(128)} %broadcast_xor_fusion.ids, bf16[2,2,1024,4096]{3,2,1,0:T(8,128)(2,1)} %cross.21, bf16[2,2,512,512]{3,2,1,0:T(8,128)(2,1)} %collective-permute-done.5.refs_0_.second, bf16[1,2,512,512]{3,2,1,0:T(8,128)(2,1)} %shard_map.139.refs_1_, f32[2,1024,512]{2,1,0:T(8,128)} %shard_map.134.refs_2_), custom_call_target="tpu_custom_call" | custom-call | flops 1 | bytes 1 | tf_op jit(solution)/shard_map/pallas_call | solution.py:142
  130.4 3.0 %shard_map.142.refs_1_.refs_2_.refs_3_.refs_13_ = bf16[2,2,512,512]{3,2,1,0:T(8,128)(2,1)} custom-call(s32[1]{0:T(128)} %bitcast.4.ids, bf16[2,2,512,512]{3,2,1,0:T(8,128)(2,1)} %collective-permute-done.4.second.first, bf16[2,2,512,512]{3,2,1,0:T(8,128)(2,1)} %collective-permute-done.5.refs_0_.second), custom_call_target="tpu_custom_call" | custom-call | flops 1 | bytes 1 | tf_op jit(solution)/shard_map/pallas_call | solution.py:359
  133.4 2.2 %shard_map.141.refs_1_ = bf16[1,2,512,512]{3,2,1,0:T(8,128)(2,1)} custom-call(s32[1]{0:T(128)} %bitcast.3.ids, bf16[2,2,512,512]{3,2,1,0:T(8,128)(2,1)} %collective-permute-done.3.first, bf16[2,2,512,512]{3,2,1,0:T(8,128)(2,1)} %collective-permute-done.4.second.first), custom_call_target="tpu_custom_call" | custom-call | flops 1 | bytes 1 | tf_op jit(solution)/shard_map/pallas_call | solution.py:359
  135.8 3.2 %collective-permute-done.8.w6 = bf16[1,2,512,512]{3,2,1,0:T(8,128)(2,1)} collective-permute-done((bf16[1,2,512,512]{3,2,1,0:T(8,128)(2,1)}, bf16[1,2,512,512]{3,2,1,0:T(8,128)(2,1)}, u32[]{:S(2)}, u32[]{:S(2)}) %collective-permute-start.8) | collective-permute-done | bytes 1048608 | tf_op jit(solution)/shard_map/ppermute | solution.py:23
  139.0 2.2 %collective-permute-done.10.block_re = bf16[1,1,1024,512]{3,2,1,0:T(8,128)(2,1)} collective-permute-done((bf16[1,1,1024,512]{3,2,1,0:T(8,128)(2,1)}, bf16[1,1,1024,512]{3,2,1,0:T(8,128)(2,1)}, u32[]{:S(2)}, u32[]{:S(2)}) %collective-permute-start.10) | collective-permute-done | bytes 1048608 | tf_op jit(solution)/shard_map/ppermute | solution.py:23
  141.7 1.3 collective-permute-start.13
  143.0 1.6 collective-permute-start.14
  144.7 8.5 %collective-permute-start.15 = (bf16[1,1,1024,512]{3,2,1,0:T(8,128)(2,1)}, bf16[1,1,1024,512]{3,2,1,0:T(8,128)(2,1)}, u32[]{:S(2)}, u32[]{:S(2)}) collective-permute-start(bf16[1,1,1024,512]{3,2,1,0:T(8,128)(2,1)} %shard_map.137), channel_id=1, source_target_pairs={{0,4},{2,6},{12,8},{14,10},{1,5},{3,7},{13,9},{15,11},{16,20},{18,... | collective-permute-start | bytes 3145736 | tf_op jit(solution)/shard_map/ppermute | solution.py:23
  153.1 9.6 %shard_map.144.total = f32[2,1024,512]{2,1,0:T(8,128)} custom-call(s32[2]{0:T(128)} %broadcast_xor_fusion.ids, bf16[2,2,1024,4096]{3,2,1,0:T(8,128)(2,1)} %cross.21, bf16[2,2,512,512]{3,2,1,0:T(8,128)(2,1)} %collective-permute-done.5.refs_0_.second, bf16[1,2,512,512]{3,2,1,0:T(8,128)(2,1)} %shard_map.141.refs_1_, f32[2,1024,512]{2,1,0:T(8,128)} %shard_map.135.refs_2_), custom_call_target="tpu_custom_call" | custom-call | flops 1 | bytes 1 | tf_op jit(solution)/shard_map/pallas_call | solution.py:142
  162.7 2.3 %shard_map.145.refs_4_.refs_5_ = bf16[1,2,512,512]{3,2,1,0:T(8,128)(2,1)} custom-call(s32[1]{0:T(128)} %bitcast.4.ids, bf16[1,2,512,512]{3,2,1,0:T(8,128)(2,1)} %collective-permute-done.7.w5.first, bf16[1,2,512,512]{3,2,1,0:T(8,128)(2,1)} %collective-permute-done.9.w7.second), custom_call_target="tpu_custom_call" | custom-call | flops 1 | bytes 1 | tf_op jit(solution)/shard_map/pallas_call | solution.py:359
  165.1 11.7 %shard_map.143 = (f32[8,512]{1,0:T(8,128)}, f32[2,1024,512]{2,1,0:T(8,128)}) custom-call(s32[7]{0:T(128)} %concatenate.3.ids, bf16[2,2,1024,4096]{3,2,1,0:T(8,128)(2,1)} %cross.21, bf16[1,2,512,512]{3,2,1,0:T(8,128)(2,1)} %collective-permute-done.7.w5.first, bf16[1,2,512,512]{3,2,1,0:T(8,128)(2,1)} %collective-permute-done.8.w6, ...), custom_call_target="tpu_custom_call" | custom-call | flops 1 | bytes 1 | tf_op jit(solution)/shard_map/pallas_call | solution.py:282
  177.5 11.7 %shard_map.146 = (f32[8,512]{1,0:T(8,128)}, f32[2,1024,512]{2,1,0:T(8,128)}) custom-call(s32[7]{0:T(128)} %concatenate.3.ids, bf16[2,2,1024,4096]{3,2,1,0:T(8,128)(2,1)} %cross.21, bf16[1,2,512,512]{3,2,1,0:T(8,128)(2,1)} %collective-permute-done.12.w5.refs_15_, bf16[1,2,512,512]{3,2,1,0:T(8,128)(2,1)} %collective-permute-done.13.w6, ...), custom_call_target="tpu_custom_call" | custom-call | flops 1 | bytes 1 | tf_op jit(solution)/shard_map/pallas_call | solution.py:282
  189.2 6.9 %shard_map.147 = f32[4,512]{1,0:T(4,128)} custom-call(s32[7]{0:T(128)} %concatenate.3.ids, f32[2,512]{1,0:T(2,128)} %multiply_reduce_fusion.norms, f32[2,1024,512]{2,1,0:T(8,128)} %get-tuple-element.88.refs_0_, f32[8,512]{1,0:T(8,128)} %get-tuple-element.89.refs_1_, bf16[2,2,1024,512]{3,2,1,0:T(8,128)(2,1)} %shard_map.138.refs_0_.refs_2_.refs_12_, ...), custom_call_target="tpu_custom_call" | custom-call | flops 1 | bytes 1 | tf_op jit(solution)/shard_map/pallas_call | solution.py:338
  196.5 1.5 collective-permute-start.21
  198.0 2.4 %collective-permute-done.21 = f32[4,512]{1,0:T(4,128)S(1)} collective-permute-done((f32[4,512]{1,0:T(4,128)}, f32[4,512]{1,0:T(4,128)S(1)}, u32[]{:S(2)}, u32[]{:S(2)}) %collective-permute-start.21) | collective-permute-done | bytes 8224 | tf_op jit(solution)/shard_map/ppermute | solution.py:18
  200.4 1.0 collective-permute-done.22
  201.4 0.7 add_add_fusion.1
  202.1 0.6 collective-permute-start.23
  202.7 2.3 %collective-permute-start.24 = (f32[4,512]{1,0:T(4,128)S(1)}, f32[4,512]{1,0:T(4,128)S(1)}, u32[]{:S(2)}, u32[]{:S(2)}) collective-permute-start(f32[4,512]{1,0:T(4,128)S(1)} %add_add_fusion.1), channel_id=1, source_target_pairs={{0,8},{1,9},{2,10},{3,11},{4,12},{5,13},{6,14},{7,15},{8,0},{9,1},... | collective-permute-start | bytes 24584 | tf_op jit(solution)/shard_map/ppermute | solution.py:18
  205.0 1.5 collective-permute-start.25
  206.5 0.8 collective-permute-done.24
  207.3 3.1 %collective-permute-done.25 = f32[4,512]{1,0:T(4,128)S(1)} collective-permute-done((f32[4,512]{1,0:T(4,128)S(1)}, f32[4,512]{1,0:T(4,128)S(1)}, u32[]{:S(2)}, u32[]{:S(2)}) %collective-permute-start.25) | collective-permute-done | bytes 8224 | tf_op jit(solution)/shard_map/ppermute | solution.py:18
  211.2 0.8 fusion
  (40 shorter events, 4.2 us)
Async XLA Ops:
  0.6 49.0 %collective-permute-start = (bf16[2,2,512,512]{3,2,1,0:T(8,128)(2,1)}, bf16[2,2,512,512]{3,2,1,0:T(8,128)(2,1)}, u32[]{:S(2)}, u32[]{:S(2)}) collective-permute-start(bf16[2,2,512,512]{3,2,1,0:T(8,128)(2,1)} %bitcast.12), channel_id=1, source_target_pairs={{0,2},{2,0},{4,6},{6,4},{8,10},{10,8},{12,14},{14,12},{1,3},{3,1},... | collective-permute-start | bytes 6291464 | tf_op jit(solution)/shard_map/ppermute | solution.py:18
  3.6 47.4 %collective-permute-start.1 = (bf16[2,2,512,512]{3,2,1,0:T(8,128)(2,1)}, bf16[2,2,512,512]{3,2,1,0:T(8,128)(2,1)}, u32[]{:S(2)}, u32[]{:S(2)}) collective-permute-start(bf16[2,2,512,512]{3,2,1,0:T(8,128)(2,1)} %bitcast.13), channel_id=1, source_target_pairs={{0,4},{2,6},{4,0},{6,2},{8,12},{10,14},{12,8},{14,10},{1,5},{3,7},... | collective-permute-start | bytes 6291464 | tf_op jit(solution)/shard_map/ppermute | solution.py:18
  5.2 45.8 %collective-permute-start.2 = (bf16[2,2,512,512]{3,2,1,0:T(8,128)(2,1)}, bf16[2,2,512,512]{3,2,1,0:T(8,128)(2,1)}, u32[]{:S(2)}, u32[]{:S(2)}) collective-permute-start(bf16[2,2,512,512]{3,2,1,0:T(8,128)(2,1)} %bitcast.14), channel_id=1, source_target_pairs={{4,8},{6,10},{8,4},{10,6},{5,9},{7,11},{9,5},{11,7},{20,24},{22,26... | collective-permute-start | bytes 6291464 | tf_op jit(solution)/shard_map/ppermute | solution.py:23
  18.9 3.8 %copy-start.2 = (s32[2]{0:T(128)S(1)}, s32[2]{0:T(128)}, u32[]{:S(2)}) copy-start(s32[2]{0:T(128)} %constant.107.clone) | copy-start | bytes 28
  18.9 4.3 %copy-start.1 = (s32[3]{0:T(128)S(1)}, s32[3]{0:T(128)}, u32[]{:S(2)}) copy-start(s32[3]{0:T(128)} %constant.106.clone) | copy-start | bytes 40
  51.0 51.2 %collective-permute-start.3 = (bf16[2,2,512,512]{3,2,1,0:T(8,128)(2,1)}, bf16[2,2,512,512]{3,2,1,0:T(8,128)(2,1)}, u32[]{:S(2)}, u32[]{:S(2)}) collective-permute-start(bf16[2,2,512,512]{3,2,1,0:T(8,128)(2,1)} %collective-permute-done.2.refs_2_.m), channel_id=1, source_target_pairs={{4,0},{6,2},{8,12},{10,14},{5,1},{7,3},{9,13},{11,15},{20,16},{22,... | collective-permute-start | bytes 6291464 | tf_op jit(solution)/shard_map/ppermute | solution.py:23
  52.3 49.9 %collective-permute-start.4 = (bf16[2,2,512,512]{3,2,1,0:T(8,128)(2,1)}, bf16[2,2,512,512]{3,2,1,0:T(8,128)(2,1)}, u32[]{:S(2)}, u32[]{:S(2)}) collective-permute-start(bf16[2,2,512,512]{3,2,1,0:T(8,128)(2,1)} %collective-permute-done.1.refs_1_.n), channel_id=1, source_target_pairs={{4,8},{6,10},{8,4},{10,6},{5,9},{7,11},{9,5},{11,7},{20,24},{22,26... | collective-permute-start | bytes 6291464 | tf_op jit(solution)/shard_map/ppermute | solution.py:23
  54.3 47.9 %collective-permute-start.5 = (bf16[2,2,512,512]{3,2,1,0:T(8,128)(2,1)}, bf16[2,2,512,512]{3,2,1,0:T(8,128)(2,1)}, u32[]{:S(2)}, u32[]{:S(2)}) collective-permute-start(bf16[2,2,512,512]{3,2,1,0:T(8,128)(2,1)} %collective-permute-done.1.refs_1_.n), channel_id=1, source_target_pairs={{0,2},{2,0},{4,6},{6,4},{8,10},{10,8},{12,14},{14,12},{1,3},{3,1},... | collective-permute-start | bytes 6291464 | tf_op jit(solution)/shard_map/ppermute | solution.py:18
  54.7 52.9 %collective-permute-start.6 = (bf16[1,2,1024,512]{3,2,1,0:T(8,128)(2,1)}, bf16[1,2,1024,512]{3,2,1,0:T(8,128)(2,1)}, u32[]{:S(2)}, u32[]{:S(2)}) collective-permute-start(bf16[1,2,1024,512]{3,2,1,0:T(8,128)(2,1)} %shard_map.133), channel_id=1, source_target_pairs={{0,4},{2,6},{12,8},{14,10},{1,5},{3,7},{13,9},{15,11},{16,20},{18,... | collective-permute-start | bytes 6291464 | tf_op jit(solution)/shard_map/ppermute | solution.py:23
  107.6 33.6 %collective-permute-start.11 = (bf16[2,2,1024,512]{3,2,1,0:T(8,128)(2,1)}, bf16[2,2,1024,512]{3,2,1,0:T(8,128)(2,1)}, u32[]{:S(2)}, u32[]{:S(2)}) collective-permute-start(bf16[2,2,1024,512]{3,2,1,0:T(8,128)(2,1)} %shard_map.138.refs_0_.refs_2_.refs_12_), channel_id=1, source_target_pairs={{0,1},{1,0},{2,3},{3,2},{4,5},{5,4},{6,7},{7,6},{8,9},{9,8},{10,11... | collective-permute-start | bytes 12582920 | tf_op jit(solution)/shard_map/ppermute | solution.py:18
  109.8 26.0 %collective-permute-start.7 = (bf16[1,2,512,512]{3,2,1,0:T(8,128)(2,1)}, bf16[1,2,512,512]{3,2,1,0:T(8,128)(2,1)}, u32[]{:S(2)}, u32[]{:S(2)}) collective-permute-start(bf16[1,2,512,512]{3,2,1,0:T(8,128)(2,1)} %shard_map.139.refs_1_), channel_id=1, source_target_pairs={{0,2},{2,0},{4,6},{6,4},{8,10},{10,8},{12,14},{14,12},{1,3},{3,1},... | collective-permute-start | bytes 3145736 | tf_op jit(solution)/shard_map/ppermute | solution.py:18
  111.4 27.6 %collective-permute-start.8 = (bf16[1,2,512,512]{3,2,1,0:T(8,128)(2,1)}, bf16[1,2,512,512]{3,2,1,0:T(8,128)(2,1)}, u32[]{:S(2)}, u32[]{:S(2)}) collective-permute-start(bf16[1,2,512,512]{3,2,1,0:T(8,128)(2,1)} %shard_map.139.refs_1_), channel_id=1, source_target_pairs={{4,0},{6,2},{8,12},{10,14},{5,1},{7,3},{9,13},{11,15},{20,16},{22,... | collective-permute-start | bytes 3145736 | tf_op jit(solution)/shard_map/ppermute | solution.py:23
  112.7 28.5 %collective-permute-start.10 = (bf16[1,1,1024,512]{3,2,1,0:T(8,128)(2,1)}, bf16[1,1,1024,512]{3,2,1,0:T(8,128)(2,1)}, u32[]{:S(2)}, u32[]{:S(2)}) collective-permute-start(bf16[1,1,1024,512]{3,2,1,0:T(8,128)(2,1)} %shard_map.136), channel_id=1, source_target_pairs={{0,4},{2,6},{12,8},{14,10},{1,5},{3,7},{13,9},{15,11},{16,20},{18,... | collective-permute-start | bytes 3145736 | tf_op jit(solution)/shard_map/ppermute | solution.py:23
  119.2 21.9 %collective-permute-start.9 = (bf16[1,2,512,512]{3,2,1,0:T(8,128)(2,1)}, bf16[1,2,512,512]{3,2,1,0:T(8,128)(2,1)}, u32[]{:S(2)}, u32[]{:S(2)}) collective-permute-start(bf16[1,2,512,512]{3,2,1,0:T(8,128)(2,1)} %get-tuple-element.65), channel_id=1, source_target_pairs={{4,8},{6,10},{8,4},{10,6},{5,9},{7,11},{9,5},{11,7},{20,24},{22,26... | collective-permute-start | bytes 3145736 | tf_op jit(solution)/shard_map/ppermute | solution.py:23
  141.1 23.9 %collective-permute-start.16 = (bf16[2,2,512,512]{3,2,1,0:T(8,128)(2,1)}, bf16[2,2,512,512]{3,2,1,0:T(8,128)(2,1)}, u32[]{:S(2)}, u32[]{:S(2)}) collective-permute-start(bf16[2,2,512,512]{3,2,1,0:T(8,128)(2,1)} %shard_map.142.refs_1_.refs_2_.refs_3_.refs_13_), channel_id=1, source_target_pairs={{0,1},{1,0},{2,3},{3,2},{4,5},{5,4},{6,7},{7,6},{8,9},{9,8},{10,11... | collective-permute-start | bytes 6291464 | tf_op jit(solution)/shard_map/ppermute | solution.py:18
  141.1 35.6 %collective-permute-start.12 = (bf16[1,2,512,512]{3,2,1,0:T(8,128)(2,1)}, bf16[1,2,512,512]{3,2,1,0:T(8,128)(2,1)}, u32[]{:S(2)}, u32[]{:S(2)}) collective-permute-start(bf16[1,2,512,512]{3,2,1,0:T(8,128)(2,1)} %shard_map.141.refs_1_), channel_id=1, source_target_pairs={{0,2},{2,0},{4,6},{6,4},{8,10},{10,8},{12,14},{14,12},{1,3},{3,1},... | collective-permute-start | bytes 3145736 | tf_op jit(solution)/shard_map/ppermute | solution.py:18
  141.7 35.0 %collective-permute-start.13 = (bf16[1,2,512,512]{3,2,1,0:T(8,128)(2,1)}, bf16[1,2,512,512]{3,2,1,0:T(8,128)(2,1)}, u32[]{:S(2)}, u32[]{:S(2)}) collective-permute-start(bf16[1,2,512,512]{3,2,1,0:T(8,128)(2,1)} %shard_map.141.refs_1_), channel_id=1, source_target_pairs={{4,0},{6,2},{8,12},{10,14},{5,1},{7,3},{9,13},{11,15},{20,16},{22,... | collective-permute-start | bytes 3145736 | tf_op jit(solution)/shard_map/ppermute | solution.py:23
  143.0 33.7 %collective-permute-start.14 = (bf16[1,2,512,512]{3,2,1,0:T(8,128)(2,1)}, bf16[1,2,512,512]{3,2,1,0:T(8,128)(2,1)}, u32[]{:S(2)}, u32[]{:S(2)}) collective-permute-start(bf16[1,2,512,512]{3,2,1,0:T(8,128)(2,1)} %get-tuple-element.76), channel_id=1, source_target_pairs={{4,8},{6,10},{8,4},{10,6},{5,9},{7,11},{9,5},{11,7},{20,24},{22,26... | collective-permute-start | bytes 3145736 | tf_op jit(solution)/shard_map/ppermute | solution.py:23
  144.7 32.1 %collective-permute-start.15 = (bf16[1,1,1024,512]{3,2,1,0:T(8,128)(2,1)}, bf16[1,1,1024,512]{3,2,1,0:T(8,128)(2,1)}, u32[]{:S(2)}, u32[]{:S(2)}) collective-permute-start(bf16[1,1,1024,512]{3,2,1,0:T(8,128)(2,1)} %shard_map.137), channel_id=1, source_target_pairs={{0,4},{2,6},{12,8},{14,10},{1,5},{3,7},{13,9},{15,11},{16,20},{18,... | collective-permute-start | bytes 3145736 | tf_op jit(solution)/shard_map/ppermute | solution.py:23
  176.8 12.3 %collective-permute-start.17 = (bf16[1,2,512,512]{3,2,1,0:T(8,128)(2,1)}, bf16[1,2,512,512]{3,2,1,0:T(8,128)(2,1)}, u32[]{:S(2)}, u32[]{:S(2)}) collective-permute-start(bf16[1,2,512,512]{3,2,1,0:T(8,128)(2,1)} %shard_map.145.refs_4_.refs_5_), channel_id=1, source_target_pairs={{0,1},{1,0},{2,3},{3,2},{4,5},{5,4},{6,7},{7,6},{8,9},{9,8},{10,11... | collective-permute-start | bytes 3145736 | tf_op jit(solution)/shard_map/ppermute | solution.py:18
  176.9 12.3 %collective-permute-start.18 = (bf16[1,2,512,512]{3,2,1,0:T(8,128)(2,1)}, bf16[1,2,512,512]{3,2,1,0:T(8,128)(2,1)}, u32[]{:S(2)}, u32[]{:S(2)}) collective-permute-start(bf16[1,2,512,512]{3,2,1,0:T(8,128)(2,1)} %collective-permute-done.14.w7.refs_14_), channel_id=1, source_target_pairs={{0,1},{1,0},{2,3},{3,2},{4,5},{5,4},{6,7},{7,6},{8,9},{9,8},{10,11... | collective-permute-start | bytes 3145736 | tf_op jit(solution)/shard_map/ppermute | solution.py:18
  177.4 11.8 %collective-permute-start.19 = (bf16[1,2,512,512]{3,2,1,0:T(8,128)(2,1)}, bf16[1,2,512,512]{3,2,1,0:T(8,128)(2,1)}, u32[]{:S(2)}, u32[]{:S(2)}) collective-permute-start(bf16[1,2,512,512]{3,2,1,0:T(8,128)(2,1)} %collective-permute-done.12.w5.refs_15_), channel_id=1, source_target_pairs={{0,1},{1,0},{2,3},{3,2},{4,5},{5,4},{6,7},{7,6},{8,9},{9,8},{10,11... | collective-permute-start | bytes 3145736 | tf_op jit(solution)/shard_map/ppermute | solution.py:18
  189.2 22.1 %copy-start = (s32[16]{0:T(128)S(1)}, s32[16]{0:T(128)}, u32[]{:S(2)}) copy-start(s32[16]{0:T(128)} %param.14) | copy-start | bytes 196
  196.1 2.0 collective-permute-start.20
  196.5 3.9 %collective-permute-start.21 = (f32[4,512]{1,0:T(4,128)}, f32[4,512]{1,0:T(4,128)S(1)}, u32[]{:S(2)}, u32[]{:S(2)}) collective-permute-start(f32[4,512]{1,0:T(4,128)} %shard_map.147), channel_id=1, source_target_pairs={{0,2},{1,3},{2,0},{3,1},{4,6},{5,7},{6,4},{7,5},{8,10},{9,11},{10,... | collective-permute-start | bytes 24584 | tf_op jit(solution)/shard_map/ppermute | solution.py:18
  198.0 3.4 %collective-permute-start.22 = (f32[4,512]{1,0:T(4,128)}, f32[4,512]{1,0:T(4,128)S(1)}, u32[]{:S(2)}, u32[]{:S(2)}) collective-permute-start(f32[4,512]{1,0:T(4,128)} %shard_map.147), channel_id=1, source_target_pairs={{0,3},{1,2},{2,1},{3,0},{4,7},{5,6},{6,5},{7,4},{8,11},{9,10},{10,... | collective-permute-start | bytes 24584 | tf_op jit(solution)/shard_map/ppermute | solution.py:18
  202.1 4.4 %collective-permute-start.23 = (f32[4,512]{1,0:T(4,128)S(1)}, f32[4,512]{1,0:T(4,128)S(1)}, u32[]{:S(2)}, u32[]{:S(2)}) collective-permute-start(f32[4,512]{1,0:T(4,128)S(1)} %add_add_fusion.1), channel_id=1, source_target_pairs={{0,4},{1,5},{2,6},{3,7},{4,0},{5,1},{6,2},{7,3},{8,12},{9,13},{10,... | collective-permute-start | bytes 24584 | tf_op jit(solution)/shard_map/ppermute | solution.py:18
  202.7 4.6 %collective-permute-start.24 = (f32[4,512]{1,0:T(4,128)S(1)}, f32[4,512]{1,0:T(4,128)S(1)}, u32[]{:S(2)}, u32[]{:S(2)}) collective-permute-start(f32[4,512]{1,0:T(4,128)S(1)} %add_add_fusion.1), channel_id=1, source_target_pairs={{0,8},{1,9},{2,10},{3,11},{4,12},{5,13},{6,14},{7,15},{8,0},{9,1},... | collective-permute-start | bytes 24584 | tf_op jit(solution)/shard_map/ppermute | solution.py:18
  205.0 5.4 %collective-permute-start.25 = (f32[4,512]{1,0:T(4,128)S(1)}, f32[4,512]{1,0:T(4,128)S(1)}, u32[]{:S(2)}, u32[]{:S(2)}) collective-permute-start(f32[4,512]{1,0:T(4,128)S(1)} %add_add_fusion.1), channel_id=1, source_target_pairs={{0,12},{1,13},{2,14},{3,15},{4,8},{5,9},{6,10},{7,11},{8,4},{9,5},... | collective-permute-start | bytes 24584 | tf_op jit(solution)/shard_map/ppermute | solution.py:18

commit v9 on v8

--- a/solution.py
+++ b/solution.py
@@ -18,17 +18,11 @@
     return lax.ppermute(value, axis, [(source, source ^ mask) for source in range(size)])
 
 
-def swap_some(value, mask, wanted):
-    size = lax.axis_size("row")
-    return lax.ppermute(value, "row", [(k, k ^ mask) for k in range(size) if wanted(k)])
-
-
-def middle(index):
-    return (index // 2) % 4 in (1, 2)
-
-
-def end(index):
-    return not middle(index)
+def swap_middle(value):
+    axes = ("row", "col")
+    size = lax.axis_size("row") * lax.axis_size("col")
+    target = lambda k: k ^ 12 if (k // 4) % 4 in (1, 2) else k ^ 1
+    return lax.ppermute(value, axes, [(k, target(k)) for k in range(size)])
 
 
 def after(value, *others):
@@ -83,7 +77,7 @@
     ]
 
 
-def field_kernel(freq, count, has_total, ids, cross, *refs):
+def field_kernel(freq, count, has_total, gated, ids, cross, *refs):
     w_refs, refs = refs[:count], refs[count:]
     total, refs = (refs[0], refs[1:]) if has_total else (None, refs)
     out, left, right, l_sem, w_sem, field, tot, tot_sem = refs
@@ -123,6 +117,8 @@
     @pl.when(last)
     def _():
         value = dot(left[piece], right[piece, part])
+        if gated:
+            value = jnp.where(ids[count] == 1, value, 0.0)
         if count > 1:
             value += field[part]
         if has_total:
@@ -135,12 +131,12 @@
         out[0] = value
 
 
-def add_field(cross, freq, ids, pieces, total=None):
+def add_field(cross, freq, ids, pieces, total=None, gated=False):
     rows, (width, sources) = cross.shape[2], pieces[0].shape[2:]
     count, dtype = len(pieces), pieces[0].dtype
     has_total = total is not None
     return pl.pallas_call(
-        functools.partial(field_kernel, freq, count, has_total),
+        functools.partial(field_kernel, freq, count, has_total, gated),
         out_shape=jax.ShapeDtypeStruct((2, rows, sources), jnp.float32),
         grid_spec=pltpu.PrefetchScalarGridSpec(
             num_scalar_prefetch=1,
@@ -167,7 +163,7 @@
 def start_rows(freq, ids, base, refs, rows, sem):
     width = rows.shape[1] // 2
     views = []
-    for picked, *pieces in (refs[:4], refs[4:]):
+    for picked, *pieces in (refs[:5], refs[5:]):
         views += [picked.at[freq, :, pl.ds(slot * width, width)] for slot in range(2)]
         views += [at_freq(ref, freq) for ref in pieces]
     for slot in range(2):
@@ -192,7 +188,7 @@
 
 
 def late_kernel(freq, ids, cross, w5, w6, w7, block_re, block_im, total, *refs):
-    row_refs, refs = refs[:8], refs[8:]
+    row_refs, refs = refs[:10], refs[10:]
     sums, field_out, left, right, l_sem, w_sem, field, tot, sem, rows, row_sem = refs
     step, part = pl.program_id(0), pl.program_id(1)
     width = w5.shape[2]
@@ -204,11 +200,12 @@
     second = spectra_copies(freq, ids[1], cross, left.at[1], l_sem.at[1])
     third = [
         pltpu.make_async_copy(
-            ref.at[0, min(k, ref.shape[1] - 1)],
-            left.at[2, :, pl.ds(k * width, width)],
-            l_sem.at[2, k],
+            ref.at[min(k, ref.shape[0] - 1), half],
+            left.at[2, pl.ds(half * width, width), pl.ds(k * width, width)],
+            l_sem.at[2 + half, k],
         )
         for k, ref in enumerate((block_re, block_im))
+        for half in range(2)
     ]
     total_copy = pltpu.make_async_copy(total, tot, sem.at[0])
     out_copies = [
@@ -266,7 +263,7 @@
             field[k] = field[k] + tot[k] + dot(left[1], right[1, k])
             out_copies[k].start()
 
-    @pl.when(step == 2)
+    @pl.when((step == 2) & (ids[2] == 1))
     def _():
         sums[...] += fold(rows[part], dot(left[2], right[0, part]))
 
@@ -293,7 +290,7 @@
             scratch_shapes=[
                 pltpu.VMEM((3, rows, 2 * width), dtype),
                 pltpu.VMEM((2, 2, 2 * width, sources), dtype),
-                pltpu.SemaphoreType.DMA((3, 2)),
+                pltpu.SemaphoreType.DMA((4, 2)),
                 pltpu.SemaphoreType.DMA((2, 2)),
                 pltpu.VMEM((2, rows, sources), jnp.float32),
                 pltpu.VMEM((2, rows, sources), jnp.float32),
@@ -308,7 +305,7 @@
 
 
 def dot_kernel(ids, norms, *refs):
-    groups, (out, rows, row_sem, field, sem) = (refs[:10], refs[10:20]), refs[20:]
+    groups, (out, rows, row_sem, field, sem) = (refs[:12], refs[12:24]), refs[24:]
     width = rows.shape[2] // 2
     pairs = [(slot, part) for slot in range(2) for part in range(2)]
     copies = {}
@@ -341,7 +338,7 @@
         grid_spec=pltpu.PrefetchScalarGridSpec(
             num_scalar_prefetch=1,
             grid=(1,),
-            in_specs=[whole((2, sources))] + [ANYWHERE, whole((8, sources)), *[ANYWHERE] * 8] * 2,
+            in_specs=[whole((2, sources))] + [ANYWHERE, whole((8, sources)), *[ANYWHERE] * 10] * 2,
             out_specs=whole((4, sources)),
             scratch_shapes=[
                 pltpu.VMEM((2, 2, rows, sources), groups[0][2].dtype),
@@ -355,85 +352,102 @@
     )(ids, norms, *groups[0], *groups[1])
 
 
-def copy_call(kernel, ids, shape, dtype, args, copies):
+def copy_kernel(inputs, jobs, ids, *refs):
+    refs, (stage, in_sem, out_sem) = refs[:-3], refs[-3:]
+    sources, targets = refs[:inputs], refs[inputs:]
+    writes = [
+        pltpu.make_async_copy(stage.at[k], target(targets), out_sem.at[k])
+        for k, (_, target) in enumerate(jobs)
+    ]
+
+    def each(act):
+        for k, (options, _) in enumerate(jobs):
+            for value, source in options:
+
+                @pl.when(ids[0] == value)
+                def _(k=k, source=source):
+                    act(k, pltpu.make_async_copy(source(sources, ids), stage.at[k], in_sem.at[k]))
+
+    def pass_on(k, copy):
+        copy.wait()
+        writes[k].start()
+
+    def finish(k, copy):
+        writes[k].wait()
+
+    each(lambda k, copy: copy.start())
+    each(pass_on)
+    each(finish)
+
+
+def copies(ids, args, jobs, shapes, unit, dtype, alias=None):
     return pl.pallas_call(
-        kernel,
-        out_shape=jax.ShapeDtypeStruct(shape, dtype),
+        functools.partial(copy_kernel, len(args), jobs),
+        out_shape=[jax.ShapeDtypeStruct(shape, dtype) for shape in shapes],
         grid_spec=pltpu.PrefetchScalarGridSpec(
             num_scalar_prefetch=1,
             grid=(1,),
             in_specs=[ANYWHERE] * len(args),
-            out_specs=pl.BlockSpec(shape, lambda i, ids: (0,) * len(shape)),
-            scratch_shapes=[pltpu.SemaphoreType.DMA((copies,))],
+            out_specs=[ANYWHERE] * len(shapes),
+            scratch_shapes=[
+                pltpu.VMEM((len(jobs), *unit), dtype),
+                pltpu.SemaphoreType.DMA((len(jobs),)),
+                pltpu.SemaphoreType.DMA((len(jobs),)),
+            ],
         ),
+        input_output_aliases={} if alias is None else {1 + alias: 0},
         compiler_params=pltpu.CompilerParams(vmem_limit_bytes=VMEM_LIMIT),
         cost_estimate=HINT,
     )(ids, *args)
 
 
-def block_kernel(freq, first, ids, cross, out, sem):
-    width = out.shape[3]
-    columns = pl.ds(pl.multiple_of(ids[0] * width, width), width)
-    copies = [
-        pltpu.make_async_copy(cross.at[freq, first + k, :, columns], out.at[0, k], sem.at[k])
-        for k in range(out.shape[1])
-    ]
-    for copy in copies:
-        copy.start()
-    for copy in copies:
-        copy.wait()
-
-
-def take_block(cross, freq, parts, ids, width):
-    shape = (1, len(parts), cross.shape[2], width)
-    kernel = functools.partial(block_kernel, freq, parts[0])
-    return copy_call(kernel, ids, shape, cross.dtype, [cross], len(parts))
-
-
-def pair_kernel(ids, own, x, n, m, out, sem):
-    width = own.shape[2]
-    for pair in (0, 1):
-        copies = [
-            pltpu.make_async_copy(
-                ref.at[freq], out.at[freq, :, pl.ds(slot * width, width)], sem.at[2 * freq + slot]
-            )
-            for freq in range(out.shape[0])
-            for slot, ref in enumerate(((own, x), (n, m))[pair])
-        ]
-
-        @pl.when(ids[0] == pair)
-        def _(copies=copies):
-            for copy in copies:
-                copy.start()
-            for copy in copies:
-                copy.wait()
+def block_source(at, freq, part, half, width):
+    def source(refs, ids):
+        columns = pl.ds(pl.multiple_of(ids[1] * width, width), width)
+        return refs[at].at[freq, part, pl.ds(half * width, width), columns]
+
+    return source
+
+
+def entry(at, *index):
+    return lambda refs, ids=None: refs[at].at[index]
+
+
+def fill_block(ids, piece, cross):
+    _, _, width, sources = piece.shape
+    jobs = [
+        ([(0, block_source(1, 0, part, half, width))], entry(0, part, half))
+        for part in range(2)
+        for half in range(2)
+    ]
+    return copies(ids, [piece, cross], jobs, [piece.shape], (width, sources), piece.dtype, 0)[0]
 
 
 def take_pair(ids, own, x, n, m):
     freqs, _, width, sources = own.shape
+    jobs = [
+        (
+            [(0, entry(slot, freq, part)), (1, entry(2 + slot, freq, part))],
+            entry(0, freq, part, pl.ds(slot * width, width)),
+        )
+        for freq in range(freqs)
+        for part in range(2)
+        for slot in range(2)
+    ]
     shape = (freqs, 2, 2 * width, sources)
-    return copy_call(pair_kernel, ids, shape, own.dtype, [own, x, n, m], 2 * freqs)
-
-
-def either_kernel(freqs, ids, first, second, out, sem):
-    for k, ref in enumerate((first, second)):
-
-        @pl.when(ids[0] == k)
-        def _(ref=ref):
-            copies = [
-                pltpu.make_async_copy(at_freq(ref, freq), out.at[slot], sem.at[slot])
-                for slot, freq in enumerate(freqs)
-            ]
-            for copy in copies:
-                copy.start()
-            for copy in copies:
-                copy.wait()
-
-
-def take_either(freqs, ids, first, second):
-    shape = (len(freqs), *first.shape[1:])
-    kernel = functools.partial(either_kernel, freqs)
-    return copy_call(kernel, ids, shape, first.dtype, [first, second], len(freqs))
+    return copies(ids, [own, x, n, m], jobs, [shape], (width, sources), own.dtype)[0]
+
+
+def take_next(freq, ids, ends, middles, cross):
+    _, _, width, sources = ends.shape
+    jobs = []
+    for part in range(2):
+        block = block_source(2, 1, freq, part, width)
+        jobs.append(([(0, block), (1, entry(1, freq, part))], entry(1, 0, part)))
+        jobs.append(([(0, entry(0, freq, part)), (1, entry(1, freq, part))], entry(0, 0, part)))
+    shape = (1, 2, width, sources)
+    args = [ends, middles, cross]
+    return copies(ids, args, jobs, [shape, shape], (width, sources), ends.dtype)
 
 
 def sums_by_swaps(cross, replicas, norms):
@@ -453,8 +467,8 @@
     next_masks = ((2 * (me ^ 2) % per_half + slots) ^ me) & 3
     table = lambda masks: sum(
         jnp.where(masks == mask, place, 0)
-        for mask, place in enumerate((0, 1, 0, 2, 2, 4, 1, 3))
-    ) + jnp.where(holds, 0, 5)
+        for mask, place in enumerate((0, 1, 0, 2, 3, 5, 1, 4))
+    ) + jnp.where(holds, 0, 6)
     late_ids = jnp.concatenate(
         [
             ids(5),
@@ -465,70 +479,61 @@
         ]
     ).astype(jnp.int32)
     pair = flag(((me >> 1) ^ me) & 1 != 0)
-    numbers = [ids(1, 2, 6), ids(3, 4), ids(7), late_ids, pair, flag(mid)]
+    ids_a = jnp.concatenate([ids(1, 2, 6), flag(mid)])
+    ids_z = jnp.concatenate([flag(mid), ids(7)])
+    numbers = [ids_a, ids(3, 4), ids_z, late_ids, pair]
 
     own = replicas[:, :, 0]
     x = swap(own, "row", 1)
     n = swap(own, "row", 2)
-    m = swap_some(own, 6, middle)
+    m = swap_middle(own)
     a0 = add_field(cross, 0, ids(0), [own])
     a1 = add_field(cross, 1, ids(0), [own])
-    block_a = take_block(cross, 0, (0, 1), ids(7), width)
-    x, n, m, a0, a1, block_a, norms, *numbers = barrier(x, n, m, a0, a1, block_a, norms, *numbers)
-    ids_a, ids_b, ids_7, late_ids, pair, is_mid = numbers
-
-    g = swap_some(m, 2, middle)
-    m2 = swap_some(n, 6, middle)
+    x, n, m, a0, a1, norms, *numbers = barrier(x, n, m, a0, a1, norms, *numbers)
+    ids_a, ids_b, ids_z, late_ids, pair = numbers
+
+    m = fill_block(ids_z, m, cross)
+    z = swap(m, "row", 2)
+    m2 = swap_middle(n)
     xn = swap(n, "row", 1)
-    block_a = swap_some(block_a, 2, end)
-    a0 = add_field(cross, 0, ids_a, [x, n, m], a0)
-    a1 = add_field(cross, 1, ids_a, [x, n, m], a1)
-    block_re = take_block(cross, 1, (0,), ids_7, width)
-    block_im = take_block(cross, 1, (1,), ids_7, width)
+    a0 = add_field(cross, 0, ids_a, [x, n, m], a0, gated=True)
+    a1 = add_field(cross, 1, ids_a, [x, n, m], a1, gated=True)
     mine = take_pair(pair, own, x, n, m)
     x_a, x_b = x[0:1], x[1:2]
-    g, m2, xn, block_a, a0, a1, block_re, block_im, mine, x_a, x_b = barrier(
-        g, m2, xn, block_a, a0, a1, block_re, block_im, mine, x_a, x_b
-    )
-
-    w4_a = take_either((0,), is_mid, g, m2)
+    z, m2, xn, a0, a1, mine, x_a, x_b = barrier(z, m2, xn, a0, a1, mine, x_a, x_b)
+
+    w4_a, send_a = take_next(0, ids_z, z, m2, cross)
     x5_a = swap(w4_a, "row", 1)
-    w6_a = swap_some(w4_a, 2, middle)
-    w7_a = swap_some(x_a, 6, middle)
-    block_re = swap_some(block_re, 2, end)
+    z_a = swap(send_a, "row", 2)
+    w7_a = swap_middle(x_a)
     other = swap(mine, "col", 1)
     b0 = add_field(cross, 0, ids_b, [xn, w4_a], a0)
-    w4_b = take_either((1,), after(is_mid, b0), g, m2)
-    later = take_either((0, 1), after(pair, b0), m2, xn)
+    w4_b, send_b = take_next(1, after(ids_z, b0), z, m2, cross)
     b1 = add_field(cross, 1, ids_b, [xn, w4_b], a1)
-    x5_a, w6_a, w7_a, block_re, other, b0, w4_b, later, x_b, block_im = barrier(
-        x5_a, w6_a, w7_a, block_re, other, b0, w4_b, later, x_b, block_im
+    x5_a, z_a, w7_a, other, b0, w4_b, send_b, x_b, xn, m2 = barrier(
+        x5_a, z_a, w7_a, other, b0, w4_b, send_b, x_b, xn, m2
     )
 
     x5_b = swap(w4_b, "row", 1)
-    w6_b = swap_some(w4_b, 2, middle)
-    w7_b = swap_some(x_b, 6, middle)
-    block_im = swap_some(block_im, 2, end)
-    other_later = swap(later, "col", 1)
-    early = [mine, later, later, later, other, other_later, other_later, other_later]
-    sums_a, field_a = add_late(
-        cross, 0, late_ids, [x5_a, w6_a, w7_a], [block_a, block_a], b0, early
+    z_b = swap(send_b, "row", 2)
+    w7_b = swap_middle(x_b)
+    other_xn = swap(xn, "col", 1)
+    other_m2 = swap(m2, "col", 1)
+    early = [mine, xn, m2, xn, xn, other, other_xn, other_m2, other_xn, other_xn]
+    sums_a, field_a = add_late(cross, 0, late_ids, [x5_a, z_a, w7_a], [z, z], b0, early)
+    x5_b, z_b, w7_b, sums_a, field_a, b1, other_xn, other_m2, x5_a, w7_a = barrier(
+        x5_b, z_b, w7_b, sums_a, field_a, b1, other_xn, other_m2, x5_a, w7_a
     )
-    late_a = take_either((0,), pair, x5_a, w7_a)
-    x5_b, w6_b, w7_b, block_im, sums_a, field_a, b1, late_a, other_later = barrier(
-        x5_b, w6_b, w7_b, block_im, sums_a, field_a, b1, late_a, other_later
-    )
-
-    other_late_a = swap(late_a, "col", 1)
-    other_w7_b = swap(w7_b, "col", 1)
-    other_x5_b = swap(x5_b, "col", 1)
-    early[5:] = [other_later] * 3
-    sums_b, field_b = add_late(
-        cross, 1, late_ids, [x5_b, w6_b, w7_b], [block_re, block_im], b1, early
-    )
-    rows_a = [mine, later, late_a, late_a, other, other_later, other_late_a, other_late_a]
-    rows_b = [mine, later, w7_b, x5_b, other, other_later, other_w7_b, other_x5_b]
-    groups = [(field_a, sums_a, *rows_a), (field_b, sums_b, *rows_b)]
+
+    late = [w7_a, x5_a, w7_b, x5_b]
+    others = [swap(piece, "col", 1) for piece in late]
+    early = [mine, xn, m2, xn, xn, other, other_xn, other_m2, other_xn, other_xn]
+    sums_b, field_b = add_late(cross, 1, late_ids, [x5_b, z_b, w7_b], [z_a, z_b], b1, early)
+    here, there = [mine, xn, m2], [other, other_xn, other_m2]
+    groups = [
+        (field_a, sums_a, *here, *late[:2], *there, *others[:2]),
+        (field_b, sums_b, *here, *late[2:], *there, *others[2:]),
+    ]
     return dot_rows(late_ids, norms, groups)
 
 

time: 213 us -> 195 us (0.915)
  starting transfers between devices: 51.3 us -> 20.9 us
  waiting for transfers between devices: 42.9 us -> 66.5 us
  Pallas kernels: 107 us -> 96.6 us
    ppermute x10 -> x4, starting transfers between devices: 37.1 us -> 0.01 us  [swap_middle(): return lax.ppermute(value, axes, [(k, target(k)) for k in range(size)])]
    ppermute x16 -> x21, waiting for transfers between devices: 32.2 us -> 66.5 us  [swap(): lax.ppermute(value, axis, [(source, source ^ mask) for source in range(si...]
    ppermute x10 -> x4, waiting for transfers between devices: 10.7 us -> 0.01 us  [swap_middle(): return lax.ppermute(value, axes, [(k, target(k)) for k in range(size)])]
    pallas_call x14 -> x10, Pallas kernels: 76.9 us -> 68.6 us  [the longest x6 55.7 us: add_field(): pl.pallas_call(functools.partial(field_kernel, freq, count, has_total, ga...]
    ppermute x16 -> x21, starting transfers between devices: 14.2 us -> 20.9 us  [swap(): lax.ppermute(value, axis, [(source, source ^ mask) for source in range(si...]
    pallas_call x2, Pallas kernels: 23.4 us -> 21.1 us  [add_late(): pl.pallas_call(functools.partial(late_kernel, freq), out_shape=(jax.Shape...]
  transfers between devices with their start and end apart: 26 -> 25, of which waited for: 10 -> 11; matrix products, arithmetic and copies ran while one was open for 4% -> 4% of each run, Pallas kernels for 47% -> 44%
where the time goes in v9:
time: 195 us
  Pallas kernels  96.6 us (50%)
  waiting for transfers between devices  66.5 us (34%)
  starting transfers between devices  20.9 us (11%)
  other arithmetic  4.66 us (2%)
  local copies, waits for them, and re-layouts  4.36 us (2%)
    ppermute x21, waiting for transfers between devices, swap(): lax.ppermute(value, axis, [(source, source ^ mask) for source in range(si...  66.5 us
    pallas_call x6, Pallas kernels, add_field(): pl.pallas_call(functools.partial(field_kernel, freq, count, has_total, ga...  55.7 us
    pallas_call x2, Pallas kernels, add_late(): pl.pallas_call(functools.partial(late_kernel, freq), out_shape=(jax.Shape...  21.1 us
    ppermute x21, starting transfers between devices, swap(): lax.ppermute(value, axis, [(source, source ^ mask) for source in range(si...  20.9 us
    pallas_call x4, Pallas kernels, copies(): pl.pallas_call(functools.partial(copy_kernel, len(args), jobs), out_shape...  12.9 us
    pallas_call x1, Pallas kernels, dot_rows(): pl.pallas_call(dot_kernel, out_shape=jax.ShapeDtypeStruct((4, sources), j...  6.87 us
  transfers between devices with their start and end apart: 25, of which 11 were waited for; matrix products, arithmetic and copies ran while one was open for 4% of the time, Pallas kernels for 44%

profile of v9, /device:TPU:0, one launch (start us, length us, event | category | flops | bytes accessed | tf_op | source)
XLA Modules:
  0.0 194.8 jit_solution(3490450414870129192)
XLA Ops:
  0.6 3.0 %collective-permute-start = (bf16[2,2,512,512]{3,2,1,0:T(8,128)(2,1)}, bf16[2,2,512,512]{3,2,1,0:T(8,128)(2,1)}, u32[]{:S(2)}, u32[]{:S(2)}) collective-permute-start(bf16[2,2,512,512]{3,2,1,0:T(8,128)(2,1)} %bitcast.12), channel_id=1, source_target_pairs={{0,2},{2,0},{4,6},{6,4},{8,10},{10,8},{12,14},{14,12},{1,3},{3,1},... | collective-permute-start | bytes 6291464 | tf_op jit(solution)/shard_map/ppermute | solution.py:18
  3.6 1.6 collective-permute-start.1
  5.2 5.9 %shard_map.122.refs_3_ = f32[2,1024,512]{2,1,0:T(8,128)} custom-call(s32[1]{0:T(128)} %bitcast.1.ids, bf16[2,2,1024,4096]{3,2,1,0:T(8,128)(2,1)} %cross.15, bf16[2,2,512,512]{3,2,1,0:T(8,128)(2,1)} %bitcast.15), custom_call_target="tpu_custom_call" | custom-call | flops 1 | bytes 1 | tf_op jit(solution)/shard_map/pallas_call | solution.py:138
  11.1 5.8 %shard_map.123.refs_3_ = f32[2,1024,512]{2,1,0:T(8,128)} custom-call(s32[1]{0:T(128)} %bitcast.1.ids, bf16[2,2,1024,4096]{3,2,1,0:T(8,128)(2,1)} %cross.15, bf16[2,2,512,512]{3,2,1,0:T(8,128)(2,1)} %bitcast.16), custom_call_target="tpu_custom_call" | custom-call | flops 1 | bytes 1 | tf_op jit(solution)/shard_map/pallas_call | solution.py:138
  17.1 0.7 concatenate.11.ids
  17.7 0.6 pad_add_fusion.ids
  18.3 0.6 pad_add_fusion.1
  18.9 2.6 %multiply_reduce_fusion.norms = f32[2,512]{1,0:T(2,128)} fusion(bf16[2,2,1,512,512]{4,3,2,1,0:T(8,128)(2,1)} %param.12), kind=kLoop, calls=%fused_computation | loop fusion | flops 3144704 | bytes 2101248 | tf_op jit(solution)/shard_map/reduce_sum | solution.py:558
  21.5 28.0 %collective-permute-done.refs_0_.refs_1_ = bf16[2,2,512,512]{3,2,1,0:T(8,128)(2,1)} collective-permute-done((bf16[2,2,512,512]{3,2,1,0:T(8,128)(2,1)}, bf16[2,2,512,512]{3,2,1,0:T(8,128)(2,1)}, u32[]{:S(2)}, u32[]{:S(2)}) %collective-permute-start) | collective-permute-done | bytes 2097184 | tf_op jit(solution)/shard_map/ppermute | solution.py:18
  49.6 1.5 collective-permute-done.1.refs_1_.refs_2_
  51.0 3.1 %shard_map.124.refs_2_.refs_3_ = bf16[2,2,512,512]{3,2,1,0:T(8,128)(2,1)} custom-call(s32[2]{0:T(128)} %get-tuple-element.69.ids, bf16[2,2,512,512]{3,2,1,0:T(8,128)(2,1)} %collective-permute-done.2.refs_0_, bf16[2,2,1024,4096]{3,2,1,0:T(8,128)(2,1)} %cross.15), custom_call_target="tpu_custom_call", output_to_operand_aliasing={{}: (1, {})} | custom-call | flops 1 | bytes 1 | tf_op jit(solution)/shard_map/pallas_call | solution.py:384
  54.2 0.5 collective-permute-start.3
  54.6 0.5 collective-permute-start.5
  55.2 3.6 %shard_map.127.refs_0_.refs_2_.refs_14_ = bf16[2,2,1024,512]{3,2,1,0:T(8,128)(2,1)} custom-call(s32[1]{0:T(128)} %bitcast.4.ids, bf16[2,2,512,512]{3,2,1,0:T(8,128)(2,1)} %bitcast.17, bf16[2,2,512,512]{3,2,1,0:T(8,128)(2,1)} %collective-permute-done.refs_0_.refs_1_, bf16[2,2,512,512]{3,2,1,0:T(8,128)(2,1)} %collective-permute-done.1.refs_1_.refs_2_, ...), custom_call_target="tpu_custom_call" | custom-call | flops 1 | bytes 1 | tf_op jit(solution)/shard_map/pallas_call | solution.py:384
  58.8 12.4 %shard_map.126.refs_2_ = f32[2,1024,512]{2,1,0:T(8,128)} custom-call(s32[4]{0:T(128)} %pad_add_fusion.ids, bf16[2,2,1024,4096]{3,2,1,0:T(8,128)(2,1)} %cross.15, bf16[2,2,512,512]{3,2,1,0:T(8,128)(2,1)} %collective-permute-done.refs_0_.refs_1_, bf16[2,2,512,512]{3,2,1,0:T(8,128)(2,1)} %collective-permute-done.1.refs_1_.refs_2_, ...), custom_call_target="tpu_custom_call" | custom-call | flops 1 | bytes 1 | tf_op jit(solution)/shard_map/pallas_call | solution.py:138
  71.1 12.3 %shard_map.125.refs_2_ = f32[2,1024,512]{2,1,0:T(8,128)} custom-call(s32[4]{0:T(128)} %pad_add_fusion.ids, bf16[2,2,1024,4096]{3,2,1,0:T(8,128)(2,1)} %cross.15, bf16[2,2,512,512]{3,2,1,0:T(8,128)(2,1)} %collective-permute-done.refs_0_.refs_1_, bf16[2,2,512,512]{3,2,1,0:T(8,128)(2,1)} %collective-permute-done.1.refs_1_.refs_2_, ...), custom_call_target="tpu_custom_call" | custom-call | flops 1 | bytes 1 | tf_op jit(solution)/shard_map/pallas_call | solution.py:138
  83.5 3.0 %fusion.18 = (bf16[1,2,512,512]{3,2,1,0:T(8,128)(2,1)}, bf16[1,2,512,512]{3,2,1,0:T(8,128)(2,1)}) fusion(bf16[2,2,512,512]{3,2,1,0:T(8,128)(2,1)} %collective-permute-done.refs_0_.refs_1_), kind=kLoop, calls=%fused_computation.41 | loop fusion | bytes 4194304 | tf_op jit(solution)/shard_map/slice | solution.py:502
  86.5 14.3 %collective-permute-done.3.refs_0_.block_re.block_im = bf16[2,2,512,512]{3,2,1,0:T(8,128)(2,1)} collective-permute-done((bf16[2,2,512,512]{3,2,1,0:T(8,128)(2,1)}, bf16[2,2,512,512]{3,2,1,0:T(8,128)(2,1)}, u32[]{:S(2)}, u32[]{:S(2)}) %collective-permute-start.3) | collective-permute-done | bytes 2097184 | tf_op jit(solution)/shard_map/ppermute | solution.py:18
  100.7 2.3 %collective-permute-done.5.refs_0_.refs_1_.refs_3_.refs_4_.refs_15_ = bf16[2,2,512,512]{3,2,1,0:T(8,128)(2,1)} collective-permute-done((bf16[2,2,512,512]{3,2,1,0:T(8,128)(2,1)}, bf16[2,2,512,512]{3,2,1,0:T(8,128)(2,1)}, u32[]{:S(2)}, u32[]{:S(2)}) %collective-permute-start.5) | collective-permute-done | bytes 2097184 | tf_op jit(solution)/shard_map/ppermute | solution.py:18
  103.0 3.1 %shard_map.128 = (bf16[1,2,512,512]{3,2,1,0:T(8,128)(2,1)}, bf16[1,2,512,512]{3,2,1,0:T(8,128)(2,1)}) custom-call(s32[2]{0:T(128)} %get-tuple-element.69.ids, bf16[2,2,512,512]{3,2,1,0:T(8,128)(2,1)} %collective-permute-done.3.refs_0_.block_re.block_im, bf16[2,2,512,512]{3,2,1,0:T(8,128)(2,1)} %collective-permute-done.4.refs_1_.refs_2_.refs_4_.refs_16_, ...), custom_call_target="tpu_custom_call" | custom-call | flops 1 | bytes 1 | tf_op jit(solution)/shard_map/pallas_call | solution.py:384
  106.1 0.6 collective-permute-start.6
  106.7 2.4 %collective-permute-start.7 = (bf16[1,2,512,512]{3,2,1,0:T(8,128)(2,1)}, bf16[1,2,512,512]{3,2,1,0:T(8,128)(2,1)}, u32[]{:S(2)}, u32[]{:S(2)}) collective-permute-start(bf16[1,2,512,512]{3,2,1,0:T(8,128)(2,1)} %get-tuple-element.63), channel_id=1, source_target_pairs={{0,4},{2,6},{4,0},{6,2},{8,12},{10,14},{12,8},{14,10},{1,5},{3,7},... | collective-permute-start | bytes 3145736 | tf_op jit(solution)/shard_map/ppermute | solution.py:18
  109.1 9.8 %shard_map.129.total = f32[2,1024,512]{2,1,0:T(8,128)} custom-call(s32[2]{0:T(128)} %get-tuple-element.66.ids, bf16[2,2,1024,4096]{3,2,1,0:T(8,128)(2,1)} %cross.15, bf16[2,2,512,512]{3,2,1,0:T(8,128)(2,1)} %collective-permute-done.5.refs_0_.refs_1_.refs_3_.refs_4_.refs_15_, bf16[1,2,512,512]{3,2,1,0:T(8,128)(2,1)} %get-tuple-element.62.refs_1_, ...), custom_call_target="tpu_custom_call" | custom-call | flops 1 | bytes 1 | tf_op jit(solution)/shard_map/pallas_call | solution.py:138
  118.9 3.1 %shard_map.130 = (bf16[1,2,512,512]{3,2,1,0:T(8,128)(2,1)}, bf16[1,2,512,512]{3,2,1,0:T(8,128)(2,1)}) custom-call(s32[2]{0:T(128)} %get-tuple-element.69.ids, bf16[2,2,512,512]{3,2,1,0:T(8,128)(2,1)} %collective-permute-done.3.refs_0_.block_re.block_im, bf16[2,2,512,512]{3,2,1,0:T(8,128)(2,1)} %collective-permute-done.4.refs_1_.refs_2_.refs_4_.refs_16_, ...), custom_call_target="tpu_custom_call" | custom-call | flops 1 | bytes 1 | tf_op jit(solution)/shard_map/pallas_call | solution.py:384
  122.0 10.0 %collective-permute-done.6.w5.refs_6_ = bf16[1,2,512,512]{3,2,1,0:T(8,128)(2,1)} collective-permute-done((bf16[1,2,512,512]{3,2,1,0:T(8,128)(2,1)}, bf16[1,2,512,512]{3,2,1,0:T(8,128)(2,1)}, u32[]{:S(2)}, u32[]{:S(2)}) %collective-permute-start.6) | collective-permute-done | bytes 1048608 | tf_op jit(solution)/shard_map/ppermute | solution.py:18
  132.0 1.0 collective-permute-done.7.w6.block_re
  133.0 0.5 collective-permute-start.14
  133.5 1.4 collective-permute-start.10
  134.9 1.8 collective-permute-start.11
  136.7 9.6 %shard_map.132.total = f32[2,1024,512]{2,1,0:T(8,128)} custom-call(s32[2]{0:T(128)} %get-tuple-element.66.ids, bf16[2,2,1024,4096]{3,2,1,0:T(8,128)(2,1)} %cross.15, bf16[2,2,512,512]{3,2,1,0:T(8,128)(2,1)} %collective-permute-done.5.refs_0_.refs_1_.refs_3_.refs_4_.refs_15_, bf16[1,2,512,512]{3,2,1,0:T(8,128)(2,1)} %get-tuple-element.73.refs_1_, ...), custom_call_target="tpu_custom_call" | custom-call | flops 1 | bytes 1 | tf_op jit(solution)/shard_map/pallas_call | solution.py:138
  146.3 10.5 %shard_map.131 = (f32[8,512]{1,0:T(8,128)}, f32[2,1024,512]{2,1,0:T(8,128)}) custom-call(s32[7]{0:T(128)} %concatenate.11.ids, bf16[2,2,1024,4096]{3,2,1,0:T(8,128)(2,1)} %cross.15, bf16[1,2,512,512]{3,2,1,0:T(8,128)(2,1)} %collective-permute-done.6.w5.refs_6_, bf16[1,2,512,512]{3,2,1,0:T(8,128)(2,1)} %collective-permute-done.7.w6.block_re, ...), custom_call_target="tpu_custom_call" | custom-call | flops 1 | bytes 1 | tf_op jit(solution)/shard_map/pallas_call | solution.py:279
  156.8 2.2 %collective-permute-done.10.w5.refs_18_ = bf16[1,2,512,512]{3,2,1,0:T(8,128)(2,1)} collective-permute-done((bf16[1,2,512,512]{3,2,1,0:T(8,128)(2,1)}, bf16[1,2,512,512]{3,2,1,0:T(8,128)(2,1)}, u32[]{:S(2)}, u32[]{:S(2)}) %collective-permute-start.10) | collective-permute-done | bytes 1048608 | tf_op jit(solution)/shard_map/ppermute | solution.py:18
  159.0 1.1 collective-permute-done.11.w6.block_im
  160.1 0.5 collective-permute-start.16
  160.6 0.5 collective-permute-start.18
  161.1 10.6 %shard_map.133 = (f32[8,512]{1,0:T(8,128)}, f32[2,1024,512]{2,1,0:T(8,128)}) custom-call(s32[7]{0:T(128)} %concatenate.11.ids, bf16[2,2,1024,4096]{3,2,1,0:T(8,128)(2,1)} %cross.15, bf16[1,2,512,512]{3,2,1,0:T(8,128)(2,1)} %collective-permute-done.10.w5.refs_18_, bf16[1,2,512,512]{3,2,1,0:T(8,128)(2,1)} %collective-permute-done.11.w6.block_im, ...), custom_call_target="tpu_custom_call" | custom-call | flops 1 | bytes 1 | tf_op jit(solution)/shard_map/pallas_call | solution.py:279
  171.8 6.9 %shard_map.134 = f32[4,512]{1,0:T(4,128)} custom-call(s32[7]{0:T(128)} %concatenate.11.ids, f32[2,512]{1,0:T(2,128)} %multiply_reduce_fusion.norms, f32[2,1024,512]{2,1,0:T(8,128)} %get-tuple-element.86.refs_0_, f32[8,512]{1,0:T(8,128)} %get-tuple-element.87.refs_1_, bf16[2,2,1024,512]{3,2,1,0:T(8,128)(2,1)} %shard_map.127.refs_0_.refs_2_.refs_14_, ...), custom_call_target="tpu_custom_call" | custom-call | flops 1 | bytes 1 | tf_op jit(solution)/shard_map/pallas_call | solution.py:335
  178.8 0.7 collective-permute-start.20
  179.5 1.2 collective-permute-start.21
  180.7 2.1 %collective-permute-done.20 = f32[4,512]{1,0:T(4,128)S(1)} collective-permute-done((f32[4,512]{1,0:T(4,128)}, f32[4,512]{1,0:T(4,128)S(1)}, u32[]{:S(2)}, u32[]{:S(2)}) %collective-permute-start.20) | collective-permute-done | bytes 8224 | tf_op jit(solution)/shard_map/ppermute | solution.py:18
  182.8 0.7 add_add_fusion.1
  183.5 3.0 %collective-permute-start.22 = (f32[4,512]{1,0:T(4,128)S(1)}, f32[4,512]{1,0:T(4,128)S(1)}, u32[]{:S(2)}, u32[]{:S(2)}) collective-permute-start(f32[4,512]{1,0:T(4,128)S(1)} %add_add_fusion.1), channel_id=1, source_target_pairs={{0,4},{1,5},{2,6},{3,7},{4,0},{5,1},{6,2},{7,3},{8,12},{9,13},{10,... | collective-permute-start | bytes 24584 | tf_op jit(solution)/shard_map/ppermute | solution.py:18
  186.6 1.2 collective-permute-start.23
  187.8 1.4 collective-permute-start.24
  189.2 1.9 collective-permute-done.23
  191.1 2.1 %collective-permute-done.24 = f32[4,512]{1,0:T(4,128)S(1)} collective-permute-done((f32[4,512]{1,0:T(4,128)S(1)}, f32[4,512]{1,0:T(4,128)S(1)}, u32[]{:S(2)}, u32[]{:S(2)}) %collective-permute-start.24) | collective-permute-done | bytes 8224 | tf_op jit(solution)/shard_map/ppermute | solution.py:18
  193.4 0.6 constant_dynamic-slice_fusion
  194.0 0.8 fusion
  (35 shorter events, 0.4 us)
Async XLA Ops:
  0.6 49.0 %collective-permute-start = (bf16[2,2,512,512]{3,2,1,0:T(8,128)(2,1)}, bf16[2,2,512,512]{3,2,1,0:T(8,128)(2,1)}, u32[]{:S(2)}, u32[]{:S(2)}) collective-permute-start(bf16[2,2,512,512]{3,2,1,0:T(8,128)(2,1)} %bitcast.12), channel_id=1, source_target_pairs={{0,2},{2,0},{4,6},{6,4},{8,10},{10,8},{12,14},{14,12},{1,3},{3,1},... | collective-permute-start | bytes 6291464 | tf_op jit(solution)/shard_map/ppermute | solution.py:18
  3.6 47.4 %collective-permute-start.1 = (bf16[2,2,512,512]{3,2,1,0:T(8,128)(2,1)}, bf16[2,2,512,512]{3,2,1,0:T(8,128)(2,1)}, u32[]{:S(2)}, u32[]{:S(2)}) collective-permute-start(bf16[2,2,512,512]{3,2,1,0:T(8,128)(2,1)} %bitcast.13), channel_id=1, source_target_pairs={{0,4},{2,6},{4,0},{6,2},{8,12},{10,14},{12,8},{14,10},{1,5},{3,7},... | collective-permute-start | bytes 6291464 | tf_op jit(solution)/shard_map/ppermute | solution.py:18
  5.2 45.8 %collective-permute-start.2 = (bf16[2,2,512,512]{3,2,1,0:T(8,128)(2,1)}, bf16[2,2,512,512]{3,2,1,0:T(8,128)(2,1)}, u32[]{:S(2)}, u32[]{:S(2)}) collective-permute-start(bf16[2,2,512,512]{3,2,1,0:T(8,128)(2,1)} %bitcast.14), channel_id=1, source_target_pairs={{0,1},{1,0},{2,3},{3,2},{4,8},{5,9},{6,10},{7,11},{8,4},{9,5},{10,... | collective-permute-start | bytes 6291464 | tf_op jit(solution)/shard_map/ppermute | solution.py:25
  11.1 6.6 %copy-start.2 = (s32[3]{0:T(128)S(1)}, s32[3]{0:T(128)}, u32[]{:S(2)}) copy-start(s32[3]{0:T(128)} %constant.107.clone) | copy-start | bytes 40
  11.1 7.2 %copy-start = (s32[2]{0:T(128)S(1)}, s32[2]{0:T(128)}, u32[]{:S(2)}) copy-start(s32[2]{0:T(128)} %constant.108.clone) | copy-start | bytes 28
  54.2 46.6 %collective-permute-start.3 = (bf16[2,2,512,512]{3,2,1,0:T(8,128)(2,1)}, bf16[2,2,512,512]{3,2,1,0:T(8,128)(2,1)}, u32[]{:S(2)}, u32[]{:S(2)}) collective-permute-start(bf16[2,2,512,512]{3,2,1,0:T(8,128)(2,1)} %shard_map.124.refs_2_.refs_3_), channel_id=1, source_target_pairs={{0,4},{2,6},{4,0},{6,2},{8,12},{10,14},{12,8},{14,10},{1,5},{3,7},... | collective-permute-start | bytes 6291464 | tf_op jit(solution)/shard_map/ppermute | solution.py:18
  54.6 46.1 %collective-permute-start.4 = (bf16[2,2,512,512]{3,2,1,0:T(8,128)(2,1)}, bf16[2,2,512,512]{3,2,1,0:T(8,128)(2,1)}, u32[]{:S(2)}, u32[]{:S(2)}) collective-permute-start(bf16[2,2,512,512]{3,2,1,0:T(8,128)(2,1)} %collective-permute-done.1.refs_1_.refs_2_), channel_id=1, source_target_pairs={{0,1},{1,0},{2,3},{3,2},{4,8},{5,9},{6,10},{7,11},{8,4},{9,5},{10,... | collective-permute-start | bytes 6291464 | tf_op jit(solution)/shard_map/ppermute | solution.py:25
  54.6 48.4 %collective-permute-start.5 = (bf16[2,2,512,512]{3,2,1,0:T(8,128)(2,1)}, bf16[2,2,512,512]{3,2,1,0:T(8,128)(2,1)}, u32[]{:S(2)}, u32[]{:S(2)}) collective-permute-start(bf16[2,2,512,512]{3,2,1,0:T(8,128)(2,1)} %collective-permute-done.1.refs_1_.refs_2_), channel_id=1, source_target_pairs={{0,2},{2,0},{4,6},{6,4},{8,10},{10,8},{12,14},{14,12},{1,3},{3,1},... | collective-permute-start | bytes 6291464 | tf_op jit(solution)/shard_map/ppermute | solution.py:18
  103.0 30.0 %collective-permute-start.9 = (bf16[2,2,1024,512]{3,2,1,0:T(8,128)(2,1)}, bf16[2,2,1024,512]{3,2,1,0:T(8,128)(2,1)}, u32[]{:S(2)}, u32[]{:S(2)}) collective-permute-start(bf16[2,2,1024,512]{3,2,1,0:T(8,128)(2,1)} %shard_map.127.refs_0_.refs_2_.refs_14_), channel_id=1, source_target_pairs={{0,1},{1,0},{2,3},{3,2},{4,5},{5,4},{6,7},{7,6},{8,9},{9,8},{10,11... | collective-permute-start | bytes 12582920 | tf_op jit(solution)/shard_map/ppermute | solution.py:18
  106.1 26.0 %collective-permute-start.6 = (bf16[1,2,512,512]{3,2,1,0:T(8,128)(2,1)}, bf16[1,2,512,512]{3,2,1,0:T(8,128)(2,1)}, u32[]{:S(2)}, u32[]{:S(2)}) collective-permute-start(bf16[1,2,512,512]{3,2,1,0:T(8,128)(2,1)} %get-tuple-element.62.refs_1_), channel_id=1, source_target_pairs={{0,2},{2,0},{4,6},{6,4},{8,10},{10,8},{12,14},{14,12},{1,3},{3,1},... | collective-permute-start | bytes 3145736 | tf_op jit(solution)/shard_map/ppermute | solution.py:18
  106.7 26.3 %collective-permute-start.7 = (bf16[1,2,512,512]{3,2,1,0:T(8,128)(2,1)}, bf16[1,2,512,512]{3,2,1,0:T(8,128)(2,1)}, u32[]{:S(2)}, u32[]{:S(2)}) collective-permute-start(bf16[1,2,512,512]{3,2,1,0:T(8,128)(2,1)} %get-tuple-element.63), channel_id=1, source_target_pairs={{0,4},{2,6},{4,0},{6,2},{8,12},{10,14},{12,8},{14,10},{1,5},{3,7},... | collective-permute-start | bytes 3145736 | tf_op jit(solution)/shard_map/ppermute | solution.py:18
  109.1 23.9 %collective-permute-start.8 = (bf16[1,2,512,512]{3,2,1,0:T(8,128)(2,1)}, bf16[1,2,512,512]{3,2,1,0:T(8,128)(2,1)}, u32[]{:S(2)}, u32[]{:S(2)}) collective-permute-start(bf16[1,2,512,512]{3,2,1,0:T(8,128)(2,1)} %get-tuple-element.64), channel_id=1, source_target_pairs={{0,1},{1,0},{2,3},{3,2},{4,8},{5,9},{6,10},{7,11},{8,4},{9,5},{10,... | collective-permute-start | bytes 3145736 | tf_op jit(solution)/shard_map/ppermute | solution.py:25
  133.0 13.3 %collective-permute-start.13 = (bf16[2,2,512,512]{3,2,1,0:T(8,128)(2,1)}, bf16[2,2,512,512]{3,2,1,0:T(8,128)(2,1)}, u32[]{:S(2)}, u32[]{:S(2)}) collective-permute-start(bf16[2,2,512,512]{3,2,1,0:T(8,128)(2,1)} %collective-permute-done.5.refs_0_.refs_1_.refs_3_.refs_4_.refs_15_), channel_id=1, source_target_pairs={{0,1},{1,0},{2,3},{3,2},{4,5},{5,4},{6,7},{7,6},{8,9},{9,8},{10,11... | collective-permute-start | bytes 6291464 | tf_op jit(solution)/shard_map/ppermute | solution.py:18
  133.0 13.3 %collective-permute-start.14 = (bf16[2,2,512,512]{3,2,1,0:T(8,128)(2,1)}, bf16[2,2,512,512]{3,2,1,0:T(8,128)(2,1)}, u32[]{:S(2)}, u32[]{:S(2)}) collective-permute-start(bf16[2,2,512,512]{3,2,1,0:T(8,128)(2,1)} %collective-permute-done.4.refs_1_.refs_2_.refs_4_.refs_16_), channel_id=1, source_target_pairs={{0,1},{1,0},{2,3},{3,2},{4,5},{5,4},{6,7},{7,6},{8,9},{9,8},{10,11... | collective-permute-start | bytes 6291464 | tf_op jit(solution)/shard_map/ppermute | solution.py:18
  133.5 25.5 %collective-permute-start.10 = (bf16[1,2,512,512]{3,2,1,0:T(8,128)(2,1)}, bf16[1,2,512,512]{3,2,1,0:T(8,128)(2,1)}, u32[]{:S(2)}, u32[]{:S(2)}) collective-permute-start(bf16[1,2,512,512]{3,2,1,0:T(8,128)(2,1)} %get-tuple-element.73.refs_1_), channel_id=1, source_target_pairs={{0,2},{2,0},{4,6},{6,4},{8,10},{10,8},{12,14},{14,12},{1,3},{3,1},... | collective-permute-start | bytes 3145736 | tf_op jit(solution)/shard_map/ppermute | solution.py:18
  134.9 25.2 %collective-permute-start.11 = (bf16[1,2,512,512]{3,2,1,0:T(8,128)(2,1)}, bf16[1,2,512,512]{3,2,1,0:T(8,128)(2,1)}, u32[]{:S(2)}, u32[]{:S(2)}) collective-permute-start(bf16[1,2,512,512]{3,2,1,0:T(8,128)(2,1)} %get-tuple-element.74), channel_id=1, source_target_pairs={{0,4},{2,6},{4,0},{6,2},{8,12},{10,14},{12,8},{14,10},{1,5},{3,7},... | collective-permute-start | bytes 3145736 | tf_op jit(solution)/shard_map/ppermute | solution.py:18
  136.7 23.4 %collective-permute-start.12 = (bf16[1,2,512,512]{3,2,1,0:T(8,128)(2,1)}, bf16[1,2,512,512]{3,2,1,0:T(8,128)(2,1)}, u32[]{:S(2)}, u32[]{:S(2)}) collective-permute-start(bf16[1,2,512,512]{3,2,1,0:T(8,128)(2,1)} %get-tuple-element.75), channel_id=1, source_target_pairs={{0,1},{1,0},{2,3},{3,2},{4,8},{5,9},{6,10},{7,11},{8,4},{9,5},{10,... | collective-permute-start | bytes 3145736 | tf_op jit(solution)/shard_map/ppermute | solution.py:25
  160.1 11.7 %collective-permute-start.15 = (bf16[1,2,512,512]{3,2,1,0:T(8,128)(2,1)}, bf16[1,2,512,512]{3,2,1,0:T(8,128)(2,1)}, u32[]{:S(2)}, u32[]{:S(2)}) collective-permute-start(bf16[1,2,512,512]{3,2,1,0:T(8,128)(2,1)} %collective-permute-done.8.w7.refs_5_), channel_id=1, source_target_pairs={{0,1},{1,0},{2,3},{3,2},{4,5},{5,4},{6,7},{7,6},{8,9},{9,8},{10,11... | collective-permute-start | bytes 3145736 | tf_op jit(solution)/shard_map/ppermute | solution.py:18
  160.1 11.7 %collective-permute-start.16 = (bf16[1,2,512,512]{3,2,1,0:T(8,128)(2,1)}, bf16[1,2,512,512]{3,2,1,0:T(8,128)(2,1)}, u32[]{:S(2)}, u32[]{:S(2)}) collective-permute-start(bf16[1,2,512,512]{3,2,1,0:T(8,128)(2,1)} %collective-permute-done.6.w5.refs_6_), channel_id=1, source_target_pairs={{0,1},{1,0},{2,3},{3,2},{4,5},{5,4},{6,7},{7,6},{8,9},{9,8},{10,11... | collective-permute-start | bytes 3145736 | tf_op jit(solution)/shard_map/ppermute | solution.py:18
  160.6 11.2 %collective-permute-start.17 = (bf16[1,2,512,512]{3,2,1,0:T(8,128)(2,1)}, bf16[1,2,512,512]{3,2,1,0:T(8,128)(2,1)}, u32[]{:S(2)}, u32[]{:S(2)}) collective-permute-start(bf16[1,2,512,512]{3,2,1,0:T(8,128)(2,1)} %collective-permute-done.12.w7.refs_17_), channel_id=1, source_target_pairs={{0,1},{1,0},{2,3},{3,2},{4,5},{5,4},{6,7},{7,6},{8,9},{9,8},{10,11... | collective-permute-start | bytes 3145736 | tf_op jit(solution)/shard_map/ppermute | solution.py:18
  160.6 11.2 %collective-permute-start.18 = (bf16[1,2,512,512]{3,2,1,0:T(8,128)(2,1)}, bf16[1,2,512,512]{3,2,1,0:T(8,128)(2,1)}, u32[]{:S(2)}, u32[]{:S(2)}) collective-permute-start(bf16[1,2,512,512]{3,2,1,0:T(8,128)(2,1)} %collective-permute-done.10.w5.refs_18_), channel_id=1, source_target_pairs={{0,1},{1,0},{2,3},{3,2},{4,5},{5,4},{6,7},{7,6},{8,9},{9,8},{10,11... | collective-permute-start | bytes 3145736 | tf_op jit(solution)/shard_map/ppermute | solution.py:18
  171.8 22.2 %copy-start.1 = (s32[16]{0:T(128)S(1)}, s32[16]{0:T(128)}, u32[]{:S(2)}) copy-start(s32[16]{0:T(128)} %param.13) | copy-start | bytes 196
  178.7 1.9 collective-permute-start.19
  178.8 4.0 %collective-permute-start.20 = (f32[4,512]{1,0:T(4,128)}, f32[4,512]{1,0:T(4,128)S(1)}, u32[]{:S(2)}, u32[]{:S(2)}) collective-permute-start(f32[4,512]{1,0:T(4,128)} %shard_map.134), channel_id=1, source_target_pairs={{0,2},{1,3},{2,0},{3,1},{4,6},{5,7},{6,4},{7,5},{8,10},{9,11},{10,... | collective-permute-start | bytes 24584 | tf_op jit(solution)/shard_map/ppermute | solution.py:18
  179.5 3.4 %collective-permute-start.21 = (f32[4,512]{1,0:T(4,128)}, f32[4,512]{1,0:T(4,128)S(1)}, u32[]{:S(2)}, u32[]{:S(2)}) collective-permute-start(f32[4,512]{1,0:T(4,128)} %shard_map.134), channel_id=1, source_target_pairs={{0,3},{1,2},{2,1},{3,0},{4,7},{5,6},{6,5},{7,4},{8,11},{9,10},{10,... | collective-permute-start | bytes 24584 | tf_op jit(solution)/shard_map/ppermute | solution.py:18
  183.5 5.7 %collective-permute-start.22 = (f32[4,512]{1,0:T(4,128)S(1)}, f32[4,512]{1,0:T(4,128)S(1)}, u32[]{:S(2)}, u32[]{:S(2)}) collective-permute-start(f32[4,512]{1,0:T(4,128)S(1)} %add_add_fusion.1), channel_id=1, source_target_pairs={{0,4},{1,5},{2,6},{3,7},{4,0},{5,1},{6,2},{7,3},{8,12},{9,13},{10,... | collective-permute-start | bytes 24584 | tf_op jit(solution)/shard_map/ppermute | solution.py:18
  186.6 4.5 %collective-permute-start.23 = (f32[4,512]{1,0:T(4,128)S(1)}, f32[4,512]{1,0:T(4,128)S(1)}, u32[]{:S(2)}, u32[]{:S(2)}) collective-permute-start(f32[4,512]{1,0:T(4,128)S(1)} %add_add_fusion.1), channel_id=1, source_target_pairs={{0,8},{1,9},{2,10},{3,11},{4,12},{5,13},{6,14},{7,15},{8,0},{9,1},... | collective-permute-start | bytes 24584 | tf_op jit(solution)/shard_map/ppermute | solution.py:18
  187.8 5.4 %collective-permute-start.24 = (f32[4,512]{1,0:T(4,128)S(1)}, f32[4,512]{1,0:T(4,128)S(1)}, u32[]{:S(2)}, u32[]{:S(2)}) collective-permute-start(f32[4,512]{1,0:T(4,128)S(1)} %add_add_fusion.1), channel_id=1, source_target_pairs={{0,12},{1,13},{2,14},{3,15},{4,8},{5,9},{6,10},{7,11},{8,4},{9,5},... | collective-permute-start | bytes 24584 | tf_op jit(solution)/shard_map/ppermute | solution.py:18

commit v10 on v9

--- a/solution.py
+++ b/solution.py
@@ -190,6 +190,7 @@
 def late_kernel(freq, ids, cross, w5, w6, w7, block_re, block_im, total, *refs):
     row_refs, refs = refs[:10], refs[10:]
     sums, field_out, left, right, l_sem, w_sem, field, tot, sem, rows, row_sem = refs
+    late = ids[7]
     step, part = pl.program_id(0), pl.program_id(1)
     width = w5.shape[2]
     first = weight_copies(freq, w5, right.at[0], w_sem.at[0]) + spectra_copies(
@@ -208,8 +209,10 @@
         for half in range(2)
     ]
     total_copy = pltpu.make_async_copy(total, tot, sem.at[0])
+    late_rows = pl.ds(pl.multiple_of(jnp.minimum(late, 1) * width, width), width)
     out_copies = [
-        pltpu.make_async_copy(field.at[k], field_out.at[k], sem.at[1 + k]) for k in range(2)
+        pltpu.make_async_copy(field.at[k, late_rows], field_out.at[k], sem.at[1 + k])
+        for k in range(2)
     ]
 
     @pl.when((step == 0) & (part == 0))
@@ -233,6 +236,7 @@
                 copy.start()
 
         total_copy.start()
+        start_rows(freq, ids, 3, row_refs, rows.at[0], row_sem.at[0])
         spread(right.at[0])
 
     @pl.when((step == 1) & (part == 0))
@@ -241,8 +245,10 @@
             copy.wait()
         for copy in third:
             copy.start()
-        start_rows(freq, ids, 5, row_refs, rows, row_sem)
+        start_rows(freq, ids, 5, row_refs, rows.at[1], row_sem.at[1])
         total_copy.wait()
+        for slot in range(2):
+            wait_rows(freq, slot, row_refs, rows.at[0], row_sem.at[0])
         spread(right.at[1])
 
     @pl.when((step == 2) & (part == 0))
@@ -250,7 +256,7 @@
         for copy in third:
             copy.wait()
         for slot in range(2):
-            wait_rows(freq, slot, row_refs, rows, row_sem)
+            wait_rows(freq, slot, row_refs, rows.at[1], row_sem.at[1])
 
     @pl.when(step == 0)
     def _():
@@ -262,10 +268,16 @@
         def _(k=k):
             field[k] = field[k] + tot[k] + dot(left[1], right[1, k])
             out_copies[k].start()
+            for slot in range(2):
+
+                @pl.when(late != slot)
+                def _(slot=slot):
+                    here = slice(slot * width, (slot + 1) * width)
+                    sums[...] += fold(rows[0, k, here], field[k, here])
 
     @pl.when((step == 2) & (ids[2] == 1))
     def _():
-        sums[...] += fold(rows[part], dot(left[2], right[0, part]))
+        sums[...] += fold(rows[1, part], dot(left[2], right[0, part]))
 
     @pl.when((step == 2) & (part == 1))
     def _():
@@ -280,7 +292,7 @@
         functools.partial(late_kernel, freq),
         out_shape=(
             jax.ShapeDtypeStruct((8, sources), jnp.float32),
-            jax.ShapeDtypeStruct(total.shape, total.dtype),
+            jax.ShapeDtypeStruct((2, width, sources), jnp.float32),
         ),
         grid_spec=pltpu.PrefetchScalarGridSpec(
             num_scalar_prefetch=1,
@@ -295,8 +307,8 @@
                 pltpu.VMEM((2, rows, sources), jnp.float32),
                 pltpu.VMEM((2, rows, sources), jnp.float32),
                 pltpu.SemaphoreType.DMA((3,)),
-                pltpu.VMEM((2, rows, sources), dtype),
-                pltpu.SemaphoreType.DMA((2,)),
+                pltpu.VMEM((2, 2, rows, sources), dtype),
+                pltpu.SemaphoreType.DMA((2, 2)),
             ],
         ),
         compiler_params=pltpu.CompilerParams(vmem_limit_bytes=VMEM_LIMIT),
@@ -305,32 +317,35 @@
 
 
 def dot_kernel(ids, norms, *refs):
-    groups, (out, rows, row_sem, field, sem) = (refs[:12], refs[12:24]), refs[24:]
-    width = rows.shape[2] // 2
-    pairs = [(slot, part) for slot in range(2) for part in range(2)]
-    copies = {}
-    for freq, (field_ref, _, *row_refs) in enumerate(groups):
-        start_rows(freq, ids, 3, row_refs, rows.at[freq], row_sem.at[freq])
-        for slot, part in pairs:
-            here = pl.ds(slot * width, width)
-            copies[freq, slot, part] = pltpu.make_async_copy(
-                field_ref.at[part, here], field.at[freq, part, here], sem.at[freq, 2 * slot + part]
-            )
-            copies[freq, slot, part].start()
-    for freq, (_, sums_ref, *row_refs) in enumerate(groups):
-        sums = sums_ref[...]
-        for slot, part in pairs:
-            if part == 0:
-                wait_rows(freq, slot, row_refs, rows.at[freq], row_sem.at[freq])
-            copies[freq, slot, part].wait()
-            here = slice(slot * width, (slot + 1) * width)
-            sums += fold(rows[freq, part, here], field[freq, part, here])
-        out[freq : freq + 1] = jnp.sum(sums, axis=0, keepdims=True)
+    groups, (out, rows, field, sem) = (refs[:6], refs[6:12]), refs[12:]
+    for freq, (field_ref, _, *sources) in enumerate(groups):
+
+        @pl.when(ids[0] < 4)
+        def _(freq=freq, field_ref=field_ref):
+            pltpu.make_async_copy(field_ref, field.at[freq], sem.at[0, freq]).start()
+
+        for k, source in enumerate(sources):
+
+            @pl.when(ids[0] == k)
+            def _(freq=freq, source=source):
+                pltpu.make_async_copy(source.at[0], rows.at[freq], sem.at[1, freq]).start()
+
+    for freq, (field_ref, sums, *sources) in enumerate(groups):
+        out[freq : freq + 1] = jnp.sum(sums[...], axis=0, keepdims=True)
+
+        @pl.when(ids[0] < 4)
+        def _(freq=freq, field_ref=field_ref, sources=sources):
+            pltpu.make_async_copy(field_ref, field.at[freq], sem.at[0, freq]).wait()
+            pltpu.make_async_copy(sources[0].at[0], rows.at[freq], sem.at[1, freq]).wait()
+            more = sum(fold(rows[freq, part], field[freq, part]) for part in range(2))
+            out[freq : freq + 1] += jnp.sum(more, axis=0, keepdims=True)
+
     out[2:4] = norms[...]
 
 
 def dot_rows(ids, norms, groups):
-    _, rows, sources = groups[0][0].shape
+    late_shape, dtype = groups[0][0].shape, groups[0][2].dtype
+    sources = late_shape[-1]
     whole = lambda shape: pl.BlockSpec(shape, lambda i, ids: (0, 0))
     return pl.pallas_call(
         dot_kernel,
@@ -338,13 +353,12 @@
         grid_spec=pltpu.PrefetchScalarGridSpec(
             num_scalar_prefetch=1,
             grid=(1,),
-            in_specs=[whole((2, sources))] + [ANYWHERE, whole((8, sources)), *[ANYWHERE] * 10] * 2,
+            in_specs=[whole((2, sources))] + [ANYWHERE, whole((8, sources)), *[ANYWHERE] * 4] * 2,
             out_specs=whole((4, sources)),
             scratch_shapes=[
-                pltpu.VMEM((2, 2, rows, sources), groups[0][2].dtype),
+                pltpu.VMEM((2, *late_shape), dtype),
+                pltpu.VMEM((2, *late_shape), jnp.float32),
                 pltpu.SemaphoreType.DMA((2, 2)),
-                pltpu.VMEM((2, 2, rows, sources), jnp.float32),
-                pltpu.SemaphoreType.DMA((2, 4)),
             ],
         ),
         compiler_params=pltpu.CompilerParams(vmem_limit_bytes=VMEM_LIMIT),
@@ -469,6 +483,9 @@
         jnp.where(masks == mask, place, 0)
         for mask, place in enumerate((0, 1, 0, 2, 3, 5, 1, 4))
     ) + jnp.where(holds, 0, 6)
+    late_slot = own_masks[0] & 1 ^ 1
+    late_source = jnp.where(own_masks[0] & 2 != 0, 0, 1) + jnp.where(holds, 0, 2)
+    ids_dot = jnp.where(mid, late_source, 4).astype(jnp.int32).reshape(1)
     late_ids = jnp.concatenate(
         [
             ids(5),
@@ -476,12 +493,13 @@
             flag(mid),
             table(own_masks),
             table(next_masks),
+            jnp.where(mid, late_slot, 2).reshape(1),
         ]
     ).astype(jnp.int32)
     pair = flag(((me >> 1) ^ me) & 1 != 0)
     ids_a = jnp.concatenate([ids(1, 2, 6), flag(mid)])
     ids_z = jnp.concatenate([flag(mid), ids(7)])
-    numbers = [ids_a, ids(3, 4), ids_z, late_ids, pair]
+    numbers = [ids_a, ids(3, 4), ids_z, late_ids, pair, ids_dot]
 
     own = replicas[:, :, 0]
     x = swap(own, "row", 1)
@@ -489,10 +507,10 @@
     m = swap_middle(own)
     a0 = add_field(cross, 0, ids(0), [own])
     a1 = add_field(cross, 1, ids(0), [own])
+    m = fill_block(ids_z, m, cross)
     x, n, m, a0, a1, norms, *numbers = barrier(x, n, m, a0, a1, norms, *numbers)
-    ids_a, ids_b, ids_z, late_ids, pair = numbers
-
-    m = fill_block(ids_z, m, cross)
+    ids_a, ids_b, ids_z, late_ids, pair, ids_dot = numbers
+
     z = swap(m, "row", 2)
     m2 = swap_middle(n)
     xn = swap(n, "row", 1)
@@ -529,12 +547,11 @@
     others = [swap(piece, "col", 1) for piece in late]
     early = [mine, xn, m2, xn, xn, other, other_xn, other_m2, other_xn, other_xn]
     sums_b, field_b = add_late(cross, 1, late_ids, [x5_b, z_b, w7_b], [z_a, z_b], b1, early)
-    here, there = [mine, xn, m2], [other, other_xn, other_m2]
     groups = [
-        (field_a, sums_a, *here, *late[:2], *there, *others[:2]),
-        (field_b, sums_b, *here, *late[2:], *there, *others[2:]),
-    ]
-    return dot_rows(late_ids, norms, groups)
+        (field_a, sums_a, *late[:2], *others[:2]),
+        (field_b, sums_b, *late[2:], *others[2:]),
+    ]
+    return dot_rows(ids_dot, norms, groups)
 
 
 def sums_by_gather(cross, replicas, norms):

time: 195 us -> 192 us (0.985)
  starting transfers between devices: 20.9 us -> 26 us
  waiting for transfers between devices: 66.5 us -> 61.7 us
  Pallas kernels: 96.6 us -> 92.4 us
    pallas_call x1, Pallas kernels: 6.87 us -> 1.41 us  [dot_rows(): pl.pallas_call(dot_kernel, out_shape=jax.ShapeDtypeStruct((4, sources), j...]
    ppermute x21, waiting for transfers between devices: 66.5 us -> 61.7 us  [swap(): lax.ppermute(value, axis, [(source, source ^ mask) for source in range(si...]
    ppermute x21, starting transfers between devices: 20.9 us -> 25 us  [swap(): lax.ppermute(value, axis, [(source, source ^ mask) for source in range(si...]
  transfers between devices with their start and end apart: 25 -> 25, of which waited for: 11 -> 12; matrix products, arithmetic and copies ran while one was open for 4% -> 4% of each run, Pallas kernels for 44% -> 48%
where the time goes in v10:
time: 192 us
  Pallas kernels  92.4 us (48%)
  waiting for transfers between devices  61.7 us (32%)
  starting transfers between devices  26 us (14%)
  other arithmetic  5.14 us (3%)
  local copies, waits for them, and re-layouts  4.38 us (2%)
    ppermute x21, waiting for transfers between devices, swap(): lax.ppermute(value, axis, [(source, source ^ mask) for source in range(si...  61.7 us
    pallas_call x6, Pallas kernels, add_field(): pl.pallas_call(functools.partial(field_kernel, freq, count, has_total, ga...  55.7 us
    ppermute x21, starting transfers between devices, swap(): lax.ppermute(value, axis, [(source, source ^ mask) for source in range(si...  25 us
    pallas_call x2, Pallas kernels, add_late(): pl.pallas_call(functools.partial(late_kernel, freq), out_shape=(jax.Shape...  22.3 us
    pallas_call x4, Pallas kernels, copies(): pl.pallas_call(functools.partial(copy_kernel, len(args), jobs), out_shape...  12.9 us
  transfers between devices with their start and end apart: 25, of which 12 were waited for; matrix products, arithmetic and copies ran while one was open for 4% of the time, Pallas kernels for 48%

profile of v10, /device:TPU:0, one launch (start us, length us, event | category | flops | bytes accessed | tf_op | source)
XLA Modules:
  0.0 191.5 jit_solution(15211356593971867065)
XLA Ops:
  0.6 0.5 collective-permute-start.2
  1.1 4.1 %collective-permute-start.1 = (bf16[2,2,512,512]{3,2,1,0:T(8,128)(2,1)}, bf16[2,2,512,512]{3,2,1,0:T(8,128)(2,1)}, u32[]{:S(2)}, u32[]{:S(2)}) collective-permute-start(bf16[2,2,512,512]{3,2,1,0:T(8,128)(2,1)} %bitcast.18), channel_id=1, source_target_pairs={{0,4},{2,6},{4,0},{6,2},{8,12},{10,14},{12,8},{14,10},{1,5},{3,7},... | collective-permute-start | bytes 6291464 | tf_op jit(solution)/shard_map/ppermute | solution.py:18
  5.3 1.5 collective-permute-start
  6.8 5.8 %shard_map.124.refs_3_ = f32[2,1024,512]{2,1,0:T(8,128)} custom-call(s32[1]{0:T(128)} %bitcast.2.ids, bf16[2,2,1024,4096]{3,2,1,0:T(8,128)(2,1)} %cross.15, bf16[2,2,512,512]{3,2,1,0:T(8,128)(2,1)} %bitcast.20), custom_call_target="tpu_custom_call" | custom-call | flops 1 | bytes 1 | tf_op jit(solution)/shard_map/pallas_call | solution.py:138
  12.6 5.9 %shard_map.123.refs_3_ = f32[2,1024,512]{2,1,0:T(8,128)} custom-call(s32[1]{0:T(128)} %bitcast.2.ids, bf16[2,2,1024,4096]{3,2,1,0:T(8,128)(2,1)} %cross.15, bf16[2,2,512,512]{3,2,1,0:T(8,128)(2,1)} %bitcast.21), custom_call_target="tpu_custom_call" | custom-call | flops 1 | bytes 1 | tf_op jit(solution)/shard_map/pallas_call | solution.py:138
  18.7 0.5 fusion.16
  19.2 0.7 concatenate.11.ids
  19.9 0.6 pad_add_fusion.ids
  20.5 0.6 pad_add_fusion.1.ids
  21.1 2.6 %multiply_reduce_fusion.norms = f32[2,512]{1,0:T(2,128)} fusion(bf16[2,2,1,512,512]{4,3,2,1,0:T(8,128)(2,1)} %param.12), kind=kLoop, calls=%fused_computation | loop fusion | flops 3144704 | bytes 2101248 | tf_op jit(solution)/shard_map/reduce_sum | solution.py:575
  23.7 3.1 %shard_map.122.refs_2_.refs_3_ = bf16[2,2,512,512]{3,2,1,0:T(8,128)(2,1)} custom-call(s32[2]{0:T(128)} %pad_add_fusion.ids, bf16[2,2,512,512]{3,2,1,0:T(8,128)(2,1)} %collective-permute-done.2.refs_0_, bf16[2,2,1024,4096]{3,2,1,0:T(8,128)(2,1)} %cross.15), custom_call_target="tpu_custom_call", output_to_operand_aliasing={{}: (1, {})} | custom-call | flops 1 | bytes 1 | tf_op jit(solution)/shard_map/pallas_call | solution.py:398
  26.8 24.2 %collective-permute-done.1.refs_1_.refs_2_ = bf16[2,2,512,512]{3,2,1,0:T(8,128)(2,1)} collective-permute-done((bf16[2,2,512,512]{3,2,1,0:T(8,128)(2,1)}, bf16[2,2,512,512]{3,2,1,0:T(8,128)(2,1)}, u32[]{:S(2)}, u32[]{:S(2)}) %collective-permute-start.1) | collective-permute-done | bytes 2097184 | tf_op jit(solution)/shard_map/ppermute | solution.py:18
  51.0 1.4 collective-permute-done.refs_0_.refs_1_
  52.7 1.5 collective-permute-start.5
  54.2 12.3 %shard_map.125.refs_2_ = f32[2,1024,512]{2,1,0:T(8,128)} custom-call(s32[4]{0:T(128)} %pad_add_fusion.1.ids, bf16[2,2,1024,4096]{3,2,1,0:T(8,128)(2,1)} %cross.15, bf16[2,2,512,512]{3,2,1,0:T(8,128)(2,1)} %collective-permute-done.refs_0_.refs_1_, bf16[2,2,512,512]{3,2,1,0:T(8,128)(2,1)} %collective-permute-done.1.refs_1_.refs_2_, ...), custom_call_target="tpu_custom_call" | custom-call | flops 1 | bytes 1 | tf_op jit(solution)/shard_map/pallas_call | solution.py:138
  66.5 12.4 %shard_map.126.refs_2_ = f32[2,1024,512]{2,1,0:T(8,128)} custom-call(s32[4]{0:T(128)} %pad_add_fusion.1.ids, bf16[2,2,1024,4096]{3,2,1,0:T(8,128)(2,1)} %cross.15, bf16[2,2,512,512]{3,2,1,0:T(8,128)(2,1)} %collective-permute-done.refs_0_.refs_1_, bf16[2,2,512,512]{3,2,1,0:T(8,128)(2,1)} %collective-permute-done.1.refs_1_.refs_2_, ...), custom_call_target="tpu_custom_call" | custom-call | flops 1 | bytes 1 | tf_op jit(solution)/shard_map/pallas_call | solution.py:138
  78.9 3.6 %shard_map.127.refs_0_ = bf16[2,2,1024,512]{3,2,1,0:T(8,128)(2,1)} custom-call(s32[1]{0:T(128)} %bitcast.6.ids, bf16[2,2,512,512]{3,2,1,0:T(8,128)(2,1)} %bitcast.22, bf16[2,2,512,512]{3,2,1,0:T(8,128)(2,1)} %collective-permute-done.refs_0_.refs_1_, bf16[2,2,512,512]{3,2,1,0:T(8,128)(2,1)} %collective-permute-done.1.refs_1_.refs_2_, ...), custom_call_target="tpu_custom_call" | custom-call | flops 1 | bytes 1 | tf_op jit(solution)/shard_map/pallas_call | solution.py:398
  82.5 3.0 %fusion.18 = (bf16[1,2,512,512]{3,2,1,0:T(8,128)(2,1)}, bf16[1,2,512,512]{3,2,1,0:T(8,128)(2,1)}) fusion(bf16[2,2,512,512]{3,2,1,0:T(8,128)(2,1)} %collective-permute-done.refs_0_.refs_1_), kind=kLoop, calls=%fused_computation.42 | loop fusion | bytes 4194304 | tf_op jit(solution)/shard_map/slice | solution.py:520
  85.6 13.1 %collective-permute-done.3.refs_0_.block_re.block_im = bf16[2,2,512,512]{3,2,1,0:T(8,128)(2,1)} collective-permute-done((bf16[2,2,512,512]{3,2,1,0:T(8,128)(2,1)}, bf16[2,2,512,512]{3,2,1,0:T(8,128)(2,1)}, u32[]{:S(2)}, u32[]{:S(2)}) %collective-permute-start.3) | collective-permute-done | bytes 2097184 | tf_op jit(solution)/shard_map/ppermute | solution.py:18
  98.9 0.5 collective-permute-start.8
  99.4 3.1 %shard_map.128 = (bf16[1,2,512,512]{3,2,1,0:T(8,128)(2,1)}, bf16[1,2,512,512]{3,2,1,0:T(8,128)(2,1)}) custom-call(s32[2]{0:T(128)} %pad_add_fusion.ids, bf16[2,2,512,512]{3,2,1,0:T(8,128)(2,1)} %collective-permute-done.3.refs_0_.block_re.block_im, bf16[2,2,512,512]{3,2,1,0:T(8,128)(2,1)} %collective-permute-done.4.refs_1_.refs_2_, ...), custom_call_target="tpu_custom_call" | custom-call | flops 1 | bytes 1 | tf_op jit(solution)/shard_map/pallas_call | solution.py:398
  102.6 4.8 %collective-permute-start.7 = (bf16[1,2,512,512]{3,2,1,0:T(8,128)(2,1)}, bf16[1,2,512,512]{3,2,1,0:T(8,128)(2,1)}, u32[]{:S(2)}, u32[]{:S(2)}) collective-permute-start(bf16[1,2,512,512]{3,2,1,0:T(8,128)(2,1)} %get-tuple-element.64), channel_id=1, source_target_pairs={{0,4},{2,6},{4,0},{6,2},{8,12},{10,14},{12,8},{14,10},{1,5},{3,7},... | collective-permute-start | bytes 3145736 | tf_op jit(solution)/shard_map/ppermute | solution.py:18
  107.3 0.5 collective-permute-start.6
  107.9 9.8 %shard_map.129.total = f32[2,1024,512]{2,1,0:T(8,128)} custom-call(s32[2]{0:T(128)} %get-tuple-element.67.ids, bf16[2,2,1024,4096]{3,2,1,0:T(8,128)(2,1)} %cross.15, bf16[2,2,512,512]{3,2,1,0:T(8,128)(2,1)} %collective-permute-done.5.refs_0_.refs_1_.refs_3_.refs_4_, bf16[1,2,512,512]{3,2,1,0:T(8,128)(2,1)} %get-tuple-element.63.refs_1_, ...), custom_call_target="tpu_custom_call" | custom-call | flops 1 | bytes 1 | tf_op jit(solution)/shard_map/pallas_call | solution.py:138
  117.6 3.1 %shard_map.130 = (bf16[1,2,512,512]{3,2,1,0:T(8,128)(2,1)}, bf16[1,2,512,512]{3,2,1,0:T(8,128)(2,1)}) custom-call(s32[2]{0:T(128)} %pad_add_fusion.ids, bf16[2,2,512,512]{3,2,1,0:T(8,128)(2,1)} %collective-permute-done.3.refs_0_.block_re.block_im, bf16[2,2,512,512]{3,2,1,0:T(8,128)(2,1)} %collective-permute-done.4.refs_1_.refs_2_, ...), custom_call_target="tpu_custom_call" | custom-call | flops 1 | bytes 1 | tf_op jit(solution)/shard_map/pallas_call | solution.py:398
  120.7 10.5 %collective-permute-done.7.w6.block_re = bf16[1,2,512,512]{3,2,1,0:T(8,128)(2,1)} collective-permute-done((bf16[1,2,512,512]{3,2,1,0:T(8,128)(2,1)}, bf16[1,2,512,512]{3,2,1,0:T(8,128)(2,1)}, u32[]{:S(2)}, u32[]{:S(2)}) %collective-permute-start.7) | collective-permute-done | bytes 1048608 | tf_op jit(solution)/shard_map/ppermute | solution.py:18
  131.2 1.5 collective-permute-done.6.w5.refs_3_
  132.7 0.5 collective-permute-start.14
  133.2 0.5 collective-permute-start.10
  133.7 0.4 collective-permute-start.11
  134.1 9.6 %shard_map.132.total = f32[2,1024,512]{2,1,0:T(8,128)} custom-call(s32[2]{0:T(128)} %get-tuple-element.67.ids, bf16[2,2,1024,4096]{3,2,1,0:T(8,128)(2,1)} %cross.15, bf16[2,2,512,512]{3,2,1,0:T(8,128)(2,1)} %collective-permute-done.5.refs_0_.refs_1_.refs_3_.refs_4_, bf16[1,2,512,512]{3,2,1,0:T(8,128)(2,1)} %get-tuple-element.74.refs_1_, ...), custom_call_target="tpu_custom_call" | custom-call | flops 1 | bytes 1 | tf_op jit(solution)/shard_map/pallas_call | solution.py:138
  143.7 11.0 %shard_map.131 = (f32[8,512]{1,0:T(8,128)}, f32[2,512,512]{2,1,0:T(8,128)}) custom-call(s32[8]{0:T(128)} %concatenate.11.ids, bf16[2,2,1024,4096]{3,2,1,0:T(8,128)(2,1)} %cross.15, bf16[1,2,512,512]{3,2,1,0:T(8,128)(2,1)} %collective-permute-done.6.w5.refs_3_, bf16[1,2,512,512]{3,2,1,0:T(8,128)(2,1)} %collective-permute-done.7.w6.block_re, ...), custom_call_target="tpu_custom_call" | custom-call | flops 1 | bytes 1 | tf_op jit(solution)/shard_map/pallas_call | solution.py:291
  154.8 3.8 %collective-permute-done.10.w5.refs_9_ = bf16[1,2,512,512]{3,2,1,0:T(8,128)(2,1)} collective-permute-done((bf16[1,2,512,512]{3,2,1,0:T(8,128)(2,1)}, bf16[1,2,512,512]{3,2,1,0:T(8,128)(2,1)}, u32[]{:S(2)}, u32[]{:S(2)}) %collective-permute-start.10) | collective-permute-done | bytes 1048608 | tf_op jit(solution)/shard_map/ppermute | solution.py:18
  158.8 0.5 collective-permute-start.16
  159.3 0.5 collective-permute-start.17
  159.9 11.2 %shard_map.133 = (f32[8,512]{1,0:T(8,128)}, f32[2,512,512]{2,1,0:T(8,128)}) custom-call(s32[8]{0:T(128)} %concatenate.11.ids, bf16[2,2,1024,4096]{3,2,1,0:T(8,128)(2,1)} %cross.15, bf16[1,2,512,512]{3,2,1,0:T(8,128)(2,1)} %collective-permute-done.10.w5.refs_9_, bf16[1,2,512,512]{3,2,1,0:T(8,128)(2,1)} %collective-permute-done.11.w6.block_im, ...), custom_call_target="tpu_custom_call" | custom-call | flops 1 | bytes 1 | tf_op jit(solution)/shard_map/pallas_call | solution.py:291
  171.2 1.4 shard_map.134
  172.6 1.2 collective-permute-start.21
  173.7 0.5 collective-permute-start.20
  174.5 1.4 collective-permute-done.21
  175.9 1.7 collective-permute-done.20
  177.6 0.7 add_add_fusion.1
  178.3 1.2 collective-permute-start.24
  179.5 6.7 %collective-permute-start.23 = (f32[4,512]{1,0:T(4,128)S(1)}, f32[4,512]{1,0:T(4,128)S(1)}, u32[]{:S(2)}, u32[]{:S(2)}) collective-permute-start(f32[4,512]{1,0:T(4,128)S(1)} %add_add_fusion.1), channel_id=1, source_target_pairs={{0,8},{1,9},{2,10},{3,11},{4,12},{5,13},{6,14},{7,15},{8,0},{9,1},... | collective-permute-start | bytes 24584 | tf_op jit(solution)/shard_map/ppermute | solution.py:18
  186.2 1.7 collective-permute-done.23
  188.0 1.9 %collective-permute-done.22 = f32[4,512]{1,0:T(4,128)S(1)} collective-permute-done((f32[4,512]{1,0:T(4,128)S(1)}, f32[4,512]{1,0:T(4,128)S(1)}, u32[]{:S(2)}, u32[]{:S(2)}) %collective-permute-start.22) | collective-permute-done | bytes 8224 | tf_op jit(solution)/shard_map/ppermute | solution.py:18
  190.1 0.6 constant_dynamic-slice_fusion
  190.7 0.8 fusion
  (36 shorter events, 1.4 us)
Async XLA Ops:
  0.6 23.1 %collective-permute-start.2 = (bf16[2,2,512,512]{3,2,1,0:T(8,128)(2,1)}, bf16[2,2,512,512]{3,2,1,0:T(8,128)(2,1)}, u32[]{:S(2)}, u32[]{:S(2)}) collective-permute-start(bf16[2,2,512,512]{3,2,1,0:T(8,128)(2,1)} %bitcast.17), channel_id=1, source_target_pairs={{0,1},{1,0},{2,3},{3,2},{4,8},{5,9},{6,10},{7,11},{8,4},{9,5},{10,... | collective-permute-start | bytes 6291464 | tf_op jit(solution)/shard_map/ppermute | solution.py:25
  1.1 49.8 %collective-permute-start.1 = (bf16[2,2,512,512]{3,2,1,0:T(8,128)(2,1)}, bf16[2,2,512,512]{3,2,1,0:T(8,128)(2,1)}, u32[]{:S(2)}, u32[]{:S(2)}) collective-permute-start(bf16[2,2,512,512]{3,2,1,0:T(8,128)(2,1)} %bitcast.18), channel_id=1, source_target_pairs={{0,4},{2,6},{4,0},{6,2},{8,12},{10,14},{12,8},{14,10},{1,5},{3,7},... | collective-permute-start | bytes 6291464 | tf_op jit(solution)/shard_map/ppermute | solution.py:18
  5.3 47.1 %collective-permute-start = (bf16[2,2,512,512]{3,2,1,0:T(8,128)(2,1)}, bf16[2,2,512,512]{3,2,1,0:T(8,128)(2,1)}, u32[]{:S(2)}, u32[]{:S(2)}) collective-permute-start(bf16[2,2,512,512]{3,2,1,0:T(8,128)(2,1)} %bitcast.19), channel_id=1, source_target_pairs={{0,2},{2,0},{4,6},{6,4},{8,10},{10,8},{12,14},{14,12},{1,3},{3,1},... | collective-permute-start | bytes 6291464 | tf_op jit(solution)/shard_map/ppermute | solution.py:18
  12.6 6.1 %copy-start = (s32[2]{0:T(128)S(1)}, s32[2]{0:T(128)}, u32[]{:S(2)}) copy-start(s32[2]{0:T(128)} %constant.117.clone) | copy-start | bytes 28
  12.6 7.9 %copy-start.2 = (s32[3]{0:T(128)S(1)}, s32[3]{0:T(128)}, u32[]{:S(2)}) copy-start(s32[3]{0:T(128)} %constant.116.clone) | copy-start | bytes 40
  52.4 46.2 %collective-permute-start.3 = (bf16[2,2,512,512]{3,2,1,0:T(8,128)(2,1)}, bf16[2,2,512,512]{3,2,1,0:T(8,128)(2,1)}, u32[]{:S(2)}, u32[]{:S(2)}) collective-permute-start(bf16[2,2,512,512]{3,2,1,0:T(8,128)(2,1)} %shard_map.122.refs_2_.refs_3_), channel_id=1, source_target_pairs={{0,4},{2,6},{4,0},{6,2},{8,12},{10,14},{12,8},{14,10},{1,5},{3,7},... | collective-permute-start | bytes 6291464 | tf_op jit(solution)/shard_map/ppermute | solution.py:18
  52.7 46.2 %collective-permute-start.5 = (bf16[2,2,512,512]{3,2,1,0:T(8,128)(2,1)}, bf16[2,2,512,512]{3,2,1,0:T(8,128)(2,1)}, u32[]{:S(2)}, u32[]{:S(2)}) collective-permute-start(bf16[2,2,512,512]{3,2,1,0:T(8,128)(2,1)} %collective-permute-done.1.refs_1_.refs_2_), channel_id=1, source_target_pairs={{0,2},{2,0},{4,6},{6,4},{8,10},{10,8},{12,14},{14,12},{1,3},{3,1},... | collective-permute-start | bytes 6291464 | tf_op jit(solution)/shard_map/ppermute | solution.py:18
  54.2 44.7 %collective-permute-start.4 = (bf16[2,2,512,512]{3,2,1,0:T(8,128)(2,1)}, bf16[2,2,512,512]{3,2,1,0:T(8,128)(2,1)}, u32[]{:S(2)}, u32[]{:S(2)}) collective-permute-start(bf16[2,2,512,512]{3,2,1,0:T(8,128)(2,1)} %collective-permute-done.1.refs_1_.refs_2_), channel_id=1, source_target_pairs={{0,1},{1,0},{2,3},{3,2},{4,8},{5,9},{6,10},{7,11},{8,4},{9,5},{10,... | collective-permute-start | bytes 6291464 | tf_op jit(solution)/shard_map/ppermute | solution.py:25
  98.9 33.7 %collective-permute-start.9 = (bf16[2,2,1024,512]{3,2,1,0:T(8,128)(2,1)}, bf16[2,2,1024,512]{3,2,1,0:T(8,128)(2,1)}, u32[]{:S(2)}, u32[]{:S(2)}) collective-permute-start(bf16[2,2,1024,512]{3,2,1,0:T(8,128)(2,1)} %shard_map.127.refs_0_), channel_id=1, source_target_pairs={{0,1},{1,0},{2,3},{3,2},{4,5},{5,4},{6,7},{7,6},{8,9},{9,8},{10,11... | collective-permute-start | bytes 12582920 | tf_op jit(solution)/shard_map/ppermute | solution.py:18
  98.9 21.8 %collective-permute-start.8 = (bf16[1,2,512,512]{3,2,1,0:T(8,128)(2,1)}, bf16[1,2,512,512]{3,2,1,0:T(8,128)(2,1)}, u32[]{:S(2)}, u32[]{:S(2)}) collective-permute-start(bf16[1,2,512,512]{3,2,1,0:T(8,128)(2,1)} %get-tuple-element.65), channel_id=1, source_target_pairs={{0,1},{1,0},{2,3},{3,2},{4,8},{5,9},{6,10},{7,11},{8,4},{9,5},{10,... | collective-permute-start | bytes 3145736 | tf_op jit(solution)/shard_map/ppermute | solution.py:25
  102.6 28.6 %collective-permute-start.7 = (bf16[1,2,512,512]{3,2,1,0:T(8,128)(2,1)}, bf16[1,2,512,512]{3,2,1,0:T(8,128)(2,1)}, u32[]{:S(2)}, u32[]{:S(2)}) collective-permute-start(bf16[1,2,512,512]{3,2,1,0:T(8,128)(2,1)} %get-tuple-element.64), channel_id=1, source_target_pairs={{0,4},{2,6},{4,0},{6,2},{8,12},{10,14},{12,8},{14,10},{1,5},{3,7},... | collective-permute-start | bytes 3145736 | tf_op jit(solution)/shard_map/ppermute | solution.py:18
  107.3 25.3 %collective-permute-start.6 = (bf16[1,2,512,512]{3,2,1,0:T(8,128)(2,1)}, bf16[1,2,512,512]{3,2,1,0:T(8,128)(2,1)}, u32[]{:S(2)}, u32[]{:S(2)}) collective-permute-start(bf16[1,2,512,512]{3,2,1,0:T(8,128)(2,1)} %get-tuple-element.63.refs_1_), channel_id=1, source_target_pairs={{0,2},{2,0},{4,6},{6,4},{8,10},{10,8},{12,14},{14,12},{1,3},{3,1},... | collective-permute-start | bytes 3145736 | tf_op jit(solution)/shard_map/ppermute | solution.py:18
  132.7 11.0 %collective-permute-start.13 = (bf16[2,2,512,512]{3,2,1,0:T(8,128)(2,1)}, bf16[2,2,512,512]{3,2,1,0:T(8,128)(2,1)}, u32[]{:S(2)}, u32[]{:S(2)}) collective-permute-start(bf16[2,2,512,512]{3,2,1,0:T(8,128)(2,1)} %collective-permute-done.5.refs_0_.refs_1_.refs_3_.refs_4_), channel_id=1, source_target_pairs={{0,1},{1,0},{2,3},{3,2},{4,5},{5,4},{6,7},{7,6},{8,9},{9,8},{10,11... | collective-permute-start | bytes 6291464 | tf_op jit(solution)/shard_map/ppermute | solution.py:18
  132.7 11.0 %collective-permute-start.14 = (bf16[2,2,512,512]{3,2,1,0:T(8,128)(2,1)}, bf16[2,2,512,512]{3,2,1,0:T(8,128)(2,1)}, u32[]{:S(2)}, u32[]{:S(2)}) collective-permute-start(bf16[2,2,512,512]{3,2,1,0:T(8,128)(2,1)} %collective-permute-done.4.refs_1_.refs_2_), channel_id=1, source_target_pairs={{0,1},{1,0},{2,3},{3,2},{4,5},{5,4},{6,7},{7,6},{8,9},{9,8},{10,11... | collective-permute-start | bytes 6291464 | tf_op jit(solution)/shard_map/ppermute | solution.py:18
  133.2 25.4 %collective-permute-start.10 = (bf16[1,2,512,512]{3,2,1,0:T(8,128)(2,1)}, bf16[1,2,512,512]{3,2,1,0:T(8,128)(2,1)}, u32[]{:S(2)}, u32[]{:S(2)}) collective-permute-start(bf16[1,2,512,512]{3,2,1,0:T(8,128)(2,1)} %get-tuple-element.74.refs_1_), channel_id=1, source_target_pairs={{0,2},{2,0},{4,6},{6,4},{8,10},{10,8},{12,14},{14,12},{1,3},{3,1},... | collective-permute-start | bytes 3145736 | tf_op jit(solution)/shard_map/ppermute | solution.py:18
  133.7 25.1 %collective-permute-start.11 = (bf16[1,2,512,512]{3,2,1,0:T(8,128)(2,1)}, bf16[1,2,512,512]{3,2,1,0:T(8,128)(2,1)}, u32[]{:S(2)}, u32[]{:S(2)}) collective-permute-start(bf16[1,2,512,512]{3,2,1,0:T(8,128)(2,1)} %get-tuple-element.75), channel_id=1, source_target_pairs={{0,4},{2,6},{4,0},{6,2},{8,12},{10,14},{12,8},{14,10},{1,5},{3,7},... | collective-permute-start | bytes 3145736 | tf_op jit(solution)/shard_map/ppermute | solution.py:18
  134.1 24.7 %collective-permute-start.12 = (bf16[1,2,512,512]{3,2,1,0:T(8,128)(2,1)}, bf16[1,2,512,512]{3,2,1,0:T(8,128)(2,1)}, u32[]{:S(2)}, u32[]{:S(2)}) collective-permute-start(bf16[1,2,512,512]{3,2,1,0:T(8,128)(2,1)} %get-tuple-element.76), channel_id=1, source_target_pairs={{0,1},{1,0},{2,3},{3,2},{4,8},{5,9},{6,10},{7,11},{8,4},{9,5},{10,... | collective-permute-start | bytes 3145736 | tf_op jit(solution)/shard_map/ppermute | solution.py:25
  158.8 12.3 %collective-permute-start.15 = (bf16[1,2,512,512]{3,2,1,0:T(8,128)(2,1)}, bf16[1,2,512,512]{3,2,1,0:T(8,128)(2,1)}, u32[]{:S(2)}, u32[]{:S(2)}) collective-permute-start(bf16[1,2,512,512]{3,2,1,0:T(8,128)(2,1)} %collective-permute-done.8.w7.refs_2_), channel_id=1, source_target_pairs={{0,1},{1,0},{2,3},{3,2},{4,5},{5,4},{6,7},{7,6},{8,9},{9,8},{10,11... | collective-permute-start | bytes 3145736 | tf_op jit(solution)/shard_map/ppermute | solution.py:18
  158.8 12.3 %collective-permute-start.16 = (bf16[1,2,512,512]{3,2,1,0:T(8,128)(2,1)}, bf16[1,2,512,512]{3,2,1,0:T(8,128)(2,1)}, u32[]{:S(2)}, u32[]{:S(2)}) collective-permute-start(bf16[1,2,512,512]{3,2,1,0:T(8,128)(2,1)} %collective-permute-done.6.w5.refs_3_), channel_id=1, source_target_pairs={{0,1},{1,0},{2,3},{3,2},{4,5},{5,4},{6,7},{7,6},{8,9},{9,8},{10,11... | collective-permute-start | bytes 3145736 | tf_op jit(solution)/shard_map/ppermute | solution.py:18
  159.3 11.8 %collective-permute-start.18 = (bf16[1,2,512,512]{3,2,1,0:T(8,128)(2,1)}, bf16[1,2,512,512]{3,2,1,0:T(8,128)(2,1)}, u32[]{:S(2)}, u32[]{:S(2)}) collective-permute-start(bf16[1,2,512,512]{3,2,1,0:T(8,128)(2,1)} %collective-permute-done.10.w5.refs_9_), channel_id=1, source_target_pairs={{0,1},{1,0},{2,3},{3,2},{4,5},{5,4},{6,7},{7,6},{8,9},{9,8},{10,11... | collective-permute-start | bytes 3145736 | tf_op jit(solution)/shard_map/ppermute | solution.py:18
  159.3 11.8 %collective-permute-start.17 = (bf16[1,2,512,512]{3,2,1,0:T(8,128)(2,1)}, bf16[1,2,512,512]{3,2,1,0:T(8,128)(2,1)}, u32[]{:S(2)}, u32[]{:S(2)}) collective-permute-start(bf16[1,2,512,512]{3,2,1,0:T(8,128)(2,1)} %collective-permute-done.12.w7.refs_8_), channel_id=1, source_target_pairs={{0,1},{1,0},{2,3},{3,2},{4,5},{5,4},{6,7},{7,6},{8,9},{9,8},{10,11... | collective-permute-start | bytes 3145736 | tf_op jit(solution)/shard_map/ppermute | solution.py:18
  171.2 19.5 %copy-start.1 = (s32[16]{0:T(128)S(1)}, s32[16]{0:T(128)}, u32[]{:S(2)}) copy-start(s32[16]{0:T(128)} %param.13) | copy-start | bytes 196
  172.6 3.4 %collective-permute-start.21 = (f32[4,512]{1,0:T(4,128)}, f32[4,512]{1,0:T(4,128)S(1)}, u32[]{:S(2)}, u32[]{:S(2)}) collective-permute-start(f32[4,512]{1,0:T(4,128)} %shard_map.134), channel_id=1, source_target_pairs={{0,3},{1,2},{2,1},{3,0},{4,7},{5,6},{6,5},{7,4},{8,11},{9,10},{10,... | collective-permute-start | bytes 24584 | tf_op jit(solution)/shard_map/ppermute | solution.py:18
  173.7 3.9 %collective-permute-start.20 = (f32[4,512]{1,0:T(4,128)}, f32[4,512]{1,0:T(4,128)S(1)}, u32[]{:S(2)}, u32[]{:S(2)}) collective-permute-start(f32[4,512]{1,0:T(4,128)} %shard_map.134), channel_id=1, source_target_pairs={{0,2},{1,3},{2,0},{3,1},{4,6},{5,7},{6,4},{7,5},{8,10},{9,11},{10,... | collective-permute-start | bytes 24584 | tf_op jit(solution)/shard_map/ppermute | solution.py:18
  174.3 3.3 %collective-permute-start.19 = (f32[4,512]{1,0:T(4,128)}, f32[4,512]{1,0:T(4,128)S(1)}, u32[]{:S(2)}, u32[]{:S(2)}) collective-permute-start(f32[4,512]{1,0:T(4,128)} %shard_map.134), channel_id=1, source_target_pairs={{0,1},{1,0},{2,3},{3,2},{4,5},{5,4},{6,7},{7,6},{8,9},{9,8},{10,11... | collective-permute-start | bytes 24584 | tf_op jit(solution)/shard_map/ppermute | solution.py:18
  178.3 7.9 %collective-permute-start.24 = (f32[4,512]{1,0:T(4,128)S(1)}, f32[4,512]{1,0:T(4,128)S(1)}, u32[]{:S(2)}, u32[]{:S(2)}) collective-permute-start(f32[4,512]{1,0:T(4,128)S(1)} %add_add_fusion.1), channel_id=1, source_target_pairs={{0,12},{1,13},{2,14},{3,15},{4,8},{5,9},{6,10},{7,11},{8,4},{9,5},... | collective-permute-start | bytes 24584 | tf_op jit(solution)/shard_map/ppermute | solution.py:18
  179.5 8.4 %collective-permute-start.23 = (f32[4,512]{1,0:T(4,128)S(1)}, f32[4,512]{1,0:T(4,128)S(1)}, u32[]{:S(2)}, u32[]{:S(2)}) collective-permute-start(f32[4,512]{1,0:T(4,128)S(1)} %add_add_fusion.1), channel_id=1, source_target_pairs={{0,8},{1,9},{2,10},{3,11},{4,12},{5,13},{6,14},{7,15},{8,0},{9,1},... | collective-permute-start | bytes 24584 | tf_op jit(solution)/shard_map/ppermute | solution.py:18
  186.2 3.7 %collective-permute-start.22 = (f32[4,512]{1,0:T(4,128)S(1)}, f32[4,512]{1,0:T(4,128)S(1)}, u32[]{:S(2)}, u32[]{:S(2)}) collective-permute-start(f32[4,512]{1,0:T(4,128)S(1)} %add_add_fusion.1), channel_id=1, source_target_pairs={{0,4},{1,5},{2,6},{3,7},{4,0},{5,1},{6,2},{7,3},{8,12},{9,13},{10,... | collective-permute-start | bytes 24584 | tf_op jit(solution)/shard_map/ppermute | solution.py:18

commit v11 on v10

--- a/solution.py
+++ b/solution.py
@@ -32,15 +32,10 @@
 def sum_all(value):
     axes = ("row", "col")
     size = lax.axis_size("row") * lax.axis_size("col")
-    if size > 16 or size & (size - 1):
+    if size > 16:
         return lax.psum(value, axes)
-    mask = 1
-    while mask < size:
-        near = value + swap(value, axes, mask)
-        if 2 * mask < size:
-            near = near + (swap(value, axes, 2 * mask) + swap(value, axes, 3 * mask))
-        value, mask = near, 4 * mask
-    return value
+    copies = jnp.broadcast_to(value[None], (size, *value.shape))
+    return jnp.sum(lax.all_to_all(copies, axes, 0, 0, tiled=True), axis=0)
 
 
 def dot(a, b):

time: 192 us -> 193 us (level)
    ppermute x21 -> x15, starting transfers between devices: 25 us -> 15.2 us  [swap(): lax.ppermute(value, axis, [(source, source ^ mask) for source in range(si...]
    all_to_all x0 -> x1, starting transfers between devices: none -> 8.79 us  [sum_all(): return jnp.sum(lax.all_to_all(copies, axes, 0, 0, tiled=True), axis=0)]
    all_to_all x0 -> x1, waiting for transfers between devices: none -> 7.93 us  [sum_all(): return jnp.sum(lax.all_to_all(copies, axes, 0, 0, tiled=True), axis=0)]
    ppermute x21 -> x15, waiting for transfers between devices: 61.7 us -> 55 us  [swap(): lax.ppermute(value, axis, [(source, source ^ mask) for source in range(si...]
  transfers between devices with their start and end apart: 25 -> 20, of which waited for: 12 -> 9; matrix products, arithmetic and copies ran while one was open for 4% -> 4% of each run, Pallas kernels for 48% -> 47%
where the time goes in v11:
time: 193 us; the launch traced here: 192 us
  Pallas kernels  92.3 us (48%)
  waiting for transfers between devices  63 us (33%)
  starting transfers between devices  25 us (13%)
  local copies, waits for them, and re-layouts  5.67 us (3%)
  other arithmetic  4.57 us (2%)
    pallas_call x6, Pallas kernels, add_field(): pl.pallas_call(functools.partial(field_kernel, freq, count, has_total, ga...  55.7 us
    ppermute x15, waiting for transfers between devices, swap(): lax.ppermute(value, axis, [(source, source ^ mask) for source in range(si...  55 us
    pallas_call x2, Pallas kernels, add_late(): pl.pallas_call(functools.partial(late_kernel, freq), out_shape=(jax.Shape...  22.3 us
    ppermute x15, starting transfers between devices, swap(): lax.ppermute(value, axis, [(source, source ^ mask) for source in range(si...  15.2 us
    pallas_call x4, Pallas kernels, copies(): pl.pallas_call(functools.partial(copy_kernel, len(args), jobs), out_shape...  12.9 us
    all_to_all x1, starting transfers between devices, sum_all(): return jnp.sum(lax.all_to_all(copies, axes, 0, 0, tiled=True), axis=0)  8.79 us
    all_to_all x1, waiting for transfers between devices, sum_all(): return jnp.sum(lax.all_to_all(copies, axes, 0, 0, tiled=True), axis=0)  7.93 us
  transfers between devices with their start and end apart: 20, of which 9 were waited for; matrix products, arithmetic and copies ran while one was open for 4% of the time, Pallas kernels for 47%

profile of v11, /device:TPU:0, one launch (start us, length us, event | category | flops | bytes accessed | tf_op | source)
XLA Modules:
  0.0 192.3 jit_solution(11002093015315975287)
XLA Ops:
  0.6 0.5 collective-permute-start.2
  1.1 4.1 %collective-permute-start.1 = (bf16[2,2,512,512]{3,2,1,0:T(8,128)(2,1)}, bf16[2,2,512,512]{3,2,1,0:T(8,128)(2,1)}, u32[]{:S(2)}, u32[]{:S(2)}) collective-permute-start(bf16[2,2,512,512]{3,2,1,0:T(8,128)(2,1)} %bitcast.18), channel_id=1, source_target_pairs={{0,4},{2,6},{4,0},{6,2},{8,12},{10,14},{12,8},{14,10},{1,5},{3,7},... | collective-permute-start | bytes 6291464 | tf_op jit(solution)/shard_map/ppermute | solution.py:18
  5.3 1.5 collective-permute-start
  6.8 5.8 %shard_map.124.refs_3_ = f32[2,1024,512]{2,1,0:T(8,128)} custom-call(s32[1]{0:T(128)} %bitcast.2.ids, bf16[2,2,1024,4096]{3,2,1,0:T(8,128)(2,1)} %cross.15, bf16[2,2,512,512]{3,2,1,0:T(8,128)(2,1)} %bitcast.20), custom_call_target="tpu_custom_call" | custom-call | flops 1 | bytes 1 | tf_op jit(solution)/shard_map/pallas_call | solution.py:133
  12.6 0.0 copy-start
  12.6 5.9 %shard_map.123.refs_3_ = f32[2,1024,512]{2,1,0:T(8,128)} custom-call(s32[1]{0:T(128)} %bitcast.2.ids, bf16[2,2,1024,4096]{3,2,1,0:T(8,128)(2,1)} %cross.15, bf16[2,2,512,512]{3,2,1,0:T(8,128)(2,1)} %bitcast.21), custom_call_target="tpu_custom_call" | custom-call | flops 1 | bytes 1 | tf_op jit(solution)/shard_map/pallas_call | solution.py:133
  18.7 0.5 fusion.16
  19.2 0.6 concatenate.11.ids
  19.8 0.7 pad_add_fusion.ids
  20.5 0.6 pad_add_fusion.1.ids
  21.1 2.6 %multiply_reduce_fusion.norms = f32[2,512]{1,0:T(2,128)} fusion(bf16[2,2,1,512,512]{4,3,2,1,0:T(8,128)(2,1)} %param.12), kind=kLoop, calls=%fused_computation | loop fusion | flops 3144704 | bytes 2101248 | tf_op jit(solution)/shard_map/reduce_sum | solution.py:570
  23.7 3.1 %shard_map.122.refs_2_.refs_3_ = bf16[2,2,512,512]{3,2,1,0:T(8,128)(2,1)} custom-call(s32[2]{0:T(128)} %pad_add_fusion.ids, bf16[2,2,512,512]{3,2,1,0:T(8,128)(2,1)} %collective-permute-done.2.refs_0_, bf16[2,2,1024,4096]{3,2,1,0:T(8,128)(2,1)} %cross.15), custom_call_target="tpu_custom_call", output_to_operand_aliasing={{}: (1, {})} | custom-call | flops 1 | bytes 1 | tf_op jit(solution)/shard_map/pallas_call | solution.py:393
  26.8 24.2 %collective-permute-done.1.refs_1_.refs_2_ = bf16[2,2,512,512]{3,2,1,0:T(8,128)(2,1)} collective-permute-done((bf16[2,2,512,512]{3,2,1,0:T(8,128)(2,1)}, bf16[2,2,512,512]{3,2,1,0:T(8,128)(2,1)}, u32[]{:S(2)}, u32[]{:S(2)}) %collective-permute-start.1) | collective-permute-done | bytes 2097184 | tf_op jit(solution)/shard_map/ppermute | solution.py:18
  51.0 1.4 collective-permute-done.refs_0_.refs_1_
  52.4 0.3 collective-permute-start.3
  52.7 1.5 collective-permute-start.5
  54.2 12.3 %shard_map.125.refs_2_ = f32[2,1024,512]{2,1,0:T(8,128)} custom-call(s32[4]{0:T(128)} %pad_add_fusion.1.ids, bf16[2,2,1024,4096]{3,2,1,0:T(8,128)(2,1)} %cross.15, bf16[2,2,512,512]{3,2,1,0:T(8,128)(2,1)} %collective-permute-done.refs_0_.refs_1_, bf16[2,2,512,512]{3,2,1,0:T(8,128)(2,1)} %collective-permute-done.1.refs_1_.refs_2_, ...), custom_call_target="tpu_custom_call" | custom-call | flops 1 | bytes 1 | tf_op jit(solution)/shard_map/pallas_call | solution.py:133
  66.5 12.4 %shard_map.126.refs_2_ = f32[2,1024,512]{2,1,0:T(8,128)} custom-call(s32[4]{0:T(128)} %pad_add_fusion.1.ids, bf16[2,2,1024,4096]{3,2,1,0:T(8,128)(2,1)} %cross.15, bf16[2,2,512,512]{3,2,1,0:T(8,128)(2,1)} %collective-permute-done.refs_0_.refs_1_, bf16[2,2,512,512]{3,2,1,0:T(8,128)(2,1)} %collective-permute-done.1.refs_1_.refs_2_, ...), custom_call_target="tpu_custom_call" | custom-call | flops 1 | bytes 1 | tf_op jit(solution)/shard_map/pallas_call | solution.py:133
  78.9 3.6 %shard_map.127.refs_0_ = bf16[2,2,1024,512]{3,2,1,0:T(8,128)(2,1)} custom-call(s32[1]{0:T(128)} %bitcast.6.ids, bf16[2,2,512,512]{3,2,1,0:T(8,128)(2,1)} %bitcast.22, bf16[2,2,512,512]{3,2,1,0:T(8,128)(2,1)} %collective-permute-done.refs_0_.refs_1_, bf16[2,2,512,512]{3,2,1,0:T(8,128)(2,1)} %collective-permute-done.1.refs_1_.refs_2_, ...), custom_call_target="tpu_custom_call" | custom-call | flops 1 | bytes 1 | tf_op jit(solution)/shard_map/pallas_call | solution.py:393
  82.5 3.0 %fusion.18 = (bf16[1,2,512,512]{3,2,1,0:T(8,128)(2,1)}, bf16[1,2,512,512]{3,2,1,0:T(8,128)(2,1)}) fusion(bf16[2,2,512,512]{3,2,1,0:T(8,128)(2,1)} %collective-permute-done.refs_0_.refs_1_), kind=kLoop, calls=%fused_computation.40 | loop fusion | bytes 4194304 | tf_op jit(solution)/shard_map/slice | solution.py:515
  85.5 13.1 %collective-permute-done.3.refs_0_.block_re.block_im = bf16[2,2,512,512]{3,2,1,0:T(8,128)(2,1)} collective-permute-done((bf16[2,2,512,512]{3,2,1,0:T(8,128)(2,1)}, bf16[2,2,512,512]{3,2,1,0:T(8,128)(2,1)}, u32[]{:S(2)}, u32[]{:S(2)}) %collective-permute-start.3) | collective-permute-done | bytes 2097184 | tf_op jit(solution)/shard_map/ppermute | solution.py:18
  98.6 0.3 collective-permute-done.5.refs_0_.refs_1_.refs_3_.refs_4_
  98.9 0.5 collective-permute-start.8
  99.4 3.1 %shard_map.128 = (bf16[1,2,512,512]{3,2,1,0:T(8,128)(2,1)}, bf16[1,2,512,512]{3,2,1,0:T(8,128)(2,1)}) custom-call(s32[2]{0:T(128)} %pad_add_fusion.ids, bf16[2,2,512,512]{3,2,1,0:T(8,128)(2,1)} %collective-permute-done.3.refs_0_.block_re.block_im, bf16[2,2,512,512]{3,2,1,0:T(8,128)(2,1)} %collective-permute-done.4.refs_1_.refs_2_, ...), custom_call_target="tpu_custom_call" | custom-call | flops 1 | bytes 1 | tf_op jit(solution)/shard_map/pallas_call | solution.py:393
  102.6 4.8 %collective-permute-start.7 = (bf16[1,2,512,512]{3,2,1,0:T(8,128)(2,1)}, bf16[1,2,512,512]{3,2,1,0:T(8,128)(2,1)}, u32[]{:S(2)}, u32[]{:S(2)}) collective-permute-start(bf16[1,2,512,512]{3,2,1,0:T(8,128)(2,1)} %get-tuple-element.64), channel_id=1, source_target_pairs={{0,4},{2,6},{4,0},{6,2},{8,12},{10,14},{12,8},{14,10},{1,5},{3,7},... | collective-permute-start | bytes 3145736 | tf_op jit(solution)/shard_map/ppermute | solution.py:18
  107.4 0.5 collective-permute-start.6
  107.9 9.8 %shard_map.129.total = f32[2,1024,512]{2,1,0:T(8,128)} custom-call(s32[2]{0:T(128)} %get-tuple-element.67.ids, bf16[2,2,1024,4096]{3,2,1,0:T(8,128)(2,1)} %cross.15, bf16[2,2,512,512]{3,2,1,0:T(8,128)(2,1)} %collective-permute-done.5.refs_0_.refs_1_.refs_3_.refs_4_, bf16[1,2,512,512]{3,2,1,0:T(8,128)(2,1)} %get-tuple-element.63.refs_1_, ...), custom_call_target="tpu_custom_call" | custom-call | flops 1 | bytes 1 | tf_op jit(solution)/shard_map/pallas_call | solution.py:133
  117.7 3.1 %shard_map.130 = (bf16[1,2,512,512]{3,2,1,0:T(8,128)(2,1)}, bf16[1,2,512,512]{3,2,1,0:T(8,128)(2,1)}) custom-call(s32[2]{0:T(128)} %pad_add_fusion.ids, bf16[2,2,512,512]{3,2,1,0:T(8,128)(2,1)} %collective-permute-done.3.refs_0_.block_re.block_im, bf16[2,2,512,512]{3,2,1,0:T(8,128)(2,1)} %collective-permute-done.4.refs_1_.refs_2_, ...), custom_call_target="tpu_custom_call" | custom-call | flops 1 | bytes 1 | tf_op jit(solution)/shard_map/pallas_call | solution.py:393
  120.8 10.5 %collective-permute-done.7.w6.block_re = bf16[1,2,512,512]{3,2,1,0:T(8,128)(2,1)} collective-permute-done((bf16[1,2,512,512]{3,2,1,0:T(8,128)(2,1)}, bf16[1,2,512,512]{3,2,1,0:T(8,128)(2,1)}, u32[]{:S(2)}, u32[]{:S(2)}) %collective-permute-start.7) | collective-permute-done | bytes 1048608 | tf_op jit(solution)/shard_map/ppermute | solution.py:18
  131.2 1.5 collective-permute-done.6.w5.refs_3_
  132.7 0.5 collective-permute-start.14
  133.2 0.5 collective-permute-start.10
  133.7 0.4 collective-permute-start.11
  134.1 9.6 %shard_map.132.total = f32[2,1024,512]{2,1,0:T(8,128)} custom-call(s32[2]{0:T(128)} %get-tuple-element.67.ids, bf16[2,2,1024,4096]{3,2,1,0:T(8,128)(2,1)} %cross.15, bf16[2,2,512,512]{3,2,1,0:T(8,128)(2,1)} %collective-permute-done.5.refs_0_.refs_1_.refs_3_.refs_4_, bf16[1,2,512,512]{3,2,1,0:T(8,128)(2,1)} %get-tuple-element.74.refs_1_, ...), custom_call_target="tpu_custom_call" | custom-call | flops 1 | bytes 1 | tf_op jit(solution)/shard_map/pallas_call | solution.py:133
  143.7 11.0 %shard_map.131 = (f32[8,512]{1,0:T(8,128)}, f32[2,512,512]{2,1,0:T(8,128)}) custom-call(s32[8]{0:T(128)} %concatenate.11.ids, bf16[2,2,1024,4096]{3,2,1,0:T(8,128)(2,1)} %cross.15, bf16[1,2,512,512]{3,2,1,0:T(8,128)(2,1)} %collective-permute-done.6.w5.refs_3_, bf16[1,2,512,512]{3,2,1,0:T(8,128)(2,1)} %collective-permute-done.7.w6.block_re, ...), custom_call_target="tpu_custom_call" | custom-call | flops 1 | bytes 1 | tf_op jit(solution)/shard_map/pallas_call | solution.py:286
  154.8 3.8 %collective-permute-done.10.w5.refs_9_ = bf16[1,2,512,512]{3,2,1,0:T(8,128)(2,1)} collective-permute-done((bf16[1,2,512,512]{3,2,1,0:T(8,128)(2,1)}, bf16[1,2,512,512]{3,2,1,0:T(8,128)(2,1)}, u32[]{:S(2)}, u32[]{:S(2)}) %collective-permute-start.10) | collective-permute-done | bytes 1048608 | tf_op jit(solution)/shard_map/ppermute | solution.py:18
  158.6 0.3 collective-permute-done.11.w6.block_im
  158.9 0.5 collective-permute-start.16
  159.4 0.5 collective-permute-start.17
  159.9 11.2 %shard_map.133 = (f32[8,512]{1,0:T(8,128)}, f32[2,512,512]{2,1,0:T(8,128)}) custom-call(s32[8]{0:T(128)} %concatenate.11.ids, bf16[2,2,1024,4096]{3,2,1,0:T(8,128)(2,1)} %cross.15, bf16[1,2,512,512]{3,2,1,0:T(8,128)(2,1)} %collective-permute-done.10.w5.refs_9_, bf16[1,2,512,512]{3,2,1,0:T(8,128)(2,1)} %collective-permute-done.11.w6.block_im, ...), custom_call_target="tpu_custom_call" | custom-call | flops 1 | bytes 1 | tf_op jit(solution)/shard_map/pallas_call | solution.py:286
  171.2 1.4 shard_map.134
  172.6 1.4 broadcast_in_dim.43
  173.9 8.8 %all-to-all-start = ((f32[16,4,512]{2,1,0:T(4,128)}), f32[16,4,512]{2,1,0:T(4,128)S(1)}, u32[]{:S(2)}, u32[]{:S(2)}) async-start(f32[16,4,512]{2,1,0:T(4,128)} %broadcast_in_dim.43), calls=%async_computation | async-start | bytes 262144 | tf_op jit(solution)/shard_map/all_to_all | solution.py:38
  182.7 7.9 %all-to-all-done = f32[16,4,512]{2,1,0:T(4,128)S(1)} async-done(((f32[16,4,512]{2,1,0:T(4,128)}), f32[16,4,512]{2,1,0:T(4,128)S(1)}, u32[]{:S(2)}, u32[]{:S(2)}) %all-to-all-start) | async-done | bytes 131104 | tf_op jit(solution)/shard_map/all_to_all | solution.py:38
  190.7 0.1 abs_reduce_fusion
  190.8 0.1 reshape.42
  190.9 0.6 constant_dynamic-slice_fusion
  191.5 0.8 fusion
  (26 shorter events, 0.1 us)
Async XLA Ops:
  0.6 23.1 %collective-permute-start.2 = (bf16[2,2,512,512]{3,2,1,0:T(8,128)(2,1)}, bf16[2,2,512,512]{3,2,1,0:T(8,128)(2,1)}, u32[]{:S(2)}, u32[]{:S(2)}) collective-permute-start(bf16[2,2,512,512]{3,2,1,0:T(8,128)(2,1)} %bitcast.17), channel_id=1, source_target_pairs={{0,1},{1,0},{2,3},{3,2},{4,8},{5,9},{6,10},{7,11},{8,4},{9,5},{10,... | collective-permute-start | bytes 6291464 | tf_op jit(solution)/shard_map/ppermute | solution.py:25
  1.1 49.8 %collective-permute-start.1 = (bf16[2,2,512,512]{3,2,1,0:T(8,128)(2,1)}, bf16[2,2,512,512]{3,2,1,0:T(8,128)(2,1)}, u32[]{:S(2)}, u32[]{:S(2)}) collective-permute-start(bf16[2,2,512,512]{3,2,1,0:T(8,128)(2,1)} %bitcast.18), channel_id=1, source_target_pairs={{0,4},{2,6},{4,0},{6,2},{8,12},{10,14},{12,8},{14,10},{1,5},{3,7},... | collective-permute-start | bytes 6291464 | tf_op jit(solution)/shard_map/ppermute | solution.py:18
  5.3 47.1 %collective-permute-start = (bf16[2,2,512,512]{3,2,1,0:T(8,128)(2,1)}, bf16[2,2,512,512]{3,2,1,0:T(8,128)(2,1)}, u32[]{:S(2)}, u32[]{:S(2)}) collective-permute-start(bf16[2,2,512,512]{3,2,1,0:T(8,128)(2,1)} %bitcast.19), channel_id=1, source_target_pairs={{0,2},{2,0},{4,6},{6,4},{8,10},{10,8},{12,14},{14,12},{1,3},{3,1},... | collective-permute-start | bytes 6291464 | tf_op jit(solution)/shard_map/ppermute | solution.py:18
  12.6 6.1 %copy-start = (s32[2]{0:T(128)S(1)}, s32[2]{0:T(128)}, u32[]{:S(2)}) copy-start(s32[2]{0:T(128)} %constant.117.clone) | copy-start | bytes 28
  12.6 7.9 %copy-start.2 = (s32[3]{0:T(128)S(1)}, s32[3]{0:T(128)}, u32[]{:S(2)}) copy-start(s32[3]{0:T(128)} %constant.116.clone) | copy-start | bytes 40
  52.4 46.2 %collective-permute-start.3 = (bf16[2,2,512,512]{3,2,1,0:T(8,128)(2,1)}, bf16[2,2,512,512]{3,2,1,0:T(8,128)(2,1)}, u32[]{:S(2)}, u32[]{:S(2)}) collective-permute-start(bf16[2,2,512,512]{3,2,1,0:T(8,128)(2,1)} %shard_map.122.refs_2_.refs_3_), channel_id=1, source_target_pairs={{0,4},{2,6},{4,0},{6,2},{8,12},{10,14},{12,8},{14,10},{1,5},{3,7},... | collective-permute-start | bytes 6291464 | tf_op jit(solution)/shard_map/ppermute | solution.py:18
  52.7 46.2 %collective-permute-start.5 = (bf16[2,2,512,512]{3,2,1,0:T(8,128)(2,1)}, bf16[2,2,512,512]{3,2,1,0:T(8,128)(2,1)}, u32[]{:S(2)}, u32[]{:S(2)}) collective-permute-start(bf16[2,2,512,512]{3,2,1,0:T(8,128)(2,1)} %collective-permute-done.1.refs_1_.refs_2_), channel_id=1, source_target_pairs={{0,2},{2,0},{4,6},{6,4},{8,10},{10,8},{12,14},{14,12},{1,3},{3,1},... | collective-permute-start | bytes 6291464 | tf_op jit(solution)/shard_map/ppermute | solution.py:18
  54.2 44.7 %collective-permute-start.4 = (bf16[2,2,512,512]{3,2,1,0:T(8,128)(2,1)}, bf16[2,2,512,512]{3,2,1,0:T(8,128)(2,1)}, u32[]{:S(2)}, u32[]{:S(2)}) collective-permute-start(bf16[2,2,512,512]{3,2,1,0:T(8,128)(2,1)} %collective-permute-done.1.refs_1_.refs_2_), channel_id=1, source_target_pairs={{0,1},{1,0},{2,3},{3,2},{4,8},{5,9},{6,10},{7,11},{8,4},{9,5},{10,... | collective-permute-start | bytes 6291464 | tf_op jit(solution)/shard_map/ppermute | solution.py:25
  98.9 33.8 %collective-permute-start.9 = (bf16[2,2,1024,512]{3,2,1,0:T(8,128)(2,1)}, bf16[2,2,1024,512]{3,2,1,0:T(8,128)(2,1)}, u32[]{:S(2)}, u32[]{:S(2)}) collective-permute-start(bf16[2,2,1024,512]{3,2,1,0:T(8,128)(2,1)} %shard_map.127.refs_0_), channel_id=1, source_target_pairs={{0,1},{1,0},{2,3},{3,2},{4,5},{5,4},{6,7},{7,6},{8,9},{9,8},{10,11... | collective-permute-start | bytes 12582920 | tf_op jit(solution)/shard_map/ppermute | solution.py:18
  98.9 21.8 %collective-permute-start.8 = (bf16[1,2,512,512]{3,2,1,0:T(8,128)(2,1)}, bf16[1,2,512,512]{3,2,1,0:T(8,128)(2,1)}, u32[]{:S(2)}, u32[]{:S(2)}) collective-permute-start(bf16[1,2,512,512]{3,2,1,0:T(8,128)(2,1)} %get-tuple-element.65), channel_id=1, source_target_pairs={{0,1},{1,0},{2,3},{3,2},{4,8},{5,9},{6,10},{7,11},{8,4},{9,5},{10,... | collective-permute-start | bytes 3145736 | tf_op jit(solution)/shard_map/ppermute | solution.py:25
  102.6 28.6 %collective-permute-start.7 = (bf16[1,2,512,512]{3,2,1,0:T(8,128)(2,1)}, bf16[1,2,512,512]{3,2,1,0:T(8,128)(2,1)}, u32[]{:S(2)}, u32[]{:S(2)}) collective-permute-start(bf16[1,2,512,512]{3,2,1,0:T(8,128)(2,1)} %get-tuple-element.64), channel_id=1, source_target_pairs={{0,4},{2,6},{4,0},{6,2},{8,12},{10,14},{12,8},{14,10},{1,5},{3,7},... | collective-permute-start | bytes 3145736 | tf_op jit(solution)/shard_map/ppermute | solution.py:18
  107.4 25.3 %collective-permute-start.6 = (bf16[1,2,512,512]{3,2,1,0:T(8,128)(2,1)}, bf16[1,2,512,512]{3,2,1,0:T(8,128)(2,1)}, u32[]{:S(2)}, u32[]{:S(2)}) collective-permute-start(bf16[1,2,512,512]{3,2,1,0:T(8,128)(2,1)} %get-tuple-element.63.refs_1_), channel_id=1, source_target_pairs={{0,2},{2,0},{4,6},{6,4},{8,10},{10,8},{12,14},{14,12},{1,3},{3,1},... | collective-permute-start | bytes 3145736 | tf_op jit(solution)/shard_map/ppermute | solution.py:18
  132.7 11.0 %collective-permute-start.13 = (bf16[2,2,512,512]{3,2,1,0:T(8,128)(2,1)}, bf16[2,2,512,512]{3,2,1,0:T(8,128)(2,1)}, u32[]{:S(2)}, u32[]{:S(2)}) collective-permute-start(bf16[2,2,512,512]{3,2,1,0:T(8,128)(2,1)} %collective-permute-done.5.refs_0_.refs_1_.refs_3_.refs_4_), channel_id=1, source_target_pairs={{0,1},{1,0},{2,3},{3,2},{4,5},{5,4},{6,7},{7,6},{8,9},{9,8},{10,11... | collective-permute-start | bytes 6291464 | tf_op jit(solution)/shard_map/ppermute | solution.py:18
  132.7 11.0 %collective-permute-start.14 = (bf16[2,2,512,512]{3,2,1,0:T(8,128)(2,1)}, bf16[2,2,512,512]{3,2,1,0:T(8,128)(2,1)}, u32[]{:S(2)}, u32[]{:S(2)}) collective-permute-start(bf16[2,2,512,512]{3,2,1,0:T(8,128)(2,1)} %collective-permute-done.4.refs_1_.refs_2_), channel_id=1, source_target_pairs={{0,1},{1,0},{2,3},{3,2},{4,5},{5,4},{6,7},{7,6},{8,9},{9,8},{10,11... | collective-permute-start | bytes 6291464 | tf_op jit(solution)/shard_map/ppermute | solution.py:18
  133.2 25.4 %collective-permute-start.10 = (bf16[1,2,512,512]{3,2,1,0:T(8,128)(2,1)}, bf16[1,2,512,512]{3,2,1,0:T(8,128)(2,1)}, u32[]{:S(2)}, u32[]{:S(2)}) collective-permute-start(bf16[1,2,512,512]{3,2,1,0:T(8,128)(2,1)} %get-tuple-element.74.refs_1_), channel_id=1, source_target_pairs={{0,2},{2,0},{4,6},{6,4},{8,10},{10,8},{12,14},{14,12},{1,3},{3,1},... | collective-permute-start | bytes 3145736 | tf_op jit(solution)/shard_map/ppermute | solution.py:18
  133.7 25.1 %collective-permute-start.11 = (bf16[1,2,512,512]{3,2,1,0:T(8,128)(2,1)}, bf16[1,2,512,512]{3,2,1,0:T(8,128)(2,1)}, u32[]{:S(2)}, u32[]{:S(2)}) collective-permute-start(bf16[1,2,512,512]{3,2,1,0:T(8,128)(2,1)} %get-tuple-element.75), channel_id=1, source_target_pairs={{0,4},{2,6},{4,0},{6,2},{8,12},{10,14},{12,8},{14,10},{1,5},{3,7},... | collective-permute-start | bytes 3145736 | tf_op jit(solution)/shard_map/ppermute | solution.py:18
  134.1 24.7 %collective-permute-start.12 = (bf16[1,2,512,512]{3,2,1,0:T(8,128)(2,1)}, bf16[1,2,512,512]{3,2,1,0:T(8,128)(2,1)}, u32[]{:S(2)}, u32[]{:S(2)}) collective-permute-start(bf16[1,2,512,512]{3,2,1,0:T(8,128)(2,1)} %get-tuple-element.76), channel_id=1, source_target_pairs={{0,1},{1,0},{2,3},{3,2},{4,8},{5,9},{6,10},{7,11},{8,4},{9,5},{10,... | collective-permute-start | bytes 3145736 | tf_op jit(solution)/shard_map/ppermute | solution.py:25
  158.9 12.3 %collective-permute-start.15 = (bf16[1,2,512,512]{3,2,1,0:T(8,128)(2,1)}, bf16[1,2,512,512]{3,2,1,0:T(8,128)(2,1)}, u32[]{:S(2)}, u32[]{:S(2)}) collective-permute-start(bf16[1,2,512,512]{3,2,1,0:T(8,128)(2,1)} %collective-permute-done.8.w7.refs_2_), channel_id=1, source_target_pairs={{0,1},{1,0},{2,3},{3,2},{4,5},{5,4},{6,7},{7,6},{8,9},{9,8},{10,11... | collective-permute-start | bytes 3145736 | tf_op jit(solution)/shard_map/ppermute | solution.py:18
  158.9 12.3 %collective-permute-start.16 = (bf16[1,2,512,512]{3,2,1,0:T(8,128)(2,1)}, bf16[1,2,512,512]{3,2,1,0:T(8,128)(2,1)}, u32[]{:S(2)}, u32[]{:S(2)}) collective-permute-start(bf16[1,2,512,512]{3,2,1,0:T(8,128)(2,1)} %collective-permute-done.6.w5.refs_3_), channel_id=1, source_target_pairs={{0,1},{1,0},{2,3},{3,2},{4,5},{5,4},{6,7},{7,6},{8,9},{9,8},{10,11... | collective-permute-start | bytes 3145736 | tf_op jit(solution)/shard_map/ppermute | solution.py:18
  159.4 11.8 %collective-permute-start.18 = (bf16[1,2,512,512]{3,2,1,0:T(8,128)(2,1)}, bf16[1,2,512,512]{3,2,1,0:T(8,128)(2,1)}, u32[]{:S(2)}, u32[]{:S(2)}) collective-permute-start(bf16[1,2,512,512]{3,2,1,0:T(8,128)(2,1)} %collective-permute-done.10.w5.refs_9_), channel_id=1, source_target_pairs={{0,1},{1,0},{2,3},{3,2},{4,5},{5,4},{6,7},{7,6},{8,9},{9,8},{10,11... | collective-permute-start | bytes 3145736 | tf_op jit(solution)/shard_map/ppermute | solution.py:18
  159.4 11.8 %collective-permute-start.17 = (bf16[1,2,512,512]{3,2,1,0:T(8,128)(2,1)}, bf16[1,2,512,512]{3,2,1,0:T(8,128)(2,1)}, u32[]{:S(2)}, u32[]{:S(2)}) collective-permute-start(bf16[1,2,512,512]{3,2,1,0:T(8,128)(2,1)} %collective-permute-done.12.w7.refs_8_), channel_id=1, source_target_pairs={{0,1},{1,0},{2,3},{3,2},{4,5},{5,4},{6,7},{7,6},{8,9},{9,8},{10,11... | collective-permute-start | bytes 3145736 | tf_op jit(solution)/shard_map/ppermute | solution.py:18
  171.2 20.4 %copy-start.1 = (s32[16]{0:T(128)S(1)}, s32[16]{0:T(128)}, u32[]{:S(2)}) copy-start(s32[16]{0:T(128)} %param.13) | copy-start | bytes 196
  173.9 16.7 %all-to-all-start = ((f32[16,4,512]{2,1,0:T(4,128)}), f32[16,4,512]{2,1,0:T(4,128)S(1)}, u32[]{:S(2)}, u32[]{:S(2)}) async-start(f32[16,4,512]{2,1,0:T(4,128)} %broadcast_in_dim.43), calls=%async_computation | async-start | bytes 262144 | tf_op jit(solution)/shard_map/all_to_all | solution.py:38

commit v12 on v11

--- a/solution.py
+++ b/solution.py
@@ -29,12 +29,15 @@
     return lax.optimization_barrier((value, *others))[0]
 
 
-def sum_all(value):
+def copies_to_all():
+    size = lax.axis_size("row") * lax.axis_size("col")
+    return size if size <= 16 else 1
+
+
+def sum_all(copies):
     axes = ("row", "col")
-    size = lax.axis_size("row") * lax.axis_size("col")
-    if size > 16:
-        return lax.psum(value, axes)
-    copies = jnp.broadcast_to(value[None], (size, *value.shape))
+    if copies.shape[0] == 1:
+        return lax.psum(copies[0], axes)
     return jnp.sum(lax.all_to_all(copies, axes, 0, 0, tiled=True), axis=0)
 
 
@@ -186,13 +189,27 @@
     row_refs, refs = refs[:10], refs[10:]
     sums, field_out, left, right, l_sem, w_sem, field, tot, sem, rows, row_sem = refs
     late = ids[7]
-    step, part = pl.program_id(0), pl.program_id(1)
-    width = w5.shape[2]
-    first = weight_copies(freq, w5, right.at[0], w_sem.at[0]) + spectra_copies(
-        freq, ids[0], cross, left.at[0], l_sem.at[0]
-    )
-    six = weight_copies(freq, w6, right.at[1], w_sem.at[1])
-    seven = weight_copies(freq, w7, right.at[1], w_sem.at[1])
+    step = pl.program_id(0)
+    width, sources = w5.shape[2:]
+    lanes = [slice(part * sources, (part + 1) * sources) for part in range(2)]
+
+    def weights(ref, k):
+        source = at_freq(ref, freq)
+        return [
+            pltpu.make_async_copy(
+                source.at[part],
+                right.at[k, pl.ds(0, width), pl.ds(part * sources, sources)],
+                w_sem.at[k, part],
+            )
+            for part in range(2)
+        ]
+
+    def spread_lanes(k):
+        right[k, width:, lanes[0]] = -right[k, :width, lanes[1]]
+        right[k, width:, lanes[1]] = right[k, :width, lanes[0]]
+
+    first = weights(w5, 0) + spectra_copies(freq, ids[0], cross, left.at[0], l_sem.at[0])
+    six, seven = weights(w6, 1), weights(w7, 1)
     second = spectra_copies(freq, ids[1], cross, left.at[1], l_sem.at[1])
     third = [
         pltpu.make_async_copy(
@@ -203,14 +220,21 @@
         for k, ref in enumerate((block_re, block_im))
         for half in range(2)
     ]
-    total_copy = pltpu.make_async_copy(total, tot, sem.at[0])
+    total_copies = [
+        pltpu.make_async_copy(
+            total.at[part], tot.at[:, pl.ds(part * sources, sources)], sem.at[part]
+        )
+        for part in range(2)
+    ]
     late_rows = pl.ds(pl.multiple_of(jnp.minimum(late, 1) * width, width), width)
     out_copies = [
-        pltpu.make_async_copy(field.at[k, late_rows], field_out.at[k], sem.at[1 + k])
-        for k in range(2)
-    ]
-
-    @pl.when((step == 0) & (part == 0))
+        pltpu.make_async_copy(
+            field.at[late_rows, pl.ds(part * sources, sources)], field_out.at[part], sem.at[2 + part]
+        )
+        for part in range(2)
+    ]
+
+    @pl.when(step == 0)
     def _():
         sums[...] = jnp.zeros_like(sums)
         for copy in first:
@@ -230,52 +254,48 @@
             for copy in six:
                 copy.start()
 
-        total_copy.start()
+        for copy in total_copies:
+            copy.start()
         start_rows(freq, ids, 3, row_refs, rows.at[0], row_sem.at[0])
-        spread(right.at[0])
-
-    @pl.when((step == 1) & (part == 0))
+        spread_lanes(0)
+        field[...] = dot(left[0], right[0])
+
+    @pl.when(step == 1)
     def _():
         for copy in second + six:
             copy.wait()
         for copy in third:
             copy.start()
         start_rows(freq, ids, 5, row_refs, rows.at[1], row_sem.at[1])
-        total_copy.wait()
+        for copy in total_copies:
+            copy.wait()
+        spread_lanes(1)
+        field[...] = field[...] + tot[...] + dot(left[1], right[1])
+        for copy in out_copies:
+            copy.start()
         for slot in range(2):
             wait_rows(freq, slot, row_refs, rows.at[0], row_sem.at[0])
-        spread(right.at[1])
-
-    @pl.when((step == 2) & (part == 0))
+        for slot in range(2):
+
+            @pl.when(late != slot)
+            def _(slot=slot):
+                here = slice(slot * width, (slot + 1) * width)
+                for part in range(2):
+                    sums[...] += fold(rows[0, part, here], field[here, lanes[part]])
+
+    @pl.when(step == 2)
     def _():
         for copy in third:
             copy.wait()
         for slot in range(2):
             wait_rows(freq, slot, row_refs, rows.at[1], row_sem.at[1])
 
-    @pl.when(step == 0)
-    def _():
-        field[part] = dot(left[0], right[0, part])
-
-    for k in range(2):
-
-        @pl.when((step == 1) & (part == k))
-        def _(k=k):
-            field[k] = field[k] + tot[k] + dot(left[1], right[1, k])
-            out_copies[k].start()
-            for slot in range(2):
-
-                @pl.when(late != slot)
-                def _(slot=slot):
-                    here = slice(slot * width, (slot + 1) * width)
-                    sums[...] += fold(rows[0, k, here], field[k, here])
-
-    @pl.when((step == 2) & (ids[2] == 1))
-    def _():
-        sums[...] += fold(rows[1, part], dot(left[2], right[0, part]))
-
-    @pl.when((step == 2) & (part == 1))
-    def _():
+        @pl.when(ids[2] == 1)
+        def _():
+            value = dot(left[2], right[0])
+            for part in range(2):
+                sums[...] += fold(rows[1, part], value[:, lanes[part]])
+
         for copy in out_copies:
             copy.wait()
 
@@ -291,17 +311,17 @@
         ),
         grid_spec=pltpu.PrefetchScalarGridSpec(
             num_scalar_prefetch=1,
-            grid=(3, 2),
+            grid=(3,),
             in_specs=[ANYWHERE] * (7 + len(row_refs)),
-            out_specs=(pl.BlockSpec((8, sources), lambda step, part, ids: (0, 0)), ANYWHERE),
+            out_specs=(pl.BlockSpec((8, sources), lambda step, ids: (0, 0)), ANYWHERE),
             scratch_shapes=[
                 pltpu.VMEM((3, rows, 2 * width), dtype),
-                pltpu.VMEM((2, 2, 2 * width, sources), dtype),
+                pltpu.VMEM((2, 2 * width, 2 * sources), dtype),
                 pltpu.SemaphoreType.DMA((4, 2)),
                 pltpu.SemaphoreType.DMA((2, 2)),
-                pltpu.VMEM((2, rows, sources), jnp.float32),
-                pltpu.VMEM((2, rows, sources), jnp.float32),
-                pltpu.SemaphoreType.DMA((3,)),
+                pltpu.VMEM((rows, 2 * sources), jnp.float32),
+                pltpu.VMEM((rows, 2 * sources), jnp.float32),
+                pltpu.SemaphoreType.DMA((4,)),
                 pltpu.VMEM((2, 2, rows, sources), dtype),
                 pltpu.SemaphoreType.DMA((2, 2)),
             ],
@@ -312,7 +332,7 @@
 
 
 def dot_kernel(ids, norms, *refs):
-    groups, (out, rows, field, sem) = (refs[:6], refs[6:12]), refs[12:]
+    groups, (out, rows, field, sem, total) = (refs[:6], refs[6:12]), refs[12:]
     for freq, (field_ref, _, *sources) in enumerate(groups):
 
         @pl.when(ids[0] < 4)
@@ -326,16 +346,18 @@
                 pltpu.make_async_copy(source.at[0], rows.at[freq], sem.at[1, freq]).start()
 
     for freq, (field_ref, sums, *sources) in enumerate(groups):
-        out[freq : freq + 1] = jnp.sum(sums[...], axis=0, keepdims=True)
+        total[freq : freq + 1] = jnp.sum(sums[...], axis=0, keepdims=True)
 
         @pl.when(ids[0] < 4)
         def _(freq=freq, field_ref=field_ref, sources=sources):
             pltpu.make_async_copy(field_ref, field.at[freq], sem.at[0, freq]).wait()
             pltpu.make_async_copy(sources[0].at[0], rows.at[freq], sem.at[1, freq]).wait()
             more = sum(fold(rows[freq, part], field[freq, part]) for part in range(2))
-            out[freq : freq + 1] += jnp.sum(more, axis=0, keepdims=True)
-
-    out[2:4] = norms[...]
+            total[freq : freq + 1] += jnp.sum(more, axis=0, keepdims=True)
+
+    total[2:4] = norms[...]
+    for k in range(out.shape[0]):
+        out[k] = total[...]
 
 
 def dot_rows(ids, norms, groups):
@@ -344,16 +366,17 @@
     whole = lambda shape: pl.BlockSpec(shape, lambda i, ids: (0, 0))
     return pl.pallas_call(
         dot_kernel,
-        out_shape=jax.ShapeDtypeStruct((4, sources), jnp.float32),
+        out_shape=jax.ShapeDtypeStruct((copies_to_all(), 4, sources), jnp.float32),
         grid_spec=pltpu.PrefetchScalarGridSpec(
             num_scalar_prefetch=1,
             grid=(1,),
             in_specs=[whole((2, sources))] + [ANYWHERE, whole((8, sources)), *[ANYWHERE] * 4] * 2,
-            out_specs=whole((4, sources)),
+            out_specs=pl.BlockSpec((copies_to_all(), 4, sources), lambda i, ids: (0, 0, 0)),
             scratch_shapes=[
                 pltpu.VMEM((2, *late_shape), dtype),
                 pltpu.VMEM((2, *late_shape), jnp.float32),
                 pltpu.SemaphoreType.DMA((2, 2)),
+                pltpu.VMEM((4, sources), jnp.float32),
             ],
         ),
         compiler_params=pltpu.CompilerParams(vmem_limit_bytes=VMEM_LIMIT),
@@ -560,7 +583,8 @@
     own_rows = lax.dynamic_slice_in_dim(whole, first_row - holder * half, rows, 2)
     block_rows = jnp.where(holder == col_index, own_rows, swap(own_rows, "col", 1))
     numer = jnp.sum(block_rows.astype(jnp.float32) * field, axis=(1, 2))
-    return jnp.concatenate([numer, norms])
+    sums = jnp.concatenate([numer, norms])
+    return jnp.broadcast_to(sums[None], (copies_to_all(), *sums.shape))
 
 
 def body(cross_spectra, replicas, tile_order):

time: 193 us -> 191 us (0.990)
  transfers between devices with their start and end apart: 20 -> 20, of which waited for: 9 -> 9; matrix products, arithmetic and copies ran while one was open for 4% -> 4% of each run, Pallas kernels for 47% -> 48%
where the time goes in v12:
time: 191 us; the launch traced here: 190 us
  Pallas kernels  92 us (48%)
  waiting for transfers between devices  63.1 us (33%)
  starting transfers between devices  24.7 us (13%)
  other arithmetic  4.57 us (2%)
  local copies, waits for them, and re-layouts  4.31 us (2%)
    pallas_call x6, Pallas kernels, add_field(): pl.pallas_call(functools.partial(field_kernel, freq, count, has_total, ga...  55.7 us
    ppermute x15, waiting for transfers between devices, swap(): lax.ppermute(value, axis, [(source, source ^ mask) for source in range(si...  55.2 us
    pallas_call x2, Pallas kernels, add_late(): pl.pallas_call(functools.partial(late_kernel, freq), out_shape=(jax.Shape...  21.9 us
    ppermute x15, starting transfers between devices, swap(): lax.ppermute(value, axis, [(source, source ^ mask) for source in range(si...  15.2 us
    pallas_call x4, Pallas kernels, copies(): pl.pallas_call(functools.partial(copy_kernel, len(args), jobs), out_shape...  12.9 us
    all_to_all x1, starting transfers between devices, sum_all(): return jnp.sum(lax.all_to_all(copies, axes, 0, 0, tiled=True), axis=0)  8.48 us
    all_to_all x1, waiting for transfers between devices, sum_all(): return jnp.sum(lax.all_to_all(copies, axes, 0, 0, tiled=True), axis=0)  7.93 us
  transfers between devices with their start and end apart: 20, of which 9 were waited for; matrix products, arithmetic and copies ran while one was open for 4% of the time, Pallas kernels for 48%

profile of v12, /device:TPU:0, one launch (start us, length us, event | category | flops | bytes accessed | tf_op | source)
XLA Modules:
  0.0 190.5 jit_solution(16939220987772649218)
XLA Ops:
  0.6 0.5 collective-permute-start.2
  1.1 4.1 %collective-permute-start.1 = (bf16[2,2,512,512]{3,2,1,0:T(8,128)(2,1)}, bf16[2,2,512,512]{3,2,1,0:T(8,128)(2,1)}, u32[]{:S(2)}, u32[]{:S(2)}) collective-permute-start(bf16[2,2,512,512]{3,2,1,0:T(8,128)(2,1)} %bitcast.18), channel_id=1, source_target_pairs={{0,4},{2,6},{4,0},{6,2},{8,12},{10,14},{12,8},{14,10},{1,5},{3,7},... | collective-permute-start | bytes 6291464 | tf_op jit(solution)/shard_map/ppermute | solution.py:18
  5.3 1.5 collective-permute-start
  6.8 5.8 %shard_map.124.refs_3_ = f32[2,1024,512]{2,1,0:T(8,128)} custom-call(s32[1]{0:T(128)} %bitcast.2.ids, bf16[2,2,1024,4096]{3,2,1,0:T(8,128)(2,1)} %cross.15, bf16[2,2,512,512]{3,2,1,0:T(8,128)(2,1)} %bitcast.20), custom_call_target="tpu_custom_call" | custom-call | flops 1 | bytes 1 | tf_op jit(solution)/shard_map/pallas_call | solution.py:136
  12.6 0.0 copy-start
  12.6 0.0 copy-start.2
  12.6 5.9 %shard_map.123.refs_3_ = f32[2,1024,512]{2,1,0:T(8,128)} custom-call(s32[1]{0:T(128)} %bitcast.2.ids, bf16[2,2,1024,4096]{3,2,1,0:T(8,128)(2,1)} %cross.15, bf16[2,2,512,512]{3,2,1,0:T(8,128)(2,1)} %bitcast.21), custom_call_target="tpu_custom_call" | custom-call | flops 1 | bytes 1 | tf_op jit(solution)/shard_map/pallas_call | solution.py:136
  18.7 0.5 fusion.16
  19.2 0.6 concatenate.11.ids
  19.8 0.7 pad_add_fusion.ids
  20.5 0.6 pad_add_fusion.1.ids
  21.1 2.6 %multiply_reduce_fusion.norms = f32[2,512]{1,0:T(2,128)} fusion(bf16[2,2,1,512,512]{4,3,2,1,0:T(8,128)(2,1)} %param.12), kind=kLoop, calls=%fused_computation | loop fusion | flops 3144704 | bytes 2101248 | tf_op jit(solution)/shard_map/reduce_sum | solution.py:594
  23.7 3.1 %shard_map.122.refs_2_.refs_3_ = bf16[2,2,512,512]{3,2,1,0:T(8,128)(2,1)} custom-call(s32[2]{0:T(128)} %pad_add_fusion.ids, bf16[2,2,512,512]{3,2,1,0:T(8,128)(2,1)} %collective-permute-done.2.refs_0_, bf16[2,2,1024,4096]{3,2,1,0:T(8,128)(2,1)} %cross.15), custom_call_target="tpu_custom_call", output_to_operand_aliasing={{}: (1, {})} | custom-call | flops 1 | bytes 1 | tf_op jit(solution)/shard_map/pallas_call | solution.py:416
  26.8 24.2 %collective-permute-done.1.refs_1_.refs_2_ = bf16[2,2,512,512]{3,2,1,0:T(8,128)(2,1)} collective-permute-done((bf16[2,2,512,512]{3,2,1,0:T(8,128)(2,1)}, bf16[2,2,512,512]{3,2,1,0:T(8,128)(2,1)}, u32[]{:S(2)}, u32[]{:S(2)}) %collective-permute-start.1) | collective-permute-done | bytes 2097184 | tf_op jit(solution)/shard_map/ppermute | solution.py:18
  51.0 1.4 collective-permute-done.refs_0_.refs_1_
  52.4 0.3 collective-permute-start.3
  52.7 1.5 collective-permute-start.5
  54.2 12.3 %shard_map.125.refs_2_ = f32[2,1024,512]{2,1,0:T(8,128)} custom-call(s32[4]{0:T(128)} %pad_add_fusion.1.ids, bf16[2,2,1024,4096]{3,2,1,0:T(8,128)(2,1)} %cross.15, bf16[2,2,512,512]{3,2,1,0:T(8,128)(2,1)} %collective-permute-done.refs_0_.refs_1_, bf16[2,2,512,512]{3,2,1,0:T(8,128)(2,1)} %collective-permute-done.1.refs_1_.refs_2_, ...), custom_call_target="tpu_custom_call" | custom-call | flops 1 | bytes 1 | tf_op jit(solution)/shard_map/pallas_call | solution.py:136
  66.5 12.4 %shard_map.126.refs_2_ = f32[2,1024,512]{2,1,0:T(8,128)} custom-call(s32[4]{0:T(128)} %pad_add_fusion.1.ids, bf16[2,2,1024,4096]{3,2,1,0:T(8,128)(2,1)} %cross.15, bf16[2,2,512,512]{3,2,1,0:T(8,128)(2,1)} %collective-permute-done.refs_0_.refs_1_, bf16[2,2,512,512]{3,2,1,0:T(8,128)(2,1)} %collective-permute-done.1.refs_1_.refs_2_, ...), custom_call_target="tpu_custom_call" | custom-call | flops 1 | bytes 1 | tf_op jit(solution)/shard_map/pallas_call | solution.py:136
  78.9 3.6 %shard_map.127.refs_0_ = bf16[2,2,1024,512]{3,2,1,0:T(8,128)(2,1)} custom-call(s32[1]{0:T(128)} %bitcast.6.ids, bf16[2,2,512,512]{3,2,1,0:T(8,128)(2,1)} %bitcast.22, bf16[2,2,512,512]{3,2,1,0:T(8,128)(2,1)} %collective-permute-done.refs_0_.refs_1_, bf16[2,2,512,512]{3,2,1,0:T(8,128)(2,1)} %collective-permute-done.1.refs_1_.refs_2_, ...), custom_call_target="tpu_custom_call" | custom-call | flops 1 | bytes 1 | tf_op jit(solution)/shard_map/pallas_call | solution.py:416
  82.5 3.0 %fusion.18 = (bf16[1,2,512,512]{3,2,1,0:T(8,128)(2,1)}, bf16[1,2,512,512]{3,2,1,0:T(8,128)(2,1)}) fusion(bf16[2,2,512,512]{3,2,1,0:T(8,128)(2,1)} %collective-permute-done.refs_0_.refs_1_), kind=kLoop, calls=%fused_computation.40 | loop fusion | bytes 4194304 | tf_op jit(solution)/shard_map/slice | solution.py:538
  85.5 13.1 %collective-permute-done.3.refs_0_.block_re.block_im = bf16[2,2,512,512]{3,2,1,0:T(8,128)(2,1)} collective-permute-done((bf16[2,2,512,512]{3,2,1,0:T(8,128)(2,1)}, bf16[2,2,512,512]{3,2,1,0:T(8,128)(2,1)}, u32[]{:S(2)}, u32[]{:S(2)}) %collective-permute-start.3) | collective-permute-done | bytes 2097184 | tf_op jit(solution)/shard_map/ppermute | solution.py:18
  98.6 0.3 collective-permute-done.5.refs_0_.refs_1_.refs_3_.refs_4_
  98.9 0.5 collective-permute-start.8
  99.4 3.1 %shard_map.128 = (bf16[1,2,512,512]{3,2,1,0:T(8,128)(2,1)}, bf16[1,2,512,512]{3,2,1,0:T(8,128)(2,1)}) custom-call(s32[2]{0:T(128)} %pad_add_fusion.ids, bf16[2,2,512,512]{3,2,1,0:T(8,128)(2,1)} %collective-permute-done.3.refs_0_.block_re.block_im, bf16[2,2,512,512]{3,2,1,0:T(8,128)(2,1)} %collective-permute-done.4.refs_1_.refs_2_, ...), custom_call_target="tpu_custom_call" | custom-call | flops 1 | bytes 1 | tf_op jit(solution)/shard_map/pallas_call | solution.py:416
  102.6 4.8 %collective-permute-start.7 = (bf16[1,2,512,512]{3,2,1,0:T(8,128)(2,1)}, bf16[1,2,512,512]{3,2,1,0:T(8,128)(2,1)}, u32[]{:S(2)}, u32[]{:S(2)}) collective-permute-start(bf16[1,2,512,512]{3,2,1,0:T(8,128)(2,1)} %get-tuple-element.64), channel_id=1, source_target_pairs={{0,4},{2,6},{4,0},{6,2},{8,12},{10,14},{12,8},{14,10},{1,5},{3,7},... | collective-permute-start | bytes 3145736 | tf_op jit(solution)/shard_map/ppermute | solution.py:18
  107.4 0.5 collective-permute-start.6
  107.9 9.8 %shard_map.129.total = f32[2,1024,512]{2,1,0:T(8,128)} custom-call(s32[2]{0:T(128)} %get-tuple-element.67.ids, bf16[2,2,1024,4096]{3,2,1,0:T(8,128)(2,1)} %cross.15, bf16[2,2,512,512]{3,2,1,0:T(8,128)(2,1)} %collective-permute-done.5.refs_0_.refs_1_.refs_3_.refs_4_, bf16[1,2,512,512]{3,2,1,0:T(8,128)(2,1)} %get-tuple-element.63.refs_1_, ...), custom_call_target="tpu_custom_call" | custom-call | flops 1 | bytes 1 | tf_op jit(solution)/shard_map/pallas_call | solution.py:136
  117.7 3.1 %shard_map.130 = (bf16[1,2,512,512]{3,2,1,0:T(8,128)(2,1)}, bf16[1,2,512,512]{3,2,1,0:T(8,128)(2,1)}) custom-call(s32[2]{0:T(128)} %pad_add_fusion.ids, bf16[2,2,512,512]{3,2,1,0:T(8,128)(2,1)} %collective-permute-done.3.refs_0_.block_re.block_im, bf16[2,2,512,512]{3,2,1,0:T(8,128)(2,1)} %collective-permute-done.4.refs_1_.refs_2_, ...), custom_call_target="tpu_custom_call" | custom-call | flops 1 | bytes 1 | tf_op jit(solution)/shard_map/pallas_call | solution.py:416
  120.8 10.5 %collective-permute-done.7.w6.block_re = bf16[1,2,512,512]{3,2,1,0:T(8,128)(2,1)} collective-permute-done((bf16[1,2,512,512]{3,2,1,0:T(8,128)(2,1)}, bf16[1,2,512,512]{3,2,1,0:T(8,128)(2,1)}, u32[]{:S(2)}, u32[]{:S(2)}) %collective-permute-start.7) | collective-permute-done | bytes 1048608 | tf_op jit(solution)/shard_map/ppermute | solution.py:18
  131.2 1.5 collective-permute-done.6.w5.refs_3_
  132.7 0.5 collective-permute-start.14
  133.2 0.5 collective-permute-start.10
  133.7 0.4 collective-permute-start.11
  134.1 9.6 %shard_map.132.total = f32[2,1024,512]{2,1,0:T(8,128)} custom-call(s32[2]{0:T(128)} %get-tuple-element.67.ids, bf16[2,2,1024,4096]{3,2,1,0:T(8,128)(2,1)} %cross.15, bf16[2,2,512,512]{3,2,1,0:T(8,128)(2,1)} %collective-permute-done.5.refs_0_.refs_1_.refs_3_.refs_4_, bf16[1,2,512,512]{3,2,1,0:T(8,128)(2,1)} %get-tuple-element.74.refs_1_, ...), custom_call_target="tpu_custom_call" | custom-call | flops 1 | bytes 1 | tf_op jit(solution)/shard_map/pallas_call | solution.py:136
  143.7 10.9 %shard_map.131 = (f32[8,512]{1,0:T(8,128)}, f32[2,512,512]{2,1,0:T(8,128)}) custom-call(s32[8]{0:T(128)} %concatenate.11.ids, bf16[2,2,1024,4096]{3,2,1,0:T(8,128)(2,1)} %cross.15, bf16[1,2,512,512]{3,2,1,0:T(8,128)(2,1)} %collective-permute-done.6.w5.refs_3_, bf16[1,2,512,512]{3,2,1,0:T(8,128)(2,1)} %collective-permute-done.7.w6.block_re, ...), custom_call_target="tpu_custom_call" | custom-call | flops 1 | bytes 1 | tf_op jit(solution)/shard_map/pallas_call | solution.py:306
  154.6 4.0 %collective-permute-done.10.w5.refs_9_ = bf16[1,2,512,512]{3,2,1,0:T(8,128)(2,1)} collective-permute-done((bf16[1,2,512,512]{3,2,1,0:T(8,128)(2,1)}, bf16[1,2,512,512]{3,2,1,0:T(8,128)(2,1)}, u32[]{:S(2)}, u32[]{:S(2)}) %collective-permute-start.10) | collective-permute-done | bytes 1048608 | tf_op jit(solution)/shard_map/ppermute | solution.py:18
  158.6 0.3 collective-permute-done.11.w6.block_im
  158.9 0.5 collective-permute-start.16
  159.4 0.5 collective-permute-start.17
  159.9 11.0 %shard_map.133 = (f32[8,512]{1,0:T(8,128)}, f32[2,512,512]{2,1,0:T(8,128)}) custom-call(s32[8]{0:T(128)} %concatenate.11.ids, bf16[2,2,1024,4096]{3,2,1,0:T(8,128)(2,1)} %cross.15, bf16[1,2,512,512]{3,2,1,0:T(8,128)(2,1)} %collective-permute-done.10.w5.refs_9_, bf16[1,2,512,512]{3,2,1,0:T(8,128)(2,1)} %collective-permute-done.11.w6.block_im, ...), custom_call_target="tpu_custom_call" | custom-call | flops 1 | bytes 1 | tf_op jit(solution)/shard_map/pallas_call | solution.py:306
  171.0 1.5 shard_map.134
  172.4 8.5 %all-to-all-start = ((f32[16,4,512]{2,1,0:T(4,128)}), f32[16,4,512]{2,1,0:T(4,128)S(1)}, u32[]{:S(2)}, u32[]{:S(2)}) async-start(f32[16,4,512]{2,1,0:T(4,128)} %shard_map.134), calls=%async_computation | async-start | bytes 262144 | tf_op jit(solution)/shard_map/all_to_all | solution.py:41
  180.9 7.9 %all-to-all-done = f32[16,4,512]{2,1,0:T(4,128)S(1)} async-done(((f32[16,4,512]{2,1,0:T(4,128)}), f32[16,4,512]{2,1,0:T(4,128)S(1)}, u32[]{:S(2)}, u32[]{:S(2)}) %all-to-all-start) | async-done | bytes 131104 | tf_op jit(solution)/shard_map/all_to_all | solution.py:41
  188.9 0.1 abs_reduce_fusion
  189.0 0.1 reshape.41
  189.1 0.6 constant_dynamic-slice_fusion
  189.7 0.8 fusion
  (25 shorter events, 0.1 us)
Async XLA Ops:
  0.6 23.1 %collective-permute-start.2 = (bf16[2,2,512,512]{3,2,1,0:T(8,128)(2,1)}, bf16[2,2,512,512]{3,2,1,0:T(8,128)(2,1)}, u32[]{:S(2)}, u32[]{:S(2)}) collective-permute-start(bf16[2,2,512,512]{3,2,1,0:T(8,128)(2,1)} %bitcast.17), channel_id=1, source_target_pairs={{0,1},{1,0},{2,3},{3,2},{4,8},{5,9},{6,10},{7,11},{8,4},{9,5},{10,... | collective-permute-start | bytes 6291464 | tf_op jit(solution)/shard_map/ppermute | solution.py:25
  1.1 49.8 %collective-permute-start.1 = (bf16[2,2,512,512]{3,2,1,0:T(8,128)(2,1)}, bf16[2,2,512,512]{3,2,1,0:T(8,128)(2,1)}, u32[]{:S(2)}, u32[]{:S(2)}) collective-permute-start(bf16[2,2,512,512]{3,2,1,0:T(8,128)(2,1)} %bitcast.18), channel_id=1, source_target_pairs={{0,4},{2,6},{4,0},{6,2},{8,12},{10,14},{12,8},{14,10},{1,5},{3,7},... | collective-permute-start | bytes 6291464 | tf_op jit(solution)/shard_map/ppermute | solution.py:18
  5.3 47.1 %collective-permute-start = (bf16[2,2,512,512]{3,2,1,0:T(8,128)(2,1)}, bf16[2,2,512,512]{3,2,1,0:T(8,128)(2,1)}, u32[]{:S(2)}, u32[]{:S(2)}) collective-permute-start(bf16[2,2,512,512]{3,2,1,0:T(8,128)(2,1)} %bitcast.19), channel_id=1, source_target_pairs={{0,2},{2,0},{4,6},{6,4},{8,10},{10,8},{12,14},{14,12},{1,3},{3,1},... | collective-permute-start | bytes 6291464 | tf_op jit(solution)/shard_map/ppermute | solution.py:18
  12.6 6.1 %copy-start = (s32[2]{0:T(128)S(1)}, s32[2]{0:T(128)}, u32[]{:S(2)}) copy-start(s32[2]{0:T(128)} %constant.117.clone) | copy-start | bytes 28
  12.6 7.9 %copy-start.2 = (s32[3]{0:T(128)S(1)}, s32[3]{0:T(128)}, u32[]{:S(2)}) copy-start(s32[3]{0:T(128)} %constant.116.clone) | copy-start | bytes 40
  52.4 46.2 %collective-permute-start.3 = (bf16[2,2,512,512]{3,2,1,0:T(8,128)(2,1)}, bf16[2,2,512,512]{3,2,1,0:T(8,128)(2,1)}, u32[]{:S(2)}, u32[]{:S(2)}) collective-permute-start(bf16[2,2,512,512]{3,2,1,0:T(8,128)(2,1)} %shard_map.122.refs_2_.refs_3_), channel_id=1, source_target_pairs={{0,4},{2,6},{4,0},{6,2},{8,12},{10,14},{12,8},{14,10},{1,5},{3,7},... | collective-permute-start | bytes 6291464 | tf_op jit(solution)/shard_map/ppermute | solution.py:18
  52.7 46.2 %collective-permute-start.5 = (bf16[2,2,512,512]{3,2,1,0:T(8,128)(2,1)}, bf16[2,2,512,512]{3,2,1,0:T(8,128)(2,1)}, u32[]{:S(2)}, u32[]{:S(2)}) collective-permute-start(bf16[2,2,512,512]{3,2,1,0:T(8,128)(2,1)} %collective-permute-done.1.refs_1_.refs_2_), channel_id=1, source_target_pairs={{0,2},{2,0},{4,6},{6,4},{8,10},{10,8},{12,14},{14,12},{1,3},{3,1},... | collective-permute-start | bytes 6291464 | tf_op jit(solution)/shard_map/ppermute | solution.py:18
  54.2 44.7 %collective-permute-start.4 = (bf16[2,2,512,512]{3,2,1,0:T(8,128)(2,1)}, bf16[2,2,512,512]{3,2,1,0:T(8,128)(2,1)}, u32[]{:S(2)}, u32[]{:S(2)}) collective-permute-start(bf16[2,2,512,512]{3,2,1,0:T(8,128)(2,1)} %collective-permute-done.1.refs_1_.refs_2_), channel_id=1, source_target_pairs={{0,1},{1,0},{2,3},{3,2},{4,8},{5,9},{6,10},{7,11},{8,4},{9,5},{10,... | collective-permute-start | bytes 6291464 | tf_op jit(solution)/shard_map/ppermute | solution.py:25
  98.9 33.8 %collective-permute-start.9 = (bf16[2,2,1024,512]{3,2,1,0:T(8,128)(2,1)}, bf16[2,2,1024,512]{3,2,1,0:T(8,128)(2,1)}, u32[]{:S(2)}, u32[]{:S(2)}) collective-permute-start(bf16[2,2,1024,512]{3,2,1,0:T(8,128)(2,1)} %shard_map.127.refs_0_), channel_id=1, source_target_pairs={{0,1},{1,0},{2,3},{3,2},{4,5},{5,4},{6,7},{7,6},{8,9},{9,8},{10,11... | collective-permute-start | bytes 12582920 | tf_op jit(solution)/shard_map/ppermute | solution.py:18
  98.9 21.8 %collective-permute-start.8 = (bf16[1,2,512,512]{3,2,1,0:T(8,128)(2,1)}, bf16[1,2,512,512]{3,2,1,0:T(8,128)(2,1)}, u32[]{:S(2)}, u32[]{:S(2)}) collective-permute-start(bf16[1,2,512,512]{3,2,1,0:T(8,128)(2,1)} %get-tuple-element.65), channel_id=1, source_target_pairs={{0,1},{1,0},{2,3},{3,2},{4,8},{5,9},{6,10},{7,11},{8,4},{9,5},{10,... | collective-permute-start | bytes 3145736 | tf_op jit(solution)/shard_map/ppermute | solution.py:25
  102.6 28.6 %collective-permute-start.7 = (bf16[1,2,512,512]{3,2,1,0:T(8,128)(2,1)}, bf16[1,2,512,512]{3,2,1,0:T(8,128)(2,1)}, u32[]{:S(2)}, u32[]{:S(2)}) collective-permute-start(bf16[1,2,512,512]{3,2,1,0:T(8,128)(2,1)} %get-tuple-element.64), channel_id=1, source_target_pairs={{0,4},{2,6},{4,0},{6,2},{8,12},{10,14},{12,8},{14,10},{1,5},{3,7},... | collective-permute-start | bytes 3145736 | tf_op jit(solution)/shard_map/ppermute | solution.py:18
  107.4 25.3 %collective-permute-start.6 = (bf16[1,2,512,512]{3,2,1,0:T(8,128)(2,1)}, bf16[1,2,512,512]{3,2,1,0:T(8,128)(2,1)}, u32[]{:S(2)}, u32[]{:S(2)}) collective-permute-start(bf16[1,2,512,512]{3,2,1,0:T(8,128)(2,1)} %get-tuple-element.63.refs_1_), channel_id=1, source_target_pairs={{0,2},{2,0},{4,6},{6,4},{8,10},{10,8},{12,14},{14,12},{1,3},{3,1},... | collective-permute-start | bytes 3145736 | tf_op jit(solution)/shard_map/ppermute | solution.py:18
  132.7 11.0 %collective-permute-start.13 = (bf16[2,2,512,512]{3,2,1,0:T(8,128)(2,1)}, bf16[2,2,512,512]{3,2,1,0:T(8,128)(2,1)}, u32[]{:S(2)}, u32[]{:S(2)}) collective-permute-start(bf16[2,2,512,512]{3,2,1,0:T(8,128)(2,1)} %collective-permute-done.5.refs_0_.refs_1_.refs_3_.refs_4_), channel_id=1, source_target_pairs={{0,1},{1,0},{2,3},{3,2},{4,5},{5,4},{6,7},{7,6},{8,9},{9,8},{10,11... | collective-permute-start | bytes 6291464 | tf_op jit(solution)/shard_map/ppermute | solution.py:18
  132.7 11.0 %collective-permute-start.14 = (bf16[2,2,512,512]{3,2,1,0:T(8,128)(2,1)}, bf16[2,2,512,512]{3,2,1,0:T(8,128)(2,1)}, u32[]{:S(2)}, u32[]{:S(2)}) collective-permute-start(bf16[2,2,512,512]{3,2,1,0:T(8,128)(2,1)} %collective-permute-done.4.refs_1_.refs_2_), channel_id=1, source_target_pairs={{0,1},{1,0},{2,3},{3,2},{4,5},{5,4},{6,7},{7,6},{8,9},{9,8},{10,11... | collective-permute-start | bytes 6291464 | tf_op jit(solution)/shard_map/ppermute | solution.py:18
  133.2 25.4 %collective-permute-start.10 = (bf16[1,2,512,512]{3,2,1,0:T(8,128)(2,1)}, bf16[1,2,512,512]{3,2,1,0:T(8,128)(2,1)}, u32[]{:S(2)}, u32[]{:S(2)}) collective-permute-start(bf16[1,2,512,512]{3,2,1,0:T(8,128)(2,1)} %get-tuple-element.74.refs_1_), channel_id=1, source_target_pairs={{0,2},{2,0},{4,6},{6,4},{8,10},{10,8},{12,14},{14,12},{1,3},{3,1},... | collective-permute-start | bytes 3145736 | tf_op jit(solution)/shard_map/ppermute | solution.py:18
  133.7 25.1 %collective-permute-start.11 = (bf16[1,2,512,512]{3,2,1,0:T(8,128)(2,1)}, bf16[1,2,512,512]{3,2,1,0:T(8,128)(2,1)}, u32[]{:S(2)}, u32[]{:S(2)}) collective-permute-start(bf16[1,2,512,512]{3,2,1,0:T(8,128)(2,1)} %get-tuple-element.75), channel_id=1, source_target_pairs={{0,4},{2,6},{4,0},{6,2},{8,12},{10,14},{12,8},{14,10},{1,5},{3,7},... | collective-permute-start | bytes 3145736 | tf_op jit(solution)/shard_map/ppermute | solution.py:18
  134.1 24.7 %collective-permute-start.12 = (bf16[1,2,512,512]{3,2,1,0:T(8,128)(2,1)}, bf16[1,2,512,512]{3,2,1,0:T(8,128)(2,1)}, u32[]{:S(2)}, u32[]{:S(2)}) collective-permute-start(bf16[1,2,512,512]{3,2,1,0:T(8,128)(2,1)} %get-tuple-element.76), channel_id=1, source_target_pairs={{0,1},{1,0},{2,3},{3,2},{4,8},{5,9},{6,10},{7,11},{8,4},{9,5},{10,... | collective-permute-start | bytes 3145736 | tf_op jit(solution)/shard_map/ppermute | solution.py:25
  158.9 12.0 %collective-permute-start.15 = (bf16[1,2,512,512]{3,2,1,0:T(8,128)(2,1)}, bf16[1,2,512,512]{3,2,1,0:T(8,128)(2,1)}, u32[]{:S(2)}, u32[]{:S(2)}) collective-permute-start(bf16[1,2,512,512]{3,2,1,0:T(8,128)(2,1)} %collective-permute-done.8.w7.refs_2_), channel_id=1, source_target_pairs={{0,1},{1,0},{2,3},{3,2},{4,5},{5,4},{6,7},{7,6},{8,9},{9,8},{10,11... | collective-permute-start | bytes 3145736 | tf_op jit(solution)/shard_map/ppermute | solution.py:18
  158.9 12.1 %collective-permute-start.16 = (bf16[1,2,512,512]{3,2,1,0:T(8,128)(2,1)}, bf16[1,2,512,512]{3,2,1,0:T(8,128)(2,1)}, u32[]{:S(2)}, u32[]{:S(2)}) collective-permute-start(bf16[1,2,512,512]{3,2,1,0:T(8,128)(2,1)} %collective-permute-done.6.w5.refs_3_), channel_id=1, source_target_pairs={{0,1},{1,0},{2,3},{3,2},{4,5},{5,4},{6,7},{7,6},{8,9},{9,8},{10,11... | collective-permute-start | bytes 3145736 | tf_op jit(solution)/shard_map/ppermute | solution.py:18
  159.4 11.6 %collective-permute-start.18 = (bf16[1,2,512,512]{3,2,1,0:T(8,128)(2,1)}, bf16[1,2,512,512]{3,2,1,0:T(8,128)(2,1)}, u32[]{:S(2)}, u32[]{:S(2)}) collective-permute-start(bf16[1,2,512,512]{3,2,1,0:T(8,128)(2,1)} %collective-permute-done.10.w5.refs_9_), channel_id=1, source_target_pairs={{0,1},{1,0},{2,3},{3,2},{4,5},{5,4},{6,7},{7,6},{8,9},{9,8},{10,11... | collective-permute-start | bytes 3145736 | tf_op jit(solution)/shard_map/ppermute | solution.py:18
  159.4 11.6 %collective-permute-start.17 = (bf16[1,2,512,512]{3,2,1,0:T(8,128)(2,1)}, bf16[1,2,512,512]{3,2,1,0:T(8,128)(2,1)}, u32[]{:S(2)}, u32[]{:S(2)}) collective-permute-start(bf16[1,2,512,512]{3,2,1,0:T(8,128)(2,1)} %collective-permute-done.12.w7.refs_8_), channel_id=1, source_target_pairs={{0,1},{1,0},{2,3},{3,2},{4,5},{5,4},{6,7},{7,6},{8,9},{9,8},{10,11... | collective-permute-start | bytes 3145736 | tf_op jit(solution)/shard_map/ppermute | solution.py:18
  170.9 18.8 %copy-start.1 = (s32[16]{0:T(128)S(1)}, s32[16]{0:T(128)}, u32[]{:S(2)}) copy-start(s32[16]{0:T(128)} %param.13) | copy-start | bytes 196
  172.4 16.4 %all-to-all-start = ((f32[16,4,512]{2,1,0:T(4,128)}), f32[16,4,512]{2,1,0:T(4,128)S(1)}, u32[]{:S(2)}, u32[]{:S(2)}) async-start(f32[16,4,512]{2,1,0:T(4,128)} %shard_map.134), calls=%async_computation | async-start | bytes 262144 | tf_op jit(solution)/shard_map/all_to_all | solution.py:41

commit v13 on v12

--- a/solution.py
+++ b/solution.py
@@ -331,7 +331,7 @@
     )(ids, cross, *pieces, *blocks, total, *row_refs)
 
 
-def dot_kernel(ids, norms, *refs):
+def dot_kernel(ids, *refs):
     groups, (out, rows, field, sem, total) = (refs[:6], refs[6:12]), refs[12:]
     for freq, (field_ref, _, *sources) in enumerate(groups):
 
@@ -355,33 +355,34 @@
             more = sum(fold(rows[freq, part], field[freq, part]) for part in range(2))
             total[freq : freq + 1] += jnp.sum(more, axis=0, keepdims=True)
 
-    total[2:4] = norms[...]
     for k in range(out.shape[0]):
         out[k] = total[...]
 
 
-def dot_rows(ids, norms, groups):
+def dot_rows(ids, groups):
     late_shape, dtype = groups[0][0].shape, groups[0][2].dtype
     sources = late_shape[-1]
     whole = lambda shape: pl.BlockSpec(shape, lambda i, ids: (0, 0))
     return pl.pallas_call(
         dot_kernel,
-        out_shape=jax.ShapeDtypeStruct((copies_to_all(), 4, sources), jnp.float32),
+        out_shape=jax.ShapeDtypeStruct((copies_to_all(), len(groups), sources), jnp.float32),
         grid_spec=pltpu.PrefetchScalarGridSpec(
             num_scalar_prefetch=1,
             grid=(1,),
-            in_specs=[whole((2, sources))] + [ANYWHERE, whole((8, sources)), *[ANYWHERE] * 4] * 2,
-            out_specs=pl.BlockSpec((copies_to_all(), 4, sources), lambda i, ids: (0, 0, 0)),
+            in_specs=[ANYWHERE, whole((8, sources)), *[ANYWHERE] * 4] * 2,
+            out_specs=pl.BlockSpec(
+                (copies_to_all(), len(groups), sources), lambda i, ids: (0, 0, 0)
+            ),
             scratch_shapes=[
                 pltpu.VMEM((2, *late_shape), dtype),
                 pltpu.VMEM((2, *late_shape), jnp.float32),
                 pltpu.SemaphoreType.DMA((2, 2)),
-                pltpu.VMEM((4, sources), jnp.float32),
+                pltpu.VMEM((len(groups), sources), jnp.float32),
             ],
         ),
         compiler_params=pltpu.CompilerParams(vmem_limit_bytes=VMEM_LIMIT),
         cost_estimate=HINT,
-    )(ids, norms, *groups[0], *groups[1])
+    )(ids, *groups[0], *groups[1])
 
 
 def copy_kernel(inputs, jobs, ids, *refs):
@@ -470,16 +471,63 @@
     return copies(ids, [own, x, n, m], jobs, [shape], (width, sources), own.dtype)[0]
 
 
+def next_kernel(freq, ids, ends, middles, cross, over_x, over_z, stage, in_sem, out_sem):
+    width = ends.shape[2]
+    columns = pl.ds(pl.multiple_of(ids[1] * width, width), width)
+    block = [cross.at[1, freq, pl.ds(half * width, width), columns] for half in range(2)]
+    plans = [
+        [(ends.at[freq, 0], 0), (ends.at[freq, 1], 1), (block[0], 2), (block[1], 3)],
+        [(middles.at[freq, 0], 0), (middles.at[freq, 1], 1)],
+    ]
+    for mid, plan in enumerate(plans):
+
+        @pl.when(ids[0] == mid)
+        def _(mid=mid, plan=plan):
+            reads = [
+                pltpu.make_async_copy(source, stage.at[k], in_sem.at[k]) for source, k in plan
+            ]
+            writes = [
+                [pltpu.make_async_copy(stage.at[k], over_x.at[0, k], out_sem.at[k])]
+                if k < 2
+                else [pltpu.make_async_copy(stage.at[k], over_z.at[0, k - 2], out_sem.at[k])]
+                for _, k in plan
+            ]
+            if mid:
+                for k in range(2):
+                    writes[k].append(
+                        pltpu.make_async_copy(stage.at[k], over_z.at[0, k], out_sem.at[2 + k])
+                    )
+            for copy in reads:
+                copy.start()
+            for read, group in zip(reads, writes):
+                read.wait()
+                for copy in group:
+                    copy.start()
+            for group in writes:
+                for copy in group:
+                    copy.wait()
+
+
 def take_next(freq, ids, ends, middles, cross):
     _, _, width, sources = ends.shape
-    jobs = []
-    for part in range(2):
-        block = block_source(2, 1, freq, part, width)
-        jobs.append(([(0, block), (1, entry(1, freq, part))], entry(1, 0, part)))
-        jobs.append(([(0, entry(0, freq, part)), (1, entry(1, freq, part))], entry(0, 0, part)))
-    shape = (1, 2, width, sources)
-    args = [ends, middles, cross]
-    return copies(ids, args, jobs, [shape, shape], (width, sources), ends.dtype)
+    shape = jax.ShapeDtypeStruct((1, 2, width, sources), ends.dtype)
+    return pl.pallas_call(
+        functools.partial(next_kernel, freq),
+        out_shape=[shape, shape],
+        grid_spec=pltpu.PrefetchScalarGridSpec(
+            num_scalar_prefetch=1,
+            grid=(1,),
+            in_specs=[ANYWHERE] * 3,
+            out_specs=[ANYWHERE] * 2,
+            scratch_shapes=[
+                pltpu.VMEM((4, width, sources), ends.dtype),
+                pltpu.SemaphoreType.DMA((4,)),
+                pltpu.SemaphoreType.DMA((4,)),
+            ],
+        ),
+        compiler_params=pltpu.CompilerParams(vmem_limit_bytes=VMEM_LIMIT),
+        cost_estimate=HINT,
+    )(ids, ends, middles, cross)
 
 
 def sums_by_swaps(cross, replicas, norms):
@@ -526,6 +574,7 @@
     a0 = add_field(cross, 0, ids(0), [own])
     a1 = add_field(cross, 1, ids(0), [own])
     m = fill_block(ids_z, m, cross)
+    norms += swap(norms, "col", 1)
     x, n, m, a0, a1, norms, *numbers = barrier(x, n, m, a0, a1, norms, *numbers)
     ids_a, ids_b, ids_z, late_ids, pair, ids_dot = numbers
 
@@ -536,18 +585,20 @@
     a1 = add_field(cross, 1, ids_a, [x, n, m], a1, gated=True)
     mine = take_pair(pair, own, x, n, m)
     x_a, x_b = x[0:1], x[1:2]
-    z, m2, xn, a0, a1, mine, x_a, x_b = barrier(z, m2, xn, a0, a1, mine, x_a, x_b)
+    norms += swap(norms, "row", 1)
+    z, m2, xn, a0, a1, mine, x_a, x_b, norms = barrier(z, m2, xn, a0, a1, mine, x_a, x_b, norms)
 
     w4_a, send_a = take_next(0, ids_z, z, m2, cross)
     x5_a = swap(w4_a, "row", 1)
     z_a = swap(send_a, "row", 2)
-    w7_a = swap_middle(x_a)
+    w7_a = swap_middle(after(x_a, w4_a))
     other = swap(mine, "col", 1)
     b0 = add_field(cross, 0, ids_b, [xn, w4_a], a0)
     w4_b, send_b = take_next(1, after(ids_z, b0), z, m2, cross)
     b1 = add_field(cross, 1, ids_b, [xn, w4_b], a1)
-    x5_a, z_a, w7_a, other, b0, w4_b, send_b, x_b, xn, m2 = barrier(
-        x5_a, z_a, w7_a, other, b0, w4_b, send_b, x_b, xn, m2
+    norms += swap(norms, "row", 2)
+    x5_a, z_a, w7_a, other, b0, w4_b, send_b, x_b, xn, m2, norms = barrier(
+        x5_a, z_a, w7_a, other, b0, w4_b, send_b, x_b, xn, m2, norms
     )
 
     x5_b = swap(w4_b, "row", 1)
@@ -557,8 +608,9 @@
     other_m2 = swap(m2, "col", 1)
     early = [mine, xn, m2, xn, xn, other, other_xn, other_m2, other_xn, other_xn]
     sums_a, field_a = add_late(cross, 0, late_ids, [x5_a, z_a, w7_a], [z, z], b0, early)
-    x5_b, z_b, w7_b, sums_a, field_a, b1, other_xn, other_m2, x5_a, w7_a = barrier(
-        x5_b, z_b, w7_b, sums_a, field_a, b1, other_xn, other_m2, x5_a, w7_a
+    norms += swap(after(norms, other_xn, other_m2), "row", 4)
+    x5_b, z_b, w7_b, sums_a, field_a, b1, other_xn, other_m2, x5_a, w7_a, norms = barrier(
+        x5_b, z_b, w7_b, sums_a, field_a, b1, other_xn, other_m2, x5_a, w7_a, norms
     )
 
     late = [w7_a, x5_a, w7_b, x5_b]
@@ -569,7 +621,7 @@
         (field_a, sums_a, *late[:2], *others[:2]),
         (field_b, sums_b, *late[2:], *others[2:]),
     ]
-    return dot_rows(ids_dot, norms, groups)
+    return dot_rows(ids_dot, groups), norms
 
 
 def sums_by_gather(cross, replicas, norms):
@@ -583,8 +635,7 @@
     own_rows = lax.dynamic_slice_in_dim(whole, first_row - holder * half, rows, 2)
     block_rows = jnp.where(holder == col_index, own_rows, swap(own_rows, "col", 1))
     numer = jnp.sum(block_rows.astype(jnp.float32) * field, axis=(1, 2))
-    sums = jnp.concatenate([numer, norms])
-    return jnp.broadcast_to(sums[None], (copies_to_all(), *sums.shape))
+    return jnp.broadcast_to(numer[None], (copies_to_all(), *numer.shape)), lax.psum(norms, ("row", "col"))
 
 
 def body(cross_spectra, replicas, tile_order):
@@ -598,10 +649,8 @@
         and replicas.shape[3] % 128 == 0
         and cross_spectra.shape[2] == 2 * replicas.shape[3]
     )
-    sums = (sums_by_swaps if doubling else sums_by_gather)(cross_spectra, replicas, norms)
-    sums = sum_all(sums)
-    numer, norms = sums[:fnum], sums[fnum:]
-    beam = numer / (norms + 1e-06)
+    copies, norms = (sums_by_swaps if doubling else sums_by_gather)(cross_spectra, replicas, norms)
+    beam = sum_all(copies) / (norms + 1e-06)
     width = sources // lax.axis_size("col")
     beam_half = lax.dynamic_slice_in_dim(beam, lax.axis_index("col") * width, width, 1)
     peak = jnp.max(jnp.abs(beam), axis=1) + 1e-06

time: 191 us -> 193 us (1.010)
    pallas_call x4 -> x2, Pallas kernels: 12.9 us -> 6.69 us  [copies(): pl.pallas_call(functools.partial(copy_kernel, len(args), jobs), out_shape...]
    pallas_call x0 -> x2, Pallas kernels: none -> 6.19 us  [take_next(): pl.pallas_call(functools.partial(next_kernel, freq), out_shape=[shape, sh...]
    ppermute x15 -> x19, waiting for transfers between devices: 55.2 us -> 57.1 us  [swap(): lax.ppermute(value, axis, [(source, source ^ mask) for source in range(si...]
    ppermute x15 -> x19, starting transfers between devices: 15.2 us -> 15.5 us  [swap(): lax.ppermute(value, axis, [(source, source ^ mask) for source in range(si...]
  transfers between devices with their start and end apart: 20 -> 24, of which waited for: 9 -> 8; matrix products, arithmetic and copies ran while one was open for 4% -> 4% of each run, Pallas kernels for 48% -> 47%
where the time goes in v13:
time: 193 us; the launch traced here: 192 us
  Pallas kernels  91.7 us (48%)
  waiting for transfers between devices  64 us (33%)
  starting transfers between devices  26.4 us (14%)
  local copies, waits for them, and re-layouts  4.38 us (2%)
  other arithmetic  3.97 us (2%)
    ppermute x19, waiting for transfers between devices, swap(): lax.ppermute(value, axis, [(source, source ^ mask) for source in range(si...  57.1 us
    pallas_call x6, Pallas kernels, add_field(): pl.pallas_call(functools.partial(field_kernel, freq, count, has_total, ga...  55.5 us
    pallas_call x2, Pallas kernels, add_late(): pl.pallas_call(functools.partial(late_kernel, freq), out_shape=(jax.Shape...  21.9 us
    ppermute x19, starting transfers between devices, swap(): lax.ppermute(value, axis, [(source, source ^ mask) for source in range(si...  15.5 us
    all_to_all x1, starting transfers between devices, sum_all(): return jnp.sum(lax.all_to_all(copies, axes, 0, 0, tiled=True), axis=0)  9.8 us
    all_to_all x1, waiting for transfers between devices, sum_all(): return jnp.sum(lax.all_to_all(copies, axes, 0, 0, tiled=True), axis=0)  6.9 us
    pallas_call x2, Pallas kernels, copies(): pl.pallas_call(functools.partial(copy_kernel, len(args), jobs), out_shape...  6.69 us
    pallas_call x2, Pallas kernels, take_next(): pl.pallas_call(functools.partial(next_kernel, freq), out_shape=[shape, sh...  6.19 us
  transfers between devices with their start and end apart: 24, of which 8 were waited for; matrix products, arithmetic and copies ran while one was open for 4% of the time, Pallas kernels for 47%

profile of v13, /device:TPU:0, one launch (start us, length us, event | category | flops | bytes accessed | tf_op | source)
XLA Modules:
  0.0 192.5 jit_solution(14786255023054725375)
XLA Ops:
  0.7 0.5 collective-permute-start.2
  1.2 4.1 %collective-permute-start.1 = (bf16[2,2,512,512]{3,2,1,0:T(8,128)(2,1)}, bf16[2,2,512,512]{3,2,1,0:T(8,128)(2,1)}, u32[]{:S(2)}, u32[]{:S(2)}) collective-permute-start(bf16[2,2,512,512]{3,2,1,0:T(8,128)(2,1)} %bitcast.18), channel_id=1, source_target_pairs={{0,4},{2,6},{4,0},{6,2},{8,12},{10,14},{12,8},{14,10},{1,5},{3,7},... | collective-permute-start | bytes 6291464 | tf_op jit(solution)/shard_map/ppermute | solution.py:18
  5.3 1.5 collective-permute-start
  6.8 2.1 %multiply_reduce_fusion = f32[2,512]{1,0:T(2,128)S(1)} fusion(bf16[2,2,1,512,512]{4,3,2,1,0:T(8,128)(2,1)} %param.12), kind=kLoop, calls=%fused_computation | loop fusion | flops 3144704 | bytes 2101248 | tf_op jit(solution)/shard_map/reduce_sum | solution.py:645
  9.0 0.6 pad_add_fusion.ids
  9.7 0.5 fusion.15
  10.2 0.6 pad_add_fusion.1.ids
  10.8 5.8 %shard_map.124.refs_3_ = f32[2,1024,512]{2,1,0:T(8,128)} custom-call(s32[1]{0:T(128)} %bitcast.2.ids, bf16[2,2,1024,4096]{3,2,1,0:T(8,128)(2,1)} %cross.19, bf16[2,2,512,512]{3,2,1,0:T(8,128)(2,1)} %bitcast.20), custom_call_target="tpu_custom_call" | custom-call | flops 1 | bytes 1 | tf_op jit(solution)/shard_map/pallas_call | solution.py:136
  16.6 5.9 %shard_map.123.refs_3_ = f32[2,1024,512]{2,1,0:T(8,128)} custom-call(s32[1]{0:T(128)} %bitcast.2.ids, bf16[2,2,1024,4096]{3,2,1,0:T(8,128)(2,1)} %cross.19, bf16[2,2,512,512]{3,2,1,0:T(8,128)(2,1)} %bitcast.21), custom_call_target="tpu_custom_call" | custom-call | flops 1 | bytes 1 | tf_op jit(solution)/shard_map/pallas_call | solution.py:136
  22.6 0.6 concatenate.11.ids
  23.2 3.1 %shard_map.122.refs_2_.refs_3_ = bf16[2,2,512,512]{3,2,1,0:T(8,128)(2,1)} custom-call(s32[2]{0:T(128)} %pad_add_fusion.ids, bf16[2,2,512,512]{3,2,1,0:T(8,128)(2,1)} %collective-permute-done.2.refs_0_, bf16[2,2,1024,4096]{3,2,1,0:T(8,128)(2,1)} %cross.19), custom_call_target="tpu_custom_call", output_to_operand_aliasing={{}: (1, {})} | custom-call | flops 1 | bytes 1 | tf_op jit(solution)/shard_map/pallas_call | solution.py:417
  26.3 24.7 %collective-permute-done.1.refs_1_.refs_2_ = bf16[2,2,512,512]{3,2,1,0:T(8,128)(2,1)} collective-permute-done((bf16[2,2,512,512]{3,2,1,0:T(8,128)(2,1)}, bf16[2,2,512,512]{3,2,1,0:T(8,128)(2,1)}, u32[]{:S(2)}, u32[]{:S(2)}) %collective-permute-start.1) | collective-permute-done | bytes 2097184 | tf_op jit(solution)/shard_map/ppermute | solution.py:18
  51.0 1.4 collective-permute-done.refs_0_.refs_1_
  52.4 0.3 collective-permute-start.4
  52.7 1.5 collective-permute-start.6
  54.2 0.5 collective-permute-start.7
  54.8 3.1 %fusion.16 = (bf16[1,2,512,512]{3,2,1,0:T(8,128)(2,1)}, bf16[1,2,512,512]{3,2,1,0:T(8,128)(2,1)}) fusion(bf16[2,2,512,512]{3,2,1,0:T(8,128)(2,1)} %collective-permute-done.refs_0_.refs_1_), kind=kLoop, calls=%fused_computation.39 | loop fusion | bytes 4194304 | tf_op jit(solution)/shard_map/slice | solution.py:587
  57.8 12.3 %shard_map.125.refs_2_ = f32[2,1024,512]{2,1,0:T(8,128)} custom-call(s32[4]{0:T(128)} %pad_add_fusion.1.ids, bf16[2,2,1024,4096]{3,2,1,0:T(8,128)(2,1)} %cross.19, bf16[2,2,512,512]{3,2,1,0:T(8,128)(2,1)} %collective-permute-done.refs_0_.refs_1_, bf16[2,2,512,512]{3,2,1,0:T(8,128)(2,1)} %collective-permute-done.1.refs_1_.refs_2_, ...), custom_call_target="tpu_custom_call" | custom-call | flops 1 | bytes 1 | tf_op jit(solution)/shard_map/pallas_call | solution.py:136
  70.2 12.4 %shard_map.126.refs_2_ = f32[2,1024,512]{2,1,0:T(8,128)} custom-call(s32[4]{0:T(128)} %pad_add_fusion.1.ids, bf16[2,2,1024,4096]{3,2,1,0:T(8,128)(2,1)} %cross.19, bf16[2,2,512,512]{3,2,1,0:T(8,128)(2,1)} %collective-permute-done.refs_0_.refs_1_, bf16[2,2,512,512]{3,2,1,0:T(8,128)(2,1)} %collective-permute-done.1.refs_1_.refs_2_, ...), custom_call_target="tpu_custom_call" | custom-call | flops 1 | bytes 1 | tf_op jit(solution)/shard_map/pallas_call | solution.py:136
  82.5 3.6 %shard_map.127.refs_0_ = bf16[2,2,1024,512]{3,2,1,0:T(8,128)(2,1)} custom-call(s32[1]{0:T(128)} %bitcast.6.ids, bf16[2,2,512,512]{3,2,1,0:T(8,128)(2,1)} %bitcast.22, bf16[2,2,512,512]{3,2,1,0:T(8,128)(2,1)} %collective-permute-done.refs_0_.refs_1_, bf16[2,2,512,512]{3,2,1,0:T(8,128)(2,1)} %collective-permute-done.1.refs_1_.refs_2_, ...), custom_call_target="tpu_custom_call" | custom-call | flops 1 | bytes 1 | tf_op jit(solution)/shard_map/pallas_call | solution.py:417
  86.1 12.9 %collective-permute-done.7 = f32[2,512]{1,0:T(2,128)S(1)} collective-permute-done((f32[2,512]{1,0:T(2,128)S(1)}, f32[2,512]{1,0:T(2,128)S(1)}, u32[]{:S(2)}, u32[]{:S(2)}) %collective-permute-start.7) | collective-permute-done | bytes 4128 | tf_op jit(solution)/shard_map/ppermute | solution.py:18
  99.1 3.1 %shard_map.128 = (bf16[1,2,512,512]{3,2,1,0:T(8,128)(2,1)}, bf16[1,2,512,512]{3,2,1,0:T(8,128)(2,1)}) custom-call(s32[2]{0:T(128)} %pad_add_fusion.ids, bf16[2,2,512,512]{3,2,1,0:T(8,128)(2,1)} %collective-permute-done.4.ends.block_re.block_im, bf16[2,2,512,512]{3,2,1,0:T(8,128)(2,1)} %collective-permute-done.5.middles.refs_2_, bf16[2,2,1024,4096]{3,2,1,0:T(8,128)(2,1)} %cross.19), custom_call_target="tpu_custom_call" | custom-call | flops 1 | bytes 1 | tf_op jit(solution)/shard_map/pallas_call | solution.py:514
  102.2 0.6 collective-permute-start.10
  102.8 4.1 %collective-permute-start.9 = (bf16[1,2,512,512]{3,2,1,0:T(8,128)(2,1)}, bf16[1,2,512,512]{3,2,1,0:T(8,128)(2,1)}, u32[]{:S(2)}, u32[]{:S(2)}) collective-permute-start(bf16[1,2,512,512]{3,2,1,0:T(8,128)(2,1)} %get-tuple-element.69), channel_id=1, source_target_pairs={{0,4},{2,6},{4,0},{6,2},{8,12},{10,14},{12,8},{14,10},{1,5},{3,7},... | collective-permute-start | bytes 3145736 | tf_op jit(solution)/shard_map/ppermute | solution.py:18
  106.9 0.5 collective-permute-start.8
  107.5 9.6 %shard_map.129.total = f32[2,1024,512]{2,1,0:T(8,128)} custom-call(s32[2]{0:T(128)} %get-tuple-element.73.ids, bf16[2,2,1024,4096]{3,2,1,0:T(8,128)(2,1)} %cross.19, bf16[2,2,512,512]{3,2,1,0:T(8,128)(2,1)} %collective-permute-done.6.refs_0_.refs_1_.refs_3_.refs_4_, bf16[1,2,512,512]{3,2,1,0:T(8,128)(2,1)} %get-tuple-element.68.refs_1_, ...), custom_call_target="tpu_custom_call" | custom-call | flops 1 | bytes 1 | tf_op jit(solution)/shard_map/pallas_call | solution.py:136
  117.0 3.1 %shard_map.130 = (bf16[1,2,512,512]{3,2,1,0:T(8,128)(2,1)}, bf16[1,2,512,512]{3,2,1,0:T(8,128)(2,1)}) custom-call(s32[2]{0:T(128)} %pad_add_fusion.ids, bf16[2,2,512,512]{3,2,1,0:T(8,128)(2,1)} %collective-permute-done.4.ends.block_re.block_im, bf16[2,2,512,512]{3,2,1,0:T(8,128)(2,1)} %collective-permute-done.5.middles.refs_2_, bf16[2,2,1024,4096]{3,2,1,0:T(8,128)(2,1)} %cross.19), custom_call_target="tpu_custom_call" | custom-call | flops 1 | bytes 1 | tf_op jit(solution)/shard_map/pallas_call | solution.py:514
  120.1 10.7 %collective-permute-done.12 = f32[2,512]{1,0:T(2,128)S(1)} collective-permute-done((f32[2,512]{1,0:T(2,128)S(1)}, f32[2,512]{1,0:T(2,128)S(1)}, u32[]{:S(2)}, u32[]{:S(2)}) %collective-permute-start.12) | collective-permute-done | bytes 4128 | tf_op jit(solution)/shard_map/ppermute | solution.py:18
  130.9 1.4 collective-permute-done.8.w5.refs_3_
  132.3 0.5 collective-permute-start.17
  132.8 0.5 collective-permute-start.13
  133.3 0.4 collective-permute-start.14
  133.7 3.0 %collective-permute-done.16.refs_6_.refs_8_.refs_9_ = bf16[2,2,512,512]{3,2,1,0:T(8,128)(2,1)} collective-permute-done((bf16[2,2,512,512]{3,2,1,0:T(8,128)(2,1)}, bf16[2,2,512,512]{3,2,1,0:T(8,128)(2,1)}, u32[]{:S(2)}, u32[]{:S(2)}) %collective-permute-start.16) | collective-permute-done | bytes 2097184 | tf_op jit(solution)/shard_map/ppermute | solution.py:18
  136.8 3.0 %collective-permute-done.17.refs_7_ = bf16[2,2,512,512]{3,2,1,0:T(8,128)(2,1)} collective-permute-done((bf16[2,2,512,512]{3,2,1,0:T(8,128)(2,1)}, bf16[2,2,512,512]{3,2,1,0:T(8,128)(2,1)}, u32[]{:S(2)}, u32[]{:S(2)}) %collective-permute-start.17) | collective-permute-done | bytes 2097184 | tf_op jit(solution)/shard_map/ppermute | solution.py:18
  139.8 0.2 collective-permute-start.18
  140.0 9.6 %shard_map.132.total = f32[2,1024,512]{2,1,0:T(8,128)} custom-call(s32[2]{0:T(128)} %get-tuple-element.73.ids, bf16[2,2,1024,4096]{3,2,1,0:T(8,128)(2,1)} %cross.19, bf16[2,2,512,512]{3,2,1,0:T(8,128)(2,1)} %collective-permute-done.6.refs_0_.refs_1_.refs_3_.refs_4_, bf16[1,2,512,512]{3,2,1,0:T(8,128)(2,1)} %get-tuple-element.81.refs_1_, ...), custom_call_target="tpu_custom_call" | custom-call | flops 1 | bytes 1 | tf_op jit(solution)/shard_map/pallas_call | solution.py:136
  149.6 10.9 %shard_map.131 = (f32[8,512]{1,0:T(8,128)}, f32[2,512,512]{2,1,0:T(8,128)}) custom-call(s32[8]{0:T(128)} %concatenate.11.ids, bf16[2,2,1024,4096]{3,2,1,0:T(8,128)(2,1)} %cross.19, bf16[1,2,512,512]{3,2,1,0:T(8,128)(2,1)} %collective-permute-done.8.w5.refs_3_, bf16[1,2,512,512]{3,2,1,0:T(8,128)(2,1)} %collective-permute-done.9.w6.block_re, ...), custom_call_target="tpu_custom_call" | custom-call | flops 1 | bytes 1 | tf_op jit(solution)/shard_map/pallas_call | solution.py:306
  160.6 0.5 collective-permute-start.20
  161.1 0.1 collective-permute-start.22
  161.2 0.4 collective-permute-start.21
  161.6 11.0 %shard_map.133 = (f32[8,512]{1,0:T(8,128)}, f32[2,512,512]{2,1,0:T(8,128)}) custom-call(s32[8]{0:T(128)} %concatenate.11.ids, bf16[2,2,1024,4096]{3,2,1,0:T(8,128)(2,1)} %cross.19, bf16[1,2,512,512]{3,2,1,0:T(8,128)(2,1)} %collective-permute-done.13.w5.refs_9_, bf16[1,2,512,512]{3,2,1,0:T(8,128)(2,1)} %collective-permute-done.14.w6.block_im, ...), custom_call_target="tpu_custom_call" | custom-call | flops 1 | bytes 1 | tf_op jit(solution)/shard_map/pallas_call | solution.py:306
  172.7 1.4 shard_map.134
  174.1 9.8 %all-to-all-start = ((f32[16,2,512]{2,1,0:T(2,128)}), f32[16,2,512]{2,1,0:T(2,128)S(1)}, u32[]{:S(2)}, u32[]{:S(2)}) async-start(f32[16,2,512]{2,1,0:T(2,128)} %shard_map.134), calls=%async_computation | async-start | bytes 131072 | tf_op jit(solution)/shard_map/all_to_all | solution.py:41
  183.9 6.9 %all-to-all-done = f32[16,2,512]{2,1,0:T(2,128)S(1)} async-done(((f32[16,2,512]{2,1,0:T(2,128)}), f32[16,2,512]{2,1,0:T(2,128)S(1)}, u32[]{:S(2)}, u32[]{:S(2)}) %all-to-all-start) | async-done | bytes 65568 | tf_op jit(solution)/shard_map/all_to_all | solution.py:41
  190.9 0.1 abs_reduce_fusion
  191.0 0.1 reshape.41
  191.1 0.6 constant_dynamic-slice_fusion
  191.7 0.8 fusion
  (37 shorter events, 0.4 us)
Async XLA Ops:
  0.6 9.0 %copy-start.2 = (s32[3]{0:T(128)S(1)}, s32[3]{0:T(128)}, u32[]{:S(2)}) copy-start(s32[3]{0:T(128)} %constant.116.clone) | copy-start | bytes 40
  0.6 9.1 %copy-start = (s32[2]{0:T(128)S(1)}, s32[2]{0:T(128)}, u32[]{:S(2)}) copy-start(s32[2]{0:T(128)} %constant.117.clone) | copy-start | bytes 28
  0.7 22.6 %collective-permute-start.2 = (bf16[2,2,512,512]{3,2,1,0:T(8,128)(2,1)}, bf16[2,2,512,512]{3,2,1,0:T(8,128)(2,1)}, u32[]{:S(2)}, u32[]{:S(2)}) collective-permute-start(bf16[2,2,512,512]{3,2,1,0:T(8,128)(2,1)} %bitcast.17), channel_id=1, source_target_pairs={{0,1},{1,0},{2,3},{3,2},{4,8},{5,9},{6,10},{7,11},{8,4},{9,5},{10,... | collective-permute-start | bytes 6291464 | tf_op jit(solution)/shard_map/ppermute | solution.py:25
  1.2 49.8 %collective-permute-start.1 = (bf16[2,2,512,512]{3,2,1,0:T(8,128)(2,1)}, bf16[2,2,512,512]{3,2,1,0:T(8,128)(2,1)}, u32[]{:S(2)}, u32[]{:S(2)}) collective-permute-start(bf16[2,2,512,512]{3,2,1,0:T(8,128)(2,1)} %bitcast.18), channel_id=1, source_target_pairs={{0,4},{2,6},{4,0},{6,2},{8,12},{10,14},{12,8},{14,10},{1,5},{3,7},... | collective-permute-start | bytes 6291464 | tf_op jit(solution)/shard_map/ppermute | solution.py:18
  5.3 47.1 %collective-permute-start = (bf16[2,2,512,512]{3,2,1,0:T(8,128)(2,1)}, bf16[2,2,512,512]{3,2,1,0:T(8,128)(2,1)}, u32[]{:S(2)}, u32[]{:S(2)}) collective-permute-start(bf16[2,2,512,512]{3,2,1,0:T(8,128)(2,1)} %bitcast.19), channel_id=1, source_target_pairs={{0,2},{2,0},{4,6},{6,4},{8,10},{10,8},{12,14},{14,12},{1,3},{3,1},... | collective-permute-start | bytes 6291464 | tf_op jit(solution)/shard_map/ppermute | solution.py:18
  8.9 14.3 %collective-permute-start.3 = (f32[2,512]{1,0:T(2,128)S(1)}, f32[2,512]{1,0:T(2,128)S(1)}, u32[]{:S(2)}, u32[]{:S(2)}) collective-permute-start(f32[2,512]{1,0:T(2,128)S(1)} %multiply_reduce_fusion), channel_id=1, source_target_pairs={{0,1},{1,0},{2,3},{3,2},{4,5},{5,4},{6,7},{7,6},{8,9},{9,8},{10,11... | collective-permute-start | bytes 12296 | tf_op jit(solution)/shard_map/ppermute | solution.py:18
  52.4 46.6 %collective-permute-start.4 = (bf16[2,2,512,512]{3,2,1,0:T(8,128)(2,1)}, bf16[2,2,512,512]{3,2,1,0:T(8,128)(2,1)}, u32[]{:S(2)}, u32[]{:S(2)}) collective-permute-start(bf16[2,2,512,512]{3,2,1,0:T(8,128)(2,1)} %shard_map.122.refs_2_.refs_3_), channel_id=1, source_target_pairs={{0,4},{2,6},{4,0},{6,2},{8,12},{10,14},{12,8},{14,10},{1,5},{3,7},... | collective-permute-start | bytes 6291464 | tf_op jit(solution)/shard_map/ppermute | solution.py:18
  52.7 46.3 %collective-permute-start.6 = (bf16[2,2,512,512]{3,2,1,0:T(8,128)(2,1)}, bf16[2,2,512,512]{3,2,1,0:T(8,128)(2,1)}, u32[]{:S(2)}, u32[]{:S(2)}) collective-permute-start(bf16[2,2,512,512]{3,2,1,0:T(8,128)(2,1)} %collective-permute-done.1.refs_1_.refs_2_), channel_id=1, source_target_pairs={{0,2},{2,0},{4,6},{6,4},{8,10},{10,8},{12,14},{14,12},{1,3},{3,1},... | collective-permute-start | bytes 6291464 | tf_op jit(solution)/shard_map/ppermute | solution.py:18
  54.2 44.8 %collective-permute-start.5 = (bf16[2,2,512,512]{3,2,1,0:T(8,128)(2,1)}, bf16[2,2,512,512]{3,2,1,0:T(8,128)(2,1)}, u32[]{:S(2)}, u32[]{:S(2)}) collective-permute-start(bf16[2,2,512,512]{3,2,1,0:T(8,128)(2,1)} %collective-permute-done.1.refs_1_.refs_2_), channel_id=1, source_target_pairs={{0,1},{1,0},{2,3},{3,2},{4,8},{5,9},{6,10},{7,11},{8,4},{9,5},{10,... | collective-permute-start | bytes 6291464 | tf_op jit(solution)/shard_map/ppermute | solution.py:25
  54.2 44.8 %collective-permute-start.7 = (f32[2,512]{1,0:T(2,128)S(1)}, f32[2,512]{1,0:T(2,128)S(1)}, u32[]{:S(2)}, u32[]{:S(2)}) collective-permute-start(f32[2,512]{1,0:T(2,128)S(1)} %add.101), channel_id=1, source_target_pairs={{0,2},{2,0},{4,6},{6,4},{8,10},{10,8},{12,14},{14,12},{1,3},{3,1},... | collective-permute-start | bytes 12296 | tf_op jit(solution)/shard_map/ppermute | solution.py:18
  99.0 33.2 %collective-permute-start.11 = (bf16[2,2,1024,512]{3,2,1,0:T(8,128)(2,1)}, bf16[2,2,1024,512]{3,2,1,0:T(8,128)(2,1)}, u32[]{:S(2)}, u32[]{:S(2)}) collective-permute-start(bf16[2,2,1024,512]{3,2,1,0:T(8,128)(2,1)} %shard_map.127.refs_0_), channel_id=1, source_target_pairs={{0,1},{1,0},{2,3},{3,2},{4,5},{5,4},{6,7},{7,6},{8,9},{9,8},{10,11... | collective-permute-start | bytes 12582920 | tf_op jit(solution)/shard_map/ppermute | solution.py:18
  102.2 28.6 %collective-permute-start.10 = (bf16[1,2,512,512]{3,2,1,0:T(8,128)(2,1)}, bf16[1,2,512,512]{3,2,1,0:T(8,128)(2,1)}, u32[]{:S(2)}, u32[]{:S(2)}) collective-permute-start(bf16[1,2,512,512]{3,2,1,0:T(8,128)(2,1)} %get-tuple-element.71), channel_id=1, source_target_pairs={{0,1},{1,0},{2,3},{3,2},{4,8},{5,9},{6,10},{7,11},{8,4},{9,5},{10,... | collective-permute-start | bytes 3145736 | tf_op jit(solution)/shard_map/ppermute | solution.py:25
  102.8 28.1 %collective-permute-start.9 = (bf16[1,2,512,512]{3,2,1,0:T(8,128)(2,1)}, bf16[1,2,512,512]{3,2,1,0:T(8,128)(2,1)}, u32[]{:S(2)}, u32[]{:S(2)}) collective-permute-start(bf16[1,2,512,512]{3,2,1,0:T(8,128)(2,1)} %get-tuple-element.69), channel_id=1, source_target_pairs={{0,4},{2,6},{4,0},{6,2},{8,12},{10,14},{12,8},{14,10},{1,5},{3,7},... | collective-permute-start | bytes 3145736 | tf_op jit(solution)/shard_map/ppermute | solution.py:18
  106.9 25.3 %collective-permute-start.8 = (bf16[1,2,512,512]{3,2,1,0:T(8,128)(2,1)}, bf16[1,2,512,512]{3,2,1,0:T(8,128)(2,1)}, u32[]{:S(2)}, u32[]{:S(2)}) collective-permute-start(bf16[1,2,512,512]{3,2,1,0:T(8,128)(2,1)} %get-tuple-element.68.refs_1_), channel_id=1, source_target_pairs={{0,2},{2,0},{4,6},{6,4},{8,10},{10,8},{12,14},{14,12},{1,3},{3,1},... | collective-permute-start | bytes 3145736 | tf_op jit(solution)/shard_map/ppermute | solution.py:18
  107.5 23.4 %collective-permute-start.12 = (f32[2,512]{1,0:T(2,128)S(1)}, f32[2,512]{1,0:T(2,128)S(1)}, u32[]{:S(2)}, u32[]{:S(2)}) collective-permute-start(f32[2,512]{1,0:T(2,128)S(1)} %add.122), channel_id=1, source_target_pairs={{0,4},{2,6},{4,0},{6,2},{8,12},{10,14},{12,8},{14,10},{1,5},{3,7},... | collective-permute-start | bytes 12296 | tf_op jit(solution)/shard_map/ppermute | solution.py:18
  132.3 4.5 %collective-permute-start.16 = (bf16[2,2,512,512]{3,2,1,0:T(8,128)(2,1)}, bf16[2,2,512,512]{3,2,1,0:T(8,128)(2,1)}, u32[]{:S(2)}, u32[]{:S(2)}) collective-permute-start(bf16[2,2,512,512]{3,2,1,0:T(8,128)(2,1)} %collective-permute-done.6.refs_0_.refs_1_.refs_3_.refs_4_), channel_id=1, source_target_pairs={{0,1},{1,0},{2,3},{3,2},{4,5},{5,4},{6,7},{7,6},{8,9},{9,8},{10,11... | collective-permute-start | bytes 6291464 | tf_op jit(solution)/shard_map/ppermute | solution.py:18
  132.3 7.5 %collective-permute-start.17 = (bf16[2,2,512,512]{3,2,1,0:T(8,128)(2,1)}, bf16[2,2,512,512]{3,2,1,0:T(8,128)(2,1)}, u32[]{:S(2)}, u32[]{:S(2)}) collective-permute-start(bf16[2,2,512,512]{3,2,1,0:T(8,128)(2,1)} %collective-permute-done.5.middles.refs_2_), channel_id=1, source_target_pairs={{0,1},{1,0},{2,3},{3,2},{4,5},{5,4},{6,7},{7,6},{8,9},{9,8},{10,11... | collective-permute-start | bytes 6291464 | tf_op jit(solution)/shard_map/ppermute | solution.py:18
  132.8 27.7 %collective-permute-start.13 = (bf16[1,2,512,512]{3,2,1,0:T(8,128)(2,1)}, bf16[1,2,512,512]{3,2,1,0:T(8,128)(2,1)}, u32[]{:S(2)}, u32[]{:S(2)}) collective-permute-start(bf16[1,2,512,512]{3,2,1,0:T(8,128)(2,1)} %get-tuple-element.81.refs_1_), channel_id=1, source_target_pairs={{0,2},{2,0},{4,6},{6,4},{8,10},{10,8},{12,14},{14,12},{1,3},{3,1},... | collective-permute-start | bytes 3145736 | tf_op jit(solution)/shard_map/ppermute | solution.py:18
  133.3 27.2 %collective-permute-start.14 = (bf16[1,2,512,512]{3,2,1,0:T(8,128)(2,1)}, bf16[1,2,512,512]{3,2,1,0:T(8,128)(2,1)}, u32[]{:S(2)}, u32[]{:S(2)}) collective-permute-start(bf16[1,2,512,512]{3,2,1,0:T(8,128)(2,1)} %get-tuple-element.82), channel_id=1, source_target_pairs={{0,4},{2,6},{4,0},{6,2},{8,12},{10,14},{12,8},{14,10},{1,5},{3,7},... | collective-permute-start | bytes 3145736 | tf_op jit(solution)/shard_map/ppermute | solution.py:18
  133.7 26.8 %collective-permute-start.15 = (bf16[1,2,512,512]{3,2,1,0:T(8,128)(2,1)}, bf16[1,2,512,512]{3,2,1,0:T(8,128)(2,1)}, u32[]{:S(2)}, u32[]{:S(2)}) collective-permute-start(bf16[1,2,512,512]{3,2,1,0:T(8,128)(2,1)} %get-tuple-element.83), channel_id=1, source_target_pairs={{0,1},{1,0},{2,3},{3,2},{4,8},{5,9},{6,10},{7,11},{8,4},{9,5},{10,... | collective-permute-start | bytes 3145736 | tf_op jit(solution)/shard_map/ppermute | solution.py:25
  139.8 20.7 %collective-permute-start.18 = (f32[2,512]{1,0:T(2,128)S(1)}, f32[2,512]{1,0:T(2,128)S(1)}, u32[]{:S(2)}, u32[]{:S(2)}) collective-permute-start(f32[2,512]{1,0:T(2,128)S(1)} %add.123), channel_id=1, source_target_pairs={{0,8},{2,10},{4,12},{6,14},{8,0},{10,2},{12,4},{14,6},{1,9},{3,11}... | collective-permute-start | bytes 12296 | tf_op jit(solution)/shard_map/ppermute | solution.py:18
  160.5 12.1 %collective-permute-start.19 = (bf16[1,2,512,512]{3,2,1,0:T(8,128)(2,1)}, bf16[1,2,512,512]{3,2,1,0:T(8,128)(2,1)}, u32[]{:S(2)}, u32[]{:S(2)}) collective-permute-start(bf16[1,2,512,512]{3,2,1,0:T(8,128)(2,1)} %collective-permute-done.10.w7.refs_2_), channel_id=1, source_target_pairs={{0,1},{1,0},{2,3},{3,2},{4,5},{5,4},{6,7},{7,6},{8,9},{9,8},{10,11... | collective-permute-start | bytes 3145736 | tf_op jit(solution)/shard_map/ppermute | solution.py:18
  160.6 12.0 %collective-permute-start.20 = (bf16[1,2,512,512]{3,2,1,0:T(8,128)(2,1)}, bf16[1,2,512,512]{3,2,1,0:T(8,128)(2,1)}, u32[]{:S(2)}, u32[]{:S(2)}) collective-permute-start(bf16[1,2,512,512]{3,2,1,0:T(8,128)(2,1)} %collective-permute-done.8.w5.refs_3_), channel_id=1, source_target_pairs={{0,1},{1,0},{2,3},{3,2},{4,5},{5,4},{6,7},{7,6},{8,9},{9,8},{10,11... | collective-permute-start | bytes 3145736 | tf_op jit(solution)/shard_map/ppermute | solution.py:18
  161.1 11.6 %collective-permute-start.22 = (bf16[1,2,512,512]{3,2,1,0:T(8,128)(2,1)}, bf16[1,2,512,512]{3,2,1,0:T(8,128)(2,1)}, u32[]{:S(2)}, u32[]{:S(2)}) collective-permute-start(bf16[1,2,512,512]{3,2,1,0:T(8,128)(2,1)} %collective-permute-done.13.w5.refs_9_), channel_id=1, source_target_pairs={{0,1},{1,0},{2,3},{3,2},{4,5},{5,4},{6,7},{7,6},{8,9},{9,8},{10,11... | collective-permute-start | bytes 3145736 | tf_op jit(solution)/shard_map/ppermute | solution.py:18
  161.2 11.5 %collective-permute-start.21 = (bf16[1,2,512,512]{3,2,1,0:T(8,128)(2,1)}, bf16[1,2,512,512]{3,2,1,0:T(8,128)(2,1)}, u32[]{:S(2)}, u32[]{:S(2)}) collective-permute-start(bf16[1,2,512,512]{3,2,1,0:T(8,128)(2,1)} %collective-permute-done.15.w7.refs_8_), channel_id=1, source_target_pairs={{0,1},{1,0},{2,3},{3,2},{4,5},{5,4},{6,7},{7,6},{8,9},{9,8},{10,11... | collective-permute-start | bytes 3145736 | tf_op jit(solution)/shard_map/ppermute | solution.py:18
  172.7 19.0 %copy-start.1 = (s32[16]{0:T(128)S(1)}, s32[16]{0:T(128)}, u32[]{:S(2)}) copy-start(s32[16]{0:T(128)} %param.13) | copy-start | bytes 196
  174.1 16.7 %all-to-all-start = ((f32[16,2,512]{2,1,0:T(2,128)}), f32[16,2,512]{2,1,0:T(2,128)S(1)}, u32[]{:S(2)}, u32[]{:S(2)}) async-start(f32[16,2,512]{2,1,0:T(2,128)} %shard_map.134), calls=%async_computation | async-start | bytes 131072 | tf_op jit(solution)/shard_map/all_to_all | solution.py:41

commit v14 on v13

--- a/solution.py
+++ b/solution.py
@@ -331,7 +331,7 @@
     )(ids, cross, *pieces, *blocks, total, *row_refs)
 
 
-def dot_kernel(ids, *refs):
+def dot_kernel(ids, norms, *refs):
     groups, (out, rows, field, sem, total) = (refs[:6], refs[6:12]), refs[12:]
     for freq, (field_ref, _, *sources) in enumerate(groups):
 
@@ -355,34 +355,33 @@
             more = sum(fold(rows[freq, part], field[freq, part]) for part in range(2))
             total[freq : freq + 1] += jnp.sum(more, axis=0, keepdims=True)
 
+    total[2:4] = norms[...]
     for k in range(out.shape[0]):
         out[k] = total[...]
 
 
-def dot_rows(ids, groups):
+def dot_rows(ids, norms, groups):
     late_shape, dtype = groups[0][0].shape, groups[0][2].dtype
     sources = late_shape[-1]
     whole = lambda shape: pl.BlockSpec(shape, lambda i, ids: (0, 0))
     return pl.pallas_call(
         dot_kernel,
-        out_shape=jax.ShapeDtypeStruct((copies_to_all(), len(groups), sources), jnp.float32),
+        out_shape=jax.ShapeDtypeStruct((copies_to_all(), 4, sources), jnp.float32),
         grid_spec=pltpu.PrefetchScalarGridSpec(
             num_scalar_prefetch=1,
             grid=(1,),
-            in_specs=[ANYWHERE, whole((8, sources)), *[ANYWHERE] * 4] * 2,
-            out_specs=pl.BlockSpec(
-                (copies_to_all(), len(groups), sources), lambda i, ids: (0, 0, 0)
-            ),
+            in_specs=[whole((2, sources))] + [ANYWHERE, whole((8, sources)), *[ANYWHERE] * 4] * 2,
+            out_specs=pl.BlockSpec((copies_to_all(), 4, sources), lambda i, ids: (0, 0, 0)),
             scratch_shapes=[
                 pltpu.VMEM((2, *late_shape), dtype),
                 pltpu.VMEM((2, *late_shape), jnp.float32),
                 pltpu.SemaphoreType.DMA((2, 2)),
-                pltpu.VMEM((len(groups), sources), jnp.float32),
+                pltpu.VMEM((4, sources), jnp.float32),
             ],
         ),
         compiler_params=pltpu.CompilerParams(vmem_limit_bytes=VMEM_LIMIT),
         cost_estimate=HINT,
-    )(ids, *groups[0], *groups[1])
+    )(ids, norms, *groups[0], *groups[1])
 
 
 def copy_kernel(inputs, jobs, ids, *refs):
@@ -574,7 +573,6 @@
     a0 = add_field(cross, 0, ids(0), [own])
     a1 = add_field(cross, 1, ids(0), [own])
     m = fill_block(ids_z, m, cross)
-    norms += swap(norms, "col", 1)
     x, n, m, a0, a1, norms, *numbers = barrier(x, n, m, a0, a1, norms, *numbers)
     ids_a, ids_b, ids_z, late_ids, pair, ids_dot = numbers
 
@@ -585,8 +583,7 @@
     a1 = add_field(cross, 1, ids_a, [x, n, m], a1, gated=True)
     mine = take_pair(pair, own, x, n, m)
     x_a, x_b = x[0:1], x[1:2]
-    norms += swap(norms, "row", 1)
-    z, m2, xn, a0, a1, mine, x_a, x_b, norms = barrier(z, m2, xn, a0, a1, mine, x_a, x_b, norms)
+    z, m2, xn, a0, a1, mine, x_a, x_b = barrier(z, m2, xn, a0, a1, mine, x_a, x_b)
 
     w4_a, send_a = take_next(0, ids_z, z, m2, cross)
     x5_a = swap(w4_a, "row", 1)
@@ -596,9 +593,8 @@
     b0 = add_field(cross, 0, ids_b, [xn, w4_a], a0)
     w4_b, send_b = take_next(1, after(ids_z, b0), z, m2, cross)
     b1 = add_field(cross, 1, ids_b, [xn, w4_b], a1)
-    norms += swap(norms, "row", 2)
-    x5_a, z_a, w7_a, other, b0, w4_b, send_b, x_b, xn, m2, norms = barrier(
-        x5_a, z_a, w7_a, other, b0, w4_b, send_b, x_b, xn, m2, norms
+    x5_a, z_a, w7_a, other, b0, w4_b, send_b, x_b, xn, m2 = barrier(
+        x5_a, z_a, w7_a, other, b0, w4_b, send_b, x_b, xn, m2
     )
 
     x5_b = swap(w4_b, "row", 1)
@@ -608,9 +604,8 @@
     other_m2 = swap(m2, "col", 1)
     early = [mine, xn, m2, xn, xn, other, other_xn, other_m2, other_xn, other_xn]
     sums_a, field_a = add_late(cross, 0, late_ids, [x5_a, z_a, w7_a], [z, z], b0, early)
-    norms += swap(after(norms, other_xn, other_m2), "row", 4)
-    x5_b, z_b, w7_b, sums_a, field_a, b1, other_xn, other_m2, x5_a, w7_a, norms = barrier(
-        x5_b, z_b, w7_b, sums_a, field_a, b1, other_xn, other_m2, x5_a, w7_a, norms
+    x5_b, z_b, w7_b, sums_a, field_a, b1, other_xn, other_m2, x5_a, w7_a = barrier(
+        x5_b, z_b, w7_b, sums_a, field_a, b1, other_xn, other_m2, x5_a, w7_a
     )
 
     late = [w7_a, x5_a, w7_b, x5_b]
@@ -621,7 +616,7 @@
         (field_a, sums_a, *late[:2], *others[:2]),
         (field_b, sums_b, *late[2:], *others[2:]),
     ]
-    return dot_rows(ids_dot, groups), norms
+    return dot_rows(ids_dot, norms, groups)
 
 
 def sums_by_gather(cross, replicas, norms):
@@ -635,7 +630,8 @@
     own_rows = lax.dynamic_slice_in_dim(whole, first_row - holder * half, rows, 2)
     block_rows = jnp.where(holder == col_index, own_rows, swap(own_rows, "col", 1))
     numer = jnp.sum(block_rows.astype(jnp.float32) * field, axis=(1, 2))
-    return jnp.broadcast_to(numer[None], (copies_to_all(), *numer.shape)), lax.psum(norms, ("row", "col"))
+    sums = jnp.concatenate([numer, norms])
+    return jnp.broadcast_to(sums[None], (copies_to_all(), *sums.shape))
 
 
 def body(cross_spectra, replicas, tile_order):
@@ -649,8 +645,10 @@
         and replicas.shape[3] % 128 == 0
         and cross_spectra.shape[2] == 2 * replicas.shape[3]
     )
-    copies, norms = (sums_by_swaps if doubling else sums_by_gather)(cross_spectra, replicas, norms)
-    beam = sum_all(copies) / (norms + 1e-06)
+    sums = (sums_by_swaps if doubling else sums_by_gather)(cross_spectra, replicas, norms)
+    sums = sum_all(sums)
+    numer, norms = sums[:fnum], sums[fnum:]
+    beam = numer / (norms + 1e-06)
     width = sources // lax.axis_size("col")
     beam_half = lax.dynamic_slice_in_dim(beam, lax.axis_index("col") * width, width, 1)
     peak = jnp.max(jnp.abs(beam), axis=1) + 1e-06

time: 193 us -> 191 us (0.990)
  starting transfers between devices: 26.4 us -> 24.2 us
    ppermute x19 -> x15, waiting for transfers between devices: 57.1 us -> 55.3 us  [swap(): lax.ppermute(value, axis, [(source, source ^ mask) for source in range(si...]
    ppermute x19 -> x15, starting transfers between devices: 15.5 us -> 14.6 us  [swap(): lax.ppermute(value, axis, [(source, source ^ mask) for source in range(si...]
  transfers between devices with their start and end apart: 24 -> 20, of which waited for: 8 -> 9; matrix products, arithmetic and copies ran while one was open for 4% -> 4% of each run, Pallas kernels for 47% -> 48%
where the time goes in v14:
time: 191 us; the launch traced here: 190 us
  Pallas kernels  91.9 us (48%)
  waiting for transfers between devices  63.2 us (33%)
  starting transfers between devices  24.2 us (13%)
  other arithmetic  4.57 us (2%)
  local copies, waits for them, and re-layouts  4.31 us (2%)
    pallas_call x6, Pallas kernels, add_field(): pl.pallas_call(functools.partial(field_kernel, freq, count, has_total, ga...  55.7 us
    ppermute x15, waiting for transfers between devices, swap(): lax.ppermute(value, axis, [(source, source ^ mask) for source in range(si...  55.3 us
    pallas_call x2, Pallas kernels, add_late(): pl.pallas_call(functools.partial(late_kernel, freq), out_shape=(jax.Shape...  21.9 us
    ppermute x15, starting transfers between devices, swap(): lax.ppermute(value, axis, [(source, source ^ mask) for source in range(si...  14.6 us
    all_to_all x1, starting transfers between devices, sum_all(): return jnp.sum(lax.all_to_all(copies, axes, 0, 0, tiled=True), axis=0)  8.49 us
    all_to_all x1, waiting for transfers between devices, sum_all(): return jnp.sum(lax.all_to_all(copies, axes, 0, 0, tiled=True), axis=0)  7.93 us
    pallas_call x2, Pallas kernels, copies(): pl.pallas_call(functools.partial(copy_kernel, len(args), jobs), out_shape...  6.7 us
    pallas_call x2, Pallas kernels, take_next(): pl.pallas_call(functools.partial(next_kernel, freq), out_shape=[shape, sh...  6.18 us
  transfers between devices with their start and end apart: 20, of which 9 were waited for; matrix products, arithmetic and copies ran while one was open for 4% of the time, Pallas kernels for 48%

profile of v14, /device:TPU:0, one launch (start us, length us, event | category | flops | bytes accessed | tf_op | source)
XLA Modules:
  0.0 190.0 jit_solution(8722919608549757524)
XLA Ops:
  0.6 0.5 collective-permute-start.2
  1.1 4.1 %collective-permute-start.1 = (bf16[2,2,512,512]{3,2,1,0:T(8,128)(2,1)}, bf16[2,2,512,512]{3,2,1,0:T(8,128)(2,1)}, u32[]{:S(2)}, u32[]{:S(2)}) collective-permute-start(bf16[2,2,512,512]{3,2,1,0:T(8,128)(2,1)} %bitcast.18), channel_id=1, source_target_pairs={{0,4},{2,6},{4,0},{6,2},{8,12},{10,14},{12,8},{14,10},{1,5},{3,7},... | collective-permute-start | bytes 6291464 | tf_op jit(solution)/shard_map/ppermute | solution.py:18
  5.3 1.5 collective-permute-start
  6.8 5.8 %shard_map.124.refs_3_ = f32[2,1024,512]{2,1,0:T(8,128)} custom-call(s32[1]{0:T(128)} %bitcast.2.ids, bf16[2,2,1024,4096]{3,2,1,0:T(8,128)(2,1)} %cross.19, bf16[2,2,512,512]{3,2,1,0:T(8,128)(2,1)} %bitcast.20), custom_call_target="tpu_custom_call" | custom-call | flops 1 | bytes 1 | tf_op jit(solution)/shard_map/pallas_call | solution.py:136
  12.6 0.0 copy-start
  12.6 0.0 copy-start.2
  12.6 5.9 %shard_map.123.refs_3_ = f32[2,1024,512]{2,1,0:T(8,128)} custom-call(s32[1]{0:T(128)} %bitcast.2.ids, bf16[2,2,1024,4096]{3,2,1,0:T(8,128)(2,1)} %cross.19, bf16[2,2,512,512]{3,2,1,0:T(8,128)(2,1)} %bitcast.21), custom_call_target="tpu_custom_call" | custom-call | flops 1 | bytes 1 | tf_op jit(solution)/shard_map/pallas_call | solution.py:136
  18.7 0.5 fusion.16
  19.2 0.6 concatenate.11.ids
  19.8 0.7 pad_add_fusion.ids
  20.5 0.6 pad_add_fusion.1.ids
  21.1 2.6 %multiply_reduce_fusion.norms = f32[2,512]{1,0:T(2,128)} fusion(bf16[2,2,1,512,512]{4,3,2,1,0:T(8,128)(2,1)} %param.12), kind=kLoop, calls=%fused_computation | loop fusion | flops 3144704 | bytes 2101248 | tf_op jit(solution)/shard_map/reduce_sum | solution.py:641
  23.7 3.1 %shard_map.122.refs_2_.refs_3_ = bf16[2,2,512,512]{3,2,1,0:T(8,128)(2,1)} custom-call(s32[2]{0:T(128)} %pad_add_fusion.ids, bf16[2,2,512,512]{3,2,1,0:T(8,128)(2,1)} %collective-permute-done.2.refs_0_, bf16[2,2,1024,4096]{3,2,1,0:T(8,128)(2,1)} %cross.19), custom_call_target="tpu_custom_call", output_to_operand_aliasing={{}: (1, {})} | custom-call | flops 1 | bytes 1 | tf_op jit(solution)/shard_map/pallas_call | solution.py:416
  26.8 24.2 %collective-permute-done.1.refs_1_.refs_2_ = bf16[2,2,512,512]{3,2,1,0:T(8,128)(2,1)} collective-permute-done((bf16[2,2,512,512]{3,2,1,0:T(8,128)(2,1)}, bf16[2,2,512,512]{3,2,1,0:T(8,128)(2,1)}, u32[]{:S(2)}, u32[]{:S(2)}) %collective-permute-start.1) | collective-permute-done | bytes 2097184 | tf_op jit(solution)/shard_map/ppermute | solution.py:18
  51.0 1.4 collective-permute-done.refs_0_.refs_1_
  52.4 0.3 collective-permute-start.3
  52.7 1.5 collective-permute-start.5
  54.2 12.3 %shard_map.125.refs_2_ = f32[2,1024,512]{2,1,0:T(8,128)} custom-call(s32[4]{0:T(128)} %pad_add_fusion.1.ids, bf16[2,2,1024,4096]{3,2,1,0:T(8,128)(2,1)} %cross.19, bf16[2,2,512,512]{3,2,1,0:T(8,128)(2,1)} %collective-permute-done.refs_0_.refs_1_, bf16[2,2,512,512]{3,2,1,0:T(8,128)(2,1)} %collective-permute-done.1.refs_1_.refs_2_, ...), custom_call_target="tpu_custom_call" | custom-call | flops 1 | bytes 1 | tf_op jit(solution)/shard_map/pallas_call | solution.py:136
  66.5 12.4 %shard_map.126.refs_2_ = f32[2,1024,512]{2,1,0:T(8,128)} custom-call(s32[4]{0:T(128)} %pad_add_fusion.1.ids, bf16[2,2,1024,4096]{3,2,1,0:T(8,128)(2,1)} %cross.19, bf16[2,2,512,512]{3,2,1,0:T(8,128)(2,1)} %collective-permute-done.refs_0_.refs_1_, bf16[2,2,512,512]{3,2,1,0:T(8,128)(2,1)} %collective-permute-done.1.refs_1_.refs_2_, ...), custom_call_target="tpu_custom_call" | custom-call | flops 1 | bytes 1 | tf_op jit(solution)/shard_map/pallas_call | solution.py:136
  78.9 3.6 %shard_map.127.refs_0_ = bf16[2,2,1024,512]{3,2,1,0:T(8,128)(2,1)} custom-call(s32[1]{0:T(128)} %bitcast.6.ids, bf16[2,2,512,512]{3,2,1,0:T(8,128)(2,1)} %bitcast.22, bf16[2,2,512,512]{3,2,1,0:T(8,128)(2,1)} %collective-permute-done.refs_0_.refs_1_, bf16[2,2,512,512]{3,2,1,0:T(8,128)(2,1)} %collective-permute-done.1.refs_1_.refs_2_, ...), custom_call_target="tpu_custom_call" | custom-call | flops 1 | bytes 1 | tf_op jit(solution)/shard_map/pallas_call | solution.py:416
  82.5 3.0 %fusion.18 = (bf16[1,2,512,512]{3,2,1,0:T(8,128)(2,1)}, bf16[1,2,512,512]{3,2,1,0:T(8,128)(2,1)}) fusion(bf16[2,2,512,512]{3,2,1,0:T(8,128)(2,1)} %collective-permute-done.refs_0_.refs_1_), kind=kLoop, calls=%fused_computation.40 | loop fusion | bytes 4194304 | tf_op jit(solution)/shard_map/slice | solution.py:585
  85.5 13.1 %collective-permute-done.3.ends.block_re.block_im = bf16[2,2,512,512]{3,2,1,0:T(8,128)(2,1)} collective-permute-done((bf16[2,2,512,512]{3,2,1,0:T(8,128)(2,1)}, bf16[2,2,512,512]{3,2,1,0:T(8,128)(2,1)}, u32[]{:S(2)}, u32[]{:S(2)}) %collective-permute-start.3) | collective-permute-done | bytes 2097184 | tf_op jit(solution)/shard_map/ppermute | solution.py:18
  98.6 0.3 collective-permute-done.5.refs_0_.refs_1_.refs_3_.refs_4_
  98.9 3.1 %shard_map.128 = (bf16[1,2,512,512]{3,2,1,0:T(8,128)(2,1)}, bf16[1,2,512,512]{3,2,1,0:T(8,128)(2,1)}) custom-call(s32[2]{0:T(128)} %pad_add_fusion.ids, bf16[2,2,512,512]{3,2,1,0:T(8,128)(2,1)} %collective-permute-done.3.ends.block_re.block_im, bf16[2,2,512,512]{3,2,1,0:T(8,128)(2,1)} %collective-permute-done.4.middles.refs_2_, bf16[2,2,1024,4096]{3,2,1,0:T(8,128)(2,1)} %cross.19), custom_call_target="tpu_custom_call" | custom-call | flops 1 | bytes 1 | tf_op jit(solution)/shard_map/pallas_call | solution.py:513
  102.0 0.6 collective-permute-start.8
  102.6 4.3 %collective-permute-start.7 = (bf16[1,2,512,512]{3,2,1,0:T(8,128)(2,1)}, bf16[1,2,512,512]{3,2,1,0:T(8,128)(2,1)}, u32[]{:S(2)}, u32[]{:S(2)}) collective-permute-start(bf16[1,2,512,512]{3,2,1,0:T(8,128)(2,1)} %get-tuple-element.65), channel_id=1, source_target_pairs={{0,4},{2,6},{4,0},{6,2},{8,12},{10,14},{12,8},{14,10},{1,5},{3,7},... | collective-permute-start | bytes 3145736 | tf_op jit(solution)/shard_map/ppermute | solution.py:18
  106.9 0.5 collective-permute-start.6
  107.4 9.8 %shard_map.129.total = f32[2,1024,512]{2,1,0:T(8,128)} custom-call(s32[2]{0:T(128)} %get-tuple-element.69.ids, bf16[2,2,1024,4096]{3,2,1,0:T(8,128)(2,1)} %cross.19, bf16[2,2,512,512]{3,2,1,0:T(8,128)(2,1)} %collective-permute-done.5.refs_0_.refs_1_.refs_3_.refs_4_, bf16[1,2,512,512]{3,2,1,0:T(8,128)(2,1)} %get-tuple-element.64.refs_1_, ...), custom_call_target="tpu_custom_call" | custom-call | flops 1 | bytes 1 | tf_op jit(solution)/shard_map/pallas_call | solution.py:136
  117.2 3.1 %shard_map.130 = (bf16[1,2,512,512]{3,2,1,0:T(8,128)(2,1)}, bf16[1,2,512,512]{3,2,1,0:T(8,128)(2,1)}) custom-call(s32[2]{0:T(128)} %pad_add_fusion.ids, bf16[2,2,512,512]{3,2,1,0:T(8,128)(2,1)} %collective-permute-done.3.ends.block_re.block_im, bf16[2,2,512,512]{3,2,1,0:T(8,128)(2,1)} %collective-permute-done.4.middles.refs_2_, bf16[2,2,1024,4096]{3,2,1,0:T(8,128)(2,1)} %cross.19), custom_call_target="tpu_custom_call" | custom-call | flops 1 | bytes 1 | tf_op jit(solution)/shard_map/pallas_call | solution.py:513
  120.3 10.5 %collective-permute-done.7.w6.block_re = bf16[1,2,512,512]{3,2,1,0:T(8,128)(2,1)} collective-permute-done((bf16[1,2,512,512]{3,2,1,0:T(8,128)(2,1)}, bf16[1,2,512,512]{3,2,1,0:T(8,128)(2,1)}, u32[]{:S(2)}, u32[]{:S(2)}) %collective-permute-start.7) | collective-permute-done | bytes 1048608 | tf_op jit(solution)/shard_map/ppermute | solution.py:18
  130.8 1.5 collective-permute-done.6.w5.refs_3_
  132.2 0.5 collective-permute-start.14
  132.7 0.5 collective-permute-start.10
  133.3 0.3 collective-permute-start.11
  133.6 9.6 %shard_map.132.total = f32[2,1024,512]{2,1,0:T(8,128)} custom-call(s32[2]{0:T(128)} %get-tuple-element.69.ids, bf16[2,2,1024,4096]{3,2,1,0:T(8,128)(2,1)} %cross.19, bf16[2,2,512,512]{3,2,1,0:T(8,128)(2,1)} %collective-permute-done.5.refs_0_.refs_1_.refs_3_.refs_4_, bf16[1,2,512,512]{3,2,1,0:T(8,128)(2,1)} %get-tuple-element.76.refs_1_, ...), custom_call_target="tpu_custom_call" | custom-call | flops 1 | bytes 1 | tf_op jit(solution)/shard_map/pallas_call | solution.py:136
  143.2 10.9 %shard_map.131 = (f32[8,512]{1,0:T(8,128)}, f32[2,512,512]{2,1,0:T(8,128)}) custom-call(s32[8]{0:T(128)} %concatenate.11.ids, bf16[2,2,1024,4096]{3,2,1,0:T(8,128)(2,1)} %cross.19, bf16[1,2,512,512]{3,2,1,0:T(8,128)(2,1)} %collective-permute-done.6.w5.refs_3_, bf16[1,2,512,512]{3,2,1,0:T(8,128)(2,1)} %collective-permute-done.7.w6.block_re, ...), custom_call_target="tpu_custom_call" | custom-call | flops 1 | bytes 1 | tf_op jit(solution)/shard_map/pallas_call | solution.py:306
  154.1 4.1 %collective-permute-done.10.w5.refs_9_ = bf16[1,2,512,512]{3,2,1,0:T(8,128)(2,1)} collective-permute-done((bf16[1,2,512,512]{3,2,1,0:T(8,128)(2,1)}, bf16[1,2,512,512]{3,2,1,0:T(8,128)(2,1)}, u32[]{:S(2)}, u32[]{:S(2)}) %collective-permute-start.10) | collective-permute-done | bytes 1048608 | tf_op jit(solution)/shard_map/ppermute | solution.py:18
  158.1 0.3 collective-permute-done.11.w6.block_im
  158.4 0.5 collective-permute-start.16
  158.9 0.5 collective-permute-start.17
  159.4 11.0 %shard_map.133 = (f32[8,512]{1,0:T(8,128)}, f32[2,512,512]{2,1,0:T(8,128)}) custom-call(s32[8]{0:T(128)} %concatenate.11.ids, bf16[2,2,1024,4096]{3,2,1,0:T(8,128)(2,1)} %cross.19, bf16[1,2,512,512]{3,2,1,0:T(8,128)(2,1)} %collective-permute-done.10.w5.refs_9_, bf16[1,2,512,512]{3,2,1,0:T(8,128)(2,1)} %collective-permute-done.11.w6.block_im, ...), custom_call_target="tpu_custom_call" | custom-call | flops 1 | bytes 1 | tf_op jit(solution)/shard_map/pallas_call | solution.py:306
  170.5 1.5 shard_map.134
  171.9 8.5 %all-to-all-start = ((f32[16,4,512]{2,1,0:T(4,128)}), f32[16,4,512]{2,1,0:T(4,128)S(1)}, u32[]{:S(2)}, u32[]{:S(2)}) async-start(f32[16,4,512]{2,1,0:T(4,128)} %shard_map.134), calls=%async_computation | async-start | bytes 262144 | tf_op jit(solution)/shard_map/all_to_all | solution.py:41
  180.5 7.9 %all-to-all-done = f32[16,4,512]{2,1,0:T(4,128)S(1)} async-done(((f32[16,4,512]{2,1,0:T(4,128)}), f32[16,4,512]{2,1,0:T(4,128)S(1)}, u32[]{:S(2)}, u32[]{:S(2)}) %all-to-all-start) | async-done | bytes 131104 | tf_op jit(solution)/shard_map/all_to_all | solution.py:41
  188.4 0.1 abs_reduce_fusion
  188.6 0.1 reshape.41
  188.6 0.6 constant_dynamic-slice_fusion
  189.2 0.8 fusion
  (25 shorter events, 0.1 us)
Async XLA Ops:
  0.6 23.1 %collective-permute-start.2 = (bf16[2,2,512,512]{3,2,1,0:T(8,128)(2,1)}, bf16[2,2,512,512]{3,2,1,0:T(8,128)(2,1)}, u32[]{:S(2)}, u32[]{:S(2)}) collective-permute-start(bf16[2,2,512,512]{3,2,1,0:T(8,128)(2,1)} %bitcast.17), channel_id=1, source_target_pairs={{0,1},{1,0},{2,3},{3,2},{4,8},{5,9},{6,10},{7,11},{8,4},{9,5},{10,... | collective-permute-start | bytes 6291464 | tf_op jit(solution)/shard_map/ppermute | solution.py:25
  1.1 49.8 %collective-permute-start.1 = (bf16[2,2,512,512]{3,2,1,0:T(8,128)(2,1)}, bf16[2,2,512,512]{3,2,1,0:T(8,128)(2,1)}, u32[]{:S(2)}, u32[]{:S(2)}) collective-permute-start(bf16[2,2,512,512]{3,2,1,0:T(8,128)(2,1)} %bitcast.18), channel_id=1, source_target_pairs={{0,4},{2,6},{4,0},{6,2},{8,12},{10,14},{12,8},{14,10},{1,5},{3,7},... | collective-permute-start | bytes 6291464 | tf_op jit(solution)/shard_map/ppermute | solution.py:18
  5.3 47.1 %collective-permute-start = (bf16[2,2,512,512]{3,2,1,0:T(8,128)(2,1)}, bf16[2,2,512,512]{3,2,1,0:T(8,128)(2,1)}, u32[]{:S(2)}, u32[]{:S(2)}) collective-permute-start(bf16[2,2,512,512]{3,2,1,0:T(8,128)(2,1)} %bitcast.19), channel_id=1, source_target_pairs={{0,2},{2,0},{4,6},{6,4},{8,10},{10,8},{12,14},{14,12},{1,3},{3,1},... | collective-permute-start | bytes 6291464 | tf_op jit(solution)/shard_map/ppermute | solution.py:18
  12.6 6.1 %copy-start = (s32[2]{0:T(128)S(1)}, s32[2]{0:T(128)}, u32[]{:S(2)}) copy-start(s32[2]{0:T(128)} %constant.117.clone) | copy-start | bytes 28
  12.6 7.9 %copy-start.2 = (s32[3]{0:T(128)S(1)}, s32[3]{0:T(128)}, u32[]{:S(2)}) copy-start(s32[3]{0:T(128)} %constant.116.clone) | copy-start | bytes 40
  52.4 46.2 %collective-permute-start.3 = (bf16[2,2,512,512]{3,2,1,0:T(8,128)(2,1)}, bf16[2,2,512,512]{3,2,1,0:T(8,128)(2,1)}, u32[]{:S(2)}, u32[]{:S(2)}) collective-permute-start(bf16[2,2,512,512]{3,2,1,0:T(8,128)(2,1)} %shard_map.122.refs_2_.refs_3_), channel_id=1, source_target_pairs={{0,4},{2,6},{4,0},{6,2},{8,12},{10,14},{12,8},{14,10},{1,5},{3,7},... | collective-permute-start | bytes 6291464 | tf_op jit(solution)/shard_map/ppermute | solution.py:18
  52.7 46.2 %collective-permute-start.5 = (bf16[2,2,512,512]{3,2,1,0:T(8,128)(2,1)}, bf16[2,2,512,512]{3,2,1,0:T(8,128)(2,1)}, u32[]{:S(2)}, u32[]{:S(2)}) collective-permute-start(bf16[2,2,512,512]{3,2,1,0:T(8,128)(2,1)} %collective-permute-done.1.refs_1_.refs_2_), channel_id=1, source_target_pairs={{0,2},{2,0},{4,6},{6,4},{8,10},{10,8},{12,14},{14,12},{1,3},{3,1},... | collective-permute-start | bytes 6291464 | tf_op jit(solution)/shard_map/ppermute | solution.py:18
  54.2 44.7 %collective-permute-start.4 = (bf16[2,2,512,512]{3,2,1,0:T(8,128)(2,1)}, bf16[2,2,512,512]{3,2,1,0:T(8,128)(2,1)}, u32[]{:S(2)}, u32[]{:S(2)}) collective-permute-start(bf16[2,2,512,512]{3,2,1,0:T(8,128)(2,1)} %collective-permute-done.1.refs_1_.refs_2_), channel_id=1, source_target_pairs={{0,1},{1,0},{2,3},{3,2},{4,8},{5,9},{6,10},{7,11},{8,4},{9,5},{10,... | collective-permute-start | bytes 6291464 | tf_op jit(solution)/shard_map/ppermute | solution.py:25
  98.9 33.3 %collective-permute-start.9 = (bf16[2,2,1024,512]{3,2,1,0:T(8,128)(2,1)}, bf16[2,2,1024,512]{3,2,1,0:T(8,128)(2,1)}, u32[]{:S(2)}, u32[]{:S(2)}) collective-permute-start(bf16[2,2,1024,512]{3,2,1,0:T(8,128)(2,1)} %shard_map.127.refs_0_), channel_id=1, source_target_pairs={{0,1},{1,0},{2,3},{3,2},{4,5},{5,4},{6,7},{7,6},{8,9},{9,8},{10,11... | collective-permute-start | bytes 12582920 | tf_op jit(solution)/shard_map/ppermute | solution.py:18
  102.0 18.2 %collective-permute-start.8 = (bf16[1,2,512,512]{3,2,1,0:T(8,128)(2,1)}, bf16[1,2,512,512]{3,2,1,0:T(8,128)(2,1)}, u32[]{:S(2)}, u32[]{:S(2)}) collective-permute-start(bf16[1,2,512,512]{3,2,1,0:T(8,128)(2,1)} %get-tuple-element.67), channel_id=1, source_target_pairs={{0,1},{1,0},{2,3},{3,2},{4,8},{5,9},{6,10},{7,11},{8,4},{9,5},{10,... | collective-permute-start | bytes 3145736 | tf_op jit(solution)/shard_map/ppermute | solution.py:25
  102.6 28.1 %collective-permute-start.7 = (bf16[1,2,512,512]{3,2,1,0:T(8,128)(2,1)}, bf16[1,2,512,512]{3,2,1,0:T(8,128)(2,1)}, u32[]{:S(2)}, u32[]{:S(2)}) collective-permute-start(bf16[1,2,512,512]{3,2,1,0:T(8,128)(2,1)} %get-tuple-element.65), channel_id=1, source_target_pairs={{0,4},{2,6},{4,0},{6,2},{8,12},{10,14},{12,8},{14,10},{1,5},{3,7},... | collective-permute-start | bytes 3145736 | tf_op jit(solution)/shard_map/ppermute | solution.py:18
  106.9 25.3 %collective-permute-start.6 = (bf16[1,2,512,512]{3,2,1,0:T(8,128)(2,1)}, bf16[1,2,512,512]{3,2,1,0:T(8,128)(2,1)}, u32[]{:S(2)}, u32[]{:S(2)}) collective-permute-start(bf16[1,2,512,512]{3,2,1,0:T(8,128)(2,1)} %get-tuple-element.64.refs_1_), channel_id=1, source_target_pairs={{0,2},{2,0},{4,6},{6,4},{8,10},{10,8},{12,14},{14,12},{1,3},{3,1},... | collective-permute-start | bytes 3145736 | tf_op jit(solution)/shard_map/ppermute | solution.py:18
  132.2 10.9 %collective-permute-start.13 = (bf16[2,2,512,512]{3,2,1,0:T(8,128)(2,1)}, bf16[2,2,512,512]{3,2,1,0:T(8,128)(2,1)}, u32[]{:S(2)}, u32[]{:S(2)}) collective-permute-start(bf16[2,2,512,512]{3,2,1,0:T(8,128)(2,1)} %collective-permute-done.5.refs_0_.refs_1_.refs_3_.refs_4_), channel_id=1, source_target_pairs={{0,1},{1,0},{2,3},{3,2},{4,5},{5,4},{6,7},{7,6},{8,9},{9,8},{10,11... | collective-permute-start | bytes 6291464 | tf_op jit(solution)/shard_map/ppermute | solution.py:18
  132.2 11.0 %collective-permute-start.14 = (bf16[2,2,512,512]{3,2,1,0:T(8,128)(2,1)}, bf16[2,2,512,512]{3,2,1,0:T(8,128)(2,1)}, u32[]{:S(2)}, u32[]{:S(2)}) collective-permute-start(bf16[2,2,512,512]{3,2,1,0:T(8,128)(2,1)} %collective-permute-done.4.middles.refs_2_), channel_id=1, source_target_pairs={{0,1},{1,0},{2,3},{3,2},{4,5},{5,4},{6,7},{7,6},{8,9},{9,8},{10,11... | collective-permute-start | bytes 6291464 | tf_op jit(solution)/shard_map/ppermute | solution.py:18
  132.7 25.4 %collective-permute-start.10 = (bf16[1,2,512,512]{3,2,1,0:T(8,128)(2,1)}, bf16[1,2,512,512]{3,2,1,0:T(8,128)(2,1)}, u32[]{:S(2)}, u32[]{:S(2)}) collective-permute-start(bf16[1,2,512,512]{3,2,1,0:T(8,128)(2,1)} %get-tuple-element.76.refs_1_), channel_id=1, source_target_pairs={{0,2},{2,0},{4,6},{6,4},{8,10},{10,8},{12,14},{14,12},{1,3},{3,1},... | collective-permute-start | bytes 3145736 | tf_op jit(solution)/shard_map/ppermute | solution.py:18
  133.3 25.1 %collective-permute-start.11 = (bf16[1,2,512,512]{3,2,1,0:T(8,128)(2,1)}, bf16[1,2,512,512]{3,2,1,0:T(8,128)(2,1)}, u32[]{:S(2)}, u32[]{:S(2)}) collective-permute-start(bf16[1,2,512,512]{3,2,1,0:T(8,128)(2,1)} %get-tuple-element.77), channel_id=1, source_target_pairs={{0,4},{2,6},{4,0},{6,2},{8,12},{10,14},{12,8},{14,10},{1,5},{3,7},... | collective-permute-start | bytes 3145736 | tf_op jit(solution)/shard_map/ppermute | solution.py:18
  133.6 24.8 %collective-permute-start.12 = (bf16[1,2,512,512]{3,2,1,0:T(8,128)(2,1)}, bf16[1,2,512,512]{3,2,1,0:T(8,128)(2,1)}, u32[]{:S(2)}, u32[]{:S(2)}) collective-permute-start(bf16[1,2,512,512]{3,2,1,0:T(8,128)(2,1)} %get-tuple-element.78), channel_id=1, source_target_pairs={{0,1},{1,0},{2,3},{3,2},{4,8},{5,9},{6,10},{7,11},{8,4},{9,5},{10,... | collective-permute-start | bytes 3145736 | tf_op jit(solution)/shard_map/ppermute | solution.py:25
  158.4 12.0 %collective-permute-start.15 = (bf16[1,2,512,512]{3,2,1,0:T(8,128)(2,1)}, bf16[1,2,512,512]{3,2,1,0:T(8,128)(2,1)}, u32[]{:S(2)}, u32[]{:S(2)}) collective-permute-start(bf16[1,2,512,512]{3,2,1,0:T(8,128)(2,1)} %collective-permute-done.8.w7.refs_2_), channel_id=1, source_target_pairs={{0,1},{1,0},{2,3},{3,2},{4,5},{5,4},{6,7},{7,6},{8,9},{9,8},{10,11... | collective-permute-start | bytes 3145736 | tf_op jit(solution)/shard_map/ppermute | solution.py:18
  158.4 12.1 %collective-permute-start.16 = (bf16[1,2,512,512]{3,2,1,0:T(8,128)(2,1)}, bf16[1,2,512,512]{3,2,1,0:T(8,128)(2,1)}, u32[]{:S(2)}, u32[]{:S(2)}) collective-permute-start(bf16[1,2,512,512]{3,2,1,0:T(8,128)(2,1)} %collective-permute-done.6.w5.refs_3_), channel_id=1, source_target_pairs={{0,1},{1,0},{2,3},{3,2},{4,5},{5,4},{6,7},{7,6},{8,9},{9,8},{10,11... | collective-permute-start | bytes 3145736 | tf_op jit(solution)/shard_map/ppermute | solution.py:18
  158.9 11.6 %collective-permute-start.18 = (bf16[1,2,512,512]{3,2,1,0:T(8,128)(2,1)}, bf16[1,2,512,512]{3,2,1,0:T(8,128)(2,1)}, u32[]{:S(2)}, u32[]{:S(2)}) collective-permute-start(bf16[1,2,512,512]{3,2,1,0:T(8,128)(2,1)} %collective-permute-done.10.w5.refs_9_), channel_id=1, source_target_pairs={{0,1},{1,0},{2,3},{3,2},{4,5},{5,4},{6,7},{7,6},{8,9},{9,8},{10,11... | collective-permute-start | bytes 3145736 | tf_op jit(solution)/shard_map/ppermute | solution.py:18
  158.9 11.6 %collective-permute-start.17 = (bf16[1,2,512,512]{3,2,1,0:T(8,128)(2,1)}, bf16[1,2,512,512]{3,2,1,0:T(8,128)(2,1)}, u32[]{:S(2)}, u32[]{:S(2)}) collective-permute-start(bf16[1,2,512,512]{3,2,1,0:T(8,128)(2,1)} %collective-permute-done.12.w7.refs_8_), channel_id=1, source_target_pairs={{0,1},{1,0},{2,3},{3,2},{4,5},{5,4},{6,7},{7,6},{8,9},{9,8},{10,11... | collective-permute-start | bytes 3145736 | tf_op jit(solution)/shard_map/ppermute | solution.py:18
  170.5 18.8 %copy-start.1 = (s32[16]{0:T(128)S(1)}, s32[16]{0:T(128)}, u32[]{:S(2)}) copy-start(s32[16]{0:T(128)} %param.13) | copy-start | bytes 196
  171.9 16.4 %all-to-all-start = ((f32[16,4,512]{2,1,0:T(4,128)}), f32[16,4,512]{2,1,0:T(4,128)S(1)}, u32[]{:S(2)}, u32[]{:S(2)}) async-start(f32[16,4,512]{2,1,0:T(4,128)} %shard_map.134), calls=%async_computation | async-start | bytes 262144 | tf_op jit(solution)/shard_map/all_to_all | solution.py:41

commit v15 on v14

--- a/solution.py
+++ b/solution.py
@@ -473,29 +473,27 @@
 def next_kernel(freq, ids, ends, middles, cross, over_x, over_z, stage, in_sem, out_sem):
     width = ends.shape[2]
     columns = pl.ds(pl.multiple_of(ids[1] * width, width), width)
-    block = [cross.at[1, freq, pl.ds(half * width, width), columns] for half in range(2)]
-    plans = [
-        [(ends.at[freq, 0], 0), (ends.at[freq, 1], 1), (block[0], 2), (block[1], 3)],
-        [(middles.at[freq, 0], 0), (middles.at[freq, 1], 1)],
-    ]
+    chunk = width // 4
+    plans = [[], []]
+    for part in range(2):
+        for k in range(4):
+            here = pl.ds(k * chunk, chunk)
+            block = cross.at[1, freq, pl.ds(part * width + k * chunk, chunk), columns]
+            plans[0].append((ends.at[freq, part, here], over_x.at[0, part, here]))
+            plans[0].append((block, over_z.at[0, part, here]))
+            plans[1].append((middles.at[freq, part, here], over_x.at[0, part, here]))
+            plans[1].append((None, over_z.at[0, part, here]))
     for mid, plan in enumerate(plans):
 
         @pl.when(ids[0] == mid)
-        def _(mid=mid, plan=plan):
-            reads = [
-                pltpu.make_async_copy(source, stage.at[k], in_sem.at[k]) for source, k in plan
-            ]
-            writes = [
-                [pltpu.make_async_copy(stage.at[k], over_x.at[0, k], out_sem.at[k])]
-                if k < 2
-                else [pltpu.make_async_copy(stage.at[k], over_z.at[0, k - 2], out_sem.at[k])]
-                for _, k in plan
-            ]
-            if mid:
-                for k in range(2):
-                    writes[k].append(
-                        pltpu.make_async_copy(stage.at[k], over_z.at[0, k], out_sem.at[2 + k])
-                    )
+        def _(plan=plan):
+            reads, writes = [], []
+            for k, (source, target) in enumerate(plan):
+                place = k if source is not None else k - 1
+                if source is not None:
+                    reads.append(pltpu.make_async_copy(source, stage.at[k], in_sem.at[k]))
+                    writes.append([])
+                writes[-1].append(pltpu.make_async_copy(stage.at[place], target, out_sem.at[k]))
             for copy in reads:
                 copy.start()
             for read, group in zip(reads, writes):
@@ -519,9 +517,9 @@
             in_specs=[ANYWHERE] * 3,
             out_specs=[ANYWHERE] * 2,
             scratch_shapes=[
-                pltpu.VMEM((4, width, sources), ends.dtype),
-                pltpu.SemaphoreType.DMA((4,)),
-                pltpu.SemaphoreType.DMA((4,)),
+                pltpu.VMEM((16, width // 4, sources), ends.dtype),
+                pltpu.SemaphoreType.DMA((16,)),
+                pltpu.SemaphoreType.DMA((16,)),
             ],
         ),
         compiler_params=pltpu.CompilerParams(vmem_limit_bytes=VMEM_LIMIT),

time: 191 us -> 191 us (level)
  no operation moved by 1% of the time
where the time goes in v15:
time: 191 us; the launch traced here: 190 us
  Pallas kernels  92.1 us (48%)
  waiting for transfers between devices  63.2 us (33%)
  starting transfers between devices  24.2 us (13%)
  other arithmetic  4.57 us (2%)
  local copies, waits for them, and re-layouts  4.31 us (2%)
    pallas_call x6, Pallas kernels, add_field(): pl.pallas_call(functools.partial(field_kernel, freq, count, has_total, ga...  55.5 us
    ppermute x15, waiting for transfers between devices, swap(): lax.ppermute(value, axis, [(source, source ^ mask) for source in range(si...  55.3 us
    pallas_call x2, Pallas kernels, add_late(): pl.pallas_call(functools.partial(late_kernel, freq), out_shape=(jax.Shape...  21.9 us
    ppermute x15, starting transfers between devices, swap(): lax.ppermute(value, axis, [(source, source ^ mask) for source in range(si...  14.6 us
    all_to_all x1, starting transfers between devices, sum_all(): return jnp.sum(lax.all_to_all(copies, axes, 0, 0, tiled=True), axis=0)  8.49 us
    all_to_all x1, waiting for transfers between devices, sum_all(): return jnp.sum(lax.all_to_all(copies, axes, 0, 0, tiled=True), axis=0)  7.93 us
    pallas_call x2, Pallas kernels, copies(): pl.pallas_call(functools.partial(copy_kernel, len(args), jobs), out_shape...  6.7 us
    pallas_call x2, Pallas kernels, take_next(): pl.pallas_call(functools.partial(next_kernel, freq), out_shape=[shape, sh...  6.55 us
  transfers between devices with their start and end apart: 20, of which 9 were waited for; matrix products, arithmetic and copies ran while one was open for 4% of the time, Pallas kernels for 48%

profile of v15, /device:TPU:0, one launch (start us, length us, event | category | flops | bytes accessed | tf_op | source)
XLA Modules:
  0.0 190.3 jit_solution(9953686555303528919)
XLA Ops:
  0.6 0.5 collective-permute-start.2
  1.1 4.1 %collective-permute-start.1 = (bf16[2,2,512,512]{3,2,1,0:T(8,128)(2,1)}, bf16[2,2,512,512]{3,2,1,0:T(8,128)(2,1)}, u32[]{:S(2)}, u32[]{:S(2)}) collective-permute-start(bf16[2,2,512,512]{3,2,1,0:T(8,128)(2,1)} %bitcast.18), channel_id=1, source_target_pairs={{0,4},{2,6},{4,0},{6,2},{8,12},{10,14},{12,8},{14,10},{1,5},{3,7},... | collective-permute-start | bytes 6291464 | tf_op jit(solution)/shard_map/ppermute | solution.py:18
  5.3 1.5 collective-permute-start
  6.8 5.8 %shard_map.124.refs_3_ = f32[2,1024,512]{2,1,0:T(8,128)} custom-call(s32[1]{0:T(128)} %bitcast.2.ids, bf16[2,2,1024,4096]{3,2,1,0:T(8,128)(2,1)} %cross.19, bf16[2,2,512,512]{3,2,1,0:T(8,128)(2,1)} %bitcast.20), custom_call_target="tpu_custom_call" | custom-call | flops 1 | bytes 1 | tf_op jit(solution)/shard_map/pallas_call | solution.py:136
  12.6 0.0 copy-start
  12.6 0.0 copy-start.2
  12.6 5.9 %shard_map.123.refs_3_ = f32[2,1024,512]{2,1,0:T(8,128)} custom-call(s32[1]{0:T(128)} %bitcast.2.ids, bf16[2,2,1024,4096]{3,2,1,0:T(8,128)(2,1)} %cross.19, bf16[2,2,512,512]{3,2,1,0:T(8,128)(2,1)} %bitcast.21), custom_call_target="tpu_custom_call" | custom-call | flops 1 | bytes 1 | tf_op jit(solution)/shard_map/pallas_call | solution.py:136
  18.7 0.5 fusion.16
  19.2 0.6 concatenate.11.ids
  19.8 0.7 pad_add_fusion.ids
  20.5 0.6 pad_add_fusion.1.ids
  21.1 2.6 %multiply_reduce_fusion.norms = f32[2,512]{1,0:T(2,128)} fusion(bf16[2,2,1,512,512]{4,3,2,1,0:T(8,128)(2,1)} %param.12), kind=kLoop, calls=%fused_computation | loop fusion | flops 3144704 | bytes 2101248 | tf_op jit(solution)/shard_map/reduce_sum | solution.py:639
  23.7 3.1 %shard_map.122.refs_2_.refs_3_ = bf16[2,2,512,512]{3,2,1,0:T(8,128)(2,1)} custom-call(s32[2]{0:T(128)} %pad_add_fusion.ids, bf16[2,2,512,512]{3,2,1,0:T(8,128)(2,1)} %collective-permute-done.2.refs_0_, bf16[2,2,1024,4096]{3,2,1,0:T(8,128)(2,1)} %cross.19), custom_call_target="tpu_custom_call", output_to_operand_aliasing={{}: (1, {})} | custom-call | flops 1 | bytes 1 | tf_op jit(solution)/shard_map/pallas_call | solution.py:416
  26.8 24.2 %collective-permute-done.1.refs_1_.refs_2_ = bf16[2,2,512,512]{3,2,1,0:T(8,128)(2,1)} collective-permute-done((bf16[2,2,512,512]{3,2,1,0:T(8,128)(2,1)}, bf16[2,2,512,512]{3,2,1,0:T(8,128)(2,1)}, u32[]{:S(2)}, u32[]{:S(2)}) %collective-permute-start.1) | collective-permute-done | bytes 2097184 | tf_op jit(solution)/shard_map/ppermute | solution.py:18
  51.0 1.4 collective-permute-done.refs_0_.refs_1_
  52.4 0.3 collective-permute-start.3
  52.7 1.5 collective-permute-start.5
  54.2 12.3 %shard_map.125.refs_2_ = f32[2,1024,512]{2,1,0:T(8,128)} custom-call(s32[4]{0:T(128)} %pad_add_fusion.1.ids, bf16[2,2,1024,4096]{3,2,1,0:T(8,128)(2,1)} %cross.19, bf16[2,2,512,512]{3,2,1,0:T(8,128)(2,1)} %collective-permute-done.refs_0_.refs_1_, bf16[2,2,512,512]{3,2,1,0:T(8,128)(2,1)} %collective-permute-done.1.refs_1_.refs_2_, ...), custom_call_target="tpu_custom_call" | custom-call | flops 1 | bytes 1 | tf_op jit(solution)/shard_map/pallas_call | solution.py:136
  66.5 12.4 %shard_map.126.refs_2_ = f32[2,1024,512]{2,1,0:T(8,128)} custom-call(s32[4]{0:T(128)} %pad_add_fusion.1.ids, bf16[2,2,1024,4096]{3,2,1,0:T(8,128)(2,1)} %cross.19, bf16[2,2,512,512]{3,2,1,0:T(8,128)(2,1)} %collective-permute-done.refs_0_.refs_1_, bf16[2,2,512,512]{3,2,1,0:T(8,128)(2,1)} %collective-permute-done.1.refs_1_.refs_2_, ...), custom_call_target="tpu_custom_call" | custom-call | flops 1 | bytes 1 | tf_op jit(solution)/shard_map/pallas_call | solution.py:136
  78.9 3.6 %shard_map.127.refs_0_ = bf16[2,2,1024,512]{3,2,1,0:T(8,128)(2,1)} custom-call(s32[1]{0:T(128)} %bitcast.6.ids, bf16[2,2,512,512]{3,2,1,0:T(8,128)(2,1)} %bitcast.22, bf16[2,2,512,512]{3,2,1,0:T(8,128)(2,1)} %collective-permute-done.refs_0_.refs_1_, bf16[2,2,512,512]{3,2,1,0:T(8,128)(2,1)} %collective-permute-done.1.refs_1_.refs_2_, ...), custom_call_target="tpu_custom_call" | custom-call | flops 1 | bytes 1 | tf_op jit(solution)/shard_map/pallas_call | solution.py:416
  82.5 3.0 %fusion.18 = (bf16[1,2,512,512]{3,2,1,0:T(8,128)(2,1)}, bf16[1,2,512,512]{3,2,1,0:T(8,128)(2,1)}) fusion(bf16[2,2,512,512]{3,2,1,0:T(8,128)(2,1)} %collective-permute-done.refs_0_.refs_1_), kind=kLoop, calls=%fused_computation.40 | loop fusion | bytes 4194304 | tf_op jit(solution)/shard_map/slice | solution.py:583
  85.5 13.1 %collective-permute-done.3.ends.block_re.block_im = bf16[2,2,512,512]{3,2,1,0:T(8,128)(2,1)} collective-permute-done((bf16[2,2,512,512]{3,2,1,0:T(8,128)(2,1)}, bf16[2,2,512,512]{3,2,1,0:T(8,128)(2,1)}, u32[]{:S(2)}, u32[]{:S(2)}) %collective-permute-start.3) | collective-permute-done | bytes 2097184 | tf_op jit(solution)/shard_map/ppermute | solution.py:18
  98.6 0.3 collective-permute-done.5.refs_0_.refs_1_.refs_3_.refs_4_
  98.9 3.3 %shard_map.128 = (bf16[1,2,512,512]{3,2,1,0:T(8,128)(2,1)}, bf16[1,2,512,512]{3,2,1,0:T(8,128)(2,1)}) custom-call(s32[2]{0:T(128)} %pad_add_fusion.ids, bf16[2,2,512,512]{3,2,1,0:T(8,128)(2,1)} %collective-permute-done.3.ends.block_re.block_im, bf16[2,2,512,512]{3,2,1,0:T(8,128)(2,1)} %collective-permute-done.4.middles.refs_2_, bf16[2,2,1024,4096]{3,2,1,0:T(8,128)(2,1)} %cross.19), custom_call_target="tpu_custom_call" | custom-call | flops 1 | bytes 1 | tf_op jit(solution)/shard_map/pallas_call | solution.py:511
  102.2 0.6 collective-permute-start.8
  102.8 4.3 %collective-permute-start.7 = (bf16[1,2,512,512]{3,2,1,0:T(8,128)(2,1)}, bf16[1,2,512,512]{3,2,1,0:T(8,128)(2,1)}, u32[]{:S(2)}, u32[]{:S(2)}) collective-permute-start(bf16[1,2,512,512]{3,2,1,0:T(8,128)(2,1)} %get-tuple-element.65), channel_id=1, source_target_pairs={{0,4},{2,6},{4,0},{6,2},{8,12},{10,14},{12,8},{14,10},{1,5},{3,7},... | collective-permute-start | bytes 3145736 | tf_op jit(solution)/shard_map/ppermute | solution.py:18
  107.2 0.5 collective-permute-start.6
  107.7 9.6 %shard_map.129.total = f32[2,1024,512]{2,1,0:T(8,128)} custom-call(s32[2]{0:T(128)} %get-tuple-element.69.ids, bf16[2,2,1024,4096]{3,2,1,0:T(8,128)(2,1)} %cross.19, bf16[2,2,512,512]{3,2,1,0:T(8,128)(2,1)} %collective-permute-done.5.refs_0_.refs_1_.refs_3_.refs_4_, bf16[1,2,512,512]{3,2,1,0:T(8,128)(2,1)} %get-tuple-element.64.refs_1_, ...), custom_call_target="tpu_custom_call" | custom-call | flops 1 | bytes 1 | tf_op jit(solution)/shard_map/pallas_call | solution.py:136
  117.3 3.2 %shard_map.130 = (bf16[1,2,512,512]{3,2,1,0:T(8,128)(2,1)}, bf16[1,2,512,512]{3,2,1,0:T(8,128)(2,1)}) custom-call(s32[2]{0:T(128)} %pad_add_fusion.ids, bf16[2,2,512,512]{3,2,1,0:T(8,128)(2,1)} %collective-permute-done.3.ends.block_re.block_im, bf16[2,2,512,512]{3,2,1,0:T(8,128)(2,1)} %collective-permute-done.4.middles.refs_2_, bf16[2,2,1024,4096]{3,2,1,0:T(8,128)(2,1)} %cross.19), custom_call_target="tpu_custom_call" | custom-call | flops 1 | bytes 1 | tf_op jit(solution)/shard_map/pallas_call | solution.py:511
  120.5 10.5 %collective-permute-done.7.w6.block_re = bf16[1,2,512,512]{3,2,1,0:T(8,128)(2,1)} collective-permute-done((bf16[1,2,512,512]{3,2,1,0:T(8,128)(2,1)}, bf16[1,2,512,512]{3,2,1,0:T(8,128)(2,1)}, u32[]{:S(2)}, u32[]{:S(2)}) %collective-permute-start.7) | collective-permute-done | bytes 1048608 | tf_op jit(solution)/shard_map/ppermute | solution.py:18
  131.0 1.5 collective-permute-done.6.w5.refs_3_
  132.5 0.5 collective-permute-start.14
  133.0 0.5 collective-permute-start.10
  133.5 0.3 collective-permute-start.11
  133.8 9.6 %shard_map.132.total = f32[2,1024,512]{2,1,0:T(8,128)} custom-call(s32[2]{0:T(128)} %get-tuple-element.69.ids, bf16[2,2,1024,4096]{3,2,1,0:T(8,128)(2,1)} %cross.19, bf16[2,2,512,512]{3,2,1,0:T(8,128)(2,1)} %collective-permute-done.5.refs_0_.refs_1_.refs_3_.refs_4_, bf16[1,2,512,512]{3,2,1,0:T(8,128)(2,1)} %get-tuple-element.76.refs_1_, ...), custom_call_target="tpu_custom_call" | custom-call | flops 1 | bytes 1 | tf_op jit(solution)/shard_map/pallas_call | solution.py:136
  143.4 10.9 %shard_map.131 = (f32[8,512]{1,0:T(8,128)}, f32[2,512,512]{2,1,0:T(8,128)}) custom-call(s32[8]{0:T(128)} %concatenate.11.ids, bf16[2,2,1024,4096]{3,2,1,0:T(8,128)(2,1)} %cross.19, bf16[1,2,512,512]{3,2,1,0:T(8,128)(2,1)} %collective-permute-done.6.w5.refs_3_, bf16[1,2,512,512]{3,2,1,0:T(8,128)(2,1)} %collective-permute-done.7.w6.block_re, ...), custom_call_target="tpu_custom_call" | custom-call | flops 1 | bytes 1 | tf_op jit(solution)/shard_map/pallas_call | solution.py:306
  154.3 4.1 %collective-permute-done.10.w5.refs_9_ = bf16[1,2,512,512]{3,2,1,0:T(8,128)(2,1)} collective-permute-done((bf16[1,2,512,512]{3,2,1,0:T(8,128)(2,1)}, bf16[1,2,512,512]{3,2,1,0:T(8,128)(2,1)}, u32[]{:S(2)}, u32[]{:S(2)}) %collective-permute-start.10) | collective-permute-done | bytes 1048608 | tf_op jit(solution)/shard_map/ppermute | solution.py:18
  158.4 0.3 collective-permute-done.11.w6.block_im
  158.6 0.5 collective-permute-start.16
  159.2 0.5 collective-permute-start.17
  159.7 11.0 %shard_map.133 = (f32[8,512]{1,0:T(8,128)}, f32[2,512,512]{2,1,0:T(8,128)}) custom-call(s32[8]{0:T(128)} %concatenate.11.ids, bf16[2,2,1024,4096]{3,2,1,0:T(8,128)(2,1)} %cross.19, bf16[1,2,512,512]{3,2,1,0:T(8,128)(2,1)} %collective-permute-done.10.w5.refs_9_, bf16[1,2,512,512]{3,2,1,0:T(8,128)(2,1)} %collective-permute-done.11.w6.block_im, ...), custom_call_target="tpu_custom_call" | custom-call | flops 1 | bytes 1 | tf_op jit(solution)/shard_map/pallas_call | solution.py:306
  170.7 1.5 shard_map.134
  172.2 8.5 %all-to-all-start = ((f32[16,4,512]{2,1,0:T(4,128)}), f32[16,4,512]{2,1,0:T(4,128)S(1)}, u32[]{:S(2)}, u32[]{:S(2)}) async-start(f32[16,4,512]{2,1,0:T(4,128)} %shard_map.134), calls=%async_computation | async-start | bytes 262144 | tf_op jit(solution)/shard_map/all_to_all | solution.py:41
  180.7 7.9 %all-to-all-done = f32[16,4,512]{2,1,0:T(4,128)S(1)} async-done(((f32[16,4,512]{2,1,0:T(4,128)}), f32[16,4,512]{2,1,0:T(4,128)S(1)}, u32[]{:S(2)}, u32[]{:S(2)}) %all-to-all-start) | async-done | bytes 131104 | tf_op jit(solution)/shard_map/all_to_all | solution.py:41
  188.7 0.1 abs_reduce_fusion
  188.8 0.1 reshape.41
  188.9 0.6 constant_dynamic-slice_fusion
  189.5 0.8 fusion
  (25 shorter events, 0.1 us)
Async XLA Ops:
  0.6 23.1 %collective-permute-start.2 = (bf16[2,2,512,512]{3,2,1,0:T(8,128)(2,1)}, bf16[2,2,512,512]{3,2,1,0:T(8,128)(2,1)}, u32[]{:S(2)}, u32[]{:S(2)}) collective-permute-start(bf16[2,2,512,512]{3,2,1,0:T(8,128)(2,1)} %bitcast.17), channel_id=1, source_target_pairs={{0,1},{1,0},{2,3},{3,2},{4,8},{5,9},{6,10},{7,11},{8,4},{9,5},{10,... | collective-permute-start | bytes 6291464 | tf_op jit(solution)/shard_map/ppermute | solution.py:25
  1.1 49.8 %collective-permute-start.1 = (bf16[2,2,512,512]{3,2,1,0:T(8,128)(2,1)}, bf16[2,2,512,512]{3,2,1,0:T(8,128)(2,1)}, u32[]{:S(2)}, u32[]{:S(2)}) collective-permute-start(bf16[2,2,512,512]{3,2,1,0:T(8,128)(2,1)} %bitcast.18), channel_id=1, source_target_pairs={{0,4},{2,6},{4,0},{6,2},{8,12},{10,14},{12,8},{14,10},{1,5},{3,7},... | collective-permute-start | bytes 6291464 | tf_op jit(solution)/shard_map/ppermute | solution.py:18
  5.3 47.1 %collective-permute-start = (bf16[2,2,512,512]{3,2,1,0:T(8,128)(2,1)}, bf16[2,2,512,512]{3,2,1,0:T(8,128)(2,1)}, u32[]{:S(2)}, u32[]{:S(2)}) collective-permute-start(bf16[2,2,512,512]{3,2,1,0:T(8,128)(2,1)} %bitcast.19), channel_id=1, source_target_pairs={{0,2},{2,0},{4,6},{6,4},{8,10},{10,8},{12,14},{14,12},{1,3},{3,1},... | collective-permute-start | bytes 6291464 | tf_op jit(solution)/shard_map/ppermute | solution.py:18
  12.6 6.1 %copy-start = (s32[2]{0:T(128)S(1)}, s32[2]{0:T(128)}, u32[]{:S(2)}) copy-start(s32[2]{0:T(128)} %constant.117.clone) | copy-start | bytes 28
  12.6 7.9 %copy-start.2 = (s32[3]{0:T(128)S(1)}, s32[3]{0:T(128)}, u32[]{:S(2)}) copy-start(s32[3]{0:T(128)} %constant.116.clone) | copy-start | bytes 40
  52.4 46.2 %collective-permute-start.3 = (bf16[2,2,512,512]{3,2,1,0:T(8,128)(2,1)}, bf16[2,2,512,512]{3,2,1,0:T(8,128)(2,1)}, u32[]{:S(2)}, u32[]{:S(2)}) collective-permute-start(bf16[2,2,512,512]{3,2,1,0:T(8,128)(2,1)} %shard_map.122.refs_2_.refs_3_), channel_id=1, source_target_pairs={{0,4},{2,6},{4,0},{6,2},{8,12},{10,14},{12,8},{14,10},{1,5},{3,7},... | collective-permute-start | bytes 6291464 | tf_op jit(solution)/shard_map/ppermute | solution.py:18
  52.7 46.2 %collective-permute-start.5 = (bf16[2,2,512,512]{3,2,1,0:T(8,128)(2,1)}, bf16[2,2,512,512]{3,2,1,0:T(8,128)(2,1)}, u32[]{:S(2)}, u32[]{:S(2)}) collective-permute-start(bf16[2,2,512,512]{3,2,1,0:T(8,128)(2,1)} %collective-permute-done.1.refs_1_.refs_2_), channel_id=1, source_target_pairs={{0,2},{2,0},{4,6},{6,4},{8,10},{10,8},{12,14},{14,12},{1,3},{3,1},... | collective-permute-start | bytes 6291464 | tf_op jit(solution)/shard_map/ppermute | solution.py:18
  54.2 44.7 %collective-permute-start.4 = (bf16[2,2,512,512]{3,2,1,0:T(8,128)(2,1)}, bf16[2,2,512,512]{3,2,1,0:T(8,128)(2,1)}, u32[]{:S(2)}, u32[]{:S(2)}) collective-permute-start(bf16[2,2,512,512]{3,2,1,0:T(8,128)(2,1)} %collective-permute-done.1.refs_1_.refs_2_), channel_id=1, source_target_pairs={{0,1},{1,0},{2,3},{3,2},{4,8},{5,9},{6,10},{7,11},{8,4},{9,5},{10,... | collective-permute-start | bytes 6291464 | tf_op jit(solution)/shard_map/ppermute | solution.py:25
  98.9 33.6 %collective-permute-start.9 = (bf16[2,2,1024,512]{3,2,1,0:T(8,128)(2,1)}, bf16[2,2,1024,512]{3,2,1,0:T(8,128)(2,1)}, u32[]{:S(2)}, u32[]{:S(2)}) collective-permute-start(bf16[2,2,1024,512]{3,2,1,0:T(8,128)(2,1)} %shard_map.127.refs_0_), channel_id=1, source_target_pairs={{0,1},{1,0},{2,3},{3,2},{4,5},{5,4},{6,7},{7,6},{8,9},{9,8},{10,11... | collective-permute-start | bytes 12582920 | tf_op jit(solution)/shard_map/ppermute | solution.py:18
  102.2 18.3 %collective-permute-start.8 = (bf16[1,2,512,512]{3,2,1,0:T(8,128)(2,1)}, bf16[1,2,512,512]{3,2,1,0:T(8,128)(2,1)}, u32[]{:S(2)}, u32[]{:S(2)}) collective-permute-start(bf16[1,2,512,512]{3,2,1,0:T(8,128)(2,1)} %get-tuple-element.67), channel_id=1, source_target_pairs={{0,1},{1,0},{2,3},{3,2},{4,8},{5,9},{6,10},{7,11},{8,4},{9,5},{10,... | collective-permute-start | bytes 3145736 | tf_op jit(solution)/shard_map/ppermute | solution.py:25
  102.8 28.2 %collective-permute-start.7 = (bf16[1,2,512,512]{3,2,1,0:T(8,128)(2,1)}, bf16[1,2,512,512]{3,2,1,0:T(8,128)(2,1)}, u32[]{:S(2)}, u32[]{:S(2)}) collective-permute-start(bf16[1,2,512,512]{3,2,1,0:T(8,128)(2,1)} %get-tuple-element.65), channel_id=1, source_target_pairs={{0,4},{2,6},{4,0},{6,2},{8,12},{10,14},{12,8},{14,10},{1,5},{3,7},... | collective-permute-start | bytes 3145736 | tf_op jit(solution)/shard_map/ppermute | solution.py:18
  107.2 25.3 %collective-permute-start.6 = (bf16[1,2,512,512]{3,2,1,0:T(8,128)(2,1)}, bf16[1,2,512,512]{3,2,1,0:T(8,128)(2,1)}, u32[]{:S(2)}, u32[]{:S(2)}) collective-permute-start(bf16[1,2,512,512]{3,2,1,0:T(8,128)(2,1)} %get-tuple-element.64.refs_1_), channel_id=1, source_target_pairs={{0,2},{2,0},{4,6},{6,4},{8,10},{10,8},{12,14},{14,12},{1,3},{3,1},... | collective-permute-start | bytes 3145736 | tf_op jit(solution)/shard_map/ppermute | solution.py:18
  132.5 10.9 %collective-permute-start.13 = (bf16[2,2,512,512]{3,2,1,0:T(8,128)(2,1)}, bf16[2,2,512,512]{3,2,1,0:T(8,128)(2,1)}, u32[]{:S(2)}, u32[]{:S(2)}) collective-permute-start(bf16[2,2,512,512]{3,2,1,0:T(8,128)(2,1)} %collective-permute-done.5.refs_0_.refs_1_.refs_3_.refs_4_), channel_id=1, source_target_pairs={{0,1},{1,0},{2,3},{3,2},{4,5},{5,4},{6,7},{7,6},{8,9},{9,8},{10,11... | collective-permute-start | bytes 6291464 | tf_op jit(solution)/shard_map/ppermute | solution.py:18
  132.5 11.0 %collective-permute-start.14 = (bf16[2,2,512,512]{3,2,1,0:T(8,128)(2,1)}, bf16[2,2,512,512]{3,2,1,0:T(8,128)(2,1)}, u32[]{:S(2)}, u32[]{:S(2)}) collective-permute-start(bf16[2,2,512,512]{3,2,1,0:T(8,128)(2,1)} %collective-permute-done.4.middles.refs_2_), channel_id=1, source_target_pairs={{0,1},{1,0},{2,3},{3,2},{4,5},{5,4},{6,7},{7,6},{8,9},{9,8},{10,11... | collective-permute-start | bytes 6291464 | tf_op jit(solution)/shard_map/ppermute | solution.py:18
  133.0 25.4 %collective-permute-start.10 = (bf16[1,2,512,512]{3,2,1,0:T(8,128)(2,1)}, bf16[1,2,512,512]{3,2,1,0:T(8,128)(2,1)}, u32[]{:S(2)}, u32[]{:S(2)}) collective-permute-start(bf16[1,2,512,512]{3,2,1,0:T(8,128)(2,1)} %get-tuple-element.76.refs_1_), channel_id=1, source_target_pairs={{0,2},{2,0},{4,6},{6,4},{8,10},{10,8},{12,14},{14,12},{1,3},{3,1},... | collective-permute-start | bytes 3145736 | tf_op jit(solution)/shard_map/ppermute | solution.py:18
  133.5 25.1 %collective-permute-start.11 = (bf16[1,2,512,512]{3,2,1,0:T(8,128)(2,1)}, bf16[1,2,512,512]{3,2,1,0:T(8,128)(2,1)}, u32[]{:S(2)}, u32[]{:S(2)}) collective-permute-start(bf16[1,2,512,512]{3,2,1,0:T(8,128)(2,1)} %get-tuple-element.77), channel_id=1, source_target_pairs={{0,4},{2,6},{4,0},{6,2},{8,12},{10,14},{12,8},{14,10},{1,5},{3,7},... | collective-permute-start | bytes 3145736 | tf_op jit(solution)/shard_map/ppermute | solution.py:18
  133.8 24.8 %collective-permute-start.12 = (bf16[1,2,512,512]{3,2,1,0:T(8,128)(2,1)}, bf16[1,2,512,512]{3,2,1,0:T(8,128)(2,1)}, u32[]{:S(2)}, u32[]{:S(2)}) collective-permute-start(bf16[1,2,512,512]{3,2,1,0:T(8,128)(2,1)} %get-tuple-element.78), channel_id=1, source_target_pairs={{0,1},{1,0},{2,3},{3,2},{4,8},{5,9},{6,10},{7,11},{8,4},{9,5},{10,... | collective-permute-start | bytes 3145736 | tf_op jit(solution)/shard_map/ppermute | solution.py:25
  158.6 12.0 %collective-permute-start.15 = (bf16[1,2,512,512]{3,2,1,0:T(8,128)(2,1)}, bf16[1,2,512,512]{3,2,1,0:T(8,128)(2,1)}, u32[]{:S(2)}, u32[]{:S(2)}) collective-permute-start(bf16[1,2,512,512]{3,2,1,0:T(8,128)(2,1)} %collective-permute-done.8.w7.refs_2_), channel_id=1, source_target_pairs={{0,1},{1,0},{2,3},{3,2},{4,5},{5,4},{6,7},{7,6},{8,9},{9,8},{10,11... | collective-permute-start | bytes 3145736 | tf_op jit(solution)/shard_map/ppermute | solution.py:18
  158.6 12.1 %collective-permute-start.16 = (bf16[1,2,512,512]{3,2,1,0:T(8,128)(2,1)}, bf16[1,2,512,512]{3,2,1,0:T(8,128)(2,1)}, u32[]{:S(2)}, u32[]{:S(2)}) collective-permute-start(bf16[1,2,512,512]{3,2,1,0:T(8,128)(2,1)} %collective-permute-done.6.w5.refs_3_), channel_id=1, source_target_pairs={{0,1},{1,0},{2,3},{3,2},{4,5},{5,4},{6,7},{7,6},{8,9},{9,8},{10,11... | collective-permute-start | bytes 3145736 | tf_op jit(solution)/shard_map/ppermute | solution.py:18
  159.1 11.6 %collective-permute-start.18 = (bf16[1,2,512,512]{3,2,1,0:T(8,128)(2,1)}, bf16[1,2,512,512]{3,2,1,0:T(8,128)(2,1)}, u32[]{:S(2)}, u32[]{:S(2)}) collective-permute-start(bf16[1,2,512,512]{3,2,1,0:T(8,128)(2,1)} %collective-permute-done.10.w5.refs_9_), channel_id=1, source_target_pairs={{0,1},{1,0},{2,3},{3,2},{4,5},{5,4},{6,7},{7,6},{8,9},{9,8},{10,11... | collective-permute-start | bytes 3145736 | tf_op jit(solution)/shard_map/ppermute | solution.py:18
  159.2 11.6 %collective-permute-start.17 = (bf16[1,2,512,512]{3,2,1,0:T(8,128)(2,1)}, bf16[1,2,512,512]{3,2,1,0:T(8,128)(2,1)}, u32[]{:S(2)}, u32[]{:S(2)}) collective-permute-start(bf16[1,2,512,512]{3,2,1,0:T(8,128)(2,1)} %collective-permute-done.12.w7.refs_8_), channel_id=1, source_target_pairs={{0,1},{1,0},{2,3},{3,2},{4,5},{5,4},{6,7},{7,6},{8,9},{9,8},{10,11... | collective-permute-start | bytes 3145736 | tf_op jit(solution)/shard_map/ppermute | solution.py:18
  170.7 18.8 %copy-start.1 = (s32[16]{0:T(128)S(1)}, s32[16]{0:T(128)}, u32[]{:S(2)}) copy-start(s32[16]{0:T(128)} %param.13) | copy-start | bytes 196
  172.2 16.4 %all-to-all-start = ((f32[16,4,512]{2,1,0:T(4,128)}), f32[16,4,512]{2,1,0:T(4,128)S(1)}, u32[]{:S(2)}, u32[]{:S(2)}) async-start(f32[16,4,512]{2,1,0:T(4,128)} %shard_map.134), calls=%async_computation | async-start | bytes 262144 | tf_op jit(solution)/shard_map/all_to_all | solution.py:41

commit v16 on v14

--- a/solution.py
+++ b/solution.py
@@ -9,6 +9,7 @@
 from jax.sharding import PartitionSpec as P
 
 VMEM_LIMIT = 63 * 1024 * 1024
+LATE_LIMIT = 40 * 1024 * 1024
 HINT = pl.CostEstimate(flops=1, bytes_accessed=1, transcendentals=0)
 ANYWHERE = pl.BlockSpec(memory_space=pl.ANY)
 
@@ -326,7 +327,7 @@
                 pltpu.SemaphoreType.DMA((2, 2)),
             ],
         ),
-        compiler_params=pltpu.CompilerParams(vmem_limit_bytes=VMEM_LIMIT),
+        compiler_params=pltpu.CompilerParams(vmem_limit_bytes=LATE_LIMIT),
         cost_estimate=HINT,
     )(ids, cross, *pieces, *blocks, total, *row_refs)
 
@@ -379,7 +380,7 @@
                 pltpu.VMEM((4, sources), jnp.float32),
             ],
         ),
-        compiler_params=pltpu.CompilerParams(vmem_limit_bytes=VMEM_LIMIT),
+        compiler_params=pltpu.CompilerParams(vmem_limit_bytes=LATE_LIMIT),
         cost_estimate=HINT,
     )(ids, norms, *groups[0], *groups[1])
 

time: 191 us -> 188 us (0.984)
  Pallas kernels: 91.9 us -> 89.2 us
  waiting for transfers between devices: 63.2 us -> 65.4 us
    ppermute x15, waiting for transfers between devices: 55.3 us -> 57.4 us  [swap(): lax.ppermute(value, axis, [(source, source ^ mask) for source in range(si...]
    pallas_call x2, Pallas kernels: 21.9 us -> 19.8 us  [add_late(): pl.pallas_call(functools.partial(late_kernel, freq), out_shape=(jax.Shape...]
  transfers between devices with their start and end apart: 20 -> 20, of which waited for: 9 -> 9; matrix products, arithmetic and copies ran while one was open for 4% -> 4% of each run, Pallas kernels for 48% -> 47%
where the time goes in v16:
time: 188 us
  Pallas kernels  89.2 us (47%)
  waiting for transfers between devices  65.4 us (35%)
  starting transfers between devices  23.7 us (13%)
  other arithmetic  3.91 us (2%)
  local copies, waits for them, and re-layouts  3.85 us (2%)
    ppermute x15, waiting for transfers between devices, swap(): lax.ppermute(value, axis, [(source, source ^ mask) for source in range(si...  57.4 us
    pallas_call x6, Pallas kernels, add_field(): pl.pallas_call(functools.partial(field_kernel, freq, count, has_total, ga...  55.7 us
    pallas_call x2, Pallas kernels, add_late(): pl.pallas_call(functools.partial(late_kernel, freq), out_shape=(jax.Shape...  19.8 us
    ppermute x15, starting transfers between devices, swap(): lax.ppermute(value, axis, [(source, source ^ mask) for source in range(si...  14.6 us
    all_to_all x1, starting transfers between devices, sum_all(): return jnp.sum(lax.all_to_all(copies, axes, 0, 0, tiled=True), axis=0)  8.05 us
    all_to_all x1, waiting for transfers between devices, sum_all(): return jnp.sum(lax.all_to_all(copies, axes, 0, 0, tiled=True), axis=0)  7.93 us
    pallas_call x2, Pallas kernels, copies(): pl.pallas_call(functools.partial(copy_kernel, len(args), jobs), out_shape...  6.7 us
    pallas_call x2, Pallas kernels, take_next(): pl.pallas_call(functools.partial(next_kernel, freq), out_shape=[shape, sh...  6.22 us
  transfers between devices with their start and end apart: 20, of which 9 were waited for; matrix products, arithmetic and copies ran while one was open for 4% of the time, Pallas kernels for 47%

profile of v16, /device:TPU:0, one launch (start us, length us, event | category | flops | bytes accessed | tf_op | source)
XLA Modules:
  0.0 187.9 jit_solution(14146462179125790560)
XLA Ops:
  0.6 0.5 collective-permute-start.2
  1.1 4.1 %collective-permute-start.1 = (bf16[2,2,512,512]{3,2,1,0:T(8,128)(2,1)}, bf16[2,2,512,512]{3,2,1,0:T(8,128)(2,1)}, u32[]{:S(2)}, u32[]{:S(2)}) collective-permute-start(bf16[2,2,512,512]{3,2,1,0:T(8,128)(2,1)} %bitcast.18), channel_id=1, source_target_pairs={{0,4},{2,6},{4,0},{6,2},{8,12},{10,14},{12,8},{14,10},{1,5},{3,7},... | collective-permute-start | bytes 6291464 | tf_op jit(solution)/shard_map/ppermute | solution.py:19
  5.3 1.5 collective-permute-start
  6.8 5.8 %shard_map.124.refs_3_ = f32[2,1024,512]{2,1,0:T(8,128)} custom-call(s32[1]{0:T(128)} %bitcast.2.ids, bf16[2,2,1024,4096]{3,2,1,0:T(8,128)(2,1)} %cross.19, bf16[2,2,512,512]{3,2,1,0:T(8,128)(2,1)} %bitcast.20), custom_call_target="tpu_custom_call" | custom-call | flops 1 | bytes 1 | tf_op jit(solution)/shard_map/pallas_call | solution.py:137
  12.6 0.0 copy-start
  12.6 0.0 copy-start.2
  12.6 5.9 %shard_map.123.refs_3_ = f32[2,1024,512]{2,1,0:T(8,128)} custom-call(s32[1]{0:T(128)} %bitcast.2.ids, bf16[2,2,1024,4096]{3,2,1,0:T(8,128)(2,1)} %cross.19, bf16[2,2,512,512]{3,2,1,0:T(8,128)(2,1)} %bitcast.21), custom_call_target="tpu_custom_call" | custom-call | flops 1 | bytes 1 | tf_op jit(solution)/shard_map/pallas_call | solution.py:137
  18.7 0.5 fusion.16
  19.2 0.1 concatenate.11.ids
  19.3 0.6 pad_add_fusion.ids
  19.9 0.6 pad_add_fusion.1.ids
  20.5 2.0 %multiply_reduce_fusion.norms = f32[2,512]{1,0:T(2,128)S(1)} fusion(bf16[2,2,1,512,512]{4,3,2,1,0:T(8,128)(2,1)} %param.12), kind=kLoop, calls=%fused_computation | loop fusion | flops 3144704 | bytes 2101248 | tf_op jit(solution)/shard_map/reduce_sum | solution.py:642
  22.5 3.1 %shard_map.122.refs_2_.refs_3_ = bf16[2,2,512,512]{3,2,1,0:T(8,128)(2,1)} custom-call(s32[2]{0:T(128)} %pad_add_fusion.ids, bf16[2,2,512,512]{3,2,1,0:T(8,128)(2,1)} %collective-permute-done.2.refs_0_, bf16[2,2,1024,4096]{3,2,1,0:T(8,128)(2,1)} %cross.19), custom_call_target="tpu_custom_call", output_to_operand_aliasing={{}: (1, {})} | custom-call | flops 1 | bytes 1 | tf_op jit(solution)/shard_map/pallas_call | solution.py:417
  25.6 25.4 %collective-permute-done.1.refs_1_.refs_2_ = bf16[2,2,512,512]{3,2,1,0:T(8,128)(2,1)} collective-permute-done((bf16[2,2,512,512]{3,2,1,0:T(8,128)(2,1)}, bf16[2,2,512,512]{3,2,1,0:T(8,128)(2,1)}, u32[]{:S(2)}, u32[]{:S(2)}) %collective-permute-start.1) | collective-permute-done | bytes 2097184 | tf_op jit(solution)/shard_map/ppermute | solution.py:19
  51.0 1.4 collective-permute-done.refs_0_.refs_1_
  52.4 0.3 collective-permute-start.3
  52.7 1.5 collective-permute-start.5
  54.2 12.3 %shard_map.125.refs_2_ = f32[2,1024,512]{2,1,0:T(8,128)} custom-call(s32[4]{0:T(128)} %pad_add_fusion.1.ids, bf16[2,2,1024,4096]{3,2,1,0:T(8,128)(2,1)} %cross.19, bf16[2,2,512,512]{3,2,1,0:T(8,128)(2,1)} %collective-permute-done.refs_0_.refs_1_, bf16[2,2,512,512]{3,2,1,0:T(8,128)(2,1)} %collective-permute-done.1.refs_1_.refs_2_, ...), custom_call_target="tpu_custom_call" | custom-call | flops 1 | bytes 1 | tf_op jit(solution)/shard_map/pallas_call | solution.py:137
  66.5 12.4 %shard_map.126.refs_2_ = f32[2,1024,512]{2,1,0:T(8,128)} custom-call(s32[4]{0:T(128)} %pad_add_fusion.1.ids, bf16[2,2,1024,4096]{3,2,1,0:T(8,128)(2,1)} %cross.19, bf16[2,2,512,512]{3,2,1,0:T(8,128)(2,1)} %collective-permute-done.refs_0_.refs_1_, bf16[2,2,512,512]{3,2,1,0:T(8,128)(2,1)} %collective-permute-done.1.refs_1_.refs_2_, ...), custom_call_target="tpu_custom_call" | custom-call | flops 1 | bytes 1 | tf_op jit(solution)/shard_map/pallas_call | solution.py:137
  78.9 3.6 %shard_map.127.refs_0_ = bf16[2,2,1024,512]{3,2,1,0:T(8,128)(2,1)} custom-call(s32[1]{0:T(128)} %bitcast.6.ids, bf16[2,2,512,512]{3,2,1,0:T(8,128)(2,1)} %bitcast.22, bf16[2,2,512,512]{3,2,1,0:T(8,128)(2,1)} %collective-permute-done.refs_0_.refs_1_, bf16[2,2,512,512]{3,2,1,0:T(8,128)(2,1)} %collective-permute-done.1.refs_1_.refs_2_, ...), custom_call_target="tpu_custom_call" | custom-call | flops 1 | bytes 1 | tf_op jit(solution)/shard_map/pallas_call | solution.py:417
  82.5 3.1 %fusion.18 = (bf16[1,2,512,512]{3,2,1,0:T(8,128)(2,1)}, bf16[1,2,512,512]{3,2,1,0:T(8,128)(2,1)}) fusion(bf16[2,2,512,512]{3,2,1,0:T(8,128)(2,1)} %collective-permute-done.refs_0_.refs_1_), kind=kLoop, calls=%fused_computation.40 | loop fusion | bytes 4194304 | tf_op jit(solution)/shard_map/slice | solution.py:586
  85.6 13.0 %collective-permute-done.3.ends.block_re.block_im = bf16[2,2,512,512]{3,2,1,0:T(8,128)(2,1)} collective-permute-done((bf16[2,2,512,512]{3,2,1,0:T(8,128)(2,1)}, bf16[2,2,512,512]{3,2,1,0:T(8,128)(2,1)}, u32[]{:S(2)}, u32[]{:S(2)}) %collective-permute-start.3) | collective-permute-done | bytes 2097184 | tf_op jit(solution)/shard_map/ppermute | solution.py:19
  98.6 0.3 collective-permute-done.5.refs_0_.refs_1_.refs_3_.refs_4_
  98.9 3.1 %shard_map.128 = (bf16[1,2,512,512]{3,2,1,0:T(8,128)(2,1)}, bf16[1,2,512,512]{3,2,1,0:T(8,128)(2,1)}) custom-call(s32[2]{0:T(128)} %pad_add_fusion.ids, bf16[2,2,512,512]{3,2,1,0:T(8,128)(2,1)} %collective-permute-done.3.ends.block_re.block_im, bf16[2,2,512,512]{3,2,1,0:T(8,128)(2,1)} %collective-permute-done.4.middles.refs_2_, bf16[2,2,1024,4096]{3,2,1,0:T(8,128)(2,1)} %cross.19), custom_call_target="tpu_custom_call" | custom-call | flops 1 | bytes 1 | tf_op jit(solution)/shard_map/pallas_call | solution.py:514
  102.1 0.6 collective-permute-start.8
  102.7 4.3 %collective-permute-start.7 = (bf16[1,2,512,512]{3,2,1,0:T(8,128)(2,1)}, bf16[1,2,512,512]{3,2,1,0:T(8,128)(2,1)}, u32[]{:S(2)}, u32[]{:S(2)}) collective-permute-start(bf16[1,2,512,512]{3,2,1,0:T(8,128)(2,1)} %get-tuple-element.65), channel_id=1, source_target_pairs={{0,4},{2,6},{4,0},{6,2},{8,12},{10,14},{12,8},{14,10},{1,5},{3,7},... | collective-permute-start | bytes 3145736 | tf_op jit(solution)/shard_map/ppermute | solution.py:19
  106.9 0.5 collective-permute-start.6
  107.5 9.8 %shard_map.129.total = f32[2,1024,512]{2,1,0:T(8,128)} custom-call(s32[2]{0:T(128)} %get-tuple-element.69.ids, bf16[2,2,1024,4096]{3,2,1,0:T(8,128)(2,1)} %cross.19, bf16[2,2,512,512]{3,2,1,0:T(8,128)(2,1)} %collective-permute-done.5.refs_0_.refs_1_.refs_3_.refs_4_, bf16[1,2,512,512]{3,2,1,0:T(8,128)(2,1)} %get-tuple-element.64.refs_1_, ...), custom_call_target="tpu_custom_call" | custom-call | flops 1 | bytes 1 | tf_op jit(solution)/shard_map/pallas_call | solution.py:137
  117.2 3.1 %shard_map.130 = (bf16[1,2,512,512]{3,2,1,0:T(8,128)(2,1)}, bf16[1,2,512,512]{3,2,1,0:T(8,128)(2,1)}) custom-call(s32[2]{0:T(128)} %pad_add_fusion.ids, bf16[2,2,512,512]{3,2,1,0:T(8,128)(2,1)} %collective-permute-done.3.ends.block_re.block_im, bf16[2,2,512,512]{3,2,1,0:T(8,128)(2,1)} %collective-permute-done.4.middles.refs_2_, bf16[2,2,1024,4096]{3,2,1,0:T(8,128)(2,1)} %cross.19), custom_call_target="tpu_custom_call" | custom-call | flops 1 | bytes 1 | tf_op jit(solution)/shard_map/pallas_call | solution.py:514
  120.3 10.5 %collective-permute-done.7.w6.block_re = bf16[1,2,512,512]{3,2,1,0:T(8,128)(2,1)} collective-permute-done((bf16[1,2,512,512]{3,2,1,0:T(8,128)(2,1)}, bf16[1,2,512,512]{3,2,1,0:T(8,128)(2,1)}, u32[]{:S(2)}, u32[]{:S(2)}) %collective-permute-start.7) | collective-permute-done | bytes 1048608 | tf_op jit(solution)/shard_map/ppermute | solution.py:19
  130.8 1.5 collective-permute-done.6.w5.refs_3_
  132.3 0.5 collective-permute-start.14
  132.8 0.5 collective-permute-start.10
  133.3 0.3 collective-permute-start.11
  133.6 9.6 %shard_map.132.total = f32[2,1024,512]{2,1,0:T(8,128)} custom-call(s32[2]{0:T(128)} %get-tuple-element.69.ids, bf16[2,2,1024,4096]{3,2,1,0:T(8,128)(2,1)} %cross.19, bf16[2,2,512,512]{3,2,1,0:T(8,128)(2,1)} %collective-permute-done.5.refs_0_.refs_1_.refs_3_.refs_4_, bf16[1,2,512,512]{3,2,1,0:T(8,128)(2,1)} %get-tuple-element.76.refs_1_, ...), custom_call_target="tpu_custom_call" | custom-call | flops 1 | bytes 1 | tf_op jit(solution)/shard_map/pallas_call | solution.py:137
  143.2 9.8 %shard_map.131 = (f32[8,512]{1,0:T(8,128)S(1)}, f32[2,512,512]{2,1,0:T(8,128)S(1)}) custom-call(s32[8]{0:T(128)S(1)} %concatenate.11.ids, bf16[2,2,1024,4096]{3,2,1,0:T(8,128)(2,1)} %cross.19, bf16[1,2,512,512]{3,2,1,0:T(8,128)(2,1)} %collective-permute-done.6.w5.refs_3_, bf16[1,2,512,512]{3,2,1,0:T(8,128)(2,1)} %collective-permute-done.7.w6.block_re, ...), custom_call_target="tpu_custom_call" | custom-call | flops 1 | bytes 1 | tf_op jit(solution)/shard_map/pallas_call | solution.py:307
  153.0 5.1 %collective-permute-done.10.w5.refs_9_ = bf16[1,2,512,512]{3,2,1,0:T(8,128)(2,1)} collective-permute-done((bf16[1,2,512,512]{3,2,1,0:T(8,128)(2,1)}, bf16[1,2,512,512]{3,2,1,0:T(8,128)(2,1)}, u32[]{:S(2)}, u32[]{:S(2)}) %collective-permute-start.10) | collective-permute-done | bytes 1048608 | tf_op jit(solution)/shard_map/ppermute | solution.py:19
  158.1 0.3 collective-permute-done.11.w6.block_im
  158.4 0.5 collective-permute-start.16
  158.9 0.5 collective-permute-start.17
  159.4 10.0 %shard_map.133 = (f32[8,512]{1,0:T(8,128)S(1)}, f32[2,512,512]{2,1,0:T(8,128)S(1)}) custom-call(s32[8]{0:T(128)S(1)} %concatenate.11.ids, bf16[2,2,1024,4096]{3,2,1,0:T(8,128)(2,1)} %cross.19, bf16[1,2,512,512]{3,2,1,0:T(8,128)(2,1)} %collective-permute-done.10.w5.refs_9_, bf16[1,2,512,512]{3,2,1,0:T(8,128)(2,1)} %collective-permute-done.11.w6.block_im, ...), custom_call_target="tpu_custom_call" | custom-call | flops 1 | bytes 1 | tf_op jit(solution)/shard_map/pallas_call | solution.py:307
  169.5 0.8 shard_map.134
  170.3 8.1 %all-to-all-start = ((f32[16,4,512]{2,1,0:T(4,128)}), f32[16,4,512]{2,1,0:T(4,128)S(1)}, u32[]{:S(2)}, u32[]{:S(2)}) async-start(f32[16,4,512]{2,1,0:T(4,128)} %shard_map.134), calls=%async_computation | async-start | bytes 262144 | tf_op jit(solution)/shard_map/all_to_all | solution.py:42
  178.4 7.9 %all-to-all-done = f32[16,4,512]{2,1,0:T(4,128)S(1)} async-done(((f32[16,4,512]{2,1,0:T(4,128)}), f32[16,4,512]{2,1,0:T(4,128)S(1)}, u32[]{:S(2)}, u32[]{:S(2)}) %all-to-all-start) | async-done | bytes 131104 | tf_op jit(solution)/shard_map/all_to_all | solution.py:42
  186.3 0.1 abs_reduce_fusion
  186.5 0.1 reshape.41
  186.5 0.6 constant_dynamic-slice_fusion
  187.1 0.8 fusion
  (25 shorter events, 0.1 us)
Async XLA Ops:
  0.6 21.9 %collective-permute-start.2 = (bf16[2,2,512,512]{3,2,1,0:T(8,128)(2,1)}, bf16[2,2,512,512]{3,2,1,0:T(8,128)(2,1)}, u32[]{:S(2)}, u32[]{:S(2)}) collective-permute-start(bf16[2,2,512,512]{3,2,1,0:T(8,128)(2,1)} %bitcast.17), channel_id=1, source_target_pairs={{0,1},{1,0},{2,3},{3,2},{4,8},{5,9},{6,10},{7,11},{8,4},{9,5},{10,... | collective-permute-start | bytes 6291464 | tf_op jit(solution)/shard_map/ppermute | solution.py:26
  1.1 49.8 %collective-permute-start.1 = (bf16[2,2,512,512]{3,2,1,0:T(8,128)(2,1)}, bf16[2,2,512,512]{3,2,1,0:T(8,128)(2,1)}, u32[]{:S(2)}, u32[]{:S(2)}) collective-permute-start(bf16[2,2,512,512]{3,2,1,0:T(8,128)(2,1)} %bitcast.18), channel_id=1, source_target_pairs={{0,4},{2,6},{4,0},{6,2},{8,12},{10,14},{12,8},{14,10},{1,5},{3,7},... | collective-permute-start | bytes 6291464 | tf_op jit(solution)/shard_map/ppermute | solution.py:19
  5.3 47.1 %collective-permute-start = (bf16[2,2,512,512]{3,2,1,0:T(8,128)(2,1)}, bf16[2,2,512,512]{3,2,1,0:T(8,128)(2,1)}, u32[]{:S(2)}, u32[]{:S(2)}) collective-permute-start(bf16[2,2,512,512]{3,2,1,0:T(8,128)(2,1)} %bitcast.19), channel_id=1, source_target_pairs={{0,2},{2,0},{4,6},{6,4},{8,10},{10,8},{12,14},{14,12},{1,3},{3,1},... | collective-permute-start | bytes 6291464 | tf_op jit(solution)/shard_map/ppermute | solution.py:19
  12.6 6.1 %copy-start = (s32[2]{0:T(128)S(1)}, s32[2]{0:T(128)}, u32[]{:S(2)}) copy-start(s32[2]{0:T(128)} %constant.117.clone) | copy-start | bytes 28
  12.6 7.3 %copy-start.2 = (s32[3]{0:T(128)S(1)}, s32[3]{0:T(128)}, u32[]{:S(2)}) copy-start(s32[3]{0:T(128)} %constant.116.clone) | copy-start | bytes 40
  52.4 46.2 %collective-permute-start.3 = (bf16[2,2,512,512]{3,2,1,0:T(8,128)(2,1)}, bf16[2,2,512,512]{3,2,1,0:T(8,128)(2,1)}, u32[]{:S(2)}, u32[]{:S(2)}) collective-permute-start(bf16[2,2,512,512]{3,2,1,0:T(8,128)(2,1)} %shard_map.122.refs_2_.refs_3_), channel_id=1, source_target_pairs={{0,4},{2,6},{4,0},{6,2},{8,12},{10,14},{12,8},{14,10},{1,5},{3,7},... | collective-permute-start | bytes 6291464 | tf_op jit(solution)/shard_map/ppermute | solution.py:19
  52.7 46.2 %collective-permute-start.5 = (bf16[2,2,512,512]{3,2,1,0:T(8,128)(2,1)}, bf16[2,2,512,512]{3,2,1,0:T(8,128)(2,1)}, u32[]{:S(2)}, u32[]{:S(2)}) collective-permute-start(bf16[2,2,512,512]{3,2,1,0:T(8,128)(2,1)} %collective-permute-done.1.refs_1_.refs_2_), channel_id=1, source_target_pairs={{0,2},{2,0},{4,6},{6,4},{8,10},{10,8},{12,14},{14,12},{1,3},{3,1},... | collective-permute-start | bytes 6291464 | tf_op jit(solution)/shard_map/ppermute | solution.py:19
  54.2 44.7 %collective-permute-start.4 = (bf16[2,2,512,512]{3,2,1,0:T(8,128)(2,1)}, bf16[2,2,512,512]{3,2,1,0:T(8,128)(2,1)}, u32[]{:S(2)}, u32[]{:S(2)}) collective-permute-start(bf16[2,2,512,512]{3,2,1,0:T(8,128)(2,1)} %collective-permute-done.1.refs_1_.refs_2_), channel_id=1, source_target_pairs={{0,1},{1,0},{2,3},{3,2},{4,8},{5,9},{6,10},{7,11},{8,4},{9,5},{10,... | collective-permute-start | bytes 6291464 | tf_op jit(solution)/shard_map/ppermute | solution.py:26
  98.9 33.3 %collective-permute-start.9 = (bf16[2,2,1024,512]{3,2,1,0:T(8,128)(2,1)}, bf16[2,2,1024,512]{3,2,1,0:T(8,128)(2,1)}, u32[]{:S(2)}, u32[]{:S(2)}) collective-permute-start(bf16[2,2,1024,512]{3,2,1,0:T(8,128)(2,1)} %shard_map.127.refs_0_), channel_id=1, source_target_pairs={{0,1},{1,0},{2,3},{3,2},{4,5},{5,4},{6,7},{7,6},{8,9},{9,8},{10,11... | collective-permute-start | bytes 12582920 | tf_op jit(solution)/shard_map/ppermute | solution.py:19
  102.1 18.2 %collective-permute-start.8 = (bf16[1,2,512,512]{3,2,1,0:T(8,128)(2,1)}, bf16[1,2,512,512]{3,2,1,0:T(8,128)(2,1)}, u32[]{:S(2)}, u32[]{:S(2)}) collective-permute-start(bf16[1,2,512,512]{3,2,1,0:T(8,128)(2,1)} %get-tuple-element.67), channel_id=1, source_target_pairs={{0,1},{1,0},{2,3},{3,2},{4,8},{5,9},{6,10},{7,11},{8,4},{9,5},{10,... | collective-permute-start | bytes 3145736 | tf_op jit(solution)/shard_map/ppermute | solution.py:26
  102.7 28.1 %collective-permute-start.7 = (bf16[1,2,512,512]{3,2,1,0:T(8,128)(2,1)}, bf16[1,2,512,512]{3,2,1,0:T(8,128)(2,1)}, u32[]{:S(2)}, u32[]{:S(2)}) collective-permute-start(bf16[1,2,512,512]{3,2,1,0:T(8,128)(2,1)} %get-tuple-element.65), channel_id=1, source_target_pairs={{0,4},{2,6},{4,0},{6,2},{8,12},{10,14},{12,8},{14,10},{1,5},{3,7},... | collective-permute-start | bytes 3145736 | tf_op jit(solution)/shard_map/ppermute | solution.py:19
  106.9 25.3 %collective-permute-start.6 = (bf16[1,2,512,512]{3,2,1,0:T(8,128)(2,1)}, bf16[1,2,512,512]{3,2,1,0:T(8,128)(2,1)}, u32[]{:S(2)}, u32[]{:S(2)}) collective-permute-start(bf16[1,2,512,512]{3,2,1,0:T(8,128)(2,1)} %get-tuple-element.64.refs_1_), channel_id=1, source_target_pairs={{0,2},{2,0},{4,6},{6,4},{8,10},{10,8},{12,14},{14,12},{1,3},{3,1},... | collective-permute-start | bytes 3145736 | tf_op jit(solution)/shard_map/ppermute | solution.py:19
  132.2 10.9 %collective-permute-start.13 = (bf16[2,2,512,512]{3,2,1,0:T(8,128)(2,1)}, bf16[2,2,512,512]{3,2,1,0:T(8,128)(2,1)}, u32[]{:S(2)}, u32[]{:S(2)}) collective-permute-start(bf16[2,2,512,512]{3,2,1,0:T(8,128)(2,1)} %collective-permute-done.5.refs_0_.refs_1_.refs_3_.refs_4_), channel_id=1, source_target_pairs={{0,1},{1,0},{2,3},{3,2},{4,5},{5,4},{6,7},{7,6},{8,9},{9,8},{10,11... | collective-permute-start | bytes 6291464 | tf_op jit(solution)/shard_map/ppermute | solution.py:19
  132.3 11.0 %collective-permute-start.14 = (bf16[2,2,512,512]{3,2,1,0:T(8,128)(2,1)}, bf16[2,2,512,512]{3,2,1,0:T(8,128)(2,1)}, u32[]{:S(2)}, u32[]{:S(2)}) collective-permute-start(bf16[2,2,512,512]{3,2,1,0:T(8,128)(2,1)} %collective-permute-done.4.middles.refs_2_), channel_id=1, source_target_pairs={{0,1},{1,0},{2,3},{3,2},{4,5},{5,4},{6,7},{7,6},{8,9},{9,8},{10,11... | collective-permute-start | bytes 6291464 | tf_op jit(solution)/shard_map/ppermute | solution.py:19
  132.8 25.4 %collective-permute-start.10 = (bf16[1,2,512,512]{3,2,1,0:T(8,128)(2,1)}, bf16[1,2,512,512]{3,2,1,0:T(8,128)(2,1)}, u32[]{:S(2)}, u32[]{:S(2)}) collective-permute-start(bf16[1,2,512,512]{3,2,1,0:T(8,128)(2,1)} %get-tuple-element.76.refs_1_), channel_id=1, source_target_pairs={{0,2},{2,0},{4,6},{6,4},{8,10},{10,8},{12,14},{14,12},{1,3},{3,1},... | collective-permute-start | bytes 3145736 | tf_op jit(solution)/shard_map/ppermute | solution.py:19
  133.3 25.1 %collective-permute-start.11 = (bf16[1,2,512,512]{3,2,1,0:T(8,128)(2,1)}, bf16[1,2,512,512]{3,2,1,0:T(8,128)(2,1)}, u32[]{:S(2)}, u32[]{:S(2)}) collective-permute-start(bf16[1,2,512,512]{3,2,1,0:T(8,128)(2,1)} %get-tuple-element.77), channel_id=1, source_target_pairs={{0,4},{2,6},{4,0},{6,2},{8,12},{10,14},{12,8},{14,10},{1,5},{3,7},... | collective-permute-start | bytes 3145736 | tf_op jit(solution)/shard_map/ppermute | solution.py:19
  133.6 24.8 %collective-permute-start.12 = (bf16[1,2,512,512]{3,2,1,0:T(8,128)(2,1)}, bf16[1,2,512,512]{3,2,1,0:T(8,128)(2,1)}, u32[]{:S(2)}, u32[]{:S(2)}) collective-permute-start(bf16[1,2,512,512]{3,2,1,0:T(8,128)(2,1)} %get-tuple-element.78), channel_id=1, source_target_pairs={{0,1},{1,0},{2,3},{3,2},{4,8},{5,9},{6,10},{7,11},{8,4},{9,5},{10,... | collective-permute-start | bytes 3145736 | tf_op jit(solution)/shard_map/ppermute | solution.py:26
  158.4 11.0 %collective-permute-start.15 = (bf16[1,2,512,512]{3,2,1,0:T(8,128)(2,1)}, bf16[1,2,512,512]{3,2,1,0:T(8,128)(2,1)S(1)}, u32[]{:S(2)}, u32[]{:S(2)}) collective-permute-start(bf16[1,2,512,512]{3,2,1,0:T(8,128)(2,1)} %collective-permute-done.8.w7.refs_2_), channel_id=1, source_target_pairs={{0,1},{1,0},{2,3},{3,2},{4,5},{5,4},{6,7},{7,6},{8,9},{9,8},{10,11... | collective-permute-start | bytes 3145736 | tf_op jit(solution)/shard_map/ppermute | solution.py:19
  158.4 11.0 %collective-permute-start.16 = (bf16[1,2,512,512]{3,2,1,0:T(8,128)(2,1)}, bf16[1,2,512,512]{3,2,1,0:T(8,128)(2,1)S(1)}, u32[]{:S(2)}, u32[]{:S(2)}) collective-permute-start(bf16[1,2,512,512]{3,2,1,0:T(8,128)(2,1)} %collective-permute-done.6.w5.refs_3_), channel_id=1, source_target_pairs={{0,1},{1,0},{2,3},{3,2},{4,5},{5,4},{6,7},{7,6},{8,9},{9,8},{10,11... | collective-permute-start | bytes 3145736 | tf_op jit(solution)/shard_map/ppermute | solution.py:19
  158.9 10.6 %collective-permute-start.18 = (bf16[1,2,512,512]{3,2,1,0:T(8,128)(2,1)}, bf16[1,2,512,512]{3,2,1,0:T(8,128)(2,1)S(1)}, u32[]{:S(2)}, u32[]{:S(2)}) collective-permute-start(bf16[1,2,512,512]{3,2,1,0:T(8,128)(2,1)} %collective-permute-done.10.w5.refs_9_), channel_id=1, source_target_pairs={{0,1},{1,0},{2,3},{3,2},{4,5},{5,4},{6,7},{7,6},{8,9},{9,8},{10,11... | collective-permute-start | bytes 3145736 | tf_op jit(solution)/shard_map/ppermute | solution.py:19
  158.9 10.6 %collective-permute-start.17 = (bf16[1,2,512,512]{3,2,1,0:T(8,128)(2,1)}, bf16[1,2,512,512]{3,2,1,0:T(8,128)(2,1)S(1)}, u32[]{:S(2)}, u32[]{:S(2)}) collective-permute-start(bf16[1,2,512,512]{3,2,1,0:T(8,128)(2,1)} %collective-permute-done.12.w7.refs_8_), channel_id=1, source_target_pairs={{0,1},{1,0},{2,3},{3,2},{4,5},{5,4},{6,7},{7,6},{8,9},{9,8},{10,11... | collective-permute-start | bytes 3145736 | tf_op jit(solution)/shard_map/ppermute | solution.py:19
  169.5 17.6 %copy-start.1 = (s32[16]{0:T(128)S(1)}, s32[16]{0:T(128)}, u32[]{:S(2)}) copy-start(s32[16]{0:T(128)} %param.13) | copy-start | bytes 196
  170.3 16.0 %all-to-all-start = ((f32[16,4,512]{2,1,0:T(4,128)}), f32[16,4,512]{2,1,0:T(4,128)S(1)}, u32[]{:S(2)}, u32[]{:S(2)}) async-start(f32[16,4,512]{2,1,0:T(4,128)} %shard_map.134), calls=%async_computation | async-start | bytes 262144 | tf_op jit(solution)/shard_map/all_to_all | solution.py:42

commit v17 on v16

--- a/solution.py
+++ b/solution.py
@@ -9,7 +9,7 @@
 from jax.sharding import PartitionSpec as P
 
 VMEM_LIMIT = 63 * 1024 * 1024
-LATE_LIMIT = 40 * 1024 * 1024
+LATE_LIMIT = 30 * 1024 * 1024
 HINT = pl.CostEstimate(flops=1, bytes_accessed=1, transcendentals=0)
 ANYWHERE = pl.BlockSpec(memory_space=pl.ANY)
 

time: 188 us -> 188 us (level)
  waiting for transfers between devices: 65.4 us -> 63.2 us
  local copies, waits for them, and re-layouts: 3.85 us -> 6.02 us
    unnamed x6 -> x10, local copies, waits for them, and re-layouts: 0.02 us -> 2.2 us
    ppermute x15, waiting for transfers between devices: 57.4 us -> 55.3 us  [swap(): lax.ppermute(value, axis, [(source, source ^ mask) for source in range(si...]
where the time goes in v17:
time: 188 us; the launch traced here: 187 us
  Pallas kernels  88.3 us (47%)
  waiting for transfers between devices  63.2 us (34%)
  starting transfers between devices  23.7 us (13%)
  local copies, waits for them, and re-layouts  6.02 us (3%)
  other arithmetic  3.91 us (2%)
    pallas_call x6, Pallas kernels, add_field(): pl.pallas_call(functools.partial(field_kernel, freq, count, has_total, ga...  55.7 us
    ppermute x15, waiting for transfers between devices, swap(): lax.ppermute(value, axis, [(source, source ^ mask) for source in range(si...  55.3 us
    pallas_call x2, Pallas kernels, add_late(): pl.pallas_call(functools.partial(late_kernel, freq), out_shape=(jax.Shape...  18.9 us
    ppermute x15, starting transfers between devices, swap(): lax.ppermute(value, axis, [(source, source ^ mask) for source in range(si...  14.6 us
    all_to_all x1, starting transfers between devices, sum_all(): return jnp.sum(lax.all_to_all(copies, axes, 0, 0, tiled=True), axis=0)  8.08 us
    all_to_all x1, waiting for transfers between devices, sum_all(): return jnp.sum(lax.all_to_all(copies, axes, 0, 0, tiled=True), axis=0)  7.93 us
    pallas_call x2, Pallas kernels, copies(): pl.pallas_call(functools.partial(copy_kernel, len(args), jobs), out_shape...  6.7 us
    pallas_call x2, Pallas kernels, take_next(): pl.pallas_call(functools.partial(next_kernel, freq), out_shape=[shape, sh...  6.22 us
  transfers between devices with their start and end apart: 20, of which 9 were waited for; matrix products, arithmetic and copies ran while one was open for 4% of the time, Pallas kernels for 47%

profile of v17, /device:TPU:0, one launch (start us, length us, event | category | flops | bytes accessed | tf_op | source)
XLA Modules:
  0.0 187.1 jit_solution(14494438140039862082)
XLA Ops:
  0.6 0.5 collective-permute-start.2
  1.1 4.1 %collective-permute-start.1 = (bf16[2,2,512,512]{3,2,1,0:T(8,128)(2,1)}, bf16[2,2,512,512]{3,2,1,0:T(8,128)(2,1)}, u32[]{:S(2)}, u32[]{:S(2)}) collective-permute-start(bf16[2,2,512,512]{3,2,1,0:T(8,128)(2,1)} %bitcast.18), channel_id=1, source_target_pairs={{0,4},{2,6},{4,0},{6,2},{8,12},{10,14},{12,8},{14,10},{1,5},{3,7},... | collective-permute-start | bytes 6291464 | tf_op jit(solution)/shard_map/ppermute | solution.py:19
  5.3 1.5 collective-permute-start
  6.8 5.8 %shard_map.124.refs_3_ = f32[2,1024,512]{2,1,0:T(8,128)} custom-call(s32[1]{0:T(128)} %bitcast.2.ids, bf16[2,2,1024,4096]{3,2,1,0:T(8,128)(2,1)} %cross.19, bf16[2,2,512,512]{3,2,1,0:T(8,128)(2,1)} %bitcast.20), custom_call_target="tpu_custom_call" | custom-call | flops 1 | bytes 1 | tf_op jit(solution)/shard_map/pallas_call | solution.py:137
  12.6 0.0 copy-start.4
  12.6 5.9 %shard_map.123.refs_3_ = f32[2,1024,512]{2,1,0:T(8,128)} custom-call(s32[1]{0:T(128)} %bitcast.2.ids, bf16[2,2,1024,4096]{3,2,1,0:T(8,128)(2,1)} %cross.19, bf16[2,2,512,512]{3,2,1,0:T(8,128)(2,1)} %bitcast.21), custom_call_target="tpu_custom_call" | custom-call | flops 1 | bytes 1 | tf_op jit(solution)/shard_map/pallas_call | solution.py:137
  18.7 0.5 fusion.16
  19.2 0.1 concatenate.11.ids
  19.3 0.6 pad_add_fusion.ids
  19.9 0.6 pad_add_fusion.1.ids
  20.5 2.0 %multiply_reduce_fusion.norms = f32[2,512]{1,0:T(2,128)S(1)} fusion(bf16[2,2,1,512,512]{4,3,2,1,0:T(8,128)(2,1)} %param.12), kind=kLoop, calls=%fused_computation | loop fusion | flops 3144704 | bytes 2101248 | tf_op jit(solution)/shard_map/reduce_sum | solution.py:642
  22.5 3.1 %shard_map.122.refs_2_.refs_3_ = bf16[2,2,512,512]{3,2,1,0:T(8,128)(2,1)} custom-call(s32[2]{0:T(128)} %pad_add_fusion.ids, bf16[2,2,512,512]{3,2,1,0:T(8,128)(2,1)} %collective-permute-done.2.refs_0_, bf16[2,2,1024,4096]{3,2,1,0:T(8,128)(2,1)} %cross.19), custom_call_target="tpu_custom_call", output_to_operand_aliasing={{}: (1, {})} | custom-call | flops 1 | bytes 1 | tf_op jit(solution)/shard_map/pallas_call | solution.py:417
  25.7 25.3 %collective-permute-done.1.refs_1_.refs_2_ = bf16[2,2,512,512]{3,2,1,0:T(8,128)(2,1)} collective-permute-done((bf16[2,2,512,512]{3,2,1,0:T(8,128)(2,1)}, bf16[2,2,512,512]{3,2,1,0:T(8,128)(2,1)}, u32[]{:S(2)}, u32[]{:S(2)}) %collective-permute-start.1) | collective-permute-done | bytes 2097184 | tf_op jit(solution)/shard_map/ppermute | solution.py:19
  51.0 1.4 collective-permute-done.refs_0_.refs_1_
  52.4 0.3 collective-permute-start.3
  52.7 1.5 collective-permute-start.5
  54.2 12.3 %shard_map.125.refs_2_ = f32[2,1024,512]{2,1,0:T(8,128)} custom-call(s32[4]{0:T(128)} %pad_add_fusion.1.ids, bf16[2,2,1024,4096]{3,2,1,0:T(8,128)(2,1)} %cross.19, bf16[2,2,512,512]{3,2,1,0:T(8,128)(2,1)} %collective-permute-done.refs_0_.refs_1_, bf16[2,2,512,512]{3,2,1,0:T(8,128)(2,1)} %collective-permute-done.1.refs_1_.refs_2_, ...), custom_call_target="tpu_custom_call" | custom-call | flops 1 | bytes 1 | tf_op jit(solution)/shard_map/pallas_call | solution.py:137
  66.5 12.4 %shard_map.126.refs_2_ = f32[2,1024,512]{2,1,0:T(8,128)} custom-call(s32[4]{0:T(128)} %pad_add_fusion.1.ids, bf16[2,2,1024,4096]{3,2,1,0:T(8,128)(2,1)} %cross.19, bf16[2,2,512,512]{3,2,1,0:T(8,128)(2,1)} %collective-permute-done.refs_0_.refs_1_, bf16[2,2,512,512]{3,2,1,0:T(8,128)(2,1)} %collective-permute-done.1.refs_1_.refs_2_, ...), custom_call_target="tpu_custom_call" | custom-call | flops 1 | bytes 1 | tf_op jit(solution)/shard_map/pallas_call | solution.py:137
  78.9 3.6 %shard_map.127.refs_0_ = bf16[2,2,1024,512]{3,2,1,0:T(8,128)(2,1)} custom-call(s32[1]{0:T(128)} %bitcast.6.ids, bf16[2,2,512,512]{3,2,1,0:T(8,128)(2,1)} %bitcast.22, bf16[2,2,512,512]{3,2,1,0:T(8,128)(2,1)} %collective-permute-done.refs_0_.refs_1_, bf16[2,2,512,512]{3,2,1,0:T(8,128)(2,1)} %collective-permute-done.1.refs_1_.refs_2_, ...), custom_call_target="tpu_custom_call" | custom-call | flops 1 | bytes 1 | tf_op jit(solution)/shard_map/pallas_call | solution.py:417
  82.5 3.1 %fusion.18 = (bf16[1,2,512,512]{3,2,1,0:T(8,128)(2,1)}, bf16[1,2,512,512]{3,2,1,0:T(8,128)(2,1)}) fusion(bf16[2,2,512,512]{3,2,1,0:T(8,128)(2,1)} %collective-permute-done.refs_0_.refs_1_), kind=kLoop, calls=%fused_computation.40 | loop fusion | bytes 4194304 | tf_op jit(solution)/shard_map/slice | solution.py:586
  85.6 13.0 %collective-permute-done.3.ends.block_re.block_im = bf16[2,2,512,512]{3,2,1,0:T(8,128)(2,1)} collective-permute-done((bf16[2,2,512,512]{3,2,1,0:T(8,128)(2,1)}, bf16[2,2,512,512]{3,2,1,0:T(8,128)(2,1)}, u32[]{:S(2)}, u32[]{:S(2)}) %collective-permute-start.3) | collective-permute-done | bytes 2097184 | tf_op jit(solution)/shard_map/ppermute | solution.py:19
  98.6 0.3 collective-permute-done.5.refs_0_.refs_1_.refs_3_.refs_4_
  98.9 3.1 %shard_map.128 = (bf16[1,2,512,512]{3,2,1,0:T(8,128)(2,1)}, bf16[1,2,512,512]{3,2,1,0:T(8,128)(2,1)}) custom-call(s32[2]{0:T(128)} %pad_add_fusion.ids, bf16[2,2,512,512]{3,2,1,0:T(8,128)(2,1)} %collective-permute-done.3.ends.block_re.block_im, bf16[2,2,512,512]{3,2,1,0:T(8,128)(2,1)} %collective-permute-done.4.middles.refs_2_, bf16[2,2,1024,4096]{3,2,1,0:T(8,128)(2,1)} %cross.19), custom_call_target="tpu_custom_call" | custom-call | flops 1 | bytes 1 | tf_op jit(solution)/shard_map/pallas_call | solution.py:514
  102.1 0.6 collective-permute-start.8
  102.6 4.3 %collective-permute-start.7 = (bf16[1,2,512,512]{3,2,1,0:T(8,128)(2,1)}, bf16[1,2,512,512]{3,2,1,0:T(8,128)(2,1)}, u32[]{:S(2)}, u32[]{:S(2)}) collective-permute-start(bf16[1,2,512,512]{3,2,1,0:T(8,128)(2,1)} %get-tuple-element.65), channel_id=1, source_target_pairs={{0,4},{2,6},{4,0},{6,2},{8,12},{10,14},{12,8},{14,10},{1,5},{3,7},... | collective-permute-start | bytes 3145736 | tf_op jit(solution)/shard_map/ppermute | solution.py:19
  106.9 0.5 collective-permute-start.6
  107.5 9.8 %shard_map.129.total = f32[2,1024,512]{2,1,0:T(8,128)} custom-call(s32[2]{0:T(128)} %get-tuple-element.69.ids, bf16[2,2,1024,4096]{3,2,1,0:T(8,128)(2,1)} %cross.19, bf16[2,2,512,512]{3,2,1,0:T(8,128)(2,1)} %collective-permute-done.5.refs_0_.refs_1_.refs_3_.refs_4_, bf16[1,2,512,512]{3,2,1,0:T(8,128)(2,1)} %get-tuple-element.64.refs_1_, ...), custom_call_target="tpu_custom_call" | custom-call | flops 1 | bytes 1 | tf_op jit(solution)/shard_map/pallas_call | solution.py:137
  117.2 3.1 %shard_map.130 = (bf16[1,2,512,512]{3,2,1,0:T(8,128)(2,1)}, bf16[1,2,512,512]{3,2,1,0:T(8,128)(2,1)}) custom-call(s32[2]{0:T(128)} %pad_add_fusion.ids, bf16[2,2,512,512]{3,2,1,0:T(8,128)(2,1)} %collective-permute-done.3.ends.block_re.block_im, bf16[2,2,512,512]{3,2,1,0:T(8,128)(2,1)} %collective-permute-done.4.middles.refs_2_, bf16[2,2,1024,4096]{3,2,1,0:T(8,128)(2,1)} %cross.19), custom_call_target="tpu_custom_call" | custom-call | flops 1 | bytes 1 | tf_op jit(solution)/shard_map/pallas_call | solution.py:514
  120.3 10.5 %collective-permute-done.7.w6.block_re = bf16[1,2,512,512]{3,2,1,0:T(8,128)(2,1)} collective-permute-done((bf16[1,2,512,512]{3,2,1,0:T(8,128)(2,1)}, bf16[1,2,512,512]{3,2,1,0:T(8,128)(2,1)}, u32[]{:S(2)}, u32[]{:S(2)}) %collective-permute-start.7) | collective-permute-done | bytes 1048608 | tf_op jit(solution)/shard_map/ppermute | solution.py:19
  130.8 1.5 collective-permute-done.6.w5.refs_3_
  132.2 0.5 collective-permute-start.14
  132.8 0.5 collective-permute-start.10
  133.3 0.3 collective-permute-start.11
  133.6 9.6 %shard_map.132.total = f32[2,1024,512]{2,1,0:T(8,128)} custom-call(s32[2]{0:T(128)} %get-tuple-element.69.ids, bf16[2,2,1024,4096]{3,2,1,0:T(8,128)(2,1)} %cross.19, bf16[2,2,512,512]{3,2,1,0:T(8,128)(2,1)} %collective-permute-done.5.refs_0_.refs_1_.refs_3_.refs_4_, bf16[1,2,512,512]{3,2,1,0:T(8,128)(2,1)} %get-tuple-element.76.refs_1_, ...), custom_call_target="tpu_custom_call" | custom-call | flops 1 | bytes 1 | tf_op jit(solution)/shard_map/pallas_call | solution.py:137
  143.2 2.2 %copy-done.1 = f32[2,1024,512]{2,1,0:T(8,128)S(1)} copy-done((f32[2,1024,512]{2,1,0:T(8,128)S(1)}, f32[2,1024,512]{2,1,0:T(8,128)}, u32[]{:S(2)}) %copy-start.1) | copy-done | bytes 4194328
  145.4 9.8 %shard_map.131 = (f32[8,512]{1,0:T(8,128)S(1)}, f32[2,512,512]{2,1,0:T(8,128)S(1)}) custom-call(s32[8]{0:T(128)S(1)} %concatenate.11.ids, bf16[2,2,1024,4096]{3,2,1,0:T(8,128)(2,1)} %cross.19, bf16[1,2,512,512]{3,2,1,0:T(8,128)(2,1)} %collective-permute-done.6.w5.refs_3_, bf16[1,2,512,512]{3,2,1,0:T(8,128)(2,1)} %collective-permute-done.7.w6.block_re, ...), custom_call_target="tpu_custom_call" | custom-call | flops 1 | bytes 1 | tf_op jit(solution)/shard_map/pallas_call | solution.py:307
  155.2 3.0 %collective-permute-done.10.w5.refs_9_ = bf16[1,2,512,512]{3,2,1,0:T(8,128)(2,1)} collective-permute-done((bf16[1,2,512,512]{3,2,1,0:T(8,128)(2,1)}, bf16[1,2,512,512]{3,2,1,0:T(8,128)(2,1)}, u32[]{:S(2)}, u32[]{:S(2)}) %collective-permute-start.10) | collective-permute-done | bytes 1048608 | tf_op jit(solution)/shard_map/ppermute | solution.py:19
  158.1 0.3 collective-permute-done.11.w6.block_im
  158.4 0.5 collective-permute-start.16
  158.9 0.5 collective-permute-start.17
  159.4 9.2 %shard_map.133 = (f32[8,512]{1,0:T(8,128)S(1)}, f32[2,512,512]{2,1,0:T(8,128)S(1)}) custom-call(s32[8]{0:T(128)S(1)} %concatenate.11.ids, bf16[2,2,1024,4096]{3,2,1,0:T(8,128)(2,1)} %cross.19, bf16[1,2,512,512]{3,2,1,0:T(8,128)(2,1)} %collective-permute-done.10.w5.refs_9_, bf16[1,2,512,512]{3,2,1,0:T(8,128)(2,1)} %collective-permute-done.11.w6.block_im, ...), custom_call_target="tpu_custom_call" | custom-call | flops 1 | bytes 1 | tf_op jit(solution)/shard_map/pallas_call | solution.py:307
  168.6 0.8 shard_map.134
  169.4 8.1 %all-to-all-start = ((f32[16,4,512]{2,1,0:T(4,128)}), f32[16,4,512]{2,1,0:T(4,128)S(1)}, u32[]{:S(2)}, u32[]{:S(2)}) async-start(f32[16,4,512]{2,1,0:T(4,128)} %shard_map.134), calls=%async_computation | async-start | bytes 262144 | tf_op jit(solution)/shard_map/all_to_all | solution.py:42
  177.5 7.9 %all-to-all-done = f32[16,4,512]{2,1,0:T(4,128)S(1)} async-done(((f32[16,4,512]{2,1,0:T(4,128)}), f32[16,4,512]{2,1,0:T(4,128)S(1)}, u32[]{:S(2)}, u32[]{:S(2)}) %all-to-all-start) | async-done | bytes 131104 | tf_op jit(solution)/shard_map/all_to_all | solution.py:42
  185.5 0.1 abs_reduce_fusion
  185.6 0.1 reshape.41
  185.7 0.6 constant_dynamic-slice_fusion
  186.3 0.8 fusion
  (29 shorter events, 0.1 us)
Async XLA Ops:
  0.6 21.9 %collective-permute-start.2 = (bf16[2,2,512,512]{3,2,1,0:T(8,128)(2,1)}, bf16[2,2,512,512]{3,2,1,0:T(8,128)(2,1)}, u32[]{:S(2)}, u32[]{:S(2)}) collective-permute-start(bf16[2,2,512,512]{3,2,1,0:T(8,128)(2,1)} %bitcast.17), channel_id=1, source_target_pairs={{0,1},{1,0},{2,3},{3,2},{4,8},{5,9},{6,10},{7,11},{8,4},{9,5},{10,... | collective-permute-start | bytes 6291464 | tf_op jit(solution)/shard_map/ppermute | solution.py:26
  1.1 49.8 %collective-permute-start.1 = (bf16[2,2,512,512]{3,2,1,0:T(8,128)(2,1)}, bf16[2,2,512,512]{3,2,1,0:T(8,128)(2,1)}, u32[]{:S(2)}, u32[]{:S(2)}) collective-permute-start(bf16[2,2,512,512]{3,2,1,0:T(8,128)(2,1)} %bitcast.18), channel_id=1, source_target_pairs={{0,4},{2,6},{4,0},{6,2},{8,12},{10,14},{12,8},{14,10},{1,5},{3,7},... | collective-permute-start | bytes 6291464 | tf_op jit(solution)/shard_map/ppermute | solution.py:19
  5.3 47.1 %collective-permute-start = (bf16[2,2,512,512]{3,2,1,0:T(8,128)(2,1)}, bf16[2,2,512,512]{3,2,1,0:T(8,128)(2,1)}, u32[]{:S(2)}, u32[]{:S(2)}) collective-permute-start(bf16[2,2,512,512]{3,2,1,0:T(8,128)(2,1)} %bitcast.19), channel_id=1, source_target_pairs={{0,2},{2,0},{4,6},{6,4},{8,10},{10,8},{12,14},{14,12},{1,3},{3,1},... | collective-permute-start | bytes 6291464 | tf_op jit(solution)/shard_map/ppermute | solution.py:19
  12.6 6.1 %copy-start.2 = (s32[2]{0:T(128)S(1)}, s32[2]{0:T(128)}, u32[]{:S(2)}) copy-start(s32[2]{0:T(128)} %constant.117.clone) | copy-start | bytes 28
  12.6 7.3 %copy-start.4 = (s32[3]{0:T(128)S(1)}, s32[3]{0:T(128)}, u32[]{:S(2)}) copy-start(s32[3]{0:T(128)} %constant.116.clone) | copy-start | bytes 40
  52.4 46.2 %collective-permute-start.3 = (bf16[2,2,512,512]{3,2,1,0:T(8,128)(2,1)}, bf16[2,2,512,512]{3,2,1,0:T(8,128)(2,1)}, u32[]{:S(2)}, u32[]{:S(2)}) collective-permute-start(bf16[2,2,512,512]{3,2,1,0:T(8,128)(2,1)} %shard_map.122.refs_2_.refs_3_), channel_id=1, source_target_pairs={{0,4},{2,6},{4,0},{6,2},{8,12},{10,14},{12,8},{14,10},{1,5},{3,7},... | collective-permute-start | bytes 6291464 | tf_op jit(solution)/shard_map/ppermute | solution.py:19
  52.7 46.2 %collective-permute-start.5 = (bf16[2,2,512,512]{3,2,1,0:T(8,128)(2,1)}, bf16[2,2,512,512]{3,2,1,0:T(8,128)(2,1)}, u32[]{:S(2)}, u32[]{:S(2)}) collective-permute-start(bf16[2,2,512,512]{3,2,1,0:T(8,128)(2,1)} %collective-permute-done.1.refs_1_.refs_2_), channel_id=1, source_target_pairs={{0,2},{2,0},{4,6},{6,4},{8,10},{10,8},{12,14},{14,12},{1,3},{3,1},... | collective-permute-start | bytes 6291464 | tf_op jit(solution)/shard_map/ppermute | solution.py:19
  54.2 44.7 %collective-permute-start.4 = (bf16[2,2,512,512]{3,2,1,0:T(8,128)(2,1)}, bf16[2,2,512,512]{3,2,1,0:T(8,128)(2,1)}, u32[]{:S(2)}, u32[]{:S(2)}) collective-permute-start(bf16[2,2,512,512]{3,2,1,0:T(8,128)(2,1)} %collective-permute-done.1.refs_1_.refs_2_), channel_id=1, source_target_pairs={{0,1},{1,0},{2,3},{3,2},{4,8},{5,9},{6,10},{7,11},{8,4},{9,5},{10,... | collective-permute-start | bytes 6291464 | tf_op jit(solution)/shard_map/ppermute | solution.py:26
  98.9 33.3 %collective-permute-start.9 = (bf16[2,2,1024,512]{3,2,1,0:T(8,128)(2,1)}, bf16[2,2,1024,512]{3,2,1,0:T(8,128)(2,1)}, u32[]{:S(2)}, u32[]{:S(2)}) collective-permute-start(bf16[2,2,1024,512]{3,2,1,0:T(8,128)(2,1)} %shard_map.127.refs_0_), channel_id=1, source_target_pairs={{0,1},{1,0},{2,3},{3,2},{4,5},{5,4},{6,7},{7,6},{8,9},{9,8},{10,11... | collective-permute-start | bytes 12582920 | tf_op jit(solution)/shard_map/ppermute | solution.py:19
  102.1 18.2 %collective-permute-start.8 = (bf16[1,2,512,512]{3,2,1,0:T(8,128)(2,1)}, bf16[1,2,512,512]{3,2,1,0:T(8,128)(2,1)}, u32[]{:S(2)}, u32[]{:S(2)}) collective-permute-start(bf16[1,2,512,512]{3,2,1,0:T(8,128)(2,1)} %get-tuple-element.67), channel_id=1, source_target_pairs={{0,1},{1,0},{2,3},{3,2},{4,8},{5,9},{6,10},{7,11},{8,4},{9,5},{10,... | collective-permute-start | bytes 3145736 | tf_op jit(solution)/shard_map/ppermute | solution.py:26
  102.6 28.1 %collective-permute-start.7 = (bf16[1,2,512,512]{3,2,1,0:T(8,128)(2,1)}, bf16[1,2,512,512]{3,2,1,0:T(8,128)(2,1)}, u32[]{:S(2)}, u32[]{:S(2)}) collective-permute-start(bf16[1,2,512,512]{3,2,1,0:T(8,128)(2,1)} %get-tuple-element.65), channel_id=1, source_target_pairs={{0,4},{2,6},{4,0},{6,2},{8,12},{10,14},{12,8},{14,10},{1,5},{3,7},... | collective-permute-start | bytes 3145736 | tf_op jit(solution)/shard_map/ppermute | solution.py:19
  106.9 25.3 %collective-permute-start.6 = (bf16[1,2,512,512]{3,2,1,0:T(8,128)(2,1)}, bf16[1,2,512,512]{3,2,1,0:T(8,128)(2,1)}, u32[]{:S(2)}, u32[]{:S(2)}) collective-permute-start(bf16[1,2,512,512]{3,2,1,0:T(8,128)(2,1)} %get-tuple-element.64.refs_1_), channel_id=1, source_target_pairs={{0,2},{2,0},{4,6},{6,4},{8,10},{10,8},{12,14},{14,12},{1,3},{3,1},... | collective-permute-start | bytes 3145736 | tf_op jit(solution)/shard_map/ppermute | solution.py:19
  132.2 10.9 %collective-permute-start.13 = (bf16[2,2,512,512]{3,2,1,0:T(8,128)(2,1)}, bf16[2,2,512,512]{3,2,1,0:T(8,128)(2,1)}, u32[]{:S(2)}, u32[]{:S(2)}) collective-permute-start(bf16[2,2,512,512]{3,2,1,0:T(8,128)(2,1)} %collective-permute-done.5.refs_0_.refs_1_.refs_3_.refs_4_), channel_id=1, source_target_pairs={{0,1},{1,0},{2,3},{3,2},{4,5},{5,4},{6,7},{7,6},{8,9},{9,8},{10,11... | collective-permute-start | bytes 6291464 | tf_op jit(solution)/shard_map/ppermute | solution.py:19
  132.2 10.9 %collective-permute-start.14 = (bf16[2,2,512,512]{3,2,1,0:T(8,128)(2,1)}, bf16[2,2,512,512]{3,2,1,0:T(8,128)(2,1)}, u32[]{:S(2)}, u32[]{:S(2)}) collective-permute-start(bf16[2,2,512,512]{3,2,1,0:T(8,128)(2,1)} %collective-permute-done.4.middles.refs_2_), channel_id=1, source_target_pairs={{0,1},{1,0},{2,3},{3,2},{4,5},{5,4},{6,7},{7,6},{8,9},{9,8},{10,11... | collective-permute-start | bytes 6291464 | tf_op jit(solution)/shard_map/ppermute | solution.py:19
  132.8 25.4 %collective-permute-start.10 = (bf16[1,2,512,512]{3,2,1,0:T(8,128)(2,1)}, bf16[1,2,512,512]{3,2,1,0:T(8,128)(2,1)}, u32[]{:S(2)}, u32[]{:S(2)}) collective-permute-start(bf16[1,2,512,512]{3,2,1,0:T(8,128)(2,1)} %get-tuple-element.76.refs_1_), channel_id=1, source_target_pairs={{0,2},{2,0},{4,6},{6,4},{8,10},{10,8},{12,14},{14,12},{1,3},{3,1},... | collective-permute-start | bytes 3145736 | tf_op jit(solution)/shard_map/ppermute | solution.py:19
  133.3 25.1 %collective-permute-start.11 = (bf16[1,2,512,512]{3,2,1,0:T(8,128)(2,1)}, bf16[1,2,512,512]{3,2,1,0:T(8,128)(2,1)}, u32[]{:S(2)}, u32[]{:S(2)}) collective-permute-start(bf16[1,2,512,512]{3,2,1,0:T(8,128)(2,1)} %get-tuple-element.77), channel_id=1, source_target_pairs={{0,4},{2,6},{4,0},{6,2},{8,12},{10,14},{12,8},{14,10},{1,5},{3,7},... | collective-permute-start | bytes 3145736 | tf_op jit(solution)/shard_map/ppermute | solution.py:19
  133.6 24.8 %collective-permute-start.12 = (bf16[1,2,512,512]{3,2,1,0:T(8,128)(2,1)}, bf16[1,2,512,512]{3,2,1,0:T(8,128)(2,1)}, u32[]{:S(2)}, u32[]{:S(2)}) collective-permute-start(bf16[1,2,512,512]{3,2,1,0:T(8,128)(2,1)} %get-tuple-element.78), channel_id=1, source_target_pairs={{0,1},{1,0},{2,3},{3,2},{4,8},{5,9},{6,10},{7,11},{8,4},{9,5},{10,... | collective-permute-start | bytes 3145736 | tf_op jit(solution)/shard_map/ppermute | solution.py:26
  143.2 2.2 %copy-start.1 = (f32[2,1024,512]{2,1,0:T(8,128)S(1)}, f32[2,1024,512]{2,1,0:T(8,128)}, u32[]{:S(2)}) copy-start(f32[2,1024,512]{2,1,0:T(8,128)} %shard_map.129.total) | copy-start | bytes 12582916
  145.4 14.0 %copy-start = (f32[2,1024,512]{2,1,0:T(8,128)S(1)}, f32[2,1024,512]{2,1,0:T(8,128)}, u32[]{:S(2)}) copy-start(f32[2,1024,512]{2,1,0:T(8,128)} %shard_map.132.total) | copy-start | bytes 12582916
  158.4 10.2 %collective-permute-start.15 = (bf16[1,2,512,512]{3,2,1,0:T(8,128)(2,1)}, bf16[1,2,512,512]{3,2,1,0:T(8,128)(2,1)S(1)}, u32[]{:S(2)}, u32[]{:S(2)}) collective-permute-start(bf16[1,2,512,512]{3,2,1,0:T(8,128)(2,1)} %collective-permute-done.8.w7.refs_2_), channel_id=1, source_target_pairs={{0,1},{1,0},{2,3},{3,2},{4,5},{5,4},{6,7},{7,6},{8,9},{9,8},{10,11... | collective-permute-start | bytes 3145736 | tf_op jit(solution)/shard_map/ppermute | solution.py:19
  158.4 10.2 %collective-permute-start.16 = (bf16[1,2,512,512]{3,2,1,0:T(8,128)(2,1)}, bf16[1,2,512,512]{3,2,1,0:T(8,128)(2,1)S(1)}, u32[]{:S(2)}, u32[]{:S(2)}) collective-permute-start(bf16[1,2,512,512]{3,2,1,0:T(8,128)(2,1)} %collective-permute-done.6.w5.refs_3_), channel_id=1, source_target_pairs={{0,1},{1,0},{2,3},{3,2},{4,5},{5,4},{6,7},{7,6},{8,9},{9,8},{10,11... | collective-permute-start | bytes 3145736 | tf_op jit(solution)/shard_map/ppermute | solution.py:19
  158.9 9.7 %collective-permute-start.18 = (bf16[1,2,512,512]{3,2,1,0:T(8,128)(2,1)}, bf16[1,2,512,512]{3,2,1,0:T(8,128)(2,1)S(1)}, u32[]{:S(2)}, u32[]{:S(2)}) collective-permute-start(bf16[1,2,512,512]{3,2,1,0:T(8,128)(2,1)} %collective-permute-done.10.w5.refs_9_), channel_id=1, source_target_pairs={{0,1},{1,0},{2,3},{3,2},{4,5},{5,4},{6,7},{7,6},{8,9},{9,8},{10,11... | collective-permute-start | bytes 3145736 | tf_op jit(solution)/shard_map/ppermute | solution.py:19
  158.9 9.7 %collective-permute-start.17 = (bf16[1,2,512,512]{3,2,1,0:T(8,128)(2,1)}, bf16[1,2,512,512]{3,2,1,0:T(8,128)(2,1)S(1)}, u32[]{:S(2)}, u32[]{:S(2)}) collective-permute-start(bf16[1,2,512,512]{3,2,1,0:T(8,128)(2,1)} %collective-permute-done.12.w7.refs_8_), channel_id=1, source_target_pairs={{0,1},{1,0},{2,3},{3,2},{4,5},{5,4},{6,7},{7,6},{8,9},{9,8},{10,11... | collective-permute-start | bytes 3145736 | tf_op jit(solution)/shard_map/ppermute | solution.py:19
  168.6 17.7 %copy-start.3 = (s32[16]{0:T(128)S(1)}, s32[16]{0:T(128)}, u32[]{:S(2)}) copy-start(s32[16]{0:T(128)} %param.13) | copy-start | bytes 196
  169.4 16.0 %all-to-all-start = ((f32[16,4,512]{2,1,0:T(4,128)}), f32[16,4,512]{2,1,0:T(4,128)S(1)}, u32[]{:S(2)}, u32[]{:S(2)}) async-start(f32[16,4,512]{2,1,0:T(4,128)} %shard_map.134), calls=%async_computation | async-start | bytes 262144 | tf_op jit(solution)/shard_map/all_to_all | solution.py:42

commit v18 on v17

--- a/solution.py
+++ b/solution.py
@@ -10,6 +10,7 @@
 
 VMEM_LIMIT = 63 * 1024 * 1024
 LATE_LIMIT = 30 * 1024 * 1024
+MIDDLE_LIMIT = 44 * 1024 * 1024
 HINT = pl.CostEstimate(flops=1, bytes_accessed=1, transcendentals=0)
 ANYWHERE = pl.BlockSpec(memory_space=pl.ANY)
 
@@ -301,7 +302,7 @@
             copy.wait()
 
 
-def add_late(cross, freq, ids, pieces, blocks, total, row_refs):
+def add_late(cross, freq, ids, pieces, blocks, total, row_refs, limit):
     rows, (width, sources) = cross.shape[2], pieces[0].shape[2:]
     dtype = pieces[0].dtype
     return pl.pallas_call(
@@ -327,7 +328,7 @@
                 pltpu.SemaphoreType.DMA((2, 2)),
             ],
         ),
-        compiler_params=pltpu.CompilerParams(vmem_limit_bytes=LATE_LIMIT),
+        compiler_params=pltpu.CompilerParams(vmem_limit_bytes=limit),
         cost_estimate=HINT,
     )(ids, cross, *pieces, *blocks, total, *row_refs)
 
@@ -604,7 +605,7 @@
     other_xn = swap(xn, "col", 1)
     other_m2 = swap(m2, "col", 1)
     early = [mine, xn, m2, xn, xn, other, other_xn, other_m2, other_xn, other_xn]
-    sums_a, field_a = add_late(cross, 0, late_ids, [x5_a, z_a, w7_a], [z, z], b0, early)
+    sums_a, field_a = add_late(cross, 0, late_ids, [x5_a, z_a, w7_a], [z, z], b0, early, MIDDLE_LIMIT)
     x5_b, z_b, w7_b, sums_a, field_a, b1, other_xn, other_m2, x5_a, w7_a = barrier(
         x5_b, z_b, w7_b, sums_a, field_a, b1, other_xn, other_m2, x5_a, w7_a
     )
@@ -612,7 +613,7 @@
     late = [w7_a, x5_a, w7_b, x5_b]
     others = [swap(piece, "col", 1) for piece in late]
     early = [mine, xn, m2, xn, xn, other, other_xn, other_m2, other_xn, other_xn]
-    sums_b, field_b = add_late(cross, 1, late_ids, [x5_b, z_b, w7_b], [z_a, z_b], b1, early)
+    sums_b, field_b = add_late(cross, 1, late_ids, [x5_b, z_b, w7_b], [z_a, z_b], b1, early, LATE_LIMIT)
     groups = [
         (field_a, sums_a, *late[:2], *others[:2]),
         (field_b, sums_b, *late[2:], *others[2:]),

time: 188 us -> 188 us (level)
  local copies, waits for them, and re-layouts: 6.02 us -> 3.85 us
    unnamed x10 -> x8, local copies, waits for them, and re-layouts: 2.2 us -> 0.02 us
where the time goes in v18:
time: 188 us; the launch traced here: 187 us
  Pallas kernels  88.9 us (47%)
  waiting for transfers between devices  65 us (35%)
  starting transfers between devices  23.7 us (13%)
  other arithmetic  3.95 us (2%)
  local copies, waits for them, and re-layouts  3.85 us (2%)
    ppermute x15, waiting for transfers between devices, swap(): lax.ppermute(value, axis, [(source, source ^ mask) for source in range(si...  57.1 us
    pallas_call x6, Pallas kernels, add_field(): pl.pallas_call(functools.partial(field_kernel, freq, count, has_total, ga...  55.7 us
    pallas_call x2, Pallas kernels, add_late(): pl.pallas_call(functools.partial(late_kernel, freq), out_shape=(jax.Shape...  19.5 us
    ppermute x15, starting transfers between devices, swap(): lax.ppermute(value, axis, [(source, source ^ mask) for source in range(si...  14.6 us
    all_to_all x1, starting transfers between devices, sum_all(): return jnp.sum(lax.all_to_all(copies, axes, 0, 0, tiled=True), axis=0)  8.05 us
    all_to_all x1, waiting for transfers between devices, sum_all(): return jnp.sum(lax.all_to_all(copies, axes, 0, 0, tiled=True), axis=0)  7.93 us
    pallas_call x2, Pallas kernels, copies(): pl.pallas_call(functools.partial(copy_kernel, len(args), jobs), out_shape...  6.71 us
    pallas_call x2, Pallas kernels, take_next(): pl.pallas_call(functools.partial(next_kernel, freq), out_shape=[shape, sh...  6.21 us
  transfers between devices with their start and end apart: 20, of which 9 were waited for; matrix products, arithmetic and copies ran while one was open for 4% of the time, Pallas kernels for 47%

profile of v18, /device:TPU:0, one launch (start us, length us, event | category | flops | bytes accessed | tf_op | source)
XLA Modules:
  0.0 187.3 jit_solution(14473456120945557829)
XLA Ops:
  0.6 0.5 collective-permute-start.2
  1.1 4.1 %collective-permute-start.1 = (bf16[2,2,512,512]{3,2,1,0:T(8,128)(2,1)}, bf16[2,2,512,512]{3,2,1,0:T(8,128)(2,1)}, u32[]{:S(2)}, u32[]{:S(2)}) collective-permute-start(bf16[2,2,512,512]{3,2,1,0:T(8,128)(2,1)} %bitcast.18), channel_id=1, source_target_pairs={{0,4},{2,6},{4,0},{6,2},{8,12},{10,14},{12,8},{14,10},{1,5},{3,7},... | collective-permute-start | bytes 6291464 | tf_op jit(solution)/shard_map/ppermute | solution.py:20
  5.3 1.5 collective-permute-start
  6.8 5.8 %shard_map.124.refs_3_ = f32[2,1024,512]{2,1,0:T(8,128)} custom-call(s32[1]{0:T(128)} %bitcast.2.ids, bf16[2,2,1024,4096]{3,2,1,0:T(8,128)(2,1)} %cross.19, bf16[2,2,512,512]{3,2,1,0:T(8,128)(2,1)} %bitcast.20), custom_call_target="tpu_custom_call" | custom-call | flops 1 | bytes 1 | tf_op jit(solution)/shard_map/pallas_call | solution.py:138
  12.6 0.0 copy-start.1
  12.6 0.0 copy-start.3
  12.6 5.9 %shard_map.123.refs_3_ = f32[2,1024,512]{2,1,0:T(8,128)} custom-call(s32[1]{0:T(128)} %bitcast.2.ids, bf16[2,2,1024,4096]{3,2,1,0:T(8,128)(2,1)} %cross.19, bf16[2,2,512,512]{3,2,1,0:T(8,128)(2,1)} %bitcast.21), custom_call_target="tpu_custom_call" | custom-call | flops 1 | bytes 1 | tf_op jit(solution)/shard_map/pallas_call | solution.py:138
  18.7 0.5 fusion.16
  19.2 0.1 concatenate.11.ids
  19.3 0.6 pad_add_fusion.ids
  19.9 0.6 pad_add_fusion.1.ids
  20.5 2.0 %multiply_reduce_fusion.norms = f32[2,512]{1,0:T(2,128)S(1)} fusion(bf16[2,2,1,512,512]{4,3,2,1,0:T(8,128)(2,1)} %param.12), kind=kLoop, calls=%fused_computation | loop fusion | flops 3144704 | bytes 2101248 | tf_op jit(solution)/shard_map/reduce_sum | solution.py:643
  22.6 3.1 %shard_map.122.refs_2_.refs_3_ = bf16[2,2,512,512]{3,2,1,0:T(8,128)(2,1)} custom-call(s32[2]{0:T(128)} %pad_add_fusion.ids, bf16[2,2,512,512]{3,2,1,0:T(8,128)(2,1)} %collective-permute-done.2.refs_0_, bf16[2,2,1024,4096]{3,2,1,0:T(8,128)(2,1)} %cross.19), custom_call_target="tpu_custom_call", output_to_operand_aliasing={{}: (1, {})} | custom-call | flops 1 | bytes 1 | tf_op jit(solution)/shard_map/pallas_call | solution.py:418
  25.7 25.3 %collective-permute-done.1.refs_1_.refs_2_ = bf16[2,2,512,512]{3,2,1,0:T(8,128)(2,1)} collective-permute-done((bf16[2,2,512,512]{3,2,1,0:T(8,128)(2,1)}, bf16[2,2,512,512]{3,2,1,0:T(8,128)(2,1)}, u32[]{:S(2)}, u32[]{:S(2)}) %collective-permute-start.1) | collective-permute-done | bytes 2097184 | tf_op jit(solution)/shard_map/ppermute | solution.py:20
  51.0 1.4 collective-permute-done.refs_0_.refs_1_
  52.4 0.3 collective-permute-start.3
  52.7 1.5 collective-permute-start.5
  54.2 12.3 %shard_map.125.refs_2_ = f32[2,1024,512]{2,1,0:T(8,128)} custom-call(s32[4]{0:T(128)} %pad_add_fusion.1.ids, bf16[2,2,1024,4096]{3,2,1,0:T(8,128)(2,1)} %cross.19, bf16[2,2,512,512]{3,2,1,0:T(8,128)(2,1)} %collective-permute-done.refs_0_.refs_1_, bf16[2,2,512,512]{3,2,1,0:T(8,128)(2,1)} %collective-permute-done.1.refs_1_.refs_2_, ...), custom_call_target="tpu_custom_call" | custom-call | flops 1 | bytes 1 | tf_op jit(solution)/shard_map/pallas_call | solution.py:138
  66.5 12.4 %shard_map.126.refs_2_ = f32[2,1024,512]{2,1,0:T(8,128)} custom-call(s32[4]{0:T(128)} %pad_add_fusion.1.ids, bf16[2,2,1024,4096]{3,2,1,0:T(8,128)(2,1)} %cross.19, bf16[2,2,512,512]{3,2,1,0:T(8,128)(2,1)} %collective-permute-done.refs_0_.refs_1_, bf16[2,2,512,512]{3,2,1,0:T(8,128)(2,1)} %collective-permute-done.1.refs_1_.refs_2_, ...), custom_call_target="tpu_custom_call" | custom-call | flops 1 | bytes 1 | tf_op jit(solution)/shard_map/pallas_call | solution.py:138
  78.9 3.6 %shard_map.127.refs_0_ = bf16[2,2,1024,512]{3,2,1,0:T(8,128)(2,1)} custom-call(s32[1]{0:T(128)} %bitcast.6.ids, bf16[2,2,512,512]{3,2,1,0:T(8,128)(2,1)} %bitcast.22, bf16[2,2,512,512]{3,2,1,0:T(8,128)(2,1)} %collective-permute-done.refs_0_.refs_1_, bf16[2,2,512,512]{3,2,1,0:T(8,128)(2,1)} %collective-permute-done.1.refs_1_.refs_2_, ...), custom_call_target="tpu_custom_call" | custom-call | flops 1 | bytes 1 | tf_op jit(solution)/shard_map/pallas_call | solution.py:418
  82.5 3.1 %fusion.18 = (bf16[1,2,512,512]{3,2,1,0:T(8,128)(2,1)}, bf16[1,2,512,512]{3,2,1,0:T(8,128)(2,1)}) fusion(bf16[2,2,512,512]{3,2,1,0:T(8,128)(2,1)} %collective-permute-done.refs_0_.refs_1_), kind=kLoop, calls=%fused_computation.40 | loop fusion | bytes 4194304 | tf_op jit(solution)/shard_map/slice | solution.py:587
  85.6 13.0 %collective-permute-done.3.ends.block_re.block_im = bf16[2,2,512,512]{3,2,1,0:T(8,128)(2,1)} collective-permute-done((bf16[2,2,512,512]{3,2,1,0:T(8,128)(2,1)}, bf16[2,2,512,512]{3,2,1,0:T(8,128)(2,1)}, u32[]{:S(2)}, u32[]{:S(2)}) %collective-permute-start.3) | collective-permute-done | bytes 2097184 | tf_op jit(solution)/shard_map/ppermute | solution.py:20
  98.6 0.3 collective-permute-done.5.refs_0_.refs_1_.refs_3_.refs_4_
  98.9 3.1 %shard_map.128 = (bf16[1,2,512,512]{3,2,1,0:T(8,128)(2,1)}, bf16[1,2,512,512]{3,2,1,0:T(8,128)(2,1)}) custom-call(s32[2]{0:T(128)} %pad_add_fusion.ids, bf16[2,2,512,512]{3,2,1,0:T(8,128)(2,1)} %collective-permute-done.3.ends.block_re.block_im, bf16[2,2,512,512]{3,2,1,0:T(8,128)(2,1)} %collective-permute-done.4.middles.refs_2_, bf16[2,2,1024,4096]{3,2,1,0:T(8,128)(2,1)} %cross.19), custom_call_target="tpu_custom_call" | custom-call | flops 1 | bytes 1 | tf_op jit(solution)/shard_map/pallas_call | solution.py:515
  102.1 0.6 collective-permute-start.8
  102.6 4.3 %collective-permute-start.7 = (bf16[1,2,512,512]{3,2,1,0:T(8,128)(2,1)}, bf16[1,2,512,512]{3,2,1,0:T(8,128)(2,1)}, u32[]{:S(2)}, u32[]{:S(2)}) collective-permute-start(bf16[1,2,512,512]{3,2,1,0:T(8,128)(2,1)} %get-tuple-element.65), channel_id=1, source_target_pairs={{0,4},{2,6},{4,0},{6,2},{8,12},{10,14},{12,8},{14,10},{1,5},{3,7},... | collective-permute-start | bytes 3145736 | tf_op jit(solution)/shard_map/ppermute | solution.py:20
  106.9 0.5 collective-permute-start.6
  107.4 9.8 %shard_map.129.total = f32[2,1024,512]{2,1,0:T(8,128)} custom-call(s32[2]{0:T(128)} %get-tuple-element.69.ids, bf16[2,2,1024,4096]{3,2,1,0:T(8,128)(2,1)} %cross.19, bf16[2,2,512,512]{3,2,1,0:T(8,128)(2,1)} %collective-permute-done.5.refs_0_.refs_1_.refs_3_.refs_4_, bf16[1,2,512,512]{3,2,1,0:T(8,128)(2,1)} %get-tuple-element.64.refs_1_, ...), custom_call_target="tpu_custom_call" | custom-call | flops 1 | bytes 1 | tf_op jit(solution)/shard_map/pallas_call | solution.py:138
  117.2 3.1 %shard_map.130 = (bf16[1,2,512,512]{3,2,1,0:T(8,128)(2,1)}, bf16[1,2,512,512]{3,2,1,0:T(8,128)(2,1)}) custom-call(s32[2]{0:T(128)} %pad_add_fusion.ids, bf16[2,2,512,512]{3,2,1,0:T(8,128)(2,1)} %collective-permute-done.3.ends.block_re.block_im, bf16[2,2,512,512]{3,2,1,0:T(8,128)(2,1)} %collective-permute-done.4.middles.refs_2_, bf16[2,2,1024,4096]{3,2,1,0:T(8,128)(2,1)} %cross.19), custom_call_target="tpu_custom_call" | custom-call | flops 1 | bytes 1 | tf_op jit(solution)/shard_map/pallas_call | solution.py:515
  120.3 10.5 %collective-permute-done.7.w6.block_re = bf16[1,2,512,512]{3,2,1,0:T(8,128)(2,1)} collective-permute-done((bf16[1,2,512,512]{3,2,1,0:T(8,128)(2,1)}, bf16[1,2,512,512]{3,2,1,0:T(8,128)(2,1)}, u32[]{:S(2)}, u32[]{:S(2)}) %collective-permute-start.7) | collective-permute-done | bytes 1048608 | tf_op jit(solution)/shard_map/ppermute | solution.py:20
  130.8 1.5 collective-permute-done.6.w5.refs_3_
  132.2 0.5 collective-permute-start.14
  132.8 0.5 collective-permute-start.10
  133.3 0.3 collective-permute-start.11
  133.6 9.6 %shard_map.132.total = f32[2,1024,512]{2,1,0:T(8,128)} custom-call(s32[2]{0:T(128)} %get-tuple-element.69.ids, bf16[2,2,1024,4096]{3,2,1,0:T(8,128)(2,1)} %cross.19, bf16[2,2,512,512]{3,2,1,0:T(8,128)(2,1)} %collective-permute-done.5.refs_0_.refs_1_.refs_3_.refs_4_, bf16[1,2,512,512]{3,2,1,0:T(8,128)(2,1)} %get-tuple-element.76.refs_1_, ...), custom_call_target="tpu_custom_call" | custom-call | flops 1 | bytes 1 | tf_op jit(solution)/shard_map/pallas_call | solution.py:138
  143.2 10.1 %shard_map.131 = (f32[8,512]{1,0:T(8,128)S(1)}, f32[2,512,512]{2,1,0:T(8,128)S(1)}) custom-call(s32[8]{0:T(128)S(1)} %concatenate.11.ids, bf16[2,2,1024,4096]{3,2,1,0:T(8,128)(2,1)} %cross.19, bf16[1,2,512,512]{3,2,1,0:T(8,128)(2,1)} %collective-permute-done.6.w5.refs_3_, bf16[1,2,512,512]{3,2,1,0:T(8,128)(2,1)} %collective-permute-done.7.w6.block_re, ...), custom_call_target="tpu_custom_call" | custom-call | flops 1 | bytes 1 | tf_op jit(solution)/shard_map/pallas_call | solution.py:308
  153.3 4.8 %collective-permute-done.10.w5.refs_9_ = bf16[1,2,512,512]{3,2,1,0:T(8,128)(2,1)} collective-permute-done((bf16[1,2,512,512]{3,2,1,0:T(8,128)(2,1)}, bf16[1,2,512,512]{3,2,1,0:T(8,128)(2,1)}, u32[]{:S(2)}, u32[]{:S(2)}) %collective-permute-start.10) | collective-permute-done | bytes 1048608 | tf_op jit(solution)/shard_map/ppermute | solution.py:20
  158.1 0.3 collective-permute-done.11.w6.block_im
  158.4 0.5 collective-permute-start.16
  158.9 0.5 collective-permute-start.17
  159.4 9.4 %shard_map.133 = (f32[8,512]{1,0:T(8,128)S(1)}, f32[2,512,512]{2,1,0:T(8,128)S(1)}) custom-call(s32[8]{0:T(128)S(1)} %concatenate.11.ids, bf16[2,2,1024,4096]{3,2,1,0:T(8,128)(2,1)} %cross.19, bf16[1,2,512,512]{3,2,1,0:T(8,128)(2,1)} %collective-permute-done.10.w5.refs_9_, bf16[1,2,512,512]{3,2,1,0:T(8,128)(2,1)} %collective-permute-done.11.w6.block_im, ...), custom_call_target="tpu_custom_call" | custom-call | flops 1 | bytes 1 | tf_op jit(solution)/shard_map/pallas_call | solution.py:308
  168.9 0.8 shard_map.134
  169.7 8.1 %all-to-all-start = ((f32[16,4,512]{2,1,0:T(4,128)}), f32[16,4,512]{2,1,0:T(4,128)S(1)}, u32[]{:S(2)}, u32[]{:S(2)}) async-start(f32[16,4,512]{2,1,0:T(4,128)} %shard_map.134), calls=%async_computation | async-start | bytes 262144 | tf_op jit(solution)/shard_map/all_to_all | solution.py:43
  177.7 7.9 %all-to-all-done = f32[16,4,512]{2,1,0:T(4,128)S(1)} async-done(((f32[16,4,512]{2,1,0:T(4,128)}), f32[16,4,512]{2,1,0:T(4,128)S(1)}, u32[]{:S(2)}, u32[]{:S(2)}) %all-to-all-start) | async-done | bytes 131104 | tf_op jit(solution)/shard_map/all_to_all | solution.py:43
  185.7 0.1 abs_reduce_fusion
  185.8 0.1 reshape.41
  185.9 0.6 constant_dynamic-slice_fusion
  186.5 0.8 fusion
  (27 shorter events, 0.1 us)
Async XLA Ops:
  0.6 21.9 %collective-permute-start.2 = (bf16[2,2,512,512]{3,2,1,0:T(8,128)(2,1)}, bf16[2,2,512,512]{3,2,1,0:T(8,128)(2,1)}, u32[]{:S(2)}, u32[]{:S(2)}) collective-permute-start(bf16[2,2,512,512]{3,2,1,0:T(8,128)(2,1)} %bitcast.17), channel_id=1, source_target_pairs={{0,1},{1,0},{2,3},{3,2},{4,8},{5,9},{6,10},{7,11},{8,4},{9,5},{10,... | collective-permute-start | bytes 6291464 | tf_op jit(solution)/shard_map/ppermute | solution.py:27
  1.1 49.8 %collective-permute-start.1 = (bf16[2,2,512,512]{3,2,1,0:T(8,128)(2,1)}, bf16[2,2,512,512]{3,2,1,0:T(8,128)(2,1)}, u32[]{:S(2)}, u32[]{:S(2)}) collective-permute-start(bf16[2,2,512,512]{3,2,1,0:T(8,128)(2,1)} %bitcast.18), channel_id=1, source_target_pairs={{0,4},{2,6},{4,0},{6,2},{8,12},{10,14},{12,8},{14,10},{1,5},{3,7},... | collective-permute-start | bytes 6291464 | tf_op jit(solution)/shard_map/ppermute | solution.py:20
  5.3 47.1 %collective-permute-start = (bf16[2,2,512,512]{3,2,1,0:T(8,128)(2,1)}, bf16[2,2,512,512]{3,2,1,0:T(8,128)(2,1)}, u32[]{:S(2)}, u32[]{:S(2)}) collective-permute-start(bf16[2,2,512,512]{3,2,1,0:T(8,128)(2,1)} %bitcast.19), channel_id=1, source_target_pairs={{0,2},{2,0},{4,6},{6,4},{8,10},{10,8},{12,14},{14,12},{1,3},{3,1},... | collective-permute-start | bytes 6291464 | tf_op jit(solution)/shard_map/ppermute | solution.py:20
  12.6 6.1 %copy-start.1 = (s32[2]{0:T(128)S(1)}, s32[2]{0:T(128)}, u32[]{:S(2)}) copy-start(s32[2]{0:T(128)} %constant.117.clone) | copy-start | bytes 28
  12.6 7.3 %copy-start.3 = (s32[3]{0:T(128)S(1)}, s32[3]{0:T(128)}, u32[]{:S(2)}) copy-start(s32[3]{0:T(128)} %constant.116.clone) | copy-start | bytes 40
  52.4 46.2 %collective-permute-start.3 = (bf16[2,2,512,512]{3,2,1,0:T(8,128)(2,1)}, bf16[2,2,512,512]{3,2,1,0:T(8,128)(2,1)}, u32[]{:S(2)}, u32[]{:S(2)}) collective-permute-start(bf16[2,2,512,512]{3,2,1,0:T(8,128)(2,1)} %shard_map.122.refs_2_.refs_3_), channel_id=1, source_target_pairs={{0,4},{2,6},{4,0},{6,2},{8,12},{10,14},{12,8},{14,10},{1,5},{3,7},... | collective-permute-start | bytes 6291464 | tf_op jit(solution)/shard_map/ppermute | solution.py:20
  52.7 46.2 %collective-permute-start.5 = (bf16[2,2,512,512]{3,2,1,0:T(8,128)(2,1)}, bf16[2,2,512,512]{3,2,1,0:T(8,128)(2,1)}, u32[]{:S(2)}, u32[]{:S(2)}) collective-permute-start(bf16[2,2,512,512]{3,2,1,0:T(8,128)(2,1)} %collective-permute-done.1.refs_1_.refs_2_), channel_id=1, source_target_pairs={{0,2},{2,0},{4,6},{6,4},{8,10},{10,8},{12,14},{14,12},{1,3},{3,1},... | collective-permute-start | bytes 6291464 | tf_op jit(solution)/shard_map/ppermute | solution.py:20
  54.2 44.7 %collective-permute-start.4 = (bf16[2,2,512,512]{3,2,1,0:T(8,128)(2,1)}, bf16[2,2,512,512]{3,2,1,0:T(8,128)(2,1)}, u32[]{:S(2)}, u32[]{:S(2)}) collective-permute-start(bf16[2,2,512,512]{3,2,1,0:T(8,128)(2,1)} %collective-permute-done.1.refs_1_.refs_2_), channel_id=1, source_target_pairs={{0,1},{1,0},{2,3},{3,2},{4,8},{5,9},{6,10},{7,11},{8,4},{9,5},{10,... | collective-permute-start | bytes 6291464 | tf_op jit(solution)/shard_map/ppermute | solution.py:27
  98.9 33.3 %collective-permute-start.9 = (bf16[2,2,1024,512]{3,2,1,0:T(8,128)(2,1)}, bf16[2,2,1024,512]{3,2,1,0:T(8,128)(2,1)}, u32[]{:S(2)}, u32[]{:S(2)}) collective-permute-start(bf16[2,2,1024,512]{3,2,1,0:T(8,128)(2,1)} %shard_map.127.refs_0_), channel_id=1, source_target_pairs={{0,1},{1,0},{2,3},{3,2},{4,5},{5,4},{6,7},{7,6},{8,9},{9,8},{10,11... | collective-permute-start | bytes 12582920 | tf_op jit(solution)/shard_map/ppermute | solution.py:20
  102.1 18.2 %collective-permute-start.8 = (bf16[1,2,512,512]{3,2,1,0:T(8,128)(2,1)}, bf16[1,2,512,512]{3,2,1,0:T(8,128)(2,1)}, u32[]{:S(2)}, u32[]{:S(2)}) collective-permute-start(bf16[1,2,512,512]{3,2,1,0:T(8,128)(2,1)} %get-tuple-element.67), channel_id=1, source_target_pairs={{0,1},{1,0},{2,3},{3,2},{4,8},{5,9},{6,10},{7,11},{8,4},{9,5},{10,... | collective-permute-start | bytes 3145736 | tf_op jit(solution)/shard_map/ppermute | solution.py:27
  102.6 28.1 %collective-permute-start.7 = (bf16[1,2,512,512]{3,2,1,0:T(8,128)(2,1)}, bf16[1,2,512,512]{3,2,1,0:T(8,128)(2,1)}, u32[]{:S(2)}, u32[]{:S(2)}) collective-permute-start(bf16[1,2,512,512]{3,2,1,0:T(8,128)(2,1)} %get-tuple-element.65), channel_id=1, source_target_pairs={{0,4},{2,6},{4,0},{6,2},{8,12},{10,14},{12,8},{14,10},{1,5},{3,7},... | collective-permute-start | bytes 3145736 | tf_op jit(solution)/shard_map/ppermute | solution.py:20
  106.9 25.3 %collective-permute-start.6 = (bf16[1,2,512,512]{3,2,1,0:T(8,128)(2,1)}, bf16[1,2,512,512]{3,2,1,0:T(8,128)(2,1)}, u32[]{:S(2)}, u32[]{:S(2)}) collective-permute-start(bf16[1,2,512,512]{3,2,1,0:T(8,128)(2,1)} %get-tuple-element.64.refs_1_), channel_id=1, source_target_pairs={{0,2},{2,0},{4,6},{6,4},{8,10},{10,8},{12,14},{14,12},{1,3},{3,1},... | collective-permute-start | bytes 3145736 | tf_op jit(solution)/shard_map/ppermute | solution.py:20
  132.2 10.9 %collective-permute-start.13 = (bf16[2,2,512,512]{3,2,1,0:T(8,128)(2,1)}, bf16[2,2,512,512]{3,2,1,0:T(8,128)(2,1)}, u32[]{:S(2)}, u32[]{:S(2)}) collective-permute-start(bf16[2,2,512,512]{3,2,1,0:T(8,128)(2,1)} %collective-permute-done.5.refs_0_.refs_1_.refs_3_.refs_4_), channel_id=1, source_target_pairs={{0,1},{1,0},{2,3},{3,2},{4,5},{5,4},{6,7},{7,6},{8,9},{9,8},{10,11... | collective-permute-start | bytes 6291464 | tf_op jit(solution)/shard_map/ppermute | solution.py:20
  132.2 11.0 %collective-permute-start.14 = (bf16[2,2,512,512]{3,2,1,0:T(8,128)(2,1)}, bf16[2,2,512,512]{3,2,1,0:T(8,128)(2,1)}, u32[]{:S(2)}, u32[]{:S(2)}) collective-permute-start(bf16[2,2,512,512]{3,2,1,0:T(8,128)(2,1)} %collective-permute-done.4.middles.refs_2_), channel_id=1, source_target_pairs={{0,1},{1,0},{2,3},{3,2},{4,5},{5,4},{6,7},{7,6},{8,9},{9,8},{10,11... | collective-permute-start | bytes 6291464 | tf_op jit(solution)/shard_map/ppermute | solution.py:20
  132.8 25.4 %collective-permute-start.10 = (bf16[1,2,512,512]{3,2,1,0:T(8,128)(2,1)}, bf16[1,2,512,512]{3,2,1,0:T(8,128)(2,1)}, u32[]{:S(2)}, u32[]{:S(2)}) collective-permute-start(bf16[1,2,512,512]{3,2,1,0:T(8,128)(2,1)} %get-tuple-element.76.refs_1_), channel_id=1, source_target_pairs={{0,2},{2,0},{4,6},{6,4},{8,10},{10,8},{12,14},{14,12},{1,3},{3,1},... | collective-permute-start | bytes 3145736 | tf_op jit(solution)/shard_map/ppermute | solution.py:20
  133.3 25.1 %collective-permute-start.11 = (bf16[1,2,512,512]{3,2,1,0:T(8,128)(2,1)}, bf16[1,2,512,512]{3,2,1,0:T(8,128)(2,1)}, u32[]{:S(2)}, u32[]{:S(2)}) collective-permute-start(bf16[1,2,512,512]{3,2,1,0:T(8,128)(2,1)} %get-tuple-element.77), channel_id=1, source_target_pairs={{0,4},{2,6},{4,0},{6,2},{8,12},{10,14},{12,8},{14,10},{1,5},{3,7},... | collective-permute-start | bytes 3145736 | tf_op jit(solution)/shard_map/ppermute | solution.py:20
  133.6 24.8 %collective-permute-start.12 = (bf16[1,2,512,512]{3,2,1,0:T(8,128)(2,1)}, bf16[1,2,512,512]{3,2,1,0:T(8,128)(2,1)}, u32[]{:S(2)}, u32[]{:S(2)}) collective-permute-start(bf16[1,2,512,512]{3,2,1,0:T(8,128)(2,1)} %get-tuple-element.78), channel_id=1, source_target_pairs={{0,1},{1,0},{2,3},{3,2},{4,8},{5,9},{6,10},{7,11},{8,4},{9,5},{10,... | collective-permute-start | bytes 3145736 | tf_op jit(solution)/shard_map/ppermute | solution.py:27
  143.2 16.2 %copy-start = (f32[2,1024,512]{2,1,0:T(8,128)S(1)}, f32[2,1024,512]{2,1,0:T(8,128)}, u32[]{:S(2)}) copy-start(f32[2,1024,512]{2,1,0:T(8,128)} %shard_map.132.total) | copy-start | bytes 12582916
  158.4 10.4 %collective-permute-start.15 = (bf16[1,2,512,512]{3,2,1,0:T(8,128)(2,1)}, bf16[1,2,512,512]{3,2,1,0:T(8,128)(2,1)S(1)}, u32[]{:S(2)}, u32[]{:S(2)}) collective-permute-start(bf16[1,2,512,512]{3,2,1,0:T(8,128)(2,1)} %collective-permute-done.8.w7.refs_2_), channel_id=1, source_target_pairs={{0,1},{1,0},{2,3},{3,2},{4,5},{5,4},{6,7},{7,6},{8,9},{9,8},{10,11... | collective-permute-start | bytes 3145736 | tf_op jit(solution)/shard_map/ppermute | solution.py:20
  158.4 10.4 %collective-permute-start.16 = (bf16[1,2,512,512]{3,2,1,0:T(8,128)(2,1)}, bf16[1,2,512,512]{3,2,1,0:T(8,128)(2,1)S(1)}, u32[]{:S(2)}, u32[]{:S(2)}) collective-permute-start(bf16[1,2,512,512]{3,2,1,0:T(8,128)(2,1)} %collective-permute-done.6.w5.refs_3_), channel_id=1, source_target_pairs={{0,1},{1,0},{2,3},{3,2},{4,5},{5,4},{6,7},{7,6},{8,9},{9,8},{10,11... | collective-permute-start | bytes 3145736 | tf_op jit(solution)/shard_map/ppermute | solution.py:20
  158.9 9.9 %collective-permute-start.18 = (bf16[1,2,512,512]{3,2,1,0:T(8,128)(2,1)}, bf16[1,2,512,512]{3,2,1,0:T(8,128)(2,1)S(1)}, u32[]{:S(2)}, u32[]{:S(2)}) collective-permute-start(bf16[1,2,512,512]{3,2,1,0:T(8,128)(2,1)} %collective-permute-done.10.w5.refs_9_), channel_id=1, source_target_pairs={{0,1},{1,0},{2,3},{3,2},{4,5},{5,4},{6,7},{7,6},{8,9},{9,8},{10,11... | collective-permute-start | bytes 3145736 | tf_op jit(solution)/shard_map/ppermute | solution.py:20
  158.9 9.9 %collective-permute-start.17 = (bf16[1,2,512,512]{3,2,1,0:T(8,128)(2,1)}, bf16[1,2,512,512]{3,2,1,0:T(8,128)(2,1)S(1)}, u32[]{:S(2)}, u32[]{:S(2)}) collective-permute-start(bf16[1,2,512,512]{3,2,1,0:T(8,128)(2,1)} %collective-permute-done.12.w7.refs_8_), channel_id=1, source_target_pairs={{0,1},{1,0},{2,3},{3,2},{4,5},{5,4},{6,7},{7,6},{8,9},{9,8},{10,11... | collective-permute-start | bytes 3145736 | tf_op jit(solution)/shard_map/ppermute | solution.py:20
  168.9 17.6 %copy-start.2 = (s32[16]{0:T(128)S(1)}, s32[16]{0:T(128)}, u32[]{:S(2)}) copy-start(s32[16]{0:T(128)} %param.13) | copy-start | bytes 196
  169.7 16.0 %all-to-all-start = ((f32[16,4,512]{2,1,0:T(4,128)}), f32[16,4,512]{2,1,0:T(4,128)S(1)}, u32[]{:S(2)}, u32[]{:S(2)}) async-start(f32[16,4,512]{2,1,0:T(4,128)} %shard_map.134), calls=%async_computation | async-start | bytes 262144 | tf_op jit(solution)/shard_map/all_to_all | solution.py:43
